TPU v7x, 32 devices: a whole 2x2x4 slice. The times are simulated.
32 devices in a mesh: rep: 4 (over z), ep: 8 (over y, x, core).
Axes of the slice: x: 2, y: 2, z: 4, core: 2. Of those that a mesh axis runs over, the one named last changes fastest.
Arguments:
- tokens: bfloat16 [8192, 2048], P(('rep', 'ep')), may hold values from -6 to 6
- cotangent: bfloat16 [8192, 2048], P(('rep', 'ep')), may hold values from -6 to 6
- w_qkv: bfloat16 [2048, 6144], P(('rep', 'ep')), may hold values from -0.125 to 0.125
- w_o: bfloat16 [2048, 2048], P(('rep', 'ep')), may hold values from -1 to 1
- w_router: bfloat16 [2048, 16], P(('rep', 'ep')), may hold values from -0.06591797 to 0.06591797
- norm_gains: bfloat16 [4096], P(('rep', 'ep')), may hold values from 0.5 to 1.5
- qk_gain: bfloat16 [256], replicated, may hold values from 1 to 2
- w_in: bfloat16 [16, 2048, 2048], P('ep', 'rep'), may hold values from -0.125 to 0.125
- w_out: bfloat16 [16, 1024, 2048], P('ep', 'rep'), may hold values from -0.5 to 0.5
- segments: int32 [4, 2, 1024], P('rep'), may hold values from 0 to 3, never falling along the last dimension, each value on 1 to 512 neighbouring positions
- routes: int32 [8192, 8], P(('rep', 'ep')), may hold values from 0 to 15, all different within a row; in each aligned block of 128 rows (0 to 127, 128 to 255, ...) at most 68 rows name the same one
Outputs:
- output: bfloat16 [8192, 2048], P(('rep', 'ep'))
- grad_tokens: float32 [8192, 2048], P(('rep', 'ep'))
- grad_w_qkv: float32 [2048, 6144], P(('rep', 'ep'))
- grad_w_o: float32 [2048, 2048], P(('rep', 'ep'))
- grad_w_router: float32 [2048, 16], P(('rep', 'ep'))
- grad_norm_gains: float32 [4096], P(('rep', 'ep'))
- grad_qk_gain: float32 [256], replicated
- grad_w_in: float32 [16, 2048, 2048], P('ep', 'rep')
- grad_w_out: float32 [16, 1024, 2048], P('ep', 'rep')
Inputs may be any that keep to these rules, and one draw needn't show every extreme that they name: `routes`: in each aligned block of 128 rows (one micro-batch of one device on this slice) no expert is named by more than 68 rows, a bound that some block reaches; a row names 8 different experts. `segments`: never falls along a sequence.
All inputs are finite; a program needn't handle non-finite values.
Results may differ from a plain program's by a relative error of at most 0.018.
The roundings to bfloat16 on the way count: a program that leaves them out, or rounds other values in their place, can miss the bound.
Values may be sent and summed in bfloat16 or wider, within the bound.
No kernel may reach another device: no remote copies, remote signals or barrier semaphores. Data moves between devices by JAX's collectives and lax.ppermute only.
A program may use at most 384 MiB of HBM per device.

v0:
```python
from functools import partial
import math

import jax
import jax.numpy as jnp
from jax import lax
from jax.sharding import PartitionSpec as P

D = 2048
HEADS = 16
HD = 128
FF = 1024
TOP = 8
HALF = 512


epsilon = 1e-06
rope_base = 50000.0


def rms_scale(value, gain):
    return value * lax.rsqrt(jnp.mean(value * value, axis=-1, keepdims=True) + epsilon) * gain


def rotate(value, cosine, sine):
    half = value.shape[-1] // 2
    turned = jnp.concatenate([-value[..., half:], value[..., :half]], axis=-1)
    return value * cosine + turned * sine


def doc_positions(segment):
    index = jnp.arange(segment.shape[0], dtype=jnp.int32)
    change = jnp.concatenate([jnp.ones((1,), dtype=jnp.bool_), segment[1:] != segment[:-1]])
    start = lax.cummax(jnp.where(change, index, 0), axis=0)
    return index - start


def rope_tables(position, width):
    steps = jnp.arange(width // 2, dtype=jnp.float32) * (2.0 / width)
    rates = jnp.exp(-steps * math.log(rope_base))
    angle = position.astype(jnp.float32)[:, None] * rates[None, :]
    angle = jnp.concatenate([angle, angle], axis=-1)
    return (jnp.cos(angle), jnp.sin(angle))


def block_slots(route_block, experts):
    flat = route_block.reshape(-1)
    one_hot = (flat[:, None] == jnp.arange(experts, dtype=jnp.int32)[None, :]).astype(jnp.int32)
    before = jnp.cumsum(one_hot, axis=0) - one_hot
    return jnp.sum(before * one_hot, axis=1).reshape(route_block.shape)


def route_gates(route_rows, logits):
    chosen = jnp.take_along_axis(logits, route_rows, axis=1)
    chosen = jnp.exp(chosen - jnp.max(chosen, axis=1, keepdims=True))
    return chosen / jnp.sum(chosen, axis=1, keepdims=True)


def prepare(projected, qk_gains, cosine, sine):
    count = projected.shape[0]
    query = projected[:, :D].reshape(count, HEADS, HD)
    keys = projected[:, D : 2 * D].reshape(count, HEADS, HD)
    values = projected[:, 2 * D :].reshape(count, HEADS, HD)
    query = rotate(rms_scale(query, qk_gains[:HD]), cosine, sine)
    keys = rotate(rms_scale(keys, qk_gains[HD:]), cosine, sine)
    return (query, keys, values)


def block_scores(query, keys, segment, start, first, block, span):
    scale = 1.0 / math.sqrt(query.shape[2])
    q_rows = lax.dynamic_slice_in_dim(query, start, block, 0)
    k_rows = lax.dynamic_slice_in_dim(keys, first, span, 0)
    q_index = start + jnp.arange(block, dtype=jnp.int32)
    k_index = first + jnp.arange(span, dtype=jnp.int32)
    q_seg = lax.dynamic_slice_in_dim(segment, start, block, 0)
    k_seg = lax.dynamic_slice_in_dim(segment, first, span, 0)
    keep = (jnp.abs(q_index[:, None] - k_index[None, :]) <= HALF) & (
        q_seg[:, None] == k_seg[None, :]
    )
    scores = jnp.einsum("qhd,khd->hqk", q_rows, k_rows, preferred_element_type=jnp.float32) * scale
    return (jnp.where(keep[None], scores, -1e30), q_rows, k_rows, scale)


def attention_forward(query, keys, values, segment):
    total = query.shape[0]
    block = min(512, total)
    span = min(total, block + 2 * HALF)

    def one_block(number):
        start = number * block
        first = jnp.clip(start - HALF, 0, total - span)
        scores, q_rows, k_rows, scale = block_scores(
            query, keys, segment, start, first, block, span
        )
        v_rows = lax.dynamic_slice_in_dim(values, first, span, 0)
        top = jnp.max(scores, axis=2, keepdims=True)
        lse = top + jnp.log(jnp.sum(jnp.exp(scores - top), axis=2, keepdims=True))
        weights = jnp.exp(scores - lse).astype(jnp.bfloat16)
        mixed = jnp.einsum("hqk,khd->qhd", weights, v_rows, preferred_element_type=jnp.float32)
        return (mixed, lse[..., 0])

    mixed, lses = lax.map(one_block, jnp.arange(total // block, dtype=jnp.int32))
    return (mixed.reshape(total, query.shape[1], query.shape[2]), lses)


def attention_backward(query, keys, values, segment, lses, grad_out):
    total = query.shape[0]
    block = min(512, total)
    span = min(total, block + 2 * HALF)

    def one_block(carry, item):
        grad_keys, grad_values = carry
        number, lse = item
        start = number * block
        first = jnp.clip(start - HALF, 0, total - span)
        scores, q_rows, k_rows, scale = block_scores(
            query, keys, segment, start, first, block, span
        )
        v_rows = lax.dynamic_slice_in_dim(values, first, span, 0)
        g_rows = lax.dynamic_slice_in_dim(grad_out, start, block, 0)
        weights = jnp.exp(scores - lse[..., None])
        weights_low = weights.astype(jnp.bfloat16)
        grad_weights = jnp.einsum(
            "qhd,khd->hqk", g_rows, v_rows, preferred_element_type=jnp.float32
        )
        delta = jnp.sum(weights * grad_weights, axis=2, keepdims=True)
        grad_scores = (weights * (grad_weights - delta)).astype(jnp.bfloat16)
        grad_q = (
            jnp.einsum("hqk,khd->qhd", grad_scores, k_rows, preferred_element_type=jnp.float32)
            * scale
        )
        grad_k = (
            jnp.einsum("hqk,qhd->khd", grad_scores, q_rows, preferred_element_type=jnp.float32)
            * scale
        )
        grad_v = jnp.einsum("hqk,qhd->khd", weights_low, g_rows, preferred_element_type=jnp.float32)
        grad_keys = lax.dynamic_update_slice_in_dim(
            grad_keys, lax.dynamic_slice_in_dim(grad_keys, first, span, 0) + grad_k, first, 0
        )
        grad_values = lax.dynamic_update_slice_in_dim(
            grad_values, lax.dynamic_slice_in_dim(grad_values, first, span, 0) + grad_v, first, 0
        )
        return ((grad_keys, grad_values), grad_q)

    empty = jnp.zeros(query.shape, jnp.float32)
    numbers = jnp.arange(total // block, dtype=jnp.int32)
    (grad_keys, grad_values), grad_query = lax.scan(one_block, (empty, empty), (numbers, lses))
    return (grad_query.reshape(query.shape), grad_keys, grad_values)


def on_device(
    tokens, cotangent, w_qkv, w_o, w_router, norm_gains, qk_gain, w_in, w_out, segments, routes
):
    ranks = lax.axis_size("ep")
    rank = lax.axis_index("ep")
    everyone = lax.axis_size("rep") * ranks
    micro_count = segments.shape[1]
    rows_micro = tokens.shape[0] // micro_count
    experts_local = w_in.shape[0]
    experts_all = experts_local * ranks
    capacity = rows_micro * TOP * 17 // (16 * experts_all)
    qk_gains = qk_gain.astype(jnp.float32)
    outputs = []
    grad_inputs = []
    dense_sum = None
    expert_sum = None
    for step in range(micro_count):
        dense_full = (
            lax.all_gather(w_qkv, ("rep", "ep"), axis=0, tiled=True),
            lax.all_gather(w_o, ("rep", "ep"), axis=0, tiled=True),
            lax.all_gather(w_router, ("rep", "ep"), axis=0, tiled=True),
            lax.all_gather(norm_gains, ("rep", "ep"), axis=0, tiled=True),
        )
        expert_full = (
            lax.all_gather(w_in, "rep", axis=1, tiled=True),
            lax.all_gather(w_out, "rep", axis=1, tiled=True),
        )
        qkv_weight, out_weight, router_weight, gain_pair = dense_full
        in_weight, out_expert = expert_full
        first_gain = gain_pair[:D].astype(jnp.float32)
        second_gain = gain_pair[D:].astype(jnp.float32)
        lower = step * rows_micro
        stream = tokens[lower : lower + rows_micro].astype(jnp.float32)
        upstream = cotangent[lower : lower + rows_micro].astype(jnp.float32)
        route_rows = routes[lower : lower + rows_micro]
        segment = segments[0, step]
        position = lax.dynamic_slice_in_dim(
            doc_positions(segment), rank * rows_micro, rows_micro, 0
        )
        cosine, sine = rope_tables(position, HD)
        cosine = cosine[:, None, :]
        sine = sine[:, None, :]
        normed_f, norm_one_back = jax.vjp(rms_scale, stream, first_gain)
        normed = normed_f.astype(jnp.bfloat16)
        projected = jnp.dot(normed, qkv_weight, preferred_element_type=jnp.float32)

        def shape_heads(projection_in, gains_in):
            return prepare(projection_in, gains_in, cosine, sine)

        (query_f, keys_f, values_f), heads_pullback = jax.vjp(shape_heads, projected, qk_gains)
        query = query_f.astype(jnp.bfloat16)
        keys = keys_f.astype(jnp.bfloat16)
        values = values_f.astype(jnp.bfloat16)
        query_h, keys_h, values_h = (
            lax.all_to_all(query, "ep", split_axis=1, concat_axis=0, tiled=True),
            lax.all_to_all(keys, "ep", split_axis=1, concat_axis=0, tiled=True),
            lax.all_to_all(values, "ep", split_axis=1, concat_axis=0, tiled=True),
        )
        mixed_h, lses = attention_forward(query_h, keys_h, values_h, segment)
        mixed_h = mixed_h.astype(jnp.bfloat16)
        mixed = lax.all_to_all(mixed_h, "ep", split_axis=0, concat_axis=1, tiled=True).reshape(
            rows_micro, D
        )
        hidden_state = stream + jnp.dot(mixed, out_weight, preferred_element_type=jnp.float32)
        normed_two_f, norm_two_back = jax.vjp(rms_scale, hidden_state, second_gain)
        normed_two = normed_two_f.astype(jnp.bfloat16)
        logits = jnp.dot(normed_two, router_weight, preferred_element_type=jnp.float32)
        gates, gate_pullback = jax.vjp(partial(route_gates, route_rows), logits)
        slots = block_slots(route_rows, experts_all)
        dest = (route_rows * capacity + slots).reshape(-1)
        spread = jnp.broadcast_to(normed_two[:, None, :], (rows_micro, TOP, D)).reshape(-1, D)
        send = jnp.zeros((experts_all * capacity, D), jnp.bfloat16).at[dest].set(spread)
        arrived = lax.all_to_all(
            send.reshape(ranks, experts_local * capacity, D),
            "ep",
            split_axis=0,
            concat_axis=0,
            tiled=True,
        )
        arrived = arrived.reshape(ranks, experts_local, capacity, D)
        both = jnp.einsum("sjcd,jdf->sjcf", arrived, in_weight, preferred_element_type=jnp.float32)
        gate_part = both[..., :FF]
        up_part = both[..., FF:]
        sigma = 1.0 / (1.0 + jnp.exp(-gate_part))
        silu_part = gate_part / (1.0 + jnp.exp(-gate_part))
        active = (silu_part * up_part).astype(jnp.bfloat16)
        produced = jnp.einsum(
            "sjcf,jfd->sjcd", active, out_expert, preferred_element_type=jnp.float32
        ).astype(jnp.bfloat16)
        returned = lax.all_to_all(
            produced.reshape(ranks, experts_local * capacity, D),
            "ep",
            split_axis=0,
            concat_axis=0,
            tiled=True,
        )
        picked = returned.reshape(-1, D)[dest].reshape(rows_micro, TOP, D)
        mixture = jnp.einsum("tk,tkd->td", gates, picked, preferred_element_type=jnp.float32)
        outputs.append((hidden_state + mixture).astype(jnp.bfloat16))
        grad_gates = jnp.einsum("td,tkd->tk", upstream, picked, preferred_element_type=jnp.float32)
        grad_rows = (gates[:, :, None] * upstream[:, None, :]).astype(jnp.bfloat16).reshape(-1, D)
        grad_send = jnp.zeros((experts_all * capacity, D), jnp.bfloat16).at[dest].set(grad_rows)
        grad_arrived = lax.all_to_all(
            grad_send.reshape(ranks, experts_local * capacity, D),
            "ep",
            split_axis=0,
            concat_axis=0,
            tiled=True,
        )
        grad_arrived = grad_arrived.reshape(ranks, experts_local, capacity, D)
        grad_active = jnp.einsum(
            "sjcd,jfd->sjcf", grad_arrived, out_expert, preferred_element_type=jnp.float32
        ).astype(jnp.bfloat16)
        grad_out_expert = jnp.einsum(
            "sjcf,sjcd->jfd", active, grad_arrived, preferred_element_type=jnp.float32
        )
        grad_gate = grad_active * up_part * (sigma + gate_part * sigma * (1.0 - sigma))
        grad_up = grad_active * silu_part
        grad_both = jnp.concatenate([grad_gate, grad_up], axis=-1).astype(jnp.bfloat16)
        grad_in_expert = jnp.einsum(
            "sjcd,sjcf->jdf", arrived, grad_both, preferred_element_type=jnp.float32
        )
        grad_rows_in = jnp.einsum(
            "sjcf,jdf->sjcd", grad_both, in_weight, preferred_element_type=jnp.float32
        ).astype(jnp.bfloat16)
        grad_returned = lax.all_to_all(
            grad_rows_in.reshape(ranks, experts_local * capacity, D),
            "ep",
            split_axis=0,
            concat_axis=0,
            tiled=True,
        )
        grad_picked = grad_returned.reshape(-1, D)[dest].reshape(rows_micro, TOP, D)
        grad_normed_two = jnp.sum(grad_picked.astype(jnp.float32), axis=1)
        grad_logits = gate_pullback(grad_gates)[0].astype(jnp.bfloat16)
        grad_normed_two = grad_normed_two + jnp.einsum(
            "te,de->td", grad_logits, router_weight, preferred_element_type=jnp.float32
        )
        grad_router = jnp.einsum(
            "td,te->de", normed_two, grad_logits, preferred_element_type=jnp.float32
        )
        grad_hidden_part, grad_second_gain = norm_two_back(grad_normed_two)
        grad_hidden = upstream + grad_hidden_part
        grad_branch = grad_hidden.astype(jnp.bfloat16)
        grad_mixed = jnp.einsum(
            "te,de->td", grad_branch, out_weight, preferred_element_type=jnp.float32
        ).astype(jnp.bfloat16)
        grad_out_weight = jnp.einsum(
            "td,te->de", mixed, grad_branch, preferred_element_type=jnp.float32
        )
        grad_mixed_h = lax.all_to_all(
            grad_mixed.reshape(rows_micro, HEADS, HD), "ep", split_axis=1, concat_axis=0, tiled=True
        )
        grad_q_h, grad_k_h, grad_v_h = attention_backward(
            query_h, keys_h, values_h, segment, lses, grad_mixed_h
        )
        grad_q, grad_k, grad_v = (
            lax.all_to_all(
                grad_q_h.astype(jnp.bfloat16), "ep", split_axis=0, concat_axis=1, tiled=True
            ),
            lax.all_to_all(
                grad_k_h.astype(jnp.bfloat16), "ep", split_axis=0, concat_axis=1, tiled=True
            ),
            lax.all_to_all(
                grad_v_h.astype(jnp.bfloat16), "ep", split_axis=0, concat_axis=1, tiled=True
            ),
        )
        grad_projected, grad_qk = heads_pullback(
            (grad_q.astype(jnp.float32), grad_k.astype(jnp.float32), grad_v.astype(jnp.float32))
        )
        grad_projected = grad_projected.astype(jnp.bfloat16)
        grad_normed = jnp.einsum(
            "te,de->td", grad_projected, qkv_weight, preferred_element_type=jnp.float32
        )
        grad_qkv_weight = jnp.einsum(
            "td,te->de", normed, grad_projected, preferred_element_type=jnp.float32
        )
        grad_stream, grad_first_gain = norm_one_back(grad_normed)
        grad_inputs.append(grad_hidden + grad_stream)
        dense_local = (
            grad_qkv_weight,
            grad_out_weight,
            grad_router,
            jnp.concatenate([grad_first_gain, grad_second_gain]),
            grad_qk,
        )
        expert_local = (grad_in_expert, grad_out_expert)
        dense_sum = (
            dense_local if dense_sum is None else jax.tree.map(jnp.add, dense_sum, dense_local)
        )
        expert_sum = (
            expert_local if expert_sum is None else jax.tree.map(jnp.add, expert_sum, expert_local)
        )
    qk_rows = jnp.broadcast_to(dense_sum[4][None, :], (everyone, dense_sum[4].shape[0]))
    dense_sum = (
        lax.psum_scatter(dense_sum[0], ("rep", "ep"), scatter_dimension=0, tiled=True),
        lax.psum_scatter(dense_sum[1], ("rep", "ep"), scatter_dimension=0, tiled=True),
        lax.psum_scatter(dense_sum[2], ("rep", "ep"), scatter_dimension=0, tiled=True),
        lax.psum_scatter(dense_sum[3], ("rep", "ep"), scatter_dimension=0, tiled=True),
        lax.psum_scatter(qk_rows, ("rep", "ep"), scatter_dimension=0, tiled=True)[0],
    )
    expert_sum = (
        lax.psum_scatter(
            expert_sum[0].astype(jnp.bfloat16), "rep", scatter_dimension=1, tiled=True
        ).astype(jnp.float32),
        lax.psum_scatter(
            expert_sum[1].astype(jnp.bfloat16), "rep", scatter_dimension=1, tiled=True
        ).astype(jnp.float32),
    )
    return (
        jnp.concatenate(outputs, axis=0),
        jnp.concatenate(grad_inputs, axis=0),
        dense_sum[0],
        dense_sum[1],
        dense_sum[2],
        dense_sum[3],
        dense_sum[4],
        expert_sum[0],
        expert_sum[1],
    )


def solution(mesh):
    placed = (
        P(("rep", "ep"), None),
        P(("rep", "ep"), None),
        P(("rep", "ep"), None),
        P(("rep", "ep"), None),
        P(("rep", "ep"), None),
        P(("rep", "ep")),
        P(),
        P("ep", "rep", None),
        P("ep", "rep", None),
        P("rep", None, None),
        P(("rep", "ep"), None),
    )
    return jax.shard_map(
        on_device,
        mesh=mesh,
        in_specs=placed,
        out_specs=(
            P(("rep", "ep"), None),
            P(("rep", "ep"), None),
            P(("rep", "ep"), None),
            P(("rep", "ep"), None),
            P(("rep", "ep"), None),
            P(("rep", "ep")),
            P(),
            P("ep", "rep", None),
            P("ep", "rep", None),
        ),
        check_vma=False,
    )
```

profile of v0, /device:TPU:0, one launch (start us, length us, event | category | flops | bytes accessed | tf_op | source)
XLA Modules:
  0.0 2313.2 jit_solution(2231742871863273868)
XLA Ops:
  10.9 43.4 %all-gather = bf16[32,1,128]{2,1,0:T(2,128)(2,1)S(1)} all-gather(bf16[1,1,128]{2,1,0:T(2,128)(2,1)S(1)} %bitcast.684), channel_id=1, replica_groups=mesh['rep'=4,'ep'=8] {'rep','ep'}, dimensions={0}, use_global_device_ids=true | all-gather | bytes 8448 | tf_op jit(solution)/shard_map/all_gather | solution.py:172
  57.2 111.2 %all-gather.7.cloned.1.call-done = bf16[2048,6144]{1,0:T(8,128)(2,1)} async-done(((bf16[64,6144]{1,0:T(8,128)(2,1)}), bf16[2048,6144]{1,0:T(8,128)(2,1)}) %all-gather.7.cloned.1.call-update) | async-done | bytes 25165840 | tf_op jit(solution)/shard_map/all_gather | solution.py:169
  332.1 82.3 %all-gather.1 = bf16[32,64,16]{1,2,0:T(8,128)(2,1)S(1)} all-gather(bf16[1,64,16]{1,2,0:T(8,128)(2,1)S(1)} %bitcast.682), channel_id=1, replica_groups=mesh['rep'=4,'ep'=8] {'rep','ep'}, dimensions={0}, use_global_device_ids=true | all-gather | bytes 67584 | tf_op jit(solution)/shard_map/all_gather | solution.py:171
  465.2 26.7 %all-to-all-done.12 = bf16[8,136,2048]{2,1,0:T(8,128)(2,1)} async-done(((bf16[8,136,2048]{2,1,0:T(8,128)(2,1)}), bf16[8,136,2048]{2,1,0:T(8,128)(2,1)}, u32[]{:S(2)}, u32[]{:S(2)}) %all-to-all-start.12) | async-done | bytes 4456480 | tf_op jit(solution)/shard_map/all_to_all | solution.py:253
  502.6 37.5 %all-gather.11.cloned.1.call-done = bf16[2,2048,2048]{2,1,0:T(8,128)(2,1)} async-done(((bf16[2,512,2048]{2,1,0:T(8,128)(2,1)}), bf16[2,2048,2048]{2,1,0:T(8,128)(2,1)}) %all-gather.11.cloned.1.call-update) | async-done | bytes 16777232 | tf_op jit(solution)/shard_map/all_gather | solution.py:175
  540.1 21.2 fusion.112
  561.3 128.2 %all-gather.13.cloned.1.call-done = bf16[2,1024,2048]{2,1,0:T(8,128)(2,1)} async-done(((bf16[2,256,2048]{2,1,0:T(8,128)(2,1)}), bf16[2,1024,2048]{2,1,0:T(8,128)(2,1)}) %all-gather.13.cloned.1.call-update) | async-done | bytes 8388624 | tf_op jit(solution)/shard_map/all_gather | solution.py:176
  689.5 17.9 fusion.106
  753.9 35.9 %all-to-all-done.13 = bf16[8,136,2048]{2,1,0:T(8,128)(2,1)} async-done(((bf16[8,136,2048]{2,1,0:T(8,128)(2,1)}), bf16[8,136,2048]{2,1,0:T(8,128)(2,1)}, u32[]{:S(2)}, u32[]{:S(2)}) %all-to-all-start.13) | async-done | bytes 4456480 | tf_op jit(solution)/shard_map/all_to_all | solution.py:276
  824.0 22.5 all-to-all-done.5
  912.5 27.3 %all-to-all-done.10 = bf16[8,136,2048]{2,1,0:T(8,128)(2,1)} async-done(((bf16[8,136,2048]{2,1,0:T(8,128)(2,1)}), bf16[8,136,2048]{2,1,0:T(8,128)(2,1)}, u32[]{:S(2)}, u32[]{:S(2)}) %all-to-all-start.10) | async-done | bytes 4456480 | tf_op jit(solution)/shard_map/all_to_all | solution.py:223
  944.3 22.9 fusion.123
  1041.4 18.8 fusion.127
  1060.3 20.2 fusion.83
  1124.2 25.8 %fusion.82 = bf16[2,2048,2048]{2,1,0:T(8,128)(2,1)} fusion(f32[2,2048,2048,1]{2,1,3,0:T(8,128)} %fusion.123, bf16[8,2,68,2048]{3,0,2,1:T(8,128)(2,1)} %bitcast.617, bf16[8,2,68,2048]{3,2,0,1:T(8,128)(2,1)} %pad_maximum_fusion.1), kind=kOutput, calls=%fused_computation.119 | convolution fusion | flops 9143582720 | bytes 59244544 | tf_op jit(solution)/shard_map/sjcd,sjcf->jdf/dot_general | solution.py:270
  1185.2 52.6 %all-to-all-done.19 = bf16[8,136,2048]{2,1,0:T(8,128)(2,1)} async-done(((bf16[8,136,2048]{2,1,0:T(8,128)(2,1)}), bf16[8,136,2048]{2,1,0:T(8,128)(2,1)}, u32[]{:S(2)}, u32[]{:S(2)}) %all-to-all-start.19) | async-done | bytes 4456480 | tf_op jit(solution)/shard_map/all_to_all | solution.py:276
  1297.6 38.7 %while.65 = (s32[]{:T(128)}, f32[1024,2,128]{0,2,1:T(8,128)}, f32[1024,2,128]{0,2,1:T(8,128)}, bf16[2,512,2,128]{3,1,0,2:T(8,128)(2,1)}, s32[2]{0:T(128)S(1)}, /...) while((s32[]{:T(128)}, f32[1024,2,128]{0,2,1:T(8,128)}, ...), condition=%wide.region_54.56_spmd.clone, body=%wide.region_52.55_spmd.clone.sunk | while | flops 1361969664 | bytes 78694816 | solution.py:147
  1357.7 38.9 %while.64 = (s32[]{:T(128)}, f32[1024,2,128]{0,2,1:T(8,128)}, f32[1024,2,128]{0,2,1:T(8,128)}, bf16[2,512,2,128]{3,1,0,2:T(8,128)(2,1)}, s32[2]{0:T(128)S(1)}, /...) while((s32[]{:T(128)}, f32[1024,2,128]{0,2,1:T(8,128)}, ...), condition=%wide.region_41.43_spmd.clone, body=%wide.region_39.42_spmd.clone.sunk | while | flops 1361969664 | bytes 78694816 | solution.py:147
  1467.1 21.4 fusion.227
  1488.5 32.7 %convolution_add_fusion = f32[2048,6144]{1,0:T(8,128)} fusion(f32[2048,6144]{1,0:T(8,128)} %fusion.227, f32[128,2048]{0,1:T(8,128)S(1)} %bitcast.620, f32[128,2048]{0,1:T(8,128)} %bitcast.626, bf16[128,2048]{0,1:T(8,128)(2,1)} %bitcast.632, f32[128]{0:T(128)S(1)} %copy-done.136, f32[2048]{0:T(1024)S(1)} %bitcast.657, bf16[256,2048]{1,0:T(8,128)(2,1)S(1)} %copy-done.9), kind=kOutput, calls=%fused_computation.120 | convolution fusion | flops 3238002688 | bytes 103817728 | tf_op jit(solution)/shard_map/td,te->de/dot_general | solution.py:325
  1555.2 43.3 %all-reduce.20 = (f32[4096]{0:T(1024)S(1)}, f32[32,256]{1,0:T(8,128)S(1)}) all-reduce(f32[4096]{0:T(1024)S(1)} %maximum_add_fusion, f32[32,256]{1,0:T(8,128)S(1)} %broadcast_in_dim.248), channel_id=5, replica_groups=mesh['rep'=4,'ep'=8] {'rep','ep'}, use_global_device_ids=true, to_apply=%region_65.67.clone | all-reduce | flops 12288 | bytes 98304
  1607.6 71.9 %reduce-scatter.12.cloned.1.call-done = bf16[2,512,2048]{2,1,0:T(8,128)(2,1)} async-done(((bf16[2,2048,2048]{2,1,0:T(8,128)(2,1)}), bf16[2,512,2048]{2,1,0:T(8,128)(2,1)}) %reduce-scatter.12.cloned.1.call-update) | async-done | bytes 4194320 | tf_op jit(solution)/shard_map/reduce_scatter | solution.py:353
  1686.2 179.7 %reduce-scatter.10.cloned.1.call-done = f32[64,2048]{1,0:T(8,128)} async-done(((f32[2048,2048]{1,0:T(8,128)}), f32[64,2048]{1,0:T(8,128)}) %reduce-scatter.10.cloned.1.call-update) | async-done | bytes 524304 | tf_op jit(solution)/shard_map/reduce_scatter | solution.py:347
  1865.9 440.3 %reduce-scatter.8.cloned.1.call-done = f32[64,6144]{1,0:T(8,128)} async-done(((f32[2048,6144]{1,0:T(8,128)}), f32[64,6144]{1,0:T(8,128)}) %reduce-scatter.8.cloned.1.call-update) | async-done | bytes 1572880 | tf_op jit(solution)/shard_map/reduce_scatter | solution.py:346
  (767 shorter events, 836.9 us)
Async XLA Ops:
  7.2 161.1 %all-gather.7.cloned.1.call-start = ((), (), s32[]{:S(2)}) async-start(), calls=%async_computation.29 | async-start | bytes 25952256 | tf_op jit(solution)/shard_map/all_gather | solution.py:169
  8.0 295.5 %all-gather.9.cloned.1.call-start = ((), (), s32[]{:S(2)}) async-start(), calls=%async_computation.30 | async-start | bytes 8650752 | tf_op jit(solution)/shard_map/all_gather | solution.py:170
  8.7 531.4 %all-gather.11.cloned.1.call-start = ((), (), s32[]{:S(2)}) async-start(), calls=%async_computation.31 | async-start | bytes 20971520 | tf_op jit(solution)/shard_map/all_gather | solution.py:175
  9.4 680.0 %all-gather.13.cloned.1.call-start = ((), (), s32[]{:S(2)}) async-start(), calls=%async_computation.32 | async-start | bytes 10485760 | tf_op jit(solution)/shard_map/all_gather | solution.py:176
  207.4 14.3 all-to-all-start
  221.7 19.1 all-to-all-start.1
  327.5 107.8 %all-to-all-start.4 = ((bf16[8,136,2048]{2,1,0:T(8,128)(2,1)}), bf16[8,136,2048]{2,1,0:T(8,128)(2,1)}, u32[]{:S(2)}, u32[]{:S(2)}) async-start(bf16[8,136,2048]{2,1,0:T(8,128)(2,1)} %bitcast.601), calls=%async_computation.4 | async-start | bytes 8912896 | tf_op jit(solution)/shard_map/all_to_all | solution.py:223
  435.3 56.7 %all-to-all-start.12 = ((bf16[8,136,2048]{2,1,0:T(8,128)(2,1)}), bf16[8,136,2048]{2,1,0:T(8,128)(2,1)}, u32[]{:S(2)}, u32[]{:S(2)}) async-start(bf16[8,136,2048]{2,1,0:T(8,128)(2,1)} %bitcast.600), calls=%async_computation.12 | async-start | bytes 8912896 | tf_op jit(solution)/shard_map/all_to_all | solution.py:253
  492.0 241.3 %all-to-all-start.9 = ((bf16[1024,2,128]{2,1,0:T(2,128)(2,1)}), bf16[1024,2,128]{2,1,0:T(2,128)(2,1)S(1)}, u32[]{:S(2)}, u32[]{:S(2)}) async-start(bf16[1024,2,128]{2,1,0:T(2,128)(2,1)} %copy.541), calls=%async_computation.9 | async-start | bytes 1048576 | tf_op jit(solution)/shard_map/all_to_all | solution.py:211
  733.3 56.5 %all-to-all-start.13 = ((bf16[8,136,2048]{2,1,0:T(8,128)(2,1)}), bf16[8,136,2048]{2,1,0:T(8,128)(2,1)}, u32[]{:S(2)}, u32[]{:S(2)}) async-start(bf16[8,136,2048]{2,1,0:T(8,128)(2,1)} %copy.554), calls=%async_computation.13 | async-start | bytes 8912896 | tf_op jit(solution)/shard_map/all_to_all | solution.py:276
  789.8 56.7 %all-to-all-start.5 = ((bf16[8,136,2048]{2,1,0:T(8,128)(2,1)}), bf16[8,136,2048]{2,1,0:T(8,128)(2,1)}, u32[]{:S(2)}, u32[]{:S(2)}) async-start(bf16[8,136,2048]{2,1,0:T(8,128)(2,1)} %copy.531), calls=%async_computation.5 | async-start | bytes 8912896 | tf_op jit(solution)/shard_map/all_to_all | solution.py:240
  883.2 56.5 %all-to-all-start.10 = ((bf16[8,136,2048]{2,1,0:T(8,128)(2,1)}), bf16[8,136,2048]{2,1,0:T(8,128)(2,1)}, u32[]{:S(2)}, u32[]{:S(2)}) async-start(bf16[8,136,2048]{2,1,0:T(8,128)(2,1)} %bitcast.602), calls=%async_computation.10 | async-start | bytes 8912896 | tf_op jit(solution)/shard_map/all_to_all | solution.py:223
  939.8 56.5 %all-to-all-start.18 = ((bf16[8,136,2048]{2,1,0:T(8,128)(2,1)}), bf16[8,136,2048]{2,1,0:T(8,128)(2,1)}, u32[]{:S(2)}, u32[]{:S(2)}) async-start(bf16[8,136,2048]{2,1,0:T(8,128)(2,1)} %bitcast.603), calls=%async_computation.18 | async-start | bytes 8912896 | tf_op jit(solution)/shard_map/all_to_all | solution.py:253
  1036.6 56.6 %all-to-all-start.11 = ((bf16[8,136,2048]{2,1,0:T(8,128)(2,1)}), bf16[8,136,2048]{2,1,0:T(8,128)(2,1)}, u32[]{:S(2)}, u32[]{:S(2)}) async-start(bf16[8,136,2048]{2,1,0:T(8,128)(2,1)} %copy.550), calls=%async_computation.11 | async-start | bytes 8912896 | tf_op jit(solution)/shard_map/all_to_all | solution.py:240
  1041.3 482.3 %reduce-scatter.16.cloned.1.call-start = ((), (), s32[]{:S(2)}) async-start(), calls=%async_computation.37 | async-start | bytes 1081344
  1118.8 484.7 %reduce-scatter.14.cloned.1.call-start = ((), (), s32[]{:S(2)}) async-start(), calls=%async_computation.36 | async-start | bytes 10485760 | tf_op jit(solution)/shard_map/reduce_scatter | solution.py:356
  1124.2 555.3 %reduce-scatter.12.cloned.1.call-start = ((), (), s32[]{:S(2)}) async-start(), calls=%async_computation.35 | async-start | bytes 20971520 | tf_op jit(solution)/shard_map/reduce_scatter | solution.py:353
  1177.0 60.9 %all-to-all-start.19 = ((bf16[8,136,2048]{2,1,0:T(8,128)(2,1)}), bf16[8,136,2048]{2,1,0:T(8,128)(2,1)}, u32[]{:S(2)}, u32[]{:S(2)}) async-start(bf16[8,136,2048]{2,1,0:T(8,128)(2,1)} %copy.577), calls=%async_computation.19 | async-start | bytes 8912896 | tf_op jit(solution)/shard_map/all_to_all | solution.py:276
  1181.7 684.2 %reduce-scatter.10.cloned.1.call-start = ((), (), s32[]{:S(2)}) async-start(), calls=%async_computation.34 | async-start | bytes 17301504 | tf_op jit(solution)/shard_map/reduce_scatter | solution.py:347
  1291.8 46.8 %all-to-all-start.14 = ((bf16[128,16,128]{2,0,1:T(8,128)(2,1)}), bf16[128,16,128]{2,0,1:T(8,128)(2,1)}, u32[]{:S(2)}, u32[]{:S(2)}) async-start(bf16[128,16,128]{2,0,1:T(8,128)(2,1)} %bitcast.537), calls=%async_computation.14 | async-start | bytes 1048576 | tf_op jit(solution)/shard_map/all_to_all | solution.py:301
  1352.4 46.5 %all-to-all-start.23 = ((bf16[1024,2,128]{2,1,0:T(2,128)(2,1)}), bf16[1024,2,128]{2,1,0:T(2,128)(2,1)}, u32[]{:S(2)}, u32[]{:S(2)}) async-start(bf16[1024,2,128]{2,1,0:T(2,128)(2,1)} %copy.591), calls=%async_computation.23 | async-start | bytes 1048576 | tf_op jit(solution)/shard_map/all_to_all | solution.py:308
  1426.7 17.7 all-to-all-start.21
  1444.4 18.7 all-to-all-start.15
  1448.6 857.7 %reduce-scatter.8.cloned.1.call-start = ((), (), s32[]{:S(2)}) async-start(), calls=%async_computation.33 | async-start | bytes 51904512 | tf_op jit(solution)/shard_map/reduce_scatter | solution.py:346
  (183 other events, 3601.0 us)
Sparse Core Ops, SparseCore 0:
  10.9 157.3 all-gather.6
  171.2 82.5 all-gather.8
  255.3 284.6 all-gather.10
  541.5 147.9 all-gather.12
  1119.0 132.4 reduce-scatter.15
  1254.4 140.5 reduce-scatter.13
  1397.5 282.0 reduce-scatter.11
  1682.4 183.4 reduce-scatter.9
  1872.9 433.2 reduce-scatter.7
where the time goes:
time: 2330 us; the launch traced here: 2310 us
  waiting for transfers between devices  1220 us (52%)
  matrix products  446 us (19%)
  local copies, waits for them, and re-layouts  220 us (9%)
  blocking collectives  169 us (7%)
  other arithmetic  138 us (6%)
  starting transfers between devices  100 us (4%)
    reduce_scatter x1, waiting for transfers between devices, on_device(): lax.psum_scatter(dense_sum[0], ('rep', 'ep'), scatter_dimension=0, tiled=...  440 us
    reduce_scatter x1, waiting for transfers between devices, on_device(): lax.psum_scatter(dense_sum[1], ('rep', 'ep'), scatter_dimension=0, tiled=...  180 us
    all_gather x1, waiting for transfers between devices, on_device(): lax.all_gather(w_out, 'rep', axis=1, tiled=True)  128 us
    all_gather x1, waiting for transfers between devices, on_device(): lax.all_gather(w_qkv, ('rep', 'ep'), axis=0, tiled=True)  111 us
    all_to_all x2, waiting for transfers between devices, on_device(): lax.all_to_all(grad_rows_in.reshape(ranks, experts_local * capacity, D),...  88.6 us
    all_gather x1, blocking collectives, on_device(): lax.all_gather(w_router, ('rep', 'ep'), axis=0, tiled=True)  82.3 us
    reduce_scatter x1, waiting for transfers between devices, on_device(): lax.psum_scatter(expert_sum[0].astype(jnp.bfloat16), 'rep', scatter_dimen...  71.9 us
    dot_general x2, matrix products, on_device(): jnp.einsum('td,te->de', normed, grad_projected, preferred_element_type=jn...  54.1 us
  transfers between devices with their start and end apart: 33, of which 24 were waited for; matrix products, arithmetic and copies ran while one was open for 30% of the time, Pallas kernels for 0%

commit v1 on v0

v1 whole, which is shorter than its diff:
```python
import math

import jax
import jax.numpy as jnp
from jax import lax
from jax.experimental import pallas as pl
from jax.experimental.pallas import tpu as pltpu
from jax.sharding import PartitionSpec as P

D = 2048
HEADS = 16
HD = 128
FF = 1024
TOP = 8
HALF = 512
PAD = 128

epsilon = 1e-06
rope_base = 50000.0
bf16 = jnp.bfloat16
f32 = jnp.float32


def dot(a, b, dims=((1,), (0,))):
    return lax.dot_general(a, b, (dims, ((), ())), preferred_element_type=f32)


def inverse_rms(value):
    return lax.rsqrt(jnp.mean(value * value, axis=-1, keepdims=True) + epsilon)


def rms_backward(value, inverse, gain, grad):
    scaled = grad * gain
    inner = jnp.mean(scaled * value, axis=-1, keepdims=True)
    return inverse * (scaled - value * (inverse * inverse * inner))


def doc_positions(segment):
    index = jnp.arange(segment.shape[0], dtype=jnp.int32)
    change = jnp.concatenate([jnp.ones((1,), dtype=jnp.bool_), segment[1:] != segment[:-1]])
    start = lax.cummax(jnp.where(change, index, 0), axis=0)
    return index - start


def rope_tables(position, width):
    steps = jnp.arange(width // 2, dtype=f32) * (2.0 / width)
    rates = jnp.exp(-steps * math.log(rope_base))
    angle = position.astype(f32)[:, None] * rates[None, :]
    angle = jnp.concatenate([angle, angle], axis=-1)
    return (jnp.cos(angle), jnp.sin(angle))


def norm_rope(value, gain, cosine, sine):
    inverse = lax.rsqrt(jnp.mean(value * value, axis=1, keepdims=True) + epsilon)
    value = value * inverse * gain
    return value * cosine + pltpu.roll(value, HD // 2, 1) * sine


def norm_rope_back(value, gain, cosine, sine, grad):
    inverse = lax.rsqrt(jnp.mean(value * value, axis=1, keepdims=True) + epsilon)
    grad = grad * cosine + pltpu.roll(grad * sine, HD // 2, 1)
    normal = value * inverse
    scaled = grad * gain
    inner = jnp.mean(scaled * normal, axis=1, keepdims=True)
    return inverse * (scaled - normal * inner), jnp.sum(grad * normal, axis=0, keepdims=True)


def kept_scores(query, keys, q_seg, k_seg, start):
    scores = dot(query, keys, ((1,), (1,))) * (1.0 / math.sqrt(HD))
    q_index = start + lax.broadcasted_iota(jnp.int32, scores.shape, 0)
    k_index = lax.broadcasted_iota(jnp.int32, scores.shape, 1)
    keep = (jnp.abs(q_index - k_index) <= HALF) & (q_seg == k_seg)
    return jnp.where(keep, scores, -1e30)


Q_BLOCK = 256


def forward_kernel(
    heads, proj, cosine, sine, seg_column, seg_row, gains, mixed, query, keys, values, lses
):
    length = proj.shape[1]
    k_seg = seg_row[0]
    for head in range(heads):
        at = slice(head * HD, (head + 1) * HD)
        raw_q = proj[0, :, head * HD : (head + 1) * HD]
        raw_k = proj[0, :, (heads + head) * HD : (heads + head + 1) * HD]
        raw_v = proj[0, :, (2 * heads + head) * HD : (2 * heads + head + 1) * HD]
        query[0, :, at] = norm_rope(raw_q, gains[0:1], cosine[0], sine[0]).astype(bf16)
        keys[0, :, at] = norm_rope(raw_k, gains[1:2], cosine[0], sine[0]).astype(bf16)
        values[0, :, at] = raw_v.astype(bf16)

        @pl.loop(0, length // Q_BLOCK)
        def one_block(number, head=head, at=at):
            start = pl.multiple_of(number * Q_BLOCK, Q_BLOCK)
            rows = pl.ds(start, Q_BLOCK)
            scores = kept_scores(
                query[0, rows, at], keys[0, :, at], seg_column[0, rows], k_seg, start
            )
            top = jnp.max(scores, axis=1, keepdims=True)
            weights = jnp.exp(scores - top)
            total = jnp.sum(weights, axis=1, keepdims=True)
            lses[0, head, rows] = top + jnp.log(total)
            weights = (weights * (1.0 / total)).astype(bf16)
            mixed[0, rows, at] = dot(weights, values[0, :, at]).astype(bf16)


def backward_kernel(
    heads, proj, cosine, sine, seg_column, seg_row, gains, query, keys, values, lses, grad_mixed,
    grad_proj, grad_gains, grad_q, grad_k, grad_v,
):
    length = proj.shape[1]
    k_seg = seg_row[0]
    scale = 1.0 / math.sqrt(HD)
    sum_q = jnp.zeros((1, HD), f32)
    sum_k = jnp.zeros((1, HD), f32)
    for head in range(heads):
        at = slice(head * HD, (head + 1) * HD)
        grad_k[...] = jnp.zeros_like(grad_k)
        grad_v[...] = jnp.zeros_like(grad_v)

        @pl.loop(0, length // Q_BLOCK)
        def one_block(number, head=head, at=at):
            start = pl.multiple_of(number * Q_BLOCK, Q_BLOCK)
            rows = pl.ds(start, Q_BLOCK)
            q_rows = query[0, rows, at]
            g_rows = grad_mixed[0, rows, at]
            k_all = keys[0, :, at]
            scores = kept_scores(q_rows, k_all, seg_column[0, rows], k_seg, start)
            weights = jnp.exp(scores - lses[0, head, rows])
            grad_weights = dot(g_rows, values[0, :, at], ((1,), (1,)))
            delta = jnp.sum(weights * grad_weights, axis=1, keepdims=True)
            grad_scores = (weights * (grad_weights - delta)).astype(bf16)
            grad_q[rows] = dot(grad_scores, k_all) * scale
            grad_k[...] += dot(grad_scores, q_rows, ((0,), (0,)))
            grad_v[...] += dot(weights.astype(bf16), g_rows, ((0,), (0,)))

        def rounded(value):
            return value.astype(bf16).astype(f32)

        raw_q = proj[0, :, head * HD : (head + 1) * HD]
        raw_k = proj[0, :, (heads + head) * HD : (heads + head + 1) * HD]
        back_q, gain_q = norm_rope_back(
            raw_q, gains[0:1], cosine[0], sine[0], rounded(grad_q[...])
        )
        back_k, gain_k = norm_rope_back(
            raw_k, gains[1:2], cosine[0], sine[0], rounded(grad_k[...] * scale)
        )
        sum_q, sum_k = sum_q + gain_q, sum_k + gain_k
        grad_proj[0, :, at] = back_q.astype(bf16)
        grad_proj[0, :, (heads + head) * HD : (heads + head + 1) * HD] = back_k.astype(bf16)
        grad_proj[0, :, (2 * heads + head) * HD : (2 * heads + head + 1) * HD] = grad_v[
            ...
        ].astype(bf16)
    grad_gains[0, 0:1] = sum_q
    grad_gains[0, 1:2] = sum_k


def whole_spec(shape):
    return pl.BlockSpec((1,) + shape[1:], lambda i: (i,) + (0,) * (len(shape) - 1))


def batch_call(kernel, out_shape, scratch, args, shared):
    specs = [
        pl.BlockSpec(value.shape, lambda i, n=value.ndim: (0,) * n)
        if place in shared
        else whole_spec(value.shape)
        for place, value in enumerate(args)
    ]
    return pl.pallas_call(
        kernel,
        grid=(args[0].shape[0],),
        in_specs=specs,
        out_specs=[whole_spec(out.shape) for out in out_shape],
        out_shape=out_shape,
        scratch_shapes=scratch,
        compiler_params=pltpu.CompilerParams(vmem_limit_bytes=48 * 1024 * 1024),
    )(*args)


def attention_forward(proj, cosine, sine, seg_column, seg_row, gains):
    count, length, width = proj.shape
    width = width // 3
    heads = width // HD
    part = jax.ShapeDtypeStruct((count, length, width), bf16)
    lses = jax.ShapeDtypeStruct((count, heads, length, 1), f32)
    return batch_call(
        lambda *refs: forward_kernel(heads, *refs),
        [part, part, part, part, lses],
        [],
        (proj, cosine, sine, seg_column, seg_row, gains),
        (5,),
    )


def attention_backward(
    proj, cosine, sine, seg_column, seg_row, gains, query, keys, values, lses, grad_mixed
):
    count, length, width = proj.shape
    heads = width // 3 // HD
    return batch_call(
        lambda *refs: backward_kernel(heads, *refs),
        [
            jax.ShapeDtypeStruct((count, length, width), bf16),
            jax.ShapeDtypeStruct((count, 2, HD), f32),
        ],
        [pltpu.VMEM((length, HD), f32)] * 3,
        (proj, cosine, sine, seg_column, seg_row, gains, query, keys, values, lses, grad_mixed),
        (5,),
    )


def shift_rep(value, step):
    count = lax.axis_size("rep")
    return lax.ppermute(value, "rep", [(i, (i + step) % count) for i in range(count)])


def after(value, *others):
    return lax.optimization_barrier((value,) + others)[0]


def two_parts(value):
    high = lax.reduce_precision(value, 8, 7)
    return high.astype(bf16), (value - high).astype(bf16)


def shift_order(count):
    return sorted(range(1, count), key=lambda step: (-min(step, count - step), step))


def place_rep(pieces):
    count = len(pieces)
    rank = lax.axis_index("rep")
    rows = pieces[0].shape[0]
    full = jnp.zeros((count * rows,) + pieces[0].shape[1:], pieces[0].dtype)
    for step, piece in enumerate(pieces):
        full = lax.dynamic_update_slice_in_dim(full, piece, (rank - step) % count * rows, 0)
    return full


class Chain:
    def __init__(self, depth):
        self.depth = depth
        self.done = []

    def send(self, value, step):
        if len(self.done) >= self.depth:
            value = after(value, self.done[-self.depth])
        value = shift_rep(value, step)
        self.done.append(value)
        return value


def on_device(
    tokens, cotangent, w_qkv, w_o, w_router, norm_gains, qk_gain, w_in, w_out, segments, routes
):
    planes = lax.axis_size("rep")
    ranks = lax.axis_size("ep")
    plane = lax.axis_index("rep")
    rank = lax.axis_index("ep")
    share = w_in.shape[0]
    own = plane % share
    experts = share * ranks
    expert = rank * share + own
    micro = segments.shape[1]
    mine = tokens.shape[0]
    rows = mine // micro
    length = rows * ranks
    capacity = rows * TOP * 17 // (16 * experts)
    block = share * mine
    slots = -(-share * micro * capacity // 16) * 16
    width = HEADS // ranks * HD
    qk_gains = qk_gain.astype(f32).reshape(2, HD)
    dense_rows = w_qkv.shape[0]

    def exchange(value, step):
        pairs = [(i, i // share * share + (i % share + step) % share) for i in range(planes)]
        return lax.ppermute(value, "rep", pairs)

    def with_group(value):
        return jnp.stack([value] + [exchange(value, step) for step in range(1, share)])

    def gather_ranks(value):
        return lax.all_gather(value, "ep", axis=0)

    stream_all = gather_ranks(tokens)
    out_pieces = [w_o] + [shift_rep(w_o, step) for step in range(1, planes)]
    upstream_group = with_group(cotangent)
    slab = jnp.concatenate(
        [
            w_qkv.reshape(dense_rows, 3, ranks, width)
            .transpose(2, 0, 1, 3)
            .reshape(ranks, dense_rows, 3 * width),
            jnp.broadcast_to(
                jnp.concatenate(
                    [
                        w_router,
                        norm_gains.reshape(dense_rows, 2),
                        jnp.zeros((dense_rows, PAD - experts - 2), bf16),
                    ],
                    axis=1,
                )[None],
                (ranks, dense_rows, PAD),
            ),
        ],
        axis=2,
    )
    slab = lax.all_to_all(slab, "ep", split_axis=0, concat_axis=0, tiled=True)
    slab = slab.reshape(ranks * dense_rows, 3 * width + PAD)
    slab_pieces = [slab] + [shift_rep(slab, step) for step in range(1, planes)]
    slab = place_rep(slab_pieces)
    qkv_weight = slab[:, : 3 * width]
    router_weight = slab[:, 3 * width : 3 * width + experts]
    gain_pair = slab[:, 3 * width + experts : 3 * width + experts + 2].reshape(-1).astype(f32)
    first_gain = gain_pair[:D]
    second_gain = gain_pair[D:]
    out_weight = gather_ranks(after(place_rep(out_pieces), stream_all))
    out_weight = (
        out_weight.reshape(ranks, planes, -1, D).transpose(1, 0, 2, 3).reshape(D, D)
    )

    chain = Chain(2)
    gate = slab_pieces[-1]

    def collect(weight):
        pieces = [lax.dynamic_index_in_dim(weight, own, 0, keepdims=False)] + [None] * (planes - 1)
        for step in shift_order(planes):
            part = lax.dynamic_index_in_dim(weight, (own + step) % share, 0, keepdims=False)
            pieces[step] = chain.send(after(part, gate), step)
        return place_rep(pieces)

    in_weight = collect(w_in)
    out_expert = collect(w_out)

    def by_sequence(value):
        return value.reshape(ranks, micro, rows, -1).transpose(1, 0, 2, 3).reshape(
            micro, length, -1
        )

    stream = by_sequence(stream_all).astype(f32)
    inverse = inverse_rms(stream)
    normed = (stream * inverse * first_gain).astype(bf16)
    proj = dot(normed.reshape(micro * length, D), qkv_weight).reshape(micro, length, 3 * width)
    segment = segments[0]
    cosine, sine = jax.vmap(lambda one: rope_tables(doc_positions(one), HD))(segment)
    sine = jnp.where(jnp.arange(HD) < HD // 2, -sine, sine)
    seg_column = segment[:, :, None]
    seg_row = segment[:, None, :]
    tables = (cosine, sine, seg_column, seg_row, qk_gains)
    mixed_h, query, keys, values, lses = attention_forward(proj, *tables)
    mixed = lax.all_to_all(
        mixed_h.reshape(micro, ranks, rows, width), "ep", split_axis=1, concat_axis=3, tiled=True
    ).reshape(mine, D)
    own_stream = tokens.astype(f32)
    hidden = own_stream + dot(mixed, out_weight)
    second_inverse = inverse_rms(hidden)
    normed_two = (hidden * second_inverse * second_gain).astype(bf16)
    logits = dot(normed_two, router_weight)
    routed = jnp.any(routes[:, :, None] == jnp.arange(experts, dtype=jnp.int32), axis=1)
    logits = jnp.where(routed, logits, -1e30)
    gates = jnp.where(routed, jnp.exp(logits - jnp.max(logits, axis=1, keepdims=True)), 0.0)
    gates = gates / jnp.sum(gates, axis=1, keepdims=True)
    high, low = two_parts(gates)
    payload = jnp.concatenate(
        [normed_two, high, low, jnp.zeros((mine, PAD - 2 * experts), bf16)], axis=1
    )
    payload = gather_ranks(with_group(payload)).reshape(ranks, block, D + PAD)
    upstream_all = gather_ranks(after(upstream_group, payload)).reshape(ranks, block, D)

    order = jnp.arange(block, dtype=jnp.int32)
    earlier = (order[:, None] < order[None, :]).astype(bf16)
    taken = lax.dynamic_index_in_dim(payload, D + expert, 2, keepdims=False) > 0
    slot = dot(taken.astype(bf16), earlier).astype(jnp.int32)
    slot = jnp.where(taken, slot, -1)
    select = (slot[:, None, :] == jnp.arange(slots, dtype=jnp.int32)[None, :, None]).astype(bf16)

    def pick(value):
        value = jnp.einsum("bst,btd->bsd", select, value, preferred_element_type=f32)
        return value.astype(bf16).reshape(ranks * slots, -1)

    rows_all = pick(payload)
    upstream_rows = pick(upstream_all).astype(f32)
    rows_in = rows_all[:, :D]
    gate_rows = lax.dynamic_slice_in_dim(rows_all, D + expert, 1, 1).astype(
        f32
    ) + lax.dynamic_slice_in_dim(rows_all, D + experts + expert, 1, 1).astype(f32)
    both = dot(rows_in, in_weight)
    gate_part = both[:, :FF]
    up_part = both[:, FF:]
    sigma = 1.0 / (1.0 + jnp.exp(-gate_part))
    silu_part = gate_part / (1.0 + jnp.exp(-gate_part))
    active = (silu_part * up_part).astype(bf16)
    grad_produced = (gate_rows * upstream_rows).astype(bf16)
    grad_out_expert = dot(active, grad_produced, ((0,), (0,)))
    produced = dot(active, out_expert).astype(bf16).astype(f32)
    grad_gate_rows = jnp.sum(upstream_rows * produced, axis=1, keepdims=True)
    weighted = (gate_rows * produced).astype(bf16)
    grad_active = dot(grad_produced, out_expert, ((1,), (1,))).astype(bf16)
    grad_gate = grad_active * up_part * (sigma + gate_part * sigma * (1.0 - sigma))
    grad_up = grad_active * silu_part
    grad_both = jnp.concatenate([grad_gate, grad_up], axis=1).astype(bf16)
    grad_rows_in = dot(grad_both, in_weight, ((1,), (1,))).astype(bf16)
    grad_in_expert = dot(rows_in, grad_both, ((0,), (0,)))
    high, low = two_parts(grad_gate_rows)
    columns = jnp.arange(PAD, dtype=jnp.int32)[None, :]
    zero = jnp.zeros((), bf16)
    extra = jnp.where(columns == expert, high, jnp.where(columns == experts + expert, low, zero))
    grad_rows_in = jnp.concatenate([grad_rows_in, extra], axis=1)

    select_parts = select.reshape(ranks, slots, share, micro, rows)

    def spread(step, value):
        value = jnp.einsum(
            "bskt,bsd->bktd",
            select_parts[:, :, :, step],
            value.reshape(ranks, slots, -1),
            preferred_element_type=f32,
        ).astype(bf16)
        return lax.psum_scatter(value, "ep", scatter_dimension=0)

    def join(parts):
        total = parts[0].astype(f32)
        for step in range(1, share):
            total = total + exchange(parts[step], share - step).astype(f32)
        return total

    chain = Chain(2)

    def scatter_rep(value):
        count = value.shape[0] // planes
        sums = [None] * share
        for step in [0] + shift_order(planes):
            part = lax.dynamic_slice_in_dim(value, (plane + step) % planes * count, count, 0)
            if step:
                part = chain.send(part.astype(bf16), step).astype(f32)
            sums[step % share] = part if sums[step % share] is None else sums[step % share] + part
        return jnp.stack(
            [
                sum(jnp.where((own - step) % share == j, sums[step], 0.0) for step in range(share))
                for j in range(share)
            ]
        )

    grad_w_out = scatter_rep(grad_out_expert)
    grad_w_in = scatter_rep(grad_in_expert)

    spread_back = [spread(step, grad_rows_in) for step in range(micro)]
    grad_inputs, branches = [], []
    router_sum = gain_two_sum = gain_one_sum = qk_sum = qkv_sum = 0.0
    for step in range(micro):
        at = slice(step * rows, (step + 1) * rows)
        upstream = cotangent[at].astype(f32)
        returned = join(spread_back[step])
        grad_gates = returned[:, D : D + experts] + returned[:, D + experts : D + 2 * experts]
        grad_logits = gates[at] * (
            grad_gates - jnp.sum(gates[at] * grad_gates, axis=1, keepdims=True)
        )
        grad_logits = grad_logits.astype(bf16)
        grad_normed_two = returned[:, :D] + dot(grad_logits, router_weight, ((1,), (1,)))
        router_sum = router_sum + dot(normed_two[at], grad_logits, ((0,), (0,)))
        gain_two_sum = gain_two_sum + jnp.sum(
            grad_normed_two * hidden[at] * second_inverse[at], axis=0
        )
        grad_hidden = upstream + rms_backward(
            hidden[at], second_inverse[at], second_gain, grad_normed_two
        )
        grad_branch = grad_hidden.astype(bf16)
        branches.append(grad_branch)
        grad_mixed = dot(grad_branch, out_weight, ((1,), (1,))).astype(bf16)
        grad_mixed_h = lax.all_to_all(grad_mixed, "ep", split_axis=1, concat_axis=0, tiled=True)
        one = slice(step, step + 1)
        grad_proj, grad_qk = attention_backward(
            proj[one],
            *(table[one] for table in tables[:4]),
            qk_gains,
            query[one], keys[one], values[one], lses[one], grad_mixed_h[None],
        )
        grad_proj = grad_proj[0]
        qk_sum = qk_sum + grad_qk.reshape(-1)
        qkv_sum = qkv_sum + dot(normed[step], grad_proj, ((0,), (0,)))
        grad_normed = dot(grad_proj, qkv_weight, ((1,), (1,)))
        gain_one_sum = gain_one_sum + jnp.sum(grad_normed * stream[step] * inverse[step], axis=0)
        grad_normed = lax.psum_scatter(
            grad_normed.astype(bf16), "ep", scatter_dimension=0, tiled=True
        ).astype(f32)
        own_inverse = inverse_rms(own_stream[at])
        grad_inputs.append(
            grad_hidden + rms_backward(own_stream[at], own_inverse, first_gain, grad_normed)
        )
    mixture = [join(spread(step, weighted)) for step in range(micro)]
    output = (hidden + jnp.concatenate(mixture, axis=0)).astype(bf16)
    out_sum = dot(mixed, jnp.concatenate(branches, axis=0), ((0,), (0,))).astype(bf16)
    out_sum = out_sum.reshape(planes, ranks, dense_rows, D).transpose(1, 0, 2, 3)
    out_sum = lax.psum_scatter(out_sum, "ep", scatter_dimension=0)
    grad_w_o = lax.dynamic_index_in_dim(out_sum, plane, 0, keepdims=False).astype(f32)
    for step in range(1, planes):
        part = lax.dynamic_index_in_dim(out_sum, (plane + step) % planes, 0, keepdims=False)
        grad_w_o = grad_w_o + shift_rep(part, step).astype(f32)

    qk_columns = qk_sum.shape[0] // dense_rows
    small = jnp.concatenate(
        [
            router_sum,
            jnp.concatenate([gain_one_sum, gain_two_sum]).reshape(D, 2),
            jnp.tile(qk_sum.reshape(dense_rows, qk_columns), (planes * ranks, 1)),
        ],
        axis=1,
    )
    count = small.shape[1]

    def pack(main, small):
        high, low = two_parts(small)
        blank = jnp.zeros((small.shape[0], PAD - 2 * count), bf16)
        return jnp.concatenate([main.astype(bf16), high, low, blank], axis=1)

    def unpack(packed):
        packed = packed.astype(f32)
        split = packed.shape[-1] - PAD
        tail = packed[..., split:]
        return packed[..., :split], tail[..., :count] + tail[..., count : 2 * count]

    packed = pack(qkv_sum, small)
    part_rows = D // planes
    main = lax.dynamic_slice_in_dim(qkv_sum, plane * part_rows, part_rows, 0)
    small = lax.dynamic_slice_in_dim(small, plane * part_rows, part_rows, 0)
    for step in range(1, planes):
        part = lax.dynamic_slice_in_dim(
            packed, (plane + step) % planes * part_rows, part_rows, 0
        )
        part_main, part_small = unpack(shift_rep(part, step))
        main, small = main + part_main, small + part_small
    packed = pack(main, small).reshape(ranks, dense_rows, -1)
    packed = lax.all_to_all(packed, "ep", split_axis=0, concat_axis=0, tiled=True)
    main, small = unpack(packed)
    grad_w_qkv = (
        main.reshape(ranks, dense_rows, 3, width).transpose(1, 2, 0, 3).reshape(dense_rows, 3 * D)
    )
    small = jnp.sum(small, axis=0)
    return (
        output,
        jnp.concatenate(grad_inputs, axis=0),
        grad_w_qkv,
        grad_w_o,
        small[:, :experts],
        small[:, experts : experts + 2].reshape(-1),
        small[:, experts + 2 :].reshape(-1),
        grad_w_in,
        grad_w_out,
    )


def solution(mesh):
    placed = (
        P(("rep", "ep"), None),
        P(("rep", "ep"), None),
        P(("rep", "ep"), None),
        P(("rep", "ep"), None),
        P(("rep", "ep"), None),
        P(("rep", "ep")),
        P(),
        P("ep", "rep", None),
        P("ep", "rep", None),
        P("rep", None, None),
        P(("rep", "ep"), None),
    )
    return jax.shard_map(
        on_device,
        mesh=mesh,
        in_specs=placed,
        out_specs=(
            P(("rep", "ep"), None),
            P(("rep", "ep"), None),
            P(("rep", "ep"), None),
            P(("rep", "ep"), None),
            P(("rep", "ep"), None),
            P(("rep", "ep")),
            P(),
            P("ep", "rep", None),
            P("ep", "rep", None),
        ),
        check_vma=False,
    )
```

time: 2330 us -> 1660 us (0.71)
  waiting for transfers between devices: 1220 us -> 929 us
  matrix products: 446 us -> 269 us
  blocking collectives: 169 us -> 0 us
  Pallas kernels: 0 us -> 54.7 us
  local copies, waits for them, and re-layouts: 220 us -> 180 us
    ppermute x0 -> x30, waiting for transfers between devices: none -> 669 us  [the longest x24 616 us: shift_rep(): lax.ppermute(value, 'rep', [(i, (i + step) % count) for i in range(count)])]
    reduce_scatter x4 -> x7, waiting for transfers between devices: 692 us -> 94 us  [the longest x4 94 us: spread(): return lax.psum_scatter(value, 'ep', scatter_dimension=0)]
    all_to_all x24 -> x5, waiting for transfers between devices: 246 us -> 62.4 us  [the longest x1 19.5 us: on_device(): slab = lax.all_to_all(slab, 'ep', split_axis=0, concat_axis=0, tiled=True)]
    dot_general x62 -> x27, matrix products: 446 us -> 269 us  [the longest x21 198 us: dot(): return lax.dot_general(a, b, (dims, ((), ())), preferred_element_type=f32)]
    all_gather x4, waiting for transfers between devices: 277 us -> 103 us  [gather_ranks(): return lax.all_gather(value, 'ep', axis=0)]
    all_gather x2 -> x0, blocking collectives: 126 us -> none  [the longest x1 82.3 us: on_device(): lax.all_gather(w_router, ('rep', 'ep'), axis=0, tiled=True)]
    all_to_all x24 -> x5, starting transfers between devices: 99.4 us -> 18.2 us  [the longest x2 6.99 us: on_device(): lax.all_to_all(grad_mixed, 'ep', split_axis=1, concat_axis=0, tiled=True)]
    ppermute x0 -> x30, starting transfers between devices: none -> 62.7 us  [the longest x24 35.8 us: shift_rep(): lax.ppermute(value, 'rep', [(i, (i + step) % count) for i in range(count)])]
  transfers between devices with their start and end apart: 33 -> 46, of which waited for: 24 -> 30; matrix products, arithmetic and copies ran while one was open for 30% -> 23% of each run, Pallas kernels for 0% -> 3%
where the time goes in v1:
time: 1660 us; the launch traced here: 1650 us
  waiting for transfers between devices  929 us (56%)
  matrix products  269 us (16%)
  local copies, waits for them, and re-layouts  180 us (11%)
  other arithmetic  121 us (7%)
  starting transfers between devices  81.4 us (5%)
  Pallas kernels  54.7 us (3%)
    ppermute x24, waiting for transfers between devices, shift_rep(): lax.ppermute(value, 'rep', [(i, (i + step) % count) for i in range(count)])  616 us
    dot_general x21, matrix products, dot(): return lax.dot_general(a, b, (dims, ((), ())), preferred_element_type=f32)  198 us
    all_gather x4, waiting for transfers between devices, gather_ranks(): return lax.all_gather(value, 'ep', axis=0)  103 us
    reduce_scatter x4, waiting for transfers between devices, spread(): return lax.psum_scatter(value, 'ep', scatter_dimension=0)  94 us
    pallas_call x3, Pallas kernels, batch_call(): pl.pallas_call(kernel, grid=(args[0].shape[0],), in_specs=specs, out_spec...  54.7 us
    ppermute x6, waiting for transfers between devices, exchange(): return lax.ppermute(value, 'rep', pairs)  53.3 us
    dot_general x4, matrix products, spread(): jnp.einsum('bskt,bsd->bktd', select_parts[:, :, :, step], value.reshape(r...  45.7 us
    ppermute x24, starting transfers between devices, shift_rep(): lax.ppermute(value, 'rep', [(i, (i + step) % count) for i in range(count)])  35.8 us
  transfers between devices with their start and end apart: 46, of which 30 were waited for; matrix products, arithmetic and copies ran while one was open for 23% of the time, Pallas kernels for 3%

profile of v1, /device:TPU:0, one launch (start us, length us, event | category | flops | bytes accessed | tf_op | source)
XLA Modules:
  0.0 1650.5 jit_solution(7075789897700171217)
XLA Ops:
  36.5 30.5 %all-gather.9.cloned.1.call-done = bf16[2048,2048]{1,0:T(8,128)(2,1)} async-done(((bf16[256,2048]{1,0:T(8,128)(2,1)}), bf16[2048,2048]{1,0:T(8,128)(2,1)}) %all-gather.9.cloned.1.call-update) | async-done | bytes 8388624 | tf_op jit(solution)/shard_map/all_gather | solution.py:284
  75.0 19.5 %all-to-all-done = bf16[8,64,896]{2,1,0:T(8,128)(2,1)S(1)} async-done(((bf16[8,64,896]{2,1,0:T(8,128)(2,1)}), bf16[8,64,896]{2,1,0:T(8,128)(2,1)S(1)}, u32[]{:S(2)}, u32[]{:S(2)}) %all-to-all-start) | async-done | bytes 917536 | tf_op jit(solution)/shard_map/all_to_all | solution.py:308
  107.9 31.6 %collective-permute-done = bf16[512,896]{1,0:T(8,128)(2,1)} collective-permute-done((bf16[512,896]{1,0:T(8,128)(2,1)S(1)}, bf16[512,896]{1,0:T(8,128)(2,1)}, u32[]{:S(2)}, u32[]{:S(2)}) %collective-permute-start) | collective-permute-done | bytes 917536 | tf_op jit(solution)/shard_map/ppermute | solution.py:215
  204.4 21.6 %shard_map.178 = (bf16[2,1024,256]{2,1,0:T(8,128)(2,1)S(1)}, bf16[2,1024,256]{2,1,0:T(8,128)(2,1)S(1)}, bf16[2,1024,256]{2,1,0:T(8,128)(2,1)S(1)}, bf16[2,1024,256]{2,1,0:T(8,128)(2,1)S(1)}, f32[2,2,1024,1]{3,2,1,0:T(8,128)}) custom-call(f32[2,1024,768]{2,1,0:T(8,128)} %bitcast.282, f32[2,1024,128]{2,1,0:T(8,128)S(1)} %get-tuple-element.149.refs_1_, ...), custom_call_target="tpu_custom_call" | custom-call | tf_op jit(solution)/shard_map/pallas_call | solution.py:170
  270.1 20.2 %collective-permute-start.6 = (bf16[256,2176]{1,0:T(8,128)(2,1)}, bf16[256,2176]{1,0:T(8,128)(2,1)S(1)}, u32[]{:S(2)}, u32[]{:S(2)}) collective-permute-start(bf16[256,2176]{1,0:T(8,128)(2,1)} %concatenate.48), channel_id=1, source_target_pairs={{0,8},{8,0},{16,24},{24,16},{1,9},{9,1},{17,25},{25,17},{2,10},{10... | collective-permute-start | bytes 3342344 | tf_op jit(solution)/shard_map/ppermute | solution.py:278
  290.3 22.0 %collective-permute-done.6 = bf16[256,2176]{1,0:T(8,128)(2,1)S(1)} collective-permute-done((bf16[256,2176]{1,0:T(8,128)(2,1)}, bf16[256,2176]{1,0:T(8,128)(2,1)S(1)}, u32[]{:S(2)}, u32[]{:S(2)}) %collective-permute-start.6) | collective-permute-done | bytes 1114144 | tf_op jit(solution)/shard_map/ppermute | solution.py:278
  317.0 19.9 %collective-permute-done.15 = bf16[256,2048]{1,0:T(8,128)(2,1)S(1)} collective-permute-done((bf16[256,2048]{1,0:T(8,128)(2,1)}, bf16[256,2048]{1,0:T(8,128)(2,1)S(1)}, u32[]{:S(2)}, u32[]{:S(2)}) %collective-permute-start.15) | collective-permute-done | bytes 1048608 | tf_op jit(solution)/shard_map/ppermute | solution.py:278
  339.7 72.4 %all-gather.13.cloned.1.call-done = bf16[16,256,2176]{2,1,0:T(8,128)(2,1)} async-done(((bf16[2,256,2176]{2,1,0:T(8,128)(2,1)}), bf16[16,256,2176]{2,1,0:T(8,128)(2,1)}) %all-gather.13.cloned.1.call-update) | async-done | bytes 17825808 | tf_op jit(solution)/shard_map/all_gather | solution.py:284
  412.1 24.2 %copy.165 = bf16[8,512,2176]{1,0,2:T(8,128)(2,1)} copy(bf16[8,512,2176]{2,1,0:T(8,128)(2,1)} %bitcast.270) | data formatting | bytes 35651584 | tf_op jit(solution)/shard_map/reshape | solution.py:367
  445.9 134.7 %collective-permute-done.8 = bf16[512,2048]{1,0:T(8,128)(2,1)S(1)} collective-permute-done((bf16[512,2048]{1,0:T(8,128)(2,1)S(1)}, bf16[512,2048]{1,0:T(8,128)(2,1)S(1)}, u32[]{:S(2)}, u32[]{:S(2)}) %collective-permute-start.8) | collective-permute-done | bytes 2097184 | tf_op jit(solution)/shard_map/ppermute | solution.py:215
  587.3 41.8 %collective-permute-done.9 = bf16[512,2048]{1,0:T(8,128)(2,1)} collective-permute-done((bf16[512,2048]{1,0:T(8,128)(2,1)}, bf16[512,2048]{1,0:T(8,128)(2,1)}, u32[]{:S(2)}, u32[]{:S(2)}) %collective-permute-start.9) | collective-permute-done | bytes 2097184 | tf_op jit(solution)/shard_map/ppermute | solution.py:215
  630.1 63.4 %collective-permute-done.11 = bf16[256,2048]{1,0:T(8,128)(2,1)S(1)} collective-permute-done((bf16[256,2048]{1,0:T(8,128)(2,1)}, bf16[256,2048]{1,0:T(8,128)(2,1)S(1)}, u32[]{:S(2)}, u32[]{:S(2)}) %collective-permute-start.11) | collective-permute-done | bytes 1048608 | tf_op jit(solution)/shard_map/ppermute | solution.py:215
  696.0 20.9 %collective-permute-done.12 = bf16[256,2048]{1,0:T(8,128)(2,1)S(1)} collective-permute-done((bf16[256,2048]{1,0:T(8,128)(2,1)S(1)}, bf16[256,2048]{1,0:T(8,128)(2,1)S(1)}, u32[]{:S(2)}, u32[]{:S(2)}) %collective-permute-start.12) | collective-permute-done | bytes 1048608 | tf_op jit(solution)/shard_map/ppermute | solution.py:215
  737.2 26.7 %fusion.17 = f32[2176,2048]{0,1:T(8,128)} fusion(bf16[2048,2048]{1,0:T(8,128)(2,1)} %copy-done.30, bf16[2176,2176]{1,0:T(8,128)(2,1)} %bitcast.285), kind=kOutput, calls=%fused_computation.38 | convolution fusion | flops 18253611008 | bytes 35127296 | tf_op jit(solution)/shard_map/dot_general | solution.py:25
  785.5 23.5 %fusion.8 = (bf16[2176,1024]{0,1:T(8,128)(2,1)}, bf16[2176,1024]{0,1:T(8,128)(2,1)}, bf16[2176,1024]{0,1:T(8,128)(2,1)}) fusion(f32[2176,2048]{0,1:T(8,128)} %fusion.17, bf16[2176,2048]{1,0:T(8,128)(2,1)} %fusion.1, bf16[1024,2048]{1,0:T(8,128)(2,1)} %copy-done.45), kind=kOutput, calls=%fused_computation.19 | convolution fusion | flops 9164685312 | bytes 44302336 | tf_op jit(solution)/shard_map/dot_general | solution.py:25
  826.5 23.1 %convolution_convert_fusion = bf16[2176,2048]{0,1:T(8,128)(2,1)S(1)} fusion(bf16[2048,2048]{1,0:T(8,128)(2,1)} %copy-done.30, bf16[2176,1024]{0,1:T(8,128)(2,1)} %get-tuple-element.98, bf16[2176,1024]{0,1:T(8,128)(2,1)S(1)} %copy-done.97), kind=kOutput, calls=%fused_computation.13 | convolution fusion | flops 18275893248 | bytes 26214400 | tf_op jit(solution)/shard_map/dot_general | solution.py:25
  935.6 20.1 %reduce-scatter.12.cloned.1.call-done = bf16[1,2,128,2176]{3,2,1,0:T(8,128)(2,1)} async-done(((bf16[8,2,128,2176]{3,2,1,0:T(8,128)(2,1)}), bf16[1,2,128,2176]{3,2,1,0:T(8,128)(2,1)}) %reduce-scatter.12.cloned.1.call-update) | async-done | bytes 1114128 | tf_op jit(solution)/shard_map/reduce_scatter | solution.py:419
  959.1 73.9 %reduce-scatter.16.cloned.1.call-done = bf16[1,2,128,2176]{3,2,1,0:T(8,128)(2,1)} async-done(((bf16[8,2,128,2176]{3,2,1,0:T(8,128)(2,1)}), bf16[1,2,128,2176]{3,2,1,0:T(8,128)(2,1)}) %reduce-scatter.16.cloned.1.call-update) | async-done | bytes 1114128 | tf_op jit(solution)/shard_map/reduce_scatter | solution.py:419
  1178.6 27.6 %fusion.15 = f32[2048,2048]{1,0:T(8,128)} fusion(bf16[2176,2176]{1,0:T(8,128)(2,1)} %bitcast.286, bf16[2176,1024]{0,1:T(8,128)(2,1)} %get-tuple-element.98, bf16[2176,1024]{0,1:T(8,128)(2,1)} %get-tuple-element.97), kind=kOutput, calls=%fused_computation.36 | convolution fusion | flops 18271436800 | bytes 34603008 | tf_op jit(solution)/shard_map/dot_general | solution.py:25
  1216.9 81.3 %collective-permute-done.26 = bf16[256,2048]{1,0:T(8,128)(2,1)S(1)} collective-permute-done((bf16[256,2048]{1,0:T(8,128)(2,1)S(1)}, bf16[256,2048]{1,0:T(8,128)(2,1)S(1)}, u32[]{:S(2)}, u32[]{:S(2)}) %collective-permute-start.26) | collective-permute-done | bytes 1048608 | tf_op jit(solution)/shard_map/ppermute | solution.py:215
  1314.6 50.0 %collective-permute-done.27 = bf16[256,2048]{1,0:T(8,128)(2,1)} collective-permute-done((bf16[256,2048]{1,0:T(8,128)(2,1)}, bf16[256,2048]{1,0:T(8,128)(2,1)}, u32[]{:S(2)}, u32[]{:S(2)}) %collective-permute-start.27) | collective-permute-done | bytes 1048608 | tf_op jit(solution)/shard_map/ppermute | solution.py:215
  1385.3 30.0 %collective-permute-done.28 = bf16[512,2048]{1,0:T(8,128)(2,1)} collective-permute-done((bf16[512,2048]{1,0:T(8,128)(2,1)}, bf16[512,2048]{1,0:T(8,128)(2,1)}, u32[]{:S(2)}, u32[]{:S(2)}) %collective-permute-start.28) | collective-permute-done | bytes 2097184 | tf_op jit(solution)/shard_map/ppermute | solution.py:215
  1415.3 42.2 %collective-permute-done.29 = bf16[512,2048]{1,0:T(8,128)(2,1)} collective-permute-done((bf16[512,2048]{1,0:T(8,128)(2,1)}, bf16[512,2048]{1,0:T(8,128)(2,1)}, u32[]{:S(2)}, u32[]{:S(2)}) %collective-permute-start.29) | collective-permute-done | bytes 2097184 | tf_op jit(solution)/shard_map/ppermute | solution.py:215
  1537.4 37.7 %collective-permute-done.19 = bf16[512,896]{0,1:T(8,128)(2,1)} collective-permute-done((bf16[512,896]{0,1:T(8,128)(2,1)S(1)}, bf16[512,896]{0,1:T(8,128)(2,1)}, u32[]{:S(2)}, u32[]{:S(2)}) %collective-permute-start.19) | collective-permute-done | bytes 917536 | tf_op jit(solution)/shard_map/ppermute | solution.py:215
  (473 shorter events, 675.8 us)
Async XLA Ops:
  7.2 59.8 %all-gather.9.cloned.1.call-start = ((), (), s32[]{:S(2)}) async-start(), calls=%async_computation.19 | async-start | bytes 9437184 | tf_op jit(solution)/shard_map/all_gather | solution.py:284
  7.9 241.0 %all-gather.11.cloned.1.call-start = ((), (), s32[]{:S(2)}) async-start(), calls=%async_computation.20 | async-start | bytes 9437184 | tf_op jit(solution)/shard_map/all_gather | solution.py:284
  94.5 59.8 %collective-permute-start.1 = (bf16[512,896]{1,0:T(8,128)(2,1)S(1)}, bf16[512,896]{1,0:T(8,128)(2,1)}, u32[]{:S(2)}, u32[]{:S(2)}) collective-permute-start(bf16[512,896]{1,0:T(8,128)(2,1)S(1)} %bitcast.298), channel_id=1, source_target_pairs={{0,16},{8,24},{16,0},{24,8},{1,17},{9,25},{17,1},{25,9},{2,18},{10... | collective-permute-start | bytes 2752520 | tf_op jit(solution)/shard_map/ppermute | solution.py:215
  98.7 56.9 %collective-permute-start.2 = (bf16[512,896]{1,0:T(8,128)(2,1)S(1)}, bf16[512,896]{1,0:T(8,128)(2,1)}, u32[]{:S(2)}, u32[]{:S(2)}) collective-permute-start(bf16[512,896]{1,0:T(8,128)(2,1)S(1)} %bitcast.300), channel_id=1, source_target_pairs={{0,24},{8,0},{16,8},{24,16},{1,25},{9,1},{17,9},{25,17},{2,26},{10... | collective-permute-start | bytes 2752520 | tf_op jit(solution)/shard_map/ppermute | solution.py:215
  232.7 179.5 %all-gather.13.cloned.1.call-start = ((), (), s32[]{:S(2)}) async-start(), calls=%async_computation.21 | async-start | bytes 20054016 | tf_op jit(solution)/shard_map/all_gather | solution.py:284
  315.2 448.8 %all-gather.15.cloned.1.call-start = ((), (), s32[]{:S(2)}) async-start(), calls=%async_computation.22 | async-start | bytes 18874368 | tf_op jit(solution)/shard_map/all_gather | solution.py:284
  436.4 519.3 %reduce-scatter.12.cloned.1.call-start = ((), (), s32[]{:S(2)}) async-start(), calls=%async_computation.14 | async-start | bytes 10027008 | tf_op jit(solution)/shard_map/reduce_scatter | solution.py:419
  442.0 138.6 %collective-permute-start.8 = (bf16[512,2048]{1,0:T(8,128)(2,1)S(1)}, bf16[512,2048]{1,0:T(8,128)(2,1)S(1)}, u32[]{:S(2)}, u32[]{:S(2)}) collective-permute-start(bf16[512,2048]{1,0:T(8,128)(2,1)S(1)} %get-tuple-element.37), channel_id=1, source_target_pairs={{0,16},{8,24},{16,0},{24,8},{1,17},{9,25},{17,1},{25,9},{2,18},{10... | collective-permute-start | bytes 6291464 | tf_op jit(solution)/shard_map/ppermute | solution.py:215
  444.4 138.1 %collective-permute-start.7 = (bf16[512,2048]{1,0:T(8,128)(2,1)S(1)}, bf16[512,2048]{1,0:T(8,128)(2,1)S(1)}, u32[]{:S(2)}, u32[]{:S(2)}) collective-permute-start(bf16[512,2048]{1,0:T(8,128)(2,1)S(1)} %get-tuple-element.36), channel_id=1, source_target_pairs={{0,8},{8,16},{16,24},{24,0},{1,9},{9,17},{17,25},{25,1},{2,10},{10... | collective-permute-start | bytes 6291464 | tf_op jit(solution)/shard_map/ppermute | solution.py:215
  584.2 109.4 %collective-permute-start.11 = (bf16[256,2048]{1,0:T(8,128)(2,1)}, bf16[256,2048]{1,0:T(8,128)(2,1)S(1)}, u32[]{:S(2)}, u32[]{:S(2)}) collective-permute-start(bf16[256,2048]{1,0:T(8,128)(2,1)} %get-tuple-element.43), channel_id=1, source_target_pairs={{0,16},{8,24},{16,0},{24,8},{1,17},{9,25},{17,1},{25,9},{2,18},{10... | collective-permute-start | bytes 3145736 | tf_op jit(solution)/shard_map/ppermute | solution.py:215
  629.1 66.6 %collective-permute-start.10 = (bf16[256,2048]{1,0:T(8,128)(2,1)S(1)}, bf16[256,2048]{1,0:T(8,128)(2,1)S(1)}, u32[]{:S(2)}, u32[]{:S(2)}) collective-permute-start(bf16[256,2048]{1,0:T(8,128)(2,1)S(1)} %copy-done.58), channel_id=1, source_target_pairs={{0,8},{8,16},{16,24},{24,0},{1,9},{9,17},{17,25},{25,1},{2,10},{10... | collective-permute-start | bytes 3145736 | tf_op jit(solution)/shard_map/ppermute | solution.py:215
  882.8 150.2 %reduce-scatter.16.cloned.1.call-start = ((), (), s32[]{:S(2)}) async-start(), calls=%async_computation.16 | async-start | bytes 10027008 | tf_op jit(solution)/shard_map/reduce_scatter | solution.py:419
  894.4 572.3 %reduce-scatter.8.cloned.1.call-start = ((), (), s32[]{:S(2)}) async-start(), calls=%async_computation.12 | async-start | bytes 9437184 | tf_op jit(solution)/shard_map/reduce_scatter | solution.py:419
  906.0 591.2 %reduce-scatter.10.cloned.1.call-start = ((), (), s32[]{:S(2)}) async-start(), calls=%async_computation.13 | async-start | bytes 9437184 | tf_op jit(solution)/shard_map/reduce_scatter | solution.py:419
  957.6 78.0 %collective-permute-start.16 = (bf16[128,2176]{1,0:T(8,128)(2,1)}, bf16[128,2176]{1,0:T(8,128)(2,1)}, u32[]{:S(2)}, u32[]{:S(2)}) collective-permute-start(bf16[128,2176]{1,0:T(8,128)(2,1)} %slice_bitcast_fusion.16), channel_id=1, source_target_pairs={{0,8},{8,0},{16,24},{24,16},{1,9},{9,1},{17,25},{25,17},{2,10},{10... | collective-permute-start | bytes 1671176 | tf_op jit(solution)/shard_map/ppermute | solution.py:278
  1063.4 547.4 %reduce-scatter.14.cloned.1.call-start = ((), (), s32[]{:S(2)}) async-start(), calls=%async_computation.15 | async-start | bytes 4718592 | tf_op jit(solution)/shard_map/reduce_scatter | solution.py:483
  1120.4 490.5 %reduce-scatter.18.cloned.1.call-start = ((), (), s32[]{:S(2)}) async-start(), calls=%async_computation.17 | async-start | bytes 4718592 | tf_op jit(solution)/shard_map/reduce_scatter | solution.py:483
  1158.1 460.4 %reduce-scatter.20.cloned.1.call-start = ((), (), s32[]{:S(2)}) async-start(), calls=%async_computation.18 | async-start | bytes 9437184 | tf_op jit(solution)/shard_map/reduce_scatter | solution.py:494
  1206.2 92.0 %collective-permute-start.26 = (bf16[256,2048]{1,0:T(8,128)(2,1)S(1)}, bf16[256,2048]{1,0:T(8,128)(2,1)S(1)}, u32[]{:S(2)}, u32[]{:S(2)}) collective-permute-start(bf16[256,2048]{1,0:T(8,128)(2,1)S(1)} %get-tuple-element.111), channel_id=1, source_target_pairs={{0,16},{8,24},{16,0},{24,8},{1,17},{9,25},{17,1},{25,9},{2,18},{10... | collective-permute-start | bytes 3145736 | tf_op jit(solution)/shard_map/ppermute | solution.py:215
  1216.3 149.0 %collective-permute-start.25 = (bf16[512,2048]{1,0:T(8,128)(2,1)}, bf16[512,2048]{1,0:T(8,128)(2,1)S(1)}, u32[]{:S(2)}, u32[]{:S(2)}) collective-permute-start(bf16[512,2048]{1,0:T(8,128)(2,1)} %get-tuple-element.55), channel_id=1, source_target_pairs={{0,16},{8,24},{16,0},{24,8},{1,17},{9,25},{17,1},{25,9},{2,18},{10... | collective-permute-start | bytes 6291464 | tf_op jit(solution)/shard_map/ppermute | solution.py:215
  1298.2 66.5 %collective-permute-start.27 = (bf16[256,2048]{1,0:T(8,128)(2,1)}, bf16[256,2048]{1,0:T(8,128)(2,1)}, u32[]{:S(2)}, u32[]{:S(2)}) collective-permute-start(bf16[256,2048]{1,0:T(8,128)(2,1)} %get-tuple-element.56), channel_id=1, source_target_pairs={{0,24},{8,0},{16,8},{24,16},{1,25},{9,1},{17,9},{25,17},{2,26},{10... | collective-permute-start | bytes 3145736 | tf_op jit(solution)/shard_map/ppermute | solution.py:215
  1365.3 92.2 %collective-permute-start.29 = (bf16[512,2048]{1,0:T(8,128)(2,1)}, bf16[512,2048]{1,0:T(8,128)(2,1)}, u32[]{:S(2)}, u32[]{:S(2)}) collective-permute-start(bf16[512,2048]{1,0:T(8,128)(2,1)} %get-tuple-element.58), channel_id=1, source_target_pairs={{0,24},{8,0},{16,8},{24,16},{1,25},{9,1},{17,9},{25,17},{2,26},{10... | collective-permute-start | bytes 6291464 | tf_op jit(solution)/shard_map/ppermute | solution.py:215
  1496.4 78.7 %collective-permute-start.19 = (bf16[512,896]{0,1:T(8,128)(2,1)S(1)}, bf16[512,896]{0,1:T(8,128)(2,1)}, u32[]{:S(2)}, u32[]{:S(2)}) collective-permute-start(bf16[512,896]{0,1:T(8,128)(2,1)S(1)} %get-tuple-element.125), channel_id=1, source_target_pairs={{0,16},{8,24},{16,0},{24,8},{1,17},{9,25},{17,1},{25,9},{2,18},{10... | collective-permute-start | bytes 2752520 | tf_op jit(solution)/shard_map/ppermute | solution.py:215
  1498.3 87.0 %collective-permute-start.14 = (bf16[128,2048]{1,0:T(8,128)(2,1)S(1)}, bf16[128,2048]{1,0:T(8,128)(2,1)}, u32[]{:S(2)}, u32[]{:S(2)}) collective-permute-start(bf16[128,2048]{1,0:T(8,128)(2,1)S(1)} %slice_bitcast_fusion.18), channel_id=1, source_target_pairs={{0,8},{8,0},{16,24},{24,16},{1,9},{9,1},{17,25},{25,17},{2,10},{10... | collective-permute-start | bytes 1572872 | tf_op jit(solution)/shard_map/ppermute | solution.py:278
  (122 other events, 2841.3 us)
Sparse Core Ops, SparseCore 0:
  9.9 57.0 all-gather.8
  69.5 60.5 all-gather.10
  315.3 96.8 all-gather.12
  436.5 89.8 all-gather.14
  883.0 72.7 reduce-scatter.11
  959.2 73.7 reduce-scatter.15
  1036.5 76.8 reduce-scatter.7
  1117.2 71.2 reduce-scatter.9
  1191.9 51.3 reduce-scatter.13
  1246.8 51.2 reduce-scatter.17
  1314.8 69.7 reduce-scatter.19

commit v2 on v1

v2 whole, which is shorter than its diff:
```python
import math

import jax
import jax.numpy as jnp
from jax import lax
from jax.experimental import pallas as pl
from jax.experimental.pallas import tpu as pltpu
from jax.sharding import PartitionSpec as P

D = 2048
HEADS = 16
HD = 128
FF = 1024
TOP = 8
HALF = 512
PAD = 128

epsilon = 1e-06
rope_base = 50000.0
bf16 = jnp.bfloat16
f32 = jnp.float32


def dot(a, b, dims=((1,), (0,))):
    return lax.dot_general(a, b, (dims, ((), ())), preferred_element_type=f32)


def inverse_rms(value):
    return lax.rsqrt(jnp.mean(value * value, axis=-1, keepdims=True) + epsilon)


def rms_backward(value, inverse, gain, grad):
    scaled = grad * gain
    inner = jnp.mean(scaled * value, axis=-1, keepdims=True)
    return inverse * (scaled - value * (inverse * inverse * inner))


def doc_positions(segment):
    index = jnp.arange(segment.shape[0], dtype=jnp.int32)
    change = jnp.concatenate([jnp.ones((1,), dtype=jnp.bool_), segment[1:] != segment[:-1]])
    start = lax.cummax(jnp.where(change, index, 0), axis=0)
    return index - start


def rope_tables(position, width):
    steps = jnp.arange(width // 2, dtype=f32) * (2.0 / width)
    rates = jnp.exp(-steps * math.log(rope_base))
    angle = position.astype(f32)[:, None] * rates[None, :]
    angle = jnp.concatenate([angle, angle], axis=-1)
    return (jnp.cos(angle), jnp.sin(angle))


def norm_rope(value, gain, cosine, sine):
    inverse = lax.rsqrt(jnp.mean(value * value, axis=1, keepdims=True) + epsilon)
    value = value * inverse * gain
    return value * cosine + pltpu.roll(value, HD // 2, 1) * sine


def norm_rope_back(value, gain, cosine, sine, grad):
    inverse = lax.rsqrt(jnp.mean(value * value, axis=1, keepdims=True) + epsilon)
    grad = grad * cosine + pltpu.roll(grad * sine, HD // 2, 1)
    normal = value * inverse
    scaled = grad * gain
    inner = jnp.mean(scaled * normal, axis=1, keepdims=True)
    return inverse * (scaled - normal * inner), jnp.sum(grad * normal, axis=0, keepdims=True)


def kept_scores(query, keys, q_seg, k_seg, start):
    scores = dot(query, keys, ((1,), (1,))) * (1.0 / math.sqrt(HD))
    q_index = start + lax.broadcasted_iota(jnp.int32, scores.shape, 0)
    k_index = lax.broadcasted_iota(jnp.int32, scores.shape, 1)
    keep = (jnp.abs(q_index - k_index) <= HALF) & (q_seg == k_seg)
    return jnp.where(keep, scores, -1e30)


BIG = 100 * 1024 * 1024 // 2


def forward_kernel(
    heads, proj, cosine, sine, seg_column, seg_row, gains, mixed, query, keys, values, lses
):
    ranks, _, rows, _ = proj.shape
    length = ranks * rows
    q_block = 2 * rows
    k_seg = seg_row[0]
    for head in range(heads):
        at = slice(head * HD, (head + 1) * HD)

        def raw(part):
            first = (part * heads + head) * HD
            return proj[:, 0, :, first : first + HD].reshape(length, HD)

        query[0, :, at] = norm_rope(raw(0), gains[0:1], cosine[0], sine[0]).astype(bf16)
        keys[0, :, at] = norm_rope(raw(1), gains[1:2], cosine[0], sine[0]).astype(bf16)
        values[0, :, at] = raw(2).astype(bf16)

        @pl.loop(0, length // q_block)
        def one_block(number, head=head, at=at):
            start = pl.multiple_of(number * q_block, q_block)
            here = pl.ds(start, q_block)
            scores = kept_scores(
                query[0, here, at], keys[0, :, at], seg_column[0, here], k_seg, start
            )
            top = jnp.max(scores, axis=1, keepdims=True)
            weights = jnp.exp(scores - top)
            total = jnp.sum(weights, axis=1, keepdims=True)
            lses[0, head, here] = top + jnp.log(total)
            weights = (weights * (1.0 / total)).astype(bf16)
            result = dot(weights, values[0, :, at]).astype(bf16)
            mixed[pl.ds(number * 2, 2), 0, :, at] = result.reshape(2, rows, HD)


def backward_kernel(
    heads, proj, cosine, sine, seg_column, seg_row, gains, query, keys, values, lses, grad_mixed,
    grad_proj, grad_gains, grad_q, grad_k, grad_v,
):
    ranks, _, rows, _ = proj.shape
    length = ranks * rows
    q_block = 2 * rows
    k_seg = seg_row[0]
    scale = 1.0 / math.sqrt(HD)
    sum_q = jnp.zeros((1, HD), f32)
    sum_k = jnp.zeros((1, HD), f32)
    for head in range(heads):
        at = slice(head * HD, (head + 1) * HD)
        grad_k[...] = jnp.zeros_like(grad_k)
        grad_v[...] = jnp.zeros_like(grad_v)

        @pl.loop(0, length // q_block)
        def one_block(number, head=head, at=at):
            start = pl.multiple_of(number * q_block, q_block)
            here = pl.ds(start, q_block)
            q_rows = query[0, here, at]
            g_rows = grad_mixed[here, at]
            k_all = keys[0, :, at]
            scores = kept_scores(q_rows, k_all, seg_column[0, here], k_seg, start)
            weights = jnp.exp(scores - lses[0, head, here])
            grad_weights = dot(g_rows, values[0, :, at], ((1,), (1,)))
            delta = jnp.sum(weights * grad_weights, axis=1, keepdims=True)
            grad_scores = (weights * (grad_weights - delta)).astype(bf16)
            grad_q[here] = dot(grad_scores, k_all) * scale
            grad_k[...] += dot(grad_scores, q_rows, ((0,), (0,)))
            grad_v[...] += dot(weights.astype(bf16), g_rows, ((0,), (0,)))

        def rounded(value):
            return value.astype(bf16).astype(f32)

        def raw(part):
            first = (part * heads + head) * HD
            return proj[:, 0, :, first : first + HD].reshape(length, HD)

        def put(part, value):
            first = (part * heads + head) * HD
            grad_proj[:, :, first : first + HD] = value.astype(bf16).reshape(ranks, rows, HD)

        back_q, gain_q = norm_rope_back(
            raw(0), gains[0:1], cosine[0], sine[0], rounded(grad_q[...])
        )
        back_k, gain_k = norm_rope_back(
            raw(1), gains[1:2], cosine[0], sine[0], rounded(grad_k[...] * scale)
        )
        sum_q, sum_k = sum_q + gain_q, sum_k + gain_k
        put(0, back_q)
        put(1, back_k)
        put(2, grad_v[...])
    grad_gains[0:1] = sum_q
    grad_gains[1:2] = sum_k


def fixed(shape):
    return pl.BlockSpec(shape, lambda *_: (0,) * len(shape), pipeline_mode=pl.Buffered(1))


def leading(shape):
    return pl.BlockSpec((1,) + shape[1:], lambda i: (i,) + (0,) * (len(shape) - 1))


def params():
    return pltpu.CompilerParams(vmem_limit_bytes=BIG)


def out(shape, dtype=bf16):
    return jax.ShapeDtypeStruct(shape, dtype)


def attention_forward(proj, cosine, sine, seg_column, seg_row, gains):
    ranks, micro, rows, width = proj.shape
    length = ranks * rows
    width = width // 3
    heads = width // HD
    part = out((micro, length, width))
    by_rank = lambda n: pl.BlockSpec((ranks, 1, rows, n), lambda i: (0, i, 0, 0))
    lses = out((micro, heads, length, 1), f32)
    return pl.pallas_call(
        lambda *refs: forward_kernel(heads, *refs),
        grid=(micro,),
        in_specs=[by_rank(3 * width)]
        + [leading(v.shape) for v in (cosine, sine, seg_column, seg_row)]
        + [fixed(gains.shape)],
        out_specs=[by_rank(width)] + [leading(part.shape)] * 3 + [leading(lses.shape)],
        out_shape=[out((ranks, micro, rows, width)), part, part, part, lses],
        compiler_params=params(),
    )(proj, cosine, sine, seg_column, seg_row, gains)


def attention_backward(
    step, proj, cosine, sine, seg_column, seg_row, gains, query, keys, values, lses, grad_mixed
):
    ranks, micro, rows, width = proj.shape
    length = ranks * rows
    heads = width // 3 // HD

    def part(value):
        return pl.BlockSpec((1,) + value.shape[1:], lambda i: (step,) + (0,) * (value.ndim - 1))

    return pl.pallas_call(
        lambda *refs: backward_kernel(heads, *refs),
        grid=(1,),
        in_specs=[pl.BlockSpec((ranks, 1, rows, width), lambda i: (0, step, 0, 0))]
        + [part(v) for v in (cosine, sine, seg_column, seg_row)]
        + [fixed(gains.shape)]
        + [part(v) for v in (query, keys, values, lses)]
        + [fixed(grad_mixed.shape)],
        out_specs=[fixed((ranks, rows, width)), fixed((2, HD))],
        out_shape=[out((ranks, rows, width)), out((2, HD), f32)],
        scratch_shapes=[pltpu.VMEM((length, HD), f32)] * 3,
        compiler_params=params(),
    )(
        proj, cosine, sine, seg_column, seg_row, gains, query, keys, values, lses, grad_mixed
    )


def project(tokens, gain, slab):
    ranks, count, _ = tokens.shape
    width = slab.shape[1] - PAD

    def kernel(value, gain, weight, normed, proj):
        value = value[0].astype(f32)
        result = (value * inverse_rms(value) * gain[...]).astype(bf16)
        normed[0] = result
        proj[0] = dot(result, weight[:, :width])

    return pl.pallas_call(
        kernel,
        grid=(ranks,),
        in_specs=[leading(tokens.shape), fixed((1, D)), fixed(slab.shape)],
        out_specs=[leading((ranks, count, D)), leading((ranks, count, width))],
        out_shape=[out((ranks, count, D)), out((ranks, count, width), f32)],
        compiler_params=params(),
    )(tokens, gain, slab)


TILE = 256


def tiles(count):
    return pl.loop(0, count // TILE)


def tile(number):
    return pl.ds(pl.multiple_of(number * TILE, TILE), TILE)


def route(mixed, tokens, out_weight, gain, router, routes, experts):
    count = tokens.shape[0]

    def kernel(mixed, tokens, out_weight, gain, router, routes, hidden, payload, gates):
        @tiles(D)
        def _(number):
            at = tile(number)
            hidden[:, at] = tokens[:, at].astype(f32) + dot(mixed[...], out_weight[:, at])

        value = hidden[...]
        normed = (value * inverse_rms(value) * gain[...]).astype(bf16)
        payload[:, :D] = normed
        logits = dot(normed, router[...])
        column = lax.broadcasted_iota(jnp.int32, logits.shape, 1)
        routed = column == routes[:, 0:1]
        for choice in range(1, TOP):
            routed = routed | (column == routes[:, choice : choice + 1])
        logits = jnp.where(routed, logits, -1e30)
        weights = jnp.exp(logits - jnp.max(logits, axis=1, keepdims=True))
        weights = jnp.where(routed, weights, 0.0)
        weights = weights / jnp.sum(weights, axis=1, keepdims=True)
        gates[...] = weights
        high = weights.astype(bf16).astype(f32)
        payload[:, D:] = (high + pltpu.roll(weights - high, experts, 1)).astype(bf16)

    return pl.pallas_call(
        kernel,
        out_shape=[out((count, D), f32), out((count, D + PAD)), out((count, PAD), f32)],
        compiler_params=params(),
    )(mixed, tokens, out_weight, gain, router, routes)


def lane(value, number):
    column = lax.broadcasted_iota(jnp.int32, value.shape, 1)
    return jnp.sum(jnp.where(column == number, value.astype(f32), 0.0), axis=1, keepdims=True)


def expert_forward(expert, payload, upstream, in_weight, slots, experts):
    ranks, share, micro, rows, _ = payload.shape
    block = 2 * share * rows

    def kernel(
        expert, payload, upstream, in_weight, rows_in, tail, both, active, grad_produced,
        up_rows, places,
    ):
        number = expert[0]
        value = payload[...].reshape(block, D + PAD)
        marks = value[:, D:]
        first = lax.broadcasted_iota(jnp.int32, (8, PAD), 1) == number
        taken = dot(first.astype(bf16), marks, ((1,), (1,))) > 0.0
        before = lax.broadcasted_iota(jnp.int32, (block, block), 0)
        behind = lax.broadcasted_iota(jnp.int32, (block, block), 1)
        slot = dot(taken.astype(bf16), (before < behind).astype(bf16))
        slot = jnp.where(taken, slot, -1.0)[0:1]
        place = lax.broadcasted_iota(jnp.int32, (slots, block), 0).astype(f32)
        select = (place == slot).astype(bf16)
        taken = lane(marks, number) > 0.0
        wide = jnp.broadcast_to(taken, (block, PAD))
        slot = dot((before > behind).astype(bf16), wide.astype(bf16))
        places[0, 0] = jnp.where(wide, slot, -1.0)
        rows_in[0, 0] = dot(select, value[:, :D]).astype(bf16)
        marks = dot(select, marks)
        tail[0, 0] = marks
        gate = lane(marks, number) + lane(marks, experts + number)

        @tiles(D)
        def _(number):
            at = tile(number)
            picked = dot(select, upstream[:, :, 0, :, at].reshape(block, TILE))
            up_rows[0, 0, :, at] = picked.astype(bf16)
            grad_produced[0, 0, :, at] = (gate * picked).astype(bf16)

        @tiles(FF)
        def _(number):
            at = tile(number)
            more = pl.ds(pl.multiple_of(FF + number * TILE, TILE), TILE)
            gate_part = dot(rows_in[0, 0], in_weight[:, at])
            up_part = dot(rows_in[0, 0], in_weight[:, more])
            both[0, 0, :, at] = gate_part
            both[0, 0, :, more] = up_part
            active[0, 0, :, at] = (
                gate_part / (1.0 + jnp.exp(-gate_part)) * up_part
            ).astype(bf16)

    def tokens_spec(width):
        return pl.BlockSpec((2, share, 1, rows, width), lambda m, b, _: (b, 0, m, 0, 0))

    shapes = [
        out((micro, ranks // 2, slots, D)),
        out((micro, ranks // 2, slots, PAD), f32),
        out((micro, ranks // 2, slots, 2 * FF), f32),
        out((micro, ranks // 2, slots, FF)),
        out((micro, ranks // 2, slots, D)),
        out((micro, ranks // 2, slots, D)),
        out((micro, ranks // 2, block, PAD), f32),
    ]
    return pl.pallas_call(
        kernel,
        grid_spec=pltpu.PrefetchScalarGridSpec(
            num_scalar_prefetch=1,
            grid=(micro, ranks // 2),
            in_specs=[tokens_spec(D + PAD), tokens_spec(D), fixed(in_weight.shape)],
            out_specs=[
                pl.BlockSpec((1, 1) + s.shape[2:], lambda m, b, _: (m, b, 0, 0)) for s in shapes
            ],
        ),
        out_shape=shapes,
        compiler_params=params(),
    )(expert, payload, upstream, in_weight)


def expert_backward(
    step, expert, tail, both, active, grad_produced, up_rows, places, in_weight, out_weight,
    share, rows, experts,
):
    pairs, slots = tail.shape[1:3]
    block = places.shape[2]

    def kernel(
        expert, tail, both, active, grad_produced, up_rows, places, in_weight, out_weight,
        mixture, grad_tokens, grad_both,
    ):
        number = expert[0]
        gate = lane(tail[0, 0], number) + lane(tail[0, 0], experts + number)
        place = lax.broadcasted_iota(jnp.int32, (block, slots), 1).astype(f32)
        select = (places[0, 0][:, 0:1] == place).astype(bf16)
        shape = (2, share, rows)

        def produce(number, grad_gate):
            at = tile(number)
            produced = dot(active[0, 0], out_weight[:, at]).astype(bf16).astype(f32)
            weighted = (gate * produced).astype(bf16)
            mixture[:, :, :, at] = dot(select, weighted).astype(bf16).reshape(shape + (TILE,))
            return grad_gate + jnp.sum(
                up_rows[0, 0, :, at].astype(f32) * produced, axis=1, keepdims=True
            )

        grad_gate = lax.fori_loop(0, D // TILE, produce, jnp.zeros((slots, 1), f32))

        @tiles(FF)
        def _(number):
            at = tile(number)
            more = pl.ds(pl.multiple_of(FF + number * TILE, TILE), TILE)
            grad_active = dot(grad_produced[0, 0], out_weight[at, :], ((1,), (1,)))
            grad_active = grad_active.astype(bf16).astype(f32)
            gate_part = both[0, 0, :, at]
            up_part = both[0, 0, :, more]
            sigma = 1.0 / (1.0 + jnp.exp(-gate_part))
            grad_both[0, :, at] = (
                grad_active * up_part * (sigma * (1.0 + gate_part * (1.0 - sigma)))
            ).astype(bf16)
            grad_both[0, :, more] = (grad_active * (gate_part * sigma)).astype(bf16)

        @tiles(D)
        def _(number):
            at = tile(number)
            grad_rows = dot(grad_both[0], in_weight[at, :], ((1,), (1,))).astype(bf16)
            grad_tokens[:, :, :, at] = dot(select, grad_rows).astype(bf16).reshape(shape + (TILE,))

        high = grad_gate.astype(bf16).astype(f32)
        column = lax.broadcasted_iota(jnp.int32, (slots, PAD), 1)
        extra = jnp.where(column == number, high, 0.0)
        extra = jnp.where(column == experts + number, grad_gate - high, extra)
        grad_tokens[:, :, :, D:] = (
            dot(select, extra.astype(bf16)).astype(bf16).reshape(shape + (PAD,))
        )

    def part(value):
        return pl.BlockSpec((1, 1) + value.shape[2:], lambda b, _: (step, b, 0, 0))

    def tokens_spec(width):
        return pl.BlockSpec((2, share, rows, width), lambda b, _: (b, 0, 0, 0))

    return pl.pallas_call(
        kernel,
        grid_spec=pltpu.PrefetchScalarGridSpec(
            num_scalar_prefetch=1,
            grid=(pairs,),
            in_specs=[part(v) for v in (tail, both, active, grad_produced, up_rows, places)]
            + [fixed(in_weight.shape), fixed(out_weight.shape)],
            out_specs=[
                tokens_spec(D),
                tokens_spec(D + PAD),
                pl.BlockSpec((1, slots, 2 * FF), lambda b, _: (b, 0, 0)),
            ],
        ),
        out_shape=[
            out((2 * pairs, share, rows, D)),
            out((2 * pairs, share, rows, D + PAD)),
            out((pairs, slots, 2 * FF)),
        ],
        compiler_params=params(),
    )(
        expert, tail, both, active, grad_produced, up_rows, places, in_weight, out_weight
    )


def hidden_backward(parts, hidden, gates, upstream, gain, router, out_weight, experts):
    count = hidden.shape[0]
    terms = len(parts)

    def kernel(*refs):
        parts = refs[:terms]
        hidden, gates, upstream, gain, router, out_weight = refs[terms : terms + 6]
        grad_hidden, grad_branch, grad_mixed, grad_logits, grad_gain = refs[terms + 6 :]
        returned = sum(part[...].astype(f32) for part in parts)
        tail = returned[:, D:]
        grad_gates = gates[...] * (tail + pltpu.roll(tail, PAD - experts, 1))
        logits = grad_gates - gates[...] * jnp.sum(grad_gates, axis=1, keepdims=True)
        logits = logits.astype(bf16)
        grad_logits[...] = logits
        grad_normed = returned[:, :D] + dot(logits, router[...], ((1,), (1,)))
        value = hidden[...]
        inverse = inverse_rms(value)
        grad_gain[...] = jnp.sum(grad_normed * value * inverse, axis=0, keepdims=True)
        grad = upstream[...].astype(f32) + rms_backward(value, inverse, gain[...], grad_normed)
        grad_hidden[...] = grad
        grad_branch[...] = grad.astype(bf16)

        @tiles(D)
        def _(number):
            at = tile(number)
            grad_mixed[:, at] = dot(grad_branch[...], out_weight[at, :], ((1,), (1,))).astype(bf16)

    return pl.pallas_call(
        kernel,
        out_shape=[
            out((count, D), f32), out((count, D)), out((count, D)), out((count, PAD)),
            out((1, D), f32),
        ],
        compiler_params=params(),
    )(*parts, hidden, gates, upstream, gain, router, out_weight)


def project_backward(step, grad_proj, tokens, slab):
    ranks, micro, rows, _ = tokens.shape
    width = slab.shape[1] - PAD

    def kernel(grad_proj, tokens, weight, grad_normed, grad_gain):
        value = tokens[0, 0].astype(f32)
        inverse = inverse_rms(value)
        grad = dot(grad_proj[0], weight[:, :width], ((1,), (1,)))
        grad_normed[...] = grad.astype(bf16)

        @pl.when(pl.program_id(0) == 0)
        def _():
            grad_gain[...] = jnp.zeros_like(grad_gain)

        grad_gain[...] += jnp.sum(grad * value * inverse, axis=0, keepdims=True)

    return pl.pallas_call(
        kernel,
        grid=(ranks,),
        in_specs=[
            leading(grad_proj.shape),
            pl.BlockSpec((1, 1, rows, D), lambda i: (i, step, 0, 0)),
            fixed(slab.shape),
        ],
        out_specs=[pl.BlockSpec((rows, D), lambda i: (i, 0)), fixed((1, D))],
        out_shape=[out((ranks * rows, D)), out((1, D), f32)],
        compiler_params=params(),
    )(grad_proj, tokens, slab)


def shift_rep(value, step):
    count = lax.axis_size("rep")
    return lax.ppermute(value, "rep", [(i, (i + step) % count) for i in range(count)])


def after(value, *others):
    return lax.optimization_barrier((value,) + others)[0]


def two_parts(value):
    high = lax.reduce_precision(value, 8, 7)
    return high.astype(bf16), (value - high).astype(bf16)


def shift_order(count):
    return sorted(range(1, count), key=lambda step: (min(step, count - step), step))


def place_rep(pieces):
    count = len(pieces)
    rank = lax.axis_index("rep")
    rows = pieces[0].shape[0]
    full = jnp.zeros((count * rows,) + pieces[0].shape[1:], pieces[0].dtype)
    for step, piece in enumerate(pieces):
        full = lax.dynamic_update_slice_in_dim(full, piece, (rank - step) % count * rows, 0)
    return full


def on_device(
    tokens, cotangent, w_qkv, w_o, w_router, norm_gains, qk_gain, w_in, w_out, segments, routes
):
    planes = lax.axis_size("rep")
    ranks = lax.axis_size("ep")
    plane = lax.axis_index("rep")
    rank = lax.axis_index("ep")
    share = w_in.shape[0]
    own = plane % share
    experts = share * ranks
    expert = (rank * share + own).astype(jnp.int32).reshape(1)
    micro = segments.shape[1]
    mine = tokens.shape[0]
    rows = mine // micro
    length = rows * ranks
    capacity = rows * TOP * 17 // (16 * experts)
    slots = -(-2 * share * capacity // 16) * 16
    width = HEADS // ranks * HD
    qk_gains = qk_gain.astype(f32).reshape(2, HD)
    dense_rows = w_qkv.shape[0]

    def exchange(value, step):
        pairs = [(i, i // share * share + (i % share + step) % share) for i in range(planes)]
        return lax.ppermute(value, "rep", pairs)

    def with_group(value):
        return jnp.stack([value] + [exchange(value, step) for step in range(1, share)])

    def gather_ranks(value):
        return lax.all_gather(value, "ep", axis=0)

    stream = gather_ranks(tokens)
    slab = jnp.concatenate(
        [
            w_qkv.reshape(dense_rows, 3, ranks, width)
            .transpose(2, 0, 1, 3)
            .reshape(ranks, dense_rows, 3 * width),
            jnp.broadcast_to(
                jnp.concatenate(
                    [
                        w_router,
                        norm_gains.reshape(dense_rows, 2),
                        jnp.zeros((dense_rows, PAD - experts - 2), bf16),
                    ],
                    axis=1,
                )[None],
                (ranks, dense_rows, PAD),
            ),
        ],
        axis=2,
    )
    slab = lax.all_to_all(slab, "ep", split_axis=0, concat_axis=0, tiled=True)
    slab = slab.reshape(ranks * dense_rows, 3 * width + PAD)
    w_o, cotangent_late = after((w_o, cotangent), slab)
    out_pieces = [w_o] + [shift_rep(w_o, step) for step in range(1, planes)]
    slab_pieces = [slab] + [shift_rep(slab, step) for step in range(1, planes)]
    upstream_group = with_group(cotangent_late)
    slab = place_rep(slab_pieces)
    router = slab[:, 3 * width :]
    gain_pair = router[:, experts : experts + 2].reshape(-1).astype(f32)
    first_gain = gain_pair[None, :D]
    second_gain = gain_pair[None, D:]
    out_weight = gather_ranks(after(place_rep(out_pieces), stream))
    out_weight = (
        out_weight.reshape(ranks, planes, -1, D).transpose(1, 0, 2, 3).reshape(D, D)
    )
    upstream_all = gather_ranks(after(upstream_group, out_weight))

    def send_weight(weight, step):
        part = lax.dynamic_index_in_dim(weight, (own + step) % share, 0, keepdims=False)
        return shift_rep(part, step) if step else part

    order = shift_order(planes)
    early, late = after((w_in, (w_in, w_out)), slab)
    in_pieces = {0: send_weight(w_in, 0), order[0]: send_weight(early, order[0])}

    normed, proj = project(stream, first_gain, slab)
    proj = proj.reshape(ranks, micro, rows, 3 * width)
    segment = segments[0]
    cosine, sine = jax.vmap(lambda one: rope_tables(doc_positions(one), HD))(segment)
    sine = jnp.where(jnp.arange(HD) < HD // 2, -sine, sine)
    tables = (cosine, sine, segment[:, :, None], segment[:, None, :], qk_gains)
    mixed_h, query, keys, values, lses = attention_forward(proj, *tables)
    mixed_h, out_weight = lax.optimization_barrier((mixed_h, out_weight))
    mixed = lax.all_to_all(mixed_h, "ep", split_axis=0, concat_axis=3, tiled=True)
    mixed = mixed.reshape(mine, D)
    hidden, payload, gates = route(
        mixed, tokens, out_weight, second_gain, router, routes, experts
    )
    normed_two = payload[:, :D]
    (payload, in_pieces[order[0]]), late = after(
        ((payload, in_pieces[order[0]]), late), payload, in_pieces[order[0]]
    )
    payload = with_group(payload)
    payload, late = lax.optimization_barrier((payload, late))
    for step in order[1:]:
        in_pieces[step] = send_weight(late[0], step)
    out_parts = {step: send_weight(late[1], step) for step in [0] + order}
    in_weight = place_rep([in_pieces[step] for step in range(planes)])
    out_expert = place_rep([out_parts[step] for step in range(planes)])
    payload = gather_ranks(after(payload, upstream_all))

    shape = (ranks, share, micro, rows, -1)
    rows_in, tail, both, active, grad_produced, up_rows, places = expert_forward(
        expert, payload.reshape(shape), upstream_all.reshape(shape), in_weight, slots, experts
    )
    in_rows = micro * ranks // 2 * slots

    def flat(value):
        return value.reshape(in_rows, -1)

    grad_out_expert = dot(flat(active), flat(grad_produced), ((0,), (0,)))

    def by_expert(sums):
        return jnp.stack(
            [
                sum(jnp.where((own - step) % share == j, sums[step], 0.0) for step in range(share))
                for j in range(share)
            ]
        )

    def scatter_rep(value):
        count = value.shape[0] // planes
        sums = [None] * share
        for step in [0] + order:
            part = lax.dynamic_slice_in_dim(value, (plane + step) % planes * count, count, 0)
            if step:
                part = shift_rep(part.astype(bf16), step).astype(f32)
            sums[step % share] = part if sums[step % share] is None else sums[step % share] + part
        return by_expert(sums)

    grad_w_out = scatter_rep(grad_out_expert)
    back = [
        expert_backward(
            step, expert, tail, both, active, grad_produced, up_rows, places, in_weight,
            out_expert, share, rows, experts,
        )
        for step in range(micro)
    ]
    grad_in_expert = sum(
        dot(
            rows_in[step].reshape(in_rows // micro, D),
            back[step][2].reshape(in_rows // micro, 2 * FF),
            ((0,), (0,)),
        )
        for step in range(micro)
    )
    grad_w_in = scatter_rep(grad_in_expert)

    def scatter_ranks(value):
        value = lax.psum_scatter(value, "ep", scatter_dimension=0)
        return [value[0]] + [exchange(value[step], share - step) for step in range(1, share)]

    returned = [scatter_ranks(back[step][1]) for step in range(micro)]
    grad_inputs, branches, logit_grads = [], [], []
    gain_two_sum = gain_one_sum = qk_sum = qkv_sum = 0.0
    by_rank = stream.reshape(ranks, micro, rows, D)
    for step in range(micro):
        at = slice(step * rows, (step + 1) * rows)
        grad_hidden, grad_branch, grad_mixed, grad_logits, gain_two = hidden_backward(
            returned[step], hidden[at], gates[at], cotangent[at], second_gain, router, out_weight,
            experts,
        )
        branches.append(grad_branch)
        logit_grads.append(grad_logits)
        gain_two_sum = gain_two_sum + gain_two
        grad_mixed = lax.all_to_all(grad_mixed, "ep", split_axis=1, concat_axis=0, tiled=True)
        grad_proj, grad_qk = attention_backward(
            step, proj, *tables, query, keys, values, lses, grad_mixed
        )
        qk_sum = qk_sum + grad_qk.reshape(-1)
        grad_normed, gain_one = project_backward(step, grad_proj, by_rank, slab)
        gain_one_sum = gain_one_sum + gain_one
        qkv_sum = qkv_sum + dot(
            normed.reshape(ranks, micro, rows, D)[:, step].reshape(length, D),
            grad_proj.reshape(length, 3 * width),
            ((0,), (0,)),
        )
        grad_normed = lax.psum_scatter(
            grad_normed, "ep", scatter_dimension=0, tiled=True
        ).astype(f32)
        own_stream = tokens[at].astype(f32)
        own_inverse = inverse_rms(own_stream)
        grad_inputs.append(
            grad_hidden + rms_backward(own_stream, own_inverse, first_gain, grad_normed)
        )
    mixture = [
        sum(part.astype(f32) for part in scatter_ranks(back[step][0])) for step in range(micro)
    ]
    output = (hidden + jnp.concatenate(mixture, axis=0)).astype(bf16)
    out_sum = dot(mixed, jnp.concatenate(branches, axis=0), ((0,), (0,))).astype(bf16)
    out_sum = out_sum.reshape(planes, ranks, dense_rows, D).transpose(1, 0, 2, 3)
    out_sum = lax.psum_scatter(out_sum, "ep", scatter_dimension=0)
    grad_w_o = lax.dynamic_index_in_dim(out_sum, plane, 0, keepdims=False).astype(f32)
    for step in range(1, planes):
        part = lax.dynamic_index_in_dim(out_sum, (plane + step) % planes, 0, keepdims=False)
        grad_w_o = grad_w_o + shift_rep(part, step).astype(f32)

    router_sum = dot(normed_two, jnp.concatenate(logit_grads, axis=0), ((0,), (0,)))
    qk_columns = qk_sum.shape[0] // dense_rows
    small = jnp.concatenate(
        [
            router_sum[:, :experts],
            jnp.concatenate([gain_one_sum, gain_two_sum], axis=1).reshape(D, 2),
            jnp.tile(qk_sum.reshape(dense_rows, qk_columns), (planes * ranks, 1)),
        ],
        axis=1,
    )
    count = small.shape[1]

    def pack(main, small):
        high, low = two_parts(small)
        blank = jnp.zeros((small.shape[0], PAD - 2 * count), bf16)
        return jnp.concatenate([main.astype(bf16), high, low, blank], axis=1)

    def unpack(packed):
        packed = packed.astype(f32)
        split = packed.shape[-1] - PAD
        tail = packed[..., split:]
        return packed[..., :split], tail[..., :count] + tail[..., count : 2 * count]

    packed = pack(qkv_sum, small)
    part_rows = D // planes
    main = lax.dynamic_slice_in_dim(qkv_sum, plane * part_rows, part_rows, 0)
    small = lax.dynamic_slice_in_dim(small, plane * part_rows, part_rows, 0)
    for step in range(1, planes):
        part = lax.dynamic_slice_in_dim(
            packed, (plane + step) % planes * part_rows, part_rows, 0
        )
        part_main, part_small = unpack(shift_rep(part, step))
        main, small = main + part_main, small + part_small
    packed = pack(main, small).reshape(ranks, dense_rows, -1)
    packed = lax.all_to_all(packed, "ep", split_axis=0, concat_axis=0, tiled=True)
    main, small = unpack(packed)
    grad_w_qkv = (
        main.reshape(ranks, dense_rows, 3, width).transpose(1, 2, 0, 3).reshape(dense_rows, 3 * D)
    )
    small = jnp.sum(small, axis=0)
    return (
        output,
        jnp.concatenate(grad_inputs, axis=0),
        grad_w_qkv,
        grad_w_o,
        small[:, :experts],
        small[:, experts : experts + 2].reshape(-1),
        small[:, experts + 2 :].reshape(-1),
        grad_w_in,
        grad_w_out,
    )


def solution(mesh):
    placed = (
        P(("rep", "ep"), None),
        P(("rep", "ep"), None),
        P(("rep", "ep"), None),
        P(("rep", "ep"), None),
        P(("rep", "ep"), None),
        P(("rep", "ep")),
        P(),
        P("ep", "rep", None),
        P("ep", "rep", None),
        P("rep", None, None),
        P(("rep", "ep"), None),
    )
    return jax.shard_map(
        on_device,
        mesh=mesh,
        in_specs=placed,
        out_specs=(
            P(("rep", "ep"), None),
            P(("rep", "ep"), None),
            P(("rep", "ep"), None),
            P(("rep", "ep"), None),
            P(("rep", "ep"), None),
            P(("rep", "ep")),
            P(),
            P("ep", "rep", None),
            P("ep", "rep", None),
        ),
        check_vma=False,
    )
```

time: 1660 us -> 1490 us (0.90)
  Pallas kernels: 54.7 us -> 342 us
  matrix products: 269 us -> 70.7 us
  waiting for transfers between devices: 929 us -> 743 us
  other arithmetic: 121 us -> 54.1 us
  local copies, waits for them, and re-layouts: 180 us -> 130 us
  blocking collectives: 0 us -> 49 us
    pallas_call x3 -> x12, Pallas kernels: 54.7 us -> 342 us  [the longest x2 156 us: expert_backward(): pl.pallas_call(kernel, grid_spec=pltpu.PrefetchScalarGridSpec(num_scalar_...]
    dot_general x21 -> x7, matrix products: 198 us -> 70.7 us  [dot(): return lax.dot_general(a, b, (dims, ((), ())), preferred_element_type=f32)]
    reduce_scatter x6, waiting for transfers between devices: 94 us -> 22.3 us  [the longest x4 22.3 us: scatter_ranks(): value = lax.psum_scatter(value, 'ep', scatter_dimension=0)]
    dot_general x6 -> x0, matrix products: 70.8 us -> none  [the longest x4 45.7 us: spread(): jnp.einsum('bskt,bsd->bktd', select_parts[:, :, :, step], value.reshape(r...]
    all_gather x4, waiting for transfers between devices: 103 us -> 44.1 us  [gather_ranks(): return lax.all_gather(value, 'ep', axis=0)]
    all_to_all x0 -> x2, blocking collectives: none -> 49 us  [the longest x1 27 us: on_device(): slab = lax.all_to_all(slab, 'ep', split_axis=0, concat_axis=0, tiled=True)]
    ppermute x24, waiting for transfers between devices: 616 us -> 567 us  [shift_rep(): lax.ppermute(value, 'rep', [(i, (i + step) % count) for i in range(count)])]
    convert_element_type x9 -> x1, other arithmetic: 40.3 us -> 1.24 us  [on_device(): gain_pair = router[:, experts:experts + 2].reshape(-1).astype(f32)]
  transfers between devices with their start and end apart: 46 -> 44, of which waited for: 30 -> 23; matrix products, arithmetic and copies ran while one was open for 23% -> 16% of each run, Pallas kernels for 3% -> 14%
where the time goes in v2:
time: 1490 us; the launch traced here: 1480 us
  waiting for transfers between devices  743 us (50%)
  Pallas kernels  342 us (23%)
  local copies, waits for them, and re-layouts  130 us (9%)
  starting transfers between devices  77.6 us (5%)
  matrix products  70.7 us (5%)
  other arithmetic  54.1 us (4%)
  blocking collectives  49 us (3%)
  between operations  14.9 us (1%)
    ppermute x24, waiting for transfers between devices, shift_rep(): lax.ppermute(value, 'rep', [(i, (i + step) % count) for i in range(count)])  567 us
    pallas_call x2, Pallas kernels, expert_backward(): pl.pallas_call(kernel, grid_spec=pltpu.PrefetchScalarGridSpec(num_scalar_...  156 us
    dot_general x7, matrix products, dot(): return lax.dot_general(a, b, (dims, ((), ())), preferred_element_type=f32)  70.7 us
    ppermute x6, waiting for transfers between devices, exchange(): return lax.ppermute(value, 'rep', pairs)  68.9 us
    pallas_call x1, Pallas kernels, expert_forward(): pl.pallas_call(kernel, grid_spec=pltpu.PrefetchScalarGridSpec(num_scalar_...  58.9 us
    ppermute x24, starting transfers between devices, shift_rep(): lax.ppermute(value, 'rep', [(i, (i + step) % count) for i in range(count)])  57 us
    all_gather x4, waiting for transfers between devices, gather_ranks(): return lax.all_gather(value, 'ep', axis=0)  44.1 us
    pallas_call x2, Pallas kernels, attention_backward(): pl.pallas_call(lambda *refs: backward_kernel(heads, *refs), grid=(1,), in...  33.4 us
  transfers between devices with their start and end apart: 44, of which 23 were waited for; matrix products, arithmetic and copies ran while one was open for 16% of the time, Pallas kernels for 14%

profile of v2, /device:TPU:0, one launch (start us, length us, event | category | flops | bytes accessed | tf_op | source)
XLA Modules:
  0.0 1481.7 jit_solution(8012302590425122374)
XLA Ops:
  12.5 27.0 %all_to_all.63 = bf16[8,64,896]{2,1,0:T(8,128)(2,1)S(1)} all-to-all(bf16[8,64,896]{2,1,0:T(8,128)(2,1)S(1)} %pad_maximum_fusion.6), channel_id=1, replica_groups=mesh['rep'=4,'ep'=8] {'ep'}, dimensions={0} | all-to-all | bytes 1835008 | tf_op jit(solution)/shard_map/all_to_all | solution.py:607
  76.0 23.8 %collective-permute-done.8 = bf16[256,2048]{1,0:T(8,128)(2,1)S(1)} collective-permute-done((bf16[256,2048]{1,0:T(8,128)(2,1)S(1)}, bf16[256,2048]{1,0:T(8,128)(2,1)S(1)}, u32[]{:S(2)}, u32[]{:S(2)}) %collective-permute-start.8) | collective-permute-done | bytes 1048608 | tf_op jit(solution)/shard_map/ppermute | solution.py:579
  101.4 29.9 %all-gather.11.cloned.1.call-done = bf16[2048,2048]{1,0:T(8,128)(2,1)} async-done(((bf16[256,2048]{1,0:T(8,128)(2,1)}), bf16[2048,2048]{1,0:T(8,128)(2,1)}) %all-gather.11.cloned.1.call-update) | async-done | bytes 8388624 | tf_op jit(solution)/shard_map/all_gather | solution.py:585
  149.9 16.2 %collective-permute-done = bf16[512,896]{1,0:T(8,128)(2,1)} collective-permute-done((bf16[512,896]{1,0:T(8,128)(2,1)S(1)}, bf16[512,896]{1,0:T(8,128)(2,1)}, u32[]{:S(2)}, u32[]{:S(2)}) %collective-permute-start) | collective-permute-done | bytes 917536 | tf_op jit(solution)/shard_map/ppermute | solution.py:530
  168.3 36.3 %collective-permute-done.1 = bf16[512,896]{1,0:T(8,128)(2,1)S(1)} collective-permute-done((bf16[512,896]{1,0:T(8,128)(2,1)S(1)}, bf16[512,896]{1,0:T(8,128)(2,1)S(1)}, u32[]{:S(2)}, u32[]{:S(2)}) %collective-permute-start.1) | collective-permute-done | bytes 917536 | tf_op jit(solution)/shard_map/ppermute | solution.py:530
  209.3 19.2 %collective-permute-start.6 = (bf16[512,2048]{1,0:T(8,128)(2,1)}, bf16[512,2048]{1,0:T(8,128)(2,1)}, u32[]{:S(2)}, u32[]{:S(2)}) collective-permute-start(bf16[512,2048]{1,0:T(8,128)(2,1)} %dynamic-slice_bitcast_fusion.2), channel_id=1, source_target_pairs={{0,8},{8,16},{16,24},{24,0},{1,9},{9,17},{17,25},{25,1},{2,10},{10... | collective-permute-start | bytes 6291464 | tf_op jit(solution)/shard_map/ppermute | solution.py:530
  250.9 21.7 %shard_map.179 = (bf16[8,2,128,256]{3,2,1,0:T(8,128)(2,1)}, bf16[2,1024,256]{2,1,0:T(8,128)(2,1)S(1)}, bf16[2,1024,256]{2,1,0:T(8,128)(2,1)S(1)}, bf16[2,1024,256]{2,1,0:T(8,128)(2,1)}, f32[2,2,1024,1]{3,2,1,0:T(8,128)}) custom-call(f32[8,2,128,768]{3,2,1,0:T(8,128)} %bitcast.163, f32[2,1024,128]{2,1,0:T(8,128)} %get-tuple-element.178.refs_1_, ...), custom_call_target="tpu_custom_call" | custom-call | tf_op jit(solution)/shard_map/pallas_call | solution.py:194
  304.3 23.4 %collective-permute-done.7 = bf16[256,2176]{1,0:T(8,128)(2,1)S(1)} collective-permute-done((bf16[256,2176]{1,0:T(8,128)(2,1)S(1)}, bf16[256,2176]{1,0:T(8,128)(2,1)S(1)}, u32[]{:S(2)}, u32[]{:S(2)}) %collective-permute-start.7) | collective-permute-done | bytes 1114144 | tf_op jit(solution)/shard_map/ppermute | solution.py:579
  355.8 95.6 %collective-permute-done.11 = bf16[256,2048]{1,0:T(8,128)(2,1)} collective-permute-done((bf16[256,2048]{1,0:T(8,128)(2,1)}, bf16[256,2048]{1,0:T(8,128)(2,1)}, u32[]{:S(2)}, u32[]{:S(2)}) %collective-permute-start.11) | collective-permute-done | bytes 1048608 | tf_op jit(solution)/shard_map/ppermute | solution.py:530
  453.8 82.9 %collective-permute-done.12 = bf16[256,2048]{1,0:T(8,128)(2,1)} collective-permute-done((bf16[256,2048]{1,0:T(8,128)(2,1)}, bf16[256,2048]{1,0:T(8,128)(2,1)}, u32[]{:S(2)}, u32[]{:S(2)}) %collective-permute-start.12) | collective-permute-done | bytes 1048608 | tf_op jit(solution)/shard_map/ppermute | solution.py:530
  547.6 58.9 %shard_map.181 = (bf16[2,4,272,2048]{3,2,1,0:T(8,128)(2,1)}, f32[2,4,272,128]{3,2,1,0:T(8,128)S(1)}, f32[2,4,272,2048]{3,2,1,0:T(8,128)}, bf16[2,4,272,1024]{3,2...) custom-call(s32[1]{0:T(128)} %bitcast.12.expert, ...), custom_call_target="tpu_custom_call" | custom-call | tf_op jit(solution)/shard_map/pallas_call | solution.py:360
  606.4 78.0 %shard_map.182 = (bf16[8,2,128,2048]{3,2,1,0:T(8,128)(2,1)}, bf16[8,2,128,2176]{3,2,1,0:T(8,128)(2,1)}, bf16[4,272,2048]{2,1,0:T(8,128)(2,1)}) custom-call(s32[1]{0:T(128)} %bitcast.12.expert, f32[2,4,272,128]{3,2,1,0:T(8,128)S(1)} %get-tuple-element.87.tail, f32[2,4,272,2048]{3,2,1,0:T(8,128)} %get-tuple-element.88.both, ...), custom_call_target="tpu_custom_call" | custom-call | tf_op jit(solution)/shard_map/pallas_call | solution.py:437
  685.7 77.6 %shard_map.183 = (bf16[8,2,128,2048]{3,2,1,0:T(8,128)(2,1)}, bf16[8,2,128,2176]{3,2,1,0:T(8,128)(2,1)}, bf16[4,272,2048]{2,1,0:T(8,128)(2,1)}) custom-call(s32[1]{0:T(128)} %bitcast.12.expert, f32[2,4,272,128]{3,2,1,0:T(8,128)S(1)} %copy-done.11, f32[2,4,272,2048]{3,2,1,0:T(8,128)} %get-tuple-element.88.both, ...), custom_call_target="tpu_custom_call" | custom-call | tf_op jit(solution)/shard_map/pallas_call | solution.py:437
  766.5 18.6 %reduce-scatter.12.cloned.1.call-done = bf16[1,2,128,2176]{3,2,1,0:T(8,128)(2,1)} async-done(((bf16[8,2,128,2176]{3,2,1,0:T(8,128)(2,1)}), bf16[1,2,128,2176]{3,2,1,0:T(8,128)(2,1)}) %reduce-scatter.12.cloned.1.call-update) | async-done | bytes 1114128 | tf_op jit(solution)/shard_map/reduce_scatter | solution.py:706
  812.6 22.0 %all_to_all.64 = bf16[128,8,256]{2,0,1:T(8,128)(2,1)S(1)} all-to-all(bf16[128,8,256]{2,0,1:T(8,128)(2,1)S(1)} %bitcast.189), channel_id=1, replica_groups=mesh['rep'=4,'ep'=8] {'ep'}, dimensions={1} | all-to-all | bytes 1048576 | tf_op jit(solution)/shard_map/all_to_all | solution.py:722
  834.7 16.6 %shard_map.185 = (bf16[8,128,768]{2,1,0:T(8,128)(2,1)}, f32[2,128]{1,0:T(2,128)S(1)}) custom-call(f32[8,2,128,768]{3,2,1,0:T(8,128)} %bitcast.164, f32[2,1024,128]{2,1,0:T(8,128)S(1)} %copy-done.3, f32[2,1024,128]{2,1,0:T(8,128)S(1)} %copy-done.2, s32[2,1024,1]{2,1,0:T(8,128)S(1)} %copy-done.1, s32[2,1,1024]{2,1,0:T(1,128)S(1)} %broadcast_in_dim_squeeze.7.refs_4_, ...), custom_call_target="tpu_custom_call" | custom-call | tf_op jit(solution)/shard_map/pallas_call | solution.py:216
  903.9 15.4 %all-to-all-done.3 = bf16[128,8,256]{2,0,1:T(8,128)(2,1)} async-done(((bf16[128,8,256]{2,0,1:T(8,128)(2,1)}), bf16[128,8,256]{2,0,1:T(8,128)(2,1)}, u32[]{:S(2)}, u32[]{:S(2)}) %all-to-all-start.3) | async-done | bytes 524320 | tf_op jit(solution)/shard_map/all_to_all | solution.py:722
  920.6 16.8 %shard_map.188 = (bf16[8,128,768]{2,1,0:T(8,128)(2,1)}, f32[2,128]{1,0:T(2,128)S(1)}) custom-call(f32[8,2,128,768]{3,2,1,0:T(8,128)} %bitcast.165, f32[2,1024,128]{2,1,0:T(8,128)S(1)} %copy-done.4, f32[2,1024,128]{2,1,0:T(8,128)S(1)} %copy-done.2, s32[2,1024,1]{2,1,0:T(8,128)S(1)} %copy-done.1, s32[2,1,1024]{2,1,0:T(1,128)S(1)} %broadcast_in_dim_squeeze.7.refs_4_, ...), custom_call_target="tpu_custom_call" | custom-call | tf_op jit(solution)/shard_map/pallas_call | solution.py:216
  979.8 16.6 %fusion.40 = f32[2048,2048]{1,0:T(8,128)} fusion(bf16[1088,2048]{1,0:T(8,128)(2,1)S(1)} %bitcast.175, bf16[1088,2048]{1,0:T(8,128)(2,1)} %bitcast.200), kind=kOutput, calls=%fused_computation.149 | convolution fusion | flops 9126805504 | bytes 25690112 | tf_op jit(solution)/shard_map/dot_general | solution.py:25
  1010.6 20.5 %convolution_add_fusion = f32[2048,2048]{1,0:T(8,128)} fusion(f32[2048,2048]{1,0:T(8,128)} %fusion.40, bf16[1088,2048]{1,0:T(8,128)(2,1)} %bitcast.174, bf16[1088,2048]{1,0:T(8,128)(2,1)} %bitcast.199), kind=kOutput, calls=%fused_computation.2 | convolution fusion | flops 9130999808 | bytes 42467328 | tf_op jit(solution)/shard_map/dot_general | solution.py:25
  1053.8 148.7 %collective-permute-done.28 = bf16[256,2048]{1,0:T(8,128)(2,1)} collective-permute-done((bf16[256,2048]{1,0:T(8,128)(2,1)}, bf16[256,2048]{1,0:T(8,128)(2,1)}, u32[]{:S(2)}, u32[]{:S(2)}) %collective-permute-start.28) | collective-permute-done | bytes 1048608 | tf_op jit(solution)/shard_map/ppermute | solution.py:530
  1202.6 85.4 %collective-permute-done.27 = bf16[256,2048]{1,0:T(8,128)(2,1)} collective-permute-done((bf16[256,2048]{1,0:T(8,128)(2,1)S(1)}, bf16[256,2048]{1,0:T(8,128)(2,1)}, u32[]{:S(2)}, u32[]{:S(2)}) %collective-permute-start.27) | collective-permute-done | bytes 1048608 | tf_op jit(solution)/shard_map/ppermute | solution.py:530
  1341.2 16.1 %collective-permute-done.20 = bf16[512,896]{0,1:T(8,128)(2,1)} collective-permute-done((bf16[512,896]{0,1:T(8,128)(2,1)}, bf16[512,896]{0,1:T(8,128)(2,1)}, u32[]{:S(2)}, u32[]{:S(2)}) %collective-permute-start.20) | collective-permute-done | bytes 917536 | tf_op jit(solution)/shard_map/ppermute | solution.py:530
  1358.8 54.2 %collective-permute-done.19 = bf16[512,896]{0,1:T(8,128)(2,1)} collective-permute-done((bf16[512,896]{0,1:T(8,128)(2,1)}, bf16[512,896]{0,1:T(8,128)(2,1)}, u32[]{:S(2)}, u32[]{:S(2)}) %collective-permute-start.19) | collective-permute-done | bytes 917536 | tf_op jit(solution)/shard_map/ppermute | solution.py:530
  (295 shorter events, 445.2 us)
Async XLA Ops:
  7.9 123.3 %all-gather.11.cloned.1.call-start = ((), (), s32[]{:S(2)}) async-start(), calls=%async_computation.20 | async-start | bytes 9437184 | tf_op jit(solution)/shard_map/all_gather | solution.py:585
  74.4 473.2 %all-gather.13.cloned.1.call-start = ((), (), s32[]{:S(2)}) async-start(), calls=%async_computation.21 | async-start | bytes 18874368 | tf_op jit(solution)/shard_map/all_gather | solution.py:585
  209.3 94.9 %collective-permute-start.6 = (bf16[512,2048]{1,0:T(8,128)(2,1)}, bf16[512,2048]{1,0:T(8,128)(2,1)}, u32[]{:S(2)}, u32[]{:S(2)}) collective-permute-start(bf16[512,2048]{1,0:T(8,128)(2,1)} %dynamic-slice_bitcast_fusion.2), channel_id=1, source_target_pairs={{0,8},{8,16},{16,24},{24,0},{1,9},{9,17},{17,25},{25,1},{2,10},{10... | collective-permute-start | bytes 6291464 | tf_op jit(solution)/shard_map/ppermute | solution.py:530
  278.2 269.4 %all-gather.15.cloned.1.call-start = ((), (), s32[]{:S(2)}) async-start(), calls=%async_computation.22 | async-start | bytes 20054016 | tf_op jit(solution)/shard_map/all_gather | solution.py:585
  329.4 455.8 %reduce-scatter.12.cloned.1.call-start = ((), (), s32[]{:S(2)}) async-start(), calls=%async_computation.14 | async-start | bytes 10027008 | tf_op jit(solution)/shard_map/reduce_scatter | solution.py:706
  334.4 206.8 %collective-permute-start.9 = (bf16[512,2048]{1,0:T(8,128)(2,1)}, bf16[512,2048]{1,0:T(8,128)(2,1)}, u32[]{:S(2)}, u32[]{:S(2)}) collective-permute-start(bf16[512,2048]{1,0:T(8,128)(2,1)} %get-tuple-element.155), channel_id=1, source_target_pairs={{0,16},{8,24},{16,0},{24,8},{1,17},{9,25},{17,1},{25,9},{2,18},{10... | collective-permute-start | bytes 6291464 | tf_op jit(solution)/shard_map/ppermute | solution.py:530
  336.8 207.6 %collective-permute-start.10 = (bf16[512,2048]{1,0:T(8,128)(2,1)}, bf16[512,2048]{1,0:T(8,128)(2,1)}, u32[]{:S(2)}, u32[]{:S(2)}) collective-permute-start(bf16[512,2048]{1,0:T(8,128)(2,1)} %get-tuple-element.154), channel_id=1, source_target_pairs={{0,24},{8,0},{16,8},{24,16},{1,25},{9,1},{17,9},{25,17},{2,26},{10... | collective-permute-start | bytes 6291464 | tf_op jit(solution)/shard_map/ppermute | solution.py:530
  338.9 112.5 %collective-permute-start.11 = (bf16[256,2048]{1,0:T(8,128)(2,1)}, bf16[256,2048]{1,0:T(8,128)(2,1)}, u32[]{:S(2)}, u32[]{:S(2)}) collective-permute-start(bf16[256,2048]{1,0:T(8,128)(2,1)} %get-tuple-element.163), channel_id=1, source_target_pairs={{0,8},{8,16},{16,24},{24,0},{1,9},{9,17},{17,25},{25,1},{2,10},{10... | collective-permute-start | bytes 3145736 | tf_op jit(solution)/shard_map/ppermute | solution.py:530
  340.6 196.0 %collective-permute-start.12 = (bf16[256,2048]{1,0:T(8,128)(2,1)}, bf16[256,2048]{1,0:T(8,128)(2,1)}, u32[]{:S(2)}, u32[]{:S(2)}) collective-permute-start(bf16[256,2048]{1,0:T(8,128)(2,1)} %get-tuple-element.162), channel_id=1, source_target_pairs={{0,16},{8,24},{16,0},{24,8},{1,17},{9,25},{17,1},{25,9},{2,18},{10... | collective-permute-start | bytes 3145736 | tf_op jit(solution)/shard_map/ppermute | solution.py:530
  341.2 197.8 %collective-permute-start.13 = (bf16[256,2048]{1,0:T(8,128)(2,1)}, bf16[256,2048]{1,0:T(8,128)(2,1)}, u32[]{:S(2)}, u32[]{:S(2)}) collective-permute-start(bf16[256,2048]{1,0:T(8,128)(2,1)} %get-tuple-element.161), channel_id=1, source_target_pairs={{0,24},{8,0},{16,8},{24,16},{1,25},{9,1},{17,9},{25,17},{2,26},{10... | collective-permute-start | bytes 3145736 | tf_op jit(solution)/shard_map/ppermute | solution.py:530
  684.4 186.0 %reduce-scatter.16.cloned.1.call-start = ((), (), s32[]{:S(2)}) async-start(), calls=%async_computation.16 | async-start | bytes 10027008 | tf_op jit(solution)/shard_map/reduce_scatter | solution.py:706
  763.4 540.4 %reduce-scatter.10.cloned.1.call-start = ((), (), s32[]{:S(2)}) async-start(), calls=%async_computation.13 | async-start | bytes 9437184 | tf_op jit(solution)/shard_map/reduce_scatter | solution.py:706
  764.1 573.0 %reduce-scatter.8.cloned.1.call-start = ((), (), s32[]{:S(2)}) async-start(), calls=%async_computation.12 | async-start | bytes 9437184 | tf_op jit(solution)/shard_map/reduce_scatter | solution.py:706
  764.9 681.4 %reduce-scatter.14.cloned.1.call-start = ((), (), s32[]{:S(2)}) async-start(), calls=%async_computation.15 | async-start | bytes 4718592 | tf_op jit(solution)/shard_map/reduce_scatter | solution.py:734
  903.6 542.6 %reduce-scatter.18.cloned.1.call-start = ((), (), s32[]{:S(2)}) async-start(), calls=%async_computation.17 | async-start | bytes 4718592 | tf_op jit(solution)/shard_map/reduce_scatter | solution.py:734
  952.7 497.7 %reduce-scatter.20.cloned.1.call-start = ((), (), s32[]{:S(2)}) async-start(), calls=%async_computation.18 | async-start | bytes 9437184 | tf_op jit(solution)/shard_map/reduce_scatter | solution.py:748
  1039.2 254.7 %collective-permute-start.26 = (bf16[512,2048]{1,0:T(8,128)(2,1)}, bf16[512,2048]{1,0:T(8,128)(2,1)}, u32[]{:S(2)}, u32[]{:S(2)}) collective-permute-start(bf16[512,2048]{1,0:T(8,128)(2,1)} %get-tuple-element.143), channel_id=1, source_target_pairs={{0,24},{8,0},{16,8},{24,16},{1,25},{9,1},{17,9},{25,17},{2,26},{10... | collective-permute-start | bytes 6291464 | tf_op jit(solution)/shard_map/ppermute | solution.py:530
  1042.7 251.2 %collective-permute-start.25 = (bf16[512,2048]{1,0:T(8,128)(2,1)}, bf16[512,2048]{1,0:T(8,128)(2,1)}, u32[]{:S(2)}, u32[]{:S(2)}) collective-permute-start(bf16[512,2048]{1,0:T(8,128)(2,1)} %get-tuple-element.144), channel_id=1, source_target_pairs={{0,8},{8,16},{16,24},{24,0},{1,9},{9,17},{17,25},{25,1},{2,10},{10... | collective-permute-start | bytes 6291464 | tf_op jit(solution)/shard_map/ppermute | solution.py:530
  1042.7 251.2 %collective-permute-start.24 = (bf16[512,2048]{1,0:T(8,128)(2,1)}, bf16[512,2048]{1,0:T(8,128)(2,1)}, u32[]{:S(2)}, u32[]{:S(2)}) collective-permute-start(bf16[512,2048]{1,0:T(8,128)(2,1)} %get-tuple-element.142), channel_id=1, source_target_pairs={{0,16},{8,24},{16,0},{24,8},{1,17},{9,25},{17,1},{25,9},{2,18},{10... | collective-permute-start | bytes 6291464 | tf_op jit(solution)/shard_map/ppermute | solution.py:530
  1043.8 158.8 %collective-permute-start.28 = (bf16[256,2048]{1,0:T(8,128)(2,1)}, bf16[256,2048]{1,0:T(8,128)(2,1)}, u32[]{:S(2)}, u32[]{:S(2)}) collective-permute-start(bf16[256,2048]{1,0:T(8,128)(2,1)} %get-tuple-element.151), channel_id=1, source_target_pairs={{0,8},{8,16},{16,24},{24,0},{1,9},{9,17},{17,25},{25,1},{2,10},{10... | collective-permute-start | bytes 3145736 | tf_op jit(solution)/shard_map/ppermute | solution.py:530
  1047.1 240.9 %collective-permute-start.27 = (bf16[256,2048]{1,0:T(8,128)(2,1)S(1)}, bf16[256,2048]{1,0:T(8,128)(2,1)}, u32[]{:S(2)}, u32[]{:S(2)}) collective-permute-start(bf16[256,2048]{1,0:T(8,128)(2,1)S(1)} %get-tuple-element.149), channel_id=1, source_target_pairs={{0,16},{8,24},{16,0},{24,8},{1,17},{9,25},{17,1},{25,9},{2,18},{10... | collective-permute-start | bytes 3145736 | tf_op jit(solution)/shard_map/ppermute | solution.py:530
  1334.5 78.5 %collective-permute-start.19 = (bf16[512,896]{0,1:T(8,128)(2,1)}, bf16[512,896]{0,1:T(8,128)(2,1)}, u32[]{:S(2)}, u32[]{:S(2)}) collective-permute-start(bf16[512,896]{0,1:T(8,128)(2,1)} %get-tuple-element.158), channel_id=1, source_target_pairs={{0,16},{8,24},{16,0},{24,8},{1,17},{9,25},{17,1},{25,9},{2,18},{10... | collective-permute-start | bytes 2752520 | tf_op jit(solution)/shard_map/ppermute | solution.py:530
  1335.3 79.1 %collective-permute-start.18 = (bf16[512,896]{0,1:T(8,128)(2,1)S(1)}, bf16[512,896]{0,1:T(8,128)(2,1)}, u32[]{:S(2)}, u32[]{:S(2)}) collective-permute-start(bf16[512,896]{0,1:T(8,128)(2,1)S(1)} %get-tuple-element.156), channel_id=1, source_target_pairs={{0,8},{8,16},{16,24},{24,0},{1,9},{9,17},{17,25},{25,1},{2,10},{10... | collective-permute-start | bytes 2752520 | tf_op jit(solution)/shard_map/ppermute | solution.py:530
  1339.0 84.4 %collective-permute-start.14 = (bf16[128,2048]{1,0:T(8,128)(2,1)}, bf16[128,2048]{1,0:T(8,128)(2,1)}, u32[]{:S(2)}, u32[]{:S(2)}) collective-permute-start(bf16[128,2048]{1,0:T(8,128)(2,1)} %slice_bitcast_fusion.6), channel_id=1, source_target_pairs={{0,8},{8,0},{16,24},{24,16},{1,9},{9,1},{17,25},{25,17},{2,10},{10... | collective-permute-start | bytes 1572872 | tf_op jit(solution)/shard_map/ppermute | solution.py:579
  (59 other events, 1302.7 us)
Sparse Core Ops, SparseCore 0:
  9.9 64.4 all-gather.8
  76.8 54.3 all-gather.10
  139.8 89.8 all-gather.12
  329.5 95.4 all-gather.14
  684.5 100.5 reduce-scatter.11
  788.6 81.8 reduce-scatter.15
  873.9 76.8 reduce-scatter.9
  954.6 71.2 reduce-scatter.7
  1029.3 51.3 reduce-scatter.13
  1084.2 51.3 reduce-scatter.17
  1139.0 71.2 reduce-scatter.19

commit v3 on v2

--- a/solution.py
+++ b/solution.py
@@ -250,7 +250,7 @@
     )(tokens, gain, slab)
 
 
-TILE = 256
+TILE = 512
 
 
 def tiles(count):
@@ -298,45 +298,45 @@
     return jnp.sum(jnp.where(column == number, value.astype(f32), 0.0), axis=1, keepdims=True)
 
 
+def one_hot(slot, slots):
+    place = lax.broadcasted_iota(jnp.int32, (slots, slot.shape[1]), 0).astype(f32)
+    return (place == slot).astype(bf16)
+
+
 def expert_forward(expert, payload, upstream, in_weight, slots, experts):
     ranks, share, micro, rows, _ = payload.shape
-    block = 2 * share * rows
+    count = share * rows
+    block = 2 * slots
 
     def kernel(
         expert, payload, upstream, in_weight, rows_in, tail, both, active, grad_produced,
         up_rows, places,
     ):
         number = expert[0]
-        value = payload[...].reshape(block, D + PAD)
-        marks = value[:, D:]
-        first = lax.broadcasted_iota(jnp.int32, (8, PAD), 1) == number
-        taken = dot(first.astype(bf16), marks, ((1,), (1,))) > 0.0
-        before = lax.broadcasted_iota(jnp.int32, (block, block), 0)
-        behind = lax.broadcasted_iota(jnp.int32, (block, block), 1)
-        slot = dot(taken.astype(bf16), (before < behind).astype(bf16))
-        slot = jnp.where(taken, slot, -1.0)[0:1]
-        place = lax.broadcasted_iota(jnp.int32, (slots, block), 0).astype(f32)
-        select = (place == slot).astype(bf16)
-        taken = lane(marks, number) > 0.0
-        wide = jnp.broadcast_to(taken, (block, PAD))
-        slot = dot((before > behind).astype(bf16), wide.astype(bf16))
-        places[0, 0] = jnp.where(wide, slot, -1.0)
-        rows_in[0, 0] = dot(select, value[:, :D]).astype(bf16)
-        marks = dot(select, marks)
-        tail[0, 0] = marks
-        gate = lane(marks, number) + lane(marks, experts + number)
-
-        @tiles(D)
-        def _(number):
-            at = tile(number)
-            picked = dot(select, upstream[:, :, 0, :, at].reshape(block, TILE))
-            up_rows[0, 0, :, at] = picked.astype(bf16)
-            grad_produced[0, 0, :, at] = (gate * picked).astype(bf16)
-
-        @tiles(FF)
-        def _(number):
-            at = tile(number)
-            more = pl.ds(pl.multiple_of(FF + number * TILE, TILE), TILE)
+        for part in range(2):
+            here = slice(part * slots, (part + 1) * slots)
+            value = payload[part].reshape(count, D + PAD)
+            marks = value[:, D:]
+            first = lax.broadcasted_iota(jnp.int32, (8, PAD), 1) == number
+            taken = dot(first.astype(bf16), marks, ((1,), (1,))) > 0.0
+            before = lax.broadcasted_iota(jnp.int32, (count, count), 0)
+            behind = lax.broadcasted_iota(jnp.int32, (count, count), 1)
+            slot = dot(taken.astype(bf16), (before < behind).astype(bf16))
+            select = one_hot(jnp.where(taken, slot, -1.0)[0:1], slots)
+            wide = jnp.broadcast_to(lane(marks, number) > 0.0, (count, PAD))
+            slot = dot((before > behind).astype(bf16), wide.astype(bf16))
+            places[0, 0, part] = jnp.where(wide, slot, -1.0)
+            rows_in[0, 0, here] = dot(select, value[:, :D]).astype(bf16)
+            marks = dot(select, marks)
+            tail[0, 0, here] = marks
+            gate = lane(marks, number) + lane(marks, experts + number)
+            picked = dot(select, upstream[part].reshape(count, D))
+            up_rows[0, 0, here] = picked.astype(bf16)
+            grad_produced[0, 0, here] = (gate * picked).astype(bf16)
+
+        for number in range(FF // TILE):
+            at = slice(number * TILE, (number + 1) * TILE)
+            more = slice(FF + number * TILE, FF + (number + 1) * TILE)
             gate_part = dot(rows_in[0, 0], in_weight[:, at])
             up_part = dot(rows_in[0, 0], in_weight[:, more])
             both[0, 0, :, at] = gate_part
@@ -348,23 +348,27 @@
     def tokens_spec(width):
         return pl.BlockSpec((2, share, 1, rows, width), lambda m, b, _: (b, 0, m, 0, 0))
 
+    pairs = ranks // 2
     shapes = [
-        out((micro, ranks // 2, slots, D)),
-        out((micro, ranks // 2, slots, PAD), f32),
-        out((micro, ranks // 2, slots, 2 * FF), f32),
-        out((micro, ranks // 2, slots, FF)),
-        out((micro, ranks // 2, slots, D)),
-        out((micro, ranks // 2, slots, D)),
-        out((micro, ranks // 2, block, PAD), f32),
+        out((micro, pairs, block, D)),
+        out((micro, pairs, block, PAD), f32),
+        out((micro, pairs, block, 2 * FF), f32),
+        out((micro, pairs, block, FF)),
+        out((micro, pairs, block, D)),
+        out((micro, pairs, block, D)),
+        out((micro, pairs, 2, count, PAD), f32),
     ]
     return pl.pallas_call(
         kernel,
         grid_spec=pltpu.PrefetchScalarGridSpec(
             num_scalar_prefetch=1,
-            grid=(micro, ranks // 2),
+            grid=(micro, pairs),
             in_specs=[tokens_spec(D + PAD), tokens_spec(D), fixed(in_weight.shape)],
             out_specs=[
-                pl.BlockSpec((1, 1) + s.shape[2:], lambda m, b, _: (m, b, 0, 0)) for s in shapes
+                pl.BlockSpec(
+                    (1, 1) + s.shape[2:], lambda m, b, _, n=len(s.shape): (m, b) + (0,) * (n - 2)
+                )
+                for s in shapes
             ],
         ),
         out_shape=shapes,
@@ -376,8 +380,9 @@
     step, expert, tail, both, active, grad_produced, up_rows, places, in_weight, out_weight,
     share, rows, experts,
 ):
-    pairs, slots = tail.shape[1:3]
-    block = places.shape[2]
+    pairs, block = tail.shape[1:3]
+    slots = block // 2
+    count = places.shape[3]
 
     def kernel(
         expert, tail, both, active, grad_produced, up_rows, places, in_weight, out_weight,
@@ -385,25 +390,26 @@
     ):
         number = expert[0]
         gate = lane(tail[0, 0], number) + lane(tail[0, 0], experts + number)
-        place = lax.broadcasted_iota(jnp.int32, (block, slots), 1).astype(f32)
-        select = (places[0, 0][:, 0:1] == place).astype(bf16)
-        shape = (2, share, rows)
-
-        def produce(number, grad_gate):
-            at = tile(number)
+        place = lax.broadcasted_iota(jnp.int32, (count, slots), 1).astype(f32)
+        selects = [(places[0, 0, part][:, 0:1] == place).astype(bf16) for part in range(2)]
+
+        def spread(target, at, value):
+            for part in range(2):
+                result = dot(selects[part], value[part * slots : (part + 1) * slots])
+                target[part, :, :, at] = result.astype(bf16).reshape(share, rows, -1)
+
+        grad_gate = jnp.zeros((block, 1), f32)
+        for tile in range(D // TILE):
+            at = slice(tile * TILE, (tile + 1) * TILE)
             produced = dot(active[0, 0], out_weight[:, at]).astype(bf16).astype(f32)
-            weighted = (gate * produced).astype(bf16)
-            mixture[:, :, :, at] = dot(select, weighted).astype(bf16).reshape(shape + (TILE,))
-            return grad_gate + jnp.sum(
+            spread(mixture, at, (gate * produced).astype(bf16))
+            grad_gate = grad_gate + jnp.sum(
                 up_rows[0, 0, :, at].astype(f32) * produced, axis=1, keepdims=True
             )
 
-        grad_gate = lax.fori_loop(0, D // TILE, produce, jnp.zeros((slots, 1), f32))
-
-        @tiles(FF)
-        def _(number):
-            at = tile(number)
-            more = pl.ds(pl.multiple_of(FF + number * TILE, TILE), TILE)
+        for tile in range(FF // TILE):
+            at = slice(tile * TILE, (tile + 1) * TILE)
+            more = slice(FF + tile * TILE, FF + (tile + 1) * TILE)
             grad_active = dot(grad_produced[0, 0], out_weight[at, :], ((1,), (1,)))
             grad_active = grad_active.astype(bf16).astype(f32)
             gate_part = both[0, 0, :, at]
@@ -414,22 +420,21 @@
             ).astype(bf16)
             grad_both[0, :, more] = (grad_active * (gate_part * sigma)).astype(bf16)
 
-        @tiles(D)
-        def _(number):
-            at = tile(number)
+        for tile in range(D // TILE):
+            at = slice(tile * TILE, (tile + 1) * TILE)
             grad_rows = dot(grad_both[0], in_weight[at, :], ((1,), (1,))).astype(bf16)
-            grad_tokens[:, :, :, at] = dot(select, grad_rows).astype(bf16).reshape(shape + (TILE,))
+            spread(grad_tokens, at, grad_rows)
 
         high = grad_gate.astype(bf16).astype(f32)
-        column = lax.broadcasted_iota(jnp.int32, (slots, PAD), 1)
+        column = lax.broadcasted_iota(jnp.int32, (block, PAD), 1)
         extra = jnp.where(column == number, high, 0.0)
         extra = jnp.where(column == experts + number, grad_gate - high, extra)
-        grad_tokens[:, :, :, D:] = (
-            dot(select, extra.astype(bf16)).astype(bf16).reshape(shape + (PAD,))
-        )
+        spread(grad_tokens, slice(D, D + PAD), extra.astype(bf16))
 
     def part(value):
-        return pl.BlockSpec((1, 1) + value.shape[2:], lambda b, _: (step, b, 0, 0))
+        return pl.BlockSpec(
+            (1, 1) + value.shape[2:], lambda b, _: (step, b) + (0,) * (value.ndim - 2)
+        )
 
     def tokens_spec(width):
         return pl.BlockSpec((2, share, rows, width), lambda b, _: (b, 0, 0, 0))
@@ -444,13 +449,13 @@
             out_specs=[
                 tokens_spec(D),
                 tokens_spec(D + PAD),
-                pl.BlockSpec((1, slots, 2 * FF), lambda b, _: (b, 0, 0)),
+                pl.BlockSpec((1, block, 2 * FF), lambda b, _: (b, 0, 0)),
             ],
         ),
         out_shape=[
             out((2 * pairs, share, rows, D)),
             out((2 * pairs, share, rows, D + PAD)),
-            out((pairs, slots, 2 * FF)),
+            out((pairs, block, 2 * FF)),
         ],
         compiler_params=params(),
     )(
@@ -569,7 +574,7 @@
     rows = mine // micro
     length = rows * ranks
     capacity = rows * TOP * 17 // (16 * experts)
-    slots = -(-2 * share * capacity // 16) * 16
+    slots = -(-share * capacity // 16) * 16
     width = HEADS // ranks * HD
     qk_gains = qk_gain.astype(f32).reshape(2, HD)
     dense_rows = w_qkv.shape[0]
@@ -585,6 +590,8 @@
         return lax.all_gather(value, "ep", axis=0)
 
     stream = gather_ranks(tokens)
+    out_pieces = [w_o] + [shift_rep(w_o, step) for step in range(1, planes)]
+    upstream_group = with_group(cotangent)
     slab = jnp.concatenate(
         [
             w_qkv.reshape(dense_rows, 3, ranks, width)
@@ -606,31 +613,30 @@
     )
     slab = lax.all_to_all(slab, "ep", split_axis=0, concat_axis=0, tiled=True)
     slab = slab.reshape(ranks * dense_rows, 3 * width + PAD)
-    w_o, cotangent_late = after((w_o, cotangent), slab)
-    out_pieces = [w_o] + [shift_rep(w_o, step) for step in range(1, planes)]
+    out_pieces, slab = lax.optimization_barrier((out_pieces, slab))
     slab_pieces = [slab] + [shift_rep(slab, step) for step in range(1, planes)]
-    upstream_group = with_group(cotangent_late)
     slab = place_rep(slab_pieces)
     router = slab[:, 3 * width :]
     gain_pair = router[:, experts : experts + 2].reshape(-1).astype(f32)
     first_gain = gain_pair[None, :D]
     second_gain = gain_pair[None, D:]
-    out_weight = gather_ranks(after(place_rep(out_pieces), stream))
+    out_weight = gather_ranks(place_rep(out_pieces))
     out_weight = (
         out_weight.reshape(ranks, planes, -1, D).transpose(1, 0, 2, 3).reshape(D, D)
     )
-    upstream_all = gather_ranks(after(upstream_group, out_weight))
 
     def send_weight(weight, step):
         part = lax.dynamic_index_in_dim(weight, (own + step) % share, 0, keepdims=False)
         return shift_rep(part, step) if step else part
 
     order = shift_order(planes)
-    early, late = after((w_in, (w_in, w_out)), slab)
-    in_pieces = {0: send_weight(w_in, 0), order[0]: send_weight(early, order[0])}
+    early = after((w_in, w_out), slab)
+    in_pieces = {step: send_weight(early[0], step) for step in [0] + order[:1]}
+    out_parts = {step: send_weight(early[1], step) for step in [0] + order[:1]}
 
     normed, proj = project(stream, first_gain, slab)
     proj = proj.reshape(ranks, micro, rows, 3 * width)
+    upstream_all = gather_ranks(after(upstream_group, proj))
     segment = segments[0]
     cosine, sine = jax.vmap(lambda one: rope_tables(doc_positions(one), HD))(segment)
     sine = jnp.where(jnp.arange(HD) < HD // 2, -sine, sine)
@@ -643,30 +649,40 @@
         mixed, tokens, out_weight, second_gain, router, routes, experts
     )
     normed_two = payload[:, :D]
-    (payload, in_pieces[order[0]]), late = after(
-        ((payload, in_pieces[order[0]]), late), payload, in_pieces[order[0]]
-    )
+    payload, in_pieces, out_parts = lax.optimization_barrier((payload, in_pieces, out_parts))
     payload = with_group(payload)
-    payload, late = lax.optimization_barrier((payload, late))
+    payload, late = lax.optimization_barrier((payload, (w_in, w_out)))
     for step in order[1:]:
         in_pieces[step] = send_weight(late[0], step)
-    out_parts = {step: send_weight(late[1], step) for step in [0] + order}
+    for step in order[1:]:
+        out_parts[step] = send_weight(late[1], step)
     in_weight = place_rep([in_pieces[step] for step in range(planes)])
-    out_expert = place_rep([out_parts[step] for step in range(planes)])
-    payload = gather_ranks(after(payload, upstream_all))
+    payload = gather_ranks(payload)
 
     shape = (ranks, share, micro, rows, -1)
     rows_in, tail, both, active, grad_produced, up_rows, places = expert_forward(
         expert, payload.reshape(shape), upstream_all.reshape(shape), in_weight, slots, experts
     )
-    in_rows = micro * ranks // 2 * slots
+    in_rows = micro * ranks * slots
 
     def flat(value):
         return value.reshape(in_rows, -1)
 
     grad_out_expert = dot(flat(active), flat(grad_produced), ((0,), (0,)))
 
-    def by_expert(sums):
+    def cut_rep(value):
+        count = value.shape[0] // planes
+        parts = {}
+        for step in [0] + order:
+            part = lax.dynamic_slice_in_dim(value, (plane + step) % planes * count, count, 0)
+            parts[step] = part.astype(bf16) if step else part
+        return parts
+
+    def sum_rep(parts):
+        sums = [None] * share
+        for step in [0] + order:
+            part = parts[step].astype(f32)
+            sums[step % share] = part if sums[step % share] is None else sums[step % share] + part
         return jnp.stack(
             [
                 sum(jnp.where((own - step) % share == j, sums[step], 0.0) for step in range(share))
@@ -674,24 +690,34 @@
             ]
         )
 
-    def scatter_rep(value):
-        count = value.shape[0] // planes
-        sums = [None] * share
-        for step in [0] + order:
-            part = lax.dynamic_slice_in_dim(value, (plane + step) % planes * count, count, 0)
-            if step:
-                part = shift_rep(part.astype(bf16), step).astype(f32)
-            sums[step % share] = part if sums[step % share] is None else sums[step % share] + part
-        return by_expert(sums)
-
-    grad_w_out = scatter_rep(grad_out_expert)
-    back = [
-        expert_backward(
-            step, expert, tail, both, active, grad_produced, up_rows, places, in_weight,
-            out_expert, share, rows, experts,
-        )
-        for step in range(micro)
-    ]
+    def send(parts, steps):
+        return {step: shift_rep(parts[step], step) for step in steps}
+
+    out_cut = cut_rep(grad_out_expert)
+    out_expert = place_rep([out_parts[step] for step in range(planes)])
+    out_expert, out_cut = lax.optimization_barrier((out_expert, out_cut))
+    out_sent = send(out_cut, order)
+    back = []
+    returned = []
+
+    def scatter_ranks(value):
+        return lax.psum_scatter(value, "ep", scatter_dimension=0)
+
+    def exchange_back(value):
+        return [value[0]] + [exchange(value[step], share - step) for step in range(1, share)]
+
+    for step in range(micro):
+        back.append(
+            expert_backward(
+                step, expert, tail, both, active, grad_produced, up_rows, places, in_weight,
+                out_expert, share, rows, experts,
+            )
+        )
+        returned.append(scatter_ranks(back[step][1]))
+        out_expert = after(out_expert, back[step][1])
+    short = {step: out_sent[step] for step in order[:2]}
+    rows_in, out_expert, short = lax.optimization_barrier((rows_in, out_expert, short))
+    out_sent.update(short)
     grad_in_expert = sum(
         dot(
             rows_in[step].reshape(in_rows // micro, D),
@@ -700,56 +726,73 @@
         )
         for step in range(micro)
     )
-    grad_w_in = scatter_rep(grad_in_expert)
-
-    def scatter_ranks(value):
-        value = lax.psum_scatter(value, "ep", scatter_dimension=0)
-        return [value[0]] + [exchange(value[step], share - step) for step in range(1, share)]
-
-    returned = [scatter_ranks(back[step][1]) for step in range(micro)]
+    in_cut = cut_rep(grad_in_expert)
+    in_sent = {}
+
+    def swap(value, step):
+        return lax.ppermute(value, "ep", [(i, i ^ step) for i in range(ranks)])
+
+    def pair_sum(value):
+        halves = value.reshape((ranks // 2, 2) + value.shape[1:])
+        keep = lax.dynamic_index_in_dim(halves, rank % 2, 1, keepdims=False)
+        give = lax.dynamic_index_in_dim(halves, 1 - rank % 2, 1, keepdims=False)
+        return (keep.astype(f32) + swap(give, 1).astype(f32)).astype(bf16)
+
+    def cross(value):
+        parts = []
+        for step in range(ranks // 2):
+            part = lax.dynamic_index_in_dim(value, rank // 2 ^ step, 0, keepdims=False)
+            parts.append(swap(part, 2 * step) if step else part)
+        return parts
+
+    def total(parts):
+        return sum(part.astype(f32) for part in parts)
+
     grad_inputs, branches, logit_grads = [], [], []
     gain_two_sum = gain_one_sum = qk_sum = qkv_sum = 0.0
     by_rank = stream.reshape(ranks, micro, rows, D)
+    in_cut, mixtures = lax.optimization_barrier((in_cut, [part[0] for part in back]))
+    mixtures = [pair_sum(part) for part in mixtures]
+    crossed = []
+    releases = [order[:1]] + [[]] * (micro - 2) + [order[1:]] if micro > 1 else [order]
     for step in range(micro):
         at = slice(step * rows, (step + 1) * rows)
+        parts, out_sent, in_sent, mixtures = lax.optimization_barrier(
+            (returned[step], out_sent, in_sent, mixtures)
+        )
+        parts = exchange_back(parts)
+        parts, in_cut = lax.optimization_barrier((parts, in_cut))
+        in_sent.update(send(in_cut, releases[step]))
         grad_hidden, grad_branch, grad_mixed, grad_logits, gain_two = hidden_backward(
-            returned[step], hidden[at], gates[at], cotangent[at], second_gain, router, out_weight,
-            experts,
+            parts, hidden[at], gates[at], cotangent[at], second_gain, router, out_weight, experts
         )
         branches.append(grad_branch)
         logit_grads.append(grad_logits)
         gain_two_sum = gain_two_sum + gain_two
         grad_mixed = lax.all_to_all(grad_mixed, "ep", split_axis=1, concat_axis=0, tiled=True)
+        if step == micro - 1:
+            crossed = [cross(part) for part in after(mixtures[:1], parts)]
+            grad_mixed, crossed, mixtures = lax.optimization_barrier(
+                (grad_mixed, crossed, mixtures)
+            )
+            crossed += [cross(part) for part in mixtures[1:]]
         grad_proj, grad_qk = attention_backward(
             step, proj, *tables, query, keys, values, lses, grad_mixed
         )
         qk_sum = qk_sum + grad_qk.reshape(-1)
         grad_normed, gain_one = project_backward(step, grad_proj, by_rank, slab)
         gain_one_sum = gain_one_sum + gain_one
+        grad_inputs.append(
+            (at, grad_hidden, lax.psum_scatter(grad_normed, "ep", scatter_dimension=0, tiled=True))
+        )
+        grad_proj = after(grad_proj, grad_normed)
         qkv_sum = qkv_sum + dot(
             normed.reshape(ranks, micro, rows, D)[:, step].reshape(length, D),
             grad_proj.reshape(length, 3 * width),
             ((0,), (0,)),
         )
-        grad_normed = lax.psum_scatter(
-            grad_normed, "ep", scatter_dimension=0, tiled=True
-        ).astype(f32)
-        own_stream = tokens[at].astype(f32)
-        own_inverse = inverse_rms(own_stream)
-        grad_inputs.append(
-            grad_hidden + rms_backward(own_stream, own_inverse, first_gain, grad_normed)
-        )
-    mixture = [
-        sum(part.astype(f32) for part in scatter_ranks(back[step][0])) for step in range(micro)
-    ]
-    output = (hidden + jnp.concatenate(mixture, axis=0)).astype(bf16)
-    out_sum = dot(mixed, jnp.concatenate(branches, axis=0), ((0,), (0,))).astype(bf16)
-    out_sum = out_sum.reshape(planes, ranks, dense_rows, D).transpose(1, 0, 2, 3)
-    out_sum = lax.psum_scatter(out_sum, "ep", scatter_dimension=0)
-    grad_w_o = lax.dynamic_index_in_dim(out_sum, plane, 0, keepdims=False).astype(f32)
-    for step in range(1, planes):
-        part = lax.dynamic_index_in_dim(out_sum, (plane + step) % planes, 0, keepdims=False)
-        grad_w_o = grad_w_o + shift_rep(part, step).astype(f32)
+    grad_w_out = sum_rep({0: out_cut[0], **out_sent})
+    grad_w_in = sum_rep({0: in_cut[0], **in_sent})
 
     router_sum = dot(normed_two, jnp.concatenate(logit_grads, axis=0), ((0,), (0,)))
     qk_columns = qk_sum.shape[0] // dense_rows
@@ -774,15 +817,38 @@
         tail = packed[..., split:]
         return packed[..., :split], tail[..., :count] + tail[..., count : 2 * count]
 
-    packed = pack(qkv_sum, small)
+    packed, crossed, branches = lax.optimization_barrier(
+        (pack(qkv_sum, small), crossed, branches)
+    )
     part_rows = D // planes
     main = lax.dynamic_slice_in_dim(qkv_sum, plane * part_rows, part_rows, 0)
     small = lax.dynamic_slice_in_dim(small, plane * part_rows, part_rows, 0)
-    for step in range(1, planes):
-        part = lax.dynamic_slice_in_dim(
-            packed, (plane + step) % planes * part_rows, part_rows, 0
-        )
-        part_main, part_small = unpack(shift_rep(part, step))
+    packed_sent = [
+        shift_rep(
+            lax.dynamic_slice_in_dim(packed, (plane + step) % planes * part_rows, part_rows, 0),
+            step,
+        )
+        for step in range(1, planes)
+    ]
+    out_sum = dot(mixed, jnp.concatenate(branches, axis=0), ((0,), (0,))).astype(bf16)
+    out_sum = out_sum.reshape(planes, ranks, dense_rows, D).transpose(1, 0, 2, 3)
+    out_crossed = cross(pair_sum(out_sum))
+    mixture = []
+    for parts in crossed:
+        parts = total(parts)
+        mixture.append(parts[0] + total(exchange_back(parts.astype(bf16))[1:]))
+    output = (hidden + jnp.concatenate(mixture, axis=0)).astype(bf16)
+    grad_tokens = []
+    for at, grad_hidden, grad_normed in grad_inputs:
+        own_stream = tokens[at].astype(f32)
+        grad_tokens.append(
+            grad_hidden
+            + rms_backward(
+                own_stream, inverse_rms(own_stream), first_gain, grad_normed.astype(f32)
+            )
+        )
+    for part in packed_sent:
+        part_main, part_small = unpack(part)
         main, small = main + part_main, small + part_small
     packed = pack(main, small).reshape(ranks, dense_rows, -1)
     packed = lax.all_to_all(packed, "ep", split_axis=0, concat_axis=0, tiled=True)
@@ -791,9 +857,15 @@
         main.reshape(ranks, dense_rows, 3, width).transpose(1, 2, 0, 3).reshape(dense_rows, 3 * D)
     )
     small = jnp.sum(small, axis=0)
+    out_sum = total(out_crossed)
+    grad_w_o = lax.dynamic_index_in_dim(out_sum, plane, 0, keepdims=False)
+    out_sum = out_sum.astype(bf16)
+    for step in range(1, planes):
+        part = lax.dynamic_index_in_dim(out_sum, (plane + step) % planes, 0, keepdims=False)
+        grad_w_o = grad_w_o + shift_rep(part, step).astype(f32)
     return (
         output,
-        jnp.concatenate(grad_inputs, axis=0),
+        jnp.concatenate(grad_tokens, axis=0),
         grad_w_qkv,
         grad_w_o,
         small[:, :experts],

time: 1490 us -> 1240 us (0.83)
  waiting for transfers between devices: 743 us -> 557 us
  Pallas kernels: 342 us -> 242 us
  blocking collectives: 49 us -> 15.8 us
  other arithmetic: 54.1 us -> 86.3 us
  local copies, waits for them, and re-layouts: 130 us -> 154 us
    ppermute x24, waiting for transfers between devices: 567 us -> 344 us  [shift_rep(): lax.ppermute(value, 'rep', [(i, (i + step) % count) for i in range(count)])]
    pallas_call x2, Pallas kernels: 156 us -> 79.5 us  [expert_backward(): pl.pallas_call(kernel, grid_spec=pltpu.PrefetchScalarGridSpec(num_scalar_...]
    ppermute x0 -> x12, waiting for transfers between devices: none -> 68.4 us  [swap(): return lax.ppermute(value, 'ep', [(i, i ^ step) for i in range(ranks)])]
    all_gather x4, waiting for transfers between devices: 44.1 us -> 0.03 us  [gather_ranks(): return lax.all_gather(value, 'ep', axis=0)]
    all_to_all x1 -> x0, blocking collectives: 27 us -> none  [on_device(): slab = lax.all_to_all(slab, 'ep', split_axis=0, concat_axis=0, tiled=True)]
    convert_element_type x0 -> x4, other arithmetic: none -> 24.3 us  [the longest x3 21.3 us: pair_sum(): return (keep.astype(f32) + swap(give, 1).astype(f32)).astype(bf16)]
    ppermute x6, waiting for transfers between devices: 68.9 us -> 91.5 us  [exchange(): return lax.ppermute(value, 'rep', pairs)]
    reduce_scatter x5 -> x2, waiting for transfers between devices: 22.3 us -> 0.01 us  [scatter_ranks(): return lax.psum_scatter(value, 'ep', scatter_dimension=0)]
  transfers between devices with their start and end apart: 44 -> 54, of which waited for: 23 -> 24; matrix products, arithmetic and copies ran while one was open for 16% -> 23% of each run, Pallas kernels for 14% -> 13%
where the time goes in v3:
time: 1240 us; the launch traced here: 1230 us
  waiting for transfers between devices  557 us (45%)
  Pallas kernels  242 us (20%)
  local copies, waits for them, and re-layouts  154 us (12%)
  starting transfers between devices  88.6 us (7%)
  other arithmetic  86.3 us (7%)
  matrix products  72.9 us (6%)
  blocking collectives  15.8 us (1%)
  between operations  15.3 us (1%)
    ppermute x24, waiting for transfers between devices, shift_rep(): lax.ppermute(value, 'rep', [(i, (i + step) % count) for i in range(count)])  344 us
    ppermute x6, waiting for transfers between devices, exchange(): return lax.ppermute(value, 'rep', pairs)  91.5 us
    pallas_call x2, Pallas kernels, expert_backward(): pl.pallas_call(kernel, grid_spec=pltpu.PrefetchScalarGridSpec(num_scalar_...  79.5 us
    dot_general x7, matrix products, dot(): return lax.dot_general(a, b, (dims, ((), ())), preferred_element_type=f32)  72.9 us
    ppermute x12, waiting for transfers between devices, swap(): return lax.ppermute(value, 'ep', [(i, i ^ step) for i in range(ranks)])  68.4 us
    ppermute x24, starting transfers between devices, shift_rep(): lax.ppermute(value, 'rep', [(i, (i + step) % count) for i in range(count)])  48.2 us
    pallas_call x1, Pallas kernels, expert_forward(): pl.pallas_call(kernel, grid_spec=pltpu.PrefetchScalarGridSpec(num_scalar_...  38.6 us
    pallas_call x2, Pallas kernels, attention_backward(): pl.pallas_call(lambda *refs: backward_kernel(heads, *refs), grid=(1,), in...  33.7 us
  transfers between devices with their start and end apart: 54, of which 24 were waited for; matrix products, arithmetic and copies ran while one was open for 23% of the time, Pallas kernels for 13%

profile of v3, /device:TPU:0, one launch (start us, length us, event | category | flops | bytes accessed | tf_op | source)
XLA Modules:
  0.0 1232.4 jit_solution(4849317940450209558)
XLA Ops:
  58.4 55.6 %collective-permute-done.9 = bf16[256,2048]{1,0:T(8,128)(2,1)S(1)} collective-permute-done((bf16[256,2048]{1,0:T(8,128)(2,1)S(1)}, bf16[256,2048]{1,0:T(8,128)(2,1)S(1)}, u32[]{:S(2)}, u32[]{:S(2)}) %collective-permute-start.9) | collective-permute-done | bytes 1048608 | tf_op jit(solution)/shard_map/ppermute | solution.py:584
  137.8 14.5 %shard_map.178 = (bf16[8,256,2048]{2,1,0:T(8,128)(2,1)}, f32[8,256,768]{2,1,0:T(8,128)}) custom-call(bf16[8,256,2048]{2,1,0:T(8,128)(2,1)} %bitcast.218, f32[1,2048]{1,0:T(1,128)S(1)} %broadcast_in_dim.67.gain, bf16[2048,896]{1,0:T(8,128)(2,1)} %constant_dynamic-update-slice_fusion.8.weight), custom_call_target="tpu_custom_call" | custom-call | tf_op jit(solution)/shard_map/pallas_call | solution.py:243
  169.0 21.7 %shard_map.179 = (bf16[8,2,128,256]{3,2,1,0:T(8,128)(2,1)}, bf16[2,1024,256]{2,1,0:T(8,128)(2,1)S(1)}, bf16[2,1024,256]{2,1,0:T(8,128)(2,1)S(1)}, bf16[2,1024,256]{2,1,0:T(8,128)(2,1)}, f32[2,2,1024,1]{3,2,1,0:T(8,128)}) custom-call(f32[8,2,128,768]{3,2,1,0:T(8,128)} %bitcast.221, f32[2,1024,128]{2,1,0:T(8,128)} %get-tuple-element.316.refs_1_, ...), custom_call_target="tpu_custom_call" | custom-call | tf_op jit(solution)/shard_map/pallas_call | solution.py:194
  208.8 25.2 %all-to-all-done.1 = bf16[8,2,128,256]{3,2,1,0:T(8,128)(2,1)S(1)} async-done(((bf16[8,2,128,256]{3,2,1,0:T(8,128)(2,1)}), bf16[8,2,128,256]{3,2,1,0:T(8,128)(2,1)S(1)}, u32[]{:S(2)}, u32[]{:S(2)}) %all-to-all-start.1) | async-done | bytes 1048608 | tf_op jit(solution)/shard_map/all_to_all | solution.py:646
  247.2 21.6 %collective-permute-done.8 = bf16[256,2176]{1,0:T(8,128)(2,1)S(1)} collective-permute-done((bf16[256,2176]{1,0:T(8,128)(2,1)S(1)}, bf16[256,2176]{1,0:T(8,128)(2,1)S(1)}, u32[]{:S(2)}, u32[]{:S(2)}) %collective-permute-start.8) | collective-permute-done | bytes 1114144 | tf_op jit(solution)/shard_map/ppermute | solution.py:584
  296.1 160.2 %collective-permute-done.12 = bf16[256,2048]{1,0:T(8,128)(2,1)S(1)} collective-permute-done((bf16[256,2048]{1,0:T(8,128)(2,1)S(1)}, bf16[256,2048]{1,0:T(8,128)(2,1)S(1)}, u32[]{:S(2)}, u32[]{:S(2)}) %collective-permute-start.12) | collective-permute-done | bytes 1048608 | tf_op jit(solution)/shard_map/ppermute | solution.py:535
  463.0 38.6 %shard_map.181 = (bf16[2,4,288,2048]{3,2,1,0:T(8,128)(2,1)}, f32[2,4,288,128]{3,2,1,0:T(8,128)S(1)}, f32[2,4,288,2048]{3,2,1,0:T(8,128)}, bf16[2,4,288,1024]{3,2...) custom-call(s32[1]{0:T(128)} %bitcast.19.expert, ...), custom_call_target="tpu_custom_call" | custom-call | tf_op jit(solution)/shard_map/pallas_call | solution.py:361
  501.6 14.5 %convolution_bitcast_fusion = f32[1024,2048]{1,0:T(8,128)S(1)} fusion(bf16[2,4,288,1024]{3,2,1,0:T(8,128)(2,1)} %get-tuple-element.153.active, bf16[2,4,288,2048]{3,2,1,0:T(8,128)(2,1)} %get-tuple-element.154.grad_produced), kind=kOutput, calls=%fused_computation.9 | convolution fusion | flops 9663676416 | bytes 22544384 | tf_op jit(solution)/shard_map/dot_general | solution.py:25
  519.4 38.9 %shard_map.182 = (bf16[8,2,128,2048]{3,2,1,0:T(8,128)(2,1)}, bf16[8,2,128,2176]{3,2,1,0:T(8,128)(2,1)}, bf16[4,288,2048]{2,1,0:T(8,128)(2,1)}) custom-call(s32[1]{0:T(128)} %bitcast.19.expert, f32[2,4,288,128]{3,2,1,0:T(8,128)S(1)} %get-tuple-element.151.tail, f32[2,4,288,2048]{3,2,1,0:T(8,128)} %get-tuple-element.152.both, ...), custom_call_target="tpu_custom_call" | custom-call | tf_op jit(solution)/shard_map/pallas_call | solution.py:442
  558.3 21.0 %collective-permute-start.14 = (bf16[256,2048]{1,0:T(8,128)(2,1)}, bf16[256,2048]{1,0:T(8,128)(2,1)}, u32[]{:S(2)}, u32[]{:S(2)}) collective-permute-start(bf16[256,2048]{1,0:T(8,128)(2,1)} %get-tuple-element.163), channel_id=1, source_target_pairs={{0,8},{8,16},{16,24},{24,0},{1,9},{9,17},{17,25},{25,1},{2,10},{10... | collective-permute-start | bytes 3145736 | tf_op jit(solution)/shard_map/ppermute | solution.py:535
  582.2 40.6 %shard_map.183 = (bf16[8,2,128,2048]{3,2,1,0:T(8,128)(2,1)}, bf16[8,2,128,2176]{3,2,1,0:T(8,128)(2,1)}, bf16[4,288,2048]{2,1,0:T(8,128)(2,1)}) custom-call(s32[1]{0:T(128)} %bitcast.19.expert, f32[2,4,288,128]{3,2,1,0:T(8,128)S(1)} %copy-done.11, f32[2,4,288,2048]{3,2,1,0:T(8,128)} %get-tuple-element.152.both, ...), custom_call_target="tpu_custom_call" | custom-call | tf_op jit(solution)/shard_map/pallas_call | solution.py:442
  633.5 17.8 %fusion.50 = f32[2048,2048]{1,0:T(8,128)} fusion(bf16[1152,2048]{1,0:T(8,128)(2,1)} %bitcast.238, bf16[1152,2048]{1,0:T(8,128)(2,1)} %bitcast.265), kind=kOutput, calls=%fused_computation.182 | convolution fusion | flops 9663676416 | bytes 26214400 | tf_op jit(solution)/shard_map/dot_general | solution.py:25
  651.3 19.4 %convolution_add_fusion = f32[2048,2048]{1,0:T(8,128)} fusion(f32[2048,2048]{1,0:T(8,128)} %fusion.50, bf16[1152,2048]{1,0:T(8,128)(2,1)S(1)} %bitcast.237, bf16[1152,2048]{1,0:T(8,128)(2,1)} %bitcast.264), kind=kOutput, calls=%fused_computation.7 | convolution fusion | flops 9667870720 | bytes 42991616 | tf_op jit(solution)/shard_map/dot_general | solution.py:25
  710.1 31.6 %collective-permute-done.16 = bf16[256,2048]{1,0:T(8,128)(2,1)S(1)} collective-permute-done((bf16[256,2048]{1,0:T(8,128)(2,1)}, bf16[256,2048]{1,0:T(8,128)(2,1)S(1)}, u32[]{:S(2)}, u32[]{:S(2)}) %collective-permute-start.16) | collective-permute-done | bytes 1048608 | tf_op jit(solution)/shard_map/ppermute | solution.py:535
  768.1 15.8 %all_to_all.63 = bf16[128,8,256]{2,0,1:T(8,128)(2,1)S(1)} all-to-all(bf16[128,8,256]{2,0,1:T(8,128)(2,1)S(1)} %bitcast.252), channel_id=1, replica_groups=mesh['rep'=4,'ep'=8] {'ep'}, dimensions={1} | all-to-all | bytes 1048576 | tf_op jit(solution)/shard_map/all_to_all | solution.py:772
  783.9 16.7 %shard_map.185 = (bf16[8,128,768]{2,1,0:T(8,128)(2,1)}, f32[2,128]{1,0:T(2,128)S(1)}) custom-call(f32[8,2,128,768]{3,2,1,0:T(8,128)} %bitcast.222, f32[2,1024,128]{2,1,0:T(8,128)S(1)} %copy-done.3, f32[2,1024,128]{2,1,0:T(8,128)S(1)} %copy-done.2, s32[2,1024,1]{2,1,0:T(8,128)S(1)} %copy-done.1, s32[2,1,1024]{2,1,0:T(1,128)S(1)} %copy-done.26, ...), custom_call_target="tpu_custom_call" | custom-call | tf_op jit(solution)/shard_map/pallas_call | solution.py:216
  824.2 40.6 %collective-permute-done.20 = bf16[512,2048]{1,0:T(8,128)(2,1)} collective-permute-done((bf16[512,2048]{1,0:T(8,128)(2,1)}, bf16[512,2048]{1,0:T(8,128)(2,1)}, u32[]{:S(2)}, u32[]{:S(2)}) %collective-permute-start.20) | collective-permute-done | bytes 2097184 | tf_op jit(solution)/shard_map/ppermute | solution.py:535
  910.7 24.0 %all-to-all-done.3 = bf16[128,8,256]{2,0,1:T(8,128)(2,1)} async-done(((bf16[128,8,256]{2,0,1:T(8,128)(2,1)}), bf16[128,8,256]{2,0,1:T(8,128)(2,1)}, u32[]{:S(2)}, u32[]{:S(2)}) %all-to-all-start.3) | async-done | bytes 524320 | tf_op jit(solution)/shard_map/all_to_all | solution.py:772
  935.9 17.0 %shard_map.188 = (bf16[8,128,768]{2,1,0:T(8,128)(2,1)}, f32[2,128]{1,0:T(2,128)S(1)}) custom-call(f32[8,2,128,768]{3,2,1,0:T(8,128)} %bitcast.223, f32[2,1024,128]{2,1,0:T(8,128)S(1)} %copy-done.4, f32[2,1024,128]{2,1,0:T(8,128)S(1)} %copy-done.2, s32[2,1024,1]{2,1,0:T(8,128)S(1)} %copy-done.1, s32[2,1,1024]{2,1,0:T(1,128)S(1)} %copy-done.26, ...), custom_call_target="tpu_custom_call" | custom-call | tf_op jit(solution)/shard_map/pallas_call | solution.py:216
  954.3 13.9 %shard_map.189 = (bf16[1024,2048]{1,0:T(8,128)(2,1)}, f32[1,2048]{1,0:T(1,128)S(1)}) custom-call(bf16[8,128,768]{2,1,0:T(8,128)(2,1)S(1)} %copy-done.17, bf16[8,2,128,2048]{3,2,1,0:T(8,128)(2,1)} %bitcast.220, bf16[2048,896]{1,0:T(8,128)(2,1)} %constant_dynamic-update-slice_fusion.8.weight), custom_call_target="tpu_custom_call" | custom-call | tf_op jit(solution)/shard_map/pallas_call | solution.py:519
  1007.0 23.2 %collective-permute-done.27 = bf16[2,128,2048]{2,1,0:T(8,128)(2,1)} collective-permute-done((bf16[2,128,2048]{2,1,0:T(8,128)(2,1)}, bf16[2,128,2048]{2,1,0:T(8,128)(2,1)}, u32[]{:S(2)}, u32[]{:S(2)}) %collective-permute-start.27) | collective-permute-done | bytes 1048608 | tf_op jit(solution)/shard_map/ppermute | solution.py:733
  1062.3 15.6 %collective-permute-done.32 = bf16[512,896]{0,1:T(8,128)(2,1)S(1)} collective-permute-done((bf16[512,896]{0,1:T(8,128)(2,1)S(1)}, bf16[512,896]{0,1:T(8,128)(2,1)S(1)}, u32[]{:S(2)}, u32[]{:S(2)}) %collective-permute-start.32) | collective-permute-done | bytes 917536 | tf_op jit(solution)/shard_map/ppermute | solution.py:535
  1078.2 47.8 %collective-permute-done.31 = bf16[512,896]{0,1:T(8,128)(2,1)} collective-permute-done((bf16[512,896]{0,1:T(8,128)(2,1)S(1)}, bf16[512,896]{0,1:T(8,128)(2,1)}, u32[]{:S(2)}, u32[]{:S(2)}) %collective-permute-start.31) | collective-permute-done | bytes 917536 | tf_op jit(solution)/shard_map/ppermute | solution.py:535
  1174.2 22.0 %collective-permute-done.35 = bf16[4,64,2048]{2,1,0:T(8,128)(2,1)} collective-permute-done((bf16[4,64,2048]{2,1,0:T(8,128)(2,1)}, bf16[4,64,2048]{2,1,0:T(8,128)(2,1)}, u32[]{:S(2)}, u32[]{:S(2)}) %collective-permute-start.35) | collective-permute-done | bytes 1048608 | tf_op jit(solution)/shard_map/ppermute | solution.py:733
  (373 shorter events, 459.4 us)
Async XLA Ops:
  7.2 130.6 %all-gather.10.cloned.1.call-start = ((), (), s32[]{:S(2)}) async-start(), calls=%async_computation.14 | async-start | bytes 9437184 | tf_op jit(solution)/shard_map/all_gather | solution.py:590
  18.6 174.1 %all-gather.8.cloned.1.call-start = ((), (), s32[]{:S(2)}) async-start(), calls=%async_computation.9 | async-start | bytes 9437184 | tf_op jit(solution)/shard_map/all_gather | solution.py:590
  44.8 418.1 %all-gather.14.cloned.1.call-start = ((), (), s32[]{:S(2)}) async-start(), calls=%async_computation.16 | async-start | bytes 18874368 | tf_op jit(solution)/shard_map/all_gather | solution.py:590
  44.9 69.1 %collective-permute-start.9 = (bf16[256,2048]{1,0:T(8,128)(2,1)S(1)}, bf16[256,2048]{1,0:T(8,128)(2,1)S(1)}, u32[]{:S(2)}, u32[]{:S(2)}) collective-permute-start(bf16[256,2048]{1,0:T(8,128)(2,1)S(1)} %copy-done.49), channel_id=1, source_target_pairs={{0,8},{8,0},{16,24},{24,16},{1,9},{9,1},{17,25},{25,17},{2,10},{10... | collective-permute-start | bytes 3145736 | tf_op jit(solution)/shard_map/ppermute | solution.py:584
  50.7 64.8 %collective-permute-start.3 = (bf16[512,896]{1,0:T(8,128)(2,1)S(1)}, bf16[512,896]{1,0:T(8,128)(2,1)}, u32[]{:S(2)}, u32[]{:S(2)}) collective-permute-start(bf16[512,896]{1,0:T(8,128)(2,1)S(1)} %bitcast.246), channel_id=1, source_target_pairs={{0,8},{8,16},{16,24},{24,0},{1,9},{9,17},{17,25},{25,1},{2,10},{10... | collective-permute-start | bytes 2752520 | tf_op jit(solution)/shard_map/ppermute | solution.py:535
  50.7 66.9 %collective-permute-start.4 = (bf16[512,896]{1,0:T(8,128)(2,1)S(1)}, bf16[512,896]{1,0:T(8,128)(2,1)}, u32[]{:S(2)}, u32[]{:S(2)}) collective-permute-start(bf16[512,896]{1,0:T(8,128)(2,1)S(1)} %bitcast.247), channel_id=1, source_target_pairs={{0,16},{8,24},{16,0},{24,8},{1,17},{9,25},{17,1},{25,9},{2,18},{10... | collective-permute-start | bytes 2752520 | tf_op jit(solution)/shard_map/ppermute | solution.py:535
  52.4 80.7 %collective-permute-start.5 = (bf16[512,896]{1,0:T(8,128)(2,1)S(1)}, bf16[512,896]{1,0:T(8,128)(2,1)}, u32[]{:S(2)}, u32[]{:S(2)}) collective-permute-start(bf16[512,896]{1,0:T(8,128)(2,1)S(1)} %bitcast.248), channel_id=1, source_target_pairs={{0,24},{8,0},{16,8},{24,16},{1,25},{9,1},{17,9},{25,17},{2,26},{10... | collective-permute-start | bytes 2752520 | tf_op jit(solution)/shard_map/ppermute | solution.py:535
  158.4 85.4 %collective-permute-start.6 = (bf16[512,2048]{1,0:T(8,128)(2,1)}, bf16[512,2048]{1,0:T(8,128)(2,1)}, u32[]{:S(2)}, u32[]{:S(2)}) collective-permute-start(bf16[512,2048]{1,0:T(8,128)(2,1)} %get-tuple-element.291), channel_id=1, source_target_pairs={{0,8},{8,16},{16,24},{24,0},{1,9},{9,17},{17,25},{25,1},{2,10},{10... | collective-permute-start | bytes 6291464 | tf_op jit(solution)/shard_map/ppermute | solution.py:535
  166.8 77.0 %collective-permute-start.7 = (bf16[256,2048]{1,0:T(8,128)(2,1)}, bf16[256,2048]{1,0:T(8,128)(2,1)}, u32[]{:S(2)}, u32[]{:S(2)}) collective-permute-start(bf16[256,2048]{1,0:T(8,128)(2,1)} %get-tuple-element.300), channel_id=1, source_target_pairs={{0,8},{8,16},{16,24},{24,0},{1,9},{9,17},{17,25},{25,1},{2,10},{10... | collective-permute-start | bytes 3145736 | tf_op jit(solution)/shard_map/ppermute | solution.py:535
  207.2 255.8 %all-gather.12.cloned.1.call-start = ((), (), s32[]{:S(2)}) async-start(), calls=%async_computation.15 | async-start | bytes 20054016 | tf_op jit(solution)/shard_map/all_gather | solution.py:590
  270.4 471.4 %reduce-scatter.5.cloned.1.call-start = ((), (), s32[]{:S(2)}) async-start(), calls=%async_computation.10 | async-start | bytes 10027008 | tf_op jit(solution)/shard_map/reduce_scatter | solution.py:704
  275.4 182.9 %collective-permute-start.10 = (bf16[512,2048]{1,0:T(8,128)(2,1)}, bf16[512,2048]{1,0:T(8,128)(2,1)}, u32[]{:S(2)}, u32[]{:S(2)}) collective-permute-start(bf16[512,2048]{1,0:T(8,128)(2,1)} %get-tuple-element.290), channel_id=1, source_target_pairs={{0,16},{8,24},{16,0},{24,8},{1,17},{9,25},{17,1},{25,9},{2,18},{10... | collective-permute-start | bytes 6291464 | tf_op jit(solution)/shard_map/ppermute | solution.py:535
  276.5 185.0 %collective-permute-start.11 = (bf16[512,2048]{1,0:T(8,128)(2,1)}, bf16[512,2048]{1,0:T(8,128)(2,1)S(1)}, u32[]{:S(2)}, u32[]{:S(2)}) collective-permute-start(bf16[512,2048]{1,0:T(8,128)(2,1)} %get-tuple-element.289), channel_id=1, source_target_pairs={{0,24},{8,0},{16,8},{24,16},{1,25},{9,1},{17,9},{25,17},{2,26},{10... | collective-permute-start | bytes 6291464 | tf_op jit(solution)/shard_map/ppermute | solution.py:535
  279.8 176.5 %collective-permute-start.12 = (bf16[256,2048]{1,0:T(8,128)(2,1)S(1)}, bf16[256,2048]{1,0:T(8,128)(2,1)S(1)}, u32[]{:S(2)}, u32[]{:S(2)}) collective-permute-start(bf16[256,2048]{1,0:T(8,128)(2,1)S(1)} %get-tuple-element.299), channel_id=1, source_target_pairs={{0,16},{8,24},{16,0},{24,8},{1,17},{9,25},{17,1},{25,9},{2,18},{10... | collective-permute-start | bytes 3145736 | tf_op jit(solution)/shard_map/ppermute | solution.py:535
  283.4 173.9 %collective-permute-start.13 = (bf16[256,2048]{1,0:T(8,128)(2,1)S(1)}, bf16[256,2048]{1,0:T(8,128)(2,1)S(1)}, u32[]{:S(2)}, u32[]{:S(2)}) collective-permute-start(bf16[256,2048]{1,0:T(8,128)(2,1)S(1)} %get-tuple-element.298), channel_id=1, source_target_pairs={{0,24},{8,0},{16,8},{24,16},{1,25},{9,1},{17,9},{25,17},{2,26},{10... | collective-permute-start | bytes 3145736 | tf_op jit(solution)/shard_map/ppermute | solution.py:535
  558.2 265.9 %reduce-scatter.7.cloned.1.call-start = ((), (), s32[]{:S(2)}) async-start(), calls=%async_computation.11 | async-start | bytes 10027008 | tf_op jit(solution)/shard_map/reduce_scatter | solution.py:704
  622.9 579.2 %reduce-scatter.9.cloned.1.call-start = ((), (), s32[]{:S(2)}) async-start(), calls=%async_computation.12 | async-start | bytes 4718592 | tf_op jit(solution)/shard_map/reduce_scatter | solution.py:786
  903.7 298.3 %reduce-scatter.11.cloned.1.call-start = ((), (), s32[]{:S(2)}) async-start(), calls=%async_computation.13 | async-start | bytes 4718592 | tf_op jit(solution)/shard_map/reduce_scatter | solution.py:786
  908.6 140.2 %collective-permute-start.41 = (bf16[512,2048]{1,0:T(8,128)(2,1)}, bf16[512,2048]{1,0:T(8,128)(2,1)}, u32[]{:S(2)}, u32[]{:S(2)}) collective-permute-start(bf16[512,2048]{1,0:T(8,128)(2,1)} %get-tuple-element.240), channel_id=1, source_target_pairs={{0,24},{8,0},{16,8},{24,16},{1,25},{9,1},{17,9},{25,17},{2,26},{10... | collective-permute-start | bytes 6291464 | tf_op jit(solution)/shard_map/ppermute | solution.py:535
  909.6 141.0 %collective-permute-start.40 = (bf16[512,2048]{1,0:T(8,128)(2,1)}, bf16[512,2048]{1,0:T(8,128)(2,1)}, u32[]{:S(2)}, u32[]{:S(2)}) collective-permute-start(bf16[512,2048]{1,0:T(8,128)(2,1)} %get-tuple-element.238), channel_id=1, source_target_pairs={{0,16},{8,24},{16,0},{24,8},{1,17},{9,25},{17,1},{25,9},{2,18},{10... | collective-permute-start | bytes 6291464 | tf_op jit(solution)/shard_map/ppermute | solution.py:535
  1042.7 94.5 %collective-permute-start.33 = (bf16[4,4,64,2048]{3,2,1,0:T(8,128)(2,1)}, bf16[4,4,64,2048]{3,2,1,0:T(8,128)(2,1)}, u32[]{:S(2)}, u32[]{:S(2)}) collective-permute-start(bf16[4,4,64,2048]{3,2,1,0:T(8,128)(2,1)} %bitcast.200), channel_id=1, source_target_pairs={{0,1},{1,0},{2,3},{3,2},{4,5},{5,4},{6,7},{7,6},{8,9},{9,8},{10,11... | collective-permute-start | bytes 12582920 | tf_op jit(solution)/shard_map/ppermute | solution.py:733
  1048.9 77.1 %collective-permute-start.31 = (bf16[512,896]{0,1:T(8,128)(2,1)S(1)}, bf16[512,896]{0,1:T(8,128)(2,1)}, u32[]{:S(2)}, u32[]{:S(2)}) collective-permute-start(bf16[512,896]{0,1:T(8,128)(2,1)S(1)} %get-tuple-element.295), channel_id=1, source_target_pairs={{0,16},{8,24},{16,0},{24,8},{1,17},{9,25},{17,1},{25,9},{2,18},{10... | collective-permute-start | bytes 2752520 | tf_op jit(solution)/shard_map/ppermute | solution.py:535
  1050.6 76.8 %collective-permute-start.30 = (bf16[512,896]{0,1:T(8,128)(2,1)S(1)}, bf16[512,896]{0,1:T(8,128)(2,1)}, u32[]{:S(2)}, u32[]{:S(2)}) collective-permute-start(bf16[512,896]{0,1:T(8,128)(2,1)S(1)} %get-tuple-element.293), channel_id=1, source_target_pairs={{0,8},{8,16},{16,24},{24,0},{1,9},{9,17},{17,25},{25,1},{2,10},{10... | collective-permute-start | bytes 2752520 | tf_op jit(solution)/shard_map/ppermute | solution.py:535
  1059.5 88.4 %collective-permute-start.28 = (bf16[128,2048]{1,0:T(8,128)(2,1)}, bf16[128,2048]{1,0:T(8,128)(2,1)S(1)}, u32[]{:S(2)}, u32[]{:S(2)}) collective-permute-start(bf16[128,2048]{1,0:T(8,128)(2,1)} %fusion.25), channel_id=1, source_target_pairs={{0,8},{8,0},{16,24},{24,16},{1,9},{9,1},{17,25},{25,17},{2,10},{10... | collective-permute-start | bytes 1572872 | tf_op jit(solution)/shard_map/ppermute | solution.py:584
  (92 other events, 1756.4 us)
Sparse Core Ops, SparseCore 0:
  9.9 65.4 all-gather.9
  77.2 54.3 all-gather.7
  152.4 102.4 all-gather.13
  270.5 93.6 all-gather.11
  558.4 95.8 reduce-scatter.4
  657.7 73.7 reduce-scatter.6
  816.0 49.9 reduce-scatter.8
  976.3 68.2 reduce-scatter.10

commit v4 on v3

--- a/solution.py
+++ b/solution.py
@@ -177,6 +177,10 @@
 
 def params():
     return pltpu.CompilerParams(vmem_limit_bytes=BIG)
+
+
+def cost(products):
+    return pl.CostEstimate(flops=2 * products, bytes_accessed=0, transcendentals=0)
 
 
 def out(shape, dtype=bf16):
@@ -230,8 +234,8 @@
     )
 
 
-def project(tokens, gain, slab):
-    ranks, count, _ = tokens.shape
+def project(count, tokens, gain, slab):
+    ranks = tokens.shape[0]
     width = slab.shape[1] - PAD
 
     def kernel(value, gain, weight, normed, proj):
@@ -243,7 +247,7 @@
     return pl.pallas_call(
         kernel,
         grid=(ranks,),
-        in_specs=[leading(tokens.shape), fixed((1, D)), fixed(slab.shape)],
+        in_specs=[leading((ranks, count, D)), fixed((1, D)), fixed(slab.shape)],
         out_specs=[leading((ranks, count, D)), leading((ranks, count, width))],
         out_shape=[out((ranks, count, D)), out((ranks, count, width), f32)],
         compiler_params=params(),
@@ -261,10 +265,56 @@
     return pl.ds(pl.multiple_of(number * TILE, TILE), TILE)
 
 
-def route(mixed, tokens, out_weight, gain, router, routes, experts):
+HBM = pl.BlockSpec(memory_space=pl.ANY)
+
+
+def copies(pairs, sems):
+    started = [
+        pltpu.make_async_copy(source, target, sems.at[place])
+        for place, (source, target) in enumerate(pairs)
+    ]
+    for copy in started:
+        copy.start()
+
+    def wait():
+        for copy in started:
+            copy.wait()
+
+    return wait
+
+
+def plane_pairs(plane, pieces, target):
+    planes = len(pieces)
+    rows = target.shape[0] // planes
+    return [
+        (piece, target.at[pl.ds((plane + planes - step) % planes * rows, rows)])
+        for step, piece in enumerate(pieces)
+    ]
+
+
+def out_weight_pairs(plane, planes, count, gathered, target):
+    ranks = gathered.shape[0]
+    rows = D // (planes * ranks)
+    return [
+        (
+            gathered.at[rank, pl.ds(count + step * rows, rows)],
+            target.at[pl.ds(((plane + planes - step) % planes * ranks + rank) * rows, rows)],
+        )
+        for rank in range(ranks)
+        for step in range(planes)
+    ]
+
+
+def route(plane, planes, mixed, tokens, gathered, gain, router, routes, experts):
     count = tokens.shape[0]
-
-    def kernel(mixed, tokens, out_weight, gain, router, routes, hidden, payload, gates):
+    pieces = planes * gathered.shape[0]
+
+    def kernel(
+        plane, mixed, tokens, gathered, gain, router, routes, hidden, payload, gates,
+        out_weight, sems,
+    ):
+        copies(out_weight_pairs(plane[0], planes, count, gathered, out_weight), sems)()
+
         @tiles(D)
         def _(number):
             at = tile(number)
@@ -286,11 +336,22 @@
         high = weights.astype(bf16).astype(f32)
         payload[:, D:] = (high + pltpu.roll(weights - high, experts, 1)).astype(bf16)
 
+    shapes = [out((count, D), f32), out((count, D + PAD)), out((count, PAD), f32)]
     return pl.pallas_call(
         kernel,
-        out_shape=[out((count, D), f32), out((count, D + PAD)), out((count, PAD), f32)],
+        grid_spec=pltpu.PrefetchScalarGridSpec(
+            num_scalar_prefetch=1,
+            grid=(1,),
+            in_specs=[
+                HBM if value is gathered else fixed(value.shape)
+                for value in (mixed, tokens, gathered, gain, router, routes)
+            ],
+            out_specs=[fixed(shape.shape) for shape in shapes],
+            scratch_shapes=[pltpu.VMEM((D, D), bf16), pltpu.SemaphoreType.DMA((pieces,))],
+        ),
+        out_shape=shapes,
         compiler_params=params(),
-    )(mixed, tokens, out_weight, gain, router, routes)
+    )(plane, mixed, tokens, gathered, gain, router, routes)
 
 
 def lane(value, number):
@@ -303,16 +364,23 @@
     return (place == slot).astype(bf16)
 
 
-def expert_forward(expert, payload, upstream, in_weight, slots, experts):
+def expert_forward(where, payload, upstream, in_pieces, slots, experts):
     ranks, share, micro, rows, _ = payload.shape
     count = share * rows
     block = 2 * slots
 
-    def kernel(
-        expert, payload, upstream, in_weight, rows_in, tail, both, active, grad_produced,
-        up_rows, places,
-    ):
-        number = expert[0]
+    planes = len(in_pieces)
+
+    def kernel(where, payload, upstream, *refs):
+        (
+            rows_in, tail, both, active, grad_produced, up_rows, places, in_weight, sems
+        ) = refs[planes:]
+        number = where[0]
+
+        @pl.when((pl.program_id(0) == 0) & (pl.program_id(1) == 0))
+        def _():
+            copies(plane_pairs(where[1], refs[:planes], in_weight), sems)()
+
         for part in range(2):
             here = slice(part * slots, (part + 1) * slots)
             value = payload[part].reshape(count, D + PAD)
@@ -363,46 +431,63 @@
         grid_spec=pltpu.PrefetchScalarGridSpec(
             num_scalar_prefetch=1,
             grid=(micro, pairs),
-            in_specs=[tokens_spec(D + PAD), tokens_spec(D), fixed(in_weight.shape)],
+            in_specs=[tokens_spec(D + PAD), tokens_spec(D)] + [HBM] * planes,
             out_specs=[
                 pl.BlockSpec(
                     (1, 1) + s.shape[2:], lambda m, b, _, n=len(s.shape): (m, b) + (0,) * (n - 2)
                 )
                 for s in shapes
             ],
+            scratch_shapes=[pltpu.VMEM((D, 2 * FF), bf16), pltpu.SemaphoreType.DMA((planes,))],
         ),
         out_shape=shapes,
+        cost_estimate=cost(micro * pairs * block * D * (2 * FF + 2 * count)),
         compiler_params=params(),
-    )(expert, payload, upstream, in_weight)
+    )(where, payload, upstream, *in_pieces)
 
 
 def expert_backward(
-    step, expert, tail, both, active, grad_produced, up_rows, places, in_weight, out_weight,
+    step, where, tail, both, active, grad_produced, up_rows, places, in_pieces, out_pieces,
     share, rows, experts,
 ):
     pairs, block = tail.shape[1:3]
     slots = block // 2
     count = places.shape[3]
 
-    def kernel(
-        expert, tail, both, active, grad_produced, up_rows, places, in_weight, out_weight,
-        mixture, grad_tokens, grad_both,
-    ):
-        number = expert[0]
+    planes = len(in_pieces)
+
+    def kernel(where, tail, both, active, grad_produced, up_rows, places, *refs):
+        keep, give, grad_tokens, grad_both, in_weight, out_weight, sems = refs[2 * planes :]
+        number = where[0]
+        odd = where[2] == 1
+
+        @pl.when(pl.program_id(0) == 0)
+        def _():
+            copies(
+                plane_pairs(where[1], refs[:planes], in_weight)
+                + plane_pairs(where[1], refs[planes : 2 * planes], out_weight),
+                sems,
+            )()
+
         gate = lane(tail[0, 0], number) + lane(tail[0, 0], experts + number)
         place = lax.broadcasted_iota(jnp.int32, (count, slots), 1).astype(f32)
         selects = [(places[0, 0, part][:, 0:1] == place).astype(bf16) for part in range(2)]
 
-        def spread(target, at, value):
-            for part in range(2):
-                result = dot(selects[part], value[part * slots : (part + 1) * slots])
-                target[part, :, :, at] = result.astype(bf16).reshape(share, rows, -1)
+        def spread(value):
+            return [
+                dot(selects[part], value[part * slots : (part + 1) * slots])
+                .astype(bf16)
+                .reshape(share, rows, -1)
+                for part in range(2)
+            ]
 
         grad_gate = jnp.zeros((block, 1), f32)
         for tile in range(D // TILE):
             at = slice(tile * TILE, (tile + 1) * TILE)
             produced = dot(active[0, 0], out_weight[:, at]).astype(bf16).astype(f32)
-            spread(mixture, at, (gate * produced).astype(bf16))
+            even_rank, odd_rank = spread((gate * produced).astype(bf16))
+            keep[0, :, :, at] = jnp.where(odd, odd_rank, even_rank)
+            give[0, :, :, at] = jnp.where(odd, even_rank, odd_rank)
             grad_gate = grad_gate + jnp.sum(
                 up_rows[0, 0, :, at].astype(f32) * produced, axis=1, keepdims=True
             )
@@ -423,21 +508,21 @@
         for tile in range(D // TILE):
             at = slice(tile * TILE, (tile + 1) * TILE)
             grad_rows = dot(grad_both[0], in_weight[at, :], ((1,), (1,))).astype(bf16)
-            spread(grad_tokens, at, grad_rows)
+            grad_tokens[0, :, :, at], grad_tokens[1, :, :, at] = spread(grad_rows)
 
         high = grad_gate.astype(bf16).astype(f32)
         column = lax.broadcasted_iota(jnp.int32, (block, PAD), 1)
         extra = jnp.where(column == number, high, 0.0)
         extra = jnp.where(column == experts + number, grad_gate - high, extra)
-        spread(grad_tokens, slice(D, D + PAD), extra.astype(bf16))
+        grad_tokens[0, :, :, D:], grad_tokens[1, :, :, D:] = spread(extra.astype(bf16))
 
     def part(value):
         return pl.BlockSpec(
             (1, 1) + value.shape[2:], lambda b, _: (step, b) + (0,) * (value.ndim - 2)
         )
 
-    def tokens_spec(width):
-        return pl.BlockSpec((2, share, rows, width), lambda b, _: (b, 0, 0, 0))
+    def tokens_spec(count, width):
+        return pl.BlockSpec((count, share, rows, width), lambda b, _: (b, 0, 0, 0))
 
     return pl.pallas_call(
         kernel,
@@ -445,32 +530,78 @@
             num_scalar_prefetch=1,
             grid=(pairs,),
             in_specs=[part(v) for v in (tail, both, active, grad_produced, up_rows, places)]
-            + [fixed(in_weight.shape), fixed(out_weight.shape)],
+            + [HBM] * (2 * planes),
             out_specs=[
-                tokens_spec(D),
-                tokens_spec(D + PAD),
+                tokens_spec(1, D),
+                tokens_spec(1, D),
+                tokens_spec(2, D + PAD),
                 pl.BlockSpec((1, block, 2 * FF), lambda b, _: (b, 0, 0)),
+            ],
+            scratch_shapes=[
+                pltpu.VMEM((D, 2 * FF), bf16),
+                pltpu.VMEM((FF, D), bf16),
+                pltpu.SemaphoreType.DMA((2 * planes,)),
             ],
         ),
         out_shape=[
-            out((2 * pairs, share, rows, D)),
+            out((pairs, share, rows, D)),
+            out((pairs, share, rows, D)),
             out((2 * pairs, share, rows, D + PAD)),
             out((pairs, block, 2 * FF)),
         ],
+        cost_estimate=cost(pairs * block * D * (4 * FF + 2 * count)),
         compiler_params=params(),
     )(
-        expert, tail, both, active, grad_produced, up_rows, places, in_weight, out_weight
-    )
-
-
-def hidden_backward(parts, hidden, gates, upstream, gain, router, out_weight, experts):
+        where, tail, both, active, grad_produced, up_rows, places, *in_pieces, *out_pieces
+    )
+
+
+def weight_gradient(where, planes, left, rights):
+    count, width = left.shape
+    parts = len(rights)
+    part_rows = count // parts
+    columns = rights[0].shape[1]
+    width = width // planes
+
+    def kernel(where, left, *refs):
+        rights, target = refs[:parts], refs[parts]
+        for number in range(columns // TILE):
+            at = slice(number * TILE, (number + 1) * TILE)
+            target[0, :, at] = sum(
+                dot(left[part * part_rows : (part + 1) * part_rows], right[:, at], ((0,), (0,)))
+                for part, right in enumerate(rights)
+            ).astype(bf16)
+
+    return pl.pallas_call(
+        kernel,
+        grid_spec=pltpu.PrefetchScalarGridSpec(
+            num_scalar_prefetch=1,
+            grid=(planes,),
+            in_specs=[
+                pl.BlockSpec((count, width), lambda i, where: (0, (where[1] + i) % planes))
+            ]
+            + [fixed(right.shape) for right in rights],
+            out_specs=pl.BlockSpec((1, width, columns), lambda i, _: (i, 0, 0)),
+        ),
+        out_shape=out((planes, width, columns)),
+        cost_estimate=cost(count * planes * width * columns),
+        compiler_params=params(),
+    )(where, left, *rights)
+
+
+def hidden_backward(
+    plane, planes, own_rows, parts, hidden, gates, upstream, gain, router, gathered, experts
+):
     count = hidden.shape[0]
     terms = len(parts)
 
-    def kernel(*refs):
+    def kernel(plane, *refs):
         parts = refs[:terms]
-        hidden, gates, upstream, gain, router, out_weight = refs[terms : terms + 6]
-        grad_hidden, grad_branch, grad_mixed, grad_logits, grad_gain = refs[terms + 6 :]
+        hidden, gates, upstream, gain, router, gathered = refs[terms : terms + 6]
+        (
+            grad_hidden, grad_branch, grad_mixed, grad_logits, grad_gain, out_weight, sems
+        ) = refs[terms + 6 :]
+        wait = copies(out_weight_pairs(plane[0], planes, own_rows, gathered, out_weight), sems)
         returned = sum(part[...].astype(f32) for part in parts)
         tail = returned[:, D:]
         grad_gates = gates[...] * (tail + pltpu.roll(tail, PAD - experts, 1))
@@ -484,28 +615,41 @@
         grad = upstream[...].astype(f32) + rms_backward(value, inverse, gain[...], grad_normed)
         grad_hidden[...] = grad
         grad_branch[...] = grad.astype(bf16)
+        wait()
 
         @tiles(D)
         def _(number):
             at = tile(number)
             grad_mixed[:, at] = dot(grad_branch[...], out_weight[at, :], ((1,), (1,))).astype(bf16)
 
+    shapes = [
+        out((count, D), f32), out((count, D)), out((count, D)), out((count, PAD)),
+        out((1, D), f32),
+    ]
+    args = (*parts, hidden, gates, upstream, gain, router, gathered)
     return pl.pallas_call(
         kernel,
-        out_shape=[
-            out((count, D), f32), out((count, D)), out((count, D)), out((count, PAD)),
-            out((1, D), f32),
-        ],
+        grid_spec=pltpu.PrefetchScalarGridSpec(
+            num_scalar_prefetch=1,
+            grid=(1,),
+            in_specs=[HBM if value is gathered else fixed(value.shape) for value in args],
+            out_specs=[fixed(shape.shape) for shape in shapes],
+            scratch_shapes=[
+                pltpu.VMEM((D, D), bf16),
+                pltpu.SemaphoreType.DMA((planes * gathered.shape[0],)),
+            ],
+        ),
+        out_shape=shapes,
         compiler_params=params(),
-    )(*parts, hidden, gates, upstream, gain, router, out_weight)
+    )(plane, *args)
 
 
 def project_backward(step, grad_proj, tokens, slab):
-    ranks, micro, rows, _ = tokens.shape
+    ranks, rows, _ = grad_proj.shape
     width = slab.shape[1] - PAD
 
     def kernel(grad_proj, tokens, weight, grad_normed, grad_gain):
-        value = tokens[0, 0].astype(f32)
+        value = tokens[0].astype(f32)
         inverse = inverse_rms(value)
         grad = dot(grad_proj[0], weight[:, :width], ((1,), (1,)))
         grad_normed[...] = grad.astype(bf16)
@@ -521,7 +665,7 @@
         grid=(ranks,),
         in_specs=[
             leading(grad_proj.shape),
-            pl.BlockSpec((1, 1, rows, D), lambda i: (i, step, 0, 0)),
+            pl.BlockSpec((1, rows, D), lambda i: (i, step, 0)),
             fixed(slab.shape),
         ],
         out_specs=[pl.BlockSpec((rows, D), lambda i: (i, 0)), fixed((1, D))],
@@ -548,13 +692,15 @@
     return sorted(range(1, count), key=lambda step: (min(step, count - step), step))
 
 
-def place_rep(pieces):
-    count = len(pieces)
+def ring_rep(value):
+    count = lax.axis_size("rep")
     rank = lax.axis_index("rep")
-    rows = pieces[0].shape[0]
-    full = jnp.zeros((count * rows,) + pieces[0].shape[1:], pieces[0].dtype)
-    for step, piece in enumerate(pieces):
-        full = lax.dynamic_update_slice_in_dim(full, piece, (rank - step) % count * rows, 0)
+    rows = value.shape[0]
+    full = jnp.zeros((count * rows,) + value.shape[1:], value.dtype)
+    full = lax.dynamic_update_slice_in_dim(full, value, rank * rows, 0)
+    for step in range(1, count):
+        value = shift_rep(value, 1)
+        full = lax.dynamic_update_slice_in_dim(full, value, (rank - step) % count * rows, 0)
     return full
 
 
@@ -568,7 +714,7 @@
     share = w_in.shape[0]
     own = plane % share
     experts = share * ranks
-    expert = (rank * share + own).astype(jnp.int32).reshape(1)
+    where = jnp.stack([rank * share + own, plane, rank % 2]).astype(jnp.int32)
     micro = segments.shape[1]
     mine = tokens.shape[0]
     rows = mine // micro
@@ -589,8 +735,7 @@
     def gather_ranks(value):
         return lax.all_gather(value, "ep", axis=0)
 
-    stream = gather_ranks(tokens)
-    out_pieces = [w_o] + [shift_rep(w_o, step) for step in range(1, planes)]
+    out_rows = [w_o] + [shift_rep(w_o, step) for step in range(1, planes)]
     upstream_group = with_group(cotangent)
     slab = jnp.concatenate(
         [
@@ -613,17 +758,13 @@
     )
     slab = lax.all_to_all(slab, "ep", split_axis=0, concat_axis=0, tiled=True)
     slab = slab.reshape(ranks * dense_rows, 3 * width + PAD)
-    out_pieces, slab = lax.optimization_barrier((out_pieces, slab))
-    slab_pieces = [slab] + [shift_rep(slab, step) for step in range(1, planes)]
-    slab = place_rep(slab_pieces)
+    out_rows, upstream_group, slab = lax.optimization_barrier((out_rows, upstream_group, slab))
+    gathered = gather_ranks(jnp.concatenate([tokens, *out_rows], axis=0))
+    slab = ring_rep(slab)
     router = slab[:, 3 * width :]
     gain_pair = router[:, experts : experts + 2].reshape(-1).astype(f32)
     first_gain = gain_pair[None, :D]
     second_gain = gain_pair[None, D:]
-    out_weight = gather_ranks(place_rep(out_pieces))
-    out_weight = (
-        out_weight.reshape(ranks, planes, -1, D).transpose(1, 0, 2, 3).reshape(D, D)
-    )
 
     def send_weight(weight, step):
         part = lax.dynamic_index_in_dim(weight, (own + step) % share, 0, keepdims=False)
@@ -634,19 +775,19 @@
     in_pieces = {step: send_weight(early[0], step) for step in [0] + order[:1]}
     out_parts = {step: send_weight(early[1], step) for step in [0] + order[:1]}
 
-    normed, proj = project(stream, first_gain, slab)
-    proj = proj.reshape(ranks, micro, rows, 3 * width)
-    upstream_all = gather_ranks(after(upstream_group, proj))
     segment = segments[0]
     cosine, sine = jax.vmap(lambda one: rope_tables(doc_positions(one), HD))(segment)
     sine = jnp.where(jnp.arange(HD) < HD // 2, -sine, sine)
     tables = (cosine, sine, segment[:, :, None], segment[:, None, :], qk_gains)
+    gathered, tables = lax.optimization_barrier((gathered, tables))
+    normed, proj = project(mine, gathered, first_gain, slab)
+    proj = proj.reshape(ranks, micro, rows, 3 * width)
+    upstream_all = gather_ranks(after(upstream_group, proj))
     mixed_h, query, keys, values, lses = attention_forward(proj, *tables)
-    mixed_h, out_weight = lax.optimization_barrier((mixed_h, out_weight))
     mixed = lax.all_to_all(mixed_h, "ep", split_axis=0, concat_axis=3, tiled=True)
     mixed = mixed.reshape(mine, D)
     hidden, payload, gates = route(
-        mixed, tokens, out_weight, second_gain, router, routes, experts
+        where[1:2], planes, mixed, tokens, gathered, second_gain, router, routes, experts
     )
     normed_two = payload[:, :D]
     payload, in_pieces, out_parts = lax.optimization_barrier((payload, in_pieces, out_parts))
@@ -654,35 +795,26 @@
     payload, late = lax.optimization_barrier((payload, (w_in, w_out)))
     for step in order[1:]:
         in_pieces[step] = send_weight(late[0], step)
+    in_pieces, late = lax.optimization_barrier((in_pieces, late))
     for step in order[1:]:
         out_parts[step] = send_weight(late[1], step)
-    in_weight = place_rep([in_pieces[step] for step in range(planes)])
+    in_pieces = [in_pieces[step] for step in range(planes)]
     payload = gather_ranks(payload)
 
     shape = (ranks, share, micro, rows, -1)
     rows_in, tail, both, active, grad_produced, up_rows, places = expert_forward(
-        expert, payload.reshape(shape), upstream_all.reshape(shape), in_weight, slots, experts
+        where, payload.reshape(shape), upstream_all.reshape(shape), in_pieces, slots, experts
     )
     in_rows = micro * ranks * slots
-
-    def flat(value):
-        return value.reshape(in_rows, -1)
-
-    grad_out_expert = dot(flat(active), flat(grad_produced), ((0,), (0,)))
-
-    def cut_rep(value):
-        count = value.shape[0] // planes
-        parts = {}
-        for step in [0] + order:
-            part = lax.dynamic_slice_in_dim(value, (plane + step) % planes * count, count, 0)
-            parts[step] = part.astype(bf16) if step else part
-        return parts
+    out_cut = weight_gradient(
+        where, planes, active.reshape(in_rows, FF), [grad_produced.reshape(in_rows, D)]
+    )
 
     def sum_rep(parts):
-        sums = [None] * share
-        for step in [0] + order:
-            part = parts[step].astype(f32)
-            sums[step % share] = part if sums[step % share] is None else sums[step % share] + part
+        sums = [
+            sum(parts[step].astype(f32) for step in range(first, planes, share))
+            for first in range(share)
+        ]
         return jnp.stack(
             [
                 sum(jnp.where((own - step) % share == j, sums[step], 0.0) for step in range(share))
@@ -693,10 +825,9 @@
     def send(parts, steps):
         return {step: shift_rep(parts[step], step) for step in steps}
 
-    out_cut = cut_rep(grad_out_expert)
-    out_expert = place_rep([out_parts[step] for step in range(planes)])
-    out_expert, out_cut = lax.optimization_barrier((out_expert, out_cut))
+    tail, out_cut = lax.optimization_barrier((tail, out_cut))
     out_sent = send(out_cut, order)
+    out_pieces = [out_parts[step] for step in range(planes)]
     back = []
     returned = []
 
@@ -709,33 +840,25 @@
     for step in range(micro):
         back.append(
             expert_backward(
-                step, expert, tail, both, active, grad_produced, up_rows, places, in_weight,
-                out_expert, share, rows, experts,
+                step, where, tail, both, active, grad_produced, up_rows, places, in_pieces,
+                out_pieces, share, rows, experts,
             )
         )
-        returned.append(scatter_ranks(back[step][1]))
-        out_expert = after(out_expert, back[step][1])
-    short = {step: out_sent[step] for step in order[:2]}
-    rows_in, out_expert, short = lax.optimization_barrier((rows_in, out_expert, short))
-    out_sent.update(short)
-    grad_in_expert = sum(
-        dot(
-            rows_in[step].reshape(in_rows // micro, D),
-            back[step][2].reshape(in_rows // micro, 2 * FF),
-            ((0,), (0,)),
-        )
-        for step in range(micro)
-    )
-    in_cut = cut_rep(grad_in_expert)
+        returned.append(scatter_ranks(back[step][2]))
+        tail, out_sent[order[step]] = after((tail, out_sent[order[step]]), back[step][2])
+    rows_in = after(rows_in, tail)
+    in_cut = weight_gradient(
+        where,
+        planes,
+        rows_in.reshape(in_rows, D),
+        [back[step][3].reshape(in_rows // micro, 2 * FF) for step in range(micro)],
+    )
     in_sent = {}
 
     def swap(value, step):
         return lax.ppermute(value, "ep", [(i, i ^ step) for i in range(ranks)])
 
-    def pair_sum(value):
-        halves = value.reshape((ranks // 2, 2) + value.shape[1:])
-        keep = lax.dynamic_index_in_dim(halves, rank % 2, 1, keepdims=False)
-        give = lax.dynamic_index_in_dim(halves, 1 - rank % 2, 1, keepdims=False)
+    def pair_sum(keep, give):
         return (keep.astype(f32) + swap(give, 1).astype(f32)).astype(bf16)
 
     def cross(value):
@@ -750,37 +873,39 @@
 
     grad_inputs, branches, logit_grads = [], [], []
     gain_two_sum = gain_one_sum = qk_sum = qkv_sum = 0.0
-    by_rank = stream.reshape(ranks, micro, rows, D)
-    in_cut, mixtures = lax.optimization_barrier((in_cut, [part[0] for part in back]))
-    mixtures = [pair_sum(part) for part in mixtures]
+    in_cut, mixtures, out_sent = lax.optimization_barrier(
+        (in_cut, [part[:2] for part in back], out_sent)
+    )
+    mixtures = [pair_sum(*part) for part in mixtures]
     crossed = []
-    releases = [order[:1]] + [[]] * (micro - 2) + [order[1:]] if micro > 1 else [order]
+    releases = [order[:1]] + [[]] * (micro - 2) + [order[1:-1]]
     for step in range(micro):
         at = slice(step * rows, (step + 1) * rows)
-        parts, out_sent, in_sent, mixtures = lax.optimization_barrier(
-            (returned[step], out_sent, in_sent, mixtures)
-        )
+        parts, in_sent, mixtures = lax.optimization_barrier((returned[step], in_sent, mixtures))
         parts = exchange_back(parts)
         parts, in_cut = lax.optimization_barrier((parts, in_cut))
         in_sent.update(send(in_cut, releases[step]))
         grad_hidden, grad_branch, grad_mixed, grad_logits, gain_two = hidden_backward(
-            parts, hidden[at], gates[at], cotangent[at], second_gain, router, out_weight, experts
+            where[1:2], planes, mine, parts, hidden[at], gates[at], cotangent[at], second_gain,
+            router, gathered, experts,
         )
         branches.append(grad_branch)
         logit_grads.append(grad_logits)
         gain_two_sum = gain_two_sum + gain_two
         grad_mixed = lax.all_to_all(grad_mixed, "ep", split_axis=1, concat_axis=0, tiled=True)
         if step == micro - 1:
-            crossed = [cross(part) for part in after(mixtures[:1], parts)]
-            grad_mixed, crossed, mixtures = lax.optimization_barrier(
-                (grad_mixed, crossed, mixtures)
-            )
-            crossed += [cross(part) for part in mixtures[1:]]
+            grad_mixed, mixtures = lax.optimization_barrier((grad_mixed, mixtures))
+            crossed = [cross(part) for part in mixtures]
         grad_proj, grad_qk = attention_backward(
             step, proj, *tables, query, keys, values, lses, grad_mixed
         )
+        if step == micro - 1:
+            last = in_cut[order[-1]]
+            half = last.shape[0] // 2
+            grad_proj, in_sent, last = lax.optimization_barrier((grad_proj, in_sent, last))
+            last_sent = [shift_rep(last[:half], order[-1])]
         qk_sum = qk_sum + grad_qk.reshape(-1)
-        grad_normed, gain_one = project_backward(step, grad_proj, by_rank, slab)
+        grad_normed, gain_one = project_backward(step, grad_proj, gathered, slab)
         gain_one_sum = gain_one_sum + gain_one
         grad_inputs.append(
             (at, grad_hidden, lax.psum_scatter(grad_normed, "ep", scatter_dimension=0, tiled=True))
@@ -792,7 +917,17 @@
             ((0,), (0,)),
         )
     grad_w_out = sum_rep({0: out_cut[0], **out_sent})
-    grad_w_in = sum_rep({0: in_cut[0], **in_sent})
+
+    out_sum = dot(mixed, after(jnp.concatenate(branches, axis=0), grad_normed), ((0,), (0,))).astype(bf16)
+    out_sum = out_sum.reshape(planes, ranks // 2, 2, dense_rows, D).transpose(2, 1, 0, 3, 4)
+    out_crossed = cross(
+        pair_sum(
+            *(
+                lax.dynamic_index_in_dim(out_sum, rank % 2 ^ other, 0, keepdims=False)
+                for other in range(2)
+            )
+        )
+    )
 
     router_sum = dot(normed_two, jnp.concatenate(logit_grads, axis=0), ((0,), (0,)))
     qk_columns = qk_sum.shape[0] // dense_rows
@@ -817,9 +952,10 @@
         tail = packed[..., split:]
         return packed[..., :split], tail[..., :count] + tail[..., count : 2 * count]
 
-    packed, crossed, branches = lax.optimization_barrier(
-        (pack(qkv_sum, small), crossed, branches)
-    )
+    packed, crossed, last_sent, last = lax.optimization_barrier(
+        (pack(qkv_sum, small), crossed, last_sent, last)
+    )
+    last_sent = last_sent + [shift_rep(last[half:], order[-1])]
     part_rows = D // planes
     main = lax.dynamic_slice_in_dim(qkv_sum, plane * part_rows, part_rows, 0)
     small = lax.dynamic_slice_in_dim(small, plane * part_rows, part_rows, 0)
@@ -830,9 +966,6 @@
         )
         for step in range(1, planes)
     ]
-    out_sum = dot(mixed, jnp.concatenate(branches, axis=0), ((0,), (0,))).astype(bf16)
-    out_sum = out_sum.reshape(planes, ranks, dense_rows, D).transpose(1, 0, 2, 3)
-    out_crossed = cross(pair_sum(out_sum))
     mixture = []
     for parts in crossed:
         parts = total(parts)
@@ -847,6 +980,8 @@
                 own_stream, inverse_rms(own_stream), first_gain, grad_normed.astype(f32)
             )
         )
+    packed_sent, last_sent = lax.optimization_barrier((packed_sent, last_sent))
+    in_sent[order[-1]] = jnp.concatenate(last_sent, axis=0)
     for part in packed_sent:
         part_main, part_small = unpack(part)
         main, small = main + part_main, small + part_small
@@ -857,6 +992,7 @@
         main.reshape(ranks, dense_rows, 3, width).transpose(1, 2, 0, 3).reshape(dense_rows, 3 * D)
     )
     small = jnp.sum(small, axis=0)
+    grad_w_in = sum_rep({0: in_cut[0], **in_sent})
     out_sum = total(out_crossed)
     grad_w_o = lax.dynamic_index_in_dim(out_sum, plane, 0, keepdims=False)
     out_sum = out_sum.astype(bf16)

time: 1240 us -> 1200 us (0.968)
  starting transfers between devices: 88.6 us -> 146 us
  matrix products: 72.9 us -> 17.1 us
  local copies, waits for them, and re-layouts: 154 us -> 98.7 us
  Pallas kernels: 242 us -> 293 us
  other arithmetic: 86.3 us -> 67.6 us
  blocking collectives: 15.8 us -> 0 us
    ppermute x24 -> x25, waiting for transfers between devices: 344 us -> 274 us  [shift_rep(): lax.ppermute(value, 'rep', [(i, (i + step) % count) for i in range(count)])]
    dot_general x7 -> x4, matrix products: 72.9 us -> 17.1 us  [dot(): return lax.dot_general(a, b, (dims, ((), ())), preferred_element_type=f32)]
    pallas_call x4 -> x6, Pallas kernels: 40.8 us -> 87.8 us  [the longest x2 46.2 us: weight_gradient(): pl.pallas_call(kernel, grid_spec=pltpu.PrefetchScalarGridSpec(num_scalar_...]
    ppermute x24 -> x25, starting transfers between devices: 48.2 us -> 95 us  [shift_rep(): lax.ppermute(value, 'rep', [(i, (i + step) % count) for i in range(count)])]
    ppermute x12, waiting for transfers between devices: 68.4 us -> 106 us  [swap(): return lax.ppermute(value, 'ep', [(i, i ^ step) for i in range(ranks)])]
    ppermute x6, waiting for transfers between devices: 91.5 us -> 120 us  [exchange(): return lax.ppermute(value, 'rep', pairs)]
    dynamic_update_slice x16 -> x4, local copies, waits for them, and re-layouts: 24.3 us -> 4.08 us  [the longest x3 2.76 us: ring_rep(): lax.dynamic_update_slice_in_dim(full, value, (rank - step) % count * rows...]
    all_gather x4 -> x3, waiting for transfers between devices: 0.03 us -> 19 us  [gather_ranks(): return lax.all_gather(value, 'ep', axis=0)]
  transfers between devices with their start and end apart: 54 -> 55, of which waited for: 24 -> 31; matrix products, arithmetic and copies ran while one was open for 23% -> 14% of each run, Pallas kernels for 13% -> 20%
where the time goes in v4:
time: 1200 us; the launch traced here: 1190 us
  waiting for transfers between devices  554 us (46%)
  Pallas kernels  293 us (24%)
  starting transfers between devices  146 us (12%)
  local copies, waits for them, and re-layouts  98.7 us (8%)
  other arithmetic  67.6 us (6%)
  matrix products  17.1 us (1%)
  between operations  15.8 us (1%)
    ppermute x25, waiting for transfers between devices, shift_rep(): lax.ppermute(value, 'rep', [(i, (i + step) % count) for i in range(count)])  274 us
    ppermute x6, waiting for transfers between devices, exchange(): return lax.ppermute(value, 'rep', pairs)  120 us
    ppermute x12, waiting for transfers between devices, swap(): return lax.ppermute(value, 'ep', [(i, i ^ step) for i in range(ranks)])  106 us
    ppermute x25, starting transfers between devices, shift_rep(): lax.ppermute(value, 'rep', [(i, (i + step) % count) for i in range(count)])  95 us
    pallas_call x2, Pallas kernels, expert_backward(): pl.pallas_call(kernel, grid_spec=pltpu.PrefetchScalarGridSpec(num_scalar_...  81 us
    pallas_call x2, Pallas kernels, weight_gradient(): pl.pallas_call(kernel, grid_spec=pltpu.PrefetchScalarGridSpec(num_scalar_...  46.2 us
    pallas_call x1, Pallas kernels, expert_forward(): pl.pallas_call(kernel, grid_spec=pltpu.PrefetchScalarGridSpec(num_scalar_...  40.3 us
    pallas_call x2, Pallas kernels, attention_backward(): pl.pallas_call(lambda *refs: backward_kernel(heads, *refs), grid=(1,), in...  34 us
  transfers between devices with their start and end apart: 55, of which 31 were waited for; matrix products, arithmetic and copies ran while one was open for 14% of the time, Pallas kernels for 20%

profile of v4, /device:TPU:0, one launch (start us, length us, event | category | flops | bytes accessed | tf_op | source)
XLA Modules:
  0.0 1192.5 jit_solution(18375647880256371377)
XLA Ops:
  25.7 20.1 %collective-permute-done.3 = bf16[256,2048]{1,0:T(8,128)(2,1)} collective-permute-done((bf16[256,2048]{1,0:T(8,128)(2,1)}, bf16[256,2048]{1,0:T(8,128)(2,1)}, u32[]{:S(2)}, u32[]{:S(2)}) %collective-permute-start.3) | collective-permute-done | bytes 1048608 | tf_op jit(solution)/shard_map/ppermute | solution.py:730
  55.8 22.8 %collective-permute-done.4 = bf16[512,896]{1,0:T(8,128)(2,1)S(1)} collective-permute-done((bf16[512,896]{1,0:T(8,128)(2,1)}, bf16[512,896]{1,0:T(8,128)(2,1)S(1)}, u32[]{:S(2)}, u32[]{:S(2)}) %collective-permute-start.4) | collective-permute-done | bytes 917536 | tf_op jit(solution)/shard_map/ppermute | solution.py:679
  79.4 21.7 %collective-permute-done.5 = bf16[512,896]{1,0:T(8,128)(2,1)} collective-permute-done((bf16[512,896]{1,0:T(8,128)(2,1)S(1)}, bf16[512,896]{1,0:T(8,128)(2,1)}, u32[]{:S(2)}, u32[]{:S(2)}) %collective-permute-start.5) | collective-permute-done | bytes 917536 | tf_op jit(solution)/shard_map/ppermute | solution.py:679
  127.4 19.0 %all-gather.7.cloned.1.call-done = bf16[4096,2048]{1,0:T(8,128)(2,1)} async-done(((bf16[512,2048]{1,0:T(8,128)(2,1)}), bf16[4096,2048]{1,0:T(8,128)(2,1)}) %all-gather.7.cloned.1.call-update) | async-done | bytes 16777232 | tf_op jit(solution)/shard_map/all_gather | solution.py:736
  172.3 22.0 %shard_map.179 = (bf16[8,2,128,256]{3,2,1,0:T(8,128)(2,1)S(1)}, bf16[2,1024,256]{2,1,0:T(8,128)(2,1)S(1)}, bf16[2,1024,256]{2,1,0:T(8,128)(2,1)S(1)}, bf16[2,1024,256]{2,1,0:T(8,128)(2,1)}, f32[2,2,1024,1]{3,2,1,0:T(8,128)}) custom-call(f32[8,2,128,768]{3,2,1,0:T(8,128)} %bitcast.209, f32[2,1024,128]{2,1,0:T(8,128)} %get-tuple-element.139.refs_1_, ...), custom_call_target="tpu_custom_call" | custom-call | tf_op jit(solution)/shard_map/pallas_call | solution.py:198
  205.2 23.0 %all-to-all-done.1 = bf16[8,2,128,256]{3,2,1,0:T(8,128)(2,1)} async-done(((bf16[8,2,128,256]{3,2,1,0:T(8,128)(2,1)}), bf16[8,2,128,256]{3,2,1,0:T(8,128)(2,1)}, u32[]{:S(2)}, u32[]{:S(2)}) %all-to-all-start.1) | async-done | bytes 1048608 | tf_op jit(solution)/shard_map/all_to_all | solution.py:787
  241.2 23.9 %collective-permute-done.9 = bf16[256,2176]{1,0:T(8,128)(2,1)S(1)} collective-permute-done((bf16[256,2176]{1,0:T(8,128)(2,1)S(1)}, bf16[256,2176]{1,0:T(8,128)(2,1)S(1)}, u32[]{:S(2)}, u32[]{:S(2)}) %collective-permute-start.9) | collective-permute-done | bytes 1114144 | tf_op jit(solution)/shard_map/ppermute | solution.py:730
  274.3 88.2 %collective-permute-done.10.refs_2_ = bf16[512,2048]{1,0:T(8,128)(2,1)} collective-permute-done((bf16[512,2048]{1,0:T(8,128)(2,1)}, bf16[512,2048]{1,0:T(8,128)(2,1)}, u32[]{:S(2)}, u32[]{:S(2)}) %collective-permute-start.10) | collective-permute-done | bytes 2097184 | tf_op jit(solution)/shard_map/ppermute | solution.py:679
  365.7 44.4 %collective-permute-start.12 = (bf16[256,2048]{1,0:T(8,128)(2,1)}, bf16[256,2048]{1,0:T(8,128)(2,1)S(1)}, u32[]{:S(2)}, u32[]{:S(2)}) collective-permute-start(bf16[256,2048]{1,0:T(8,128)(2,1)} %get-tuple-element.304), channel_id=1, source_target_pairs={{0,16},{8,24},{16,0},{24,8},{1,17},{9,25},{17,1},{25,9},{2,18},{10... | collective-permute-start | bytes 3145736 | tf_op jit(solution)/shard_map/ppermute | solution.py:679
  413.4 40.3 %shard_map.181 = (bf16[2,4,288,2048]{3,2,1,0:T(8,128)(2,1)}, f32[2,4,288,128]{3,2,1,0:T(8,128)S(1)}, f32[2,4,288,2048]{3,2,1,0:T(8,128)}, bf16[2,4,288,1024]{3,2...) custom-call(s32[3]{0:T(128)S(1)} %pad_add_fusion.where, ...), custom_call_target="tpu_custom_call" | custom-call | flops 24159191040 | tf_op jit(solution)/shard_map/pallas_call | solution.py:429
  453.8 16.8 %shard_map.182 = bf16[4,256,2048]{2,1,0:T(8,128)(2,1)} custom-call(s32[3]{0:T(128)S(1)} %pad_add_fusion.where, bf16[2304,1024]{1,0:T(8,128)(2,1)} %bitcast.239, bf16[2304,2048]{1,0:T(8,128)(2,1)} %bitcast.237), custom_call_target="tpu_custom_call" | custom-call | flops 9663676416 | tf_op jit(solution)/shard_map/pallas_call | solution.py:575
  470.6 40.3 %shard_map.183 = (bf16[4,2,128,2048]{3,2,1,0:T(8,128)(2,1)}, bf16[4,2,128,2048]{3,2,1,0:T(8,128)(2,1)}, bf16[8,2,128,2176]{3,2,1,0:T(8,128)(2,1)}, bf16[4,288,2048]{2,1,0:T(8,128)(2,1)}) custom-call(s32[3]{0:T(128)S(1)} %pad_add_fusion.where, f32[2,4,288,128]{3,2,1,0:T(8,128)} %copy-done.23, f32[2,4,288,2048]{3,2,1,0:T(8,128)} %get-tuple-element.170.both, ...), custom_call_target="tpu_custom_call" | custom-call | flops 21743271936 | tf_op jit(solution)/shard_map/pallas_call | solution.py:527
  523.4 26.1 %collective-permute-done.14 = bf16[256,2048]{1,0:T(8,128)(2,1)} collective-permute-done((bf16[256,2048]{1,0:T(8,128)(2,1)S(1)}, bf16[256,2048]{1,0:T(8,128)(2,1)}, u32[]{:S(2)}, u32[]{:S(2)}) %collective-permute-start.14) | collective-permute-done | bytes 1048608 | tf_op jit(solution)/shard_map/ppermute | solution.py:679
  549.5 40.7 %shard_map.184 = (bf16[4,2,128,2048]{3,2,1,0:T(8,128)(2,1)}, bf16[4,2,128,2048]{3,2,1,0:T(8,128)(2,1)}, bf16[8,2,128,2176]{3,2,1,0:T(8,128)(2,1)}, bf16[4,288,2048]{2,1,0:T(8,128)(2,1)}) custom-call(s32[3]{0:T(128)S(1)} %pad_add_fusion.where, f32[2,4,288,128]{3,2,1,0:T(8,128)} %copy-done.23, f32[2,4,288,2048]{3,2,1,0:T(8,128)} %get-tuple-element.170.both, ...), custom_call_target="tpu_custom_call" | custom-call | flops 21743271936 | tf_op jit(solution)/shard_map/pallas_call | solution.py:527
  591.9 24.8 %collective-permute-done.16 = bf16[256,2048]{1,0:T(8,128)(2,1)S(1)} collective-permute-done((bf16[256,2048]{1,0:T(8,128)(2,1)}, bf16[256,2048]{1,0:T(8,128)(2,1)S(1)}, u32[]{:S(2)}, u32[]{:S(2)}) %collective-permute-start.16) | collective-permute-done | bytes 1048608 | tf_op jit(solution)/shard_map/ppermute | solution.py:679
  617.7 29.4 %shard_map.185 = bf16[4,512,2048]{2,1,0:T(8,128)(2,1)} custom-call(s32[3]{0:T(128)S(1)} %pad_add_fusion.where, bf16[2304,2048]{1,0:T(8,128)(2,1)} %bitcast.236, bf16[1152,2048]{1,0:T(8,128)(2,1)} %bitcast.238, bf16[1152,2048]{1,0:T(8,128)(2,1)} %bitcast.240), custom_call_target="tpu_custom_call" | custom-call | flops 19327352832 | tf_op jit(solution)/shard_map/pallas_call | solution.py:575
  730.8 17.1 %shard_map.187 = (bf16[8,128,768]{2,1,0:T(8,128)(2,1)}, f32[2,128]{1,0:T(2,128)S(1)}) custom-call(f32[8,2,128,768]{3,2,1,0:T(8,128)} %bitcast.210, f32[2,1024,128]{2,1,0:T(8,128)S(1)} %copy-done.3, f32[2,1024,128]{2,1,0:T(8,128)S(1)} %copy-done.2, s32[2,1024,1]{2,1,0:T(8,128)S(1)} %copy-done.4, s32[2,1,1024]{2,1,0:T(1,128)S(1)} %broadcast_in_dim_squeeze.7.refs_4_, ...), custom_call_target="tpu_custom_call" | custom-call | tf_op jit(solution)/shard_map/pallas_call | solution.py:220
  829.1 16.9 %shard_map.190 = (bf16[8,128,768]{2,1,0:T(8,128)(2,1)}, f32[2,128]{1,0:T(2,128)S(1)}) custom-call(f32[8,2,128,768]{3,2,1,0:T(8,128)} %bitcast.211, f32[2,1024,128]{2,1,0:T(8,128)S(1)} %copy-done.3, f32[2,1024,128]{2,1,0:T(8,128)S(1)} %copy-done.2, s32[2,1024,1]{2,1,0:T(8,128)S(1)} %copy-done.4, s32[2,1,1024]{2,1,0:T(1,128)S(1)} %broadcast_in_dim_squeeze.7.refs_4_, ...), custom_call_target="tpu_custom_call" | custom-call | tf_op jit(solution)/shard_map/pallas_call | solution.py:220
  909.4 26.4 %collective-permute-done.26 = bf16[2,128,2048]{2,1,0:T(8,128)(2,1)} collective-permute-done((bf16[2,128,2048]{2,1,0:T(8,128)(2,1)}, bf16[2,128,2048]{2,1,0:T(8,128)(2,1)}, u32[]{:S(2)}, u32[]{:S(2)}) %collective-permute-start.26) | collective-permute-done | bytes 1048608 | tf_op jit(solution)/shard_map/ppermute | solution.py:859
  943.2 16.0 %collective-permute-done.28 = bf16[2,128,2048]{2,1,0:T(8,128)(2,1)S(1)} collective-permute-done((bf16[2,128,2048]{2,1,0:T(8,128)(2,1)S(1)}, bf16[2,128,2048]{2,1,0:T(8,128)(2,1)S(1)}, u32[]{:S(2)}, u32[]{:S(2)}) %collective-permute-start.28) | collective-permute-done | bytes 1048608 | tf_op jit(solution)/shard_map/ppermute | solution.py:859
  969.0 44.1 %collective-permute-done.31 = bf16[128,2048]{1,0:T(8,128)(2,1)S(1)} collective-permute-done((bf16[128,2048]{1,0:T(8,128)(2,1)S(1)}, bf16[128,2048]{1,0:T(8,128)(2,1)S(1)}, u32[]{:S(2)}, u32[]{:S(2)}) %collective-permute-start.31) | collective-permute-done | bytes 524320 | tf_op jit(solution)/shard_map/ppermute | solution.py:730
  1023.3 31.0 %collective-permute-done.33 = bf16[512,896]{0,1:T(8,128)(2,1)S(1)} collective-permute-done((bf16[512,896]{0,1:T(8,128)(2,1)S(1)}, bf16[512,896]{0,1:T(8,128)(2,1)S(1)}, u32[]{:S(2)}, u32[]{:S(2)}) %collective-permute-start.33) | collective-permute-done | bytes 917536 | tf_op jit(solution)/shard_map/ppermute | solution.py:679
  1112.4 18.0 %collective-permute-done.38 = bf16[4,64,2048]{2,1,0:T(8,128)(2,1)} collective-permute-done((bf16[4,64,2048]{2,1,0:T(8,128)(2,1)}, bf16[4,64,2048]{2,1,0:T(8,128)(2,1)}, u32[]{:S(2)}, u32[]{:S(2)}) %collective-permute-start.38) | collective-permute-done | bytes 1048608 | tf_op jit(solution)/shard_map/ppermute | solution.py:859
  1137.6 18.5 %collective-permute-start.42 = (bf16[64,2048]{1,0:T(8,128)(2,1)S(1)}, bf16[64,2048]{1,0:T(8,128)(2,1)}, u32[]{:S(2)}, u32[]{:S(2)}) collective-permute-start(bf16[64,2048]{1,0:T(8,128)(2,1)S(1)} %get-tuple-element.314), channel_id=1, source_target_pairs={{0,24},{8,0},{16,8},{24,16},{1,25},{9,1},{17,9},{25,17},{2,26},{10... | collective-permute-start | bytes 786440 | tf_op jit(solution)/shard_map/ppermute | solution.py:679
  (345 shorter events, 485.2 us)
Async XLA Ops:
  20.0 126.3 %all-gather.7.cloned.1.call-start = ((), (), s32[]{:S(2)}) async-start(), calls=%async_computation.13 | async-start | bytes 18874368 | tf_op jit(solution)/shard_map/all_gather | solution.py:736
  54.9 358.5 %all-gather.11.cloned.1.call-start = ((), (), s32[]{:S(2)}) async-start(), calls=%async_computation.15 | async-start | bytes 18874368 | tf_op jit(solution)/shard_map/all_gather | solution.py:736
  166.8 72.7 %collective-permute-start.7 = (bf16[512,2048]{1,0:T(8,128)(2,1)}, bf16[512,2048]{1,0:T(8,128)(2,1)}, u32[]{:S(2)}, u32[]{:S(2)}) collective-permute-start(bf16[512,2048]{1,0:T(8,128)(2,1)} %get-tuple-element.296), channel_id=1, source_target_pairs={{0,8},{8,16},{16,24},{24,0},{1,9},{9,17},{17,25},{25,1},{2,10},{10... | collective-permute-start | bytes 6291464 | tf_op jit(solution)/shard_map/ppermute | solution.py:679
  169.4 70.0 %collective-permute-start.8 = (bf16[256,2048]{1,0:T(8,128)(2,1)}, bf16[256,2048]{1,0:T(8,128)(2,1)}, u32[]{:S(2)}, u32[]{:S(2)}) collective-permute-start(bf16[256,2048]{1,0:T(8,128)(2,1)} %get-tuple-element.305), channel_id=1, source_target_pairs={{0,8},{8,16},{16,24},{24,0},{1,9},{9,17},{17,25},{25,1},{2,10},{10... | collective-permute-start | bytes 3145736 | tf_op jit(solution)/shard_map/ppermute | solution.py:679
  201.6 211.8 %all-gather.9.cloned.1.call-start = ((), (), s32[]{:S(2)}) async-start(), calls=%async_computation.14 | async-start | bytes 20054016 | tf_op jit(solution)/shard_map/all_gather | solution.py:736
  266.7 414.5 %reduce-scatter.5.cloned.1.call-start = ((), (), s32[]{:S(2)}) async-start(), calls=%async_computation.9 | async-start | bytes 10027008 | tf_op jit(solution)/shard_map/reduce_scatter | solution.py:835
  271.6 90.9 %collective-permute-start.10 = (bf16[512,2048]{1,0:T(8,128)(2,1)}, bf16[512,2048]{1,0:T(8,128)(2,1)}, u32[]{:S(2)}, u32[]{:S(2)}) collective-permute-start(bf16[512,2048]{1,0:T(8,128)(2,1)} %get-tuple-element.295), channel_id=1, source_target_pairs={{0,16},{8,24},{16,0},{24,8},{1,17},{9,25},{17,1},{25,9},{2,18},{10... | collective-permute-start | bytes 6291464 | tf_op jit(solution)/shard_map/ppermute | solution.py:679
  272.2 90.3 %collective-permute-start.11 = (bf16[512,2048]{1,0:T(8,128)(2,1)}, bf16[512,2048]{1,0:T(8,128)(2,1)}, u32[]{:S(2)}, u32[]{:S(2)}) collective-permute-start(bf16[512,2048]{1,0:T(8,128)(2,1)} %get-tuple-element.294), channel_id=1, source_target_pairs={{0,24},{8,0},{16,8},{24,16},{1,25},{9,1},{17,9},{25,17},{2,26},{10... | collective-permute-start | bytes 6291464 | tf_op jit(solution)/shard_map/ppermute | solution.py:679
  365.7 104.9 %collective-permute-start.12 = (bf16[256,2048]{1,0:T(8,128)(2,1)}, bf16[256,2048]{1,0:T(8,128)(2,1)S(1)}, u32[]{:S(2)}, u32[]{:S(2)}) collective-permute-start(bf16[256,2048]{1,0:T(8,128)(2,1)} %get-tuple-element.304), channel_id=1, source_target_pairs={{0,16},{8,24},{16,0},{24,8},{1,17},{9,25},{17,1},{25,9},{2,18},{10... | collective-permute-start | bytes 3145736 | tf_op jit(solution)/shard_map/ppermute | solution.py:679
  410.1 60.5 %collective-permute-start.13 = (bf16[256,2048]{1,0:T(8,128)(2,1)}, bf16[256,2048]{1,0:T(8,128)(2,1)}, u32[]{:S(2)}, u32[]{:S(2)}) collective-permute-start(bf16[256,2048]{1,0:T(8,128)(2,1)} %get-tuple-element.303), channel_id=1, source_target_pairs={{0,24},{8,0},{16,8},{24,16},{1,25},{9,1},{17,9},{25,17},{2,26},{10... | collective-permute-start | bytes 3145736 | tf_op jit(solution)/shard_map/ppermute | solution.py:679
  510.9 260.7 %reduce-scatter.7.cloned.1.call-start = ((), (), s32[]{:S(2)}) async-start(), calls=%async_computation.10 | async-start | bytes 10027008 | tf_op jit(solution)/shard_map/reduce_scatter | solution.py:835
  591.9 66.1 %collective-permute-start.15 = (bf16[256,2048]{1,0:T(8,128)(2,1)S(1)}, bf16[256,2048]{1,0:T(8,128)(2,1)S(1)}, u32[]{:S(2)}, u32[]{:S(2)}) collective-permute-start(bf16[256,2048]{1,0:T(8,128)(2,1)S(1)} %copy-done.49), channel_id=1, source_target_pairs={{0,16},{8,24},{16,0},{24,8},{1,17},{9,25},{17,1},{25,9},{2,18},{10... | collective-permute-start | bytes 3145736 | tf_op jit(solution)/shard_map/ppermute | solution.py:679
  721.0 460.1 %reduce-scatter.9.cloned.1.call-start = ((), (), s32[]{:S(2)}) async-start(), calls=%async_computation.11 | async-start | bytes 4718592 | tf_op jit(solution)/shard_map/reduce_scatter | solution.py:911
  794.9 62.2 %collective-permute-start.22 = (bf16[512,2048]{1,0:T(8,128)(2,1)}, bf16[512,2048]{1,0:T(8,128)(2,1)}, u32[]{:S(2)}, u32[]{:S(2)}) collective-permute-start(bf16[512,2048]{1,0:T(8,128)(2,1)} %get-tuple-element.277), channel_id=1, source_target_pairs={{0,24},{8,0},{16,8},{24,16},{1,25},{9,1},{17,9},{25,17},{2,26},{10... | collective-permute-start | bytes 6291464 | tf_op jit(solution)/shard_map/ppermute | solution.py:679
  819.4 361.8 %reduce-scatter.11.cloned.1.call-start = ((), (), s32[]{:S(2)}) async-start(), calls=%async_computation.12 | async-start | bytes 4718592 | tf_op jit(solution)/shard_map/reduce_scatter | solution.py:911
  852.0 57.4 %collective-permute-start.25 = (bf16[2,128,2048]{2,1,0:T(8,128)(2,1)}, bf16[2,128,2048]{2,1,0:T(8,128)(2,1)}, u32[]{:S(2)}, u32[]{:S(2)}) collective-permute-start(bf16[2,128,2048]{2,1,0:T(8,128)(2,1)} %get-tuple-element.287), channel_id=1, source_target_pairs={{0,6},{1,7},{2,4},{3,5},{4,2},{5,3},{6,0},{7,1},{8,14},{9,15},{10,... | collective-permute-start | bytes 3145736 | tf_op jit(solution)/shard_map/ppermute | solution.py:859
  856.5 79.3 %collective-permute-start.26 = (bf16[2,128,2048]{2,1,0:T(8,128)(2,1)}, bf16[2,128,2048]{2,1,0:T(8,128)(2,1)}, u32[]{:S(2)}, u32[]{:S(2)}) collective-permute-start(bf16[2,128,2048]{2,1,0:T(8,128)(2,1)} %get-tuple-element.285), channel_id=1, source_target_pairs={{0,2},{1,3},{2,0},{3,1},{4,6},{5,7},{6,4},{7,5},{8,10},{9,11},{10,... | collective-permute-start | bytes 3145736 | tf_op jit(solution)/shard_map/ppermute | solution.py:859
  857.1 86.1 %collective-permute-start.27 = (bf16[2,128,2048]{2,1,0:T(8,128)(2,1)}, bf16[2,128,2048]{2,1,0:T(8,128)(2,1)}, u32[]{:S(2)}, u32[]{:S(2)}) collective-permute-start(bf16[2,128,2048]{2,1,0:T(8,128)(2,1)} %get-tuple-element.284), channel_id=1, source_target_pairs={{0,4},{1,5},{2,6},{3,7},{4,0},{5,1},{6,2},{7,3},{8,12},{9,13},{10,... | collective-permute-start | bytes 3145736 | tf_op jit(solution)/shard_map/ppermute | solution.py:859
  888.0 71.2 %collective-permute-start.28 = (bf16[2,128,2048]{2,1,0:T(8,128)(2,1)S(1)}, bf16[2,128,2048]{2,1,0:T(8,128)(2,1)S(1)}, u32[]{:S(2)}, u32[]{:S(2)}) collective-permute-start(bf16[2,128,2048]{2,1,0:T(8,128)(2,1)S(1)} %copy-done.45), channel_id=1, source_target_pairs={{0,6},{1,7},{2,4},{3,5},{4,2},{5,3},{6,0},{7,1},{8,14},{9,15},{10,... | collective-permute-start | bytes 3145736 | tf_op jit(solution)/shard_map/ppermute | solution.py:859
  900.7 58.5 %collective-permute-start.29 = (bf16[256,2048]{1,0:T(8,128)(2,1)S(1)}, bf16[256,2048]{1,0:T(8,128)(2,1)S(1)}, u32[]{:S(2)}, u32[]{:S(2)}) collective-permute-start(bf16[256,2048]{1,0:T(8,128)(2,1)S(1)} %copy-done.46), channel_id=1, source_target_pairs={{0,16},{8,24},{16,0},{24,8},{1,17},{9,25},{17,1},{25,9},{2,18},{10... | collective-permute-start | bytes 3145736 | tf_op jit(solution)/shard_map/ppermute | solution.py:679
  909.4 170.3 %collective-permute-start.36 = (bf16[4,4,64,2048]{3,2,0,1:T(8,128)(2,1)S(1)}, bf16[4,4,64,2048]{3,2,0,1:T(8,128)(2,1)S(1)}, u32[]{:S(2)}, u32[]{:S(2)}) collective-permute-start(bf16[4,4,64,2048]{3,2,0,1:T(8,128)(2,1)S(1)} %dynamic-slice_bitcast_fusion), channel_id=1, source_target_pairs={{0,1},{1,0},{2,3},{3,2},{4,5},{5,4},{6,7},{7,6},{8,9},{9,8},{10,11... | collective-permute-start | bytes 12582920 | tf_op jit(solution)/shard_map/ppermute | solution.py:859
  968.9 85.3 %collective-permute-start.33 = (bf16[512,896]{0,1:T(8,128)(2,1)S(1)}, bf16[512,896]{0,1:T(8,128)(2,1)S(1)}, u32[]{:S(2)}, u32[]{:S(2)}) collective-permute-start(bf16[512,896]{0,1:T(8,128)(2,1)S(1)} %get-tuple-element.299), channel_id=1, source_target_pairs={{0,16},{8,24},{16,0},{24,8},{1,17},{9,25},{17,1},{25,9},{2,18},{10... | collective-permute-start | bytes 2752520 | tf_op jit(solution)/shard_map/ppermute | solution.py:679
  1013.1 63.7 %collective-permute-start.35 = (bf16[256,2048]{1,0:T(8,128)(2,1)S(1)}, bf16[256,2048]{1,0:T(8,128)(2,1)S(1)}, u32[]{:S(2)}, u32[]{:S(2)}) collective-permute-start(bf16[256,2048]{1,0:T(8,128)(2,1)S(1)} %slice.212), channel_id=1, source_target_pairs={{0,16},{8,24},{16,0},{24,8},{1,17},{9,25},{17,1},{25,9},{2,18},{10... | collective-permute-start | bytes 3145736 | tf_op jit(solution)/shard_map/ppermute | solution.py:679
  1090.2 71.8 %all-to-all-start.4 = ((bf16[8,64,896]{2,1,0:T(8,128)(2,1)}), bf16[8,64,896]{2,1,0:T(8,128)(2,1)S(1)}, u32[]{:S(2)}, u32[]{:S(2)}) async-start(bf16[8,64,896]{2,1,0:T(8,128)(2,1)} %bitcast.64), calls=%async_computation.8 | async-start | bytes 1835008 | tf_op jit(solution)/shard_map/all_to_all | solution.py:989
  (86 other events, 2092.6 us)
Sparse Core Ops, SparseCore 0:
  55.0 91.2 all-gather.6
  161.8 101.0 all-gather.10
  266.8 92.6 all-gather.8
  511.1 83.2 reduce-scatter.4
  597.8 73.7 reduce-scatter.6
  763.4 48.8 reduce-scatter.8
  875.4 86.4 reduce-scatter.10

commit v5 on v4

--- a/solution.py
+++ b/solution.py
@@ -180,7 +180,7 @@
 
 
 def cost(products):
-    return pl.CostEstimate(flops=2 * products, bytes_accessed=0, transcendentals=0)
+    return pl.CostEstimate(flops=6 * products, bytes_accessed=0, transcendentals=0)
 
 
 def out(shape, dtype=bf16):
@@ -234,8 +234,8 @@
     )
 
 
-def project(count, tokens, gain, slab):
-    ranks = tokens.shape[0]
+def project(tokens, gain, slab):
+    ranks, count, _ = tokens.shape
     width = slab.shape[1] - PAD
 
     def kernel(value, gain, weight, normed, proj):
@@ -292,12 +292,12 @@
     ]
 
 
-def out_weight_pairs(plane, planes, count, gathered, target):
+def out_weight_pairs(plane, planes, gathered, target):
     ranks = gathered.shape[0]
     rows = D // (planes * ranks)
     return [
         (
-            gathered.at[rank, pl.ds(count + step * rows, rows)],
+            gathered.at[rank, pl.ds(step * rows, rows)],
             target.at[pl.ds(((plane + planes - step) % planes * ranks + rank) * rows, rows)],
         )
         for rank in range(ranks)
@@ -313,7 +313,7 @@
         plane, mixed, tokens, gathered, gain, router, routes, hidden, payload, gates,
         out_weight, sems,
     ):
-        copies(out_weight_pairs(plane[0], planes, count, gathered, out_weight), sems)()
+        copies(out_weight_pairs(plane[0], planes, gathered, out_weight), sems)()
 
         @tiles(D)
         def _(number):
@@ -556,17 +556,25 @@
     )
 
 
-def weight_gradient(where, planes, left, rights):
+def weight_gradient(where, planes, left, rights, tail=None):
     count, width = left.shape
     parts = len(rights)
     part_rows = count // parts
     columns = rights[0].shape[1]
     width = width // planes
+    step = min(TILE, columns & -columns)
+    tails = [] if tail is None else [tail]
+    whole = columns + sum(value.shape[1] for value in tails)
+
+    def of_plane(i, where):
+        return (where[1] + i) % planes
 
     def kernel(where, left, *refs):
-        rights, target = refs[:parts], refs[parts]
-        for number in range(columns // TILE):
-            at = slice(number * TILE, (number + 1) * TILE)
+        rights, target = refs[:parts], refs[-1]
+        for value in refs[parts:-1]:
+            target[0, :, columns:] = value[...]
+        for number in range(columns // step):
+            at = slice(number * step, (number + 1) * step)
             target[0, :, at] = sum(
                 dot(left[part * part_rows : (part + 1) * part_rows], right[:, at], ((0,), (0,)))
                 for part, right in enumerate(rights)
@@ -577,20 +585,22 @@
         grid_spec=pltpu.PrefetchScalarGridSpec(
             num_scalar_prefetch=1,
             grid=(planes,),
-            in_specs=[
-                pl.BlockSpec((count, width), lambda i, where: (0, (where[1] + i) % planes))
-            ]
-            + [fixed(right.shape) for right in rights],
-            out_specs=pl.BlockSpec((1, width, columns), lambda i, _: (i, 0, 0)),
+            in_specs=[pl.BlockSpec((count, width), lambda i, where: (0, of_plane(i, where)))]
+            + [fixed(right.shape) for right in rights]
+            + [
+                pl.BlockSpec((width, value.shape[1]), lambda i, where: (of_plane(i, where), 0))
+                for value in tails
+            ],
+            out_specs=pl.BlockSpec((1, width, whole), lambda i, _: (i, 0, 0)),
         ),
-        out_shape=out((planes, width, columns)),
+        out_shape=out((planes, width, whole)),
         cost_estimate=cost(count * planes * width * columns),
         compiler_params=params(),
-    )(where, left, *rights)
+    )(where, left, *rights, *tails)
 
 
 def hidden_backward(
-    plane, planes, own_rows, parts, hidden, gates, upstream, gain, router, gathered, experts
+    plane, planes, parts, hidden, gates, upstream, gain, router, gathered, experts
 ):
     count = hidden.shape[0]
     terms = len(parts)
@@ -601,7 +611,7 @@
         (
             grad_hidden, grad_branch, grad_mixed, grad_logits, grad_gain, out_weight, sems
         ) = refs[terms + 6 :]
-        wait = copies(out_weight_pairs(plane[0], planes, own_rows, gathered, out_weight), sems)
+        wait = copies(out_weight_pairs(plane[0], planes, gathered, out_weight), sems)
         returned = sum(part[...].astype(f32) for part in parts)
         tail = returned[:, D:]
         grad_gates = gates[...] * (tail + pltpu.roll(tail, PAD - experts, 1))
@@ -735,8 +745,22 @@
     def gather_ranks(value):
         return lax.all_gather(value, "ep", axis=0)
 
+    order = shift_order(planes)
+    in_parts, out_parts = (
+        {
+            step: lax.dynamic_index_in_dim(weight, (own + step) % share, 0, keepdims=False)
+            for step in [0] + order
+        }
+        for weight in (w_in, w_out)
+    )
+
+    def send(parts, steps):
+        return {step: shift_rep(parts[step], step) for step in steps}
+
+    stream = gather_ranks(tokens)
     out_rows = [w_o] + [shift_rep(w_o, step) for step in range(1, planes)]
     upstream_group = with_group(cotangent)
+    out_pieces = {0: out_parts[0], **send(out_parts, order[:1])}
     slab = jnp.concatenate(
         [
             w_qkv.reshape(dense_rows, 3, ranks, width)
@@ -758,29 +782,25 @@
     )
     slab = lax.all_to_all(slab, "ep", split_axis=0, concat_axis=0, tiled=True)
     slab = slab.reshape(ranks * dense_rows, 3 * width + PAD)
-    out_rows, upstream_group, slab = lax.optimization_barrier((out_rows, upstream_group, slab))
-    gathered = gather_ranks(jnp.concatenate([tokens, *out_rows], axis=0))
+    out_rows, upstream_group, out_pieces, slab = lax.optimization_barrier(
+        (out_rows, upstream_group, out_pieces, slab)
+    )
+    gathered = gather_ranks(jnp.concatenate(out_rows, axis=0))
     slab = ring_rep(slab)
     router = slab[:, 3 * width :]
     gain_pair = router[:, experts : experts + 2].reshape(-1).astype(f32)
     first_gain = gain_pair[None, :D]
     second_gain = gain_pair[None, D:]
-
-    def send_weight(weight, step):
-        part = lax.dynamic_index_in_dim(weight, (own + step) % share, 0, keepdims=False)
-        return shift_rep(part, step) if step else part
-
-    order = shift_order(planes)
-    early = after((w_in, w_out), slab)
-    in_pieces = {step: send_weight(early[0], step) for step in [0] + order[:1]}
-    out_parts = {step: send_weight(early[1], step) for step in [0] + order[:1]}
+    in_parts, out_parts = after((in_parts, out_parts), slab)
+    in_pieces = {0: in_parts[0], **send(in_parts, order[:1])}
+    out_pieces.update(send(out_parts, order[1:2]))
 
     segment = segments[0]
     cosine, sine = jax.vmap(lambda one: rope_tables(doc_positions(one), HD))(segment)
     sine = jnp.where(jnp.arange(HD) < HD // 2, -sine, sine)
     tables = (cosine, sine, segment[:, :, None], segment[:, None, :], qk_gains)
-    gathered, tables = lax.optimization_barrier((gathered, tables))
-    normed, proj = project(mine, gathered, first_gain, slab)
+    stream, tables = lax.optimization_barrier((stream, tables))
+    normed, proj = project(stream, first_gain, slab)
     proj = proj.reshape(ranks, micro, rows, 3 * width)
     upstream_all = gather_ranks(after(upstream_group, proj))
     mixed_h, query, keys, values, lses = attention_forward(proj, *tables)
@@ -790,15 +810,14 @@
         where[1:2], planes, mixed, tokens, gathered, second_gain, router, routes, experts
     )
     normed_two = payload[:, :D]
-    payload, in_pieces, out_parts = lax.optimization_barrier((payload, in_pieces, out_parts))
+    payload, in_pieces, out_pieces = lax.optimization_barrier((payload, in_pieces, out_pieces))
     payload = with_group(payload)
-    payload, late = lax.optimization_barrier((payload, (w_in, w_out)))
-    for step in order[1:]:
-        in_pieces[step] = send_weight(late[0], step)
-    in_pieces, late = lax.optimization_barrier((in_pieces, late))
-    for step in order[1:]:
-        out_parts[step] = send_weight(late[1], step)
+    payload, in_parts, out_parts = lax.optimization_barrier((payload, in_parts, out_parts))
+    in_pieces.update(send(in_parts, order[1:]))
+    in_pieces, out_parts = lax.optimization_barrier((in_pieces, out_parts))
+    out_pieces.update(send(out_parts, order[2:]))
     in_pieces = [in_pieces[step] for step in range(planes)]
+    out_pieces = [out_pieces[step] for step in range(planes)]
     payload = gather_ranks(payload)
 
     shape = (ranks, share, micro, rows, -1)
@@ -822,12 +841,8 @@
             ]
         )
 
-    def send(parts, steps):
-        return {step: shift_rep(parts[step], step) for step in steps}
-
     tail, out_cut = lax.optimization_barrier((tail, out_cut))
     out_sent = send(out_cut, order)
-    out_pieces = [out_parts[step] for step in range(planes)]
     back = []
     returned = []
 
@@ -871,8 +886,8 @@
     def total(parts):
         return sum(part.astype(f32) for part in parts)
 
-    grad_inputs, branches, logit_grads = [], [], []
-    gain_two_sum = gain_one_sum = qk_sum = qkv_sum = 0.0
+    grad_inputs, branches, logit_grads, grad_projs = [], [], [], []
+    gain_two_sum = gain_one_sum = qk_sum = 0.0
     in_cut, mixtures, out_sent = lax.optimization_barrier(
         (in_cut, [part[:2] for part in back], out_sent)
     )
@@ -881,51 +896,55 @@
     releases = [order[:1]] + [[]] * (micro - 2) + [order[1:-1]]
     for step in range(micro):
         at = slice(step * rows, (step + 1) * rows)
-        parts, in_sent, mixtures = lax.optimization_barrier((returned[step], in_sent, mixtures))
+        parts = after(returned[step], [one[2] for one in grad_inputs])
+        parts, in_sent, crossed = lax.optimization_barrier((parts, in_sent, crossed))
         parts = exchange_back(parts)
-        parts, in_cut = lax.optimization_barrier((parts, in_cut))
+        parts, in_cut, mixtures = lax.optimization_barrier((parts, in_cut, mixtures))
         in_sent.update(send(in_cut, releases[step]))
+        if step == micro - 1:
+            crossed.append(cross(mixtures[step]))
         grad_hidden, grad_branch, grad_mixed, grad_logits, gain_two = hidden_backward(
-            where[1:2], planes, mine, parts, hidden[at], gates[at], cotangent[at], second_gain,
+            where[1:2], planes, parts, hidden[at], gates[at], cotangent[at], second_gain,
             router, gathered, experts,
         )
         branches.append(grad_branch)
         logit_grads.append(grad_logits)
         gain_two_sum = gain_two_sum + gain_two
         grad_mixed = lax.all_to_all(grad_mixed, "ep", split_axis=1, concat_axis=0, tiled=True)
-        if step == micro - 1:
+        if step < micro - 1:
             grad_mixed, mixtures = lax.optimization_barrier((grad_mixed, mixtures))
-            crossed = [cross(part) for part in mixtures]
+            crossed.append(cross(mixtures[step]))
         grad_proj, grad_qk = attention_backward(
             step, proj, *tables, query, keys, values, lses, grad_mixed
         )
+        qk_sum = qk_sum + grad_qk.reshape(-1)
         if step == micro - 1:
             last = in_cut[order[-1]]
             half = last.shape[0] // 2
-            grad_proj, in_sent, last = lax.optimization_barrier((grad_proj, in_sent, last))
+            grad_proj, in_sent, last, crossed = lax.optimization_barrier(
+                (grad_proj, in_sent, last, crossed)
+            )
             last_sent = [shift_rep(last[:half], order[-1])]
-        qk_sum = qk_sum + grad_qk.reshape(-1)
-        grad_normed, gain_one = project_backward(step, grad_proj, gathered, slab)
+        grad_projs.append(grad_proj)
+        grad_normed, gain_one = project_backward(step, grad_proj, stream, slab)
         gain_one_sum = gain_one_sum + gain_one
         grad_inputs.append(
-            (at, grad_hidden, lax.psum_scatter(grad_normed, "ep", scatter_dimension=0, tiled=True))
+            (
+                at,
+                grad_hidden,
+                grad_normed,
+                lax.psum_scatter(grad_normed, "ep", scatter_dimension=0, tiled=True),
+            )
         )
-        grad_proj = after(grad_proj, grad_normed)
-        qkv_sum = qkv_sum + dot(
-            normed.reshape(ranks, micro, rows, D)[:, step].reshape(length, D),
-            grad_proj.reshape(length, 3 * width),
-            ((0,), (0,)),
-        )
-    grad_w_out = sum_rep({0: out_cut[0], **out_sent})
-
-    out_sum = dot(mixed, after(jnp.concatenate(branches, axis=0), grad_normed), ((0,), (0,))).astype(bf16)
-    out_sum = out_sum.reshape(planes, ranks // 2, 2, dense_rows, D).transpose(2, 1, 0, 3, 4)
-    out_crossed = cross(
-        pair_sum(
-            *(
-                lax.dynamic_index_in_dim(out_sum, rank % 2 ^ other, 0, keepdims=False)
-                for other in range(2)
+    branches = after(jnp.concatenate(branches, axis=0), grad_normed)
+    out_sum = dot(mixed, branches, ((0,), (0,))).astype(bf16)
+    out_sum = out_sum.reshape(planes, ranks // 2, 2, dense_rows, D)
+    out_sum = pair_sum(
+        *(
+            lax.dynamic_index_in_dim(out_sum, rank % 2 ^ other, 2, keepdims=False).transpose(
+                1, 0, 2, 3
             )
+            for other in range(2)
         )
     )
 
@@ -941,38 +960,35 @@
     )
     count = small.shape[1]
 
-    def pack(main, small):
-        high, low = two_parts(small)
-        blank = jnp.zeros((small.shape[0], PAD - 2 * count), bf16)
-        return jnp.concatenate([main.astype(bf16), high, low, blank], axis=1)
-
-    def unpack(packed):
-        packed = packed.astype(f32)
-        split = packed.shape[-1] - PAD
-        tail = packed[..., split:]
-        return packed[..., :split], tail[..., :count] + tail[..., count : 2 * count]
-
-    packed, crossed, last_sent, last = lax.optimization_barrier(
-        (pack(qkv_sum, small), crossed, last_sent, last)
-    )
+    def halves(value):
+        high, low = two_parts(value)
+        blank = jnp.zeros((value.shape[0], PAD - 2 * count), bf16)
+        return jnp.concatenate([high, low, blank], axis=1)
+
+    def joined(value):
+        return value[..., :count].astype(f32) + value[..., count : 2 * count].astype(f32)
+
+    grad_projs, out_sum = lax.optimization_barrier((grad_projs, out_sum))
+    out_crossed = cross(out_sum)
+    packed = weight_gradient(
+        where,
+        planes,
+        normed.reshape(ranks * mine, D),
+        [jnp.stack(grad_projs, axis=1).reshape(ranks * mine, 3 * width)],
+        halves(small),
+    )
+    packed, last_sent, last = lax.optimization_barrier((packed, last_sent, last))
+    packed_sent = [packed[0]] + [shift_rep(packed[step], step) for step in range(1, planes)]
     last_sent = last_sent + [shift_rep(last[half:], order[-1])]
-    part_rows = D // planes
-    main = lax.dynamic_slice_in_dim(qkv_sum, plane * part_rows, part_rows, 0)
-    small = lax.dynamic_slice_in_dim(small, plane * part_rows, part_rows, 0)
-    packed_sent = [
-        shift_rep(
-            lax.dynamic_slice_in_dim(packed, (plane + step) % planes * part_rows, part_rows, 0),
-            step,
-        )
-        for step in range(1, planes)
-    ]
+    packed_sent, last_sent = lax.optimization_barrier((packed_sent, last_sent))
     mixture = []
     for parts in crossed:
         parts = total(parts)
         mixture.append(parts[0] + total(exchange_back(parts.astype(bf16))[1:]))
     output = (hidden + jnp.concatenate(mixture, axis=0)).astype(bf16)
     grad_tokens = []
-    for at, grad_hidden, grad_normed in grad_inputs:
+    for at, grad_hidden, _, grad_normed in grad_inputs:
+        grad_normed = after(grad_normed, packed_sent)
         own_stream = tokens[at].astype(f32)
         grad_tokens.append(
             grad_hidden
@@ -980,18 +996,17 @@
                 own_stream, inverse_rms(own_stream), first_gain, grad_normed.astype(f32)
             )
         )
-    packed_sent, last_sent = lax.optimization_barrier((packed_sent, last_sent))
     in_sent[order[-1]] = jnp.concatenate(last_sent, axis=0)
-    for part in packed_sent:
-        part_main, part_small = unpack(part)
-        main, small = main + part_main, small + part_small
-    packed = pack(main, small).reshape(ranks, dense_rows, -1)
+    main = total([part[:, : 3 * width] for part in packed_sent]).astype(bf16)
+    small = sum(joined(part[:, 3 * width :]) for part in packed_sent)
+    packed = jnp.concatenate([main, halves(small)], axis=1).reshape(ranks, dense_rows, -1)
     packed = lax.all_to_all(packed, "ep", split_axis=0, concat_axis=0, tiled=True)
-    main, small = unpack(packed)
+    main = packed[..., : 3 * width].astype(f32)
+    small = jnp.sum(joined(packed[..., 3 * width :]), axis=0)
     grad_w_qkv = (
         main.reshape(ranks, dense_rows, 3, width).transpose(1, 2, 0, 3).reshape(dense_rows, 3 * D)
     )
-    small = jnp.sum(small, axis=0)
+    grad_w_out = sum_rep({0: out_cut[0], **out_sent})
     grad_w_in = sum_rep({0: in_cut[0], **in_sent})
     out_sum = total(out_crossed)
     grad_w_o = lax.dynamic_index_in_dim(out_sum, plane, 0, keepdims=False)

time: 1200 us -> 1150 us (0.958)
  waiting for transfers between devices: 554 us -> 514 us
  matrix products: 17.1 us -> 3.87 us
    ppermute x12, waiting for transfers between devices: 106 us -> 33 us  [swap(): return lax.ppermute(value, 'ep', [(i, i ^ step) for i in range(ranks)])]
    all_to_all x2, waiting for transfers between devices: 11.6 us -> 55.2 us  [on_device(): lax.all_to_all(grad_mixed, 'ep', split_axis=1, concat_axis=0, tiled=True)]
    ppermute x25, waiting for transfers between devices: 274 us -> 303 us  [shift_rep(): lax.ppermute(value, 'rep', [(i, (i + step) % count) for i in range(count)])]
    ppermute x6, waiting for transfers between devices: 120 us -> 97.4 us  [exchange(): return lax.ppermute(value, 'rep', pairs)]
    ppermute x25, starting transfers between devices: 95 us -> 73 us  [shift_rep(): lax.ppermute(value, 'rep', [(i, (i + step) % count) for i in range(count)])]
    all_gather x3 -> x4, waiting for transfers between devices: 19 us -> 0.04 us  [gather_ranks(): return lax.all_gather(value, 'ep', axis=0)]
    ppermute x6, starting transfers between devices: 17.9 us -> 32.2 us  [exchange(): return lax.ppermute(value, 'rep', pairs)]
    dot_general x4 -> x2, matrix products: 17.1 us -> 3.87 us  [dot(): return lax.dot_general(a, b, (dims, ((), ())), preferred_element_type=f32)]
  transfers between devices with their start and end apart: 55 -> 56, of which waited for: 31 -> 21; matrix products, arithmetic and copies ran while one was open for 14% -> 12% of each run, Pallas kernels for 20% -> 23%
where the time goes in v5:
time: 1150 us; the launch traced here: 1140 us
  waiting for transfers between devices  514 us (45%)
  Pallas kernels  304 us (26%)
  starting transfers between devices  140 us (12%)
  local copies, waits for them, and re-layouts  89.4 us (8%)
  other arithmetic  76.2 us (7%)
  between operations  15.6 us (1%)
    ppermute x25, waiting for transfers between devices, shift_rep(): lax.ppermute(value, 'rep', [(i, (i + step) % count) for i in range(count)])  303 us
    ppermute x6, waiting for transfers between devices, exchange(): return lax.ppermute(value, 'rep', pairs)  97.4 us
    pallas_call x2, Pallas kernels, expert_backward(): pl.pallas_call(kernel, grid_spec=pltpu.PrefetchScalarGridSpec(num_scalar_...  81 us
    ppermute x25, starting transfers between devices, shift_rep(): lax.ppermute(value, 'rep', [(i, (i + step) % count) for i in range(count)])  73 us
    pallas_call x3, Pallas kernels, weight_gradient(): pl.pallas_call(kernel, grid_spec=pltpu.PrefetchScalarGridSpec(num_scalar_...  56.7 us
    all_to_all x2, waiting for transfers between devices, on_device(): lax.all_to_all(grad_mixed, 'ep', split_axis=1, concat_axis=0, tiled=True)  55.2 us
    pallas_call x1, Pallas kernels, expert_forward(): pl.pallas_call(kernel, grid_spec=pltpu.PrefetchScalarGridSpec(num_scalar_...  40.3 us
    pallas_call x2, Pallas kernels, attention_backward(): pl.pallas_call(lambda *refs: backward_kernel(heads, *refs), grid=(1,), in...  34.4 us
  transfers between devices with their start and end apart: 56, of which 21 were waited for; matrix products, arithmetic and copies ran while one was open for 12% of the time, Pallas kernels for 23%

profile of v5, /device:TPU:0, one launch (start us, length us, event | category | flops | bytes accessed | tf_op | source)
XLA Modules:
  0.0 1142.9 jit_solution(14900122660914967483)
XLA Ops:
  28.4 40.7 %collective-permute-done.3 = bf16[256,2048]{1,0:T(8,128)(2,1)} collective-permute-done((bf16[256,2048]{1,0:T(8,128)(2,1)}, bf16[256,2048]{1,0:T(8,128)(2,1)}, u32[]{:S(2)}, u32[]{:S(2)}) %collective-permute-start.3) | collective-permute-done | bytes 1048608 | tf_op jit(solution)/shard_map/ppermute | solution.py:740
  78.3 21.6 %collective-permute-done.5 = bf16[512,896]{1,0:T(8,128)(2,1)} collective-permute-done((bf16[512,896]{1,0:T(8,128)(2,1)S(1)}, bf16[512,896]{1,0:T(8,128)(2,1)}, u32[]{:S(2)}, u32[]{:S(2)}) %collective-permute-start.5) | collective-permute-done | bytes 917536 | tf_op jit(solution)/shard_map/ppermute | solution.py:689
  100.7 21.9 %collective-permute-done.6 = bf16[512,896]{1,0:T(8,128)(2,1)} collective-permute-done((bf16[512,896]{1,0:T(8,128)(2,1)}, bf16[512,896]{1,0:T(8,128)(2,1)}, u32[]{:S(2)}, u32[]{:S(2)}) %collective-permute-start.6) | collective-permute-done | bytes 917536 | tf_op jit(solution)/shard_map/ppermute | solution.py:689
  175.2 21.7 %shard_map.179 = (bf16[8,2,128,256]{3,2,1,0:T(8,128)(2,1)}, bf16[2,1024,256]{2,1,0:T(8,128)(2,1)S(1)}, bf16[2,1024,256]{2,1,0:T(8,128)(2,1)S(1)}, bf16[2,1024,256]{2,1,0:T(8,128)(2,1)}, f32[2,2,1024,1]{3,2,1,0:T(8,128)}) custom-call(f32[8,2,128,768]{3,2,1,0:T(8,128)} %bitcast.215, f32[2,1024,128]{2,1,0:T(8,128)} %get-tuple-element.150.refs_1_, ...), custom_call_target="tpu_custom_call" | custom-call | tf_op jit(solution)/shard_map/pallas_call | solution.py:198
  204.6 24.8 %all-to-all-done.1 = bf16[8,2,128,256]{3,2,1,0:T(8,128)(2,1)S(1)} async-done(((bf16[8,2,128,256]{3,2,1,0:T(8,128)(2,1)}), bf16[8,2,128,256]{3,2,1,0:T(8,128)(2,1)S(1)}, u32[]{:S(2)}, u32[]{:S(2)}) %all-to-all-start.1) | async-done | bytes 1048608 | tf_op jit(solution)/shard_map/all_to_all | solution.py:807
  239.6 23.1 %collective-permute-done.10 = bf16[256,2176]{1,0:T(8,128)(2,1)S(1)} collective-permute-done((bf16[256,2176]{1,0:T(8,128)(2,1)S(1)}, bf16[256,2176]{1,0:T(8,128)(2,1)S(1)}, u32[]{:S(2)}, u32[]{:S(2)}) %collective-permute-start.10) | collective-permute-done | bytes 1114144 | tf_op jit(solution)/shard_map/ppermute | solution.py:740
  267.2 86.9 %collective-permute-done.11.refs_2_ = bf16[512,2048]{1,0:T(8,128)(2,1)} collective-permute-done((bf16[512,2048]{1,0:T(8,128)(2,1)}, bf16[512,2048]{1,0:T(8,128)(2,1)}, u32[]{:S(2)}, u32[]{:S(2)}) %collective-permute-start.11) | collective-permute-done | bytes 2097184 | tf_op jit(solution)/shard_map/ppermute | solution.py:689
  354.1 44.4 %collective-permute-start.14 = (bf16[256,2048]{1,0:T(8,128)(2,1)}, bf16[256,2048]{1,0:T(8,128)(2,1)}, u32[]{:S(2)}, u32[]{:S(2)}) collective-permute-start(bf16[256,2048]{1,0:T(8,128)(2,1)} %get-tuple-element.197), channel_id=1, source_target_pairs={{0,16},{8,24},{16,0},{24,8},{1,17},{9,25},{17,1},{25,9},{2,18},{10... | collective-permute-start | bytes 3145736 | tf_op jit(solution)/shard_map/ppermute | solution.py:689
  398.4 40.3 %shard_map.181 = (bf16[2,4,288,2048]{3,2,1,0:T(8,128)(2,1)}, f32[2,4,288,128]{3,2,1,0:T(8,128)S(1)}, f32[2,4,288,2048]{3,2,1,0:T(8,128)}, bf16[2,4,288,1024]{3,2...) custom-call(s32[3]{0:T(128)S(1)} %pad_add_fusion.where, ...), custom_call_target="tpu_custom_call" | custom-call | flops 72477573120 | tf_op jit(solution)/shard_map/pallas_call | solution.py:429
  441.2 16.3 %shard_map.182 = bf16[4,256,2048]{2,1,0:T(8,128)(2,1)} custom-call(s32[3]{0:T(128)S(1)} %pad_add_fusion.where, bf16[2304,1024]{1,0:T(8,128)(2,1)} %bitcast.247, bf16[2304,2048]{1,0:T(8,128)(2,1)} %bitcast.245), custom_call_target="tpu_custom_call" | custom-call | flops 28991029248 | tf_op jit(solution)/shard_map/pallas_call | solution.py:583
  457.5 40.3 %shard_map.183 = (bf16[4,2,128,2048]{3,2,1,0:T(8,128)(2,1)}, bf16[4,2,128,2048]{3,2,1,0:T(8,128)(2,1)}, bf16[8,2,128,2176]{3,2,1,0:T(8,128)(2,1)}, bf16[4,288,2048]{2,1,0:T(8,128)(2,1)}) custom-call(s32[3]{0:T(128)S(1)} %pad_add_fusion.where, f32[2,4,288,128]{3,2,1,0:T(8,128)} %copy-done.38, f32[2,4,288,2048]{3,2,1,0:T(8,128)} %get-tuple-element.192.both, ...), custom_call_target="tpu_custom_call" | custom-call | flops 65229815808 | tf_op jit(solution)/shard_map/pallas_call | solution.py:527
  505.5 24.2 %collective-permute-done.13 = bf16[256,2048]{1,0:T(8,128)(2,1)} collective-permute-done((bf16[256,2048]{1,0:T(8,128)(2,1)S(1)}, bf16[256,2048]{1,0:T(8,128)(2,1)}, u32[]{:S(2)}, u32[]{:S(2)}) %collective-permute-start.13) | collective-permute-done | bytes 1048608 | tf_op jit(solution)/shard_map/ppermute | solution.py:689
  529.7 40.7 %shard_map.184 = (bf16[4,2,128,2048]{3,2,1,0:T(8,128)(2,1)}, bf16[4,2,128,2048]{3,2,1,0:T(8,128)(2,1)}, bf16[8,2,128,2176]{3,2,1,0:T(8,128)(2,1)}, bf16[4,288,2048]{2,1,0:T(8,128)(2,1)}) custom-call(s32[3]{0:T(128)S(1)} %pad_add_fusion.where, f32[2,4,288,128]{3,2,1,0:T(8,128)} %copy-done.38, f32[2,4,288,2048]{3,2,1,0:T(8,128)} %get-tuple-element.192.both, ...), custom_call_target="tpu_custom_call" | custom-call | flops 65229815808 | tf_op jit(solution)/shard_map/pallas_call | solution.py:527
  570.4 29.5 %shard_map.185 = bf16[4,512,2048]{2,1,0:T(8,128)(2,1)} custom-call(s32[3]{0:T(128)S(1)} %pad_add_fusion.where, bf16[2304,2048]{1,0:T(8,128)(2,1)} %bitcast.244, bf16[1152,2048]{1,0:T(8,128)(2,1)} %bitcast.246, bf16[1152,2048]{1,0:T(8,128)(2,1)} %bitcast.248), custom_call_target="tpu_custom_call" | custom-call | flops 57982058496 | tf_op jit(solution)/shard_map/pallas_call | solution.py:583
  655.0 15.1 %all-to-all-done.2 = bf16[128,8,256]{2,0,1:T(8,128)(2,1)S(1)} async-done(((bf16[128,8,256]{2,0,1:T(8,128)(2,1)}), bf16[128,8,256]{2,0,1:T(8,128)(2,1)S(1)}, u32[]{:S(2)}, u32[]{:S(2)}) %all-to-all-start.2) | async-done | bytes 524320 | tf_op jit(solution)/shard_map/all_to_all | solution.py:913
  679.0 17.0 %shard_map.187 = (bf16[8,128,768]{2,1,0:T(8,128)(2,1)}, f32[2,128]{1,0:T(2,128)S(1)}) custom-call(f32[8,2,128,768]{3,2,1,0:T(8,128)} %bitcast.216, f32[2,1024,128]{2,1,0:T(8,128)S(1)} %copy-done.4, f32[2,1024,128]{2,1,0:T(8,128)S(1)} %copy-done.3, s32[2,1024,1]{2,1,0:T(8,128)S(1)} %copy-done.5, s32[2,1,1024]{2,1,0:T(1,128)S(1)} %copy-done.29, ...), custom_call_target="tpu_custom_call" | custom-call | tf_op jit(solution)/shard_map/pallas_call | solution.py:220
  711.4 21.8 %collective-permute-done.23 = bf16[2,128,2048]{2,1,0:T(8,128)(2,1)} collective-permute-done((bf16[2,128,2048]{2,1,0:T(8,128)(2,1)}, bf16[2,128,2048]{2,1,0:T(8,128)(2,1)}, u32[]{:S(2)}, u32[]{:S(2)}) %collective-permute-start.23) | collective-permute-done | bytes 1048608 | tf_op jit(solution)/shard_map/ppermute | solution.py:874
  735.3 27.0 %collective-permute-start.24 = (bf16[128,2176]{1,0:T(8,128)(2,1)S(1)}, bf16[128,2176]{1,0:T(8,128)(2,1)S(1)}, u32[]{:S(2)}, u32[]{:S(2)}) collective-permute-start(bf16[128,2176]{1,0:T(8,128)(2,1)S(1)} %get-tuple-element.356), channel_id=1, source_target_pairs={{0,8},{8,0},{16,24},{24,16},{1,9},{9,1},{17,25},{25,17},{2,10},{10... | collective-permute-start | bytes 1671176 | tf_op jit(solution)/shard_map/ppermute | solution.py:740
  807.9 40.1 %all-to-all-done.3 = bf16[128,8,256]{2,0,1:T(8,128)(2,1)} async-done(((bf16[128,8,256]{2,0,1:T(8,128)(2,1)}), bf16[128,8,256]{2,0,1:T(8,128)(2,1)}, u32[]{:S(2)}, u32[]{:S(2)}) %all-to-all-start.3) | async-done | bytes 524320 | tf_op jit(solution)/shard_map/all_to_all | solution.py:913
  849.3 17.4 %shard_map.190 = (bf16[8,128,768]{2,1,0:T(8,128)(2,1)}, f32[2,128]{1,0:T(2,128)S(1)}) custom-call(f32[8,2,128,768]{3,2,1,0:T(8,128)} %bitcast.217, f32[2,1024,128]{2,1,0:T(8,128)S(1)} %copy-done.4, f32[2,1024,128]{2,1,0:T(8,128)S(1)} %copy-done.3, s32[2,1024,1]{2,1,0:T(8,128)S(1)} %copy-done.6, s32[2,1,1024]{2,1,0:T(1,128)S(1)} %copy-done.29, ...), custom_call_target="tpu_custom_call" | custom-call | tf_op jit(solution)/shard_map/pallas_call | solution.py:220
  868.1 14.2 %shard_map.191 = (bf16[1024,2048]{1,0:T(8,128)(2,1)}, f32[1,2048]{1,0:T(1,128)S(1)}) custom-call(bf16[8,128,768]{2,1,0:T(8,128)(2,1)S(1)} %copy-done.13, bf16[8,256,2048]{2,1,0:T(8,128)(2,1)} %bitcast.214, bf16[2048,896]{1,0:T(8,128)(2,1)} %copy-done), custom_call_target="tpu_custom_call" | custom-call | tf_op jit(solution)/shard_map/pallas_call | solution.py:673
  914.0 16.7 %collective-permute-done.30 = bf16[128,2048]{1,0:T(8,128)(2,1)} collective-permute-done((bf16[128,2048]{1,0:T(8,128)(2,1)}, bf16[128,2048]{1,0:T(8,128)(2,1)}, u32[]{:S(2)}, u32[]{:S(2)}) %collective-permute-start.30) | collective-permute-done | bytes 524320 | tf_op jit(solution)/shard_map/ppermute | solution.py:740
  988.5 58.2 %collective-permute-done.34 = bf16[512,896]{1,0:T(8,128)(2,1)} collective-permute-done((bf16[512,896]{1,0:T(8,128)(2,1)S(1)}, bf16[512,896]{1,0:T(8,128)(2,1)}, u32[]{:S(2)}, u32[]{:S(2)}) %collective-permute-start.34) | collective-permute-done | bytes 917536 | tf_op jit(solution)/shard_map/ppermute | solution.py:689
  1047.7 40.1 %collective-permute-done.36 = bf16[256,2048]{1,0:T(8,128)(2,1)S(1)} collective-permute-done((bf16[256,2048]{1,0:T(8,128)(2,1)S(1)}, bf16[256,2048]{1,0:T(8,128)(2,1)S(1)}, u32[]{:S(2)}, u32[]{:S(2)}) %collective-permute-start.36) | collective-permute-done | bytes 1048608 | tf_op jit(solution)/shard_map/ppermute | solution.py:689
  (359 shorter events, 383.6 us)
Async XLA Ops:
  7.2 139.7 %all-gather.9.cloned.1.call-start = ((), (), s32[]{:S(2)}) async-start(), calls=%async_computation.13 | async-start | bytes 9437184 | tf_op jit(solution)/shard_map/all_gather | solution.py:746
  22.7 207.6 %all-gather.11.cloned.1.call-start = ((), (), s32[]{:S(2)}) async-start(), calls=%async_computation.14 | async-start | bytes 9437184 | tf_op jit(solution)/shard_map/all_gather | solution.py:746
  76.3 322.1 %all-gather.15.cloned.1.call-start = ((), (), s32[]{:S(2)}) async-start(), calls=%async_computation.16 | async-start | bytes 18874368 | tf_op jit(solution)/shard_map/all_gather | solution.py:746
  170.0 69.6 %collective-permute-start.8 = (bf16[512,2048]{1,0:T(8,128)(2,1)}, bf16[512,2048]{1,0:T(8,128)(2,1)}, u32[]{:S(2)}, u32[]{:S(2)}) collective-permute-start(bf16[512,2048]{1,0:T(8,128)(2,1)} %get-tuple-element.167), channel_id=1, source_target_pairs={{0,8},{8,16},{16,24},{24,0},{1,9},{9,17},{17,25},{25,1},{2,10},{10... | collective-permute-start | bytes 6291464 | tf_op jit(solution)/shard_map/ppermute | solution.py:689
  202.6 195.9 %all-gather.13.cloned.1.call-start = ((), (), s32[]{:S(2)}) async-start(), calls=%async_computation.15 | async-start | bytes 20054016 | tf_op jit(solution)/shard_map/all_gather | solution.py:746
  264.3 352.5 %reduce-scatter.7.cloned.1.call-start = ((), (), s32[]{:S(2)}) async-start(), calls=%async_computation.10 | async-start | bytes 10027008 | tf_op jit(solution)/shard_map/reduce_scatter | solution.py:850
  264.4 89.7 %collective-permute-start.11 = (bf16[512,2048]{1,0:T(8,128)(2,1)}, bf16[512,2048]{1,0:T(8,128)(2,1)}, u32[]{:S(2)}, u32[]{:S(2)}) collective-permute-start(bf16[512,2048]{1,0:T(8,128)(2,1)} %get-tuple-element.180), channel_id=1, source_target_pairs={{0,16},{8,24},{16,0},{24,8},{1,17},{9,25},{17,1},{25,9},{2,18},{10... | collective-permute-start | bytes 6291464 | tf_op jit(solution)/shard_map/ppermute | solution.py:689
  264.5 89.5 %collective-permute-start.12 = (bf16[512,2048]{1,0:T(8,128)(2,1)}, bf16[512,2048]{1,0:T(8,128)(2,1)}, u32[]{:S(2)}, u32[]{:S(2)}) collective-permute-start(bf16[512,2048]{1,0:T(8,128)(2,1)} %get-tuple-element.181), channel_id=1, source_target_pairs={{0,24},{8,0},{16,8},{24,16},{1,25},{9,1},{17,9},{25,17},{2,26},{10... | collective-permute-start | bytes 6291464 | tf_op jit(solution)/shard_map/ppermute | solution.py:689
  354.1 103.4 %collective-permute-start.14 = (bf16[256,2048]{1,0:T(8,128)(2,1)}, bf16[256,2048]{1,0:T(8,128)(2,1)}, u32[]{:S(2)}, u32[]{:S(2)}) collective-permute-start(bf16[256,2048]{1,0:T(8,128)(2,1)} %get-tuple-element.197), channel_id=1, source_target_pairs={{0,16},{8,24},{16,0},{24,8},{1,17},{9,25},{17,1},{25,9},{2,18},{10... | collective-permute-start | bytes 3145736 | tf_op jit(solution)/shard_map/ppermute | solution.py:689
  497.8 213.6 %reduce-scatter.5.cloned.1.call-start = ((), (), s32[]{:S(2)}) async-start(), calls=%async_computation.9 | async-start | bytes 10027008 | tf_op jit(solution)/shard_map/reduce_scatter | solution.py:850
  502.9 97.0 %collective-permute-start.16 = (bf16[256,2048]{1,0:T(8,128)(2,1)}, bf16[256,2048]{1,0:T(8,128)(2,1)}, u32[]{:S(2)}, u32[]{:S(2)}) collective-permute-start(bf16[256,2048]{1,0:T(8,128)(2,1)} %get-tuple-element.338), channel_id=1, source_target_pairs={{0,16},{8,24},{16,0},{24,8},{1,17},{9,25},{17,1},{25,9},{2,18},{10... | collective-permute-start | bytes 3145736 | tf_op jit(solution)/shard_map/ppermute | solution.py:689
  505.5 94.4 %collective-permute-start.17 = (bf16[256,2048]{1,0:T(8,128)(2,1)}, bf16[256,2048]{1,0:T(8,128)(2,1)}, u32[]{:S(2)}, u32[]{:S(2)}) collective-permute-start(bf16[256,2048]{1,0:T(8,128)(2,1)} %get-tuple-element.337), channel_id=1, source_target_pairs={{0,24},{8,0},{16,8},{24,16},{1,25},{9,1},{17,9},{25,17},{2,26},{10... | collective-permute-start | bytes 3145736 | tf_op jit(solution)/shard_map/ppermute | solution.py:689
  636.4 96.7 %collective-permute-start.20 = (bf16[512,2048]{1,0:T(8,128)(2,1)}, bf16[512,2048]{1,0:T(8,128)(2,1)}, u32[]{:S(2)}, u32[]{:S(2)}) collective-permute-start(bf16[512,2048]{1,0:T(8,128)(2,1)} %slice_bitcast_fusion.2), channel_id=1, source_target_pairs={{0,8},{8,16},{16,24},{24,0},{1,9},{9,17},{17,25},{25,1},{2,10},{10... | collective-permute-start | bytes 6291464 | tf_op jit(solution)/shard_map/ppermute | solution.py:689
  654.9 432.9 %reduce-scatter.9.cloned.1.call-start = ((), (), s32[]{:S(2)}) async-start(), calls=%async_computation.11 | async-start | bytes 4718592 | tf_op jit(solution)/shard_map/reduce_scatter | solution.py:936
  779.6 87.1 %collective-permute-start.25 = (bf16[512,2048]{1,0:T(8,128)(2,1)}, bf16[512,2048]{1,0:T(8,128)(2,1)}, u32[]{:S(2)}, u32[]{:S(2)}) collective-permute-start(bf16[512,2048]{1,0:T(8,128)(2,1)} %get-tuple-element.323), channel_id=1, source_target_pairs={{0,24},{8,0},{16,8},{24,16},{1,25},{9,1},{17,9},{25,17},{2,26},{10... | collective-permute-start | bytes 6291464 | tf_op jit(solution)/shard_map/ppermute | solution.py:689
  785.3 81.4 %collective-permute-start.26 = (bf16[2,128,2048]{2,1,0:T(8,128)(2,1)}, bf16[2,128,2048]{2,1,0:T(8,128)(2,1)}, u32[]{:S(2)}, u32[]{:S(2)}) collective-permute-start(bf16[2,128,2048]{2,1,0:T(8,128)(2,1)} %get-tuple-element.331), channel_id=1, source_target_pairs={{0,2},{1,3},{2,0},{3,1},{4,6},{5,7},{6,4},{7,5},{8,10},{9,11},{10,... | collective-permute-start | bytes 3145736 | tf_op jit(solution)/shard_map/ppermute | solution.py:874
  785.5 81.2 %collective-permute-start.27 = (bf16[2,128,2048]{2,1,0:T(8,128)(2,1)}, bf16[2,128,2048]{2,1,0:T(8,128)(2,1)}, u32[]{:S(2)}, u32[]{:S(2)}) collective-permute-start(bf16[2,128,2048]{2,1,0:T(8,128)(2,1)} %get-tuple-element.330), channel_id=1, source_target_pairs={{0,4},{1,5},{2,6},{3,7},{4,0},{5,1},{6,2},{7,3},{8,12},{9,13},{10,... | collective-permute-start | bytes 3145736 | tf_op jit(solution)/shard_map/ppermute | solution.py:874
  787.3 79.3 %collective-permute-start.28 = (bf16[2,128,2048]{2,1,0:T(8,128)(2,1)}, bf16[2,128,2048]{2,1,0:T(8,128)(2,1)}, u32[]{:S(2)}, u32[]{:S(2)}) collective-permute-start(bf16[2,128,2048]{2,1,0:T(8,128)(2,1)} %get-tuple-element.329), channel_id=1, source_target_pairs={{0,6},{1,7},{2,4},{3,5},{4,2},{5,3},{6,0},{7,1},{8,14},{9,15},{10,... | collective-permute-start | bytes 3145736 | tf_op jit(solution)/shard_map/ppermute | solution.py:874
  804.1 327.8 %reduce-scatter.11.cloned.1.call-start = ((), (), s32[]{:S(2)}) async-start(), calls=%async_computation.12 | async-start | bytes 4718592 | tf_op jit(solution)/shard_map/reduce_scatter | solution.py:936
  961.3 85.3 %collective-permute-start.34 = (bf16[512,896]{1,0:T(8,128)(2,1)S(1)}, bf16[512,896]{1,0:T(8,128)(2,1)}, u32[]{:S(2)}, u32[]{:S(2)}) collective-permute-start(bf16[512,896]{1,0:T(8,128)(2,1)S(1)} %get-tuple-element.345), channel_id=1, source_target_pairs={{0,16},{8,24},{16,0},{24,8},{1,17},{9,25},{17,1},{25,9},{2,18},{10... | collective-permute-start | bytes 2752520 | tf_op jit(solution)/shard_map/ppermute | solution.py:689
  964.2 83.5 %collective-permute-start.35 = (bf16[512,896]{1,0:T(8,128)(2,1)S(1)}, bf16[512,896]{1,0:T(8,128)(2,1)}, u32[]{:S(2)}, u32[]{:S(2)}) collective-permute-start(bf16[512,896]{1,0:T(8,128)(2,1)S(1)} %get-tuple-element.344), channel_id=1, source_target_pairs={{0,24},{8,0},{16,8},{24,16},{1,25},{9,1},{17,9},{25,17},{2,26},{10... | collective-permute-start | bytes 2752520 | tf_op jit(solution)/shard_map/ppermute | solution.py:689
  965.2 122.5 %collective-permute-start.36 = (bf16[256,2048]{1,0:T(8,128)(2,1)S(1)}, bf16[256,2048]{1,0:T(8,128)(2,1)S(1)}, u32[]{:S(2)}, u32[]{:S(2)}) collective-permute-start(bf16[256,2048]{1,0:T(8,128)(2,1)S(1)} %slice.230), channel_id=1, source_target_pairs={{0,16},{8,24},{16,0},{24,8},{1,17},{9,25},{17,1},{25,9},{2,18},{10... | collective-permute-start | bytes 3145736 | tf_op jit(solution)/shard_map/ppermute | solution.py:689
  971.5 124.5 %collective-permute-start.39 = (bf16[4,64,2048]{2,1,0:T(8,128)(2,1)}, bf16[4,64,2048]{2,1,0:T(8,128)(2,1)}, u32[]{:S(2)}, u32[]{:S(2)}) collective-permute-start(bf16[4,64,2048]{2,1,0:T(8,128)(2,1)} %get-tuple-element.327), channel_id=1, source_target_pairs={{0,6},{1,7},{2,4},{3,5},{4,2},{5,3},{6,0},{7,1},{8,14},{9,15},{10,... | collective-permute-start | bytes 3145736 | tf_op jit(solution)/shard_map/ppermute | solution.py:874
  986.6 109.4 %collective-permute-start.38 = (bf16[4,64,2048]{2,1,0:T(8,128)(2,1)}, bf16[4,64,2048]{2,1,0:T(8,128)(2,1)}, u32[]{:S(2)}, u32[]{:S(2)}) collective-permute-start(bf16[4,64,2048]{2,1,0:T(8,128)(2,1)} %get-tuple-element.328), channel_id=1, source_target_pairs={{0,4},{1,5},{2,6},{3,7},{4,0},{5,1},{6,2},{7,3},{8,12},{9,13},{10,... | collective-permute-start | bytes 3145736 | tf_op jit(solution)/shard_map/ppermute | solution.py:874
  (99 other events, 2850.5 us)
Sparse Core Ops, SparseCore 0:
  9.9 66.9 all-gather.8
  78.7 54.3 all-gather.10
  162.4 98.4 all-gather.14
  264.4 93.0 all-gather.12
  497.9 76.9 reduce-scatter.6
  578.4 120.9 reduce-scatter.4
  780.8 81.6 reduce-scatter.8
  911.3 49.7 reduce-scatter.10

commit v6 on v5

--- a/solution.py
+++ b/solution.py
@@ -180,7 +180,7 @@
 
 
 def cost(products):
-    return pl.CostEstimate(flops=6 * products, bytes_accessed=0, transcendentals=0)
+    return pl.CostEstimate(flops=20 * products, bytes_accessed=0, transcendentals=0)
 
 
 def out(shape, dtype=bf16):
@@ -702,16 +702,17 @@
     return sorted(range(1, count), key=lambda step: (min(step, count - step), step))
 
 
-def ring_rep(value):
+def ring_rep(value, *work):
     count = lax.axis_size("rep")
     rank = lax.axis_index("rep")
     rows = value.shape[0]
     full = jnp.zeros((count * rows,) + value.shape[1:], value.dtype)
     full = lax.dynamic_update_slice_in_dim(full, value, rank * rows, 0)
     for step in range(1, count):
+        value, work = lax.optimization_barrier((value, work)) if step == 2 else (value, work)
         value = shift_rep(value, 1)
         full = lax.dynamic_update_slice_in_dim(full, value, (rank - step) % count * rows, 0)
-    return full
+    return full, work
 
 
 def on_device(
@@ -760,7 +761,6 @@
     stream = gather_ranks(tokens)
     out_rows = [w_o] + [shift_rep(w_o, step) for step in range(1, planes)]
     upstream_group = with_group(cotangent)
-    out_pieces = {0: out_parts[0], **send(out_parts, order[:1])}
     slab = jnp.concatenate(
         [
             w_qkv.reshape(dense_rows, 3, ranks, width)
@@ -782,27 +782,26 @@
     )
     slab = lax.all_to_all(slab, "ep", split_axis=0, concat_axis=0, tiled=True)
     slab = slab.reshape(ranks * dense_rows, 3 * width + PAD)
-    out_rows, upstream_group, out_pieces, slab = lax.optimization_barrier(
-        (out_rows, upstream_group, out_pieces, slab)
-    )
+    out_rows, upstream_group, slab = lax.optimization_barrier((out_rows, upstream_group, slab))
     gathered = gather_ranks(jnp.concatenate(out_rows, axis=0))
-    slab = ring_rep(slab)
+    segment = segments[0]
+    cosine, sine = jax.vmap(lambda one: rope_tables(doc_positions(one), HD))(segment)
+    sine = jnp.where(jnp.arange(HD) < HD // 2, -sine, sine)
+    tables = (cosine, sine, segment[:, :, None], segment[:, None, :], qk_gains)
+    slab, (tables, in_parts, out_parts) = ring_rep(slab, tables, in_parts, out_parts)
     router = slab[:, 3 * width :]
     gain_pair = router[:, experts : experts + 2].reshape(-1).astype(f32)
     first_gain = gain_pair[None, :D]
     second_gain = gain_pair[None, D:]
-    in_parts, out_parts = after((in_parts, out_parts), slab)
+    in_parts, out_parts, upstream_group, stream = after(
+        (in_parts, out_parts, upstream_group, stream), slab
+    )
     in_pieces = {0: in_parts[0], **send(in_parts, order[:1])}
-    out_pieces.update(send(out_parts, order[1:2]))
-
-    segment = segments[0]
-    cosine, sine = jax.vmap(lambda one: rope_tables(doc_positions(one), HD))(segment)
-    sine = jnp.where(jnp.arange(HD) < HD // 2, -sine, sine)
-    tables = (cosine, sine, segment[:, :, None], segment[:, None, :], qk_gains)
-    stream, tables = lax.optimization_barrier((stream, tables))
+    out_pieces = {0: out_parts[0], **send(out_parts, order[:2])}
+    upstream_all = gather_ranks(upstream_group)
+
     normed, proj = project(stream, first_gain, slab)
     proj = proj.reshape(ranks, micro, rows, 3 * width)
-    upstream_all = gather_ranks(after(upstream_group, proj))
     mixed_h, query, keys, values, lses = attention_forward(proj, *tables)
     mixed = lax.all_to_all(mixed_h, "ep", split_axis=0, concat_axis=3, tiled=True)
     mixed = mixed.reshape(mine, D)
@@ -860,7 +859,10 @@
             )
         )
         returned.append(scatter_ranks(back[step][2]))
-        tail, out_sent[order[step]] = after((tail, out_sent[order[step]]), back[step][2])
+        if step == 0:
+            tail, out_sent[order[0]] = after((tail, out_sent[order[0]]), back[step][2])
+        else:
+            tail = after(tail, back[step][2])
     rows_in = after(rows_in, tail)
     in_cut = weight_gradient(
         where,
@@ -896,13 +898,11 @@
     releases = [order[:1]] + [[]] * (micro - 2) + [order[1:-1]]
     for step in range(micro):
         at = slice(step * rows, (step + 1) * rows)
-        parts = after(returned[step], [one[2] for one in grad_inputs])
+        parts = after(returned[step], [one[1] for one in grad_inputs])
         parts, in_sent, crossed = lax.optimization_barrier((parts, in_sent, crossed))
         parts = exchange_back(parts)
         parts, in_cut, mixtures = lax.optimization_barrier((parts, in_cut, mixtures))
         in_sent.update(send(in_cut, releases[step]))
-        if step == micro - 1:
-            crossed.append(cross(mixtures[step]))
         grad_hidden, grad_branch, grad_mixed, grad_logits, gain_two = hidden_backward(
             where[1:2], planes, parts, hidden[at], gates[at], cotangent[at], second_gain,
             router, gathered, experts,
@@ -911,9 +911,8 @@
         logit_grads.append(grad_logits)
         gain_two_sum = gain_two_sum + gain_two
         grad_mixed = lax.all_to_all(grad_mixed, "ep", split_axis=1, concat_axis=0, tiled=True)
-        if step < micro - 1:
-            grad_mixed, mixtures = lax.optimization_barrier((grad_mixed, mixtures))
-            crossed.append(cross(mixtures[step]))
+        grad_mixed, mixtures = lax.optimization_barrier((grad_mixed, mixtures))
+        crossed.append(cross(mixtures[step]))
         grad_proj, grad_qk = attention_backward(
             step, proj, *tables, query, keys, values, lses, grad_mixed
         )
@@ -921,8 +920,8 @@
         if step == micro - 1:
             last = in_cut[order[-1]]
             half = last.shape[0] // 2
-            grad_proj, in_sent, last, crossed = lax.optimization_barrier(
-                (grad_proj, in_sent, last, crossed)
+            grad_proj, in_sent, last, grad_inputs = lax.optimization_barrier(
+                (grad_proj, in_sent, last, grad_inputs)
             )
             last_sent = [shift_rep(last[:half], order[-1])]
         grad_projs.append(grad_proj)
@@ -930,7 +929,6 @@
         gain_one_sum = gain_one_sum + gain_one
         grad_inputs.append(
             (
-                at,
                 grad_hidden,
                 grad_normed,
                 lax.psum_scatter(grad_normed, "ep", scatter_dimension=0, tiled=True),
@@ -979,35 +977,38 @@
     )
     packed, last_sent, last = lax.optimization_barrier((packed, last_sent, last))
     packed_sent = [packed[0]] + [shift_rep(packed[step], step) for step in range(1, planes)]
+    normed_sums = [one[2] for one in grad_inputs]
+    packed_sent, normed_sums, last, crossed = lax.optimization_barrier(
+        (packed_sent, normed_sums, last, crossed)
+    )
     last_sent = last_sent + [shift_rep(last[half:], order[-1])]
-    packed_sent, last_sent = lax.optimization_barrier((packed_sent, last_sent))
     mixture = []
     for parts in crossed:
         parts = total(parts)
         mixture.append(parts[0] + total(exchange_back(parts.astype(bf16))[1:]))
     output = (hidden + jnp.concatenate(mixture, axis=0)).astype(bf16)
     grad_tokens = []
-    for at, grad_hidden, _, grad_normed in grad_inputs:
-        grad_normed = after(grad_normed, packed_sent)
-        own_stream = tokens[at].astype(f32)
+    for step in range(micro):
+        grad_hidden, grad_normed = grad_inputs[step][0], normed_sums[step]
+        own_stream = tokens[step * rows : (step + 1) * rows].astype(f32)
         grad_tokens.append(
             grad_hidden
             + rms_backward(
                 own_stream, inverse_rms(own_stream), first_gain, grad_normed.astype(f32)
             )
         )
-    in_sent[order[-1]] = jnp.concatenate(last_sent, axis=0)
     main = total([part[:, : 3 * width] for part in packed_sent]).astype(bf16)
     small = sum(joined(part[:, 3 * width :]) for part in packed_sent)
     packed = jnp.concatenate([main, halves(small)], axis=1).reshape(ranks, dense_rows, -1)
     packed = lax.all_to_all(packed, "ep", split_axis=0, concat_axis=0, tiled=True)
+    packed, last_sent = lax.optimization_barrier((packed, last_sent))
     main = packed[..., : 3 * width].astype(f32)
     small = jnp.sum(joined(packed[..., 3 * width :]), axis=0)
     grad_w_qkv = (
         main.reshape(ranks, dense_rows, 3, width).transpose(1, 2, 0, 3).reshape(dense_rows, 3 * D)
     )
     grad_w_out = sum_rep({0: out_cut[0], **out_sent})
-    grad_w_in = sum_rep({0: in_cut[0], **in_sent})
+    grad_w_in = sum_rep({0: in_cut[0], **in_sent, order[-1]: jnp.concatenate(last_sent, axis=0)})
     out_sum = total(out_crossed)
     grad_w_o = lax.dynamic_index_in_dim(out_sum, plane, 0, keepdims=False)
     out_sum = out_sum.astype(bf16)

time: 1150 us -> 1110 us (0.965)
  starting transfers between devices: 140 us -> 108 us
  waiting for transfers between devices: 514 us -> 493 us
  blocking collectives: 0 us -> 18.4 us
    ppermute x12, waiting for transfers between devices: 33 us -> 93.8 us  [swap(): return lax.ppermute(value, 'ep', [(i, i ^ step) for i in range(ranks)])]
    all_to_all x2 -> x1, waiting for transfers between devices: 55.2 us -> 7.41 us  [on_device(): lax.all_to_all(grad_mixed, 'ep', split_axis=1, concat_axis=0, tiled=True)]
    ppermute x6, starting transfers between devices: 32.2 us -> 8.21 us  [exchange(): return lax.ppermute(value, 'rep', pairs)]
    ppermute x6, waiting for transfers between devices: 97.4 us -> 74.3 us  [exchange(): return lax.ppermute(value, 'rep', pairs)]
    all_to_all x0 -> x1, blocking collectives: none -> 18.4 us  [on_device(): lax.all_to_all(grad_mixed, 'ep', split_axis=1, concat_axis=0, tiled=True)]
  transfers between devices with their start and end apart: 56 -> 55, of which waited for: 21 -> 25; matrix products, arithmetic and copies ran while one was open for 12% -> 10% of each run, Pallas kernels for 23% -> 27%
where the time goes in v6:
time: 1110 us; the launch traced here: 1100 us
  waiting for transfers between devices  493 us (44%)
  Pallas kernels  309 us (28%)
  starting transfers between devices  108 us (10%)
  local copies, waits for them, and re-layouts  81.3 us (7%)
  other arithmetic  74.4 us (7%)
  blocking collectives  18.4 us (2%)
  between operations  15.5 us (1%)
    ppermute x25, waiting for transfers between devices, shift_rep(): lax.ppermute(value, 'rep', [(i, (i + step) % count) for i in range(count)])  292 us
    ppermute x12, waiting for transfers between devices, swap(): return lax.ppermute(value, 'ep', [(i, i ^ step) for i in range(ranks)])  93.8 us
    pallas_call x2, Pallas kernels, expert_backward(): pl.pallas_call(kernel, grid_spec=pltpu.PrefetchScalarGridSpec(num_scalar_...  84.5 us
    ppermute x6, waiting for transfers between devices, exchange(): return lax.ppermute(value, 'rep', pairs)  74.3 us
    ppermute x25, starting transfers between devices, shift_rep(): lax.ppermute(value, 'rep', [(i, (i + step) % count) for i in range(count)])  73.1 us
    pallas_call x3, Pallas kernels, weight_gradient(): pl.pallas_call(kernel, grid_spec=pltpu.PrefetchScalarGridSpec(num_scalar_...  57.1 us
    pallas_call x1, Pallas kernels, expert_forward(): pl.pallas_call(kernel, grid_spec=pltpu.PrefetchScalarGridSpec(num_scalar_...  40.4 us
    pallas_call x2, Pallas kernels, attention_backward(): pl.pallas_call(lambda *refs: backward_kernel(heads, *refs), grid=(1,), in...  33.6 us
  transfers between devices with their start and end apart: 55, of which 25 were waited for; matrix products, arithmetic and copies ran while one was open for 10% of the time, Pallas kernels for 27%

profile of v6, /device:TPU:0, one launch (start us, length us, event | category | flops | bytes accessed | tf_op | source)
XLA Modules:
  0.0 1103.3 jit_solution(10104473365285206655)
XLA Ops:
  25.9 20.6 %collective-permute-done.3 = bf16[256,2048]{1,0:T(8,128)(2,1)S(1)} collective-permute-done((bf16[256,2048]{1,0:T(8,128)(2,1)}, bf16[256,2048]{1,0:T(8,128)(2,1)S(1)}, u32[]{:S(2)}, u32[]{:S(2)}) %collective-permute-start.3) | collective-permute-done | bytes 1048608 | tf_op jit(solution)/shard_map/ppermute | solution.py:741
  67.4 16.1 %collective-permute-done.4 = bf16[512,896]{1,0:T(8,128)(2,1)S(1)} collective-permute-done((bf16[512,896]{1,0:T(8,128)(2,1)S(1)}, bf16[512,896]{1,0:T(8,128)(2,1)S(1)}, u32[]{:S(2)}, u32[]{:S(2)}) %collective-permute-start.4) | collective-permute-done | bytes 917536 | tf_op jit(solution)/shard_map/ppermute | solution.py:689
  83.5 22.4 %collective-permute-done.5 = bf16[512,896]{1,0:T(8,128)(2,1)S(1)} collective-permute-done((bf16[512,896]{1,0:T(8,128)(2,1)S(1)}, bf16[512,896]{1,0:T(8,128)(2,1)S(1)}, u32[]{:S(2)}, u32[]{:S(2)}) %collective-permute-start.5) | collective-permute-done | bytes 917536 | tf_op jit(solution)/shard_map/ppermute | solution.py:689
  111.1 16.4 %collective-permute-done.6 = bf16[512,896]{1,0:T(8,128)(2,1)} collective-permute-done((bf16[512,896]{1,0:T(8,128)(2,1)S(1)}, bf16[512,896]{1,0:T(8,128)(2,1)}, u32[]{:S(2)}, u32[]{:S(2)}) %collective-permute-start.6) | collective-permute-done | bytes 917536 | tf_op jit(solution)/shard_map/ppermute | solution.py:689
  151.7 21.7 %shard_map.179 = (bf16[8,2,128,256]{3,2,1,0:T(8,128)(2,1)}, bf16[2,1024,256]{2,1,0:T(8,128)(2,1)S(1)}, bf16[2,1024,256]{2,1,0:T(8,128)(2,1)S(1)}, bf16[2,1024,256]{2,1,0:T(8,128)(2,1)}, f32[2,2,1024,1]{3,2,1,0:T(8,128)}) custom-call(f32[8,2,128,768]{3,2,1,0:T(8,128)} %bitcast.215, f32[2,1024,128]{2,1,0:T(8,128)} %get-tuple-element.174.refs_1_, ...), custom_call_target="tpu_custom_call" | custom-call | tf_op jit(solution)/shard_map/pallas_call | solution.py:198
  181.2 24.8 %all-to-all-done.1 = bf16[8,2,128,256]{3,2,1,0:T(8,128)(2,1)S(1)} async-done(((bf16[8,2,128,256]{3,2,1,0:T(8,128)(2,1)}), bf16[8,2,128,256]{3,2,1,0:T(8,128)(2,1)S(1)}, u32[]{:S(2)}, u32[]{:S(2)}) %all-to-all-start.1) | async-done | bytes 1048608 | tf_op jit(solution)/shard_map/all_to_all | solution.py:806
  221.5 25.8 %collective-permute-done.10 = bf16[256,2176]{1,0:T(8,128)(2,1)S(1)} collective-permute-done((bf16[256,2176]{1,0:T(8,128)(2,1)S(1)}, bf16[256,2176]{1,0:T(8,128)(2,1)S(1)}, u32[]{:S(2)}, u32[]{:S(2)}) %collective-permute-start.10) | collective-permute-done | bytes 1114144 | tf_op jit(solution)/shard_map/ppermute | solution.py:741
  252.1 90.0 %collective-permute-done.11.refs_2_ = bf16[512,2048]{1,0:T(8,128)(2,1)} collective-permute-done((bf16[512,2048]{1,0:T(8,128)(2,1)}, bf16[512,2048]{1,0:T(8,128)(2,1)}, u32[]{:S(2)}, u32[]{:S(2)}) %collective-permute-start.11) | collective-permute-done | bytes 2097184 | tf_op jit(solution)/shard_map/ppermute | solution.py:689
  342.1 44.1 %collective-permute-start.13 = (bf16[256,2048]{1,0:T(8,128)(2,1)}, bf16[256,2048]{1,0:T(8,128)(2,1)}, u32[]{:S(2)}, u32[]{:S(2)}) collective-permute-start(bf16[256,2048]{1,0:T(8,128)(2,1)} %get-tuple-element.220), channel_id=1, source_target_pairs={{0,16},{8,24},{16,0},{24,8},{1,17},{9,25},{17,1},{25,9},{2,18},{10... | collective-permute-start | bytes 3145736 | tf_op jit(solution)/shard_map/ppermute | solution.py:689
  386.2 40.4 %shard_map.181 = (bf16[2,4,288,2048]{3,2,1,0:T(8,128)(2,1)}, f32[2,4,288,128]{3,2,1,0:T(8,128)S(1)}, f32[2,4,288,2048]{3,2,1,0:T(8,128)}, bf16[2,4,288,1024]{3,2...) custom-call(s32[3]{0:T(128)S(1)} %pad_add_fusion.where, ...), custom_call_target="tpu_custom_call" | custom-call | flops 241591910400 | tf_op jit(solution)/shard_map/pallas_call | solution.py:429
  426.7 16.8 %shard_map.182 = bf16[4,256,2048]{2,1,0:T(8,128)(2,1)} custom-call(s32[3]{0:T(128)S(1)} %pad_add_fusion.where, bf16[2304,1024]{1,0:T(8,128)(2,1)} %bitcast.249, bf16[2304,2048]{1,0:T(8,128)(2,1)} %bitcast.248), custom_call_target="tpu_custom_call" | custom-call | flops 96636764160 | tf_op jit(solution)/shard_map/pallas_call | solution.py:583
  448.9 40.4 %shard_map.183 = (bf16[4,2,128,2048]{3,2,1,0:T(8,128)(2,1)}, bf16[4,2,128,2048]{3,2,1,0:T(8,128)(2,1)}, bf16[8,2,128,2176]{3,2,1,0:T(8,128)(2,1)}, bf16[4,288,2048]{2,1,0:T(8,128)(2,1)}) custom-call(s32[3]{0:T(128)S(1)} %pad_add_fusion.where, f32[2,4,288,128]{3,2,1,0:T(8,128)} %copy-done.28, f32[2,4,288,2048]{3,2,1,0:T(8,128)} %get-tuple-element.215.both, ...), custom_call_target="tpu_custom_call" | custom-call | flops 217432719360 | tf_op jit(solution)/shard_map/pallas_call | solution.py:527
  491.9 44.2 %shard_map.184 = (bf16[4,2,128,2048]{3,2,1,0:T(8,128)(2,1)}, bf16[4,2,128,2048]{3,2,1,0:T(8,128)(2,1)}, bf16[8,2,128,2176]{3,2,1,0:T(8,128)(2,1)}, bf16[4,288,2048]{2,1,0:T(8,128)(2,1)}) custom-call(s32[3]{0:T(128)S(1)} %pad_add_fusion.where, f32[2,4,288,128]{3,2,1,0:T(8,128)} %copy-done.28, f32[2,4,288,2048]{3,2,1,0:T(8,128)} %get-tuple-element.215.both, ...), custom_call_target="tpu_custom_call" | custom-call | flops 217432719360 | tf_op jit(solution)/shard_map/pallas_call | solution.py:527
  536.5 29.2 %shard_map.185 = bf16[4,512,2048]{2,1,0:T(8,128)(2,1)} custom-call(s32[3]{0:T(128)S(1)} %pad_add_fusion.where, bf16[2304,2048]{1,0:T(8,128)(2,1)} %bitcast.247, bf16[1152,2048]{1,0:T(8,128)(2,1)} %bitcast.250, bf16[1152,2048]{1,0:T(8,128)(2,1)} %bitcast.251), custom_call_target="tpu_custom_call" | custom-call | flops 193273528320 | tf_op jit(solution)/shard_map/pallas_call | solution.py:583
  608.9 18.4 %all_to_all.63 = bf16[128,8,256]{2,0,1:T(8,128)(2,1)S(1)} all-to-all(bf16[128,8,256]{2,0,1:T(8,128)(2,1)S(1)} %bitcast.232), channel_id=1, replica_groups=mesh['rep'=4,'ep'=8] {'ep'}, dimensions={1} | all-to-all | bytes 1048576 | tf_op jit(solution)/shard_map/all_to_all | solution.py:913
  627.4 16.8 %shard_map.187 = (bf16[8,128,768]{2,1,0:T(8,128)(2,1)}, f32[2,128]{1,0:T(2,128)S(1)}) custom-call(f32[8,2,128,768]{3,2,1,0:T(8,128)} %bitcast.216, f32[2,1024,128]{2,1,0:T(8,128)S(1)} %copy-done.2, f32[2,1024,128]{2,1,0:T(8,128)S(1)} %copy-done.1, s32[2,1024,1]{2,1,0:T(8,128)S(1)} %copy-done.3, s32[2,1,1024]{2,1,0:T(1,128)S(1)} %copy-done.22, ...), custom_call_target="tpu_custom_call" | custom-call | tf_op jit(solution)/shard_map/pallas_call | solution.py:220
  672.9 34.2 %collective-permute-done.21 = bf16[2,128,2048]{2,1,0:T(8,128)(2,1)} collective-permute-done((bf16[2,128,2048]{2,1,0:T(8,128)(2,1)}, bf16[2,128,2048]{2,1,0:T(8,128)(2,1)}, u32[]{:S(2)}, u32[]{:S(2)}) %collective-permute-start.21) | collective-permute-done | bytes 1048608 | tf_op jit(solution)/shard_map/ppermute | solution.py:876
  707.1 18.6 %collective-permute-done.22 = bf16[2,128,2048]{2,1,0:T(8,128)(2,1)} collective-permute-done((bf16[2,128,2048]{2,1,0:T(8,128)(2,1)}, bf16[2,128,2048]{2,1,0:T(8,128)(2,1)}, u32[]{:S(2)}, u32[]{:S(2)}) %collective-permute-start.22) | collective-permute-done | bytes 1048608 | tf_op jit(solution)/shard_map/ppermute | solution.py:876
  770.3 16.8 %shard_map.190 = (bf16[8,128,768]{2,1,0:T(8,128)(2,1)}, f32[2,128]{1,0:T(2,128)S(1)}) custom-call(f32[8,2,128,768]{3,2,1,0:T(8,128)} %bitcast.217, f32[2,1024,128]{2,1,0:T(8,128)S(1)} %copy-done.2, f32[2,1024,128]{2,1,0:T(8,128)S(1)} %copy-done.1, s32[2,1024,1]{2,1,0:T(8,128)S(1)} %copy-done.4, s32[2,1,1024]{2,1,0:T(1,128)S(1)} %copy-done.22, ...), custom_call_target="tpu_custom_call" | custom-call | tf_op jit(solution)/shard_map/pallas_call | solution.py:220
  845.5 24.9 %collective-permute-done.27 = bf16[256,2048]{1,0:T(8,128)(2,1)} collective-permute-done((bf16[256,2048]{1,0:T(8,128)(2,1)}, bf16[256,2048]{1,0:T(8,128)(2,1)}, u32[]{:S(2)}, u32[]{:S(2)}) %collective-permute-start.27) | collective-permute-done | bytes 1048608 | tf_op jit(solution)/shard_map/ppermute | solution.py:689
  915.2 52.0 %collective-permute-done.41 = bf16[64,2048]{1,0:T(8,128)(2,1)S(1)} collective-permute-done((bf16[64,2048]{1,0:T(8,128)(2,1)S(1)}, bf16[64,2048]{1,0:T(8,128)(2,1)S(1)}, u32[]{:S(2)}, u32[]{:S(2)}) %collective-permute-start.41) | collective-permute-done | bytes 262176 | tf_op jit(solution)/shard_map/ppermute | solution.py:689
  975.4 16.1 %collective-permute-done.29 = bf16[512,896]{1,0:T(8,128)(2,1)} collective-permute-done((bf16[512,896]{1,0:T(8,128)(2,1)S(1)}, bf16[512,896]{1,0:T(8,128)(2,1)}, u32[]{:S(2)}, u32[]{:S(2)}) %collective-permute-start.29) | collective-permute-done | bytes 917536 | tf_op jit(solution)/shard_map/ppermute | solution.py:689
  991.5 16.3 %collective-permute-done.30 = bf16[512,896]{1,0:T(8,128)(2,1)} collective-permute-done((bf16[512,896]{1,0:T(8,128)(2,1)S(1)}, bf16[512,896]{1,0:T(8,128)(2,1)}, u32[]{:S(2)}, u32[]{:S(2)}) %collective-permute-start.30) | collective-permute-done | bytes 917536 | tf_op jit(solution)/shard_map/ppermute | solution.py:689
  1052.2 24.8 %collective-permute-done.36 = bf16[256,2048]{1,0:T(8,128)(2,1)S(1)} collective-permute-done((bf16[256,2048]{1,0:T(8,128)(2,1)}, bf16[256,2048]{1,0:T(8,128)(2,1)S(1)}, u32[]{:S(2)}, u32[]{:S(2)}) %collective-permute-start.36) | collective-permute-done | bytes 1048608 | tf_op jit(solution)/shard_map/ppermute | solution.py:689
  (356 shorter events, 396.1 us)
Async XLA Ops:
  7.2 122.5 %all-gather.9.cloned.1.call-start = ((), (), s32[]{:S(2)}) async-start(), calls=%async_computation.13 | async-start | bytes 9437184 | tf_op jit(solution)/shard_map/all_gather | solution.py:747
  20.2 186.6 %all-gather.11.cloned.1.call-start = ((), (), s32[]{:S(2)}) async-start(), calls=%async_computation.14 | async-start | bytes 9437184 | tf_op jit(solution)/shard_map/all_gather | solution.py:747
  53.5 332.8 %all-gather.15.cloned.1.call-start = ((), (), s32[]{:S(2)}) async-start(), calls=%async_computation.16 | async-start | bytes 18874368 | tf_op jit(solution)/shard_map/all_gather | solution.py:747
  129.7 91.2 %collective-permute-start.7 = (bf16[512,2048]{1,0:T(8,128)(2,1)}, bf16[512,2048]{1,0:T(8,128)(2,1)}, u32[]{:S(2)}, u32[]{:S(2)}) collective-permute-start(bf16[512,2048]{1,0:T(8,128)(2,1)} %get-tuple-element.192), channel_id=1, source_target_pairs={{0,8},{8,16},{16,24},{24,0},{1,9},{9,17},{17,25},{25,1},{2,10},{10... | collective-permute-start | bytes 6291464 | tf_op jit(solution)/shard_map/ppermute | solution.py:689
  132.5 83.5 %collective-permute-start.8 = (bf16[256,2048]{1,0:T(8,128)(2,1)}, bf16[256,2048]{1,0:T(8,128)(2,1)}, u32[]{:S(2)}, u32[]{:S(2)}) collective-permute-start(bf16[256,2048]{1,0:T(8,128)(2,1)} %get-tuple-element.194), channel_id=1, source_target_pairs={{0,8},{8,16},{16,24},{24,0},{1,9},{9,17},{17,25},{25,1},{2,10},{10... | collective-permute-start | bytes 3145736 | tf_op jit(solution)/shard_map/ppermute | solution.py:689
  132.5 88.3 %collective-permute-start.9 = (bf16[256,2048]{1,0:T(8,128)(2,1)}, bf16[256,2048]{1,0:T(8,128)(2,1)}, u32[]{:S(2)}, u32[]{:S(2)}) collective-permute-start(bf16[256,2048]{1,0:T(8,128)(2,1)} %get-tuple-element.195), channel_id=1, source_target_pairs={{0,24},{8,0},{16,8},{24,16},{1,25},{9,1},{17,9},{25,17},{2,26},{10... | collective-permute-start | bytes 3145736 | tf_op jit(solution)/shard_map/ppermute | solution.py:689
  179.1 207.1 %all-gather.13.cloned.1.call-start = ((), (), s32[]{:S(2)}) async-start(), calls=%async_computation.15 | async-start | bytes 20054016 | tf_op jit(solution)/shard_map/all_gather | solution.py:747
  248.9 333.7 %reduce-scatter.5.cloned.1.call-start = ((), (), s32[]{:S(2)}) async-start(), calls=%async_computation.9 | async-start | bytes 10027008 | tf_op jit(solution)/shard_map/reduce_scatter | solution.py:849
  248.9 93.2 %collective-permute-start.11 = (bf16[512,2048]{1,0:T(8,128)(2,1)}, bf16[512,2048]{1,0:T(8,128)(2,1)}, u32[]{:S(2)}, u32[]{:S(2)}) collective-permute-start(bf16[512,2048]{1,0:T(8,128)(2,1)} %get-tuple-element.204), channel_id=1, source_target_pairs={{0,16},{8,24},{16,0},{24,8},{1,17},{9,25},{17,1},{25,9},{2,18},{10... | collective-permute-start | bytes 6291464 | tf_op jit(solution)/shard_map/ppermute | solution.py:689
  249.0 93.1 %collective-permute-start.12 = (bf16[512,2048]{1,0:T(8,128)(2,1)}, bf16[512,2048]{1,0:T(8,128)(2,1)}, u32[]{:S(2)}, u32[]{:S(2)}) collective-permute-start(bf16[512,2048]{1,0:T(8,128)(2,1)} %get-tuple-element.205), channel_id=1, source_target_pairs={{0,24},{8,0},{16,8},{24,16},{1,25},{9,1},{17,9},{25,17},{2,26},{10... | collective-permute-start | bytes 6291464 | tf_op jit(solution)/shard_map/ppermute | solution.py:689
  342.1 106.8 %collective-permute-start.13 = (bf16[256,2048]{1,0:T(8,128)(2,1)}, bf16[256,2048]{1,0:T(8,128)(2,1)}, u32[]{:S(2)}, u32[]{:S(2)}) collective-permute-start(bf16[256,2048]{1,0:T(8,128)(2,1)} %get-tuple-element.220), channel_id=1, source_target_pairs={{0,16},{8,24},{16,0},{24,8},{1,17},{9,25},{17,1},{25,9},{2,18},{10... | collective-permute-start | bytes 3145736 | tf_op jit(solution)/shard_map/ppermute | solution.py:689
  489.3 183.6 %reduce-scatter.7.cloned.1.call-start = ((), (), s32[]{:S(2)}) async-start(), calls=%async_computation.10 | async-start | bytes 10027008 | tf_op jit(solution)/shard_map/reduce_scatter | solution.py:849
  489.4 76.4 %collective-permute-start.16 = (bf16[256,2048]{1,0:T(8,128)(2,1)}, bf16[256,2048]{1,0:T(8,128)(2,1)}, u32[]{:S(2)}, u32[]{:S(2)}) collective-permute-start(bf16[256,2048]{1,0:T(8,128)(2,1)} %get-tuple-element.366), channel_id=1, source_target_pairs={{0,16},{8,24},{16,0},{24,8},{1,17},{9,25},{17,1},{25,9},{2,18},{10... | collective-permute-start | bytes 3145736 | tf_op jit(solution)/shard_map/ppermute | solution.py:689
  491.8 73.9 %collective-permute-start.17 = (bf16[256,2048]{1,0:T(8,128)(2,1)}, bf16[256,2048]{1,0:T(8,128)(2,1)}, u32[]{:S(2)}, u32[]{:S(2)}) collective-permute-start(bf16[256,2048]{1,0:T(8,128)(2,1)} %get-tuple-element.365), channel_id=1, source_target_pairs={{0,24},{8,0},{16,8},{24,16},{1,25},{9,1},{17,9},{25,17},{2,26},{10... | collective-permute-start | bytes 3145736 | tf_op jit(solution)/shard_map/ppermute | solution.py:689
  536.1 251.0 %reduce-scatter.9.cloned.1.call-start = ((), (), s32[]{:S(2)}) async-start(), calls=%async_computation.11 | async-start | bytes 4718592 | tf_op jit(solution)/shard_map/reduce_scatter | solution.py:934
  662.8 62.8 %collective-permute-start.20 = (bf16[512,2048]{1,0:T(8,128)(2,1)}, bf16[512,2048]{1,0:T(8,128)(2,1)}, u32[]{:S(2)}, u32[]{:S(2)}) collective-permute-start(bf16[512,2048]{1,0:T(8,128)(2,1)} %slice_bitcast_fusion.2), channel_id=1, source_target_pairs={{0,8},{8,16},{16,24},{24,0},{1,9},{9,17},{17,25},{25,1},{2,10},{10... | collective-permute-start | bytes 6291464 | tf_op jit(solution)/shard_map/ppermute | solution.py:689
  759.3 248.5 %reduce-scatter.11.cloned.1.call-start = ((), (), s32[]{:S(2)}) async-start(), calls=%async_computation.12 | async-start | bytes 4718592 | tf_op jit(solution)/shard_map/reduce_scatter | solution.py:934
  816.4 94.0 %collective-permute-start.31 = (bf16[2,128,2048]{2,1,0:T(8,128)(2,1)}, bf16[2,128,2048]{2,1,0:T(8,128)(2,1)}, u32[]{:S(2)}, u32[]{:S(2)}) collective-permute-start(bf16[2,128,2048]{2,1,0:T(8,128)(2,1)} %get-tuple-element.359), channel_id=1, source_target_pairs={{0,2},{1,3},{2,0},{3,1},{4,6},{5,7},{6,4},{7,5},{8,10},{9,11},{10,... | collective-permute-start | bytes 3145736 | tf_op jit(solution)/shard_map/ppermute | solution.py:876
  831.0 59.9 %collective-permute-start.38 = (bf16[4,64,2048]{2,1,0:T(8,128)(2,1)S(1)}, bf16[4,64,2048]{2,1,0:T(8,128)(2,1)}, u32[]{:S(2)}, u32[]{:S(2)}) collective-permute-start(bf16[4,64,2048]{2,1,0:T(8,128)(2,1)S(1)} %get-tuple-element.356), channel_id=1, source_target_pairs={{0,4},{1,5},{2,6},{3,7},{4,0},{5,1},{6,2},{7,3},{8,12},{9,13},{10,... | collective-permute-start | bytes 3145736 | tf_op jit(solution)/shard_map/ppermute | solution.py:876
  832.6 69.5 %collective-permute-start.37 = (bf16[4,64,2048]{2,1,0:T(8,128)(2,1)S(1)}, bf16[4,64,2048]{2,1,0:T(8,128)(2,1)}, u32[]{:S(2)}, u32[]{:S(2)}) collective-permute-start(bf16[4,64,2048]{2,1,0:T(8,128)(2,1)S(1)} %get-tuple-element.354), channel_id=1, source_target_pairs={{0,2},{1,3},{2,0},{3,1},{4,6},{5,7},{6,4},{7,5},{8,10},{9,11},{10,... | collective-permute-start | bytes 3145736 | tf_op jit(solution)/shard_map/ppermute | solution.py:876
  870.4 103.1 %collective-permute-start.32 = (bf16[2,128,2048]{2,1,0:T(8,128)(2,1)}, bf16[2,128,2048]{2,1,0:T(8,128)(2,1)S(1)}, u32[]{:S(2)}, u32[]{:S(2)}) collective-permute-start(bf16[2,128,2048]{2,1,0:T(8,128)(2,1)} %get-tuple-element.358), channel_id=1, source_target_pairs={{0,4},{1,5},{2,6},{3,7},{4,0},{5,1},{6,2},{7,3},{8,12},{9,13},{10,... | collective-permute-start | bytes 3145736 | tf_op jit(solution)/shard_map/ppermute | solution.py:876
  908.4 58.8 %collective-permute-start.40 = (bf16[64,2048]{1,0:T(8,128)(2,1)S(1)}, bf16[64,2048]{1,0:T(8,128)(2,1)S(1)}, u32[]{:S(2)}, u32[]{:S(2)}) collective-permute-start(bf16[64,2048]{1,0:T(8,128)(2,1)S(1)} %get-tuple-element.390), channel_id=1, source_target_pairs={{0,8},{8,16},{16,24},{24,0},{1,9},{9,17},{17,25},{25,1},{2,10},{10... | collective-permute-start | bytes 786440 | tf_op jit(solution)/shard_map/ppermute | solution.py:689
  910.4 63.1 %collective-permute-start.33 = (bf16[2,128,2048]{2,1,0:T(8,128)(2,1)S(1)}, bf16[2,128,2048]{2,1,0:T(8,128)(2,1)S(1)}, u32[]{:S(2)}, u32[]{:S(2)}) collective-permute-start(bf16[2,128,2048]{2,1,0:T(8,128)(2,1)S(1)} %copy-done.52), channel_id=1, source_target_pairs={{0,6},{1,7},{2,4},{3,5},{4,2},{5,3},{6,0},{7,1},{8,14},{9,15},{10,... | collective-permute-start | bytes 3145736 | tf_op jit(solution)/shard_map/ppermute | solution.py:876
  915.2 59.3 %collective-permute-start.28 = (bf16[512,896]{1,0:T(8,128)(2,1)S(1)}, bf16[512,896]{1,0:T(8,128)(2,1)}, u32[]{:S(2)}, u32[]{:S(2)}) collective-permute-start(bf16[512,896]{1,0:T(8,128)(2,1)S(1)} %get-tuple-element.374), channel_id=1, source_target_pairs={{0,8},{8,16},{16,24},{24,0},{1,9},{9,17},{17,25},{25,1},{2,10},{10... | collective-permute-start | bytes 2752520 | tf_op jit(solution)/shard_map/ppermute | solution.py:689
  (97 other events, 2536.8 us)
Sparse Core Ops, SparseCore 0:
  9.9 65.9 all-gather.8
  77.8 54.3 all-gather.10
  134.1 101.0 all-gather.14
  249.0 91.6 all-gather.12
  489.5 72.8 reduce-scatter.4
  565.8 83.7 reduce-scatter.6
  659.8 77.6 reduce-scatter.8
  818.4 89.8 reduce-scatter.10

commit v7 on v6

--- a/solution.py
+++ b/solution.py
@@ -556,7 +556,8 @@
     )
 
 
-def weight_gradient(where, planes, left, rights, tail=None):
+def weight_gradient(where, planes, left, rights, tail=None, first=0, steps=None):
+    steps = planes if steps is None else steps
     count, width = left.shape
     parts = len(rights)
     part_rows = count // parts
@@ -567,7 +568,7 @@
     whole = columns + sum(value.shape[1] for value in tails)
 
     def of_plane(i, where):
-        return (where[1] + i) % planes
+        return (where[1] + first + i) % planes
 
     def kernel(where, left, *refs):
         rights, target = refs[:parts], refs[-1]
@@ -584,7 +585,7 @@
         kernel,
         grid_spec=pltpu.PrefetchScalarGridSpec(
             num_scalar_prefetch=1,
-            grid=(planes,),
+            grid=(steps,),
             in_specs=[pl.BlockSpec((count, width), lambda i, where: (0, of_plane(i, where)))]
             + [fixed(right.shape) for right in rights]
             + [
@@ -593,8 +594,8 @@
             ],
             out_specs=pl.BlockSpec((1, width, whole), lambda i, _: (i, 0, 0)),
         ),
-        out_shape=out((planes, width, whole)),
-        cost_estimate=cost(count * planes * width * columns),
+        out_shape=out((steps, width, whole)),
+        cost_estimate=cost(0 if tails else count * steps * width * columns),
         compiler_params=params(),
     )(where, left, *rights, *tails)
 
@@ -796,8 +797,7 @@
     in_parts, out_parts, upstream_group, stream = after(
         (in_parts, out_parts, upstream_group, stream), slab
     )
-    in_pieces = {0: in_parts[0], **send(in_parts, order[:1])}
-    out_pieces = {0: out_parts[0], **send(out_parts, order[:2])}
+    in_pieces = {0: in_parts[0], **send(in_parts, order[:-1])}
     upstream_all = gather_ranks(upstream_group)
 
     normed, proj = project(stream, first_gain, slab)
@@ -809,12 +809,12 @@
         where[1:2], planes, mixed, tokens, gathered, second_gain, router, routes, experts
     )
     normed_two = payload[:, :D]
-    payload, in_pieces, out_pieces = lax.optimization_barrier((payload, in_pieces, out_pieces))
+    payload, in_pieces = lax.optimization_barrier((payload, in_pieces))
     payload = with_group(payload)
     payload, in_parts, out_parts = lax.optimization_barrier((payload, in_parts, out_parts))
-    in_pieces.update(send(in_parts, order[1:]))
+    in_pieces.update(send(in_parts, order[-1:]))
     in_pieces, out_parts = lax.optimization_barrier((in_pieces, out_parts))
-    out_pieces.update(send(out_parts, order[2:]))
+    out_pieces = {0: out_parts[0], **send(out_parts, order)}
     in_pieces = [in_pieces[step] for step in range(planes)]
     out_pieces = [out_pieces[step] for step in range(planes)]
     payload = gather_ranks(payload)
@@ -864,13 +864,16 @@
         else:
             tail = after(tail, back[step][2])
     rows_in = after(rows_in, tail)
-    in_cut = weight_gradient(
-        where,
-        planes,
-        rows_in.reshape(in_rows, D),
-        [back[step][3].reshape(in_rows // micro, 2 * FF) for step in range(micro)],
-    )
-    in_sent = {}
+    rows_flat = rows_in.reshape(in_rows, D)
+    grads_flat = [back[step][3].reshape(in_rows // micro, 2 * FF) for step in range(micro)]
+    near = weight_gradient(where, planes, rows_flat, grads_flat, first=order[0], steps=1)
+    rows_flat, near = lax.optimization_barrier((rows_flat, near))
+    far = weight_gradient(
+        where, planes, rows_flat, grads_flat, first=order[0] + 1, steps=planes - 1
+    )
+    in_cut = {(order[0] + 1 + i) % planes: far[i] for i in range(planes - 1)}
+    in_cut[order[0]] = near[0]
+    in_sent = send(in_cut, order[:1])
 
     def swap(value, step):
         return lax.ppermute(value, "ep", [(i, i ^ step) for i in range(ranks)])
@@ -878,31 +881,44 @@
     def pair_sum(keep, give):
         return (keep.astype(f32) + swap(give, 1).astype(f32)).astype(bf16)
 
-    def cross(value):
-        parts = []
-        for step in range(ranks // 2):
-            part = lax.dynamic_index_in_dim(value, rank // 2 ^ step, 0, keepdims=False)
-            parts.append(swap(part, 2 * step) if step else part)
-        return parts
+    def cross(values, places):
+        return {
+            (number, step): swap(
+                lax.dynamic_index_in_dim(values[number], rank // 2 ^ step, 0, keepdims=False),
+                2 * step,
+            )
+            for number, step in places
+        }
+
+    places = [(number, step) for number in range(micro) for step in range(1, ranks // 2)]
+    cuts = [0, len(places) // 6, len(places) // 3, 2 * len(places) // 3, len(places)]
+    shares = [places[start:end] for start, end in zip(cuts, cuts[1:])]
 
     def total(parts):
         return sum(part.astype(f32) for part in parts)
 
     grad_inputs, branches, logit_grads, grad_projs = [], [], [], []
     gain_two_sum = gain_one_sum = qk_sum = 0.0
-    in_cut, mixtures, out_sent = lax.optimization_barrier(
-        (in_cut, [part[:2] for part in back], out_sent)
-    )
-    mixtures = [pair_sum(*part) for part in mixtures]
-    crossed = []
-    releases = [order[:1]] + [[]] * (micro - 2) + [order[1:-1]]
+    in_cut, out_sent, in_sent = lax.optimization_barrier((in_cut, out_sent, in_sent))
+    mixtures = [part[:2] for part in back]
+    releases = [order[1:-1]] + [[]] * (micro - 1)
     for step in range(micro):
         at = slice(step * rows, (step + 1) * rows)
         parts = after(returned[step], [one[1] for one in grad_inputs])
-        parts, in_sent, crossed = lax.optimization_barrier((parts, in_sent, crossed))
+        parts, in_sent = lax.optimization_barrier((parts, in_sent))
+        if step == micro - 1:
+            crossed = cross(after(mixtures, parts), shares[0])
         parts = exchange_back(parts)
+        if step == 0:
+            mixtures = [pair_sum(*part) for part in after(mixtures, in_cut)]
         parts, in_cut, mixtures = lax.optimization_barrier((parts, in_cut, mixtures))
         in_sent.update(send(in_cut, releases[step]))
+        if step == micro - 1:
+            parts, crossed = lax.optimization_barrier((parts, crossed))
+            last = in_cut[order[-1]]
+            ends = [-(-last.shape[0] * part // 64) * 16 for part in range(5)]
+            last = [last[start:end] for start, end in zip(ends, ends[1:])]
+            last_sent = [shift_rep(last[0], order[-1])]
         grad_hidden, grad_branch, grad_mixed, grad_logits, gain_two = hidden_backward(
             where[1:2], planes, parts, hidden[at], gates[at], cotangent[at], second_gain,
             router, gathered, experts,
@@ -910,20 +926,31 @@
         branches.append(grad_branch)
         logit_grads.append(grad_logits)
         gain_two_sum = gain_two_sum + gain_two
+        if step == micro - 1:
+            out_sum = dot(mixed, jnp.concatenate(branches, axis=0), ((0,), (0,))).astype(bf16)
+            out_sum = out_sum.reshape(planes, ranks, dense_rows, D).transpose(1, 0, 2, 3)
         grad_mixed = lax.all_to_all(grad_mixed, "ep", split_axis=1, concat_axis=0, tiled=True)
-        grad_mixed, mixtures = lax.optimization_barrier((grad_mixed, mixtures))
-        crossed.append(cross(mixtures[step]))
+        if step == micro - 1:
+            grad_mixed, mixtures, last_sent, last, out_sum = lax.optimization_barrier(
+                (grad_mixed, mixtures, last_sent, last, out_sum)
+            )
+            out_sum = lax.psum_scatter(out_sum, "ep", scatter_dimension=0)
+            crossed.update(cross(mixtures, shares[1]))
+            last_sent.append(shift_rep(last[1], order[-1]))
         grad_proj, grad_qk = attention_backward(
             step, proj, *tables, query, keys, values, lses, grad_mixed
         )
         qk_sum = qk_sum + grad_qk.reshape(-1)
-        if step == micro - 1:
-            last = in_cut[order[-1]]
-            half = last.shape[0] // 2
-            grad_proj, in_sent, last, grad_inputs = lax.optimization_barrier(
-                (grad_proj, in_sent, last, grad_inputs)
+        if step < micro - 1:
+            grad_proj, in_sent = lax.optimization_barrier((grad_proj, in_sent))
+        else:
+            grad_proj, grad_inputs, crossed, mixtures, last_sent, last = (
+                lax.optimization_barrier(
+                    (grad_proj, grad_inputs, crossed, mixtures, last_sent, last)
+                )
             )
-            last_sent = [shift_rep(last[:half], order[-1])]
+            crossed.update(cross(mixtures, shares[2]))
+            last_sent.append(shift_rep(last[2], order[-1]))
         grad_projs.append(grad_proj)
         grad_normed, gain_one = project_backward(step, grad_proj, stream, slab)
         gain_one_sum = gain_one_sum + gain_one
@@ -934,17 +961,6 @@
                 lax.psum_scatter(grad_normed, "ep", scatter_dimension=0, tiled=True),
             )
         )
-    branches = after(jnp.concatenate(branches, axis=0), grad_normed)
-    out_sum = dot(mixed, branches, ((0,), (0,))).astype(bf16)
-    out_sum = out_sum.reshape(planes, ranks // 2, 2, dense_rows, D)
-    out_sum = pair_sum(
-        *(
-            lax.dynamic_index_in_dim(out_sum, rank % 2 ^ other, 2, keepdims=False).transpose(
-                1, 0, 2, 3
-            )
-            for other in range(2)
-        )
-    )
 
     router_sum = dot(normed_two, jnp.concatenate(logit_grads, axis=0), ((0,), (0,)))
     qk_columns = qk_sum.shape[0] // dense_rows
@@ -966,8 +982,10 @@
     def joined(value):
         return value[..., :count].astype(f32) + value[..., count : 2 * count].astype(f32)
 
-    grad_projs, out_sum = lax.optimization_barrier((grad_projs, out_sum))
-    out_crossed = cross(out_sum)
+    grad_projs, last_sent, last, _ = lax.optimization_barrier(
+        (grad_projs, last_sent, last, grad_normed)
+    )
+    last_sent.append(shift_rep(last[3], order[-1]))
     packed = weight_gradient(
         where,
         planes,
@@ -975,16 +993,19 @@
         [jnp.stack(grad_projs, axis=1).reshape(ranks * mine, 3 * width)],
         halves(small),
     )
-    packed, last_sent, last = lax.optimization_barrier((packed, last_sent, last))
+    packed, crossed, mixtures, last_sent = lax.optimization_barrier(
+        (packed, crossed, mixtures, last_sent)
+    )
     packed_sent = [packed[0]] + [shift_rep(packed[step], step) for step in range(1, planes)]
+    crossed.update(cross(mixtures, shares[3]))
     normed_sums = [one[2] for one in grad_inputs]
-    packed_sent, normed_sums, last, crossed = lax.optimization_barrier(
-        (packed_sent, normed_sums, last, crossed)
-    )
-    last_sent = last_sent + [shift_rep(last[half:], order[-1])]
+    packed_sent, crossed = lax.optimization_barrier((packed_sent, crossed))
     mixture = []
-    for parts in crossed:
-        parts = total(parts)
+    for number in range(micro):
+        parts = total(
+            [lax.dynamic_index_in_dim(mixtures[number], rank // 2, 0, keepdims=False)]
+            + [crossed[number, step] for step in range(1, ranks // 2)]
+        )
         mixture.append(parts[0] + total(exchange_back(parts.astype(bf16))[1:]))
     output = (hidden + jnp.concatenate(mixture, axis=0)).astype(bf16)
     grad_tokens = []
@@ -1001,17 +1022,15 @@
     small = sum(joined(part[:, 3 * width :]) for part in packed_sent)
     packed = jnp.concatenate([main, halves(small)], axis=1).reshape(ranks, dense_rows, -1)
     packed = lax.all_to_all(packed, "ep", split_axis=0, concat_axis=0, tiled=True)
-    packed, last_sent = lax.optimization_barrier((packed, last_sent))
     main = packed[..., : 3 * width].astype(f32)
     small = jnp.sum(joined(packed[..., 3 * width :]), axis=0)
     grad_w_qkv = (
         main.reshape(ranks, dense_rows, 3, width).transpose(1, 2, 0, 3).reshape(dense_rows, 3 * D)
     )
     grad_w_out = sum_rep({0: out_cut[0], **out_sent})
-    grad_w_in = sum_rep({0: in_cut[0], **in_sent, order[-1]: jnp.concatenate(last_sent, axis=0)})
-    out_sum = total(out_crossed)
-    grad_w_o = lax.dynamic_index_in_dim(out_sum, plane, 0, keepdims=False)
-    out_sum = out_sum.astype(bf16)
+    in_sent[order[-1]] = jnp.concatenate(last_sent, axis=0)
+    grad_w_in = sum_rep({0: in_cut[0], **in_sent})
+    grad_w_o = lax.dynamic_index_in_dim(out_sum, plane, 0, keepdims=False).astype(f32)
     for step in range(1, planes):
         part = lax.dynamic_index_in_dim(out_sum, (plane + step) % planes, 0, keepdims=False)
         grad_w_o = grad_w_o + shift_rep(part, step).astype(f32)

time: 1110 us -> 1070 us (0.964)
  waiting for transfers between devices: 493 us -> 429 us
  starting transfers between devices: 108 us -> 129 us
  other arithmetic: 74.4 us -> 61.9 us
    ppermute x25 -> x27, waiting for transfers between devices: 292 us -> 263 us  [shift_rep(): lax.ppermute(value, 'rep', [(i, (i + step) % count) for i in range(count)])]
    ppermute x12 -> x8, waiting for transfers between devices: 93.8 us -> 69.4 us  [swap(): return lax.ppermute(value, 'ep', [(i, i ^ step) for i in range(ranks)])]
    ppermute x25 -> x27, starting transfers between devices: 73.1 us -> 84.4 us  [shift_rep(): lax.ppermute(value, 'rep', [(i, (i + step) % count) for i in range(count)])]
    pallas_call x3 -> x4, Pallas kernels: 57.1 us -> 62.8 us  [weight_gradient(): pl.pallas_call(kernel, grid_spec=pltpu.PrefetchScalarGridSpec(num_scalar_...]
  transfers between devices with their start and end apart: 55 -> 54, of which waited for: 25 -> 27; matrix products, arithmetic and copies ran while one was open for 10% -> 13% of each run, Pallas kernels for 27% -> 28%
where the time goes in v7:
time: 1070 us; the launch traced here: 1060 us
  waiting for transfers between devices  429 us (40%)
  Pallas kernels  314 us (29%)
  starting transfers between devices  129 us (12%)
  local copies, waits for them, and re-layouts  89.9 us (8%)
  other arithmetic  61.9 us (6%)
  between operations  15.3 us (1%)
  blocking collectives  12.8 us (1%)
    ppermute x27, waiting for transfers between devices, shift_rep(): lax.ppermute(value, 'rep', [(i, (i + step) % count) for i in range(count)])  263 us
    ppermute x27, starting transfers between devices, shift_rep(): lax.ppermute(value, 'rep', [(i, (i + step) % count) for i in range(count)])  84.4 us
    pallas_call x2, Pallas kernels, expert_backward(): pl.pallas_call(kernel, grid_spec=pltpu.PrefetchScalarGridSpec(num_scalar_...  84.3 us
    ppermute x6, waiting for transfers between devices, exchange(): return lax.ppermute(value, 'rep', pairs)  70.4 us
    ppermute x8, waiting for transfers between devices, swap(): return lax.ppermute(value, 'ep', [(i, i ^ step) for i in range(ranks)])  69.4 us
    pallas_call x4, Pallas kernels, weight_gradient(): pl.pallas_call(kernel, grid_spec=pltpu.PrefetchScalarGridSpec(num_scalar_...  62.8 us
    pallas_call x1, Pallas kernels, expert_forward(): pl.pallas_call(kernel, grid_spec=pltpu.PrefetchScalarGridSpec(num_scalar_...  40.3 us
    pallas_call x2, Pallas kernels, attention_backward(): pl.pallas_call(lambda *refs: backward_kernel(heads, *refs), grid=(1,), in...  33.7 us
  transfers between devices with their start and end apart: 54, of which 27 were waited for; matrix products, arithmetic and copies ran while one was open for 13% of the time, Pallas kernels for 28%

profile of v7, /device:TPU:0, one launch (start us, length us, event | category | flops | bytes accessed | tf_op | source)
XLA Modules:
  0.0 1059.1 jit_solution(16785045997065913508)
XLA Ops:
  25.9 20.6 %collective-permute-done.3 = bf16[256,2048]{1,0:T(8,128)(2,1)S(1)} collective-permute-done((bf16[256,2048]{1,0:T(8,128)(2,1)}, bf16[256,2048]{1,0:T(8,128)(2,1)S(1)}, u32[]{:S(2)}, u32[]{:S(2)}) %collective-permute-start.3) | collective-permute-done | bytes 1048608 | tf_op jit(solution)/shard_map/ppermute | solution.py:742
  67.5 16.1 %collective-permute-done.4 = bf16[512,896]{1,0:T(8,128)(2,1)S(1)} collective-permute-done((bf16[512,896]{1,0:T(8,128)(2,1)S(1)}, bf16[512,896]{1,0:T(8,128)(2,1)S(1)}, u32[]{:S(2)}, u32[]{:S(2)}) %collective-permute-start.4) | collective-permute-done | bytes 917536 | tf_op jit(solution)/shard_map/ppermute | solution.py:690
  83.6 22.4 %collective-permute-done.5 = bf16[512,896]{1,0:T(8,128)(2,1)S(1)} collective-permute-done((bf16[512,896]{1,0:T(8,128)(2,1)S(1)}, bf16[512,896]{1,0:T(8,128)(2,1)S(1)}, u32[]{:S(2)}, u32[]{:S(2)}) %collective-permute-start.5) | collective-permute-done | bytes 917536 | tf_op jit(solution)/shard_map/ppermute | solution.py:690
  111.2 16.4 %collective-permute-done.6 = bf16[512,896]{1,0:T(8,128)(2,1)} collective-permute-done((bf16[512,896]{1,0:T(8,128)(2,1)S(1)}, bf16[512,896]{1,0:T(8,128)(2,1)}, u32[]{:S(2)}, u32[]{:S(2)}) %collective-permute-start.6) | collective-permute-done | bytes 917536 | tf_op jit(solution)/shard_map/ppermute | solution.py:690
  136.7 15.0 %shard_map.178 = (bf16[8,256,2048]{2,1,0:T(8,128)(2,1)}, f32[8,256,768]{2,1,0:T(8,128)}) custom-call(bf16[8,256,2048]{2,1,0:T(8,128)(2,1)} %bitcast.187, f32[1,2048]{1,0:T(1,128)S(1)} %broadcast_in_dim.63.gain, bf16[2048,896]{1,0:T(8,128)(2,1)} %constant_dynamic-update-slice_fusion.weight), custom_call_target="tpu_custom_call" | custom-call | tf_op jit(solution)/shard_map/pallas_call | solution.py:247
  151.7 21.8 %shard_map.179 = (bf16[8,2,128,256]{3,2,1,0:T(8,128)(2,1)}, bf16[2,1024,256]{2,1,0:T(8,128)(2,1)S(1)}, bf16[2,1024,256]{2,1,0:T(8,128)(2,1)S(1)}, bf16[2,1024,256]{2,1,0:T(8,128)(2,1)}, f32[2,2,1024,1]{3,2,1,0:T(8,128)}) custom-call(f32[8,2,128,768]{3,2,1,0:T(8,128)} %bitcast.190, f32[2,1024,128]{2,1,0:T(8,128)} %get-tuple-element.203.refs_1_, ...), custom_call_target="tpu_custom_call" | custom-call | tf_op jit(solution)/shard_map/pallas_call | solution.py:198
  181.2 24.9 %all-to-all-done.1 = bf16[8,2,128,256]{3,2,1,0:T(8,128)(2,1)S(1)} async-done(((bf16[8,2,128,256]{3,2,1,0:T(8,128)(2,1)}), bf16[8,2,128,256]{3,2,1,0:T(8,128)(2,1)S(1)}, u32[]{:S(2)}, u32[]{:S(2)}) %all-to-all-start.1) | async-done | bytes 1048608 | tf_op jit(solution)/shard_map/all_to_all | solution.py:806
  219.3 24.6 %collective-permute-done.9 = bf16[256,2176]{1,0:T(8,128)(2,1)S(1)} collective-permute-done((bf16[256,2176]{1,0:T(8,128)(2,1)S(1)}, bf16[256,2176]{1,0:T(8,128)(2,1)S(1)}, u32[]{:S(2)}, u32[]{:S(2)}) %collective-permute-start.9) | collective-permute-done | bytes 1114144 | tf_op jit(solution)/shard_map/ppermute | solution.py:742
  247.2 89.4 %collective-permute-done.10.refs_2_ = bf16[512,2048]{1,0:T(8,128)(2,1)} collective-permute-done((bf16[512,2048]{1,0:T(8,128)(2,1)}, bf16[512,2048]{1,0:T(8,128)(2,1)}, u32[]{:S(2)}, u32[]{:S(2)}) %collective-permute-start.10) | collective-permute-done | bytes 2097184 | tf_op jit(solution)/shard_map/ppermute | solution.py:690
  340.4 40.3 %shard_map.181 = (bf16[2,4,288,2048]{3,2,1,0:T(8,128)(2,1)}, f32[2,4,288,128]{3,2,1,0:T(8,128)S(1)}, f32[2,4,288,2048]{3,2,1,0:T(8,128)}, bf16[2,4,288,1024]{3,2...) custom-call(s32[3]{0:T(128)S(1)} %pad_add_fusion.where, ...), custom_call_target="tpu_custom_call" | custom-call | flops 241591910400 | tf_op jit(solution)/shard_map/pallas_call | solution.py:429
  380.8 16.8 %shard_map.182 = bf16[4,256,2048]{2,1,0:T(8,128)(2,1)} custom-call(s32[3]{0:T(128)S(1)} %pad_add_fusion.where, bf16[2304,1024]{1,0:T(8,128)(2,1)} %bitcast.225, bf16[2304,2048]{1,0:T(8,128)(2,1)} %bitcast.224), custom_call_target="tpu_custom_call" | custom-call | flops 96636764160 | tf_op jit(solution)/shard_map/pallas_call | solution.py:584
  409.7 40.4 %shard_map.183 = (bf16[4,2,128,2048]{3,2,1,0:T(8,128)(2,1)}, bf16[4,2,128,2048]{3,2,1,0:T(8,128)(2,1)}, bf16[8,2,128,2176]{3,2,1,0:T(8,128)(2,1)}, bf16[4,288,2048]{2,1,0:T(8,128)(2,1)}) custom-call(s32[3]{0:T(128)S(1)} %pad_add_fusion.where, f32[2,4,288,128]{3,2,1,0:T(8,128)} %copy-done.30, f32[2,4,288,2048]{3,2,1,0:T(8,128)} %get-tuple-element.247.both, ...), custom_call_target="tpu_custom_call" | custom-call | flops 217432719360 | tf_op jit(solution)/shard_map/pallas_call | solution.py:527
  450.2 42.7 %collective-permute-start.15 = (bf16[256,2048]{1,0:T(8,128)(2,1)}, bf16[256,2048]{1,0:T(8,128)(2,1)}, u32[]{:S(2)}, u32[]{:S(2)}) collective-permute-start(bf16[256,2048]{1,0:T(8,128)(2,1)} %get-tuple-element.414), channel_id=1, source_target_pairs={{0,16},{8,24},{16,0},{24,8},{1,17},{9,25},{17,1},{25,9},{2,18},{10... | collective-permute-start | bytes 3145736 | tf_op jit(solution)/shard_map/ppermute | solution.py:690
  496.4 43.9 %shard_map.184 = (bf16[4,2,128,2048]{3,2,1,0:T(8,128)(2,1)}, bf16[4,2,128,2048]{3,2,1,0:T(8,128)(2,1)}, bf16[8,2,128,2176]{3,2,1,0:T(8,128)(2,1)}, bf16[4,288,2048]{2,1,0:T(8,128)(2,1)}) custom-call(s32[3]{0:T(128)S(1)} %pad_add_fusion.where, f32[2,4,288,128]{3,2,1,0:T(8,128)} %copy-done.30, f32[2,4,288,2048]{3,2,1,0:T(8,128)} %get-tuple-element.247.both, ...), custom_call_target="tpu_custom_call" | custom-call | flops 217432719360 | tf_op jit(solution)/shard_map/pallas_call | solution.py:527
  552.6 23.3 %shard_map.186 = bf16[3,512,2048]{2,1,0:T(8,128)(2,1)} custom-call(s32[3]{0:T(128)S(1)} %pad_add_fusion.where, bf16[2304,2048]{1,0:T(8,128)(2,1)} %bitcast.223, bf16[1152,2048]{1,0:T(8,128)(2,1)} %bitcast.227, bf16[1152,2048]{1,0:T(8,128)(2,1)} %bitcast.229), custom_call_target="tpu_custom_call" | custom-call | flops 144955146240 | tf_op jit(solution)/shard_map/pallas_call | solution.py:584
  583.9 17.2 %collective-permute-done.17 = bf16[512,2048]{1,0:T(8,128)(2,1)} collective-permute-done((bf16[512,2048]{1,0:T(8,128)(2,1)}, bf16[512,2048]{1,0:T(8,128)(2,1)}, u32[]{:S(2)}, u32[]{:S(2)}) %collective-permute-start.17) | collective-permute-done | bytes 2097184 | tf_op jit(solution)/shard_map/ppermute | solution.py:690
  667.2 16.7 %shard_map.188 = (bf16[8,128,768]{2,1,0:T(8,128)(2,1)}, f32[2,128]{1,0:T(2,128)S(1)}) custom-call(f32[8,2,128,768]{3,2,1,0:T(8,128)} %bitcast.191, f32[2,1024,128]{2,1,0:T(8,128)S(1)} %copy-done.2, f32[2,1024,128]{2,1,0:T(8,128)S(1)} %copy-done.1, s32[2,1024,1]{2,1,0:T(8,128)S(1)} %copy-done.3, s32[2,1,1024]{2,1,0:T(1,128)S(1)} %copy-done.24, ...), custom_call_target="tpu_custom_call" | custom-call | tf_op jit(solution)/shard_map/pallas_call | solution.py:220
  688.7 14.0 %shard_map.189 = (bf16[1024,2048]{1,0:T(8,128)(2,1)}, f32[1,2048]{1,0:T(1,128)S(1)}) custom-call(bf16[8,128,768]{2,1,0:T(8,128)(2,1)S(1)} %copy-done.8, bf16[8,256,2048]{2,1,0:T(8,128)(2,1)} %bitcast.188, bf16[2048,896]{1,0:T(8,128)(2,1)} %constant_dynamic-update-slice_fusion.weight), custom_call_target="tpu_custom_call" | custom-call | tf_op jit(solution)/shard_map/pallas_call | solution.py:674
  723.4 14.4 %collective-permute-done.23 = bf16[2,128,2048]{2,1,0:T(8,128)(2,1)} collective-permute-done((bf16[2,128,2048]{2,1,0:T(8,128)(2,1)}, bf16[2,128,2048]{2,1,0:T(8,128)(2,1)}, u32[]{:S(2)}, u32[]{:S(2)}) %collective-permute-start.23) | collective-permute-done | bytes 1048608 | tf_op jit(solution)/shard_map/ppermute | solution.py:879
  782.5 17.0 %shard_map.191 = (bf16[8,128,768]{2,1,0:T(8,128)(2,1)}, f32[2,128]{1,0:T(2,128)S(1)}) custom-call(f32[8,2,128,768]{3,2,1,0:T(8,128)} %bitcast.192, f32[2,1024,128]{2,1,0:T(8,128)S(1)} %copy-done.2, f32[2,1024,128]{2,1,0:T(8,128)S(1)} %copy-done.1, s32[2,1024,1]{2,1,0:T(8,128)S(1)} %copy-done.4, s32[2,1,1024]{2,1,0:T(1,128)S(1)} %copy-done.24, ...), custom_call_target="tpu_custom_call" | custom-call | tf_op jit(solution)/shard_map/pallas_call | solution.py:220
  805.4 14.0 %shard_map.192 = (bf16[1024,2048]{1,0:T(8,128)(2,1)}, f32[1,2048]{1,0:T(1,128)S(1)}) custom-call(bf16[8,128,768]{2,1,0:T(8,128)(2,1)S(1)} %copy-done.10, bf16[8,256,2048]{2,1,0:T(8,128)(2,1)} %bitcast.189, bf16[2048,896]{1,0:T(8,128)(2,1)} %constant_dynamic-update-slice_fusion.weight), custom_call_target="tpu_custom_call" | custom-call | tf_op jit(solution)/shard_map/pallas_call | solution.py:674
  869.3 26.3 %collective-permute-done.29 = bf16[2,128,2048]{2,1,0:T(8,128)(2,1)} collective-permute-done((bf16[2,128,2048]{2,1,0:T(8,128)(2,1)}, bf16[2,128,2048]{2,1,0:T(8,128)(2,1)}, u32[]{:S(2)}, u32[]{:S(2)}) %collective-permute-start.29) | collective-permute-done | bytes 1048608 | tf_op jit(solution)/shard_map/ppermute | solution.py:879
  925.4 35.9 %collective-permute-done.32 = bf16[512,896]{1,0:T(8,128)(2,1)S(1)} collective-permute-done((bf16[512,896]{1,0:T(8,128)(2,1)}, bf16[512,896]{1,0:T(8,128)(2,1)S(1)}, u32[]{:S(2)}, u32[]{:S(2)}) %collective-permute-start.32) | collective-permute-done | bytes 917536 | tf_op jit(solution)/shard_map/ppermute | solution.py:690
  1033.4 16.8 %collective-permute-done.39 = bf16[64,2048]{1,0:T(8,128)(2,1)S(1)} collective-permute-done((bf16[64,2048]{1,0:T(8,128)(2,1)S(1)}, bf16[64,2048]{1,0:T(8,128)(2,1)S(1)}, u32[]{:S(2)}, u32[]{:S(2)}) %collective-permute-start.39) | collective-permute-done | bytes 262176 | tf_op jit(solution)/shard_map/ppermute | solution.py:690
  (335 shorter events, 412.8 us)
Async XLA Ops:
  7.2 122.6 %all-gather.9.cloned.1.call-start = ((), (), s32[]{:S(2)}) async-start(), calls=%async_computation.15 | async-start | bytes 9437184 | tf_op jit(solution)/shard_map/all_gather | solution.py:748
  20.2 186.8 %all-gather.11.cloned.1.call-start = ((), (), s32[]{:S(2)}) async-start(), calls=%async_computation.16 | async-start | bytes 9437184 | tf_op jit(solution)/shard_map/all_gather | solution.py:748
  53.6 286.8 %all-gather.15.cloned.1.call-start = ((), (), s32[]{:S(2)}) async-start(), calls=%async_computation.18 | async-start | bytes 18874368 | tf_op jit(solution)/shard_map/all_gather | solution.py:748
  129.8 86.3 %collective-permute-start.7 = (bf16[512,2048]{1,0:T(8,128)(2,1)}, bf16[512,2048]{1,0:T(8,128)(2,1)}, u32[]{:S(2)}, u32[]{:S(2)}) collective-permute-start(bf16[512,2048]{1,0:T(8,128)(2,1)} %get-tuple-element.221), channel_id=1, source_target_pairs={{0,8},{8,16},{16,24},{24,0},{1,9},{9,17},{17,25},{25,1},{2,10},{10... | collective-permute-start | bytes 6291464 | tf_op jit(solution)/shard_map/ppermute | solution.py:690
  129.9 89.4 %collective-permute-start.8 = (bf16[512,2048]{1,0:T(8,128)(2,1)}, bf16[512,2048]{1,0:T(8,128)(2,1)}, u32[]{:S(2)}, u32[]{:S(2)}) collective-permute-start(bf16[512,2048]{1,0:T(8,128)(2,1)} %get-tuple-element.222), channel_id=1, source_target_pairs={{0,24},{8,0},{16,8},{24,16},{1,25},{9,1},{17,9},{25,17},{2,26},{10... | collective-permute-start | bytes 6291464 | tf_op jit(solution)/shard_map/ppermute | solution.py:690
  179.3 161.1 %all-gather.13.cloned.1.call-start = ((), (), s32[]{:S(2)}) async-start(), calls=%async_computation.17 | async-start | bytes 20054016 | tf_op jit(solution)/shard_map/all_gather | solution.py:748
  245.5 372.8 %reduce-scatter.6.cloned.1.call-start = ((), (), s32[]{:S(2)}) async-start(), calls=%async_computation.10 | async-start | bytes 10027008 | tf_op jit(solution)/shard_map/reduce_scatter | solution.py:849
  245.6 91.0 %collective-permute-start.10 = (bf16[512,2048]{1,0:T(8,128)(2,1)}, bf16[512,2048]{1,0:T(8,128)(2,1)}, u32[]{:S(2)}, u32[]{:S(2)}) collective-permute-start(bf16[512,2048]{1,0:T(8,128)(2,1)} %get-tuple-element.233), channel_id=1, source_target_pairs={{0,16},{8,24},{16,0},{24,8},{1,17},{9,25},{17,1},{25,9},{2,18},{10... | collective-permute-start | bytes 6291464 | tf_op jit(solution)/shard_map/ppermute | solution.py:690
  336.6 65.3 %collective-permute-start.11 = (bf16[256,2048]{1,0:T(8,128)(2,1)}, bf16[256,2048]{1,0:T(8,128)(2,1)}, u32[]{:S(2)}, u32[]{:S(2)}) collective-permute-start(bf16[256,2048]{1,0:T(8,128)(2,1)} %get-tuple-element.251), channel_id=1, source_target_pairs={{0,8},{8,16},{16,24},{24,0},{1,9},{9,17},{17,25},{25,1},{2,10},{10... | collective-permute-start | bytes 3145736 | tf_op jit(solution)/shard_map/ppermute | solution.py:690
  336.6 73.1 %collective-permute-start.12 = (bf16[256,2048]{1,0:T(8,128)(2,1)}, bf16[256,2048]{1,0:T(8,128)(2,1)}, u32[]{:S(2)}, u32[]{:S(2)}) collective-permute-start(bf16[256,2048]{1,0:T(8,128)(2,1)} %get-tuple-element.252), channel_id=1, source_target_pairs={{0,16},{8,24},{16,0},{24,8},{1,17},{9,25},{17,1},{25,9},{2,18},{10... | collective-permute-start | bytes 3145736 | tf_op jit(solution)/shard_map/ppermute | solution.py:690
  337.4 72.3 %collective-permute-start.13 = (bf16[256,2048]{1,0:T(8,128)(2,1)}, bf16[256,2048]{1,0:T(8,128)(2,1)}, u32[]{:S(2)}, u32[]{:S(2)}) collective-permute-start(bf16[256,2048]{1,0:T(8,128)(2,1)} %get-tuple-element.253), channel_id=1, source_target_pairs={{0,24},{8,0},{16,8},{24,16},{1,25},{9,1},{17,9},{25,17},{2,26},{10... | collective-permute-start | bytes 3145736 | tf_op jit(solution)/shard_map/ppermute | solution.py:690
  401.3 95.1 %collective-permute-start.14 = (bf16[256,2048]{1,0:T(8,128)(2,1)}, bf16[256,2048]{1,0:T(8,128)(2,1)}, u32[]{:S(2)}, u32[]{:S(2)}) collective-permute-start(bf16[256,2048]{1,0:T(8,128)(2,1)} %get-tuple-element.415), channel_id=1, source_target_pairs={{0,8},{8,16},{16,24},{24,0},{1,9},{9,17},{17,25},{25,1},{2,10},{10... | collective-permute-start | bytes 3145736 | tf_op jit(solution)/shard_map/ppermute | solution.py:690
  450.2 252.6 %reduce-scatter.8.cloned.1.call-start = ((), (), s32[]{:S(2)}) async-start(), calls=%async_computation.11 | async-start | bytes 10027008 | tf_op jit(solution)/shard_map/reduce_scatter | solution.py:849
  450.2 133.7 %collective-permute-start.15 = (bf16[256,2048]{1,0:T(8,128)(2,1)}, bf16[256,2048]{1,0:T(8,128)(2,1)}, u32[]{:S(2)}, u32[]{:S(2)}) collective-permute-start(bf16[256,2048]{1,0:T(8,128)(2,1)} %get-tuple-element.414), channel_id=1, source_target_pairs={{0,16},{8,24},{16,0},{24,8},{1,17},{9,25},{17,1},{25,9},{2,18},{10... | collective-permute-start | bytes 3145736 | tf_op jit(solution)/shard_map/ppermute | solution.py:690
  492.9 91.0 %collective-permute-start.16 = (bf16[256,2048]{1,0:T(8,128)(2,1)}, bf16[256,2048]{1,0:T(8,128)(2,1)}, u32[]{:S(2)}, u32[]{:S(2)}) collective-permute-start(bf16[256,2048]{1,0:T(8,128)(2,1)} %get-tuple-element.413), channel_id=1, source_target_pairs={{0,24},{8,0},{16,8},{24,16},{1,25},{9,1},{17,9},{25,17},{2,26},{10... | collective-permute-start | bytes 3145736 | tf_op jit(solution)/shard_map/ppermute | solution.py:690
  552.4 251.6 %reduce-scatter.10.cloned.1.call-start = ((), (), s32[]{:S(2)}) async-start(), calls=%async_computation.12 | async-start | bytes 4718592 | tf_op jit(solution)/shard_map/reduce_scatter | solution.py:961
  720.3 53.0 %collective-permute-start.24 = (bf16[128,2048]{1,0:T(8,128)(2,1)}, bf16[128,2048]{1,0:T(8,128)(2,1)}, u32[]{:S(2)}, u32[]{:S(2)}) collective-permute-start(bf16[128,2048]{1,0:T(8,128)(2,1)} %get-tuple-element.429), channel_id=1, source_target_pairs={{0,16},{8,24},{16,0},{24,8},{1,17},{9,25},{17,1},{25,9},{2,18},{10... | collective-permute-start | bytes 1572872 | tf_op jit(solution)/shard_map/ppermute | solution.py:690
  757.5 263.2 %reduce-scatter.12.cloned.1.call-start = ((), (), s32[]{:S(2)}) async-start(), calls=%async_computation.13 | async-start | bytes 4718592 | tf_op jit(solution)/shard_map/reduce_scatter | solution.py:961
  819.5 205.2 %reduce-scatter.14.cloned.1.call-start = ((), (), s32[]{:S(2)}) async-start(), calls=%async_computation.14 | async-start | bytes 9437184 | tf_op jit(solution)/shard_map/reduce_scatter | solution.py:937
  835.6 60.0 %collective-permute-start.29 = (bf16[2,128,2048]{2,1,0:T(8,128)(2,1)}, bf16[2,128,2048]{2,1,0:T(8,128)(2,1)}, u32[]{:S(2)}, u32[]{:S(2)}) collective-permute-start(bf16[2,128,2048]{2,1,0:T(8,128)(2,1)} %dynamic-slice_bitcast_fusion.6), channel_id=1, source_target_pairs={{0,2},{1,3},{2,0},{3,1},{4,6},{5,7},{6,4},{7,5},{8,10},{9,11},{10,... | collective-permute-start | bytes 3145736 | tf_op jit(solution)/shard_map/ppermute | solution.py:879
  900.1 61.2 %collective-permute-start.32 = (bf16[512,896]{1,0:T(8,128)(2,1)}, bf16[512,896]{1,0:T(8,128)(2,1)S(1)}, u32[]{:S(2)}, u32[]{:S(2)}) collective-permute-start(bf16[512,896]{1,0:T(8,128)(2,1)} %get-tuple-element.421), channel_id=1, source_target_pairs={{0,16},{8,24},{16,0},{24,8},{1,17},{9,25},{17,1},{25,9},{2,18},{10... | collective-permute-start | bytes 2752520 | tf_op jit(solution)/shard_map/ppermute | solution.py:690
  900.1 61.2 %collective-permute-start.33 = (bf16[512,896]{1,0:T(8,128)(2,1)}, bf16[512,896]{1,0:T(8,128)(2,1)S(1)}, u32[]{:S(2)}, u32[]{:S(2)}) collective-permute-start(bf16[512,896]{1,0:T(8,128)(2,1)} %get-tuple-element.420), channel_id=1, source_target_pairs={{0,24},{8,0},{16,8},{24,16},{1,25},{9,1},{17,9},{25,17},{2,26},{10... | collective-permute-start | bytes 2752520 | tf_op jit(solution)/shard_map/ppermute | solution.py:690
  904.2 66.9 %collective-permute-start.34 = (bf16[2,128,2048]{2,1,0:T(8,128)(2,1)S(1)}, bf16[2,128,2048]{2,1,0:T(8,128)(2,1)S(1)}, u32[]{:S(2)}, u32[]{:S(2)}) collective-permute-start(bf16[2,128,2048]{2,1,0:T(8,128)(2,1)S(1)} %get-tuple-element.412), channel_id=1, source_target_pairs={{0,4},{1,5},{2,6},{3,7},{4,0},{5,1},{6,2},{7,3},{8,12},{9,13},{10,... | collective-permute-start | bytes 3145736 | tf_op jit(solution)/shard_map/ppermute | solution.py:879
  904.3 66.8 %collective-permute-start.35 = (bf16[2,128,2048]{2,1,0:T(8,128)(2,1)S(1)}, bf16[2,128,2048]{2,1,0:T(8,128)(2,1)S(1)}, u32[]{:S(2)}, u32[]{:S(2)}) collective-permute-start(bf16[2,128,2048]{2,1,0:T(8,128)(2,1)S(1)} %get-tuple-element.411), channel_id=1, source_target_pairs={{0,6},{1,7},{2,4},{3,5},{4,2},{5,3},{6,0},{7,1},{8,14},{9,15},{10,... | collective-permute-start | bytes 3145736 | tf_op jit(solution)/shard_map/ppermute | solution.py:879
  (87 other events, 2494.7 us)
Sparse Core Ops, SparseCore 0:
  9.9 65.9 all-gather.8
  77.8 54.3 all-gather.10
  134.1 101.0 all-gather.14
  245.6 92.4 all-gather.12
  450.3 114.1 reduce-scatter.5
  567.9 73.7 reduce-scatter.7
  702.9 56.3 reduce-scatter.9
  819.6 68.1 reduce-scatter.11
  891.3 99.7 reduce-scatter.13

commit v8 on v7

--- a/solution.py
+++ b/solution.py
@@ -571,15 +571,20 @@
         return (where[1] + first + i) % planes
 
     def kernel(where, left, *refs):
-        rights, target = refs[:parts], refs[-1]
-        for value in refs[parts:-1]:
-            target[0, :, columns:] = value[...]
-        for number in range(columns // step):
-            at = slice(number * step, (number + 1) * step)
-            target[0, :, at] = sum(
-                dot(left[part * part_rows : (part + 1) * part_rows], right[:, at], ((0,), (0,)))
-                for part, right in enumerate(rights)
-            ).astype(bf16)
+        rights, tails, targets = refs[:parts], refs[parts:-steps], refs[-steps:]
+
+        def fill(target):
+            for value in tails:
+                target[:, columns:] = value[...]
+            for number in range(columns // step):
+                at = slice(number * step, (number + 1) * step)
+                target[:, at] = sum(
+                    dot(left[part * part_rows : (part + 1) * part_rows], right[:, at], ((0,), (0,)))
+                    for part, right in enumerate(rights)
+                ).astype(bf16)
+
+        for number, target in enumerate(targets):
+            pl.when(pl.program_id(0) == number)(lambda target=target: fill(target))
 
     return pl.pallas_call(
         kernel,
@@ -592,9 +597,9 @@
                 pl.BlockSpec((width, value.shape[1]), lambda i, where: (of_plane(i, where), 0))
                 for value in tails
             ],
-            out_specs=pl.BlockSpec((1, width, whole), lambda i, _: (i, 0, 0)),
+            out_specs=[fixed((width, whole))] * steps,
         ),
-        out_shape=out((steps, width, whole)),
+        out_shape=[out((width, whole))] * steps,
         cost_estimate=cost(0 if tails else count * steps * width * columns),
         compiler_params=params(),
     )(where, left, *rights, *tails)
@@ -840,7 +845,7 @@
             ]
         )
 
-    tail, out_cut = lax.optimization_barrier((tail, out_cut))
+    tail, out_cut, out_pieces = lax.optimization_barrier((tail, out_cut, out_pieces))
     out_sent = send(out_cut, order)
     back = []
     returned = []
@@ -871,8 +876,8 @@
     far = weight_gradient(
         where, planes, rows_flat, grads_flat, first=order[0] + 1, steps=planes - 1
     )
-    in_cut = {(order[0] + 1 + i) % planes: far[i] for i in range(planes - 1)}
-    in_cut[order[0]] = near[0]
+    in_cut = {(order[0] + 1 + i) % planes: part for i, part in enumerate(far)}
+    in_cut[order[0]], = near
     in_sent = send(in_cut, order[:1])
 
     def swap(value, step):
@@ -881,18 +886,24 @@
     def pair_sum(keep, give):
         return (keep.astype(f32) + swap(give, 1).astype(f32)).astype(bf16)
 
-    def cross(values, places):
-        return {
-            (number, step): swap(
-                lax.dynamic_index_in_dim(values[number], rank // 2 ^ step, 0, keepdims=False),
-                2 * step,
+    bits = list(range((ranks // 2).bit_length() - 1))
+
+    def halve(values, phase):
+        results = []
+        for number, value in enumerate(values):
+            way = bits if number % 2 == 0 else bits[::-1]
+            bit = way[phase]
+            low = 2 ** sum(other < bit for other in way[phase:])
+            value = value.reshape((-1, 2, low) + value.shape[1:])
+            side = rank // 2 // 2**bit % 2
+            keep, give = (
+                lax.dynamic_index_in_dim(value, which, 1, keepdims=False).reshape(
+                    (-1,) + value.shape[3:]
+                )
+                for which in (side, 1 - side)
             )
-            for number, step in places
-        }
-
-    places = [(number, step) for number in range(micro) for step in range(1, ranks // 2)]
-    cuts = [0, len(places) // 6, len(places) // 3, 2 * len(places) // 3, len(places)]
-    shares = [places[start:end] for start, end in zip(cuts, cuts[1:])]
+            results.append((keep, swap(give, 2 * 2**bit)))
+        return results
 
     def total(parts):
         return sum(part.astype(f32) for part in parts)
@@ -906,15 +917,12 @@
         at = slice(step * rows, (step + 1) * rows)
         parts = after(returned[step], [one[1] for one in grad_inputs])
         parts, in_sent = lax.optimization_barrier((parts, in_sent))
-        if step == micro - 1:
-            crossed = cross(after(mixtures, parts), shares[0])
         parts = exchange_back(parts)
+        parts, in_cut, mixtures = lax.optimization_barrier((parts, in_cut, mixtures))
         if step == 0:
-            mixtures = [pair_sum(*part) for part in after(mixtures, in_cut)]
-        parts, in_cut, mixtures = lax.optimization_barrier((parts, in_cut, mixtures))
+            mixtures = [pair_sum(*part) for part in mixtures]
         in_sent.update(send(in_cut, releases[step]))
         if step == micro - 1:
-            parts, crossed = lax.optimization_barrier((parts, crossed))
             last = in_cut[order[-1]]
             ends = [-(-last.shape[0] * part // 64) * 16 for part in range(5)]
             last = [last[start:end] for start, end in zip(ends, ends[1:])]
@@ -930,12 +938,12 @@
             out_sum = dot(mixed, jnp.concatenate(branches, axis=0), ((0,), (0,))).astype(bf16)
             out_sum = out_sum.reshape(planes, ranks, dense_rows, D).transpose(1, 0, 2, 3)
         grad_mixed = lax.all_to_all(grad_mixed, "ep", split_axis=1, concat_axis=0, tiled=True)
+        grad_mixed, mixtures = lax.optimization_barrier((grad_mixed, mixtures))
         if step == micro - 1:
             grad_mixed, mixtures, last_sent, last, out_sum = lax.optimization_barrier(
                 (grad_mixed, mixtures, last_sent, last, out_sum)
             )
             out_sum = lax.psum_scatter(out_sum, "ep", scatter_dimension=0)
-            crossed.update(cross(mixtures, shares[1]))
             last_sent.append(shift_rep(last[1], order[-1]))
         grad_proj, grad_qk = attention_backward(
             step, proj, *tables, query, keys, values, lses, grad_mixed
@@ -944,12 +952,9 @@
         if step < micro - 1:
             grad_proj, in_sent = lax.optimization_barrier((grad_proj, in_sent))
         else:
-            grad_proj, grad_inputs, crossed, mixtures, last_sent, last = (
-                lax.optimization_barrier(
-                    (grad_proj, grad_inputs, crossed, mixtures, last_sent, last)
-                )
+            grad_proj, grad_inputs, last_sent, last = lax.optimization_barrier(
+                (grad_proj, grad_inputs, last_sent, last)
             )
-            crossed.update(cross(mixtures, shares[2]))
             last_sent.append(shift_rep(last[2], order[-1]))
         grad_projs.append(grad_proj)
         grad_normed, gain_one = project_backward(step, grad_proj, stream, slab)
@@ -982,8 +987,8 @@
     def joined(value):
         return value[..., :count].astype(f32) + value[..., count : 2 * count].astype(f32)
 
-    grad_projs, last_sent, last, _ = lax.optimization_barrier(
-        (grad_projs, last_sent, last, grad_normed)
+    grad_projs, last_sent, last, out_cut, out_sent, _ = lax.optimization_barrier(
+        (grad_projs, last_sent, last, out_cut, out_sent, grad_normed)
     )
     last_sent.append(shift_rep(last[3], order[-1]))
     packed = weight_gradient(
@@ -993,19 +998,19 @@
         [jnp.stack(grad_projs, axis=1).reshape(ranks * mine, 3 * width)],
         halves(small),
     )
-    packed, crossed, mixtures, last_sent = lax.optimization_barrier(
-        (packed, crossed, mixtures, last_sent)
+    packed, last_sent, out_cut, out_sent, mixtures = lax.optimization_barrier(
+        (packed, last_sent, out_cut, out_sent, mixtures)
     )
     packed_sent = [packed[0]] + [shift_rep(packed[step], step) for step in range(1, planes)]
-    crossed.update(cross(mixtures, shares[3]))
+    for phase in range(len(bits)):
+        crossed = halve(mixtures, phase)
+        if phase < len(bits) - 1:
+            mixtures = [total(parts).astype(bf16) for parts in crossed]
     normed_sums = [one[2] for one in grad_inputs]
     packed_sent, crossed = lax.optimization_barrier((packed_sent, crossed))
     mixture = []
     for number in range(micro):
-        parts = total(
-            [lax.dynamic_index_in_dim(mixtures[number], rank // 2, 0, keepdims=False)]
-            + [crossed[number, step] for step in range(1, ranks // 2)]
-        )
+        parts = total(crossed[number])[0]
         mixture.append(parts[0] + total(exchange_back(parts.astype(bf16))[1:]))
     output = (hidden + jnp.concatenate(mixture, axis=0)).astype(bf16)
     grad_tokens = []

time: 1070 us -> 1010 us (0.944)
  starting transfers between devices: 129 us -> 90.9 us
  local copies, waits for them, and re-layouts: 89.9 us -> 76.1 us
  blocking collectives: 12.8 us -> 0 us
    ppermute x27, starting transfers between devices: 84.4 us -> 51.6 us  [shift_rep(): lax.ppermute(value, 'rep', [(i, (i + step) % count) for i in range(count)])]
    ppermute x27, waiting for transfers between devices: 263 us -> 237 us  [shift_rep(): lax.ppermute(value, 'rep', [(i, (i + step) % count) for i in range(count)])]
    squeeze x8 -> x0, local copies, waits for them, and re-layouts: 24.8 us -> none  [the longest x5 8.75 us: cross(): lax.dynamic_index_in_dim(values[number], rank // 2 ^ step, 0, keepdims=Fa...]
    all_to_all x1 -> x0, blocking collectives: 12.8 us -> none  [on_device(): lax.all_to_all(grad_mixed, 'ep', split_axis=1, concat_axis=0, tiled=True)]
    ppermute x6, waiting for transfers between devices: 70.4 us -> 81.7 us  [exchange(): return lax.ppermute(value, 'rep', pairs)]
    ppermute x8 -> x6, waiting for transfers between devices: 69.4 us -> 78.8 us  [swap(): return lax.ppermute(value, 'ep', [(i, i ^ step) for i in range(ranks)])]
    unnamed x121 -> x123, local copies, waits for them, and re-layouts: 19.2 us -> 22.3 us
  transfers between devices with their start and end apart: 54 -> 53, of which waited for: 27 -> 25; matrix products, arithmetic and copies ran while one was open for 13% -> 13% of each run, Pallas kernels for 28% -> 30%
where the time goes in v8:
time: 1010 us; the launch traced here: 1000 us
  waiting for transfers between devices  425 us (42%)
  Pallas kernels  316 us (31%)
  starting transfers between devices  90.9 us (9%)
  local copies, waits for them, and re-layouts  76.1 us (8%)
  other arithmetic  69.1 us (7%)
  between operations  15.4 us (2%)
    ppermute x27, waiting for transfers between devices, shift_rep(): lax.ppermute(value, 'rep', [(i, (i + step) % count) for i in range(count)])  237 us
    pallas_call x2, Pallas kernels, expert_backward(): pl.pallas_call(kernel, grid_spec=pltpu.PrefetchScalarGridSpec(num_scalar_...  84.2 us
    ppermute x6, waiting for transfers between devices, exchange(): return lax.ppermute(value, 'rep', pairs)  81.7 us
    ppermute x6, waiting for transfers between devices, swap(): return lax.ppermute(value, 'ep', [(i, i ^ step) for i in range(ranks)])  78.8 us
    pallas_call x4, Pallas kernels, weight_gradient(): pl.pallas_call(kernel, grid_spec=pltpu.PrefetchScalarGridSpec(num_scalar_...  64.6 us
    ppermute x27, starting transfers between devices, shift_rep(): lax.ppermute(value, 'rep', [(i, (i + step) % count) for i in range(count)])  51.6 us
    pallas_call x1, Pallas kernels, expert_forward(): pl.pallas_call(kernel, grid_spec=pltpu.PrefetchScalarGridSpec(num_scalar_...  40.4 us
    pallas_call x2, Pallas kernels, attention_backward(): pl.pallas_call(lambda *refs: backward_kernel(heads, *refs), grid=(1,), in...  33.5 us
  transfers between devices with their start and end apart: 53, of which 25 were waited for; matrix products, arithmetic and copies ran while one was open for 13% of the time, Pallas kernels for 30%

profile of v8, /device:TPU:0, one launch (start us, length us, event | category | flops | bytes accessed | tf_op | source)
XLA Modules:
  0.0 1000.7 jit_solution(17291041504937735242)
XLA Ops:
  25.9 20.6 %collective-permute-done.3 = bf16[256,2048]{1,0:T(8,128)(2,1)S(1)} collective-permute-done((bf16[256,2048]{1,0:T(8,128)(2,1)}, bf16[256,2048]{1,0:T(8,128)(2,1)S(1)}, u32[]{:S(2)}, u32[]{:S(2)}) %collective-permute-start.3) | collective-permute-done | bytes 1048608 | tf_op jit(solution)/shard_map/ppermute | solution.py:747
  67.4 16.1 %collective-permute-done.4 = bf16[512,896]{1,0:T(8,128)(2,1)S(1)} collective-permute-done((bf16[512,896]{1,0:T(8,128)(2,1)S(1)}, bf16[512,896]{1,0:T(8,128)(2,1)S(1)}, u32[]{:S(2)}, u32[]{:S(2)}) %collective-permute-start.4) | collective-permute-done | bytes 917536 | tf_op jit(solution)/shard_map/ppermute | solution.py:695
  83.5 22.4 %collective-permute-done.5 = bf16[512,896]{1,0:T(8,128)(2,1)S(1)} collective-permute-done((bf16[512,896]{1,0:T(8,128)(2,1)S(1)}, bf16[512,896]{1,0:T(8,128)(2,1)S(1)}, u32[]{:S(2)}, u32[]{:S(2)}) %collective-permute-start.5) | collective-permute-done | bytes 917536 | tf_op jit(solution)/shard_map/ppermute | solution.py:695
  111.0 16.5 %collective-permute-done.6 = bf16[512,896]{1,0:T(8,128)(2,1)} collective-permute-done((bf16[512,896]{1,0:T(8,128)(2,1)S(1)}, bf16[512,896]{1,0:T(8,128)(2,1)}, u32[]{:S(2)}, u32[]{:S(2)}) %collective-permute-start.6) | collective-permute-done | bytes 917536 | tf_op jit(solution)/shard_map/ppermute | solution.py:695
  136.6 15.0 %shard_map.178 = (bf16[8,256,2048]{2,1,0:T(8,128)(2,1)}, f32[8,256,768]{2,1,0:T(8,128)}) custom-call(bf16[8,256,2048]{2,1,0:T(8,128)(2,1)} %bitcast.156, f32[1,2048]{1,0:T(1,128)S(1)} %broadcast_in_dim.63.gain, bf16[2048,896]{1,0:T(8,128)(2,1)} %constant_dynamic-update-slice_fusion.weight), custom_call_target="tpu_custom_call" | custom-call | tf_op jit(solution)/shard_map/pallas_call | solution.py:247
  151.6 21.7 %shard_map.179 = (bf16[8,2,128,256]{3,2,1,0:T(8,128)(2,1)}, bf16[2,1024,256]{2,1,0:T(8,128)(2,1)S(1)}, bf16[2,1024,256]{2,1,0:T(8,128)(2,1)S(1)}, bf16[2,1024,256]{2,1,0:T(8,128)(2,1)}, f32[2,2,1024,1]{3,2,1,0:T(8,128)}) custom-call(f32[8,2,128,768]{3,2,1,0:T(8,128)} %bitcast.159, f32[2,1024,128]{2,1,0:T(8,128)} %get-tuple-element.221.refs_1_, ...), custom_call_target="tpu_custom_call" | custom-call | tf_op jit(solution)/shard_map/pallas_call | solution.py:198
  180.8 25.0 %all-to-all-done.1 = bf16[8,2,128,256]{3,2,1,0:T(8,128)(2,1)S(1)} async-done(((bf16[8,2,128,256]{3,2,1,0:T(8,128)(2,1)}), bf16[8,2,128,256]{3,2,1,0:T(8,128)(2,1)S(1)}, u32[]{:S(2)}, u32[]{:S(2)}) %all-to-all-start.1) | async-done | bytes 1048608 | tf_op jit(solution)/shard_map/all_to_all | solution.py:811
  219.1 24.6 %collective-permute-done.9 = bf16[256,2176]{1,0:T(8,128)(2,1)S(1)} collective-permute-done((bf16[256,2176]{1,0:T(8,128)(2,1)S(1)}, bf16[256,2176]{1,0:T(8,128)(2,1)S(1)}, u32[]{:S(2)}, u32[]{:S(2)}) %collective-permute-start.9) | collective-permute-done | bytes 1114144 | tf_op jit(solution)/shard_map/ppermute | solution.py:747
  247.1 89.4 %collective-permute-done.10.refs_2_ = bf16[512,2048]{1,0:T(8,128)(2,1)} collective-permute-done((bf16[512,2048]{1,0:T(8,128)(2,1)}, bf16[512,2048]{1,0:T(8,128)(2,1)}, u32[]{:S(2)}, u32[]{:S(2)}) %collective-permute-start.10) | collective-permute-done | bytes 2097184 | tf_op jit(solution)/shard_map/ppermute | solution.py:695
  340.3 40.4 %shard_map.181 = (bf16[2,4,288,2048]{3,2,1,0:T(8,128)(2,1)}, f32[2,4,288,128]{3,2,1,0:T(8,128)S(1)}, f32[2,4,288,2048]{3,2,1,0:T(8,128)}, bf16[2,4,288,1024]{3,2...) custom-call(s32[3]{0:T(128)S(1)} %pad_add_fusion.where, ...), custom_call_target="tpu_custom_call" | custom-call | flops 241591910400 | tf_op jit(solution)/shard_map/pallas_call | solution.py:429
  383.0 16.7 %shard_map.182 = (bf16[256,2048]{1,0:T(8,128)(2,1)S(1)}, bf16[256,2048]{1,0:T(8,128)(2,1)}, bf16[256,2048]{1,0:T(8,128)(2,1)S(1)}, bf16[256,2048]{1,0:T(8,128)(2,1)}) custom-call(s32[3]{0:T(128)S(1)} %pad_add_fusion.where, bf16[2304,1024]{1,0:T(8,128)(2,1)} %bitcast.198, bf16[2304,2048]{1,0:T(8,128)(2,1)} %bitcast.197), custom_call_target="tpu_custom_call" | custom-call | flops 96636764160 | tf_op jit(solution)/shard_map/pallas_call | solution.py:589
  408.6 22.5 %collective-permute-start.14 = (bf16[256,2048]{1,0:T(8,128)(2,1)}, bf16[256,2048]{1,0:T(8,128)(2,1)}, u32[]{:S(2)}, u32[]{:S(2)}) collective-permute-start(bf16[256,2048]{1,0:T(8,128)(2,1)} %get-tuple-element.283), channel_id=1, source_target_pairs={{0,8},{8,16},{16,24},{24,0},{1,9},{9,17},{17,25},{25,1},{2,10},{10... | collective-permute-start | bytes 3145736 | tf_op jit(solution)/shard_map/ppermute | solution.py:695
  431.1 40.4 %shard_map.183 = (bf16[4,2,128,2048]{3,2,1,0:T(8,128)(2,1)}, bf16[4,2,128,2048]{3,2,1,0:T(8,128)(2,1)}, bf16[8,2,128,2176]{3,2,1,0:T(8,128)(2,1)}, bf16[4,288,2048]{2,1,0:T(8,128)(2,1)}) custom-call(s32[3]{0:T(128)S(1)} %pad_add_fusion.where, f32[2,4,288,128]{3,2,1,0:T(8,128)} %copy-done.33, f32[2,4,288,2048]{3,2,1,0:T(8,128)} %get-tuple-element.273.both, ...), custom_call_target="tpu_custom_call" | custom-call | flops 217432719360 | tf_op jit(solution)/shard_map/pallas_call | solution.py:527
  474.2 43.8 %shard_map.184 = (bf16[4,2,128,2048]{3,2,1,0:T(8,128)(2,1)}, bf16[4,2,128,2048]{3,2,1,0:T(8,128)(2,1)}, bf16[8,2,128,2176]{3,2,1,0:T(8,128)(2,1)}, bf16[4,288,2048]{2,1,0:T(8,128)(2,1)}) custom-call(s32[3]{0:T(128)S(1)} %pad_add_fusion.where, f32[2,4,288,128]{3,2,1,0:T(8,128)} %copy-done.33, f32[2,4,288,2048]{3,2,1,0:T(8,128)} %get-tuple-element.273.both, ...), custom_call_target="tpu_custom_call" | custom-call | flops 217432719360 | tf_op jit(solution)/shard_map/pallas_call | solution.py:527
  530.4 24.0 %shard_map.186 = (bf16[512,2048]{1,0:T(8,128)(2,1)S(1)}, bf16[512,2048]{1,0:T(8,128)(2,1)}, bf16[512,2048]{1,0:T(8,128)(2,1)}) custom-call(s32[3]{0:T(128)S(1)} %pad_add_fusion.where, bf16[2304,2048]{1,0:T(8,128)(2,1)} %bitcast.196, bf16[1152,2048]{1,0:T(8,128)(2,1)} %bitcast.200, bf16[1152,2048]{1,0:T(8,128)(2,1)} %bitcast.202), custom_call_target="tpu_custom_call" | custom-call | flops 144955146240 | tf_op jit(solution)/shard_map/pallas_call | solution.py:589
  555.8 23.5 %collective-permute-done.17 = bf16[512,2048]{1,0:T(8,128)(2,1)} collective-permute-done((bf16[512,2048]{1,0:T(8,128)(2,1)}, bf16[512,2048]{1,0:T(8,128)(2,1)}, u32[]{:S(2)}, u32[]{:S(2)}) %collective-permute-start.17) | collective-permute-done | bytes 2097184 | tf_op jit(solution)/shard_map/ppermute | solution.py:695
  637.2 16.7 %shard_map.188 = (bf16[8,128,768]{2,1,0:T(8,128)(2,1)}, f32[2,128]{1,0:T(2,128)S(1)}) custom-call(f32[8,2,128,768]{3,2,1,0:T(8,128)} %bitcast.160, f32[2,1024,128]{2,1,0:T(8,128)S(1)} %copy-done.2, f32[2,1024,128]{2,1,0:T(8,128)S(1)} %copy-done.1, s32[2,1024,1]{2,1,0:T(8,128)S(1)} %copy-done.3, s32[2,1,1024]{2,1,0:T(1,128)S(1)} %copy-done.25, ...), custom_call_target="tpu_custom_call" | custom-call | tf_op jit(solution)/shard_map/pallas_call | solution.py:220
  655.3 13.9 %shard_map.189 = (bf16[1024,2048]{1,0:T(8,128)(2,1)}, f32[1,2048]{1,0:T(1,128)S(1)}) custom-call(bf16[8,128,768]{2,1,0:T(8,128)(2,1)S(1)} %copy-done.8, bf16[8,256,2048]{2,1,0:T(8,128)(2,1)} %bitcast.157, bf16[2048,896]{1,0:T(8,128)(2,1)} %constant_dynamic-update-slice_fusion.weight), custom_call_target="tpu_custom_call" | custom-call | tf_op jit(solution)/shard_map/pallas_call | solution.py:679
  671.4 14.3 %collective-permute-done.22.refs_1_ = bf16[128,2176]{1,0:T(8,128)(2,1)S(1)} collective-permute-done((bf16[128,2176]{1,0:T(8,128)(2,1)S(1)}, bf16[128,2176]{1,0:T(8,128)(2,1)S(1)}, u32[]{:S(2)}, u32[]{:S(2)}) %collective-permute-start.22) | collective-permute-done | bytes 557088 | tf_op jit(solution)/shard_map/ppermute | solution.py:747
  723.4 16.7 %shard_map.191 = (bf16[8,128,768]{2,1,0:T(8,128)(2,1)}, f32[2,128]{1,0:T(2,128)S(1)}) custom-call(f32[8,2,128,768]{3,2,1,0:T(8,128)} %bitcast.161, f32[2,1024,128]{2,1,0:T(8,128)S(1)} %copy-done.2, f32[2,1024,128]{2,1,0:T(8,128)S(1)} %copy-done.1, s32[2,1024,1]{2,1,0:T(8,128)S(1)} %copy-done.4, s32[2,1,1024]{2,1,0:T(1,128)S(1)} %copy-done.25, ...), custom_call_target="tpu_custom_call" | custom-call | tf_op jit(solution)/shard_map/pallas_call | solution.py:220
  748.6 13.9 %shard_map.192 = (bf16[1024,2048]{1,0:T(8,128)(2,1)}, f32[1,2048]{1,0:T(1,128)S(1)}) custom-call(bf16[8,128,768]{2,1,0:T(8,128)(2,1)S(1)} %copy-done.10, bf16[8,256,2048]{2,1,0:T(8,128)(2,1)} %bitcast.158, bf16[2048,896]{1,0:T(8,128)(2,1)} %constant_dynamic-update-slice_fusion.weight), custom_call_target="tpu_custom_call" | custom-call | tf_op jit(solution)/shard_map/pallas_call | solution.py:679
  767.6 20.0 %collective-permute-done.25 = bf16[128,2048]{1,0:T(8,128)(2,1)} collective-permute-done((bf16[128,2048]{1,0:T(8,128)(2,1)}, bf16[128,2048]{1,0:T(8,128)(2,1)}, u32[]{:S(2)}, u32[]{:S(2)}) %collective-permute-start.25) | collective-permute-done | bytes 524320 | tf_op jit(solution)/shard_map/ppermute | solution.py:695
  830.8 51.4 %collective-permute-done.30 = bf16[2,2,128,2048]{3,2,1,0:T(8,128)(2,1)} collective-permute-done((bf16[2,2,128,2048]{3,2,1,0:T(8,128)(2,1)}, bf16[2,2,128,2048]{3,2,1,0:T(8,128)(2,1)}, u32[]{:S(2)}, u32[]{:S(2)}) %collective-permute-start.30) | collective-permute-done | bytes 2097184 | tf_op jit(solution)/shard_map/ppermute | solution.py:884
  904.2 18.4 %collective-permute-done.31 = bf16[1,2,128,2048]{3,2,1,0:T(8,128)(2,1)} collective-permute-done((bf16[1,2,128,2048]{3,2,1,0:T(8,128)(2,1)S(1)}, bf16[1,2,128,2048]{3,2,1,0:T(8,128)(2,1)}, u32[]{:S(2)}, u32[]{:S(2)}) %collective-permute-start.31) | collective-permute-done | bytes 1048608 | tf_op jit(solution)/shard_map/ppermute | solution.py:884
  (332 shorter events, 357.4 us)
Async XLA Ops:
  7.2 122.5 %all-gather.9.cloned.1.call-start = ((), (), s32[]{:S(2)}) async-start(), calls=%async_computation.15 | async-start | bytes 9437184 | tf_op jit(solution)/shard_map/all_gather | solution.py:753
  20.2 186.5 %all-gather.11.cloned.1.call-start = ((), (), s32[]{:S(2)}) async-start(), calls=%async_computation.16 | async-start | bytes 9437184 | tf_op jit(solution)/shard_map/all_gather | solution.py:753
  53.5 286.8 %all-gather.15.cloned.1.call-start = ((), (), s32[]{:S(2)}) async-start(), calls=%async_computation.18 | async-start | bytes 18874368 | tf_op jit(solution)/shard_map/all_gather | solution.py:753
  129.7 86.1 %collective-permute-start.7 = (bf16[512,2048]{1,0:T(8,128)(2,1)}, bf16[512,2048]{1,0:T(8,128)(2,1)}, u32[]{:S(2)}, u32[]{:S(2)}) collective-permute-start(bf16[512,2048]{1,0:T(8,128)(2,1)} %get-tuple-element.239), channel_id=1, source_target_pairs={{0,8},{8,16},{16,24},{24,0},{1,9},{9,17},{17,25},{25,1},{2,10},{10... | collective-permute-start | bytes 6291464 | tf_op jit(solution)/shard_map/ppermute | solution.py:695
  129.8 89.4 %collective-permute-start.8 = (bf16[512,2048]{1,0:T(8,128)(2,1)}, bf16[512,2048]{1,0:T(8,128)(2,1)}, u32[]{:S(2)}, u32[]{:S(2)}) collective-permute-start(bf16[512,2048]{1,0:T(8,128)(2,1)} %get-tuple-element.240), channel_id=1, source_target_pairs={{0,24},{8,0},{16,8},{24,16},{1,25},{9,1},{17,9},{25,17},{2,26},{10... | collective-permute-start | bytes 6291464 | tf_op jit(solution)/shard_map/ppermute | solution.py:695
  179.0 161.3 %all-gather.13.cloned.1.call-start = ((), (), s32[]{:S(2)}) async-start(), calls=%async_computation.17 | async-start | bytes 20054016 | tf_op jit(solution)/shard_map/all_gather | solution.py:753
  245.4 333.9 %reduce-scatter.6.cloned.1.call-start = ((), (), s32[]{:S(2)}) async-start(), calls=%async_computation.10 | async-start | bytes 10027008 | tf_op jit(solution)/shard_map/reduce_scatter | solution.py:854
  245.4 91.0 %collective-permute-start.10 = (bf16[512,2048]{1,0:T(8,128)(2,1)}, bf16[512,2048]{1,0:T(8,128)(2,1)}, u32[]{:S(2)}, u32[]{:S(2)}) collective-permute-start(bf16[512,2048]{1,0:T(8,128)(2,1)} %get-tuple-element.251), channel_id=1, source_target_pairs={{0,16},{8,24},{16,0},{24,8},{1,17},{9,25},{17,1},{25,9},{2,18},{10... | collective-permute-start | bytes 6291464 | tf_op jit(solution)/shard_map/ppermute | solution.py:695
  336.4 65.3 %collective-permute-start.11 = (bf16[256,2048]{1,0:T(8,128)(2,1)}, bf16[256,2048]{1,0:T(8,128)(2,1)}, u32[]{:S(2)}, u32[]{:S(2)}) collective-permute-start(bf16[256,2048]{1,0:T(8,128)(2,1)} %get-tuple-element.269), channel_id=1, source_target_pairs={{0,8},{8,16},{16,24},{24,0},{1,9},{9,17},{17,25},{25,1},{2,10},{10... | collective-permute-start | bytes 3145736 | tf_op jit(solution)/shard_map/ppermute | solution.py:695
  336.4 72.2 %collective-permute-start.12 = (bf16[256,2048]{1,0:T(8,128)(2,1)}, bf16[256,2048]{1,0:T(8,128)(2,1)}, u32[]{:S(2)}, u32[]{:S(2)}) collective-permute-start(bf16[256,2048]{1,0:T(8,128)(2,1)} %get-tuple-element.270), channel_id=1, source_target_pairs={{0,16},{8,24},{16,0},{24,8},{1,17},{9,25},{17,1},{25,9},{2,18},{10... | collective-permute-start | bytes 3145736 | tf_op jit(solution)/shard_map/ppermute | solution.py:695
  337.3 71.4 %collective-permute-start.13 = (bf16[256,2048]{1,0:T(8,128)(2,1)}, bf16[256,2048]{1,0:T(8,128)(2,1)}, u32[]{:S(2)}, u32[]{:S(2)}) collective-permute-start(bf16[256,2048]{1,0:T(8,128)(2,1)} %get-tuple-element.271), channel_id=1, source_target_pairs={{0,24},{8,0},{16,8},{24,16},{1,25},{9,1},{17,9},{25,17},{2,26},{10... | collective-permute-start | bytes 3145736 | tf_op jit(solution)/shard_map/ppermute | solution.py:695
  408.6 65.6 %collective-permute-start.14 = (bf16[256,2048]{1,0:T(8,128)(2,1)}, bf16[256,2048]{1,0:T(8,128)(2,1)}, u32[]{:S(2)}, u32[]{:S(2)}) collective-permute-start(bf16[256,2048]{1,0:T(8,128)(2,1)} %get-tuple-element.283), channel_id=1, source_target_pairs={{0,8},{8,16},{16,24},{24,0},{1,9},{9,17},{17,25},{25,1},{2,10},{10... | collective-permute-start | bytes 3145736 | tf_op jit(solution)/shard_map/ppermute | solution.py:695
  471.6 197.7 %reduce-scatter.8.cloned.1.call-start = ((), (), s32[]{:S(2)}) async-start(), calls=%async_computation.11 | async-start | bytes 10027008 | tf_op jit(solution)/shard_map/reduce_scatter | solution.py:854
  471.6 84.1 %collective-permute-start.15 = (bf16[256,2048]{1,0:T(8,128)(2,1)}, bf16[256,2048]{1,0:T(8,128)(2,1)}, u32[]{:S(2)}, u32[]{:S(2)}) collective-permute-start(bf16[256,2048]{1,0:T(8,128)(2,1)} %copy-done.30), channel_id=1, source_target_pairs={{0,16},{8,24},{16,0},{24,8},{1,17},{9,25},{17,1},{25,9},{2,18},{10... | collective-permute-start | bytes 3145736 | tf_op jit(solution)/shard_map/ppermute | solution.py:695
  471.7 84.0 %collective-permute-start.16 = (bf16[256,2048]{1,0:T(8,128)(2,1)}, bf16[256,2048]{1,0:T(8,128)(2,1)}, u32[]{:S(2)}, u32[]{:S(2)}) collective-permute-start(bf16[256,2048]{1,0:T(8,128)(2,1)} %get-tuple-element.293), channel_id=1, source_target_pairs={{0,24},{8,0},{16,8},{24,16},{1,25},{9,1},{17,9},{25,17},{2,26},{10... | collective-permute-start | bytes 3145736 | tf_op jit(solution)/shard_map/ppermute | solution.py:695
  602.8 51.1 %collective-permute-start.21 = (bf16[512,2048]{1,0:T(8,128)(2,1)}, bf16[512,2048]{1,0:T(8,128)(2,1)}, u32[]{:S(2)}, u32[]{:S(2)}) collective-permute-start(bf16[512,2048]{1,0:T(8,128)(2,1)} %get-tuple-element.314), channel_id=1, source_target_pairs={{0,24},{8,0},{16,8},{24,16},{1,25},{9,1},{17,9},{25,17},{2,26},{10... | collective-permute-start | bytes 6291464 | tf_op jit(solution)/shard_map/ppermute | solution.py:695
  621.7 125.4 %reduce-scatter.10.cloned.1.call-start = ((), (), s32[]{:S(2)}) async-start(), calls=%async_computation.12 | async-start | bytes 4718592 | tf_op jit(solution)/shard_map/reduce_scatter | solution.py:966
  704.6 260.5 %reduce-scatter.12.cloned.1.call-start = ((), (), s32[]{:S(2)}) async-start(), calls=%async_computation.13 | async-start | bytes 4718592 | tf_op jit(solution)/shard_map/reduce_scatter | solution.py:966
  762.5 206.7 %reduce-scatter.14.cloned.1.call-start = ((), (), s32[]{:S(2)}) async-start(), calls=%async_computation.14 | async-start | bytes 9437184 | tf_op jit(solution)/shard_map/reduce_scatter | solution.py:946
  814.6 67.6 %collective-permute-start.30 = (bf16[2,2,128,2048]{3,2,1,0:T(8,128)(2,1)}, bf16[2,2,128,2048]{3,2,1,0:T(8,128)(2,1)}, u32[]{:S(2)}, u32[]{:S(2)}) collective-permute-start(bf16[2,2,128,2048]{3,2,1,0:T(8,128)(2,1)} %dynamic-slice_bitcast_fusion.1), channel_id=1, source_target_pairs={{0,2},{1,3},{2,0},{3,1},{4,6},{5,7},{6,4},{7,5},{8,10},{9,11},{10,... | collective-permute-start | bytes 6291464 | tf_op jit(solution)/shard_map/ppermute | solution.py:884
  818.9 71.3 %collective-permute-start.32 = (bf16[2,2,128,2048]{3,2,1,0:T(8,128)(2,1)}, bf16[2,2,128,2048]{3,2,1,0:T(8,128)(2,1)}, u32[]{:S(2)}, u32[]{:S(2)}) collective-permute-start(bf16[2,2,128,2048]{3,2,1,0:T(8,128)(2,1)} %dynamic-slice_bitcast_fusion), channel_id=1, source_target_pairs={{0,4},{1,5},{2,6},{3,7},{4,0},{5,1},{6,2},{7,3},{8,12},{9,13},{10,... | collective-permute-start | bytes 6291464 | tf_op jit(solution)/shard_map/ppermute | solution.py:884
  820.8 83.4 %collective-permute-start.27 = (bf16[512,896]{1,0:T(8,128)(2,1)}, bf16[512,896]{1,0:T(8,128)(2,1)S(1)}, u32[]{:S(2)}, u32[]{:S(2)}) collective-permute-start(bf16[512,896]{1,0:T(8,128)(2,1)} %copy-done.31), channel_id=1, source_target_pairs={{0,8},{8,16},{16,24},{24,0},{1,9},{9,17},{17,25},{25,1},{2,10},{10... | collective-permute-start | bytes 2752520 | tf_op jit(solution)/shard_map/ppermute | solution.py:695
  820.8 83.4 %collective-permute-start.28 = (bf16[512,896]{1,0:T(8,128)(2,1)S(1)}, bf16[512,896]{1,0:T(8,128)(2,1)S(1)}, u32[]{:S(2)}, u32[]{:S(2)}) collective-permute-start(bf16[512,896]{1,0:T(8,128)(2,1)S(1)} %get-tuple-element.380), channel_id=1, source_target_pairs={{0,16},{8,24},{16,0},{24,8},{1,17},{9,25},{17,1},{25,9},{2,18},{10... | collective-permute-start | bytes 2752520 | tf_op jit(solution)/shard_map/ppermute | solution.py:695
  823.4 80.8 %collective-permute-start.29 = (bf16[512,896]{1,0:T(8,128)(2,1)}, bf16[512,896]{1,0:T(8,128)(2,1)S(1)}, u32[]{:S(2)}, u32[]{:S(2)}) collective-permute-start(bf16[512,896]{1,0:T(8,128)(2,1)} %get-tuple-element.381), channel_id=1, source_target_pairs={{0,24},{8,0},{16,8},{24,16},{1,25},{9,1},{17,9},{25,17},{2,26},{10... | collective-permute-start | bytes 2752520 | tf_op jit(solution)/shard_map/ppermute | solution.py:695
  (87 other events, 2288.9 us)
Sparse Core Ops, SparseCore 0:
  9.9 65.9 all-gather.8
  77.8 54.3 all-gather.10
  134.1 101.0 all-gather.14
  245.5 92.4 all-gather.12
  471.7 71.0 reduce-scatter.5
  546.2 73.7 reduce-scatter.7
  669.4 51.6 reduce-scatter.9
  762.6 50.2 reduce-scatter.11
  816.3 105.0 reduce-scatter.13

commit v9 on v8

--- a/solution.py
+++ b/solution.py
@@ -690,6 +690,45 @@
     )(grad_proj, tokens, slab)
 
 
+def cut_heads(weight, tail, ranks):
+    rows = weight.shape[0]
+    width = D // ranks
+
+    def kernel(weight, tail, target):
+        for rank in range(ranks):
+            for part in range(3):
+                at = part * D + rank * width
+                target[rank, :, part * width : (part + 1) * width] = weight[:, at : at + width]
+            target[rank, :, 3 * width :] = tail[...]
+
+    return pl.pallas_call(
+        kernel,
+        out_shape=out((ranks, rows, 3 * width + PAD)),
+        compiler_params=params(),
+    )(weight, tail)
+
+
+def unpack(packed, count):
+    ranks, rows, columns = packed.shape
+    width = (columns - PAD) // 3
+
+    def kernel(packed, main, small):
+        for rank in range(ranks):
+            for part in range(3):
+                at = part * D + rank * width
+                main[:, at : at + width] = packed[rank, :, part * width : (part + 1) * width].astype(
+                    f32
+                )
+        tails = sum(packed[rank, :, 3 * width :].astype(f32) for rank in range(ranks))
+        small[...] = tails + pltpu.roll(tails, PAD - count, 1)
+
+    return pl.pallas_call(
+        kernel,
+        out_shape=[out((rows, 3 * D), f32), out((rows, PAD), f32)],
+        compiler_params=params(),
+    )(packed)
+
+
 def shift_rep(value, step):
     count = lax.axis_size("rep")
     return lax.ppermute(value, "rep", [(i, (i + step) % count) for i in range(count)])
@@ -715,7 +754,7 @@
     full = jnp.zeros((count * rows,) + value.shape[1:], value.dtype)
     full = lax.dynamic_update_slice_in_dim(full, value, rank * rows, 0)
     for step in range(1, count):
-        value, work = lax.optimization_barrier((value, work)) if step == 2 else (value, work)
+        value, work = lax.optimization_barrier((value, work)) if step == count - 1 else (value, work)
         value = shift_rep(value, 1)
         full = lax.dynamic_update_slice_in_dim(full, value, (rank - step) % count * rows, 0)
     return full, work
@@ -767,24 +806,17 @@
     stream = gather_ranks(tokens)
     out_rows = [w_o] + [shift_rep(w_o, step) for step in range(1, planes)]
     upstream_group = with_group(cotangent)
-    slab = jnp.concatenate(
-        [
-            w_qkv.reshape(dense_rows, 3, ranks, width)
-            .transpose(2, 0, 1, 3)
-            .reshape(ranks, dense_rows, 3 * width),
-            jnp.broadcast_to(
-                jnp.concatenate(
-                    [
-                        w_router,
-                        norm_gains.reshape(dense_rows, 2),
-                        jnp.zeros((dense_rows, PAD - experts - 2), bf16),
-                    ],
-                    axis=1,
-                )[None],
-                (ranks, dense_rows, PAD),
-            ),
-        ],
-        axis=2,
+    slab = cut_heads(
+        w_qkv,
+        jnp.concatenate(
+            [
+                w_router,
+                norm_gains.reshape(dense_rows, 2),
+                jnp.zeros((dense_rows, PAD - experts - 2), bf16),
+            ],
+            axis=1,
+        ),
+        ranks,
     )
     slab = lax.all_to_all(slab, "ep", split_axis=0, concat_axis=0, tiled=True)
     slab = slab.reshape(ranks * dense_rows, 3 * width + PAD)
@@ -865,7 +897,9 @@
         )
         returned.append(scatter_ranks(back[step][2]))
         if step == 0:
-            tail, out_sent[order[0]] = after((tail, out_sent[order[0]]), back[step][2])
+            short = {near: out_sent[near] for near in order[:2]}
+            tail, short = after((tail, short), back[step][2])
+            out_sent.update(short)
         else:
             tail = after(tail, back[step][2])
     rows_in = after(rows_in, tail)
@@ -924,7 +958,7 @@
         in_sent.update(send(in_cut, releases[step]))
         if step == micro - 1:
             last = in_cut[order[-1]]
-            ends = [-(-last.shape[0] * part // 64) * 16 for part in range(5)]
+            ends = [-(-last.shape[0] * eighths // 128) * 16 for eighths in (0, 3, 5, 8)]
             last = [last[start:end] for start, end in zip(ends, ends[1:])]
             last_sent = [shift_rep(last[0], order[-1])]
         grad_hidden, grad_branch, grad_mixed, grad_logits, gain_two = hidden_backward(
@@ -955,7 +989,6 @@
             grad_proj, grad_inputs, last_sent, last = lax.optimization_barrier(
                 (grad_proj, grad_inputs, last_sent, last)
             )
-            last_sent.append(shift_rep(last[2], order[-1]))
         grad_projs.append(grad_proj)
         grad_normed, gain_one = project_backward(step, grad_proj, stream, slab)
         gain_one_sum = gain_one_sum + gain_one
@@ -987,10 +1020,10 @@
     def joined(value):
         return value[..., :count].astype(f32) + value[..., count : 2 * count].astype(f32)
 
-    grad_projs, last_sent, last, out_cut, out_sent, _ = lax.optimization_barrier(
-        (grad_projs, last_sent, last, out_cut, out_sent, grad_normed)
-    )
-    last_sent.append(shift_rep(last[3], order[-1]))
+    grad_projs, last, out_cut, out_sent, _ = lax.optimization_barrier(
+        (grad_projs, last, out_cut, out_sent, grad_normed)
+    )
+    last_sent.append(shift_rep(last[2], order[-1]))
     packed = weight_gradient(
         where,
         planes,
@@ -1007,46 +1040,50 @@
         if phase < len(bits) - 1:
             mixtures = [total(parts).astype(bf16) for parts in crossed]
     normed_sums = [one[2] for one in grad_inputs]
-    packed_sent, crossed = lax.optimization_barrier((packed_sent, crossed))
+    normed_sums = [one[2] for one in grad_inputs]
+    grad_tokens = []
+    for step in range(micro):
+        own_stream = tokens[step * rows : (step + 1) * rows].astype(f32)
+        grad_tokens.append(
+            grad_inputs[step][0]
+            + rms_backward(
+                own_stream, inverse_rms(own_stream), first_gain, normed_sums[step].astype(f32)
+            )
+        )
+    grad_tokens = jnp.concatenate(grad_tokens, axis=0)
+    packed_sent, grad_tokens = lax.optimization_barrier((packed_sent, grad_tokens))
+    crossed, out_sum = lax.optimization_barrier((crossed, out_sum))
     mixture = []
     for number in range(micro):
         parts = total(crossed[number])[0]
-        mixture.append(parts[0] + total(exchange_back(parts.astype(bf16))[1:]))
-    output = (hidden + jnp.concatenate(mixture, axis=0)).astype(bf16)
-    grad_tokens = []
-    for step in range(micro):
-        grad_hidden, grad_normed = grad_inputs[step][0], normed_sums[step]
-        own_stream = tokens[step * rows : (step + 1) * rows].astype(f32)
-        grad_tokens.append(
-            grad_hidden
-            + rms_backward(
-                own_stream, inverse_rms(own_stream), first_gain, grad_normed.astype(f32)
-            )
+        mixture.append((parts[0], exchange_back(parts.astype(bf16))[1:]))
+    own_sum = lax.dynamic_index_in_dim(out_sum, plane, 0, keepdims=False)
+    out_sent_back = [
+        shift_rep(
+            lax.dynamic_index_in_dim(out_sum, (plane + step) % planes, 0, keepdims=False), step
         )
+        for step in range(1, planes)
+    ]
     main = total([part[:, : 3 * width] for part in packed_sent]).astype(bf16)
     small = sum(joined(part[:, 3 * width :]) for part in packed_sent)
     packed = jnp.concatenate([main, halves(small)], axis=1).reshape(ranks, dense_rows, -1)
     packed = lax.all_to_all(packed, "ep", split_axis=0, concat_axis=0, tiled=True)
-    main = packed[..., : 3 * width].astype(f32)
-    small = jnp.sum(joined(packed[..., 3 * width :]), axis=0)
-    grad_w_qkv = (
-        main.reshape(ranks, dense_rows, 3, width).transpose(1, 2, 0, 3).reshape(dense_rows, 3 * D)
-    )
+    packed, mixture, out_sent_back = lax.optimization_barrier((packed, mixture, out_sent_back))
+    output = jnp.concatenate([mine_part + total(others) for mine_part, others in mixture], axis=0)
+    output = (hidden + output).astype(bf16)
+    grad_w_o = total([own_sum, *out_sent_back])
+    grad_w_qkv, small = unpack(packed, count)
     grad_w_out = sum_rep({0: out_cut[0], **out_sent})
     in_sent[order[-1]] = jnp.concatenate(last_sent, axis=0)
     grad_w_in = sum_rep({0: in_cut[0], **in_sent})
-    grad_w_o = lax.dynamic_index_in_dim(out_sum, plane, 0, keepdims=False).astype(f32)
-    for step in range(1, planes):
-        part = lax.dynamic_index_in_dim(out_sum, (plane + step) % planes, 0, keepdims=False)
-        grad_w_o = grad_w_o + shift_rep(part, step).astype(f32)
     return (
         output,
-        jnp.concatenate(grad_tokens, axis=0),
+        grad_tokens,
         grad_w_qkv,
         grad_w_o,
         small[:, :experts],
         small[:, experts : experts + 2].reshape(-1),
-        small[:, experts + 2 :].reshape(-1),
+        small[:, experts + 2 : count].reshape(-1),
         grad_w_in,
         grad_w_out,
     )

time: 1010 us -> 987 us (0.977)
  waiting for transfers between devices: 425 us -> 389 us
  starting transfers between devices: 90.9 us -> 106 us
    ppermute x27 -> x26, starting transfers between devices: 51.6 us -> 69.8 us  [shift_rep(): lax.ppermute(value, 'rep', [(i, (i + step) % count) for i in range(count)])]
    ppermute x27 -> x26, waiting for transfers between devices: 237 us -> 219 us  [shift_rep(): lax.ppermute(value, 'rep', [(i, (i + step) % count) for i in range(count)])]
    ppermute x6, waiting for transfers between devices: 78.8 us -> 61.7 us  [swap(): return lax.ppermute(value, 'ep', [(i, i ^ step) for i in range(ranks)])]
    reduce_scatter x1, waiting for transfers between devices: 0.02 us -> 11.9 us  [on_device(): out_sum = lax.psum_scatter(out_sum, 'ep', scatter_dimension=0)]
    ppermute x6, waiting for transfers between devices: 81.7 us -> 70.3 us  [exchange(): return lax.ppermute(value, 'rep', pairs)]
    unnamed x123 -> x113, local copies, waits for them, and re-layouts: 22.3 us -> 19.8 us
  transfers between devices with their start and end apart: 53 -> 52, of which waited for: 25 -> 23; matrix products, arithmetic and copies ran while one was open for 13% -> 12% of each run, Pallas kernels for 30% -> 31%
where the time goes in v9:
time: 987 us; the launch traced here: 978 us
  waiting for transfers between devices  389 us (39%)
  Pallas kernels  320 us (32%)
  starting transfers between devices  106 us (11%)
  local copies, waits for them, and re-layouts  70.3 us (7%)
  other arithmetic  67.1 us (7%)
  between operations  15.1 us (2%)
  matrix products  9.97 us (1%)
    ppermute x26, waiting for transfers between devices, shift_rep(): lax.ppermute(value, 'rep', [(i, (i + step) % count) for i in range(count)])  219 us
    pallas_call x2, Pallas kernels, expert_backward(): pl.pallas_call(kernel, grid_spec=pltpu.PrefetchScalarGridSpec(num_scalar_...  84.2 us
    ppermute x6, waiting for transfers between devices, exchange(): return lax.ppermute(value, 'rep', pairs)  70.3 us
    ppermute x26, starting transfers between devices, shift_rep(): lax.ppermute(value, 'rep', [(i, (i + step) % count) for i in range(count)])  69.8 us
    pallas_call x4, Pallas kernels, weight_gradient(): pl.pallas_call(kernel, grid_spec=pltpu.PrefetchScalarGridSpec(num_scalar_...  65.4 us
    ppermute x6, waiting for transfers between devices, swap(): return lax.ppermute(value, 'ep', [(i, i ^ step) for i in range(ranks)])  61.7 us
    pallas_call x1, Pallas kernels, expert_forward(): pl.pallas_call(kernel, grid_spec=pltpu.PrefetchScalarGridSpec(num_scalar_...  40.4 us
    pallas_call x2, Pallas kernels, attention_backward(): pl.pallas_call(lambda *refs: backward_kernel(heads, *refs), grid=(1,), in...  34.2 us
  transfers between devices with their start and end apart: 52, of which 23 were waited for; matrix products, arithmetic and copies ran while one was open for 12% of the time, Pallas kernels for 31%

profile of v9, /device:TPU:0, one launch (start us, length us, event | category | flops | bytes accessed | tf_op | source)
XLA Modules:
  0.0 977.9 jit_solution(6902397340830060007)
XLA Ops:
  24.3 22.3 %collective-permute-done.3 = bf16[256,2048]{1,0:T(8,128)(2,1)} collective-permute-done((bf16[256,2048]{1,0:T(8,128)(2,1)}, bf16[256,2048]{1,0:T(8,128)(2,1)}, u32[]{:S(2)}, u32[]{:S(2)}) %collective-permute-start.3) | collective-permute-done | bytes 1048608 | tf_op jit(solution)/shard_map/ppermute | solution.py:786
  59.1 18.0 %collective-permute-done.4 = bf16[512,896]{1,0:T(8,128)(2,1)S(1)} collective-permute-done((bf16[512,896]{1,0:T(8,128)(2,1)S(1)}, bf16[512,896]{1,0:T(8,128)(2,1)S(1)}, u32[]{:S(2)}, u32[]{:S(2)}) %collective-permute-start.4) | collective-permute-done | bytes 917536 | tf_op jit(solution)/shard_map/ppermute | solution.py:734
  84.4 15.2 %collective-permute-done.5 = bf16[512,896]{1,0:T(8,128)(2,1)S(1)} collective-permute-done((bf16[512,896]{1,0:T(8,128)(2,1)S(1)}, bf16[512,896]{1,0:T(8,128)(2,1)S(1)}, u32[]{:S(2)}, u32[]{:S(2)}) %collective-permute-start.5) | collective-permute-done | bytes 917536 | tf_op jit(solution)/shard_map/ppermute | solution.py:734
  104.7 16.6 %collective-permute-done.6 = bf16[512,896]{1,0:T(8,128)(2,1)} collective-permute-done((bf16[512,896]{1,0:T(8,128)(2,1)S(1)}, bf16[512,896]{1,0:T(8,128)(2,1)}, u32[]{:S(2)}, u32[]{:S(2)}) %collective-permute-start.6) | collective-permute-done | bytes 917536 | tf_op jit(solution)/shard_map/ppermute | solution.py:734
  130.4 14.8 %shard_map.179 = (bf16[8,256,2048]{2,1,0:T(8,128)(2,1)}, f32[8,256,768]{2,1,0:T(8,128)}) custom-call(bf16[8,256,2048]{2,1,0:T(8,128)(2,1)} %bitcast.144, f32[1,2048]{1,0:T(1,128)S(1)} %broadcast_in_dim.56.gain, bf16[2048,896]{1,0:T(8,128)(2,1)} %constant_dynamic-update-slice_fusion.weight), custom_call_target="tpu_custom_call" | custom-call | tf_op jit(solution)/shard_map/pallas_call | solution.py:247
  145.3 21.7 %shard_map.180 = (bf16[8,2,128,256]{3,2,1,0:T(8,128)(2,1)}, bf16[2,1024,256]{2,1,0:T(8,128)(2,1)S(1)}, bf16[2,1024,256]{2,1,0:T(8,128)(2,1)S(1)}, bf16[2,1024,256]{2,1,0:T(8,128)(2,1)}, f32[2,2,1024,1]{3,2,1,0:T(8,128)}) custom-call(f32[8,2,128,768]{3,2,1,0:T(8,128)} %bitcast.147, f32[2,1024,128]{2,1,0:T(8,128)} %get-tuple-element.228.refs_1_, ...), custom_call_target="tpu_custom_call" | custom-call | tf_op jit(solution)/shard_map/pallas_call | solution.py:198
  174.6 24.6 %all-to-all-done.1 = bf16[8,2,128,256]{3,2,1,0:T(8,128)(2,1)S(1)} async-done(((bf16[8,2,128,256]{3,2,1,0:T(8,128)(2,1)}), bf16[8,2,128,256]{3,2,1,0:T(8,128)(2,1)S(1)}, u32[]{:S(2)}, u32[]{:S(2)}) %all-to-all-start.1) | async-done | bytes 1048608 | tf_op jit(solution)/shard_map/all_to_all | solution.py:843
  213.0 24.6 %collective-permute-done.9 = bf16[256,2176]{1,0:T(8,128)(2,1)S(1)} collective-permute-done((bf16[256,2176]{1,0:T(8,128)(2,1)S(1)}, bf16[256,2176]{1,0:T(8,128)(2,1)S(1)}, u32[]{:S(2)}, u32[]{:S(2)}) %collective-permute-start.9) | collective-permute-done | bytes 1114144 | tf_op jit(solution)/shard_map/ppermute | solution.py:786
  240.9 89.4 %collective-permute-done.10.refs_2_ = bf16[512,2048]{1,0:T(8,128)(2,1)} collective-permute-done((bf16[512,2048]{1,0:T(8,128)(2,1)}, bf16[512,2048]{1,0:T(8,128)(2,1)}, u32[]{:S(2)}, u32[]{:S(2)}) %collective-permute-start.10) | collective-permute-done | bytes 2097184 | tf_op jit(solution)/shard_map/ppermute | solution.py:734
  334.2 40.4 %shard_map.182 = (bf16[2,4,288,2048]{3,2,1,0:T(8,128)(2,1)}, f32[2,4,288,128]{3,2,1,0:T(8,128)S(1)}, f32[2,4,288,2048]{3,2,1,0:T(8,128)}, bf16[2,4,288,1024]{3,2...) custom-call(s32[3]{0:T(128)S(1)} %pad_add_fusion.where, ...), custom_call_target="tpu_custom_call" | custom-call | flops 241591910400 | tf_op jit(solution)/shard_map/pallas_call | solution.py:429
  376.9 16.6 %shard_map.183 = (bf16[256,2048]{1,0:T(8,128)(2,1)S(1)}, bf16[256,2048]{1,0:T(8,128)(2,1)}, bf16[256,2048]{1,0:T(8,128)(2,1)S(1)}, bf16[256,2048]{1,0:T(8,128)(2,1)}) custom-call(s32[3]{0:T(128)S(1)} %pad_add_fusion.where, bf16[2304,1024]{1,0:T(8,128)(2,1)} %bitcast.179, bf16[2304,2048]{1,0:T(8,128)(2,1)} %bitcast.178), custom_call_target="tpu_custom_call" | custom-call | flops 96636764160 | tf_op jit(solution)/shard_map/pallas_call | solution.py:589
  402.5 43.1 %collective-permute-start.14 = (bf16[256,2048]{1,0:T(8,128)(2,1)}, bf16[256,2048]{1,0:T(8,128)(2,1)}, u32[]{:S(2)}, u32[]{:S(2)}) collective-permute-start(bf16[256,2048]{1,0:T(8,128)(2,1)} %get-tuple-element.290), channel_id=1, source_target_pairs={{0,8},{8,16},{16,24},{24,0},{1,9},{9,17},{17,25},{25,1},{2,10},{10... | collective-permute-start | bytes 3145736 | tf_op jit(solution)/shard_map/ppermute | solution.py:734
  446.1 40.4 %shard_map.184 = (bf16[4,2,128,2048]{3,2,1,0:T(8,128)(2,1)}, bf16[4,2,128,2048]{3,2,1,0:T(8,128)(2,1)}, bf16[8,2,128,2176]{3,2,1,0:T(8,128)(2,1)}, bf16[4,288,2048]{2,1,0:T(8,128)(2,1)}) custom-call(s32[3]{0:T(128)S(1)} %pad_add_fusion.where, f32[2,4,288,128]{3,2,1,0:T(8,128)} %copy-done.31, f32[2,4,288,2048]{3,2,1,0:T(8,128)} %get-tuple-element.280.both, ...), custom_call_target="tpu_custom_call" | custom-call | flops 217432719360 | tf_op jit(solution)/shard_map/pallas_call | solution.py:527
  488.1 43.8 %shard_map.185 = (bf16[4,2,128,2048]{3,2,1,0:T(8,128)(2,1)}, bf16[4,2,128,2048]{3,2,1,0:T(8,128)(2,1)}, bf16[8,2,128,2176]{3,2,1,0:T(8,128)(2,1)}, bf16[4,288,2048]{2,1,0:T(8,128)(2,1)}) custom-call(s32[3]{0:T(128)S(1)} %pad_add_fusion.where, f32[2,4,288,128]{3,2,1,0:T(8,128)} %copy-done.31, f32[2,4,288,2048]{3,2,1,0:T(8,128)} %get-tuple-element.280.both, ...), custom_call_target="tpu_custom_call" | custom-call | flops 217432719360 | tf_op jit(solution)/shard_map/pallas_call | solution.py:527
  544.2 23.9 %shard_map.187 = (bf16[512,2048]{1,0:T(8,128)(2,1)S(1)}, bf16[512,2048]{1,0:T(8,128)(2,1)}, bf16[512,2048]{1,0:T(8,128)(2,1)}) custom-call(s32[3]{0:T(128)S(1)} %pad_add_fusion.where, bf16[2304,2048]{1,0:T(8,128)(2,1)} %bitcast.177, bf16[1152,2048]{1,0:T(8,128)(2,1)} %bitcast.181, bf16[1152,2048]{1,0:T(8,128)(2,1)} %bitcast.183), custom_call_target="tpu_custom_call" | custom-call | flops 144955146240 | tf_op jit(solution)/shard_map/pallas_call | solution.py:589
  624.4 17.4 %shard_map.189 = (bf16[8,128,768]{2,1,0:T(8,128)(2,1)}, f32[2,128]{1,0:T(2,128)S(1)}) custom-call(f32[8,2,128,768]{3,2,1,0:T(8,128)} %bitcast.148, f32[2,1024,128]{2,1,0:T(8,128)S(1)} %copy-done.2, f32[2,1024,128]{2,1,0:T(8,128)S(1)} %copy-done.1, s32[2,1024,1]{2,1,0:T(8,128)S(1)} %copy-done.3, s32[2,1,1024]{2,1,0:T(1,128)S(1)} %copy-done.24, ...), custom_call_target="tpu_custom_call" | custom-call | tf_op jit(solution)/shard_map/pallas_call | solution.py:220
  643.3 13.9 %shard_map.190 = (bf16[1024,2048]{1,0:T(8,128)(2,1)}, f32[1,2048]{1,0:T(1,128)S(1)}) custom-call(bf16[8,128,768]{2,1,0:T(8,128)(2,1)S(1)} %copy-done.8, bf16[8,256,2048]{2,1,0:T(8,128)(2,1)} %bitcast.145, bf16[2048,896]{1,0:T(8,128)(2,1)} %constant_dynamic-update-slice_fusion.weight), custom_call_target="tpu_custom_call" | custom-call | tf_op jit(solution)/shard_map/pallas_call | solution.py:679
  659.8 13.9 %collective-permute-done.22.refs_1_ = bf16[128,2176]{1,0:T(8,128)(2,1)S(1)} collective-permute-done((bf16[128,2176]{1,0:T(8,128)(2,1)S(1)}, bf16[128,2176]{1,0:T(8,128)(2,1)S(1)}, u32[]{:S(2)}, u32[]{:S(2)}) %collective-permute-start.22) | collective-permute-done | bytes 557088 | tf_op jit(solution)/shard_map/ppermute | solution.py:786
  713.3 16.8 %shard_map.192 = (bf16[8,128,768]{2,1,0:T(8,128)(2,1)}, f32[2,128]{1,0:T(2,128)S(1)}) custom-call(f32[8,2,128,768]{3,2,1,0:T(8,128)} %bitcast.149, f32[2,1024,128]{2,1,0:T(8,128)S(1)} %copy-done.2, f32[2,1024,128]{2,1,0:T(8,128)S(1)} %copy-done.1, s32[2,1024,1]{2,1,0:T(8,128)S(1)} %copy-done.4, s32[2,1,1024]{2,1,0:T(1,128)S(1)} %copy-done.24, ...), custom_call_target="tpu_custom_call" | custom-call | tf_op jit(solution)/shard_map/pallas_call | solution.py:220
  736.9 13.9 %shard_map.193 = (bf16[1024,2048]{1,0:T(8,128)(2,1)}, f32[1,2048]{1,0:T(1,128)S(1)}) custom-call(bf16[8,128,768]{2,1,0:T(8,128)(2,1)S(1)} %copy-done.10, bf16[8,256,2048]{2,1,0:T(8,128)(2,1)} %bitcast.146, bf16[2048,896]{1,0:T(8,128)(2,1)} %constant_dynamic-update-slice_fusion.weight), custom_call_target="tpu_custom_call" | custom-call | tf_op jit(solution)/shard_map/pallas_call | solution.py:679
  774.9 17.2 %collective-permute-done.25 = bf16[192,2048]{1,0:T(8,128)(2,1)} collective-permute-done((bf16[192,2048]{1,0:T(8,128)(2,1)}, bf16[192,2048]{1,0:T(8,128)(2,1)}, u32[]{:S(2)}, u32[]{:S(2)}) %collective-permute-start.25) | collective-permute-done | bytes 786464 | tf_op jit(solution)/shard_map/ppermute | solution.py:734
  818.2 40.2 %collective-permute-done.29 = bf16[2,2,128,2048]{3,2,1,0:T(8,128)(2,1)} collective-permute-done((bf16[2,2,128,2048]{3,2,1,0:T(8,128)(2,1)}, bf16[2,2,128,2048]{3,2,1,0:T(8,128)(2,1)}, u32[]{:S(2)}, u32[]{:S(2)}) %collective-permute-start.29) | collective-permute-done | bytes 2097184 | tf_op jit(solution)/shard_map/ppermute | solution.py:918
  885.6 19.5 %collective-permute-done.30 = bf16[1,2,128,2048]{3,2,1,0:T(8,128)(2,1)} collective-permute-done((bf16[1,2,128,2048]{3,2,1,0:T(8,128)(2,1)}, bf16[1,2,128,2048]{3,2,1,0:T(8,128)(2,1)}, u32[]{:S(2)}, u32[]{:S(2)}) %collective-permute-start.30) | collective-permute-done | bytes 1048608 | tf_op jit(solution)/shard_map/ppermute | solution.py:918
  929.9 22.9 %collective-permute-done.35 = bf16[64,2048]{1,0:T(8,128)(2,1)} collective-permute-done((bf16[64,2048]{1,0:T(8,128)(2,1)}, bf16[64,2048]{1,0:T(8,128)(2,1)}, u32[]{:S(2)}, u32[]{:S(2)}) %collective-permute-start.35) | collective-permute-done | bytes 262176 | tf_op jit(solution)/shard_map/ppermute | solution.py:734
  (316 shorter events, 331.5 us)
Async XLA Ops:
  7.2 116.3 %all-gather.9.cloned.1.call-start = ((), (), s32[]{:S(2)}) async-start(), calls=%async_computation.15 | async-start | bytes 9437184 | tf_op jit(solution)/shard_map/all_gather | solution.py:792
  18.6 181.5 %all-gather.11.cloned.1.call-start = ((), (), s32[]{:S(2)}) async-start(), calls=%async_computation.16 | async-start | bytes 9437184 | tf_op jit(solution)/shard_map/all_gather | solution.py:792
  52.4 281.8 %all-gather.15.cloned.1.call-start = ((), (), s32[]{:S(2)}) async-start(), calls=%async_computation.18 | async-start | bytes 18874368 | tf_op jit(solution)/shard_map/all_gather | solution.py:792
  123.5 85.6 %collective-permute-start.7 = (bf16[512,2048]{1,0:T(8,128)(2,1)}, bf16[512,2048]{1,0:T(8,128)(2,1)}, u32[]{:S(2)}, u32[]{:S(2)}) collective-permute-start(bf16[512,2048]{1,0:T(8,128)(2,1)} %get-tuple-element.246), channel_id=1, source_target_pairs={{0,8},{8,16},{16,24},{24,0},{1,9},{9,17},{17,25},{25,1},{2,10},{10... | collective-permute-start | bytes 6291464 | tf_op jit(solution)/shard_map/ppermute | solution.py:734
  123.6 89.5 %collective-permute-start.8 = (bf16[512,2048]{1,0:T(8,128)(2,1)}, bf16[512,2048]{1,0:T(8,128)(2,1)}, u32[]{:S(2)}, u32[]{:S(2)}) collective-permute-start(bf16[512,2048]{1,0:T(8,128)(2,1)} %get-tuple-element.247), channel_id=1, source_target_pairs={{0,24},{8,0},{16,8},{24,16},{1,25},{9,1},{17,9},{25,17},{2,26},{10... | collective-permute-start | bytes 6291464 | tf_op jit(solution)/shard_map/ppermute | solution.py:734
  172.6 161.5 %all-gather.13.cloned.1.call-start = ((), (), s32[]{:S(2)}) async-start(), calls=%async_computation.17 | async-start | bytes 20054016 | tf_op jit(solution)/shard_map/all_gather | solution.py:792
  239.3 339.0 %reduce-scatter.6.cloned.1.call-start = ((), (), s32[]{:S(2)}) async-start(), calls=%async_computation.10 | async-start | bytes 10027008 | tf_op jit(solution)/shard_map/reduce_scatter | solution.py:886
  239.3 91.0 %collective-permute-start.10 = (bf16[512,2048]{1,0:T(8,128)(2,1)}, bf16[512,2048]{1,0:T(8,128)(2,1)}, u32[]{:S(2)}, u32[]{:S(2)}) collective-permute-start(bf16[512,2048]{1,0:T(8,128)(2,1)} %get-tuple-element.258), channel_id=1, source_target_pairs={{0,16},{8,24},{16,0},{24,8},{1,17},{9,25},{17,1},{25,9},{2,18},{10... | collective-permute-start | bytes 6291464 | tf_op jit(solution)/shard_map/ppermute | solution.py:734
  330.3 65.2 %collective-permute-start.11 = (bf16[256,2048]{1,0:T(8,128)(2,1)}, bf16[256,2048]{1,0:T(8,128)(2,1)}, u32[]{:S(2)}, u32[]{:S(2)}) collective-permute-start(bf16[256,2048]{1,0:T(8,128)(2,1)} %get-tuple-element.276), channel_id=1, source_target_pairs={{0,8},{8,16},{16,24},{24,0},{1,9},{9,17},{17,25},{25,1},{2,10},{10... | collective-permute-start | bytes 3145736 | tf_op jit(solution)/shard_map/ppermute | solution.py:734
  330.3 72.2 %collective-permute-start.12 = (bf16[256,2048]{1,0:T(8,128)(2,1)}, bf16[256,2048]{1,0:T(8,128)(2,1)}, u32[]{:S(2)}, u32[]{:S(2)}) collective-permute-start(bf16[256,2048]{1,0:T(8,128)(2,1)} %get-tuple-element.277), channel_id=1, source_target_pairs={{0,16},{8,24},{16,0},{24,8},{1,17},{9,25},{17,1},{25,9},{2,18},{10... | collective-permute-start | bytes 3145736 | tf_op jit(solution)/shard_map/ppermute | solution.py:734
  331.2 71.4 %collective-permute-start.13 = (bf16[256,2048]{1,0:T(8,128)(2,1)}, bf16[256,2048]{1,0:T(8,128)(2,1)}, u32[]{:S(2)}, u32[]{:S(2)}) collective-permute-start(bf16[256,2048]{1,0:T(8,128)(2,1)} %get-tuple-element.278), channel_id=1, source_target_pairs={{0,24},{8,0},{16,8},{24,16},{1,25},{9,1},{17,9},{25,17},{2,26},{10... | collective-permute-start | bytes 3145736 | tf_op jit(solution)/shard_map/ppermute | solution.py:734
  402.5 85.5 %collective-permute-start.14 = (bf16[256,2048]{1,0:T(8,128)(2,1)}, bf16[256,2048]{1,0:T(8,128)(2,1)}, u32[]{:S(2)}, u32[]{:S(2)}) collective-permute-start(bf16[256,2048]{1,0:T(8,128)(2,1)} %get-tuple-element.290), channel_id=1, source_target_pairs={{0,8},{8,16},{16,24},{24,0},{1,9},{9,17},{17,25},{25,1},{2,10},{10... | collective-permute-start | bytes 3145736 | tf_op jit(solution)/shard_map/ppermute | solution.py:734
  486.5 170.7 %reduce-scatter.8.cloned.1.call-start = ((), (), s32[]{:S(2)}) async-start(), calls=%async_computation.11 | async-start | bytes 10027008 | tf_op jit(solution)/shard_map/reduce_scatter | solution.py:886
  486.6 82.9 %collective-permute-start.16 = (bf16[256,2048]{1,0:T(8,128)(2,1)}, bf16[256,2048]{1,0:T(8,128)(2,1)}, u32[]{:S(2)}, u32[]{:S(2)}) collective-permute-start(bf16[256,2048]{1,0:T(8,128)(2,1)} %copy-done.29), channel_id=1, source_target_pairs={{0,16},{8,24},{16,0},{24,8},{1,17},{9,25},{17,1},{25,9},{2,18},{10... | collective-permute-start | bytes 3145736 | tf_op jit(solution)/shard_map/ppermute | solution.py:734
  590.7 51.2 %collective-permute-start.21 = (bf16[512,2048]{1,0:T(8,128)(2,1)}, bf16[512,2048]{1,0:T(8,128)(2,1)}, u32[]{:S(2)}, u32[]{:S(2)}) collective-permute-start(bf16[512,2048]{1,0:T(8,128)(2,1)} %get-tuple-element.322), channel_id=1, source_target_pairs={{0,24},{8,0},{16,8},{24,16},{1,25},{9,1},{17,9},{25,17},{2,26},{10... | collective-permute-start | bytes 6291464 | tf_op jit(solution)/shard_map/ppermute | solution.py:734
  608.9 126.6 %reduce-scatter.10.cloned.1.call-start = ((), (), s32[]{:S(2)}) async-start(), calls=%async_computation.12 | async-start | bytes 4718592 | tf_op jit(solution)/shard_map/reduce_scatter | solution.py:999
  691.9 179.7 %reduce-scatter.12.cloned.1.call-start = ((), (), s32[]{:S(2)}) async-start(), calls=%async_computation.13 | async-start | bytes 4718592 | tf_op jit(solution)/shard_map/reduce_scatter | solution.py:999
  750.8 166.2 %reduce-scatter.14.cloned.1.call-start = ((), (), s32[]{:S(2)}) async-start(), calls=%async_computation.14 | async-start | bytes 9437184 | tf_op jit(solution)/shard_map/reduce_scatter | solution.py:980
  792.2 84.6 %collective-permute-start.26 = (bf16[512,896]{1,0:T(8,128)(2,1)}, bf16[512,896]{1,0:T(8,128)(2,1)}, u32[]{:S(2)}, u32[]{:S(2)}) collective-permute-start(bf16[512,896]{1,0:T(8,128)(2,1)} %get-tuple-element.382), channel_id=1, source_target_pairs={{0,8},{8,16},{16,24},{24,0},{1,9},{9,17},{17,25},{25,1},{2,10},{10... | collective-permute-start | bytes 2752520 | tf_op jit(solution)/shard_map/ppermute | solution.py:734
  792.2 84.6 %collective-permute-start.27 = (bf16[512,896]{1,0:T(8,128)(2,1)S(1)}, bf16[512,896]{1,0:T(8,128)(2,1)}, u32[]{:S(2)}, u32[]{:S(2)}) collective-permute-start(bf16[512,896]{1,0:T(8,128)(2,1)S(1)} %get-tuple-element.383), channel_id=1, source_target_pairs={{0,16},{8,24},{16,0},{24,8},{1,17},{9,25},{17,1},{25,9},{2,18},{10... | collective-permute-start | bytes 2752520 | tf_op jit(solution)/shard_map/ppermute | solution.py:734
  795.4 81.4 %collective-permute-start.28 = (bf16[512,896]{1,0:T(8,128)(2,1)}, bf16[512,896]{1,0:T(8,128)(2,1)}, u32[]{:S(2)}, u32[]{:S(2)}) collective-permute-start(bf16[512,896]{1,0:T(8,128)(2,1)} %get-tuple-element.384), channel_id=1, source_target_pairs={{0,24},{8,0},{16,8},{24,16},{1,25},{9,1},{17,9},{25,17},{2,26},{10... | collective-permute-start | bytes 2752520 | tf_op jit(solution)/shard_map/ppermute | solution.py:734
  797.8 60.7 %collective-permute-start.29 = (bf16[2,2,128,2048]{3,2,1,0:T(8,128)(2,1)}, bf16[2,2,128,2048]{3,2,1,0:T(8,128)(2,1)}, u32[]{:S(2)}, u32[]{:S(2)}) collective-permute-start(bf16[2,2,128,2048]{3,2,1,0:T(8,128)(2,1)} %dynamic-slice_bitcast_fusion.1), channel_id=1, source_target_pairs={{0,2},{1,3},{2,0},{3,1},{4,6},{5,7},{6,4},{7,5},{8,10},{9,11},{10,... | collective-permute-start | bytes 6291464 | tf_op jit(solution)/shard_map/ppermute | solution.py:918
  802.4 64.3 %collective-permute-start.31 = (bf16[2,2,128,2048]{3,2,1,0:T(8,128)(2,1)}, bf16[2,2,128,2048]{3,2,1,0:T(8,128)(2,1)}, u32[]{:S(2)}, u32[]{:S(2)}) collective-permute-start(bf16[2,2,128,2048]{3,2,1,0:T(8,128)(2,1)} %dynamic-slice_bitcast_fusion), channel_id=1, source_target_pairs={{0,4},{1,5},{2,6},{3,7},{4,0},{5,1},{6,2},{7,3},{8,12},{9,13},{10,... | collective-permute-start | bytes 6291464 | tf_op jit(solution)/shard_map/ppermute | solution.py:918
  881.4 48.5 %all-to-all-start.4 = ((bf16[8,64,896]{2,1,0:T(8,128)(2,1)}), bf16[8,64,896]{2,1,0:T(8,128)(2,1)S(1)}, u32[]{:S(2)}, u32[]{:S(2)}) async-start(bf16[8,64,896]{2,1,0:T(8,128)(2,1)} %bitcast.48), calls=%async_computation.8 | async-start | bytes 1835008 | tf_op jit(solution)/shard_map/all_to_all | solution.py:1070
  (82 other events, 2254.6 us)
Sparse Core Ops, SparseCore 0:
  9.9 64.3 all-gather.8
  76.2 54.3 all-gather.10
  132.5 101.0 all-gather.14
  239.4 92.3 all-gather.12
  486.7 72.3 reduce-scatter.5
  562.5 79.3 reduce-scatter.7
  657.4 50.9 reduce-scatter.9
  750.9 52.8 reduce-scatter.11
  807.3 109.7 reduce-scatter.13

commit v10 on v9

--- a/solution.py
+++ b/solution.py
@@ -287,7 +287,7 @@
     planes = len(pieces)
     rows = target.shape[0] // planes
     return [
-        (piece, target.at[pl.ds((plane + planes - step) % planes * rows, rows)])
+        (piece, target.at[pl.ds(lax.bitwise_xor(plane, jnp.int32(step)) * rows, rows)])
         for step, piece in enumerate(pieces)
     ]
 
@@ -298,7 +298,9 @@
     return [
         (
             gathered.at[rank, pl.ds(step * rows, rows)],
-            target.at[pl.ds(((plane + planes - step) % planes * ranks + rank) * rows, rows)],
+            target.at[
+                pl.ds((lax.bitwise_xor(plane, jnp.int32(step)) * ranks + rank) * rows, rows)
+            ],
         )
         for rank in range(ranks)
         for step in range(planes)
@@ -568,7 +570,7 @@
     whole = columns + sum(value.shape[1] for value in tails)
 
     def of_plane(i, where):
-        return (where[1] + first + i) % planes
+        return lax.bitwise_xor(where[1], jnp.int32(first + i))
 
     def kernel(where, left, *refs):
         rights, tails, targets = refs[:parts], refs[parts:-steps], refs[-steps:]
@@ -734,6 +736,10 @@
     return lax.ppermute(value, "rep", [(i, (i + step) % count) for i in range(count)])
 
 
+def cross_rep(value, bits):
+    return lax.ppermute(value, "rep", [(i, i ^ bits) for i in range(lax.axis_size("rep"))])
+
+
 def after(value, *others):
     return lax.optimization_barrier((value,) + others)[0]
 
@@ -741,10 +747,6 @@
 def two_parts(value):
     high = lax.reduce_precision(value, 8, 7)
     return high.astype(bf16), (value - high).astype(bf16)
-
-
-def shift_order(count):
-    return sorted(range(1, count), key=lambda step: (min(step, count - step), step))
 
 
 def ring_rep(value, *work):
@@ -791,20 +793,21 @@
     def gather_ranks(value):
         return lax.all_gather(value, "ep", axis=0)
 
-    order = shift_order(planes)
+    assert planes & (planes - 1) == 0 and share & (share - 1) == 0
+    near, half, last_step = 1, planes // 2, planes - 1
     in_parts, out_parts = (
         {
-            step: lax.dynamic_index_in_dim(weight, (own + step) % share, 0, keepdims=False)
-            for step in [0] + order
+            step: lax.dynamic_index_in_dim(weight, own ^ step % share, 0, keepdims=False)
+            for step in range(planes)
         }
         for weight in (w_in, w_out)
     )
 
     def send(parts, steps):
-        return {step: shift_rep(parts[step], step) for step in steps}
+        return {step: cross_rep(parts[step], step) for step in steps}
 
     stream = gather_ranks(tokens)
-    out_rows = [w_o] + [shift_rep(w_o, step) for step in range(1, planes)]
+    out_rows = [w_o] + [cross_rep(w_o, step) for step in range(1, planes)]
     upstream_group = with_group(cotangent)
     slab = cut_heads(
         w_qkv,
@@ -834,7 +837,7 @@
     in_parts, out_parts, upstream_group, stream = after(
         (in_parts, out_parts, upstream_group, stream), slab
     )
-    in_pieces = {0: in_parts[0], **send(in_parts, order[:-1])}
+    in_pieces = {0: in_parts[0], **send(in_parts, range(last_step - 1, 0, -1))}
     upstream_all = gather_ranks(upstream_group)
 
     normed, proj = project(stream, first_gain, slab)
@@ -849,9 +852,9 @@
     payload, in_pieces = lax.optimization_barrier((payload, in_pieces))
     payload = with_group(payload)
     payload, in_parts, out_parts = lax.optimization_barrier((payload, in_parts, out_parts))
-    in_pieces.update(send(in_parts, order[-1:]))
+    in_pieces.update(send(in_parts, [last_step]))
     in_pieces, out_parts = lax.optimization_barrier((in_pieces, out_parts))
-    out_pieces = {0: out_parts[0], **send(out_parts, order)}
+    out_pieces = {0: out_parts[0], **send(out_parts, range(1, planes))}
     in_pieces = [in_pieces[step] for step in range(planes)]
     out_pieces = [out_pieces[step] for step in range(planes)]
     payload = gather_ranks(payload)
@@ -872,13 +875,13 @@
         ]
         return jnp.stack(
             [
-                sum(jnp.where((own - step) % share == j, sums[step], 0.0) for step in range(share))
+                sum(jnp.where(own ^ step == j, sums[step], 0.0) for step in range(share))
                 for j in range(share)
             ]
         )
 
     tail, out_cut, out_pieces = lax.optimization_barrier((tail, out_cut, out_pieces))
-    out_sent = send(out_cut, order)
+    out_sent = send(out_cut, range(1, planes))
     back = []
     returned = []
 
@@ -897,22 +900,26 @@
         )
         returned.append(scatter_ranks(back[step][2]))
         if step == 0:
-            short = {near: out_sent[near] for near in order[:2]}
-            tail, short = after((tail, short), back[step][2])
-            out_sent.update(short)
+            ended = {bits: out_sent[bits] for bits in (near, last_step)}
+            tail, ended = after((tail, ended), back[step][2])
+            out_sent.update(ended)
         else:
             tail = after(tail, back[step][2])
     rows_in = after(rows_in, tail)
     rows_flat = rows_in.reshape(in_rows, D)
     grads_flat = [back[step][3].reshape(in_rows // micro, 2 * FF) for step in range(micro)]
-    near = weight_gradient(where, planes, rows_flat, grads_flat, first=order[0], steps=1)
-    rows_flat, near = lax.optimization_barrier((rows_flat, near))
-    far = weight_gradient(
-        where, planes, rows_flat, grads_flat, first=order[0] + 1, steps=planes - 1
-    )
-    in_cut = {(order[0] + 1 + i) % planes: part for i, part in enumerate(far)}
-    in_cut[order[0]], = near
-    in_sent = send(in_cut, order[:1])
+    (in_last,) = weight_gradient(
+        where, planes, rows_flat, grads_flat, first=last_step, steps=1
+    )
+    rows_flat, in_last = lax.optimization_barrier((rows_flat, in_last))
+    in_cut = weight_gradient(where, planes, rows_flat, grads_flat, steps=last_step)
+
+    def cuts(value, *places):
+        ends = [-(-value.shape[0] * place // 512) * 16 for place in (0, *places, 32)]
+        return [value[start:end] for start, end in zip(ends, ends[1:])]
+
+    in_last = cuts(in_last, 11, 19, 26)
+    last_sent = [cross_rep(in_last[0], last_step)]
 
     def swap(value, step):
         return lax.ppermute(value, "ep", [(i, i ^ step) for i in range(ranks)])
@@ -944,23 +951,24 @@
 
     grad_inputs, branches, logit_grads, grad_projs = [], [], [], []
     gain_two_sum = gain_one_sum = qk_sum = 0.0
-    in_cut, out_sent, in_sent = lax.optimization_barrier((in_cut, out_sent, in_sent))
+    in_cut, out_sent, last_sent, in_last = lax.optimization_barrier(
+        (in_cut, out_sent, last_sent, in_last)
+    )
     mixtures = [part[:2] for part in back]
-    releases = [order[1:-1]] + [[]] * (micro - 1)
     for step in range(micro):
         at = slice(step * rows, (step + 1) * rows)
         parts = after(returned[step], [one[1] for one in grad_inputs])
-        parts, in_sent = lax.optimization_barrier((parts, in_sent))
+        parts, last_sent = lax.optimization_barrier((parts, last_sent))
         parts = exchange_back(parts)
-        parts, in_cut, mixtures = lax.optimization_barrier((parts, in_cut, mixtures))
+        parts, in_cut, mixtures, in_last = lax.optimization_barrier(
+            (parts, in_cut, mixtures, in_last)
+        )
         if step == 0:
             mixtures = [pair_sum(*part) for part in mixtures]
-        in_sent.update(send(in_cut, releases[step]))
+            last_sent.append(cross_rep(in_last[1], last_step))
         if step == micro - 1:
-            last = in_cut[order[-1]]
-            ends = [-(-last.shape[0] * eighths // 128) * 16 for eighths in (0, 3, 5, 8)]
-            last = [last[start:end] for start, end in zip(ends, ends[1:])]
-            last_sent = [shift_rep(last[0], order[-1])]
+            rest = [cuts(value, 12, 20) for value in in_cut[1:]]
+            rest_sent = [[cross_rep(part[0], i + 1) for i, part in enumerate(rest)]]
         grad_hidden, grad_branch, grad_mixed, grad_logits, gain_two = hidden_backward(
             where[1:2], planes, parts, hidden[at], gates[at], cotangent[at], second_gain,
             router, gathered, experts,
@@ -972,22 +980,30 @@
             out_sum = dot(mixed, jnp.concatenate(branches, axis=0), ((0,), (0,))).astype(bf16)
             out_sum = out_sum.reshape(planes, ranks, dense_rows, D).transpose(1, 0, 2, 3)
         grad_mixed = lax.all_to_all(grad_mixed, "ep", split_axis=1, concat_axis=0, tiled=True)
-        grad_mixed, mixtures = lax.optimization_barrier((grad_mixed, mixtures))
+        grad_mixed, mixtures, last_sent, in_last = lax.optimization_barrier(
+            (grad_mixed, mixtures, last_sent, in_last)
+        )
+        if step == 0:
+            last_sent.append(cross_rep(in_last[2], last_step))
         if step == micro - 1:
-            grad_mixed, mixtures, last_sent, last, out_sum = lax.optimization_barrier(
-                (grad_mixed, mixtures, last_sent, last, out_sum)
+            grad_mixed, mixtures, rest_sent, rest, out_sum = lax.optimization_barrier(
+                (grad_mixed, mixtures, rest_sent, rest, out_sum)
             )
             out_sum = lax.psum_scatter(out_sum, "ep", scatter_dimension=0)
-            last_sent.append(shift_rep(last[1], order[-1]))
+            rest_sent.append([cross_rep(part[1], i + 1) for i, part in enumerate(rest)])
         grad_proj, grad_qk = attention_backward(
             step, proj, *tables, query, keys, values, lses, grad_mixed
         )
         qk_sum = qk_sum + grad_qk.reshape(-1)
         if step < micro - 1:
-            grad_proj, in_sent = lax.optimization_barrier((grad_proj, in_sent))
+            grad_proj, last_sent, in_last = lax.optimization_barrier(
+                (grad_proj, last_sent, in_last)
+            )
+            if step == 0:
+                last_sent.append(cross_rep(in_last[3], last_step))
         else:
-            grad_proj, grad_inputs, last_sent, last = lax.optimization_barrier(
-                (grad_proj, grad_inputs, last_sent, last)
+            grad_proj, grad_inputs, rest_sent, rest = lax.optimization_barrier(
+                (grad_proj, grad_inputs, rest_sent, rest)
             )
         grad_projs.append(grad_proj)
         grad_normed, gain_one = project_backward(step, grad_proj, stream, slab)
@@ -1020,10 +1036,10 @@
     def joined(value):
         return value[..., :count].astype(f32) + value[..., count : 2 * count].astype(f32)
 
-    grad_projs, last, out_cut, out_sent, _ = lax.optimization_barrier(
-        (grad_projs, last, out_cut, out_sent, grad_normed)
-    )
-    last_sent.append(shift_rep(last[2], order[-1]))
+    grad_projs, rest, out_cut, out_sent, _ = lax.optimization_barrier(
+        (grad_projs, rest, out_cut, out_sent, grad_normed)
+    )
+    rest_sent.append([cross_rep(part[2], i + 1) for i, part in enumerate(rest)])
     packed = weight_gradient(
         where,
         planes,
@@ -1031,10 +1047,10 @@
         [jnp.stack(grad_projs, axis=1).reshape(ranks * mine, 3 * width)],
         halves(small),
     )
-    packed, last_sent, out_cut, out_sent, mixtures = lax.optimization_barrier(
-        (packed, last_sent, out_cut, out_sent, mixtures)
-    )
-    packed_sent = [packed[0]] + [shift_rep(packed[step], step) for step in range(1, planes)]
+    packed, rest_sent, out_cut, out_sent, mixtures = lax.optimization_barrier(
+        (packed, rest_sent, out_cut, out_sent, mixtures)
+    )
+    packed_sent = [packed[0]] + [cross_rep(packed[step], step) for step in range(1, planes)]
     for phase in range(len(bits)):
         crossed = halve(mixtures, phase)
         if phase < len(bits) - 1:
@@ -1059,9 +1075,7 @@
         mixture.append((parts[0], exchange_back(parts.astype(bf16))[1:]))
     own_sum = lax.dynamic_index_in_dim(out_sum, plane, 0, keepdims=False)
     out_sent_back = [
-        shift_rep(
-            lax.dynamic_index_in_dim(out_sum, (plane + step) % planes, 0, keepdims=False), step
-        )
+        cross_rep(lax.dynamic_index_in_dim(out_sum, plane ^ step, 0, keepdims=False), step)
         for step in range(1, planes)
     ]
     main = total([part[:, : 3 * width] for part in packed_sent]).astype(bf16)
@@ -1074,7 +1088,11 @@
     grad_w_o = total([own_sum, *out_sent_back])
     grad_w_qkv, small = unpack(packed, count)
     grad_w_out = sum_rep({0: out_cut[0], **out_sent})
-    in_sent[order[-1]] = jnp.concatenate(last_sent, axis=0)
+    in_sent = {
+        i + 1: jnp.concatenate([parts[i] for parts in rest_sent], axis=0)
+        for i in range(planes - 2)
+    }
+    in_sent[last_step] = jnp.concatenate(last_sent, axis=0)
     grad_w_in = sum_rep({0: in_cut[0], **in_sent})
     return (
         output,

time: 987 us -> 1010 us (1.023)
  starting transfers between devices: 106 us -> 162 us
  waiting for transfers between devices: 389 us -> 349 us
    ppermute x26 -> x3, waiting for transfers between devices: 219 us -> 50.7 us  [shift_rep(): lax.ppermute(value, 'rep', [(i, (i + step) % count) for i in range(count)])]
    ppermute x0 -> x28, waiting for transfers between devices: none -> 146 us  [cross_rep(): lax.ppermute(value, 'rep', [(i, i ^ bits) for i in range(lax.axis_size('r...]
    ppermute x0 -> x28, starting transfers between devices: none -> 91.7 us  [cross_rep(): lax.ppermute(value, 'rep', [(i, i ^ bits) for i in range(lax.axis_size('r...]
    ppermute x26 -> x3, starting transfers between devices: 69.8 us -> 0.06 us  [shift_rep(): lax.ppermute(value, 'rep', [(i, (i + step) % count) for i in range(count)])]
    ppermute x6, starting transfers between devices: 6.26 us -> 43.7 us  [exchange(): return lax.ppermute(value, 'rep', pairs)]
  transfers between devices with their start and end apart: 52 -> 57, of which waited for: 23 -> 28; matrix products, arithmetic and copies ran while one was open for 12% -> 13% of each run, Pallas kernels for 31% -> 30%
where the time goes in v10:
time: 1010 us; the launch traced here: 1000 us
  waiting for transfers between devices  349 us (35%)
  Pallas kernels  320 us (32%)
  starting transfers between devices  162 us (16%)
  local copies, waits for them, and re-layouts  73.9 us (7%)
  other arithmetic  72.3 us (7%)
  between operations  14.9 us (1%)
    ppermute x28, waiting for transfers between devices, cross_rep(): lax.ppermute(value, 'rep', [(i, i ^ bits) for i in range(lax.axis_size('r...  146 us
    ppermute x28, starting transfers between devices, cross_rep(): lax.ppermute(value, 'rep', [(i, i ^ bits) for i in range(lax.axis_size('r...  91.7 us
    pallas_call x2, Pallas kernels, expert_backward(): pl.pallas_call(kernel, grid_spec=pltpu.PrefetchScalarGridSpec(num_scalar_...  85.1 us
    pallas_call x4, Pallas kernels, weight_gradient(): pl.pallas_call(kernel, grid_spec=pltpu.PrefetchScalarGridSpec(num_scalar_...  65.2 us
    ppermute x6, waiting for transfers between devices, exchange(): return lax.ppermute(value, 'rep', pairs)  60.7 us
    ppermute x6, waiting for transfers between devices, swap(): return lax.ppermute(value, 'ep', [(i, i ^ step) for i in range(ranks)])  54.5 us
    ppermute x3, waiting for transfers between devices, shift_rep(): lax.ppermute(value, 'rep', [(i, (i + step) % count) for i in range(count)])  50.7 us
    ppermute x6, starting transfers between devices, exchange(): return lax.ppermute(value, 'rep', pairs)  43.7 us
  transfers between devices with their start and end apart: 57, of which 28 were waited for; matrix products, arithmetic and copies ran while one was open for 13% of the time, Pallas kernels for 30%

profile of v10, /device:TPU:0, one launch (start us, length us, event | category | flops | bytes accessed | tf_op | source)
XLA Modules:
  0.0 1002.7 jit_solution(6199559114355535137)
XLA Ops:
  23.1 17.8 %collective-permute-done.3 = bf16[256,2048]{1,0:T(8,128)(2,1)} collective-permute-done((bf16[256,2048]{1,0:T(8,128)(2,1)}, bf16[256,2048]{1,0:T(8,128)(2,1)}, u32[]{:S(2)}, u32[]{:S(2)}) %collective-permute-start.3) | collective-permute-done | bytes 1048608 | tf_op jit(solution)/shard_map/ppermute | solution.py:788
  56.3 22.5 %collective-permute-done.4 = bf16[512,896]{1,0:T(8,128)(2,1)S(1)} collective-permute-done((bf16[512,896]{1,0:T(8,128)(2,1)S(1)}, bf16[512,896]{1,0:T(8,128)(2,1)S(1)}, u32[]{:S(2)}, u32[]{:S(2)}) %collective-permute-start.4) | collective-permute-done | bytes 917536 | tf_op jit(solution)/shard_map/ppermute | solution.py:736
  107.6 16.8 %collective-permute-done.6 = bf16[512,896]{1,0:T(8,128)(2,1)S(1)} collective-permute-done((bf16[512,896]{1,0:T(8,128)(2,1)}, bf16[512,896]{1,0:T(8,128)(2,1)S(1)}, u32[]{:S(2)}, u32[]{:S(2)}) %collective-permute-start.6) | collective-permute-done | bytes 917536 | tf_op jit(solution)/shard_map/ppermute | solution.py:736
  128.7 14.9 %shard_map.179 = (bf16[8,256,2048]{2,1,0:T(8,128)(2,1)}, f32[8,256,768]{2,1,0:T(8,128)}) custom-call(bf16[8,256,2048]{2,1,0:T(8,128)(2,1)} %bitcast.136, f32[1,2048]{1,0:T(1,128)S(1)} %broadcast_in_dim.56.gain, bf16[2048,896]{1,0:T(8,128)(2,1)} %constant_dynamic-update-slice_fusion.weight), custom_call_target="tpu_custom_call" | custom-call | tf_op jit(solution)/shard_map/pallas_call | solution.py:247
  143.6 22.1 %shard_map.180 = (bf16[8,2,128,256]{3,2,1,0:T(8,128)(2,1)}, bf16[2,1024,256]{2,1,0:T(8,128)(2,1)S(1)}, bf16[2,1024,256]{2,1,0:T(8,128)(2,1)S(1)}, bf16[2,1024,256]{2,1,0:T(8,128)(2,1)}, f32[2,2,1024,1]{3,2,1,0:T(8,128)}) custom-call(f32[8,2,128,768]{3,2,1,0:T(8,128)} %bitcast.139, f32[2,1024,128]{2,1,0:T(8,128)} %get-tuple-element.257.refs_1_, ...), custom_call_target="tpu_custom_call" | custom-call | tf_op jit(solution)/shard_map/pallas_call | solution.py:198
  173.5 24.2 %all-to-all-done.1 = bf16[8,2,128,256]{3,2,1,0:T(8,128)(2,1)S(1)} async-done(((bf16[8,2,128,256]{3,2,1,0:T(8,128)(2,1)}), bf16[8,2,128,256]{3,2,1,0:T(8,128)(2,1)S(1)}, u32[]{:S(2)}, u32[]{:S(2)}) %all-to-all-start.1) | async-done | bytes 1048608 | tf_op jit(solution)/shard_map/all_to_all | solution.py:846
  215.3 23.6 %collective-permute-done.9 = bf16[256,2176]{1,0:T(8,128)(2,1)S(1)} collective-permute-done((bf16[256,2176]{1,0:T(8,128)(2,1)S(1)}, bf16[256,2176]{1,0:T(8,128)(2,1)S(1)}, u32[]{:S(2)}, u32[]{:S(2)}) %collective-permute-start.9) | collective-permute-done | bytes 1114144 | tf_op jit(solution)/shard_map/ppermute | solution.py:788
  240.8 47.8 %collective-permute-done.10.refs_3_ = bf16[512,2048]{1,0:T(8,128)(2,1)} collective-permute-done((bf16[512,2048]{1,0:T(8,128)(2,1)}, bf16[512,2048]{1,0:T(8,128)(2,1)}, u32[]{:S(2)}, u32[]{:S(2)}) %collective-permute-start.10) | collective-permute-done | bytes 2097184 | tf_op jit(solution)/shard_map/ppermute | solution.py:740
  288.5 42.6 %collective-permute-start.11 = (bf16[256,2048]{1,0:T(8,128)(2,1)}, bf16[256,2048]{1,0:T(8,128)(2,1)}, u32[]{:S(2)}, u32[]{:S(2)}) collective-permute-start(bf16[256,2048]{1,0:T(8,128)(2,1)} %get-tuple-element.307), channel_id=1, source_target_pairs={{0,8},{8,0},{16,24},{24,16},{1,9},{9,1},{17,25},{25,17},{2,10},{10... | collective-permute-start | bytes 3145736 | tf_op jit(solution)/shard_map/ppermute | solution.py:740
  333.5 40.4 %shard_map.182 = (bf16[2,4,288,2048]{3,2,1,0:T(8,128)(2,1)}, f32[2,4,288,128]{3,2,1,0:T(8,128)S(1)}, f32[2,4,288,2048]{3,2,1,0:T(8,128)}, bf16[2,4,288,1024]{3,2...) custom-call(s32[3]{0:T(128)S(1)} %pad_add_fusion.where, ...), custom_call_target="tpu_custom_call" | custom-call | flops 241591910400 | tf_op jit(solution)/shard_map/pallas_call | solution.py:431
  375.3 16.9 %shard_map.183 = (bf16[256,2048]{1,0:T(8,128)(2,1)S(1)}, bf16[256,2048]{1,0:T(8,128)(2,1)}, bf16[256,2048]{1,0:T(8,128)(2,1)}, bf16[256,2048]{1,0:T(8,128)(2,1)}) custom-call(s32[3]{0:T(128)S(1)} %pad_add_fusion.where, bf16[2304,1024]{1,0:T(8,128)(2,1)} %bitcast.171, bf16[2304,2048]{1,0:T(8,128)(2,1)} %bitcast.170), custom_call_target="tpu_custom_call" | custom-call | flops 96636764160 | tf_op jit(solution)/shard_map/pallas_call | solution.py:591
  403.4 19.6 %collective-permute-start.14 = (bf16[256,2048]{1,0:T(8,128)(2,1)}, bf16[256,2048]{1,0:T(8,128)(2,1)}, u32[]{:S(2)}, u32[]{:S(2)}) collective-permute-start(bf16[256,2048]{1,0:T(8,128)(2,1)} %get-tuple-element.319), channel_id=1, source_target_pairs={{0,8},{8,0},{16,24},{24,16},{1,9},{9,1},{17,25},{25,17},{2,10},{10... | collective-permute-start | bytes 3145736 | tf_op jit(solution)/shard_map/ppermute | solution.py:740
  424.5 40.9 %shard_map.184 = (bf16[4,2,128,2048]{3,2,1,0:T(8,128)(2,1)}, bf16[4,2,128,2048]{3,2,1,0:T(8,128)(2,1)}, bf16[8,2,128,2176]{3,2,1,0:T(8,128)(2,1)}, bf16[4,288,2048]{2,1,0:T(8,128)(2,1)}) custom-call(s32[3]{0:T(128)S(1)} %pad_add_fusion.where, f32[2,4,288,128]{3,2,1,0:T(8,128)} %copy-done.31, f32[2,4,288,2048]{3,2,1,0:T(8,128)} %get-tuple-element.309.both, ...), custom_call_target="tpu_custom_call" | custom-call | flops 217432719360 | tf_op jit(solution)/shard_map/pallas_call | solution.py:529
  469.8 44.2 %shard_map.185 = (bf16[4,2,128,2048]{3,2,1,0:T(8,128)(2,1)}, bf16[4,2,128,2048]{3,2,1,0:T(8,128)(2,1)}, bf16[8,2,128,2176]{3,2,1,0:T(8,128)(2,1)}, bf16[4,288,2048]{2,1,0:T(8,128)(2,1)}) custom-call(s32[3]{0:T(128)S(1)} %pad_add_fusion.where, f32[2,4,288,128]{3,2,1,0:T(8,128)} %copy-done.31, f32[2,4,288,2048]{3,2,1,0:T(8,128)} %get-tuple-element.309.both, ...), custom_call_target="tpu_custom_call" | custom-call | flops 217432719360 | tf_op jit(solution)/shard_map/pallas_call | solution.py:529
  527.2 24.6 %shard_map.187 = (bf16[512,2048]{1,0:T(8,128)(2,1)S(1)}, bf16[512,2048]{1,0:T(8,128)(2,1)}, bf16[512,2048]{1,0:T(8,128)(2,1)}) custom-call(s32[3]{0:T(128)S(1)} %pad_add_fusion.where, bf16[2304,2048]{1,0:T(8,128)(2,1)} %bitcast.169, bf16[1152,2048]{1,0:T(8,128)(2,1)} %bitcast.173, bf16[1152,2048]{1,0:T(8,128)(2,1)} %bitcast.175), custom_call_target="tpu_custom_call" | custom-call | flops 144955146240 | tf_op jit(solution)/shard_map/pallas_call | solution.py:591
  557.3 18.7 %collective-permute-start.18 = (bf16[128,2176]{1,0:T(8,128)(2,1)S(1)}, bf16[128,2176]{1,0:T(8,128)(2,1)S(1)}, u32[]{:S(2)}, u32[]{:S(2)}) collective-permute-start(bf16[128,2176]{1,0:T(8,128)(2,1)S(1)} %get-tuple-element.550), channel_id=1, source_target_pairs={{0,8},{8,0},{16,24},{24,16},{1,9},{9,1},{17,25},{25,17},{2,10},{10... | collective-permute-start | bytes 1671176 | tf_op jit(solution)/shard_map/ppermute | solution.py:788
  621.5 17.0 %shard_map.189 = (bf16[8,128,768]{2,1,0:T(8,128)(2,1)}, f32[2,128]{1,0:T(2,128)S(1)}) custom-call(f32[8,2,128,768]{3,2,1,0:T(8,128)} %bitcast.140, f32[2,1024,128]{2,1,0:T(8,128)S(1)} %copy-done.2, f32[2,1024,128]{2,1,0:T(8,128)S(1)} %copy-done.1, s32[2,1024,1]{2,1,0:T(8,128)S(1)} %copy-done.3, s32[2,1,1024]{2,1,0:T(1,128)S(1)} %copy-done.25, ...), custom_call_target="tpu_custom_call" | custom-call | tf_op jit(solution)/shard_map/pallas_call | solution.py:220
  640.0 13.9 %shard_map.190 = (bf16[1024,2048]{1,0:T(8,128)(2,1)}, f32[1,2048]{1,0:T(1,128)S(1)}) custom-call(bf16[8,128,768]{2,1,0:T(8,128)(2,1)S(1)} %copy-done.10, bf16[8,256,2048]{2,1,0:T(8,128)(2,1)} %bitcast.137, bf16[2048,896]{1,0:T(8,128)(2,1)} %constant_dynamic-update-slice_fusion.weight), custom_call_target="tpu_custom_call" | custom-call | tf_op jit(solution)/shard_map/pallas_call | solution.py:681
  668.2 18.0 %collective-permute-start.24 = (bf16[128,2176]{1,0:T(8,128)(2,1)S(1)}, bf16[128,2176]{1,0:T(8,128)(2,1)S(1)}, u32[]{:S(2)}, u32[]{:S(2)}) collective-permute-start(bf16[128,2176]{1,0:T(8,128)(2,1)S(1)} %get-tuple-element.548), channel_id=1, source_target_pairs={{0,8},{8,0},{16,24},{24,16},{1,9},{9,1},{17,25},{25,17},{2,10},{10... | collective-permute-start | bytes 1671176 | tf_op jit(solution)/shard_map/ppermute | solution.py:788
  740.9 16.9 %shard_map.192 = (bf16[8,128,768]{2,1,0:T(8,128)(2,1)}, f32[2,128]{1,0:T(2,128)S(1)}) custom-call(f32[8,2,128,768]{3,2,1,0:T(8,128)} %bitcast.141, f32[2,1024,128]{2,1,0:T(8,128)S(1)} %copy-done.2, f32[2,1024,128]{2,1,0:T(8,128)S(1)} %copy-done.1, s32[2,1024,1]{2,1,0:T(8,128)S(1)} %copy-done.4, s32[2,1,1024]{2,1,0:T(1,128)S(1)} %copy-done.25, ...), custom_call_target="tpu_custom_call" | custom-call | tf_op jit(solution)/shard_map/pallas_call | solution.py:220
  765.6 13.9 %shard_map.193 = (bf16[1024,2048]{1,0:T(8,128)(2,1)}, f32[1,2048]{1,0:T(1,128)S(1)}) custom-call(bf16[8,128,768]{2,1,0:T(8,128)(2,1)S(1)} %copy-done.12, bf16[8,256,2048]{2,1,0:T(8,128)(2,1)} %bitcast.138, bf16[2048,896]{1,0:T(8,128)(2,1)} %constant_dynamic-update-slice_fusion.weight), custom_call_target="tpu_custom_call" | custom-call | tf_op jit(solution)/shard_map/pallas_call | solution.py:681
  850.3 35.3 %collective-permute-done.34 = bf16[2,2,128,2048]{3,2,1,0:T(8,128)(2,1)} collective-permute-done((bf16[2,2,128,2048]{3,2,1,0:T(8,128)(2,1)}, bf16[2,2,128,2048]{3,2,1,0:T(8,128)(2,1)}, u32[]{:S(2)}, u32[]{:S(2)}) %collective-permute-start.34) | collective-permute-done | bytes 2097184 | tf_op jit(solution)/shard_map/ppermute | solution.py:925
  909.7 19.2 %collective-permute-done.35 = bf16[1,2,128,2048]{3,2,1,0:T(8,128)(2,1)} collective-permute-done((bf16[1,2,128,2048]{3,2,1,0:T(8,128)(2,1)}, bf16[1,2,128,2048]{3,2,1,0:T(8,128)(2,1)}, u32[]{:S(2)}, u32[]{:S(2)}) %collective-permute-start.35) | collective-permute-done | bytes 1048608 | tf_op jit(solution)/shard_map/ppermute | solution.py:925
  952.7 26.7 %collective-permute-done.40 = bf16[64,2048]{1,0:T(8,128)(2,1)} collective-permute-done((bf16[64,2048]{1,0:T(8,128)(2,1)}, bf16[64,2048]{1,0:T(8,128)(2,1)}, u32[]{:S(2)}, u32[]{:S(2)}) %collective-permute-start.40) | collective-permute-done | bytes 262176 | tf_op jit(solution)/shard_map/ppermute | solution.py:740
  (337 shorter events, 389.1 us)
Async XLA Ops:
  7.2 118.3 %all-gather.9.cloned.1.call-start = ((), (), s32[]{:S(2)}) async-start(), calls=%async_computation.15 | async-start | bytes 9437184 | tf_op jit(solution)/shard_map/all_gather | solution.py:794
  18.6 180.1 %all-gather.11.cloned.1.call-start = ((), (), s32[]{:S(2)}) async-start(), calls=%async_computation.16 | async-start | bytes 9437184 | tf_op jit(solution)/shard_map/all_gather | solution.py:794
  54.5 279.0 %all-gather.15.cloned.1.call-start = ((), (), s32[]{:S(2)}) async-start(), calls=%async_computation.18 | async-start | bytes 18874368 | tf_op jit(solution)/shard_map/all_gather | solution.py:794
  125.5 87.9 %collective-permute-start.7 = (bf16[512,2048]{1,0:T(8,128)(2,1)}, bf16[512,2048]{1,0:T(8,128)(2,1)}, u32[]{:S(2)}, u32[]{:S(2)}) collective-permute-start(bf16[512,2048]{1,0:T(8,128)(2,1)} %get-tuple-element.288), channel_id=1, source_target_pairs={{0,8},{8,0},{16,24},{24,16},{1,9},{9,1},{17,25},{25,17},{2,10},{10... | collective-permute-start | bytes 6291464 | tf_op jit(solution)/shard_map/ppermute | solution.py:740
  125.6 87.9 %collective-permute-start.8 = (bf16[512,2048]{1,0:T(8,128)(2,1)}, bf16[512,2048]{1,0:T(8,128)(2,1)}, u32[]{:S(2)}, u32[]{:S(2)}) collective-permute-start(bf16[512,2048]{1,0:T(8,128)(2,1)} %get-tuple-element.293.refs_0_), channel_id=1, source_target_pairs={{0,16},{8,24},{16,0},{24,8},{1,17},{9,25},{17,1},{25,9},{2,18},{10... | collective-permute-start | bytes 6291464 | tf_op jit(solution)/shard_map/ppermute | solution.py:740
  171.5 162.0 %all-gather.13.cloned.1.call-start = ((), (), s32[]{:S(2)}) async-start(), calls=%async_computation.17 | async-start | bytes 20054016 | tf_op jit(solution)/shard_map/all_gather | solution.py:794
  240.5 315.0 %reduce-scatter.6.cloned.1.call-start = ((), (), s32[]{:S(2)}) async-start(), calls=%async_computation.10 | async-start | bytes 10027008 | tf_op jit(solution)/shard_map/reduce_scatter | solution.py:889
  240.6 47.9 %collective-permute-start.10 = (bf16[512,2048]{1,0:T(8,128)(2,1)}, bf16[512,2048]{1,0:T(8,128)(2,1)}, u32[]{:S(2)}, u32[]{:S(2)}) collective-permute-start(bf16[512,2048]{1,0:T(8,128)(2,1)} %get-tuple-element.288), channel_id=1, source_target_pairs={{0,24},{8,16},{16,8},{24,0},{1,25},{9,17},{17,9},{25,1},{2,26},{10... | collective-permute-start | bytes 6291464 | tf_op jit(solution)/shard_map/ppermute | solution.py:740
  288.5 104.7 %collective-permute-start.11 = (bf16[256,2048]{1,0:T(8,128)(2,1)}, bf16[256,2048]{1,0:T(8,128)(2,1)}, u32[]{:S(2)}, u32[]{:S(2)}) collective-permute-start(bf16[256,2048]{1,0:T(8,128)(2,1)} %get-tuple-element.307), channel_id=1, source_target_pairs={{0,8},{8,0},{16,24},{24,16},{1,9},{9,1},{17,25},{25,17},{2,10},{10... | collective-permute-start | bytes 3145736 | tf_op jit(solution)/shard_map/ppermute | solution.py:740
  331.1 72.3 %collective-permute-start.12 = (bf16[256,2048]{1,0:T(8,128)(2,1)}, bf16[256,2048]{1,0:T(8,128)(2,1)}, u32[]{:S(2)}, u32[]{:S(2)}) collective-permute-start(bf16[256,2048]{1,0:T(8,128)(2,1)} %get-tuple-element.312.refs_4_), channel_id=1, source_target_pairs={{0,16},{8,24},{16,0},{24,8},{1,17},{9,25},{17,1},{25,9},{2,18},{10... | collective-permute-start | bytes 3145736 | tf_op jit(solution)/shard_map/ppermute | solution.py:740
  331.1 72.3 %collective-permute-start.13 = (bf16[256,2048]{1,0:T(8,128)(2,1)}, bf16[256,2048]{1,0:T(8,128)(2,1)}, u32[]{:S(2)}, u32[]{:S(2)}) collective-permute-start(bf16[256,2048]{1,0:T(8,128)(2,1)} %get-tuple-element.307), channel_id=1, source_target_pairs={{0,24},{8,16},{16,8},{24,0},{1,25},{9,17},{17,9},{25,1},{2,26},{10... | collective-permute-start | bytes 3145736 | tf_op jit(solution)/shard_map/ppermute | solution.py:740
  403.4 62.2 %collective-permute-start.14 = (bf16[256,2048]{1,0:T(8,128)(2,1)}, bf16[256,2048]{1,0:T(8,128)(2,1)}, u32[]{:S(2)}, u32[]{:S(2)}) collective-permute-start(bf16[256,2048]{1,0:T(8,128)(2,1)} %get-tuple-element.319), channel_id=1, source_target_pairs={{0,8},{8,0},{16,24},{24,16},{1,9},{9,1},{17,25},{25,17},{2,10},{10... | collective-permute-start | bytes 3145736 | tf_op jit(solution)/shard_map/ppermute | solution.py:740
  423.0 46.8 %collective-permute-start.15 = (bf16[256,2048]{1,0:T(8,128)(2,1)}, bf16[256,2048]{1,0:T(8,128)(2,1)}, u32[]{:S(2)}, u32[]{:S(2)}) collective-permute-start(bf16[256,2048]{1,0:T(8,128)(2,1)} %get-tuple-element.320), channel_id=1, source_target_pairs={{0,24},{8,16},{16,8},{24,0},{1,25},{9,17},{17,9},{25,1},{2,26},{10... | collective-permute-start | bytes 3145736 | tf_op jit(solution)/shard_map/ppermute | solution.py:740
  465.4 190.7 %reduce-scatter.8.cloned.1.call-start = ((), (), s32[]{:S(2)}) async-start(), calls=%async_computation.11 | async-start | bytes 10027008 | tf_op jit(solution)/shard_map/reduce_scatter | solution.py:889
  465.5 90.1 %collective-permute-start.16 = (bf16[256,2048]{1,0:T(8,128)(2,1)}, bf16[256,2048]{1,0:T(8,128)(2,1)}, u32[]{:S(2)}, u32[]{:S(2)}) collective-permute-start(bf16[256,2048]{1,0:T(8,128)(2,1)} %get-tuple-element.328), channel_id=1, source_target_pairs={{0,16},{8,24},{16,0},{24,8},{1,17},{9,25},{17,1},{25,9},{2,18},{10... | collective-permute-start | bytes 3145736 | tf_op jit(solution)/shard_map/ppermute | solution.py:740
  602.0 162.2 %reduce-scatter.10.cloned.1.call-start = ((), (), s32[]{:S(2)}) async-start(), calls=%async_computation.12 | async-start | bytes 4718592 | tf_op jit(solution)/shard_map/reduce_scatter | solution.py:1015
  720.3 176.1 %reduce-scatter.12.cloned.1.call-start = ((), (), s32[]{:S(2)}) async-start(), calls=%async_computation.13 | async-start | bytes 4718592 | tf_op jit(solution)/shard_map/reduce_scatter | solution.py:1015
  779.5 160.8 %reduce-scatter.14.cloned.1.call-start = ((), (), s32[]{:S(2)}) async-start(), calls=%async_computation.14 | async-start | bytes 9437184 | tf_op jit(solution)/shard_map/reduce_scatter | solution.py:992
  821.3 80.1 %collective-permute-start.31 = (bf16[512,896]{1,0:T(8,128)(2,1)}, bf16[512,896]{1,0:T(8,128)(2,1)}, u32[]{:S(2)}, u32[]{:S(2)}) collective-permute-start(bf16[512,896]{1,0:T(8,128)(2,1)} %get-tuple-element.435), channel_id=1, source_target_pairs={{0,8},{8,0},{16,24},{24,16},{1,9},{9,1},{17,25},{25,17},{2,10},{10... | collective-permute-start | bytes 2752520 | tf_op jit(solution)/shard_map/ppermute | solution.py:740
  821.3 80.1 %collective-permute-start.32 = (bf16[512,896]{1,0:T(8,128)(2,1)S(1)}, bf16[512,896]{1,0:T(8,128)(2,1)}, u32[]{:S(2)}, u32[]{:S(2)}) collective-permute-start(bf16[512,896]{1,0:T(8,128)(2,1)S(1)} %get-tuple-element.436), channel_id=1, source_target_pairs={{0,16},{8,24},{16,0},{24,8},{1,17},{9,25},{17,1},{25,9},{2,18},{10... | collective-permute-start | bytes 2752520 | tf_op jit(solution)/shard_map/ppermute | solution.py:740
  823.8 77.7 %collective-permute-start.33 = (bf16[512,896]{1,0:T(8,128)(2,1)}, bf16[512,896]{1,0:T(8,128)(2,1)}, u32[]{:S(2)}, u32[]{:S(2)}) collective-permute-start(bf16[512,896]{1,0:T(8,128)(2,1)} %get-tuple-element.437), channel_id=1, source_target_pairs={{0,24},{8,16},{16,8},{24,0},{1,25},{9,17},{17,9},{25,1},{2,26},{10... | collective-permute-start | bytes 2752520 | tf_op jit(solution)/shard_map/ppermute | solution.py:740
  827.3 58.3 %collective-permute-start.34 = (bf16[2,2,128,2048]{3,2,1,0:T(8,128)(2,1)}, bf16[2,2,128,2048]{3,2,1,0:T(8,128)(2,1)}, u32[]{:S(2)}, u32[]{:S(2)}) collective-permute-start(bf16[2,2,128,2048]{3,2,1,0:T(8,128)(2,1)} %dynamic-slice_bitcast_fusion.1), channel_id=1, source_target_pairs={{0,2},{1,3},{2,0},{3,1},{4,6},{5,7},{6,4},{7,5},{8,10},{9,11},{10,... | collective-permute-start | bytes 6291464 | tf_op jit(solution)/shard_map/ppermute | solution.py:925
  830.2 60.8 %collective-permute-start.36 = (bf16[2,2,128,2048]{3,2,1,0:T(8,128)(2,1)}, bf16[2,2,128,2048]{3,2,1,0:T(8,128)(2,1)}, u32[]{:S(2)}, u32[]{:S(2)}) collective-permute-start(bf16[2,2,128,2048]{3,2,1,0:T(8,128)(2,1)} %dynamic-slice_bitcast_fusion), channel_id=1, source_target_pairs={{0,4},{1,5},{2,6},{3,7},{4,0},{5,1},{6,2},{7,3},{8,12},{9,13},{10,... | collective-permute-start | bytes 6291464 | tf_op jit(solution)/shard_map/ppermute | solution.py:925
  906.2 46.5 %all-to-all-start.4 = ((bf16[8,64,896]{2,1,0:T(8,128)(2,1)}), bf16[8,64,896]{2,1,0:T(8,128)(2,1)S(1)}, u32[]{:S(2)}, u32[]{:S(2)}) async-start(bf16[8,64,896]{2,1,0:T(8,128)(2,1)} %bitcast.44), calls=%async_computation.8 | async-start | bytes 1835008 | tf_op jit(solution)/shard_map/all_to_all | solution.py:1084
  (89 other events, 2517.5 us)
Sparse Core Ops, SparseCore 0:
  9.9 64.3 all-gather.8
  76.8 54.3 all-gather.10
  133.1 100.2 all-gather.14
  240.7 92.3 all-gather.12
  465.5 73.5 reduce-scatter.5
  542.6 80.6 reduce-scatter.7
  654.1 69.8 reduce-scatter.9
  779.6 52.9 reduce-scatter.11
  836.1 104.0 reduce-scatter.13

commit v11 on v10

--- a/solution.py
+++ b/solution.py
@@ -558,7 +558,7 @@
     )
 
 
-def weight_gradient(where, planes, left, rights, tail=None, first=0, steps=None):
+def weight_gradient(where, planes, left, rights, tail=None, first=0, steps=None, shift=False):
     steps = planes if steps is None else steps
     count, width = left.shape
     parts = len(rights)
@@ -570,7 +570,7 @@
     whole = columns + sum(value.shape[1] for value in tails)
 
     def of_plane(i, where):
-        return lax.bitwise_xor(where[1], jnp.int32(first + i))
+        return (where[1] + first + i) % planes if shift else lax.bitwise_xor(where[1], first + i)
 
     def kernel(where, left, *refs):
         rights, tails, targets = refs[:parts], refs[parts:-steps], refs[-steps:]
@@ -868,20 +868,25 @@
         where, planes, active.reshape(in_rows, FF), [grad_produced.reshape(in_rows, D)]
     )
 
-    def sum_rep(parts):
+    def sum_rep(parts, shift=False):
         sums = [
             sum(parts[step].astype(f32) for step in range(first, planes, share))
             for first in range(share)
         ]
         return jnp.stack(
             [
-                sum(jnp.where(own ^ step == j, sums[step], 0.0) for step in range(share))
+                sum(
+                    jnp.where(((own - step) % share if shift else own ^ step) == j, sums[step], 0.0)
+                    for step in range(share)
+                )
                 for j in range(share)
             ]
         )
 
+    tail, out_cut = lax.optimization_barrier((tail, out_cut))
+    out_sent = send(out_cut, [near])
     tail, out_cut, out_pieces = lax.optimization_barrier((tail, out_cut, out_pieces))
-    out_sent = send(out_cut, range(1, planes))
+    out_sent.update(send(out_cut, range(2, planes)))
     back = []
     returned = []
 
@@ -908,18 +913,18 @@
     rows_in = after(rows_in, tail)
     rows_flat = rows_in.reshape(in_rows, D)
     grads_flat = [back[step][3].reshape(in_rows // micro, 2 * FF) for step in range(micro)]
-    (in_last,) = weight_gradient(
-        where, planes, rows_flat, grads_flat, first=last_step, steps=1
-    )
-    rows_flat, in_last = lax.optimization_barrier((rows_flat, in_last))
-    in_cut = weight_gradient(where, planes, rows_flat, grads_flat, steps=last_step)
+    (in_near,) = weight_gradient(
+        where, planes, rows_flat, grads_flat, first=1, steps=1, shift=True
+    )
+    rows_flat, in_near = lax.optimization_barrier((rows_flat, in_near))
+    *in_rest, in_back, in_own = weight_gradient(
+        where, planes, rows_flat, grads_flat, first=2, steps=last_step, shift=True
+    )
+    in_sent = {0: in_own, 1: shift_rep(in_near, 1)}
 
     def cuts(value, *places):
         ends = [-(-value.shape[0] * place // 512) * 16 for place in (0, *places, 32)]
         return [value[start:end] for start, end in zip(ends, ends[1:])]
-
-    in_last = cuts(in_last, 11, 19, 26)
-    last_sent = [cross_rep(in_last[0], last_step)]
 
     def swap(value, step):
         return lax.ppermute(value, "ep", [(i, i ^ step) for i in range(ranks)])
@@ -951,24 +956,26 @@
 
     grad_inputs, branches, logit_grads, grad_projs = [], [], [], []
     gain_two_sum = gain_one_sum = qk_sum = 0.0
-    in_cut, out_sent, last_sent, in_last = lax.optimization_barrier(
-        (in_cut, out_sent, last_sent, in_last)
+    in_rest, in_back, out_sent, in_sent = lax.optimization_barrier(
+        (in_rest, in_back, out_sent, in_sent)
     )
     mixtures = [part[:2] for part in back]
     for step in range(micro):
         at = slice(step * rows, (step + 1) * rows)
         parts = after(returned[step], [one[1] for one in grad_inputs])
-        parts, last_sent = lax.optimization_barrier((parts, last_sent))
+        parts, in_sent = lax.optimization_barrier((parts, in_sent))
+        if step == micro - 1:
+            crossed = halve(after(mixtures, parts), 0)
         parts = exchange_back(parts)
-        parts, in_cut, mixtures, in_last = lax.optimization_barrier(
-            (parts, in_cut, mixtures, in_last)
+        parts, in_rest, in_back, mixtures = lax.optimization_barrier(
+            (parts, in_rest, in_back, mixtures)
         )
         if step == 0:
             mixtures = [pair_sum(*part) for part in mixtures]
-            last_sent.append(cross_rep(in_last[1], last_step))
+            in_sent[last_step] = shift_rep(in_back, last_step)
         if step == micro - 1:
-            rest = [cuts(value, 12, 20) for value in in_cut[1:]]
-            rest_sent = [[cross_rep(part[0], i + 1) for i, part in enumerate(rest)]]
+            rest = [cuts(value, 12, 20) for value in in_rest]
+            rest_sent = [[shift_rep(part[0], i + 2) for i, part in enumerate(rest)]]
         grad_hidden, grad_branch, grad_mixed, grad_logits, gain_two = hidden_backward(
             where[1:2], planes, parts, hidden[at], gates[at], cotangent[at], second_gain,
             router, gathered, experts,
@@ -980,27 +987,19 @@
             out_sum = dot(mixed, jnp.concatenate(branches, axis=0), ((0,), (0,))).astype(bf16)
             out_sum = out_sum.reshape(planes, ranks, dense_rows, D).transpose(1, 0, 2, 3)
         grad_mixed = lax.all_to_all(grad_mixed, "ep", split_axis=1, concat_axis=0, tiled=True)
-        grad_mixed, mixtures, last_sent, in_last = lax.optimization_barrier(
-            (grad_mixed, mixtures, last_sent, in_last)
-        )
-        if step == 0:
-            last_sent.append(cross_rep(in_last[2], last_step))
+        grad_mixed, mixtures = lax.optimization_barrier((grad_mixed, mixtures))
         if step == micro - 1:
-            grad_mixed, mixtures, rest_sent, rest, out_sum = lax.optimization_barrier(
-                (grad_mixed, mixtures, rest_sent, rest, out_sum)
+            grad_mixed, crossed, rest_sent, rest, out_sum = lax.optimization_barrier(
+                (grad_mixed, crossed, rest_sent, rest, out_sum)
             )
             out_sum = lax.psum_scatter(out_sum, "ep", scatter_dimension=0)
-            rest_sent.append([cross_rep(part[1], i + 1) for i, part in enumerate(rest)])
+            rest_sent.append([shift_rep(part[1], i + 2) for i, part in enumerate(rest)])
         grad_proj, grad_qk = attention_backward(
             step, proj, *tables, query, keys, values, lses, grad_mixed
         )
         qk_sum = qk_sum + grad_qk.reshape(-1)
         if step < micro - 1:
-            grad_proj, last_sent, in_last = lax.optimization_barrier(
-                (grad_proj, last_sent, in_last)
-            )
-            if step == 0:
-                last_sent.append(cross_rep(in_last[3], last_step))
+            grad_proj, in_sent = lax.optimization_barrier((grad_proj, in_sent))
         else:
             grad_proj, grad_inputs, rest_sent, rest = lax.optimization_barrier(
                 (grad_proj, grad_inputs, rest_sent, rest)
@@ -1039,7 +1038,7 @@
     grad_projs, rest, out_cut, out_sent, _ = lax.optimization_barrier(
         (grad_projs, rest, out_cut, out_sent, grad_normed)
     )
-    rest_sent.append([cross_rep(part[2], i + 1) for i, part in enumerate(rest)])
+    rest_sent.append([shift_rep(part[2], i + 2) for i, part in enumerate(rest)])
     packed = weight_gradient(
         where,
         planes,
@@ -1047,14 +1046,13 @@
         [jnp.stack(grad_projs, axis=1).reshape(ranks * mine, 3 * width)],
         halves(small),
     )
-    packed, rest_sent, out_cut, out_sent, mixtures = lax.optimization_barrier(
-        (packed, rest_sent, out_cut, out_sent, mixtures)
+    for phase in range(1, len(bits)):
+        mixtures = [total(parts).astype(bf16) for parts in crossed]
+        crossed = halve(mixtures, phase)
+    packed, rest_sent, out_cut, out_sent, crossed = lax.optimization_barrier(
+        (packed, rest_sent, out_cut, out_sent, crossed)
     )
     packed_sent = [packed[0]] + [cross_rep(packed[step], step) for step in range(1, planes)]
-    for phase in range(len(bits)):
-        crossed = halve(mixtures, phase)
-        if phase < len(bits) - 1:
-            mixtures = [total(parts).astype(bf16) for parts in crossed]
     normed_sums = [one[2] for one in grad_inputs]
     normed_sums = [one[2] for one in grad_inputs]
     grad_tokens = []
@@ -1068,7 +1066,6 @@
         )
     grad_tokens = jnp.concatenate(grad_tokens, axis=0)
     packed_sent, grad_tokens = lax.optimization_barrier((packed_sent, grad_tokens))
-    crossed, out_sum = lax.optimization_barrier((crossed, out_sum))
     mixture = []
     for number in range(micro):
         parts = total(crossed[number])[0]
@@ -1088,12 +1085,9 @@
     grad_w_o = total([own_sum, *out_sent_back])
     grad_w_qkv, small = unpack(packed, count)
     grad_w_out = sum_rep({0: out_cut[0], **out_sent})
-    in_sent = {
-        i + 1: jnp.concatenate([parts[i] for parts in rest_sent], axis=0)
-        for i in range(planes - 2)
-    }
-    in_sent[last_step] = jnp.concatenate(last_sent, axis=0)
-    grad_w_in = sum_rep({0: in_cut[0], **in_sent})
+    for i in range(planes - 3):
+        in_sent[i + 2] = jnp.concatenate([parts[i] for parts in rest_sent], axis=0)
+    grad_w_in = sum_rep(in_sent, shift=True)
     return (
         output,
         grad_tokens,

time: 1010 us -> 982 us (0.972)
  waiting for transfers between devices: 349 us -> 327 us
  starting transfers between devices: 162 us -> 141 us
  Pallas kernels: 320 us -> 333 us
    ppermute x6, waiting for transfers between devices: 54.5 us -> 14.3 us  [swap(): return lax.ppermute(value, 'ep', [(i, i ^ step) for i in range(ranks)])]
    ppermute x6, starting transfers between devices: 43.7 us -> 9.06 us  [exchange(): return lax.ppermute(value, 'rep', pairs)]
    ppermute x28 -> x18, waiting for transfers between devices: 146 us -> 120 us  [cross_rep(): lax.ppermute(value, 'rep', [(i, i ^ bits) for i in range(lax.axis_size('r...]
    all_to_all x2, waiting for transfers between devices: 0.26 us -> 20.1 us  [on_device(): lax.all_to_all(grad_mixed, 'ep', split_axis=1, concat_axis=0, tiled=True)]
    ppermute x3 -> x8, waiting for transfers between devices: 50.7 us -> 68.1 us  [shift_rep(): lax.ppermute(value, 'rep', [(i, (i + step) % count) for i in range(count)])]
    ppermute x28 -> x18, starting transfers between devices: 91.7 us -> 105 us  [cross_rep(): lax.ppermute(value, 'rep', [(i, i ^ bits) for i in range(lax.axis_size('r...]
    pallas_call x2, Pallas kernels: 85.1 us -> 96.9 us  [expert_backward(): pl.pallas_call(kernel, grid_spec=pltpu.PrefetchScalarGridSpec(num_scalar_...]
    another operation x7 -> x6, other arithmetic: 19.2 us -> 25.4 us  [the longest x4 24.6 us: sum_rep(): jnp.stack([sum((jnp.where(((own - step) % share if shift else own ^ step)...]
  transfers between devices with their start and end apart: 57 -> 52, of which waited for: 28 -> 25; matrix products, arithmetic and copies ran while one was open for 13% -> 14% of each run, Pallas kernels for 30% -> 33%
where the time goes in v11:
time: 982 us; the launch traced here: 977 us
  Pallas kernels  333 us (34%)
  waiting for transfers between devices  327 us (33%)
  starting transfers between devices  141 us (14%)
  other arithmetic  79.9 us (8%)
  local copies, waits for them, and re-layouts  72.8 us (7%)
  between operations  15 us (2%)
    ppermute x18, waiting for transfers between devices, cross_rep(): lax.ppermute(value, 'rep', [(i, i ^ bits) for i in range(lax.axis_size('r...  120 us
    ppermute x18, starting transfers between devices, cross_rep(): lax.ppermute(value, 'rep', [(i, i ^ bits) for i in range(lax.axis_size('r...  105 us
    pallas_call x2, Pallas kernels, expert_backward(): pl.pallas_call(kernel, grid_spec=pltpu.PrefetchScalarGridSpec(num_scalar_...  96.9 us
    ppermute x8, waiting for transfers between devices, shift_rep(): lax.ppermute(value, 'rep', [(i, (i + step) % count) for i in range(count)])  68.1 us
    pallas_call x4, Pallas kernels, weight_gradient(): pl.pallas_call(kernel, grid_spec=pltpu.PrefetchScalarGridSpec(num_scalar_...  65.6 us
    ppermute x6, waiting for transfers between devices, exchange(): return lax.ppermute(value, 'rep', pairs)  63.3 us
    pallas_call x1, Pallas kernels, expert_forward(): pl.pallas_call(kernel, grid_spec=pltpu.PrefetchScalarGridSpec(num_scalar_...  40.4 us
    pallas_call x2, Pallas kernels, attention_backward(): pl.pallas_call(lambda *refs: backward_kernel(heads, *refs), grid=(1,), in...  34.6 us
  transfers between devices with their start and end apart: 52, of which 25 were waited for; matrix products, arithmetic and copies ran while one was open for 14% of the time, Pallas kernels for 33%

profile of v11, /device:TPU:0, one launch (start us, length us, event | category | flops | bytes accessed | tf_op | source)
XLA Modules:
  0.0 977.0 jit_solution(6045397385392131617)
XLA Ops:
  23.1 17.8 %collective-permute-done.3 = bf16[256,2048]{1,0:T(8,128)(2,1)} collective-permute-done((bf16[256,2048]{1,0:T(8,128)(2,1)}, bf16[256,2048]{1,0:T(8,128)(2,1)}, u32[]{:S(2)}, u32[]{:S(2)}) %collective-permute-start.3) | collective-permute-done | bytes 1048608 | tf_op jit(solution)/shard_map/ppermute | solution.py:788
  56.3 22.5 %collective-permute-done.4 = bf16[512,896]{1,0:T(8,128)(2,1)S(1)} collective-permute-done((bf16[512,896]{1,0:T(8,128)(2,1)S(1)}, bf16[512,896]{1,0:T(8,128)(2,1)S(1)}, u32[]{:S(2)}, u32[]{:S(2)}) %collective-permute-start.4) | collective-permute-done | bytes 917536 | tf_op jit(solution)/shard_map/ppermute | solution.py:736
  107.6 16.8 %collective-permute-done.6 = bf16[512,896]{1,0:T(8,128)(2,1)S(1)} collective-permute-done((bf16[512,896]{1,0:T(8,128)(2,1)}, bf16[512,896]{1,0:T(8,128)(2,1)S(1)}, u32[]{:S(2)}, u32[]{:S(2)}) %collective-permute-start.6) | collective-permute-done | bytes 917536 | tf_op jit(solution)/shard_map/ppermute | solution.py:736
  128.7 14.8 %shard_map.179 = (bf16[8,256,2048]{2,1,0:T(8,128)(2,1)}, f32[8,256,768]{2,1,0:T(8,128)}) custom-call(bf16[8,256,2048]{2,1,0:T(8,128)(2,1)} %bitcast.131, f32[1,2048]{1,0:T(1,128)S(1)} %broadcast_in_dim.56.gain, bf16[2048,896]{1,0:T(8,128)(2,1)} %constant_dynamic-update-slice_fusion.weight), custom_call_target="tpu_custom_call" | custom-call | tf_op jit(solution)/shard_map/pallas_call | solution.py:247
  143.6 22.1 %shard_map.180 = (bf16[8,2,128,256]{3,2,1,0:T(8,128)(2,1)}, bf16[2,1024,256]{2,1,0:T(8,128)(2,1)S(1)}, bf16[2,1024,256]{2,1,0:T(8,128)(2,1)S(1)}, bf16[2,1024,256]{2,1,0:T(8,128)(2,1)}, f32[2,2,1024,1]{3,2,1,0:T(8,128)}) custom-call(f32[8,2,128,768]{3,2,1,0:T(8,128)} %bitcast.134, f32[2,1024,128]{2,1,0:T(8,128)} %get-tuple-element.229.refs_1_, ...), custom_call_target="tpu_custom_call" | custom-call | tf_op jit(solution)/shard_map/pallas_call | solution.py:198
  173.4 24.6 %all-to-all-done.1 = bf16[8,2,128,256]{3,2,1,0:T(8,128)(2,1)S(1)} async-done(((bf16[8,2,128,256]{3,2,1,0:T(8,128)(2,1)}), bf16[8,2,128,256]{3,2,1,0:T(8,128)(2,1)S(1)}, u32[]{:S(2)}, u32[]{:S(2)}) %all-to-all-start.1) | async-done | bytes 1048608 | tf_op jit(solution)/shard_map/all_to_all | solution.py:846
  215.2 23.6 %collective-permute-done.9 = bf16[256,2176]{1,0:T(8,128)(2,1)S(1)} collective-permute-done((bf16[256,2176]{1,0:T(8,128)(2,1)S(1)}, bf16[256,2176]{1,0:T(8,128)(2,1)S(1)}, u32[]{:S(2)}, u32[]{:S(2)}) %collective-permute-start.9) | collective-permute-done | bytes 1114144 | tf_op jit(solution)/shard_map/ppermute | solution.py:788
  240.7 47.7 %collective-permute-done.10.refs_3_ = bf16[512,2048]{1,0:T(8,128)(2,1)} collective-permute-done((bf16[512,2048]{1,0:T(8,128)(2,1)}, bf16[512,2048]{1,0:T(8,128)(2,1)}, u32[]{:S(2)}, u32[]{:S(2)}) %collective-permute-start.10) | collective-permute-done | bytes 2097184 | tf_op jit(solution)/shard_map/ppermute | solution.py:740
  288.4 42.6 %collective-permute-start.11 = (bf16[256,2048]{1,0:T(8,128)(2,1)}, bf16[256,2048]{1,0:T(8,128)(2,1)}, u32[]{:S(2)}, u32[]{:S(2)}) collective-permute-start(bf16[256,2048]{1,0:T(8,128)(2,1)} %get-tuple-element.284), channel_id=1, source_target_pairs={{0,8},{8,0},{16,24},{24,16},{1,9},{9,1},{17,25},{25,17},{2,10},{10... | collective-permute-start | bytes 3145736 | tf_op jit(solution)/shard_map/ppermute | solution.py:740
  333.4 40.4 %shard_map.182 = (bf16[2,4,288,2048]{3,2,1,0:T(8,128)(2,1)}, f32[2,4,288,128]{3,2,1,0:T(8,128)S(1)}, f32[2,4,288,2048]{3,2,1,0:T(8,128)}, bf16[2,4,288,1024]{3,2...) custom-call(s32[3]{0:T(128)S(1)} %pad_add_fusion.where, ...), custom_call_target="tpu_custom_call" | custom-call | flops 241591910400 | tf_op jit(solution)/shard_map/pallas_call | solution.py:431
  375.2 16.9 %shard_map.183 = (bf16[256,2048]{1,0:T(8,128)(2,1)S(1)}, bf16[256,2048]{1,0:T(8,128)(2,1)}, bf16[256,2048]{1,0:T(8,128)(2,1)}, bf16[256,2048]{1,0:T(8,128)(2,1)}) custom-call(s32[3]{0:T(128)S(1)} %pad_add_fusion.where, bf16[2304,1024]{1,0:T(8,128)(2,1)} %bitcast.162, bf16[2304,2048]{1,0:T(8,128)(2,1)} %bitcast.161), custom_call_target="tpu_custom_call" | custom-call | flops 96636764160 | tf_op jit(solution)/shard_map/pallas_call | solution.py:591
  404.5 52.3 %shard_map.184 = (bf16[4,2,128,2048]{3,2,1,0:T(8,128)(2,1)}, bf16[4,2,128,2048]{3,2,1,0:T(8,128)(2,1)}, bf16[8,2,128,2176]{3,2,1,0:T(8,128)(2,1)}, bf16[4,288,2048]{2,1,0:T(8,128)(2,1)}) custom-call(s32[3]{0:T(128)S(1)} %pad_add_fusion.where, f32[2,4,288,128]{3,2,1,0:T(8,128)} %copy-done.30, f32[2,4,288,2048]{3,2,1,0:T(8,128)} %get-tuple-element.286.both, ...), custom_call_target="tpu_custom_call" | custom-call | flops 217432719360 | tf_op jit(solution)/shard_map/pallas_call | solution.py:529
  456.8 42.9 %collective-permute-start.16 = (bf16[256,2048]{1,0:T(8,128)(2,1)}, bf16[256,2048]{1,0:T(8,128)(2,1)}, u32[]{:S(2)}, u32[]{:S(2)}) collective-permute-start(bf16[256,2048]{1,0:T(8,128)(2,1)} %get-tuple-element.303), channel_id=1, source_target_pairs={{0,16},{8,24},{16,0},{24,8},{1,17},{9,25},{17,1},{25,9},{2,18},{10... | collective-permute-start | bytes 3145736 | tf_op jit(solution)/shard_map/ppermute | solution.py:740
  499.7 44.6 %shard_map.185 = (bf16[4,2,128,2048]{3,2,1,0:T(8,128)(2,1)}, bf16[4,2,128,2048]{3,2,1,0:T(8,128)(2,1)}, bf16[8,2,128,2176]{3,2,1,0:T(8,128)(2,1)}, bf16[4,288,2048]{2,1,0:T(8,128)(2,1)}) custom-call(s32[3]{0:T(128)S(1)} %pad_add_fusion.where, f32[2,4,288,128]{3,2,1,0:T(8,128)} %copy-done.30, f32[2,4,288,2048]{3,2,1,0:T(8,128)} %get-tuple-element.286.both, ...), custom_call_target="tpu_custom_call" | custom-call | flops 217432719360 | tf_op jit(solution)/shard_map/pallas_call | solution.py:529
  556.4 24.3 %shard_map.187 = (bf16[512,2048]{1,0:T(8,128)(2,1)S(1)}, bf16[512,2048]{1,0:T(8,128)(2,1)}, bf16[512,2048]{1,0:T(8,128)(2,1)}) custom-call(s32[3]{0:T(128)S(1)} %pad_add_fusion.where, bf16[2304,2048]{1,0:T(8,128)(2,1)} %bitcast.160, bf16[1152,2048]{1,0:T(8,128)(2,1)} %bitcast.164, bf16[1152,2048]{1,0:T(8,128)(2,1)} %bitcast.166), custom_call_target="tpu_custom_call" | custom-call | flops 144955146240 | tf_op jit(solution)/shard_map/pallas_call | solution.py:591
  636.0 17.5 %shard_map.189 = (bf16[8,128,768]{2,1,0:T(8,128)(2,1)}, f32[2,128]{1,0:T(2,128)S(1)}) custom-call(f32[8,2,128,768]{3,2,1,0:T(8,128)} %bitcast.135, f32[2,1024,128]{2,1,0:T(8,128)S(1)} %copy-done.2, f32[2,1024,128]{2,1,0:T(8,128)S(1)} %copy-done.1, s32[2,1024,1]{2,1,0:T(8,128)S(1)} %copy-done.3, s32[2,1,1024]{2,1,0:T(1,128)S(1)} %copy-done.24, ...), custom_call_target="tpu_custom_call" | custom-call | tf_op jit(solution)/shard_map/pallas_call | solution.py:220
  654.9 13.9 %shard_map.190 = (bf16[1024,2048]{1,0:T(8,128)(2,1)}, f32[1,2048]{1,0:T(1,128)S(1)}) custom-call(bf16[8,128,768]{2,1,0:T(8,128)(2,1)S(1)} %copy-done.8, bf16[8,256,2048]{2,1,0:T(8,128)(2,1)} %bitcast.132, bf16[2048,896]{1,0:T(8,128)(2,1)} %constant_dynamic-update-slice_fusion.weight), custom_call_target="tpu_custom_call" | custom-call | tf_op jit(solution)/shard_map/pallas_call | solution.py:681
  682.1 12.4 %collective-permute-done.22.refs_1_ = bf16[128,2176]{1,0:T(8,128)(2,1)S(1)} collective-permute-done((bf16[128,2176]{1,0:T(8,128)(2,1)S(1)}, bf16[128,2176]{1,0:T(8,128)(2,1)S(1)}, u32[]{:S(2)}, u32[]{:S(2)}) %collective-permute-start.22) | collective-permute-done | bytes 557088 | tf_op jit(solution)/shard_map/ppermute | solution.py:788
  728.5 20.1 %all-to-all-done.3 = bf16[128,8,256]{2,0,1:T(8,128)(2,1)} async-done(((bf16[128,8,256]{2,0,1:T(8,128)(2,1)}), bf16[128,8,256]{2,0,1:T(8,128)(2,1)}, u32[]{:S(2)}, u32[]{:S(2)}) %all-to-all-start.3) | async-done | bytes 524320 | tf_op jit(solution)/shard_map/all_to_all | solution.py:989
  750.6 17.2 %shard_map.192 = (bf16[8,128,768]{2,1,0:T(8,128)(2,1)}, f32[2,128]{1,0:T(2,128)S(1)}) custom-call(f32[8,2,128,768]{3,2,1,0:T(8,128)} %bitcast.136, f32[2,1024,128]{2,1,0:T(8,128)S(1)} %copy-done.2, f32[2,1024,128]{2,1,0:T(8,128)S(1)} %copy-done.1, s32[2,1024,1]{2,1,0:T(8,128)S(1)} %copy-done.4, s32[2,1,1024]{2,1,0:T(1,128)S(1)} %copy-done.24, ...), custom_call_target="tpu_custom_call" | custom-call | tf_op jit(solution)/shard_map/pallas_call | solution.py:220
  775.5 13.9 %shard_map.193 = (bf16[1024,2048]{1,0:T(8,128)(2,1)}, f32[1,2048]{1,0:T(1,128)S(1)}) custom-call(bf16[8,128,768]{2,1,0:T(8,128)(2,1)S(1)} %copy-done.10, bf16[8,256,2048]{2,1,0:T(8,128)(2,1)} %bitcast.133, bf16[2048,896]{1,0:T(8,128)(2,1)} %constant_dynamic-update-slice_fusion.weight), custom_call_target="tpu_custom_call" | custom-call | tf_op jit(solution)/shard_map/pallas_call | solution.py:681
  809.2 12.3 %shard_map.194 = (bf16[512,896]{1,0:T(8,128)(2,1)S(1)}, bf16[512,896]{1,0:T(8,128)(2,1)}, bf16[512,896]{1,0:T(8,128)(2,1)S(1)}, bf16[512,896]{1,0:T(8,128)(2,1)}) custom-call(s32[3]{0:T(128)S(1)} %pad_add_fusion.where, bf16[2048,2048]{1,0:T(8,128)(2,1)} %bitcast.142, bf16[2048,768]{1,0:T(8,128)(2,1)} %bitcast.141, ...), custom_call_target="tpu_custom_call" | custom-call | tf_op jit(solution)/shard_map/pallas_call | solution.py:591
  879.9 22.4 %collective-permute-done.31 = bf16[512,896]{1,0:T(8,128)(2,1)} collective-permute-done((bf16[512,896]{1,0:T(8,128)(2,1)S(1)}, bf16[512,896]{1,0:T(8,128)(2,1)}, u32[]{:S(2)}, u32[]{:S(2)}) %collective-permute-start.31) | collective-permute-done | bytes 917536 | tf_op jit(solution)/shard_map/ppermute | solution.py:740
  918.7 15.1 %reduce-scatter.14.cloned.1.call-done = bf16[1,4,64,2048]{3,2,1,0:T(8,128)(2,1)} async-done(((bf16[8,4,64,2048]{3,2,1,0:T(8,128)(2,1)}), bf16[1,4,64,2048]{3,2,1,0:T(8,128)(2,1)}) %reduce-scatter.14.cloned.1.call-update) | async-done | bytes 1048592 | tf_op jit(solution)/shard_map/reduce_scatter | solution.py:995
  (316 shorter events, 363.2 us)
Async XLA Ops:
  7.2 118.2 %all-gather.9.cloned.1.call-start = ((), (), s32[]{:S(2)}) async-start(), calls=%async_computation.15 | async-start | bytes 9437184 | tf_op jit(solution)/shard_map/all_gather | solution.py:794
  18.6 180.3 %all-gather.11.cloned.1.call-start = ((), (), s32[]{:S(2)}) async-start(), calls=%async_computation.16 | async-start | bytes 9437184 | tf_op jit(solution)/shard_map/all_gather | solution.py:794
  54.5 278.8 %all-gather.15.cloned.1.call-start = ((), (), s32[]{:S(2)}) async-start(), calls=%async_computation.18 | async-start | bytes 18874368 | tf_op jit(solution)/shard_map/all_gather | solution.py:794
  125.5 87.9 %collective-permute-start.7 = (bf16[512,2048]{1,0:T(8,128)(2,1)}, bf16[512,2048]{1,0:T(8,128)(2,1)}, u32[]{:S(2)}, u32[]{:S(2)}) collective-permute-start(bf16[512,2048]{1,0:T(8,128)(2,1)} %get-tuple-element.260), channel_id=1, source_target_pairs={{0,8},{8,0},{16,24},{24,16},{1,9},{9,1},{17,25},{25,17},{2,10},{10... | collective-permute-start | bytes 6291464 | tf_op jit(solution)/shard_map/ppermute | solution.py:740
  125.5 87.9 %collective-permute-start.8 = (bf16[512,2048]{1,0:T(8,128)(2,1)}, bf16[512,2048]{1,0:T(8,128)(2,1)}, u32[]{:S(2)}, u32[]{:S(2)}) collective-permute-start(bf16[512,2048]{1,0:T(8,128)(2,1)} %get-tuple-element.265.refs_0_), channel_id=1, source_target_pairs={{0,16},{8,24},{16,0},{24,8},{1,17},{9,25},{17,1},{25,9},{2,18},{10... | collective-permute-start | bytes 6291464 | tf_op jit(solution)/shard_map/ppermute | solution.py:740
  171.6 161.8 %all-gather.13.cloned.1.call-start = ((), (), s32[]{:S(2)}) async-start(), calls=%async_computation.17 | async-start | bytes 20054016 | tf_op jit(solution)/shard_map/all_gather | solution.py:794
  240.5 350.0 %reduce-scatter.6.cloned.1.call-start = ((), (), s32[]{:S(2)}) async-start(), calls=%async_computation.10 | async-start | bytes 10027008 | tf_op jit(solution)/shard_map/reduce_scatter | solution.py:894
  288.4 105.8 %collective-permute-start.11 = (bf16[256,2048]{1,0:T(8,128)(2,1)}, bf16[256,2048]{1,0:T(8,128)(2,1)}, u32[]{:S(2)}, u32[]{:S(2)}) collective-permute-start(bf16[256,2048]{1,0:T(8,128)(2,1)} %get-tuple-element.284), channel_id=1, source_target_pairs={{0,8},{8,0},{16,24},{24,16},{1,9},{9,1},{17,25},{25,17},{2,10},{10... | collective-permute-start | bytes 3145736 | tf_op jit(solution)/shard_map/ppermute | solution.py:740
  331.0 72.3 %collective-permute-start.12 = (bf16[256,2048]{1,0:T(8,128)(2,1)}, bf16[256,2048]{1,0:T(8,128)(2,1)}, u32[]{:S(2)}, u32[]{:S(2)}) collective-permute-start(bf16[256,2048]{1,0:T(8,128)(2,1)} %get-tuple-element.289.refs_4_), channel_id=1, source_target_pairs={{0,16},{8,24},{16,0},{24,8},{1,17},{9,25},{17,1},{25,9},{2,18},{10... | collective-permute-start | bytes 3145736 | tf_op jit(solution)/shard_map/ppermute | solution.py:740
  331.0 72.3 %collective-permute-start.13 = (bf16[256,2048]{1,0:T(8,128)(2,1)}, bf16[256,2048]{1,0:T(8,128)(2,1)}, u32[]{:S(2)}, u32[]{:S(2)}) collective-permute-start(bf16[256,2048]{1,0:T(8,128)(2,1)} %get-tuple-element.284), channel_id=1, source_target_pairs={{0,24},{8,16},{16,8},{24,0},{1,25},{9,17},{17,9},{25,1},{2,26},{10... | collective-permute-start | bytes 3145736 | tf_op jit(solution)/shard_map/ppermute | solution.py:740
  393.1 106.7 %collective-permute-start.14 = (bf16[256,2048]{1,0:T(8,128)(2,1)}, bf16[256,2048]{1,0:T(8,128)(2,1)}, u32[]{:S(2)}, u32[]{:S(2)}) collective-permute-start(bf16[256,2048]{1,0:T(8,128)(2,1)} %get-tuple-element.278), channel_id=1, source_target_pairs={{0,8},{8,0},{16,24},{24,16},{1,9},{9,1},{17,25},{25,17},{2,10},{10... | collective-permute-start | bytes 3145736 | tf_op jit(solution)/shard_map/ppermute | solution.py:740
  403.3 96.4 %collective-permute-start.15 = (bf16[256,2048]{1,0:T(8,128)(2,1)}, bf16[256,2048]{1,0:T(8,128)(2,1)}, u32[]{:S(2)}, u32[]{:S(2)}) collective-permute-start(bf16[256,2048]{1,0:T(8,128)(2,1)} %get-tuple-element.296), channel_id=1, source_target_pairs={{0,24},{8,16},{16,8},{24,0},{1,25},{9,17},{17,9},{25,1},{2,26},{10... | collective-permute-start | bytes 3145736 | tf_op jit(solution)/shard_map/ppermute | solution.py:740
  456.8 212.1 %reduce-scatter.8.cloned.1.call-start = ((), (), s32[]{:S(2)}) async-start(), calls=%async_computation.11 | async-start | bytes 10027008 | tf_op jit(solution)/shard_map/reduce_scatter | solution.py:894
  456.8 125.3 %collective-permute-start.16 = (bf16[256,2048]{1,0:T(8,128)(2,1)}, bf16[256,2048]{1,0:T(8,128)(2,1)}, u32[]{:S(2)}, u32[]{:S(2)}) collective-permute-start(bf16[256,2048]{1,0:T(8,128)(2,1)} %get-tuple-element.303), channel_id=1, source_target_pairs={{0,16},{8,24},{16,0},{24,8},{1,17},{9,25},{17,1},{25,9},{2,18},{10... | collective-permute-start | bytes 3145736 | tf_op jit(solution)/shard_map/ppermute | solution.py:740
  620.5 153.6 %reduce-scatter.10.cloned.1.call-start = ((), (), s32[]{:S(2)}) async-start(), calls=%async_computation.12 | async-start | bytes 4718592 | tf_op jit(solution)/shard_map/reduce_scatter | solution.py:1014
  673.9 74.7 %collective-permute-start.23 = (bf16[2,2,128,2048]{3,2,1,0:T(8,128)(2,1)}, bf16[2,2,128,2048]{3,2,1,0:T(8,128)(2,1)}, u32[]{:S(2)}, u32[]{:S(2)}) collective-permute-start(bf16[2,2,128,2048]{3,2,1,0:T(8,128)(2,1)} %get-tuple-element.480), channel_id=1, source_target_pairs={{0,2},{1,3},{2,0},{3,1},{4,6},{5,7},{6,4},{7,5},{8,10},{9,11},{10,... | collective-permute-start | bytes 6291464 | tf_op jit(solution)/shard_map/ppermute | solution.py:930
  678.4 70.2 %collective-permute-start.24 = (bf16[2,2,128,2048]{3,2,1,0:T(8,128)(2,1)}, bf16[2,2,128,2048]{3,2,1,0:T(8,128)(2,1)}, u32[]{:S(2)}, u32[]{:S(2)}) collective-permute-start(bf16[2,2,128,2048]{3,2,1,0:T(8,128)(2,1)} %get-tuple-element.478), channel_id=1, source_target_pairs={{0,4},{1,5},{2,6},{3,7},{4,0},{5,1},{6,2},{7,3},{8,12},{9,13},{10,... | collective-permute-start | bytes 6291464 | tf_op jit(solution)/shard_map/ppermute | solution.py:930
  695.8 52.8 %collective-permute-start.25 = (bf16[192,2048]{1,0:T(8,128)(2,1)}, bf16[192,2048]{1,0:T(8,128)(2,1)}, u32[]{:S(2)}, u32[]{:S(2)}) collective-permute-start(bf16[192,2048]{1,0:T(8,128)(2,1)} %get-tuple-element.491), channel_id=1, source_target_pairs={{0,16},{8,24},{16,0},{24,8},{1,17},{9,25},{17,1},{25,9},{2,18},{10... | collective-permute-start | bytes 2359304 | tf_op jit(solution)/shard_map/ppermute | solution.py:736
  712.6 152.0 %reduce-scatter.12.cloned.1.call-start = ((), (), s32[]{:S(2)}) async-start(), calls=%async_computation.13 | async-start | bytes 4718592 | tf_op jit(solution)/shard_map/reduce_scatter | solution.py:1014
  789.4 144.5 %reduce-scatter.14.cloned.1.call-start = ((), (), s32[]{:S(2)}) async-start(), calls=%async_computation.14 | async-start | bytes 9437184 | tf_op jit(solution)/shard_map/reduce_scatter | solution.py:995
  838.6 63.7 %collective-permute-start.31 = (bf16[512,896]{1,0:T(8,128)(2,1)S(1)}, bf16[512,896]{1,0:T(8,128)(2,1)}, u32[]{:S(2)}, u32[]{:S(2)}) collective-permute-start(bf16[512,896]{1,0:T(8,128)(2,1)S(1)} %get-tuple-element.388), channel_id=1, source_target_pairs={{0,16},{8,24},{16,0},{24,8},{1,17},{9,25},{17,1},{25,9},{2,18},{10... | collective-permute-start | bytes 2752520 | tf_op jit(solution)/shard_map/ppermute | solution.py:740
  840.4 61.9 %collective-permute-start.32 = (bf16[512,896]{1,0:T(8,128)(2,1)}, bf16[512,896]{1,0:T(8,128)(2,1)}, u32[]{:S(2)}, u32[]{:S(2)}) collective-permute-start(bf16[512,896]{1,0:T(8,128)(2,1)} %get-tuple-element.389), channel_id=1, source_target_pairs={{0,24},{8,16},{16,8},{24,0},{1,25},{9,17},{17,9},{25,1},{2,26},{10... | collective-permute-start | bytes 2752520 | tf_op jit(solution)/shard_map/ppermute | solution.py:740
  845.5 100.0 %collective-permute-start.33 = (bf16[128,2048]{1,0:T(8,128)(2,1)}, bf16[128,2048]{1,0:T(8,128)(2,1)}, u32[]{:S(2)}, u32[]{:S(2)}) collective-permute-start(bf16[128,2048]{1,0:T(8,128)(2,1)} %fusion.18), channel_id=1, source_target_pairs={{0,8},{8,0},{16,24},{24,16},{1,9},{9,1},{17,25},{25,17},{2,10},{10... | collective-permute-start | bytes 1572872 | tf_op jit(solution)/shard_map/ppermute | solution.py:788
  847.9 97.5 %collective-permute-start.34 = (bf16[128,2048]{1,0:T(8,128)(2,1)}, bf16[128,2048]{1,0:T(8,128)(2,1)}, u32[]{:S(2)}, u32[]{:S(2)}) collective-permute-start(bf16[128,2048]{1,0:T(8,128)(2,1)} %fusion.19), channel_id=1, source_target_pairs={{0,8},{8,0},{16,24},{24,16},{1,9},{9,1},{17,25},{25,17},{2,10},{10... | collective-permute-start | bytes 1572872 | tf_op jit(solution)/shard_map/ppermute | solution.py:788
  (82 other events, 2207.5 us)
Sparse Core Ops, SparseCore 0:
  9.9 64.3 all-gather.8
  76.8 54.3 all-gather.10
  133.1 100.3 all-gather.14
  240.6 92.1 all-gather.12
  456.9 113.4 reduce-scatter.5
  573.8 79.3 reduce-scatter.7
  668.9 68.5 reduce-scatter.9
  789.5 60.2 reduce-scatter.11
  853.3 80.5 reduce-scatter.13

commit v12 on v11

--- a/solution.py
+++ b/solution.py
@@ -234,22 +234,26 @@
     )
 
 
-def project(tokens, gain, slab):
+def project(micro, tokens, gain, slab):
     ranks, count, _ = tokens.shape
+    rows = count // micro
     width = slab.shape[1] - PAD
 
     def kernel(value, gain, weight, normed, proj):
         value = value[0].astype(f32)
         result = (value * inverse_rms(value) * gain[...]).astype(bf16)
-        normed[0] = result
+        normed[...] = result.reshape(micro, 1, rows, D)
         proj[0] = dot(result, weight[:, :width])
 
     return pl.pallas_call(
         kernel,
         grid=(ranks,),
         in_specs=[leading((ranks, count, D)), fixed((1, D)), fixed(slab.shape)],
-        out_specs=[leading((ranks, count, D)), leading((ranks, count, width))],
-        out_shape=[out((ranks, count, D)), out((ranks, count, width), f32)],
+        out_specs=[
+            pl.BlockSpec((micro, 1, rows, D), lambda i: (0, i, 0, 0)),
+            leading((ranks, count, width)),
+        ],
+        out_shape=[out((micro, ranks, rows, D)), out((ranks, count, width), f32)],
         compiler_params=params(),
     )(tokens, gain, slab)
 
@@ -794,7 +798,7 @@
         return lax.all_gather(value, "ep", axis=0)
 
     assert planes & (planes - 1) == 0 and share & (share - 1) == 0
-    near, half, last_step = 1, planes // 2, planes - 1
+    last_step = planes - 1
     in_parts, out_parts = (
         {
             step: lax.dynamic_index_in_dim(weight, own ^ step % share, 0, keepdims=False)
@@ -840,7 +844,7 @@
     in_pieces = {0: in_parts[0], **send(in_parts, range(last_step - 1, 0, -1))}
     upstream_all = gather_ranks(upstream_group)
 
-    normed, proj = project(stream, first_gain, slab)
+    normed, proj = project(micro, stream, first_gain, slab)
     proj = proj.reshape(ranks, micro, rows, 3 * width)
     mixed_h, query, keys, values, lses = attention_forward(proj, *tables)
     mixed = lax.all_to_all(mixed_h, "ep", split_axis=0, concat_axis=3, tiled=True)
@@ -883,10 +887,31 @@
             ]
         )
 
-    tail, out_cut = lax.optimization_barrier((tail, out_cut))
-    out_sent = send(out_cut, [near])
     tail, out_cut, out_pieces = lax.optimization_barrier((tail, out_cut, out_pieces))
-    out_sent.update(send(out_cut, range(2, planes)))
+    out_sent = send(out_cut, range(1, planes))
+    def swap(value, step):
+        return lax.ppermute(value, "ep", [(i, i ^ step) for i in range(ranks)])
+
+    def pair_sum(keep, give):
+        return (keep.astype(f32) + swap(give, 1).astype(f32)).astype(bf16)
+
+    bits = list(range((ranks // 2).bit_length() - 1))
+
+    def halve(number, value, phase):
+        way = bits if number % 2 == 0 else bits[::-1]
+        bit = way[phase]
+        low = 2 ** sum(other < bit for other in way[phase:])
+        value = value.reshape((-1, 2, low) + value.shape[1:])
+        side = rank // 2 // 2**bit % 2
+        keep, give = (
+            lax.dynamic_index_in_dim(value, which, 1, keepdims=False).reshape((-1,) + value.shape[3:])
+            for which in (side, 1 - side)
+        )
+        return keep, swap(give, 2 * 2**bit)
+
+    def total(parts):
+        return sum(part.astype(f32) for part in parts)
+
     back = []
     returned = []
 
@@ -905,12 +930,12 @@
         )
         returned.append(scatter_ranks(back[step][2]))
         if step == 0:
-            ended = {bits: out_sent[bits] for bits in (near, last_step)}
-            tail, ended = after((tail, ended), back[step][2])
-            out_sent.update(ended)
+            tail, out_sent[last_step] = after((tail, out_sent[last_step]), back[step][2])
         else:
             tail = after(tail, back[step][2])
-    rows_in = after(rows_in, tail)
+    early = [pair_sum(*part[:2]) for part in back[:-1]]
+    rows_in, tail, early = lax.optimization_barrier((rows_in, tail, early))
+    crossed = [halve(number, value, 0) for number, value in enumerate(early)]
     rows_flat = rows_in.reshape(in_rows, D)
     grads_flat = [back[step][3].reshape(in_rows // micro, 2 * FF) for step in range(micro)]
     (in_near,) = weight_gradient(
@@ -926,52 +951,22 @@
         ends = [-(-value.shape[0] * place // 512) * 16 for place in (0, *places, 32)]
         return [value[start:end] for start, end in zip(ends, ends[1:])]
 
-    def swap(value, step):
-        return lax.ppermute(value, "ep", [(i, i ^ step) for i in range(ranks)])
-
-    def pair_sum(keep, give):
-        return (keep.astype(f32) + swap(give, 1).astype(f32)).astype(bf16)
-
-    bits = list(range((ranks // 2).bit_length() - 1))
-
-    def halve(values, phase):
-        results = []
-        for number, value in enumerate(values):
-            way = bits if number % 2 == 0 else bits[::-1]
-            bit = way[phase]
-            low = 2 ** sum(other < bit for other in way[phase:])
-            value = value.reshape((-1, 2, low) + value.shape[1:])
-            side = rank // 2 // 2**bit % 2
-            keep, give = (
-                lax.dynamic_index_in_dim(value, which, 1, keepdims=False).reshape(
-                    (-1,) + value.shape[3:]
-                )
-                for which in (side, 1 - side)
-            )
-            results.append((keep, swap(give, 2 * 2**bit)))
-        return results
-
-    def total(parts):
-        return sum(part.astype(f32) for part in parts)
-
     grad_inputs, branches, logit_grads, grad_projs = [], [], [], []
     gain_two_sum = gain_one_sum = qk_sum = 0.0
-    in_rest, in_back, out_sent, in_sent = lax.optimization_barrier(
-        (in_rest, in_back, out_sent, in_sent)
-    )
-    mixtures = [part[:2] for part in back]
+    in_rest, in_back, out_sent, in_sent, crossed = lax.optimization_barrier(
+        (in_rest, in_back, out_sent, in_sent, crossed)
+    )
+    late = back[-1][:2]
     for step in range(micro):
         at = slice(step * rows, (step + 1) * rows)
         parts = after(returned[step], [one[1] for one in grad_inputs])
         parts, in_sent = lax.optimization_barrier((parts, in_sent))
         if step == micro - 1:
-            crossed = halve(after(mixtures, parts), 0)
+            crossed.append(halve(step, after(late, parts), 0))
         parts = exchange_back(parts)
-        parts, in_rest, in_back, mixtures = lax.optimization_barrier(
-            (parts, in_rest, in_back, mixtures)
-        )
+        parts, in_rest, in_back, late = lax.optimization_barrier((parts, in_rest, in_back, late))
         if step == 0:
-            mixtures = [pair_sum(*part) for part in mixtures]
+            late = pair_sum(*late)
             in_sent[last_step] = shift_rep(in_back, last_step)
         if step == micro - 1:
             rest = [cuts(value, 12, 20) for value in in_rest]
@@ -987,10 +982,10 @@
             out_sum = dot(mixed, jnp.concatenate(branches, axis=0), ((0,), (0,))).astype(bf16)
             out_sum = out_sum.reshape(planes, ranks, dense_rows, D).transpose(1, 0, 2, 3)
         grad_mixed = lax.all_to_all(grad_mixed, "ep", split_axis=1, concat_axis=0, tiled=True)
-        grad_mixed, mixtures = lax.optimization_barrier((grad_mixed, mixtures))
+        grad_mixed, late = lax.optimization_barrier((grad_mixed, late))
         if step == micro - 1:
-            grad_mixed, crossed, rest_sent, rest, out_sum = lax.optimization_barrier(
-                (grad_mixed, crossed, rest_sent, rest, out_sum)
+            grad_mixed, rest_sent, rest, out_sum, crossed = lax.optimization_barrier(
+                (grad_mixed, rest_sent, rest, out_sum, crossed)
             )
             out_sum = lax.psum_scatter(out_sum, "ep", scatter_dimension=0)
             rest_sent.append([shift_rep(part[1], i + 2) for i, part in enumerate(rest)])
@@ -1043,12 +1038,9 @@
         where,
         planes,
         normed.reshape(ranks * mine, D),
-        [jnp.stack(grad_projs, axis=1).reshape(ranks * mine, 3 * width)],
+        [grad.reshape(length, 3 * width) for grad in grad_projs],
         halves(small),
     )
-    for phase in range(1, len(bits)):
-        mixtures = [total(parts).astype(bf16) for parts in crossed]
-        crossed = halve(mixtures, phase)
     packed, rest_sent, out_cut, out_sent, crossed = lax.optimization_barrier(
         (packed, rest_sent, out_cut, out_sent, crossed)
     )
@@ -1066,6 +1058,9 @@
         )
     grad_tokens = jnp.concatenate(grad_tokens, axis=0)
     packed_sent, grad_tokens = lax.optimization_barrier((packed_sent, grad_tokens))
+    for phase in range(1, len(bits)):
+        mixtures = [total(parts).astype(bf16) for parts in crossed]
+        crossed = [halve(number, value, phase) for number, value in enumerate(mixtures)]
     mixture = []
     for number in range(micro):
         parts = total(crossed[number])[0]

time: 982 us -> 1010 us (1.029)
  waiting for transfers between devices: 327 us -> 354 us
  other arithmetic: 79.9 us -> 65 us
  starting transfers between devices: 141 us -> 153 us
    ppermute x8, waiting for transfers between devices: 68.1 us -> 94.6 us  [shift_rep(): lax.ppermute(value, 'rep', [(i, (i + step) % count) for i in range(count)])]
    ppermute x6, starting transfers between devices: 9.06 us -> 25.1 us  [exchange(): return lax.ppermute(value, 'rep', pairs)]
    ppermute x18, starting transfers between devices: 105 us -> 91.7 us  [cross_rep(): lax.ppermute(value, 'rep', [(i, i ^ bits) for i in range(lax.axis_size('r...]
    another operation x4, other arithmetic: 24.6 us -> 13.2 us  [sum_rep(): jnp.stack([sum((jnp.where(((own - step) % share if shift else own ^ step)...]
  transfers between devices with their start and end apart: 52 -> 52, of which waited for: 25 -> 29; matrix products, arithmetic and copies ran while one was open for 14% -> 12% of each run, Pallas kernels for 33% -> 32%
where the time goes in v12:
time: 1010 us; the launch traced here: 998 us
  waiting for transfers between devices  354 us (35%)
  Pallas kernels  333 us (33%)
  starting transfers between devices  153 us (15%)
  local copies, waits for them, and re-layouts  69.3 us (7%)
  other arithmetic  65 us (6%)
  between operations  15 us (1%)
    ppermute x18, waiting for transfers between devices, cross_rep(): lax.ppermute(value, 'rep', [(i, i ^ bits) for i in range(lax.axis_size('r...  114 us
    pallas_call x2, Pallas kernels, expert_backward(): pl.pallas_call(kernel, grid_spec=pltpu.PrefetchScalarGridSpec(num_scalar_...  97.6 us
    ppermute x8, waiting for transfers between devices, shift_rep(): lax.ppermute(value, 'rep', [(i, (i + step) % count) for i in range(count)])  94.6 us
    ppermute x18, starting transfers between devices, cross_rep(): lax.ppermute(value, 'rep', [(i, i ^ bits) for i in range(lax.axis_size('r...  91.7 us
    ppermute x6, waiting for transfers between devices, exchange(): return lax.ppermute(value, 'rep', pairs)  70.5 us
    pallas_call x4, Pallas kernels, weight_gradient(): pl.pallas_call(kernel, grid_spec=pltpu.PrefetchScalarGridSpec(num_scalar_...  66 us
    pallas_call x1, Pallas kernels, expert_forward(): pl.pallas_call(kernel, grid_spec=pltpu.PrefetchScalarGridSpec(num_scalar_...  40.4 us
    pallas_call x2, Pallas kernels, attention_backward(): pl.pallas_call(lambda *refs: backward_kernel(heads, *refs), grid=(1,), in...  33.5 us
  transfers between devices with their start and end apart: 52, of which 29 were waited for; matrix products, arithmetic and copies ran while one was open for 12% of the time, Pallas kernels for 32%

profile of v12, /device:TPU:0, one launch (start us, length us, event | category | flops | bytes accessed | tf_op | source)
XLA Modules:
  0.0 997.9 jit_solution(7182403868336096931)
XLA Ops:
  23.1 17.7 %collective-permute-done.3 = bf16[256,2048]{1,0:T(8,128)(2,1)S(1)} collective-permute-done((bf16[256,2048]{1,0:T(8,128)(2,1)}, bf16[256,2048]{1,0:T(8,128)(2,1)S(1)}, u32[]{:S(2)}, u32[]{:S(2)}) %collective-permute-start.3) | collective-permute-done | bytes 1048608 | tf_op jit(solution)/shard_map/ppermute | solution.py:792
  57.5 22.5 %collective-permute-done.4 = bf16[512,896]{1,0:T(8,128)(2,1)S(1)} collective-permute-done((bf16[512,896]{1,0:T(8,128)(2,1)S(1)}, bf16[512,896]{1,0:T(8,128)(2,1)S(1)}, u32[]{:S(2)}, u32[]{:S(2)}) %collective-permute-start.4) | collective-permute-done | bytes 917536 | tf_op jit(solution)/shard_map/ppermute | solution.py:740
  108.6 17.1 %collective-permute-done.6 = bf16[512,896]{1,0:T(8,128)(2,1)S(1)} collective-permute-done((bf16[512,896]{1,0:T(8,128)(2,1)}, bf16[512,896]{1,0:T(8,128)(2,1)S(1)}, u32[]{:S(2)}, u32[]{:S(2)}) %collective-permute-start.6) | collective-permute-done | bytes 917536 | tf_op jit(solution)/shard_map/ppermute | solution.py:740
  129.9 15.9 %shard_map.179 = (bf16[2,8,128,2048]{3,2,1,0:T(8,128)(2,1)}, f32[8,256,768]{2,1,0:T(8,128)}) custom-call(bf16[8,256,2048]{2,1,0:T(8,128)(2,1)} %bitcast.130, f32[1,2048]{1,0:T(1,128)S(1)} %broadcast_in_dim.56.gain, bf16[2048,896]{1,0:T(8,128)(2,1)} %constant_dynamic-update-slice_fusion.weight), custom_call_target="tpu_custom_call" | custom-call | tf_op jit(solution)/shard_map/pallas_call | solution.py:248
  145.9 21.7 %shard_map.180 = (bf16[8,2,128,256]{3,2,1,0:T(8,128)(2,1)}, bf16[2,1024,256]{2,1,0:T(8,128)(2,1)S(1)}, bf16[2,1024,256]{2,1,0:T(8,128)(2,1)S(1)}, bf16[2,1024,256]{2,1,0:T(8,128)(2,1)}, f32[2,2,1024,1]{3,2,1,0:T(8,128)}) custom-call(f32[8,2,128,768]{3,2,1,0:T(8,128)} %bitcast.133, f32[2,1024,128]{2,1,0:T(8,128)} %get-tuple-element.224.refs_1_, ...), custom_call_target="tpu_custom_call" | custom-call | tf_op jit(solution)/shard_map/pallas_call | solution.py:198
  175.5 24.6 %all-to-all-done.1 = bf16[8,2,128,256]{3,2,1,0:T(8,128)(2,1)S(1)} async-done(((bf16[8,2,128,256]{3,2,1,0:T(8,128)(2,1)}), bf16[8,2,128,256]{3,2,1,0:T(8,128)(2,1)S(1)}, u32[]{:S(2)}, u32[]{:S(2)}) %all-to-all-start.1) | async-done | bytes 1048608 | tf_op jit(solution)/shard_map/all_to_all | solution.py:850
  215.4 23.7 %collective-permute-done.9 = bf16[256,2176]{1,0:T(8,128)(2,1)S(1)} collective-permute-done((bf16[256,2176]{1,0:T(8,128)(2,1)S(1)}, bf16[256,2176]{1,0:T(8,128)(2,1)S(1)}, u32[]{:S(2)}, u32[]{:S(2)}) %collective-permute-start.9) | collective-permute-done | bytes 1114144 | tf_op jit(solution)/shard_map/ppermute | solution.py:792
  241.0 46.1 %collective-permute-done.10.refs_3_ = bf16[512,2048]{1,0:T(8,128)(2,1)} collective-permute-done((bf16[512,2048]{1,0:T(8,128)(2,1)}, bf16[512,2048]{1,0:T(8,128)(2,1)}, u32[]{:S(2)}, u32[]{:S(2)}) %collective-permute-start.10) | collective-permute-done | bytes 2097184 | tf_op jit(solution)/shard_map/ppermute | solution.py:744
  287.1 43.4 %collective-permute-start.11 = (bf16[256,2048]{1,0:T(8,128)(2,1)}, bf16[256,2048]{1,0:T(8,128)(2,1)}, u32[]{:S(2)}, u32[]{:S(2)}) collective-permute-start(bf16[256,2048]{1,0:T(8,128)(2,1)} %get-tuple-element.274), channel_id=1, source_target_pairs={{0,8},{8,0},{16,24},{24,16},{1,9},{9,1},{17,25},{25,17},{2,10},{10... | collective-permute-start | bytes 3145736 | tf_op jit(solution)/shard_map/ppermute | solution.py:744
  333.4 40.4 %shard_map.182 = (bf16[2,4,288,2048]{3,2,1,0:T(8,128)(2,1)}, f32[2,4,288,128]{3,2,1,0:T(8,128)S(1)}, f32[2,4,288,2048]{3,2,1,0:T(8,128)}, bf16[2,4,288,1024]{3,2...) custom-call(s32[3]{0:T(128)S(1)} %pad_add_fusion.where, ...), custom_call_target="tpu_custom_call" | custom-call | flops 241591910400 | tf_op jit(solution)/shard_map/pallas_call | solution.py:435
  375.1 16.9 %shard_map.183 = (bf16[256,2048]{1,0:T(8,128)(2,1)S(1)}, bf16[256,2048]{1,0:T(8,128)(2,1)}, bf16[256,2048]{1,0:T(8,128)(2,1)}, bf16[256,2048]{1,0:T(8,128)(2,1)}) custom-call(s32[3]{0:T(128)S(1)} %pad_add_fusion.where, bf16[2304,1024]{1,0:T(8,128)(2,1)} %bitcast.164, bf16[2304,2048]{1,0:T(8,128)(2,1)} %bitcast.161), custom_call_target="tpu_custom_call" | custom-call | flops 96636764160 | tf_op jit(solution)/shard_map/pallas_call | solution.py:595
  393.0 20.9 %collective-permute-done.12.refs_6_ = bf16[256,2048]{1,0:T(8,128)(2,1)} collective-permute-done((bf16[256,2048]{1,0:T(8,128)(2,1)}, bf16[256,2048]{1,0:T(8,128)(2,1)}, u32[]{:S(2)}, u32[]{:S(2)}) %collective-permute-start.12) | collective-permute-done | bytes 1048608 | tf_op jit(solution)/shard_map/ppermute | solution.py:744
  415.2 53.7 %shard_map.184 = (bf16[4,2,128,2048]{3,2,1,0:T(8,128)(2,1)}, bf16[4,2,128,2048]{3,2,1,0:T(8,128)(2,1)}, bf16[8,2,128,2176]{3,2,1,0:T(8,128)(2,1)}, bf16[4,288,2048]{2,1,0:T(8,128)(2,1)}) custom-call(s32[3]{0:T(128)S(1)} %pad_add_fusion.where, f32[2,4,288,128]{3,2,1,0:T(8,128)} %copy-done.29, f32[2,4,288,2048]{3,2,1,0:T(8,128)} %get-tuple-element.276.both, ...), custom_call_target="tpu_custom_call" | custom-call | flops 217432719360 | tf_op jit(solution)/shard_map/pallas_call | solution.py:533
  469.0 31.0 %collective-permute-start.16 = (bf16[256,2048]{1,0:T(8,128)(2,1)}, bf16[256,2048]{1,0:T(8,128)(2,1)}, u32[]{:S(2)}, u32[]{:S(2)}) collective-permute-start(bf16[256,2048]{1,0:T(8,128)(2,1)} %get-tuple-element.295), channel_id=1, source_target_pairs={{0,8},{8,0},{16,24},{24,16},{1,9},{9,1},{17,25},{25,17},{2,10},{10... | collective-permute-start | bytes 3145736 | tf_op jit(solution)/shard_map/ppermute | solution.py:744
  500.4 43.9 %shard_map.185 = (bf16[4,2,128,2048]{3,2,1,0:T(8,128)(2,1)}, bf16[4,2,128,2048]{3,2,1,0:T(8,128)(2,1)}, bf16[8,2,128,2176]{3,2,1,0:T(8,128)(2,1)}, bf16[4,288,2048]{2,1,0:T(8,128)(2,1)}) custom-call(s32[3]{0:T(128)S(1)} %pad_add_fusion.where, f32[2,4,288,128]{3,2,1,0:T(8,128)} %copy-done.29, f32[2,4,288,2048]{3,2,1,0:T(8,128)} %get-tuple-element.276.both, ...), custom_call_target="tpu_custom_call" | custom-call | flops 217432719360 | tf_op jit(solution)/shard_map/pallas_call | solution.py:533
  568.1 24.2 %shard_map.187 = (bf16[512,2048]{1,0:T(8,128)(2,1)S(1)}, bf16[512,2048]{1,0:T(8,128)(2,1)}, bf16[512,2048]{1,0:T(8,128)(2,1)}) custom-call(s32[3]{0:T(128)S(1)} %pad_add_fusion.where, bf16[2304,2048]{1,0:T(8,128)(2,1)} %bitcast.160, bf16[1152,2048]{1,0:T(8,128)(2,1)} %bitcast.163, bf16[1152,2048]{1,0:T(8,128)(2,1)} %bitcast.166), custom_call_target="tpu_custom_call" | custom-call | flops 144955146240 | tf_op jit(solution)/shard_map/pallas_call | solution.py:595
  593.7 18.4 %collective-permute-done.18 = bf16[512,2048]{1,0:T(8,128)(2,1)} collective-permute-done((bf16[512,2048]{1,0:T(8,128)(2,1)}, bf16[512,2048]{1,0:T(8,128)(2,1)}, u32[]{:S(2)}, u32[]{:S(2)}) %collective-permute-start.18) | collective-permute-done | bytes 2097184 | tf_op jit(solution)/shard_map/ppermute | solution.py:740
  612.1 14.0 %collective-permute-done.19 = bf16[2,2,128,2048]{3,2,1,0:T(8,128)(2,1)} collective-permute-done((bf16[2,2,128,2048]{3,2,1,0:T(8,128)(2,1)}, bf16[2,2,128,2048]{3,2,1,0:T(8,128)(2,1)}, u32[]{:S(2)}, u32[]{:S(2)}) %collective-permute-start.19) | collective-permute-done | bytes 2097184 | tf_op jit(solution)/shard_map/ppermute | solution.py:893
  673.5 16.7 %shard_map.189 = (bf16[8,128,768]{2,1,0:T(8,128)(2,1)}, f32[2,128]{1,0:T(2,128)S(1)}) custom-call(f32[8,2,128,768]{3,2,1,0:T(8,128)} %bitcast.134, f32[2,1024,128]{2,1,0:T(8,128)S(1)} %copy-done.2, f32[2,1024,128]{2,1,0:T(8,128)S(1)} %copy-done.1, s32[2,1024,1]{2,1,0:T(8,128)S(1)} %copy-done.3, s32[2,1,1024]{2,1,0:T(1,128)S(1)} %copy-done.23, ...), custom_call_target="tpu_custom_call" | custom-call | tf_op jit(solution)/shard_map/pallas_call | solution.py:220
  762.9 18.0 %all-to-all-done.3 = bf16[128,8,256]{2,0,1:T(8,128)(2,1)} async-done(((bf16[128,8,256]{2,0,1:T(8,128)(2,1)}), bf16[128,8,256]{2,0,1:T(8,128)(2,1)}, u32[]{:S(2)}, u32[]{:S(2)}) %all-to-all-start.3) | async-done | bytes 524320 | tf_op jit(solution)/shard_map/all_to_all | solution.py:984
  783.7 16.7 %shard_map.192 = (bf16[8,128,768]{2,1,0:T(8,128)(2,1)}, f32[2,128]{1,0:T(2,128)S(1)}) custom-call(f32[8,2,128,768]{3,2,1,0:T(8,128)} %bitcast.135, f32[2,1024,128]{2,1,0:T(8,128)S(1)} %copy-done.2, f32[2,1024,128]{2,1,0:T(8,128)S(1)} %copy-done.1, s32[2,1024,1]{2,1,0:T(8,128)S(1)} %copy-done.4, s32[2,1,1024]{2,1,0:T(1,128)S(1)} %copy-done.23, ...), custom_call_target="tpu_custom_call" | custom-call | tf_op jit(solution)/shard_map/pallas_call | solution.py:220
  839.8 19.1 %collective-permute-done.27 = bf16[192,2048]{1,0:T(8,128)(2,1)} collective-permute-done((bf16[192,2048]{1,0:T(8,128)(2,1)}, bf16[192,2048]{1,0:T(8,128)(2,1)}, u32[]{:S(2)}, u32[]{:S(2)}) %collective-permute-start.27) | collective-permute-done | bytes 786464 | tf_op jit(solution)/shard_map/ppermute | solution.py:740
  905.6 16.9 %collective-permute-done.29 = bf16[512,896]{1,0:T(8,128)(2,1)} collective-permute-done((bf16[512,896]{1,0:T(8,128)(2,1)S(1)}, bf16[512,896]{1,0:T(8,128)(2,1)}, u32[]{:S(2)}, u32[]{:S(2)}) %collective-permute-start.29) | collective-permute-done | bytes 917536 | tf_op jit(solution)/shard_map/ppermute | solution.py:744
  931.7 18.1 %collective-permute-start.34 = (bf16[128,2048]{1,0:T(8,128)(2,1)}, bf16[128,2048]{1,0:T(8,128)(2,1)}, u32[]{:S(2)}, u32[]{:S(2)}) collective-permute-start(bf16[128,2048]{1,0:T(8,128)(2,1)} %fusion.19), channel_id=1, source_target_pairs={{0,8},{8,0},{16,24},{24,16},{1,9},{9,1},{17,25},{25,17},{2,10},{10... | collective-permute-start | bytes 1572872 | tf_op jit(solution)/shard_map/ppermute | solution.py:792
  (309 shorter events, 381.3 us)
Async XLA Ops:
  7.2 119.5 %all-gather.9.cloned.1.call-start = ((), (), s32[]{:S(2)}) async-start(), calls=%async_computation.15 | async-start | bytes 9437184 | tf_op jit(solution)/shard_map/all_gather | solution.py:798
  18.6 182.4 %all-gather.11.cloned.1.call-start = ((), (), s32[]{:S(2)}) async-start(), calls=%async_computation.16 | async-start | bytes 9437184 | tf_op jit(solution)/shard_map/all_gather | solution.py:798
  55.7 277.1 %all-gather.15.cloned.1.call-start = ((), (), s32[]{:S(2)}) async-start(), calls=%async_computation.18 | async-start | bytes 18874368 | tf_op jit(solution)/shard_map/all_gather | solution.py:798
  126.7 87.1 %collective-permute-start.7 = (bf16[512,2048]{1,0:T(8,128)(2,1)}, bf16[512,2048]{1,0:T(8,128)(2,1)}, u32[]{:S(2)}, u32[]{:S(2)}) collective-permute-start(bf16[512,2048]{1,0:T(8,128)(2,1)} %get-tuple-element.255), channel_id=1, source_target_pairs={{0,8},{8,0},{16,24},{24,16},{1,9},{9,1},{17,25},{25,17},{2,10},{10... | collective-permute-start | bytes 6291464 | tf_op jit(solution)/shard_map/ppermute | solution.py:744
  126.8 88.4 %collective-permute-start.8 = (bf16[512,2048]{1,0:T(8,128)(2,1)}, bf16[512,2048]{1,0:T(8,128)(2,1)}, u32[]{:S(2)}, u32[]{:S(2)}) collective-permute-start(bf16[512,2048]{1,0:T(8,128)(2,1)} %get-tuple-element.260.refs_0_), channel_id=1, source_target_pairs={{0,16},{8,24},{16,0},{24,8},{1,17},{9,25},{17,1},{25,9},{2,18},{10... | collective-permute-start | bytes 6291464 | tf_op jit(solution)/shard_map/ppermute | solution.py:744
  173.4 160.0 %all-gather.13.cloned.1.call-start = ((), (), s32[]{:S(2)}) async-start(), calls=%async_computation.17 | async-start | bytes 20054016 | tf_op jit(solution)/shard_map/all_gather | solution.py:798
  240.7 385.4 %reduce-scatter.6.cloned.1.call-start = ((), (), s32[]{:S(2)}) async-start(), calls=%async_computation.10 | async-start | bytes 10027008 | tf_op jit(solution)/shard_map/reduce_scatter | solution.py:919
  287.1 105.9 %collective-permute-start.11 = (bf16[256,2048]{1,0:T(8,128)(2,1)}, bf16[256,2048]{1,0:T(8,128)(2,1)}, u32[]{:S(2)}, u32[]{:S(2)}) collective-permute-start(bf16[256,2048]{1,0:T(8,128)(2,1)} %get-tuple-element.274), channel_id=1, source_target_pairs={{0,8},{8,0},{16,24},{24,16},{1,9},{9,1},{17,25},{25,17},{2,10},{10... | collective-permute-start | bytes 3145736 | tf_op jit(solution)/shard_map/ppermute | solution.py:744
  330.5 83.5 %collective-permute-start.12 = (bf16[256,2048]{1,0:T(8,128)(2,1)}, bf16[256,2048]{1,0:T(8,128)(2,1)}, u32[]{:S(2)}, u32[]{:S(2)}) collective-permute-start(bf16[256,2048]{1,0:T(8,128)(2,1)} %get-tuple-element.279.refs_4_), channel_id=1, source_target_pairs={{0,16},{8,24},{16,0},{24,8},{1,17},{9,25},{17,1},{25,9},{2,18},{10... | collective-permute-start | bytes 3145736 | tf_op jit(solution)/shard_map/ppermute | solution.py:744
  330.5 83.5 %collective-permute-start.13 = (bf16[256,2048]{1,0:T(8,128)(2,1)}, bf16[256,2048]{1,0:T(8,128)(2,1)}, u32[]{:S(2)}, u32[]{:S(2)}) collective-permute-start(bf16[256,2048]{1,0:T(8,128)(2,1)} %get-tuple-element.274), channel_id=1, source_target_pairs={{0,24},{8,16},{16,8},{24,0},{1,25},{9,17},{17,9},{25,1},{2,26},{10... | collective-permute-start | bytes 3145736 | tf_op jit(solution)/shard_map/ppermute | solution.py:744
  414.0 86.4 %collective-permute-start.15 = (bf16[256,2048]{1,0:T(8,128)(2,1)}, bf16[256,2048]{1,0:T(8,128)(2,1)}, u32[]{:S(2)}, u32[]{:S(2)}) collective-permute-start(bf16[256,2048]{1,0:T(8,128)(2,1)} %get-tuple-element.289), channel_id=1, source_target_pairs={{0,24},{8,16},{16,8},{24,0},{1,25},{9,17},{17,9},{25,1},{2,26},{10... | collective-permute-start | bytes 3145736 | tf_op jit(solution)/shard_map/ppermute | solution.py:744
  468.9 237.0 %reduce-scatter.8.cloned.1.call-start = ((), (), s32[]{:S(2)}) async-start(), calls=%async_computation.11 | async-start | bytes 10027008 | tf_op jit(solution)/shard_map/reduce_scatter | solution.py:919
  468.9 75.4 %collective-permute-start.14 = (bf16[4,2,128,2048]{3,2,1,0:T(8,128)(2,1)}, bf16[4,2,128,2048]{3,2,1,0:T(8,128)(2,1)}, u32[]{:S(2)}, u32[]{:S(2)}) collective-permute-start(bf16[4,2,128,2048]{3,2,1,0:T(8,128)(2,1)} %get-tuple-element.286), channel_id=1, source_target_pairs={{0,1},{1,0},{2,3},{3,2},{4,5},{5,4},{6,7},{7,6},{8,9},{9,8},{10,11... | collective-permute-start | bytes 12582920 | tf_op jit(solution)/shard_map/ppermute | solution.py:893
  469.0 124.7 %collective-permute-start.16 = (bf16[256,2048]{1,0:T(8,128)(2,1)}, bf16[256,2048]{1,0:T(8,128)(2,1)}, u32[]{:S(2)}, u32[]{:S(2)}) collective-permute-start(bf16[256,2048]{1,0:T(8,128)(2,1)} %get-tuple-element.295), channel_id=1, source_target_pairs={{0,8},{8,0},{16,24},{24,16},{1,9},{9,1},{17,25},{25,17},{2,10},{10... | collective-permute-start | bytes 3145736 | tf_op jit(solution)/shard_map/ppermute | solution.py:744
  500.0 93.7 %collective-permute-start.17 = (bf16[256,2048]{1,0:T(8,128)(2,1)}, bf16[256,2048]{1,0:T(8,128)(2,1)}, u32[]{:S(2)}, u32[]{:S(2)}) collective-permute-start(bf16[256,2048]{1,0:T(8,128)(2,1)} %get-tuple-element.296), channel_id=1, source_target_pairs={{0,16},{8,24},{16,0},{24,8},{1,17},{9,25},{17,1},{25,9},{2,18},{10... | collective-permute-start | bytes 3145736 | tf_op jit(solution)/shard_map/ppermute | solution.py:744
  566.1 59.9 %collective-permute-start.19 = (bf16[2,2,128,2048]{3,2,1,0:T(8,128)(2,1)}, bf16[2,2,128,2048]{3,2,1,0:T(8,128)(2,1)}, u32[]{:S(2)}, u32[]{:S(2)}) collective-permute-start(bf16[2,2,128,2048]{3,2,1,0:T(8,128)(2,1)} %get-tuple-element.470), channel_id=1, source_target_pairs={{0,2},{1,3},{2,0},{3,1},{4,6},{5,7},{6,4},{7,5},{8,10},{9,11},{10,... | collective-permute-start | bytes 6291464 | tf_op jit(solution)/shard_map/ppermute | solution.py:893
  662.5 143.8 %reduce-scatter.10.cloned.1.call-start = ((), (), s32[]{:S(2)}) async-start(), calls=%async_computation.12 | async-start | bytes 4718592 | tf_op jit(solution)/shard_map/reduce_scatter | solution.py:1009
  710.9 70.1 %collective-permute-start.25 = (bf16[2,2,128,2048]{3,2,1,0:T(8,128)(2,1)}, bf16[2,2,128,2048]{3,2,1,0:T(8,128)(2,1)}, u32[]{:S(2)}, u32[]{:S(2)}) collective-permute-start(bf16[2,2,128,2048]{3,2,1,0:T(8,128)(2,1)} %get-tuple-element.468), channel_id=1, source_target_pairs={{0,4},{1,5},{2,6},{3,7},{4,0},{5,1},{6,2},{7,3},{8,12},{9,13},{10,... | collective-permute-start | bytes 6291464 | tf_op jit(solution)/shard_map/ppermute | solution.py:893
  727.6 53.3 %collective-permute-start.24 = (bf16[192,2048]{1,0:T(8,128)(2,1)}, bf16[192,2048]{1,0:T(8,128)(2,1)}, u32[]{:S(2)}, u32[]{:S(2)}) collective-permute-start(bf16[192,2048]{1,0:T(8,128)(2,1)} %get-tuple-element.477), channel_id=1, source_target_pairs={{0,16},{8,24},{16,0},{24,8},{1,17},{9,25},{17,1},{25,9},{2,18},{10... | collective-permute-start | bytes 2359304 | tf_op jit(solution)/shard_map/ppermute | solution.py:740
  747.0 153.5 %reduce-scatter.12.cloned.1.call-start = ((), (), s32[]{:S(2)}) async-start(), calls=%async_computation.13 | async-start | bytes 4718592 | tf_op jit(solution)/shard_map/reduce_scatter | solution.py:1009
  821.7 134.9 %reduce-scatter.14.cloned.1.call-start = ((), (), s32[]{:S(2)}) async-start(), calls=%async_computation.14 | async-start | bytes 9437184 | tf_op jit(solution)/shard_map/reduce_scatter | solution.py:990
  858.9 63.7 %collective-permute-start.29 = (bf16[512,896]{1,0:T(8,128)(2,1)S(1)}, bf16[512,896]{1,0:T(8,128)(2,1)}, u32[]{:S(2)}, u32[]{:S(2)}) collective-permute-start(bf16[512,896]{1,0:T(8,128)(2,1)S(1)} %get-tuple-element.378), channel_id=1, source_target_pairs={{0,16},{8,24},{16,0},{24,8},{1,17},{9,25},{17,1},{25,9},{2,18},{10... | collective-permute-start | bytes 2752520 | tf_op jit(solution)/shard_map/ppermute | solution.py:744
  860.6 61.9 %collective-permute-start.30 = (bf16[512,896]{1,0:T(8,128)(2,1)}, bf16[512,896]{1,0:T(8,128)(2,1)}, u32[]{:S(2)}, u32[]{:S(2)}) collective-permute-start(bf16[512,896]{1,0:T(8,128)(2,1)} %get-tuple-element.379), channel_id=1, source_target_pairs={{0,24},{8,16},{16,8},{24,0},{1,25},{9,17},{17,9},{25,1},{2,26},{10... | collective-permute-start | bytes 2752520 | tf_op jit(solution)/shard_map/ppermute | solution.py:744
  896.1 67.9 %collective-permute-start.32 = (bf16[128,2048]{1,0:T(8,128)(2,1)}, bf16[128,2048]{1,0:T(8,128)(2,1)}, u32[]{:S(2)}, u32[]{:S(2)}) collective-permute-start(bf16[128,2048]{1,0:T(8,128)(2,1)} %fusion.18), channel_id=1, source_target_pairs={{0,8},{8,0},{16,24},{24,16},{1,9},{9,1},{17,25},{25,17},{2,10},{10... | collective-permute-start | bytes 1572872 | tf_op jit(solution)/shard_map/ppermute | solution.py:792
  (79 other events, 2277.0 us)
Sparse Core Ops, SparseCore 0:
  9.9 64.3 all-gather.8
  76.8 54.3 all-gather.10
  133.1 101.0 all-gather.14
  240.8 92.4 all-gather.12
  469.0 104.7 reduce-scatter.5
  577.2 84.4 reduce-scatter.7
  705.9 71.9 reduce-scatter.9
  821.8 53.1 reduce-scatter.11
  878.4 78.1 reduce-scatter.13

commit v13 on v12

--- a/solution.py
+++ b/solution.py
@@ -888,30 +888,9 @@
         )
 
     tail, out_cut, out_pieces = lax.optimization_barrier((tail, out_cut, out_pieces))
-    out_sent = send(out_cut, range(1, planes))
-    def swap(value, step):
-        return lax.ppermute(value, "ep", [(i, i ^ step) for i in range(ranks)])
-
-    def pair_sum(keep, give):
-        return (keep.astype(f32) + swap(give, 1).astype(f32)).astype(bf16)
-
-    bits = list(range((ranks // 2).bit_length() - 1))
-
-    def halve(number, value, phase):
-        way = bits if number % 2 == 0 else bits[::-1]
-        bit = way[phase]
-        low = 2 ** sum(other < bit for other in way[phase:])
-        value = value.reshape((-1, 2, low) + value.shape[1:])
-        side = rank // 2 // 2**bit % 2
-        keep, give = (
-            lax.dynamic_index_in_dim(value, which, 1, keepdims=False).reshape((-1,) + value.shape[3:])
-            for which in (side, 1 - side)
-        )
-        return keep, swap(give, 2 * 2**bit)
-
-    def total(parts):
-        return sum(part.astype(f32) for part in parts)
-
+    first = cross_rep(out_cut[1][:16], 1)
+    tail, out_cut, first = lax.optimization_barrier((tail, out_cut, first))
+    out_sent = send([out_cut[0], out_cut[1][16:], *out_cut[2:]], range(1, planes))
     back = []
     returned = []
 
@@ -933,9 +912,7 @@
             tail, out_sent[last_step] = after((tail, out_sent[last_step]), back[step][2])
         else:
             tail = after(tail, back[step][2])
-    early = [pair_sum(*part[:2]) for part in back[:-1]]
-    rows_in, tail, early = lax.optimization_barrier((rows_in, tail, early))
-    crossed = [halve(number, value, 0) for number, value in enumerate(early)]
+    rows_in = after(rows_in, tail)
     rows_flat = rows_in.reshape(in_rows, D)
     grads_flat = [back[step][3].reshape(in_rows // micro, 2 * FF) for step in range(micro)]
     (in_near,) = weight_gradient(
@@ -951,22 +928,54 @@
         ends = [-(-value.shape[0] * place // 512) * 16 for place in (0, *places, 32)]
         return [value[start:end] for start, end in zip(ends, ends[1:])]
 
+    def swap(value, step):
+        return lax.ppermute(value, "ep", [(i, i ^ step) for i in range(ranks)])
+
+    bits = list(range((ranks // 2).bit_length() - 1))
+
+    def cut_pairs(number, value, phase):
+        way = bits if number % 2 == 0 else bits[::-1]
+        bit = way[phase]
+        low = 2 ** sum(other < bit for other in way[phase:])
+        value = value.reshape((-1, 2, low) + value.shape[1:])
+        side = rank // 2 // 2**bit % 2
+        return [
+            lax.dynamic_index_in_dim(value, which, 1, keepdims=False).reshape((-1,) + value.shape[3:])
+            for which in (side, 1 - side)
+        ]
+
+    def pair_sum(number, keep, give):
+        got = swap(give, 1)
+        return [
+            total(parts).astype(bf16)
+            for parts in zip(cut_pairs(number, keep, 0), cut_pairs(number, got, 0))
+        ]
+
+    def halve(number, halves, phase):
+        return halves[0], swap(halves[1], 2 * 2 ** (bits if number % 2 == 0 else bits[::-1])[phase])
+
+    def total(parts):
+        return sum(part.astype(f32) for part in parts)
+
     grad_inputs, branches, logit_grads, grad_projs = [], [], [], []
     gain_two_sum = gain_one_sum = qk_sum = 0.0
-    in_rest, in_back, out_sent, in_sent, crossed = lax.optimization_barrier(
-        (in_rest, in_back, out_sent, in_sent, crossed)
-    )
-    late = back[-1][:2]
+    in_rest, in_back, out_sent, in_sent = lax.optimization_barrier(
+        (in_rest, in_back, out_sent, in_sent)
+    )
+    mixtures = [part[:2] for part in back]
     for step in range(micro):
         at = slice(step * rows, (step + 1) * rows)
         parts = after(returned[step], [one[1] for one in grad_inputs])
         parts, in_sent = lax.optimization_barrier((parts, in_sent))
         if step == micro - 1:
-            crossed.append(halve(step, after(late, parts), 0))
+            mixtures = after(mixtures, parts)
+            crossed = [halve(number, value, 0) for number, value in enumerate(mixtures)]
         parts = exchange_back(parts)
-        parts, in_rest, in_back, late = lax.optimization_barrier((parts, in_rest, in_back, late))
+        parts, in_rest, in_back, mixtures = lax.optimization_barrier(
+            (parts, in_rest, in_back, mixtures)
+        )
         if step == 0:
-            late = pair_sum(*late)
+            mixtures = [pair_sum(number, *part) for number, part in enumerate(mixtures)]
             in_sent[last_step] = shift_rep(in_back, last_step)
         if step == micro - 1:
             rest = [cuts(value, 12, 20) for value in in_rest]
@@ -982,10 +991,10 @@
             out_sum = dot(mixed, jnp.concatenate(branches, axis=0), ((0,), (0,))).astype(bf16)
             out_sum = out_sum.reshape(planes, ranks, dense_rows, D).transpose(1, 0, 2, 3)
         grad_mixed = lax.all_to_all(grad_mixed, "ep", split_axis=1, concat_axis=0, tiled=True)
-        grad_mixed, late = lax.optimization_barrier((grad_mixed, late))
+        grad_mixed, mixtures = lax.optimization_barrier((grad_mixed, mixtures))
         if step == micro - 1:
-            grad_mixed, rest_sent, rest, out_sum, crossed = lax.optimization_barrier(
-                (grad_mixed, rest_sent, rest, out_sum, crossed)
+            grad_mixed, crossed, rest_sent, rest, out_sum = lax.optimization_barrier(
+                (grad_mixed, crossed, rest_sent, rest, out_sum)
             )
             out_sum = lax.psum_scatter(out_sum, "ep", scatter_dimension=0)
             rest_sent.append([shift_rep(part[1], i + 2) for i, part in enumerate(rest)])
@@ -1060,7 +1069,10 @@
     packed_sent, grad_tokens = lax.optimization_barrier((packed_sent, grad_tokens))
     for phase in range(1, len(bits)):
         mixtures = [total(parts).astype(bf16) for parts in crossed]
-        crossed = [halve(number, value, phase) for number, value in enumerate(mixtures)]
+        crossed = [
+            halve(number, cut_pairs(number, value, phase), phase)
+            for number, value in enumerate(mixtures)
+        ]
     mixture = []
     for number in range(micro):
         parts = total(crossed[number])[0]
@@ -1079,6 +1091,7 @@
     output = (hidden + output).astype(bf16)
     grad_w_o = total([own_sum, *out_sent_back])
     grad_w_qkv, small = unpack(packed, count)
+    out_sent[1] = jnp.concatenate([first, out_sent[1]], axis=0)
     grad_w_out = sum_rep({0: out_cut[0], **out_sent})
     for i in range(planes - 3):
         in_sent[i + 2] = jnp.concatenate([parts[i] for parts in rest_sent], axis=0)

time: 1010 us -> 952 us (0.943)
  waiting for transfers between devices: 354 us -> 323 us
  Pallas kernels: 333 us -> 321 us
  starting transfers between devices: 153 us -> 142 us
    ppermute x6, waiting for transfers between devices: 21.8 us -> 7.89 us  [swap(): return lax.ppermute(value, 'ep', [(i, i ^ step) for i in range(ranks)])]
    pallas_call x2, Pallas kernels: 97.6 us -> 85.4 us  [expert_backward(): pl.pallas_call(kernel, grid_spec=pltpu.PrefetchScalarGridSpec(num_scalar_...]
    ppermute x18 -> x19, waiting for transfers between devices: 114 us -> 103 us  [cross_rep(): lax.ppermute(value, 'rep', [(i, i ^ bits) for i in range(lax.axis_size('r...]
    ppermute x18 -> x19, starting transfers between devices: 91.7 us -> 82.9 us  [cross_rep(): lax.ppermute(value, 'rep', [(i, i ^ bits) for i in range(lax.axis_size('r...]
  transfers between devices with their start and end apart: 52 -> 53, of which waited for: 29 -> 28; matrix products, arithmetic and copies ran while one was open for 12% -> 12% of each run, Pallas kernels for 32% -> 32%
where the time goes in v13:
time: 952 us; the launch traced here: 942 us
  waiting for transfers between devices  323 us (34%)
  Pallas kernels  321 us (34%)
  starting transfers between devices  142 us (15%)
  local copies, waits for them, and re-layouts  66.8 us (7%)
  other arithmetic  65.9 us (7%)
  between operations  15.2 us (2%)
    ppermute x19, waiting for transfers between devices, cross_rep(): lax.ppermute(value, 'rep', [(i, i ^ bits) for i in range(lax.axis_size('r...  103 us
    ppermute x8, waiting for transfers between devices, shift_rep(): lax.ppermute(value, 'rep', [(i, (i + step) % count) for i in range(count)])  91 us
    pallas_call x2, Pallas kernels, expert_backward(): pl.pallas_call(kernel, grid_spec=pltpu.PrefetchScalarGridSpec(num_scalar_...  85.4 us
    ppermute x19, starting transfers between devices, cross_rep(): lax.ppermute(value, 'rep', [(i, i ^ bits) for i in range(lax.axis_size('r...  82.9 us
    ppermute x6, waiting for transfers between devices, exchange(): return lax.ppermute(value, 'rep', pairs)  68.6 us
    pallas_call x4, Pallas kernels, weight_gradient(): pl.pallas_call(kernel, grid_spec=pltpu.PrefetchScalarGridSpec(num_scalar_...  65.7 us
    pallas_call x1, Pallas kernels, expert_forward(): pl.pallas_call(kernel, grid_spec=pltpu.PrefetchScalarGridSpec(num_scalar_...  40.4 us
    pallas_call x2, Pallas kernels, attention_backward(): pl.pallas_call(lambda *refs: backward_kernel(heads, *refs), grid=(1,), in...  33.5 us
  transfers between devices with their start and end apart: 53, of which 28 were waited for; matrix products, arithmetic and copies ran while one was open for 12% of the time, Pallas kernels for 32%

profile of v13, /device:TPU:0, one launch (start us, length us, event | category | flops | bytes accessed | tf_op | source)
XLA Modules:
  0.0 942.2 jit_solution(15191671794759982297)
XLA Ops:
  23.1 17.7 %collective-permute-done.3 = bf16[256,2048]{1,0:T(8,128)(2,1)S(1)} collective-permute-done((bf16[256,2048]{1,0:T(8,128)(2,1)}, bf16[256,2048]{1,0:T(8,128)(2,1)S(1)}, u32[]{:S(2)}, u32[]{:S(2)}) %collective-permute-start.3) | collective-permute-done | bytes 1048608 | tf_op jit(solution)/shard_map/ppermute | solution.py:792
  57.5 22.5 %collective-permute-done.4 = bf16[512,896]{1,0:T(8,128)(2,1)S(1)} collective-permute-done((bf16[512,896]{1,0:T(8,128)(2,1)S(1)}, bf16[512,896]{1,0:T(8,128)(2,1)S(1)}, u32[]{:S(2)}, u32[]{:S(2)}) %collective-permute-start.4) | collective-permute-done | bytes 917536 | tf_op jit(solution)/shard_map/ppermute | solution.py:740
  108.6 17.1 %collective-permute-done.6 = bf16[512,896]{1,0:T(8,128)(2,1)S(1)} collective-permute-done((bf16[512,896]{1,0:T(8,128)(2,1)}, bf16[512,896]{1,0:T(8,128)(2,1)S(1)}, u32[]{:S(2)}, u32[]{:S(2)}) %collective-permute-start.6) | collective-permute-done | bytes 917536 | tf_op jit(solution)/shard_map/ppermute | solution.py:740
  129.9 15.9 %shard_map.179 = (bf16[2,8,128,2048]{3,2,1,0:T(8,128)(2,1)}, f32[8,256,768]{2,1,0:T(8,128)}) custom-call(bf16[8,256,2048]{2,1,0:T(8,128)(2,1)} %bitcast.140, f32[1,2048]{1,0:T(1,128)S(1)} %broadcast_in_dim.56.gain, bf16[2048,896]{1,0:T(8,128)(2,1)} %constant_dynamic-update-slice_fusion.weight), custom_call_target="tpu_custom_call" | custom-call | tf_op jit(solution)/shard_map/pallas_call | solution.py:248
  145.8 21.7 %shard_map.180 = (bf16[8,2,128,256]{3,2,1,0:T(8,128)(2,1)}, bf16[2,1024,256]{2,1,0:T(8,128)(2,1)S(1)}, bf16[2,1024,256]{2,1,0:T(8,128)(2,1)S(1)}, bf16[2,1024,256]{2,1,0:T(8,128)(2,1)}, f32[2,2,1024,1]{3,2,1,0:T(8,128)}) custom-call(f32[8,2,128,768]{3,2,1,0:T(8,128)} %bitcast.143, f32[2,1024,128]{2,1,0:T(8,128)} %get-tuple-element.234.refs_1_, ...), custom_call_target="tpu_custom_call" | custom-call | tf_op jit(solution)/shard_map/pallas_call | solution.py:198
  175.3 24.7 %all-to-all-done.1 = bf16[8,2,128,256]{3,2,1,0:T(8,128)(2,1)S(1)} async-done(((bf16[8,2,128,256]{3,2,1,0:T(8,128)(2,1)}), bf16[8,2,128,256]{3,2,1,0:T(8,128)(2,1)S(1)}, u32[]{:S(2)}, u32[]{:S(2)}) %all-to-all-start.1) | async-done | bytes 1048608 | tf_op jit(solution)/shard_map/all_to_all | solution.py:850
  215.6 23.6 %collective-permute-done.9 = bf16[256,2176]{1,0:T(8,128)(2,1)S(1)} collective-permute-done((bf16[256,2176]{1,0:T(8,128)(2,1)S(1)}, bf16[256,2176]{1,0:T(8,128)(2,1)S(1)}, u32[]{:S(2)}, u32[]{:S(2)}) %collective-permute-start.9) | collective-permute-done | bytes 1114144 | tf_op jit(solution)/shard_map/ppermute | solution.py:792
  241.1 46.3 %collective-permute-done.10.refs_3_ = bf16[512,2048]{1,0:T(8,128)(2,1)} collective-permute-done((bf16[512,2048]{1,0:T(8,128)(2,1)}, bf16[512,2048]{1,0:T(8,128)(2,1)}, u32[]{:S(2)}, u32[]{:S(2)}) %collective-permute-start.10) | collective-permute-done | bytes 2097184 | tf_op jit(solution)/shard_map/ppermute | solution.py:744
  287.4 43.2 %collective-permute-start.11 = (bf16[256,2048]{1,0:T(8,128)(2,1)}, bf16[256,2048]{1,0:T(8,128)(2,1)}, u32[]{:S(2)}, u32[]{:S(2)}) collective-permute-start(bf16[256,2048]{1,0:T(8,128)(2,1)} %get-tuple-element.284), channel_id=1, source_target_pairs={{0,8},{8,0},{16,24},{24,16},{1,9},{9,1},{17,25},{25,17},{2,10},{10... | collective-permute-start | bytes 3145736 | tf_op jit(solution)/shard_map/ppermute | solution.py:744
  333.4 40.4 %shard_map.182 = (bf16[2,4,288,2048]{3,2,1,0:T(8,128)(2,1)}, f32[2,4,288,128]{3,2,1,0:T(8,128)S(1)}, f32[2,4,288,2048]{3,2,1,0:T(8,128)}, bf16[2,4,288,1024]{3,2...) custom-call(s32[3]{0:T(128)S(1)} %pad_add_fusion.where, ...), custom_call_target="tpu_custom_call" | custom-call | flops 241591910400 | tf_op jit(solution)/shard_map/pallas_call | solution.py:435
  375.2 16.2 %shard_map.183 = (bf16[256,2048]{1,0:T(8,128)(2,1)S(1)}, bf16[256,2048]{1,0:T(8,128)(2,1)S(1)}, bf16[256,2048]{1,0:T(8,128)(2,1)S(1)}, bf16[256,2048]{1,0:T(8,128)(2,1)}) custom-call(s32[3]{0:T(128)S(1)} %pad_add_fusion.where, bf16[2304,1024]{1,0:T(8,128)(2,1)} %bitcast.172, bf16[2304,2048]{1,0:T(8,128)(2,1)} %bitcast.171), custom_call_target="tpu_custom_call" | custom-call | flops 96636764160 | tf_op jit(solution)/shard_map/pallas_call | solution.py:595
  402.8 19.5 %collective-permute-start.14 = (bf16[16,2048]{1,0:T(8,128)(2,1)S(1)}, bf16[16,2048]{1,0:T(8,128)(2,1)S(1)}, u32[]{:S(2)}, u32[]{:S(2)}) collective-permute-start(bf16[16,2048]{1,0:T(8,128)(2,1)S(1)} %slice.167), channel_id=1, source_target_pairs={{0,8},{8,0},{16,24},{24,16},{1,9},{9,1},{17,25},{25,17},{2,10},{10... | collective-permute-start | bytes 196616 | tf_op jit(solution)/shard_map/ppermute | solution.py:744
  426.9 41.1 %shard_map.184 = (bf16[4,2,128,2048]{3,2,1,0:T(8,128)(2,1)}, bf16[4,2,128,2048]{3,2,1,0:T(8,128)(2,1)}, bf16[8,2,128,2176]{3,2,1,0:T(8,128)(2,1)}, bf16[4,288,2048]{2,1,0:T(8,128)(2,1)}) custom-call(s32[3]{0:T(128)S(1)} %pad_add_fusion.where, f32[2,4,288,128]{3,2,1,0:T(8,128)} %copy-done.32, f32[2,4,288,2048]{3,2,1,0:T(8,128)} %get-tuple-element.291.both, ...), custom_call_target="tpu_custom_call" | custom-call | flops 217432719360 | tf_op jit(solution)/shard_map/pallas_call | solution.py:533
  472.5 44.3 %shard_map.185 = (bf16[4,2,128,2048]{3,2,1,0:T(8,128)(2,1)}, bf16[4,2,128,2048]{3,2,1,0:T(8,128)(2,1)}, bf16[8,2,128,2176]{3,2,1,0:T(8,128)(2,1)}, bf16[4,288,2048]{2,1,0:T(8,128)(2,1)}) custom-call(s32[3]{0:T(128)S(1)} %pad_add_fusion.where, f32[2,4,288,128]{3,2,1,0:T(8,128)} %copy-done.32, f32[2,4,288,2048]{3,2,1,0:T(8,128)} %get-tuple-element.291.both, ...), custom_call_target="tpu_custom_call" | custom-call | flops 217432719360 | tf_op jit(solution)/shard_map/pallas_call | solution.py:533
  530.5 24.6 %shard_map.187 = (bf16[512,2048]{1,0:T(8,128)(2,1)S(1)}, bf16[512,2048]{1,0:T(8,128)(2,1)}, bf16[512,2048]{1,0:T(8,128)(2,1)}) custom-call(s32[3]{0:T(128)S(1)} %pad_add_fusion.where, bf16[2304,2048]{1,0:T(8,128)(2,1)} %bitcast.170, bf16[1152,2048]{1,0:T(8,128)(2,1)} %bitcast.174, bf16[1152,2048]{1,0:T(8,128)(2,1)} %bitcast.176), custom_call_target="tpu_custom_call" | custom-call | flops 144955146240 | tf_op jit(solution)/shard_map/pallas_call | solution.py:595
  556.5 17.6 %collective-permute-done.18 = bf16[512,2048]{1,0:T(8,128)(2,1)} collective-permute-done((bf16[512,2048]{1,0:T(8,128)(2,1)}, bf16[512,2048]{1,0:T(8,128)(2,1)}, u32[]{:S(2)}, u32[]{:S(2)}) %collective-permute-start.18) | collective-permute-done | bytes 2097184 | tf_op jit(solution)/shard_map/ppermute | solution.py:740
  623.4 16.8 %shard_map.189 = (bf16[8,128,768]{2,1,0:T(8,128)(2,1)}, f32[2,128]{1,0:T(2,128)S(1)}) custom-call(f32[8,2,128,768]{3,2,1,0:T(8,128)} %bitcast.144, f32[2,1024,128]{2,1,0:T(8,128)S(1)} %copy-done.2, f32[2,1024,128]{2,1,0:T(8,128)S(1)} %copy-done.1, s32[2,1024,1]{2,1,0:T(8,128)S(1)} %copy-done.3, s32[2,1,1024]{2,1,0:T(1,128)S(1)} %copy-done.25, ...), custom_call_target="tpu_custom_call" | custom-call | tf_op jit(solution)/shard_map/pallas_call | solution.py:220
  641.6 13.9 %shard_map.190 = (bf16[1024,2048]{1,0:T(8,128)(2,1)}, f32[1,2048]{1,0:T(1,128)S(1)}) custom-call(bf16[8,128,768]{2,1,0:T(8,128)(2,1)S(1)} %copy-done.8, bf16[8,256,2048]{2,1,0:T(8,128)(2,1)} %bitcast.141, bf16[2048,896]{1,0:T(8,128)(2,1)} %constant_dynamic-update-slice_fusion.weight), custom_call_target="tpu_custom_call" | custom-call | tf_op jit(solution)/shard_map/pallas_call | solution.py:685
  708.7 18.6 %all-to-all-done.3 = bf16[128,8,256]{2,0,1:T(8,128)(2,1)} async-done(((bf16[128,8,256]{2,0,1:T(8,128)(2,1)}), bf16[128,8,256]{2,0,1:T(8,128)(2,1)}, u32[]{:S(2)}, u32[]{:S(2)}) %all-to-all-start.3) | async-done | bytes 524320 | tf_op jit(solution)/shard_map/all_to_all | solution.py:993
  729.6 16.7 %shard_map.192 = (bf16[8,128,768]{2,1,0:T(8,128)(2,1)}, f32[2,128]{1,0:T(2,128)S(1)}) custom-call(f32[8,2,128,768]{3,2,1,0:T(8,128)} %bitcast.145, f32[2,1024,128]{2,1,0:T(8,128)S(1)} %copy-done.2, f32[2,1024,128]{2,1,0:T(8,128)S(1)} %copy-done.1, s32[2,1024,1]{2,1,0:T(8,128)S(1)} %copy-done.4, s32[2,1,1024]{2,1,0:T(1,128)S(1)} %copy-done.25, ...), custom_call_target="tpu_custom_call" | custom-call | tf_op jit(solution)/shard_map/pallas_call | solution.py:220
  753.3 13.9 %shard_map.193 = (bf16[1024,2048]{1,0:T(8,128)(2,1)}, f32[1,2048]{1,0:T(1,128)S(1)}) custom-call(bf16[8,128,768]{2,1,0:T(8,128)(2,1)S(1)} %copy-done.9, bf16[8,256,2048]{2,1,0:T(8,128)(2,1)} %bitcast.142, bf16[2048,896]{1,0:T(8,128)(2,1)} %constant_dynamic-update-slice_fusion.weight), custom_call_target="tpu_custom_call" | custom-call | tf_op jit(solution)/shard_map/pallas_call | solution.py:685
  785.2 16.9 %collective-permute-done.28 = bf16[192,2048]{1,0:T(8,128)(2,1)} collective-permute-done((bf16[192,2048]{1,0:T(8,128)(2,1)}, bf16[192,2048]{1,0:T(8,128)(2,1)}, u32[]{:S(2)}, u32[]{:S(2)}) %collective-permute-start.28) | collective-permute-done | bytes 786464 | tf_op jit(solution)/shard_map/ppermute | solution.py:740
  850.4 15.7 %collective-permute-done.30 = bf16[512,896]{1,0:T(8,128)(2,1)} collective-permute-done((bf16[512,896]{1,0:T(8,128)(2,1)S(1)}, bf16[512,896]{1,0:T(8,128)(2,1)}, u32[]{:S(2)}, u32[]{:S(2)}) %collective-permute-start.30) | collective-permute-done | bytes 917536 | tf_op jit(solution)/shard_map/ppermute | solution.py:744
  875.8 19.0 %collective-permute-start.35 = (bf16[128,2048]{1,0:T(8,128)(2,1)}, bf16[128,2048]{1,0:T(8,128)(2,1)S(1)}, u32[]{:S(2)}, u32[]{:S(2)}) collective-permute-start(bf16[128,2048]{1,0:T(8,128)(2,1)} %fusion.23), channel_id=1, source_target_pairs={{0,8},{8,0},{16,24},{24,16},{1,9},{9,1},{17,25},{25,17},{2,10},{10... | collective-permute-start | bytes 1572872 | tf_op jit(solution)/shard_map/ppermute | solution.py:792
  (319 shorter events, 359.0 us)
Async XLA Ops:
  7.2 119.5 %all-gather.9.cloned.1.call-start = ((), (), s32[]{:S(2)}) async-start(), calls=%async_computation.15 | async-start | bytes 9437184 | tf_op jit(solution)/shard_map/all_gather | solution.py:798
  18.6 182.3 %all-gather.11.cloned.1.call-start = ((), (), s32[]{:S(2)}) async-start(), calls=%async_computation.16 | async-start | bytes 9437184 | tf_op jit(solution)/shard_map/all_gather | solution.py:798
  55.7 277.2 %all-gather.15.cloned.1.call-start = ((), (), s32[]{:S(2)}) async-start(), calls=%async_computation.18 | async-start | bytes 18874368 | tf_op jit(solution)/shard_map/all_gather | solution.py:798
  126.7 87.3 %collective-permute-start.7 = (bf16[512,2048]{1,0:T(8,128)(2,1)}, bf16[512,2048]{1,0:T(8,128)(2,1)}, u32[]{:S(2)}, u32[]{:S(2)}) collective-permute-start(bf16[512,2048]{1,0:T(8,128)(2,1)} %get-tuple-element.265), channel_id=1, source_target_pairs={{0,8},{8,0},{16,24},{24,16},{1,9},{9,1},{17,25},{25,17},{2,10},{10... | collective-permute-start | bytes 6291464 | tf_op jit(solution)/shard_map/ppermute | solution.py:744
  126.7 88.4 %collective-permute-start.8 = (bf16[512,2048]{1,0:T(8,128)(2,1)}, bf16[512,2048]{1,0:T(8,128)(2,1)}, u32[]{:S(2)}, u32[]{:S(2)}) collective-permute-start(bf16[512,2048]{1,0:T(8,128)(2,1)} %get-tuple-element.270.refs_0_), channel_id=1, source_target_pairs={{0,16},{8,24},{16,0},{24,8},{1,17},{9,25},{17,1},{25,9},{2,18},{10... | collective-permute-start | bytes 6291464 | tf_op jit(solution)/shard_map/ppermute | solution.py:744
  173.3 160.2 %all-gather.13.cloned.1.call-start = ((), (), s32[]{:S(2)}) async-start(), calls=%async_computation.17 | async-start | bytes 20054016 | tf_op jit(solution)/shard_map/all_gather | solution.py:798
  240.8 333.2 %reduce-scatter.6.cloned.1.call-start = ((), (), s32[]{:S(2)}) async-start(), calls=%async_computation.10 | async-start | bytes 10027008 | tf_op jit(solution)/shard_map/reduce_scatter | solution.py:898
  287.4 105.1 %collective-permute-start.11 = (bf16[256,2048]{1,0:T(8,128)(2,1)}, bf16[256,2048]{1,0:T(8,128)(2,1)}, u32[]{:S(2)}, u32[]{:S(2)}) collective-permute-start(bf16[256,2048]{1,0:T(8,128)(2,1)} %get-tuple-element.284), channel_id=1, source_target_pairs={{0,8},{8,0},{16,24},{24,16},{1,9},{9,1},{17,25},{25,17},{2,10},{10... | collective-permute-start | bytes 3145736 | tf_op jit(solution)/shard_map/ppermute | solution.py:744
  330.5 72.3 %collective-permute-start.12 = (bf16[256,2048]{1,0:T(8,128)(2,1)}, bf16[256,2048]{1,0:T(8,128)(2,1)}, u32[]{:S(2)}, u32[]{:S(2)}) collective-permute-start(bf16[256,2048]{1,0:T(8,128)(2,1)} %get-tuple-element.294.refs_4_), channel_id=1, source_target_pairs={{0,16},{8,24},{16,0},{24,8},{1,17},{9,25},{17,1},{25,9},{2,18},{10... | collective-permute-start | bytes 3145736 | tf_op jit(solution)/shard_map/ppermute | solution.py:744
  330.5 72.3 %collective-permute-start.13 = (bf16[256,2048]{1,0:T(8,128)(2,1)}, bf16[256,2048]{1,0:T(8,128)(2,1)}, u32[]{:S(2)}, u32[]{:S(2)}) collective-permute-start(bf16[256,2048]{1,0:T(8,128)(2,1)} %get-tuple-element.284), channel_id=1, source_target_pairs={{0,24},{8,16},{16,8},{24,0},{1,25},{9,17},{17,9},{25,1},{2,26},{10... | collective-permute-start | bytes 3145736 | tf_op jit(solution)/shard_map/ppermute | solution.py:744
  468.1 187.5 %reduce-scatter.8.cloned.1.call-start = ((), (), s32[]{:S(2)}) async-start(), calls=%async_computation.11 | async-start | bytes 10027008 | tf_op jit(solution)/shard_map/reduce_scatter | solution.py:898
  470.3 86.1 %collective-permute-start.16 = (bf16[240,2048]{1,0:T(8,128)(2,1)}, bf16[240,2048]{1,0:T(8,128)(2,1)}, u32[]{:S(2)}, u32[]{:S(2)}) collective-permute-start(bf16[240,2048]{1,0:T(8,128)(2,1)} %slice.168), channel_id=1, source_target_pairs={{0,8},{8,0},{16,24},{24,16},{1,9},{9,1},{17,25},{25,17},{2,10},{10... | collective-permute-start | bytes 2949128 | tf_op jit(solution)/shard_map/ppermute | solution.py:744
  471.9 84.5 %collective-permute-start.17 = (bf16[256,2048]{1,0:T(8,128)(2,1)}, bf16[256,2048]{1,0:T(8,128)(2,1)}, u32[]{:S(2)}, u32[]{:S(2)}) collective-permute-start(bf16[256,2048]{1,0:T(8,128)(2,1)} %copy-done.30), channel_id=1, source_target_pairs={{0,16},{8,24},{16,0},{24,8},{1,17},{9,25},{17,1},{25,9},{2,18},{10... | collective-permute-start | bytes 3145736 | tf_op jit(solution)/shard_map/ppermute | solution.py:744
  585.5 54.7 %collective-permute-start.22 = (bf16[512,2048]{1,0:T(8,128)(2,1)}, bf16[512,2048]{1,0:T(8,128)(2,1)}, u32[]{:S(2)}, u32[]{:S(2)}) collective-permute-start(bf16[512,2048]{1,0:T(8,128)(2,1)} %get-tuple-element.333), channel_id=1, source_target_pairs={{0,24},{8,0},{16,8},{24,16},{1,25},{9,1},{17,9},{25,17},{2,26},{10... | collective-permute-start | bytes 6291464 | tf_op jit(solution)/shard_map/ppermute | solution.py:740
  606.5 145.4 %reduce-scatter.10.cloned.1.call-start = ((), (), s32[]{:S(2)}) async-start(), calls=%async_computation.12 | async-start | bytes 4718592 | tf_op jit(solution)/shard_map/reduce_scatter | solution.py:1018
  655.6 71.6 %collective-permute-start.24 = (bf16[2,2,128,2048]{3,2,1,0:T(8,128)(2,1)}, bf16[2,2,128,2048]{3,2,1,0:T(8,128)(2,1)}, u32[]{:S(2)}, u32[]{:S(2)}) collective-permute-start(bf16[2,2,128,2048]{3,2,1,0:T(8,128)(2,1)} %get-tuple-element.348), channel_id=1, source_target_pairs={{0,2},{1,3},{2,0},{3,1},{4,6},{5,7},{6,4},{7,5},{8,10},{9,11},{10,... | collective-permute-start | bytes 6291464 | tf_op jit(solution)/shard_map/ppermute | solution.py:932
  657.1 70.1 %collective-permute-start.25 = (bf16[2,2,128,2048]{3,2,1,0:T(8,128)(2,1)}, bf16[2,2,128,2048]{3,2,1,0:T(8,128)(2,1)}, u32[]{:S(2)}, u32[]{:S(2)}) collective-permute-start(bf16[2,2,128,2048]{3,2,1,0:T(8,128)(2,1)} %get-tuple-element.350), channel_id=1, source_target_pairs={{0,4},{1,5},{2,6},{3,7},{4,0},{5,1},{6,2},{7,3},{8,12},{9,13},{10,... | collective-permute-start | bytes 6291464 | tf_op jit(solution)/shard_map/ppermute | solution.py:932
  675.3 51.9 %collective-permute-start.26 = (bf16[192,2048]{1,0:T(8,128)(2,1)}, bf16[192,2048]{1,0:T(8,128)(2,1)}, u32[]{:S(2)}, u32[]{:S(2)}) collective-permute-start(bf16[192,2048]{1,0:T(8,128)(2,1)} %get-tuple-element.497), channel_id=1, source_target_pairs={{0,16},{8,24},{16,0},{24,8},{1,17},{9,25},{17,1},{25,9},{2,18},{10... | collective-permute-start | bytes 2359304 | tf_op jit(solution)/shard_map/ppermute | solution.py:740
  692.7 152.5 %reduce-scatter.12.cloned.1.call-start = ((), (), s32[]{:S(2)}) async-start(), calls=%async_computation.13 | async-start | bytes 4718592 | tf_op jit(solution)/shard_map/reduce_scatter | solution.py:1018
  767.2 133.6 %reduce-scatter.14.cloned.1.call-start = ((), (), s32[]{:S(2)}) async-start(), calls=%async_computation.14 | async-start | bytes 9437184 | tf_op jit(solution)/shard_map/reduce_scatter | solution.py:999
  802.1 48.2 %collective-permute-start.29 = (bf16[512,896]{1,0:T(8,128)(2,1)}, bf16[512,896]{1,0:T(8,128)(2,1)}, u32[]{:S(2)}, u32[]{:S(2)}) collective-permute-start(bf16[512,896]{1,0:T(8,128)(2,1)} %get-tuple-element.396), channel_id=1, source_target_pairs={{0,8},{8,0},{16,24},{24,16},{1,9},{9,1},{17,25},{25,17},{2,10},{10... | collective-permute-start | bytes 2752520 | tf_op jit(solution)/shard_map/ppermute | solution.py:744
  802.2 63.9 %collective-permute-start.30 = (bf16[512,896]{1,0:T(8,128)(2,1)S(1)}, bf16[512,896]{1,0:T(8,128)(2,1)}, u32[]{:S(2)}, u32[]{:S(2)}) collective-permute-start(bf16[512,896]{1,0:T(8,128)(2,1)S(1)} %get-tuple-element.397), channel_id=1, source_target_pairs={{0,16},{8,24},{16,0},{24,8},{1,17},{9,25},{17,1},{25,9},{2,18},{10... | collective-permute-start | bytes 2752520 | tf_op jit(solution)/shard_map/ppermute | solution.py:744
  805.4 60.7 %collective-permute-start.31 = (bf16[512,896]{1,0:T(8,128)(2,1)}, bf16[512,896]{1,0:T(8,128)(2,1)}, u32[]{:S(2)}, u32[]{:S(2)}) collective-permute-start(bf16[512,896]{1,0:T(8,128)(2,1)} %get-tuple-element.398), channel_id=1, source_target_pairs={{0,24},{8,16},{16,8},{24,0},{1,25},{9,17},{17,9},{25,1},{2,26},{10... | collective-permute-start | bytes 2752520 | tf_op jit(solution)/shard_map/ppermute | solution.py:744
  840.9 67.3 %collective-permute-start.33 = (bf16[128,2048]{1,0:T(8,128)(2,1)}, bf16[128,2048]{1,0:T(8,128)(2,1)}, u32[]{:S(2)}, u32[]{:S(2)}) collective-permute-start(bf16[128,2048]{1,0:T(8,128)(2,1)} %fusion.22), channel_id=1, source_target_pairs={{0,8},{8,0},{16,24},{24,16},{1,9},{9,1},{17,25},{25,17},{2,10},{10... | collective-permute-start | bytes 1572872 | tf_op jit(solution)/shard_map/ppermute | solution.py:792
  (84 other events, 2188.9 us)
Sparse Core Ops, SparseCore 0:
  9.9 64.3 all-gather.8
  76.8 54.3 all-gather.10
  133.1 101.0 all-gather.14
  241.0 92.4 all-gather.12
  468.2 73.0 reduce-scatter.5
  544.8 79.4 reduce-scatter.7
  655.7 66.9 reduce-scatter.9
  767.3 52.2 reduce-scatter.11
  823.1 77.6 reduce-scatter.13

commit v14 on v13

--- a/solution.py
+++ b/solution.py
@@ -612,9 +612,10 @@
 
 
 def hidden_backward(
-    plane, planes, parts, hidden, gates, upstream, gain, router, gathered, experts
+    step, plane, planes, parts, hidden, gates, upstream, gain, router, gathered, experts
 ):
-    count = hidden.shape[0]
+    first = parts[0].shape
+    count = first[1]
     terms = len(parts)
 
     def kernel(plane, *refs):
@@ -624,7 +625,7 @@
             grad_hidden, grad_branch, grad_mixed, grad_logits, grad_gain, out_weight, sems
         ) = refs[terms + 6 :]
         wait = copies(out_weight_pairs(plane[0], planes, gathered, out_weight), sems)
-        returned = sum(part[...].astype(f32) for part in parts)
+        returned = sum(part[...].astype(f32) for part in parts[1:]) + parts[0][0].astype(f32)
         tail = returned[:, D:]
         grad_gates = gates[...] * (tail + pltpu.roll(tail, PAD - experts, 1))
         logits = grad_gates - gates[...] * jnp.sum(grad_gates, axis=1, keepdims=True)
@@ -649,12 +650,22 @@
         out((1, D), f32),
     ]
     args = (*parts, hidden, gates, upstream, gain, router, gathered)
+
+    def spec(value):
+        if value is gathered:
+            return HBM
+        if value is parts[0]:
+            return pl.BlockSpec((1,) + first[1:], lambda *_: (0, 0, 0))
+        if any(value is rows for rows in (hidden, gates, upstream)):
+            return pl.BlockSpec((count, value.shape[1]), lambda *_: (step, 0))
+        return fixed(value.shape)
+
     return pl.pallas_call(
         kernel,
         grid_spec=pltpu.PrefetchScalarGridSpec(
             num_scalar_prefetch=1,
             grid=(1,),
-            in_specs=[HBM if value is gathered else fixed(value.shape) for value in args],
+            in_specs=[spec(value) for value in args],
             out_specs=[fixed(shape.shape) for shape in shapes],
             scratch_shapes=[
                 pltpu.VMEM((D, D), bf16),
@@ -671,9 +682,9 @@
     width = slab.shape[1] - PAD
 
     def kernel(grad_proj, tokens, weight, grad_normed, grad_gain):
-        value = tokens[0].astype(f32)
+        value = tokens[...].reshape(2 * rows, D).astype(f32)
         inverse = inverse_rms(value)
-        grad = dot(grad_proj[0], weight[:, :width], ((1,), (1,)))
+        grad = dot(grad_proj[...].reshape(2 * rows, width), weight[:, :width], ((1,), (1,)))
         grad_normed[...] = grad.astype(bf16)
 
         @pl.when(pl.program_id(0) == 0)
@@ -684,13 +695,13 @@
 
     return pl.pallas_call(
         kernel,
-        grid=(ranks,),
+        grid=(ranks // 2,),
         in_specs=[
-            leading(grad_proj.shape),
-            pl.BlockSpec((1, rows, D), lambda i: (i, step, 0)),
+            pl.BlockSpec((2, rows, width), lambda i: (i, 0, 0)),
+            pl.BlockSpec((2, rows, D), lambda i: (i, step, 0)),
             fixed(slab.shape),
         ],
-        out_specs=[pl.BlockSpec((rows, D), lambda i: (i, 0)), fixed((1, D))],
+        out_specs=[pl.BlockSpec((2 * rows, D), lambda i: (i, 0)), fixed((1, D))],
         out_shape=[out((ranks * rows, D)), out((1, D), f32)],
         compiler_params=params(),
     )(grad_proj, tokens, slab)
@@ -898,7 +909,7 @@
         return lax.psum_scatter(value, "ep", scatter_dimension=0)
 
     def exchange_back(value):
-        return [value[0]] + [exchange(value[step], share - step) for step in range(1, share)]
+        return [value] + [exchange(value[step], share - step) for step in range(1, share)]
 
     for step in range(micro):
         back.append(
@@ -964,7 +975,6 @@
     )
     mixtures = [part[:2] for part in back]
     for step in range(micro):
-        at = slice(step * rows, (step + 1) * rows)
         parts = after(returned[step], [one[1] for one in grad_inputs])
         parts, in_sent = lax.optimization_barrier((parts, in_sent))
         if step == micro - 1:
@@ -978,11 +988,11 @@
             mixtures = [pair_sum(number, *part) for number, part in enumerate(mixtures)]
             in_sent[last_step] = shift_rep(in_back, last_step)
         if step == micro - 1:
-            rest = [cuts(value, 12, 20) for value in in_rest]
+            rest = [cuts(value, 20, 28) for value in in_rest]
             rest_sent = [[shift_rep(part[0], i + 2) for i, part in enumerate(rest)]]
         grad_hidden, grad_branch, grad_mixed, grad_logits, gain_two = hidden_backward(
-            where[1:2], planes, parts, hidden[at], gates[at], cotangent[at], second_gain,
-            router, gathered, experts,
+            step, where[1:2], planes, parts, hidden, gates, cotangent, second_gain, router, gathered,
+            experts,
         )
         branches.append(grad_branch)
         logit_grads.append(grad_logits)

time: 952 us -> 962 us (1.011)
  waiting for transfers between devices: 323 us -> 344 us
  Pallas kernels: 321 us -> 311 us
    reduce_scatter x1, waiting for transfers between devices: 5.97 us -> 35.5 us  [on_device(): out_sum = lax.psum_scatter(out_sum, 'ep', scatter_dimension=0)]
    ppermute x6, waiting for transfers between devices: 7.89 us -> 17.8 us  [swap(): return lax.ppermute(value, 'ep', [(i, i ^ step) for i in range(ranks)])]
    unnamed x115 -> x111, local copies, waits for them, and re-layouts: 17.4 us -> 20.3 us
where the time goes in v14:
time: 962 us; the launch traced here: 951 us
  waiting for transfers between devices  344 us (36%)
  Pallas kernels  311 us (32%)
  starting transfers between devices  140 us (15%)
  local copies, waits for them, and re-layouts  69.1 us (7%)
  other arithmetic  64.3 us (7%)
  between operations  15.2 us (2%)
    ppermute x19, waiting for transfers between devices, cross_rep(): lax.ppermute(value, 'rep', [(i, i ^ bits) for i in range(lax.axis_size('r...  104 us
    pallas_call x2, Pallas kernels, expert_backward(): pl.pallas_call(kernel, grid_spec=pltpu.PrefetchScalarGridSpec(num_scalar_...  85.4 us
    ppermute x8, waiting for transfers between devices, shift_rep(): lax.ppermute(value, 'rep', [(i, (i + step) % count) for i in range(count)])  83.4 us
    ppermute x19, starting transfers between devices, cross_rep(): lax.ppermute(value, 'rep', [(i, i ^ bits) for i in range(lax.axis_size('r...  83.4 us
    pallas_call x4, Pallas kernels, weight_gradient(): pl.pallas_call(kernel, grid_spec=pltpu.PrefetchScalarGridSpec(num_scalar_...  66 us
    ppermute x6, waiting for transfers between devices, exchange(): return lax.ppermute(value, 'rep', pairs)  62.9 us
    pallas_call x1, Pallas kernels, expert_forward(): pl.pallas_call(kernel, grid_spec=pltpu.PrefetchScalarGridSpec(num_scalar_...  40.4 us
    reduce_scatter x1, waiting for transfers between devices, on_device(): out_sum = lax.psum_scatter(out_sum, 'ep', scatter_dimension=0)  35.5 us
  transfers between devices with their start and end apart: 53, of which 28 were waited for; matrix products, arithmetic and copies ran while one was open for 12% of the time, Pallas kernels for 32%

profile of v14, /device:TPU:0, one launch (start us, length us, event | category | flops | bytes accessed | tf_op | source)
XLA Modules:
  0.0 951.4 jit_solution(12415668354790179369)
XLA Ops:
  23.1 17.7 %collective-permute-done.3 = bf16[256,2048]{1,0:T(8,128)(2,1)S(1)} collective-permute-done((bf16[256,2048]{1,0:T(8,128)(2,1)}, bf16[256,2048]{1,0:T(8,128)(2,1)S(1)}, u32[]{:S(2)}, u32[]{:S(2)}) %collective-permute-start.3) | collective-permute-done | bytes 1048608 | tf_op jit(solution)/shard_map/ppermute | solution.py:803
  57.5 22.5 %collective-permute-done.4 = bf16[512,896]{1,0:T(8,128)(2,1)S(1)} collective-permute-done((bf16[512,896]{1,0:T(8,128)(2,1)S(1)}, bf16[512,896]{1,0:T(8,128)(2,1)S(1)}, u32[]{:S(2)}, u32[]{:S(2)}) %collective-permute-start.4) | collective-permute-done | bytes 917536 | tf_op jit(solution)/shard_map/ppermute | solution.py:751
  108.5 17.1 %collective-permute-done.6 = bf16[512,896]{1,0:T(8,128)(2,1)S(1)} collective-permute-done((bf16[512,896]{1,0:T(8,128)(2,1)}, bf16[512,896]{1,0:T(8,128)(2,1)S(1)}, u32[]{:S(2)}, u32[]{:S(2)}) %collective-permute-start.6) | collective-permute-done | bytes 917536 | tf_op jit(solution)/shard_map/ppermute | solution.py:751
  129.9 15.9 %shard_map.179 = (bf16[2,8,128,2048]{3,2,1,0:T(8,128)(2,1)}, f32[8,256,768]{2,1,0:T(8,128)}) custom-call(bf16[8,256,2048]{2,1,0:T(8,128)(2,1)} %bitcast.136, f32[1,2048]{1,0:T(1,128)S(1)} %broadcast_in_dim.56.gain, bf16[2048,896]{1,0:T(8,128)(2,1)} %constant_dynamic-update-slice_fusion.weight), custom_call_target="tpu_custom_call" | custom-call | tf_op jit(solution)/shard_map/pallas_call | solution.py:248
  145.7 21.7 %shard_map.180 = (bf16[8,2,128,256]{3,2,1,0:T(8,128)(2,1)}, bf16[2,1024,256]{2,1,0:T(8,128)(2,1)S(1)}, bf16[2,1024,256]{2,1,0:T(8,128)(2,1)S(1)}, bf16[2,1024,256]{2,1,0:T(8,128)(2,1)}, f32[2,2,1024,1]{3,2,1,0:T(8,128)}) custom-call(f32[8,2,128,768]{3,2,1,0:T(8,128)} %bitcast.139, f32[2,1024,128]{2,1,0:T(8,128)} %get-tuple-element.234.refs_1_, ...), custom_call_target="tpu_custom_call" | custom-call | tf_op jit(solution)/shard_map/pallas_call | solution.py:198
  175.3 24.7 %all-to-all-done.1 = bf16[8,2,128,256]{3,2,1,0:T(8,128)(2,1)S(1)} async-done(((bf16[8,2,128,256]{3,2,1,0:T(8,128)(2,1)}), bf16[8,2,128,256]{3,2,1,0:T(8,128)(2,1)S(1)}, u32[]{:S(2)}, u32[]{:S(2)}) %all-to-all-start.1) | async-done | bytes 1048608 | tf_op jit(solution)/shard_map/all_to_all | solution.py:861
  215.6 23.6 %collective-permute-done.9 = bf16[256,2176]{1,0:T(8,128)(2,1)S(1)} collective-permute-done((bf16[256,2176]{1,0:T(8,128)(2,1)S(1)}, bf16[256,2176]{1,0:T(8,128)(2,1)S(1)}, u32[]{:S(2)}, u32[]{:S(2)}) %collective-permute-start.9) | collective-permute-done | bytes 1114144 | tf_op jit(solution)/shard_map/ppermute | solution.py:803
  241.1 46.4 %collective-permute-done.10.refs_3_ = bf16[512,2048]{1,0:T(8,128)(2,1)} collective-permute-done((bf16[512,2048]{1,0:T(8,128)(2,1)}, bf16[512,2048]{1,0:T(8,128)(2,1)}, u32[]{:S(2)}, u32[]{:S(2)}) %collective-permute-start.10) | collective-permute-done | bytes 2097184 | tf_op jit(solution)/shard_map/ppermute | solution.py:755
  287.5 43.1 %collective-permute-start.11 = (bf16[256,2048]{1,0:T(8,128)(2,1)}, bf16[256,2048]{1,0:T(8,128)(2,1)}, u32[]{:S(2)}, u32[]{:S(2)}) collective-permute-start(bf16[256,2048]{1,0:T(8,128)(2,1)} %get-tuple-element.284), channel_id=1, source_target_pairs={{0,8},{8,0},{16,24},{24,16},{1,9},{9,1},{17,25},{25,17},{2,10},{10... | collective-permute-start | bytes 3145736 | tf_op jit(solution)/shard_map/ppermute | solution.py:755
  333.5 40.4 %shard_map.182 = (bf16[2,4,288,2048]{3,2,1,0:T(8,128)(2,1)}, f32[2,4,288,128]{3,2,1,0:T(8,128)S(1)}, f32[2,4,288,2048]{3,2,1,0:T(8,128)}, bf16[2,4,288,1024]{3,2...) custom-call(s32[3]{0:T(128)S(1)} %pad_add_fusion.where, ...), custom_call_target="tpu_custom_call" | custom-call | flops 241591910400 | tf_op jit(solution)/shard_map/pallas_call | solution.py:435
  375.2 16.2 %shard_map.183 = (bf16[256,2048]{1,0:T(8,128)(2,1)S(1)}, bf16[256,2048]{1,0:T(8,128)(2,1)S(1)}, bf16[256,2048]{1,0:T(8,128)(2,1)S(1)}, bf16[256,2048]{1,0:T(8,128)(2,1)}) custom-call(s32[3]{0:T(128)S(1)} %pad_add_fusion.where, bf16[2304,1024]{1,0:T(8,128)(2,1)} %bitcast.170, bf16[2304,2048]{1,0:T(8,128)(2,1)} %bitcast.169), custom_call_target="tpu_custom_call" | custom-call | flops 96636764160 | tf_op jit(solution)/shard_map/pallas_call | solution.py:595
  402.9 19.5 %collective-permute-start.14 = (bf16[16,2048]{1,0:T(8,128)(2,1)S(1)}, bf16[16,2048]{1,0:T(8,128)(2,1)S(1)}, u32[]{:S(2)}, u32[]{:S(2)}) collective-permute-start(bf16[16,2048]{1,0:T(8,128)(2,1)S(1)} %slice.143), channel_id=1, source_target_pairs={{0,8},{8,0},{16,24},{24,16},{1,9},{9,1},{17,25},{25,17},{2,10},{10... | collective-permute-start | bytes 196616 | tf_op jit(solution)/shard_map/ppermute | solution.py:755
  426.9 41.1 %shard_map.184 = (bf16[4,2,128,2048]{3,2,1,0:T(8,128)(2,1)}, bf16[4,2,128,2048]{3,2,1,0:T(8,128)(2,1)}, bf16[8,2,128,2176]{3,2,1,0:T(8,128)(2,1)}, bf16[4,288,2048]{2,1,0:T(8,128)(2,1)}) custom-call(s32[3]{0:T(128)S(1)} %pad_add_fusion.where, f32[2,4,288,128]{3,2,1,0:T(8,128)} %copy-done.34, f32[2,4,288,2048]{3,2,1,0:T(8,128)} %get-tuple-element.291.both, ...), custom_call_target="tpu_custom_call" | custom-call | flops 217432719360 | tf_op jit(solution)/shard_map/pallas_call | solution.py:533
  472.5 44.3 %shard_map.185 = (bf16[4,2,128,2048]{3,2,1,0:T(8,128)(2,1)}, bf16[4,2,128,2048]{3,2,1,0:T(8,128)(2,1)}, bf16[8,2,128,2176]{3,2,1,0:T(8,128)(2,1)}, bf16[4,288,2048]{2,1,0:T(8,128)(2,1)}) custom-call(s32[3]{0:T(128)S(1)} %pad_add_fusion.where, f32[2,4,288,128]{3,2,1,0:T(8,128)} %copy-done.34, f32[2,4,288,2048]{3,2,1,0:T(8,128)} %get-tuple-element.291.both, ...), custom_call_target="tpu_custom_call" | custom-call | flops 217432719360 | tf_op jit(solution)/shard_map/pallas_call | solution.py:533
  530.5 24.6 %shard_map.187 = (bf16[512,2048]{1,0:T(8,128)(2,1)S(1)}, bf16[512,2048]{1,0:T(8,128)(2,1)}, bf16[512,2048]{1,0:T(8,128)(2,1)}) custom-call(s32[3]{0:T(128)S(1)} %pad_add_fusion.where, bf16[2304,2048]{1,0:T(8,128)(2,1)} %bitcast.168, bf16[1152,2048]{1,0:T(8,128)(2,1)} %bitcast.172, bf16[1152,2048]{1,0:T(8,128)(2,1)} %bitcast.174), custom_call_target="tpu_custom_call" | custom-call | flops 144955146240 | tf_op jit(solution)/shard_map/pallas_call | solution.py:595
  556.5 17.7 %collective-permute-done.18 = bf16[512,2048]{1,0:T(8,128)(2,1)} collective-permute-done((bf16[512,2048]{1,0:T(8,128)(2,1)}, bf16[512,2048]{1,0:T(8,128)(2,1)}, u32[]{:S(2)}, u32[]{:S(2)}) %collective-permute-start.18) | collective-permute-done | bytes 2097184 | tf_op jit(solution)/shard_map/ppermute | solution.py:751
  619.7 16.8 %shard_map.189 = (bf16[8,128,768]{2,1,0:T(8,128)(2,1)}, f32[2,128]{1,0:T(2,128)S(1)}) custom-call(f32[8,2,128,768]{3,2,1,0:T(8,128)} %bitcast.140, f32[2,1024,128]{2,1,0:T(8,128)S(1)} %copy-done.2, f32[2,1024,128]{2,1,0:T(8,128)S(1)} %copy-done.1, s32[2,1024,1]{2,1,0:T(8,128)S(1)} %copy-done.3, s32[2,1,1024]{2,1,0:T(1,128)S(1)} %copy-done.27, ...), custom_call_target="tpu_custom_call" | custom-call | tf_op jit(solution)/shard_map/pallas_call | solution.py:220
  652.4 13.2 %collective-permute-done.23.refs_1_ = bf16[128,2176]{1,0:T(8,128)(2,1)S(1)} collective-permute-done((bf16[128,2176]{1,0:T(8,128)(2,1)S(1)}, bf16[128,2176]{1,0:T(8,128)(2,1)S(1)}, u32[]{:S(2)}, u32[]{:S(2)}) %collective-permute-start.23) | collective-permute-done | bytes 557088 | tf_op jit(solution)/shard_map/ppermute | solution.py:803
  705.3 13.8 %all-to-all-done.3 = bf16[128,8,256]{2,0,1:T(8,128)(2,1)} async-done(((bf16[128,8,256]{2,0,1:T(8,128)(2,1)}), bf16[128,8,256]{2,0,1:T(8,128)(2,1)}, u32[]{:S(2)}, u32[]{:S(2)}) %all-to-all-start.3) | async-done | bytes 524320 | tf_op jit(solution)/shard_map/all_to_all | solution.py:1003
  728.1 16.8 %shard_map.192 = (bf16[8,128,768]{2,1,0:T(8,128)(2,1)}, f32[2,128]{1,0:T(2,128)S(1)}) custom-call(f32[8,2,128,768]{3,2,1,0:T(8,128)} %bitcast.141, f32[2,1024,128]{2,1,0:T(8,128)S(1)} %copy-done.2, f32[2,1024,128]{2,1,0:T(8,128)S(1)} %copy-done.1, s32[2,1024,1]{2,1,0:T(8,128)S(1)} %copy-done.4, s32[2,1,1024]{2,1,0:T(1,128)S(1)} %copy-done.27, ...), custom_call_target="tpu_custom_call" | custom-call | tf_op jit(solution)/shard_map/pallas_call | solution.py:220
  766.5 13.0 %shard_map.194 = (bf16[512,896]{1,0:T(8,128)(2,1)S(1)}, bf16[512,896]{1,0:T(8,128)(2,1)}, bf16[512,896]{1,0:T(8,128)(2,1)}, bf16[512,896]{1,0:T(8,128)(2,1)}) custom-call(s32[3]{0:T(128)S(1)} %pad_add_fusion.where, bf16[2048,2048]{1,0:T(8,128)(2,1)} %bitcast.145, bf16[1024,768]{1,0:T(8,128)(2,1)} %bitcast.127, bf16[1024,768]{1,0:T(8,128)(2,1)} %bitcast.128, ...), custom_call_target="tpu_custom_call" | custom-call | tf_op jit(solution)/shard_map/pallas_call | solution.py:595
  806.6 17.7 %collective-permute-done.32 = bf16[1,2,128,2048]{3,2,1,0:T(8,128)(2,1)S(1)} collective-permute-done((bf16[1,2,128,2048]{3,2,1,0:T(8,128)(2,1)}, bf16[1,2,128,2048]{3,2,1,0:T(8,128)(2,1)S(1)}, u32[]{:S(2)}, u32[]{:S(2)}) %collective-permute-start.32) | collective-permute-done | bytes 1048608 | tf_op jit(solution)/shard_map/ppermute | solution.py:943
  855.4 18.9 %collective-permute-start.35 = (bf16[128,2048]{1,0:T(8,128)(2,1)}, bf16[128,2048]{1,0:T(8,128)(2,1)S(1)}, u32[]{:S(2)}, u32[]{:S(2)}) collective-permute-start(bf16[128,2048]{1,0:T(8,128)(2,1)} %fusion.23), channel_id=1, source_target_pairs={{0,8},{8,0},{16,24},{24,16},{1,9},{9,1},{17,25},{25,17},{2,10},{10... | collective-permute-start | bytes 1572872 | tf_op jit(solution)/shard_map/ppermute | solution.py:803
  874.3 35.5 %reduce-scatter.14.cloned.1.call-done = bf16[1,4,64,2048]{3,2,1,0:T(8,128)(2,1)} async-done(((bf16[8,4,64,2048]{3,2,1,0:T(8,128)(2,1)}), bf16[1,4,64,2048]{3,2,1,0:T(8,128)(2,1)}) %reduce-scatter.14.cloned.1.call-update) | async-done | bytes 1048592 | tf_op jit(solution)/shard_map/reduce_scatter | solution.py:1009
  (313 shorter events, 354.0 us)
Async XLA Ops:
  7.2 119.5 %all-gather.9.cloned.1.call-start = ((), (), s32[]{:S(2)}) async-start(), calls=%async_computation.15 | async-start | bytes 9437184 | tf_op jit(solution)/shard_map/all_gather | solution.py:809
  18.6 182.3 %all-gather.11.cloned.1.call-start = ((), (), s32[]{:S(2)}) async-start(), calls=%async_computation.16 | async-start | bytes 9437184 | tf_op jit(solution)/shard_map/all_gather | solution.py:809
  55.7 277.2 %all-gather.15.cloned.1.call-start = ((), (), s32[]{:S(2)}) async-start(), calls=%async_computation.18 | async-start | bytes 18874368 | tf_op jit(solution)/shard_map/all_gather | solution.py:809
  126.7 87.3 %collective-permute-start.7 = (bf16[512,2048]{1,0:T(8,128)(2,1)}, bf16[512,2048]{1,0:T(8,128)(2,1)}, u32[]{:S(2)}, u32[]{:S(2)}) collective-permute-start(bf16[512,2048]{1,0:T(8,128)(2,1)} %get-tuple-element.265), channel_id=1, source_target_pairs={{0,8},{8,0},{16,24},{24,16},{1,9},{9,1},{17,25},{25,17},{2,10},{10... | collective-permute-start | bytes 6291464 | tf_op jit(solution)/shard_map/ppermute | solution.py:755
  126.7 88.4 %collective-permute-start.8 = (bf16[512,2048]{1,0:T(8,128)(2,1)}, bf16[512,2048]{1,0:T(8,128)(2,1)}, u32[]{:S(2)}, u32[]{:S(2)}) collective-permute-start(bf16[512,2048]{1,0:T(8,128)(2,1)} %get-tuple-element.270.refs_0_), channel_id=1, source_target_pairs={{0,16},{8,24},{16,0},{24,8},{1,17},{9,25},{17,1},{25,9},{2,18},{10... | collective-permute-start | bytes 6291464 | tf_op jit(solution)/shard_map/ppermute | solution.py:755
  173.3 160.2 %all-gather.13.cloned.1.call-start = ((), (), s32[]{:S(2)}) async-start(), calls=%async_computation.17 | async-start | bytes 20054016 | tf_op jit(solution)/shard_map/all_gather | solution.py:809
  240.9 333.3 %reduce-scatter.6.cloned.1.call-start = ((), (), s32[]{:S(2)}) async-start(), calls=%async_computation.10 | async-start | bytes 10027008 | tf_op jit(solution)/shard_map/reduce_scatter | solution.py:909
  287.5 105.9 %collective-permute-start.11 = (bf16[256,2048]{1,0:T(8,128)(2,1)}, bf16[256,2048]{1,0:T(8,128)(2,1)}, u32[]{:S(2)}, u32[]{:S(2)}) collective-permute-start(bf16[256,2048]{1,0:T(8,128)(2,1)} %get-tuple-element.284), channel_id=1, source_target_pairs={{0,8},{8,0},{16,24},{24,16},{1,9},{9,1},{17,25},{25,17},{2,10},{10... | collective-permute-start | bytes 3145736 | tf_op jit(solution)/shard_map/ppermute | solution.py:755
  330.6 72.3 %collective-permute-start.12 = (bf16[256,2048]{1,0:T(8,128)(2,1)}, bf16[256,2048]{1,0:T(8,128)(2,1)}, u32[]{:S(2)}, u32[]{:S(2)}) collective-permute-start(bf16[256,2048]{1,0:T(8,128)(2,1)} %get-tuple-element.294.refs_4_), channel_id=1, source_target_pairs={{0,16},{8,24},{16,0},{24,8},{1,17},{9,25},{17,1},{25,9},{2,18},{10... | collective-permute-start | bytes 3145736 | tf_op jit(solution)/shard_map/ppermute | solution.py:755
  330.6 72.3 %collective-permute-start.13 = (bf16[256,2048]{1,0:T(8,128)(2,1)}, bf16[256,2048]{1,0:T(8,128)(2,1)}, u32[]{:S(2)}, u32[]{:S(2)}) collective-permute-start(bf16[256,2048]{1,0:T(8,128)(2,1)} %get-tuple-element.284), channel_id=1, source_target_pairs={{0,24},{8,16},{16,8},{24,0},{1,25},{9,17},{17,9},{25,1},{2,26},{10... | collective-permute-start | bytes 3145736 | tf_op jit(solution)/shard_map/ppermute | solution.py:755
  468.1 179.0 %reduce-scatter.8.cloned.1.call-start = ((), (), s32[]{:S(2)}) async-start(), calls=%async_computation.11 | async-start | bytes 10027008 | tf_op jit(solution)/shard_map/reduce_scatter | solution.py:909
  470.3 86.2 %collective-permute-start.16 = (bf16[240,2048]{1,0:T(8,128)(2,1)}, bf16[240,2048]{1,0:T(8,128)(2,1)}, u32[]{:S(2)}, u32[]{:S(2)}) collective-permute-start(bf16[240,2048]{1,0:T(8,128)(2,1)} %slice.144), channel_id=1, source_target_pairs={{0,8},{8,0},{16,24},{24,16},{1,9},{9,1},{17,25},{25,17},{2,10},{10... | collective-permute-start | bytes 2949128 | tf_op jit(solution)/shard_map/ppermute | solution.py:755
  471.9 84.6 %collective-permute-start.17 = (bf16[256,2048]{1,0:T(8,128)(2,1)}, bf16[256,2048]{1,0:T(8,128)(2,1)}, u32[]{:S(2)}, u32[]{:S(2)}) collective-permute-start(bf16[256,2048]{1,0:T(8,128)(2,1)} %copy-done.32), channel_id=1, source_target_pairs={{0,16},{8,24},{16,0},{24,8},{1,17},{9,25},{17,1},{25,9},{2,18},{10... | collective-permute-start | bytes 3145736 | tf_op jit(solution)/shard_map/ppermute | solution.py:755
  603.0 148.5 %reduce-scatter.10.cloned.1.call-start = ((), (), s32[]{:S(2)}) async-start(), calls=%async_computation.12 | async-start | bytes 4718592 | tf_op jit(solution)/shard_map/reduce_scatter | solution.py:1028
  647.2 79.7 %collective-permute-start.24 = (bf16[2,2,128,2048]{3,2,1,0:T(8,128)(2,1)}, bf16[2,2,128,2048]{3,2,1,0:T(8,128)(2,1)}, u32[]{:S(2)}, u32[]{:S(2)}) collective-permute-start(bf16[2,2,128,2048]{3,2,1,0:T(8,128)(2,1)} %get-tuple-element.348), channel_id=1, source_target_pairs={{0,2},{1,3},{2,0},{3,1},{4,6},{5,7},{6,4},{7,5},{8,10},{9,11},{10,... | collective-permute-start | bytes 6291464 | tf_op jit(solution)/shard_map/ppermute | solution.py:943
  648.8 78.0 %collective-permute-start.25 = (bf16[2,2,128,2048]{3,2,1,0:T(8,128)(2,1)}, bf16[2,2,128,2048]{3,2,1,0:T(8,128)(2,1)}, u32[]{:S(2)}, u32[]{:S(2)}) collective-permute-start(bf16[2,2,128,2048]{3,2,1,0:T(8,128)(2,1)} %get-tuple-element.350), channel_id=1, source_target_pairs={{0,4},{1,5},{2,6},{3,7},{4,0},{5,1},{6,2},{7,3},{8,12},{9,13},{10,... | collective-permute-start | bytes 6291464 | tf_op jit(solution)/shard_map/ppermute | solution.py:943
  668.1 58.7 %collective-permute-start.26 = (bf16[320,2048]{1,0:T(8,128)(2,1)}, bf16[320,2048]{1,0:T(8,128)(2,1)}, u32[]{:S(2)}, u32[]{:S(2)}) collective-permute-start(bf16[320,2048]{1,0:T(8,128)(2,1)} %slice.147), channel_id=1, source_target_pairs={{0,16},{8,24},{16,0},{24,8},{1,17},{9,25},{17,1},{25,9},{2,18},{10... | collective-permute-start | bytes 3932168 | tf_op jit(solution)/shard_map/ppermute | solution.py:751
  689.7 140.1 %reduce-scatter.12.cloned.1.call-start = ((), (), s32[]{:S(2)}) async-start(), calls=%async_computation.13 | async-start | bytes 4718592 | tf_op jit(solution)/shard_map/reduce_scatter | solution.py:1028
  762.1 147.6 %reduce-scatter.14.cloned.1.call-start = ((), (), s32[]{:S(2)}) async-start(), calls=%async_computation.14 | async-start | bytes 9437184 | tf_op jit(solution)/shard_map/reduce_scatter | solution.py:1009
  782.4 63.9 %collective-permute-start.30 = (bf16[512,896]{1,0:T(8,128)(2,1)}, bf16[512,896]{1,0:T(8,128)(2,1)}, u32[]{:S(2)}, u32[]{:S(2)}) collective-permute-start(bf16[512,896]{1,0:T(8,128)(2,1)} %get-tuple-element.397), channel_id=1, source_target_pairs={{0,16},{8,24},{16,0},{24,8},{1,17},{9,25},{17,1},{25,9},{2,18},{10... | collective-permute-start | bytes 2752520 | tf_op jit(solution)/shard_map/ppermute | solution.py:755
  782.4 63.8 %collective-permute-start.31 = (bf16[512,896]{1,0:T(8,128)(2,1)}, bf16[512,896]{1,0:T(8,128)(2,1)}, u32[]{:S(2)}, u32[]{:S(2)}) collective-permute-start(bf16[512,896]{1,0:T(8,128)(2,1)} %get-tuple-element.398), channel_id=1, source_target_pairs={{0,24},{8,16},{16,8},{24,0},{1,25},{9,17},{17,9},{25,1},{2,26},{10... | collective-permute-start | bytes 2752520 | tf_op jit(solution)/shard_map/ppermute | solution.py:755
  825.6 91.6 %collective-permute-start.33 = (bf16[128,2048]{1,0:T(8,128)(2,1)}, bf16[128,2048]{1,0:T(8,128)(2,1)}, u32[]{:S(2)}, u32[]{:S(2)}) collective-permute-start(bf16[128,2048]{1,0:T(8,128)(2,1)} %fusion.22), channel_id=1, source_target_pairs={{0,8},{8,0},{16,24},{24,16},{1,9},{9,1},{17,25},{25,17},{2,10},{10... | collective-permute-start | bytes 1572872 | tf_op jit(solution)/shard_map/ppermute | solution.py:803
  850.9 66.3 %all-to-all-start.4 = ((bf16[8,64,896]{2,1,0:T(8,128)(2,1)}), bf16[8,64,896]{2,1,0:T(8,128)(2,1)S(1)}, u32[]{:S(2)}, u32[]{:S(2)}) async-start(bf16[8,64,896]{2,1,0:T(8,128)(2,1)} %bitcast.151), calls=%async_computation.8 | async-start | bytes 1835008 | tf_op jit(solution)/shard_map/all_to_all | solution.py:1098
  855.4 61.9 %collective-permute-start.35 = (bf16[128,2048]{1,0:T(8,128)(2,1)}, bf16[128,2048]{1,0:T(8,128)(2,1)S(1)}, u32[]{:S(2)}, u32[]{:S(2)}) collective-permute-start(bf16[128,2048]{1,0:T(8,128)(2,1)} %fusion.23), channel_id=1, source_target_pairs={{0,8},{8,0},{16,24},{24,16},{1,9},{9,1},{17,25},{25,17},{2,10},{10... | collective-permute-start | bytes 1572872 | tf_op jit(solution)/shard_map/ppermute | solution.py:803
  (82 other events, 2178.7 us)
Sparse Core Ops, SparseCore 0:
  9.9 64.3 all-gather.8
  76.8 54.3 all-gather.10
  133.1 101.0 all-gather.14
  241.0 92.4 all-gather.12
  468.2 73.1 reduce-scatter.5
  544.9 79.3 reduce-scatter.7
  647.3 68.2 reduce-scatter.9
  762.2 63.1 reduce-scatter.11
  828.9 80.7 reduce-scatter.13

commit v15 on v14

--- a/solution.py
+++ b/solution.py
@@ -562,7 +562,13 @@
     )
 
 
-def weight_gradient(where, planes, left, rights, tail=None, first=0, steps=None, shift=False):
+def cut_ends(count, places):
+    return [-(-count * place // 512) * 16 for place in (0, *places, 32)]
+
+
+def weight_gradient(
+    where, planes, left, rights, tail=None, first=0, steps=None, shift=False, cuts=None
+):
     steps = planes if steps is None else steps
     count, width = left.shape
     parts = len(rights)
@@ -573,24 +579,34 @@
     tails = [] if tail is None else [tail]
     whole = columns + sum(value.shape[1] for value in tails)
 
+    ends = [cut_ends(width, (cuts or {}).get(number, ())) for number in range(steps)]
+    shapes = [
+        out((end - start, whole)) for one in ends for start, end in zip(one, one[1:])
+    ]
+
     def of_plane(i, where):
         return (where[1] + first + i) % planes if shift else lax.bitwise_xor(where[1], first + i)
 
     def kernel(where, left, *refs):
-        rights, tails, targets = refs[:parts], refs[parts:-steps], refs[-steps:]
-
-        def fill(target):
+        rights, tails, targets = refs[:parts], refs[parts : -len(shapes)], refs[-len(shapes) :]
+
+        def fill(targets, ends):
             for value in tails:
-                target[:, columns:] = value[...]
+                targets[0][:, columns:] = value[...]
             for number in range(columns // step):
                 at = slice(number * step, (number + 1) * step)
-                target[:, at] = sum(
+                result = sum(
                     dot(left[part * part_rows : (part + 1) * part_rows], right[:, at], ((0,), (0,)))
                     for part, right in enumerate(rights)
                 ).astype(bf16)
-
-        for number, target in enumerate(targets):
-            pl.when(pl.program_id(0) == number)(lambda target=target: fill(target))
+                for target, start, end in zip(targets, ends, ends[1:]):
+                    target[:, at] = result[start:end]
+
+        done = 0
+        for number, one in enumerate(ends):
+            mine = targets[done : done + len(one) - 1]
+            done += len(one) - 1
+            pl.when(pl.program_id(0) == number)(lambda mine=mine, one=one: fill(mine, one))
 
     return pl.pallas_call(
         kernel,
@@ -603,9 +619,9 @@
                 pl.BlockSpec((width, value.shape[1]), lambda i, where: (of_plane(i, where), 0))
                 for value in tails
             ],
-            out_specs=[fixed((width, whole))] * steps,
+            out_specs=[fixed(shape.shape) for shape in shapes],
         ),
-        out_shape=[out((width, whole))] * steps,
+        out_shape=shapes,
         cost_estimate=cost(0 if tails else count * steps * width * columns),
         compiler_params=params(),
     )(where, left, *rights, *tails)
@@ -930,8 +946,62 @@
         where, planes, rows_flat, grads_flat, first=1, steps=1, shift=True
     )
     rows_flat, in_near = lax.optimization_barrier((rows_flat, in_near))
+    cuts = {number: (20, 28) for number in range(planes - 3)}
     *in_rest, in_back, in_own = weight_gradient(
-        where, planes, rows_flat, grads_flat, first=2, steps=last_step, shift=True
+        where, planes, rows_flat, grads_flat, first=2, steps=last_step, shift=True, cuts=cuts
+    )
+    in_sent = {0: in_own, 1: shift_rep(in_near, 1)}
+
+    def sum_rep(parts, shift=False):
+        sums = [
+            sum(parts[step].astype(f32) for step in range(first, planes, share))
+            for first in range(share)
+        ]
+        return jnp.stack(
+            [
+                sum(
+                    jnp.where(((own - step) % share if shift else own ^ step) == j, sums[step], 0.0)
+                    for step in range(share)
+                )
+                for j in range(share)
+            ]
+        )
+
+    tail, out_cut, out_pieces = lax.optimization_barrier((tail, out_cut, out_pieces))
+    first = cross_rep(out_cut[1][:16], 1)
+    tail, out_cut, first = lax.optimization_barrier((tail, out_cut, first))
+    out_sent = send([out_cut[0], out_cut[1][16:], *out_cut[2:]], range(1, planes))
+    back = []
+    returned = []
+
+    def scatter_ranks(value):
+        return lax.psum_scatter(value, "ep", scatter_dimension=0)
+
+    def exchange_back(value):
+        return [value] + [exchange(value[step], share - step) for step in range(1, share)]
+
+    for step in range(micro):
+        back.append(
+            expert_backward(
+                step, where, tail, both, active, grad_produced, up_rows, places, in_pieces,
+                out_pieces, share, rows, experts,
+            )
+        )
+        returned.append(scatter_ranks(back[step][2]))
+        if step == 0:
+            tail, out_sent[last_step] = after((tail, out_sent[last_step]), back[step][2])
+        else:
+            tail = after(tail, back[step][2])
+    rows_in = after(rows_in, tail)
+    rows_flat = rows_in.reshape(in_rows, D)
+    grads_flat = [back[step][3].reshape(in_rows // micro, 2 * FF) for step in range(micro)]
+    (in_near,) = weight_gradient(
+        where, planes, rows_flat, grads_flat, first=1, steps=1, shift=True
+    )
+    rows_flat, in_near = lax.optimization_barrier((rows_flat, in_near))
+    cuts = {number: (20, 28) for number in range(planes - 3)}
+    *in_rest, in_back, in_own = weight_gradient(
+        where, planes, rows_flat, grads_flat, first=2, steps=last_step, shift=True, cuts=cuts
     )
     in_sent = {0: in_own, 1: shift_rep(in_near, 1)}
 
@@ -968,7 +1038,7 @@
     def total(parts):
         return sum(part.astype(f32) for part in parts)
 
-    grad_inputs, branches, logit_grads, grad_projs = [], [], [], []
+    grad_inputs, branches, logit_grads, grad_projs, normed_sums = [], [], [], [], []
     gain_two_sum = gain_one_sum = qk_sum = 0.0
     in_rest, in_back, out_sent, in_sent = lax.optimization_barrier(
         (in_rest, in_back, out_sent, in_sent)
@@ -988,7 +1058,7 @@
             mixtures = [pair_sum(number, *part) for number, part in enumerate(mixtures)]
             in_sent[last_step] = shift_rep(in_back, last_step)
         if step == micro - 1:
-            rest = [cuts(value, 20, 28) for value in in_rest]
+            rest = [in_rest[3 * i : 3 * i + 3] for i in range(planes - 3)]
             rest_sent = [[shift_rep(part[0], i + 2) for i, part in enumerate(rest)]]
         grad_hidden, grad_branch, grad_mixed, grad_logits, gain_two = hidden_backward(
             step, where[1:2], planes, parts, hidden, gates, cotangent, second_gain, router, gathered,
@@ -1015,8 +1085,8 @@
         if step < micro - 1:
             grad_proj, in_sent = lax.optimization_barrier((grad_proj, in_sent))
         else:
-            grad_proj, grad_inputs, rest_sent, rest = lax.optimization_barrier(
-                (grad_proj, grad_inputs, rest_sent, rest)
+            grad_proj, normed_sums, rest_sent, rest = lax.optimization_barrier(
+                (grad_proj, normed_sums, rest_sent, rest)
             )
         grad_projs.append(grad_proj)
         grad_normed, gain_one = project_backward(step, grad_proj, stream, slab)
@@ -1025,9 +1095,12 @@
             (
                 grad_hidden,
                 grad_normed,
-                lax.psum_scatter(grad_normed, "ep", scatter_dimension=0, tiled=True),
             )
         )
+        if step < micro - 1:
+            normed_sums.append(
+                lax.psum_scatter(grad_normed, "ep", scatter_dimension=0, tiled=True)
+            )
 
     router_sum = dot(normed_two, jnp.concatenate(logit_grads, axis=0), ((0,), (0,)))
     qk_columns = qk_sum.shape[0] // dense_rows
@@ -1050,7 +1123,7 @@
         return value[..., :count].astype(f32) + value[..., count : 2 * count].astype(f32)
 
     grad_projs, rest, out_cut, out_sent, _ = lax.optimization_barrier(
-        (grad_projs, rest, out_cut, out_sent, grad_normed)
+        (grad_projs, rest, out_cut, out_sent, grad_inputs[-1][1])
     )
     rest_sent.append([shift_rep(part[2], i + 2) for i, part in enumerate(rest)])
     packed = weight_gradient(
@@ -1064,19 +1137,12 @@
         (packed, rest_sent, out_cut, out_sent, crossed)
     )
     packed_sent = [packed[0]] + [cross_rep(packed[step], step) for step in range(1, planes)]
-    normed_sums = [one[2] for one in grad_inputs]
-    normed_sums = [one[2] for one in grad_inputs]
-    grad_tokens = []
-    for step in range(micro):
-        own_stream = tokens[step * rows : (step + 1) * rows].astype(f32)
-        grad_tokens.append(
-            grad_inputs[step][0]
-            + rms_backward(
-                own_stream, inverse_rms(own_stream), first_gain, normed_sums[step].astype(f32)
-            )
-        )
-    grad_tokens = jnp.concatenate(grad_tokens, axis=0)
-    packed_sent, grad_tokens = lax.optimization_barrier((packed_sent, grad_tokens))
+    normed_sums.append(
+        lax.psum_scatter(
+            after(grad_inputs[-1][1], packed), "ep", scatter_dimension=0, tiled=True
+        )
+    )
+    packed_sent, out_sum = lax.optimization_barrier((packed_sent, out_sum))
     for phase in range(1, len(bits)):
         mixtures = [total(parts).astype(bf16) for parts in crossed]
         crossed = [
@@ -1096,7 +1162,19 @@
     small = sum(joined(part[:, 3 * width :]) for part in packed_sent)
     packed = jnp.concatenate([main, halves(small)], axis=1).reshape(ranks, dense_rows, -1)
     packed = lax.all_to_all(packed, "ep", split_axis=0, concat_axis=0, tiled=True)
-    packed, mixture, out_sent_back = lax.optimization_barrier((packed, mixture, out_sent_back))
+    packed, mixture, out_sent_back, normed_sums = lax.optimization_barrier(
+        (packed, mixture, out_sent_back, normed_sums)
+    )
+    grad_tokens = []
+    for step in range(micro):
+        own_stream = tokens[step * rows : (step + 1) * rows].astype(f32)
+        grad_tokens.append(
+            grad_inputs[step][0]
+            + rms_backward(
+                own_stream, inverse_rms(own_stream), first_gain, normed_sums[step].astype(f32)
+            )
+        )
+    grad_tokens = jnp.concatenate(grad_tokens, axis=0)
     output = jnp.concatenate([mine_part + total(others) for mine_part, others in mixture], axis=0)
     output = (hidden + output).astype(bf16)
     grad_w_o = total([own_sum, *out_sent_back])

time: 962 us -> 931 us (0.968)
  waiting for transfers between devices: 344 us -> 310 us
    reduce_scatter x1, waiting for transfers between devices: 35.5 us -> 0.01 us  [on_device(): out_sum = lax.psum_scatter(out_sum, 'ep', scatter_dimension=0)]
    ppermute x6, waiting for transfers between devices: 62.9 us -> 73.8 us  [exchange(): return lax.ppermute(value, 'rep', pairs)]
    ppermute x6, waiting for transfers between devices: 17.8 us -> 7.96 us  [swap(): return lax.ppermute(value, 'ep', [(i, i ^ step) for i in range(ranks)])]
    unnamed x111 -> x129, local copies, waits for them, and re-layouts: 20.3 us -> 23.8 us
  transfers between devices with their start and end apart: 53 -> 53, of which waited for: 28 -> 27; matrix products, arithmetic and copies ran while one was open for 12% -> 12% of each run, Pallas kernels for 32% -> 34%
where the time goes in v15:
time: 931 us; the launch traced here: 922 us
  Pallas kernels  312 us (34%)
  waiting for transfers between devices  310 us (33%)
  starting transfers between devices  141 us (15%)
  local copies, waits for them, and re-layouts  68 us (7%)
  other arithmetic  65.9 us (7%)
  between operations  15.2 us (2%)
  matrix products  10 us (1%)
    ppermute x19, waiting for transfers between devices, cross_rep(): lax.ppermute(value, 'rep', [(i, i ^ bits) for i in range(lax.axis_size('r...  108 us
    pallas_call x2, Pallas kernels, expert_backward(): pl.pallas_call(kernel, grid_spec=pltpu.PrefetchScalarGridSpec(num_scalar_...  85.4 us
    ppermute x19, starting transfers between devices, cross_rep(): lax.ppermute(value, 'rep', [(i, i ^ bits) for i in range(lax.axis_size('r...  82.9 us
    ppermute x8, waiting for transfers between devices, shift_rep(): lax.ppermute(value, 'rep', [(i, (i + step) % count) for i in range(count)])  75.5 us
    ppermute x6, waiting for transfers between devices, exchange(): return lax.ppermute(value, 'rep', pairs)  73.8 us
    pallas_call x4, Pallas kernels, weight_gradient(): pl.pallas_call(kernel, grid_spec=pltpu.PrefetchScalarGridSpec(num_scalar_...  65.4 us
    pallas_call x1, Pallas kernels, expert_forward(): pl.pallas_call(kernel, grid_spec=pltpu.PrefetchScalarGridSpec(num_scalar_...  40.4 us
    pallas_call x2, Pallas kernels, attention_backward(): pl.pallas_call(lambda *refs: backward_kernel(heads, *refs), grid=(1,), in...  34.7 us
  transfers between devices with their start and end apart: 53, of which 27 were waited for; matrix products, arithmetic and copies ran while one was open for 12% of the time, Pallas kernels for 34%

profile of v15, /device:TPU:0, one launch (start us, length us, event | category | flops | bytes accessed | tf_op | source)
XLA Modules:
  0.0 922.5 jit_solution(1716285518974155886)
XLA Ops:
  23.1 17.7 %collective-permute-done.3 = bf16[256,2048]{1,0:T(8,128)(2,1)S(1)} collective-permute-done((bf16[256,2048]{1,0:T(8,128)(2,1)}, bf16[256,2048]{1,0:T(8,128)(2,1)S(1)}, u32[]{:S(2)}, u32[]{:S(2)}) %collective-permute-start.3) | collective-permute-done | bytes 1048608 | tf_op jit(solution)/shard_map/ppermute | solution.py:819
  57.5 22.5 %collective-permute-done.4 = bf16[512,896]{1,0:T(8,128)(2,1)S(1)} collective-permute-done((bf16[512,896]{1,0:T(8,128)(2,1)S(1)}, bf16[512,896]{1,0:T(8,128)(2,1)S(1)}, u32[]{:S(2)}, u32[]{:S(2)}) %collective-permute-start.4) | collective-permute-done | bytes 917536 | tf_op jit(solution)/shard_map/ppermute | solution.py:767
  108.5 17.1 %collective-permute-done.6 = bf16[512,896]{1,0:T(8,128)(2,1)S(1)} collective-permute-done((bf16[512,896]{1,0:T(8,128)(2,1)}, bf16[512,896]{1,0:T(8,128)(2,1)S(1)}, u32[]{:S(2)}, u32[]{:S(2)}) %collective-permute-start.6) | collective-permute-done | bytes 917536 | tf_op jit(solution)/shard_map/ppermute | solution.py:767
  129.8 15.9 %shard_map.179 = (bf16[2,8,128,2048]{3,2,1,0:T(8,128)(2,1)}, f32[8,256,768]{2,1,0:T(8,128)}) custom-call(bf16[8,256,2048]{2,1,0:T(8,128)(2,1)} %bitcast.137, f32[1,2048]{1,0:T(1,128)S(1)} %broadcast_in_dim.56.gain, bf16[2048,896]{1,0:T(8,128)(2,1)} %constant_dynamic-update-slice_fusion.weight), custom_call_target="tpu_custom_call" | custom-call | tf_op jit(solution)/shard_map/pallas_call | solution.py:248
  145.7 21.7 %shard_map.180 = (bf16[8,2,128,256]{3,2,1,0:T(8,128)(2,1)}, bf16[2,1024,256]{2,1,0:T(8,128)(2,1)S(1)}, bf16[2,1024,256]{2,1,0:T(8,128)(2,1)S(1)}, bf16[2,1024,256]{2,1,0:T(8,128)(2,1)}, f32[2,2,1024,1]{3,2,1,0:T(8,128)}) custom-call(f32[8,2,128,768]{3,2,1,0:T(8,128)} %bitcast.140, f32[2,1024,128]{2,1,0:T(8,128)} %get-tuple-element.259.refs_1_, ...), custom_call_target="tpu_custom_call" | custom-call | tf_op jit(solution)/shard_map/pallas_call | solution.py:198
  175.2 24.7 %all-to-all-done.1 = bf16[8,2,128,256]{3,2,1,0:T(8,128)(2,1)S(1)} async-done(((bf16[8,2,128,256]{3,2,1,0:T(8,128)(2,1)}), bf16[8,2,128,256]{3,2,1,0:T(8,128)(2,1)S(1)}, u32[]{:S(2)}, u32[]{:S(2)}) %all-to-all-start.1) | async-done | bytes 1048608 | tf_op jit(solution)/shard_map/all_to_all | solution.py:877
  215.6 23.6 %collective-permute-done.9 = bf16[256,2176]{1,0:T(8,128)(2,1)S(1)} collective-permute-done((bf16[256,2176]{1,0:T(8,128)(2,1)S(1)}, bf16[256,2176]{1,0:T(8,128)(2,1)S(1)}, u32[]{:S(2)}, u32[]{:S(2)}) %collective-permute-start.9) | collective-permute-done | bytes 1114144 | tf_op jit(solution)/shard_map/ppermute | solution.py:819
  241.1 46.4 %collective-permute-done.10.refs_3_ = bf16[512,2048]{1,0:T(8,128)(2,1)} collective-permute-done((bf16[512,2048]{1,0:T(8,128)(2,1)}, bf16[512,2048]{1,0:T(8,128)(2,1)}, u32[]{:S(2)}, u32[]{:S(2)}) %collective-permute-start.10) | collective-permute-done | bytes 2097184 | tf_op jit(solution)/shard_map/ppermute | solution.py:771
  287.5 43.1 %collective-permute-start.11 = (bf16[256,2048]{1,0:T(8,128)(2,1)}, bf16[256,2048]{1,0:T(8,128)(2,1)}, u32[]{:S(2)}, u32[]{:S(2)}) collective-permute-start(bf16[256,2048]{1,0:T(8,128)(2,1)} %get-tuple-element.309), channel_id=1, source_target_pairs={{0,8},{8,0},{16,24},{24,16},{1,9},{9,1},{17,25},{25,17},{2,10},{10... | collective-permute-start | bytes 3145736 | tf_op jit(solution)/shard_map/ppermute | solution.py:771
  333.5 40.4 %shard_map.182 = (bf16[2,4,288,2048]{3,2,1,0:T(8,128)(2,1)}, f32[2,4,288,128]{3,2,1,0:T(8,128)S(1)}, f32[2,4,288,2048]{3,2,1,0:T(8,128)}, bf16[2,4,288,1024]{3,2...) custom-call(s32[3]{0:T(128)S(1)} %pad_add_fusion.where, ...), custom_call_target="tpu_custom_call" | custom-call | flops 241591910400 | tf_op jit(solution)/shard_map/pallas_call | solution.py:435
  375.3 16.3 %shard_map.183 = (bf16[256,2048]{1,0:T(8,128)(2,1)S(1)}, bf16[256,2048]{1,0:T(8,128)(2,1)S(1)}, bf16[256,2048]{1,0:T(8,128)(2,1)S(1)}, bf16[256,2048]{1,0:T(8,128)(2,1)}) custom-call(s32[3]{0:T(128)S(1)} %pad_add_fusion.where, bf16[2304,1024]{1,0:T(8,128)(2,1)} %bitcast.173, bf16[2304,2048]{1,0:T(8,128)(2,1)} %bitcast.172), custom_call_target="tpu_custom_call" | custom-call | flops 96636764160 | tf_op jit(solution)/shard_map/pallas_call | solution.py:611
  402.8 19.5 %collective-permute-start.14 = (bf16[16,2048]{1,0:T(8,128)(2,1)S(1)}, bf16[16,2048]{1,0:T(8,128)(2,1)S(1)}, u32[]{:S(2)}, u32[]{:S(2)}) collective-permute-start(bf16[16,2048]{1,0:T(8,128)(2,1)S(1)} %slice.135), channel_id=1, source_target_pairs={{0,8},{8,0},{16,24},{24,16},{1,9},{9,1},{17,25},{25,17},{2,10},{10... | collective-permute-start | bytes 196616 | tf_op jit(solution)/shard_map/ppermute | solution.py:771
  426.9 41.1 %shard_map.184 = (bf16[4,2,128,2048]{3,2,1,0:T(8,128)(2,1)}, bf16[4,2,128,2048]{3,2,1,0:T(8,128)(2,1)}, bf16[8,2,128,2176]{3,2,1,0:T(8,128)(2,1)}, bf16[4,288,2048]{2,1,0:T(8,128)(2,1)}) custom-call(s32[3]{0:T(128)S(1)} %pad_add_fusion.where, f32[2,4,288,128]{3,2,1,0:T(8,128)} %copy-done.36, f32[2,4,288,2048]{3,2,1,0:T(8,128)} %get-tuple-element.330.both, ...), custom_call_target="tpu_custom_call" | custom-call | flops 217432719360 | tf_op jit(solution)/shard_map/pallas_call | solution.py:533
  472.5 44.3 %shard_map.185 = (bf16[4,2,128,2048]{3,2,1,0:T(8,128)(2,1)}, bf16[4,2,128,2048]{3,2,1,0:T(8,128)(2,1)}, bf16[8,2,128,2176]{3,2,1,0:T(8,128)(2,1)}, bf16[4,288,2048]{2,1,0:T(8,128)(2,1)}) custom-call(s32[3]{0:T(128)S(1)} %pad_add_fusion.where, f32[2,4,288,128]{3,2,1,0:T(8,128)} %copy-done.36, f32[2,4,288,2048]{3,2,1,0:T(8,128)} %get-tuple-element.330.both, ...), custom_call_target="tpu_custom_call" | custom-call | flops 217432719360 | tf_op jit(solution)/shard_map/pallas_call | solution.py:533
  516.8 12.1 %shard_map.186 = bf16[512,2048]{1,0:T(8,128)(2,1)} custom-call(s32[3]{0:T(128)S(1)} %pad_add_fusion.where, bf16[2304,2048]{1,0:T(8,128)(2,1)} %bitcast.170, bf16[1152,2048]{1,0:T(8,128)(2,1)} %bitcast.174, bf16[1152,2048]{1,0:T(8,128)(2,1)} %bitcast.176), custom_call_target="tpu_custom_call" | custom-call | flops 48318382080 | tf_op jit(solution)/shard_map/pallas_call | solution.py:611
  530.5 24.6 %shard_map.187 = (bf16[320,2048]{1,0:T(8,128)(2,1)S(1)}, bf16[128,2048]{1,0:T(8,128)(2,1)S(1)}, bf16[64,2048]{1,0:T(8,128)(2,1)S(1)}, bf16[512,2048]{1,0:T(8,128)(2,1)}, bf16[512,2048]{1,0:T(8,128)(2,1)}) custom-call(s32[3]{0:T(128)S(1)} %pad_add_fusion.where, bf16[2304,2048]{1,0:T(8,128)(2,1)} %bitcast.171, bf16[1152,2048]{1,0:T(8,128)(2,1)} %bitcast.175, ...), custom_call_target="tpu_custom_call" | custom-call | flops 144955146240 | tf_op jit(solution)/shard_map/pallas_call | solution.py:611
  557.0 17.1 %collective-permute-done.18 = bf16[512,2048]{1,0:T(8,128)(2,1)} collective-permute-done((bf16[512,2048]{1,0:T(8,128)(2,1)}, bf16[512,2048]{1,0:T(8,128)(2,1)}, u32[]{:S(2)}, u32[]{:S(2)}) %collective-permute-start.18) | collective-permute-done | bytes 2097184 | tf_op jit(solution)/shard_map/ppermute | solution.py:767
  619.7 16.8 %shard_map.189 = (bf16[8,128,768]{2,1,0:T(8,128)(2,1)}, f32[2,128]{1,0:T(2,128)S(1)}) custom-call(f32[8,2,128,768]{3,2,1,0:T(8,128)} %bitcast.141, f32[2,1024,128]{2,1,0:T(8,128)S(1)} %copy-done.2, f32[2,1024,128]{2,1,0:T(8,128)S(1)} %copy-done.1, s32[2,1024,1]{2,1,0:T(8,128)S(1)} %copy-done.3, s32[2,1,1024]{2,1,0:T(1,128)S(1)} %copy-done.25, ...), custom_call_target="tpu_custom_call" | custom-call | tf_op jit(solution)/shard_map/pallas_call | solution.py:220
  652.4 13.2 %collective-permute-done.23.refs_1_ = bf16[128,2176]{1,0:T(8,128)(2,1)S(1)} collective-permute-done((bf16[128,2176]{1,0:T(8,128)(2,1)S(1)}, bf16[128,2176]{1,0:T(8,128)(2,1)S(1)}, u32[]{:S(2)}, u32[]{:S(2)}) %collective-permute-start.23) | collective-permute-done | bytes 557088 | tf_op jit(solution)/shard_map/ppermute | solution.py:819
  700.8 18.3 %all-to-all-done.3 = bf16[128,8,256]{2,0,1:T(8,128)(2,1)} async-done(((bf16[128,8,256]{2,0,1:T(8,128)(2,1)}), bf16[128,8,256]{2,0,1:T(8,128)(2,1)}, u32[]{:S(2)}, u32[]{:S(2)}) %all-to-all-start.3) | async-done | bytes 524320 | tf_op jit(solution)/shard_map/all_to_all | solution.py:1073
  728.7 17.9 %shard_map.192 = (bf16[8,128,768]{2,1,0:T(8,128)(2,1)}, f32[2,128]{1,0:T(2,128)S(1)}) custom-call(f32[8,2,128,768]{3,2,1,0:T(8,128)} %bitcast.142, f32[2,1024,128]{2,1,0:T(8,128)S(1)} %copy-done.2, f32[2,1024,128]{2,1,0:T(8,128)S(1)} %copy-done.1, s32[2,1024,1]{2,1,0:T(8,128)S(1)} %copy-done.4, s32[2,1,1024]{2,1,0:T(1,128)S(1)} %copy-done.25, ...), custom_call_target="tpu_custom_call" | custom-call | tf_op jit(solution)/shard_map/pallas_call | solution.py:220
  765.1 12.4 %shard_map.194 = (bf16[512,896]{1,0:T(8,128)(2,1)S(1)}, bf16[512,896]{1,0:T(8,128)(2,1)}, bf16[512,896]{1,0:T(8,128)(2,1)}, bf16[512,896]{1,0:T(8,128)(2,1)}) custom-call(s32[3]{0:T(128)S(1)} %pad_add_fusion.where, bf16[2048,2048]{1,0:T(8,128)(2,1)} %bitcast.146, bf16[1024,768]{1,0:T(8,128)(2,1)} %bitcast.128, bf16[1024,768]{1,0:T(8,128)(2,1)} %bitcast.129, ...), custom_call_target="tpu_custom_call" | custom-call | tf_op jit(solution)/shard_map/pallas_call | solution.py:611
  821.6 21.6 %collective-permute-done.30 = bf16[512,896]{1,0:T(8,128)(2,1)} collective-permute-done((bf16[512,896]{1,0:T(8,128)(2,1)}, bf16[512,896]{1,0:T(8,128)(2,1)}, u32[]{:S(2)}, u32[]{:S(2)}) %collective-permute-start.30) | collective-permute-done | bytes 917536 | tf_op jit(solution)/shard_map/ppermute | solution.py:771
  853.1 18.6 %collective-permute-start.35 = (bf16[128,2048]{1,0:T(8,128)(2,1)S(1)}, bf16[128,2048]{1,0:T(8,128)(2,1)}, u32[]{:S(2)}, u32[]{:S(2)}) collective-permute-start(bf16[128,2048]{1,0:T(8,128)(2,1)S(1)} %fusion.23), channel_id=1, source_target_pairs={{0,8},{8,0},{16,24},{24,16},{1,9},{9,1},{17,25},{25,17},{2,10},{10... | collective-permute-start | bytes 1572872 | tf_op jit(solution)/shard_map/ppermute | solution.py:819
  (328 shorter events, 340.3 us)
Async XLA Ops:
  7.2 119.5 %all-gather.9.cloned.1.call-start = ((), (), s32[]{:S(2)}) async-start(), calls=%async_computation.15 | async-start | bytes 9437184 | tf_op jit(solution)/shard_map/all_gather | solution.py:825
  18.6 182.2 %all-gather.11.cloned.1.call-start = ((), (), s32[]{:S(2)}) async-start(), calls=%async_computation.16 | async-start | bytes 9437184 | tf_op jit(solution)/shard_map/all_gather | solution.py:825
  55.7 277.2 %all-gather.15.cloned.1.call-start = ((), (), s32[]{:S(2)}) async-start(), calls=%async_computation.18 | async-start | bytes 18874368 | tf_op jit(solution)/shard_map/all_gather | solution.py:825
  126.7 87.3 %collective-permute-start.7 = (bf16[512,2048]{1,0:T(8,128)(2,1)}, bf16[512,2048]{1,0:T(8,128)(2,1)}, u32[]{:S(2)}, u32[]{:S(2)}) collective-permute-start(bf16[512,2048]{1,0:T(8,128)(2,1)} %get-tuple-element.290), channel_id=1, source_target_pairs={{0,8},{8,0},{16,24},{24,16},{1,9},{9,1},{17,25},{25,17},{2,10},{10... | collective-permute-start | bytes 6291464 | tf_op jit(solution)/shard_map/ppermute | solution.py:771
  126.7 88.4 %collective-permute-start.8 = (bf16[512,2048]{1,0:T(8,128)(2,1)}, bf16[512,2048]{1,0:T(8,128)(2,1)}, u32[]{:S(2)}, u32[]{:S(2)}) collective-permute-start(bf16[512,2048]{1,0:T(8,128)(2,1)} %get-tuple-element.295.refs_0_), channel_id=1, source_target_pairs={{0,16},{8,24},{16,0},{24,8},{1,17},{9,25},{17,1},{25,9},{2,18},{10... | collective-permute-start | bytes 6291464 | tf_op jit(solution)/shard_map/ppermute | solution.py:771
  173.3 160.2 %all-gather.13.cloned.1.call-start = ((), (), s32[]{:S(2)}) async-start(), calls=%async_computation.17 | async-start | bytes 20054016 | tf_op jit(solution)/shard_map/all_gather | solution.py:825
  240.9 333.3 %reduce-scatter.6.cloned.1.call-start = ((), (), s32[]{:S(2)}) async-start(), calls=%async_computation.10 | async-start | bytes 10027008 | tf_op jit(solution)/shard_map/reduce_scatter | solution.py:978
  287.5 106.1 %collective-permute-start.11 = (bf16[256,2048]{1,0:T(8,128)(2,1)}, bf16[256,2048]{1,0:T(8,128)(2,1)}, u32[]{:S(2)}, u32[]{:S(2)}) collective-permute-start(bf16[256,2048]{1,0:T(8,128)(2,1)} %get-tuple-element.309), channel_id=1, source_target_pairs={{0,8},{8,0},{16,24},{24,16},{1,9},{9,1},{17,25},{25,17},{2,10},{10... | collective-permute-start | bytes 3145736 | tf_op jit(solution)/shard_map/ppermute | solution.py:771
  330.6 72.3 %collective-permute-start.12 = (bf16[256,2048]{1,0:T(8,128)(2,1)}, bf16[256,2048]{1,0:T(8,128)(2,1)}, u32[]{:S(2)}, u32[]{:S(2)}) collective-permute-start(bf16[256,2048]{1,0:T(8,128)(2,1)} %get-tuple-element.333.refs_4_), channel_id=1, source_target_pairs={{0,16},{8,24},{16,0},{24,8},{1,17},{9,25},{17,1},{25,9},{2,18},{10... | collective-permute-start | bytes 3145736 | tf_op jit(solution)/shard_map/ppermute | solution.py:771
  330.6 72.3 %collective-permute-start.13 = (bf16[256,2048]{1,0:T(8,128)(2,1)}, bf16[256,2048]{1,0:T(8,128)(2,1)}, u32[]{:S(2)}, u32[]{:S(2)}) collective-permute-start(bf16[256,2048]{1,0:T(8,128)(2,1)} %get-tuple-element.309), channel_id=1, source_target_pairs={{0,24},{8,16},{16,8},{24,0},{1,25},{9,17},{17,9},{25,1},{2,26},{10... | collective-permute-start | bytes 3145736 | tf_op jit(solution)/shard_map/ppermute | solution.py:771
  468.1 179.1 %reduce-scatter.8.cloned.1.call-start = ((), (), s32[]{:S(2)}) async-start(), calls=%async_computation.11 | async-start | bytes 10027008 | tf_op jit(solution)/shard_map/reduce_scatter | solution.py:978
  470.3 86.7 %collective-permute-start.16 = (bf16[240,2048]{1,0:T(8,128)(2,1)}, bf16[240,2048]{1,0:T(8,128)(2,1)}, u32[]{:S(2)}, u32[]{:S(2)}) collective-permute-start(bf16[240,2048]{1,0:T(8,128)(2,1)} %slice.136), channel_id=1, source_target_pairs={{0,8},{8,0},{16,24},{24,16},{1,9},{9,1},{17,25},{25,17},{2,10},{10... | collective-permute-start | bytes 2949128 | tf_op jit(solution)/shard_map/ppermute | solution.py:771
  471.9 85.1 %collective-permute-start.17 = (bf16[256,2048]{1,0:T(8,128)(2,1)}, bf16[256,2048]{1,0:T(8,128)(2,1)}, u32[]{:S(2)}, u32[]{:S(2)}) collective-permute-start(bf16[256,2048]{1,0:T(8,128)(2,1)} %copy-done.31), channel_id=1, source_target_pairs={{0,16},{8,24},{16,0},{24,8},{1,17},{9,25},{17,1},{25,9},{2,18},{10... | collective-permute-start | bytes 3145736 | tf_op jit(solution)/shard_map/ppermute | solution.py:771
  585.3 51.2 %collective-permute-start.22 = (bf16[512,2048]{1,0:T(8,128)(2,1)}, bf16[512,2048]{1,0:T(8,128)(2,1)}, u32[]{:S(2)}, u32[]{:S(2)}) collective-permute-start(bf16[512,2048]{1,0:T(8,128)(2,1)} %get-tuple-element.377), channel_id=1, source_target_pairs={{0,24},{8,0},{16,8},{24,16},{1,25},{9,1},{17,9},{25,17},{2,26},{10... | collective-permute-start | bytes 6291464 | tf_op jit(solution)/shard_map/ppermute | solution.py:767
  603.0 146.1 %reduce-scatter.10.cloned.1.call-start = ((), (), s32[]{:S(2)}) async-start(), calls=%async_computation.12 | async-start | bytes 4718592 | tf_op jit(solution)/shard_map/reduce_scatter | solution.py:1102
  647.2 77.0 %collective-permute-start.24 = (bf16[2,2,128,2048]{3,2,1,0:T(8,128)(2,1)}, bf16[2,2,128,2048]{3,2,1,0:T(8,128)(2,1)}, u32[]{:S(2)}, u32[]{:S(2)}) collective-permute-start(bf16[2,2,128,2048]{3,2,1,0:T(8,128)(2,1)} %get-tuple-element.394), channel_id=1, source_target_pairs={{0,2},{1,3},{2,0},{3,1},{4,6},{5,7},{6,4},{7,5},{8,10},{9,11},{10,... | collective-permute-start | bytes 6291464 | tf_op jit(solution)/shard_map/ppermute | solution.py:1013
  648.9 75.4 %collective-permute-start.25 = (bf16[2,2,128,2048]{3,2,1,0:T(8,128)(2,1)}, bf16[2,2,128,2048]{3,2,1,0:T(8,128)(2,1)}, u32[]{:S(2)}, u32[]{:S(2)}) collective-permute-start(bf16[2,2,128,2048]{3,2,1,0:T(8,128)(2,1)} %get-tuple-element.396), channel_id=1, source_target_pairs={{0,4},{1,5},{2,6},{3,7},{4,0},{5,1},{6,2},{7,3},{8,12},{9,13},{10,... | collective-permute-start | bytes 6291464 | tf_op jit(solution)/shard_map/ppermute | solution.py:1013
  665.6 58.7 %collective-permute-start.26 = (bf16[320,2048]{1,0:T(8,128)(2,1)}, bf16[320,2048]{1,0:T(8,128)(2,1)}, u32[]{:S(2)}, u32[]{:S(2)}) collective-permute-start(bf16[320,2048]{1,0:T(8,128)(2,1)} %copy-done.30), channel_id=1, source_target_pairs={{0,16},{8,24},{16,0},{24,8},{1,17},{9,25},{17,1},{25,9},{2,18},{10... | collective-permute-start | bytes 3932168 | tf_op jit(solution)/shard_map/ppermute | solution.py:767
  684.9 158.3 %reduce-scatter.12.cloned.1.call-start = ((), (), s32[]{:S(2)}) async-start(), calls=%async_computation.13 | async-start | bytes 9437184 | tf_op jit(solution)/shard_map/reduce_scatter | solution.py:1079
  724.3 165.9 %reduce-scatter.14.cloned.1.call-start = ((), (), s32[]{:S(2)}) async-start(), calls=%async_computation.14 | async-start | bytes 4718592 | tf_op jit(solution)/shard_map/reduce_scatter | solution.py:1141
  779.4 63.9 %collective-permute-start.30 = (bf16[512,896]{1,0:T(8,128)(2,1)}, bf16[512,896]{1,0:T(8,128)(2,1)}, u32[]{:S(2)}, u32[]{:S(2)}) collective-permute-start(bf16[512,896]{1,0:T(8,128)(2,1)} %get-tuple-element.444), channel_id=1, source_target_pairs={{0,16},{8,24},{16,0},{24,8},{1,17},{9,25},{17,1},{25,9},{2,18},{10... | collective-permute-start | bytes 2752520 | tf_op jit(solution)/shard_map/ppermute | solution.py:771
  780.2 63.0 %collective-permute-start.31 = (bf16[512,896]{1,0:T(8,128)(2,1)}, bf16[512,896]{1,0:T(8,128)(2,1)}, u32[]{:S(2)}, u32[]{:S(2)}) collective-permute-start(bf16[512,896]{1,0:T(8,128)(2,1)} %get-tuple-element.445), channel_id=1, source_target_pairs={{0,24},{8,16},{16,8},{24,0},{1,25},{9,17},{17,9},{25,1},{2,26},{10... | collective-permute-start | bytes 2752520 | tf_op jit(solution)/shard_map/ppermute | solution.py:771
  817.2 62.0 %collective-permute-start.33 = (bf16[128,2048]{1,0:T(8,128)(2,1)}, bf16[128,2048]{1,0:T(8,128)(2,1)}, u32[]{:S(2)}, u32[]{:S(2)}) collective-permute-start(bf16[128,2048]{1,0:T(8,128)(2,1)} %fusion.22), channel_id=1, source_target_pairs={{0,8},{8,0},{16,24},{24,16},{1,9},{9,1},{17,25},{25,17},{2,10},{10... | collective-permute-start | bytes 1572872 | tf_op jit(solution)/shard_map/ppermute | solution.py:819
  848.1 54.3 %all-to-all-start.4 = ((bf16[8,64,896]{2,1,0:T(8,128)(2,1)}), bf16[8,64,896]{2,1,0:T(8,128)(2,1)S(1)}, u32[]{:S(2)}, u32[]{:S(2)}) async-start(bf16[8,64,896]{2,1,0:T(8,128)(2,1)} %bitcast.152), calls=%async_computation.8 | async-start | bytes 1835008 | tf_op jit(solution)/shard_map/all_to_all | solution.py:1164
  (91 other events, 2218.1 us)
Sparse Core Ops, SparseCore 0:
  9.9 64.3 all-gather.8
  76.8 54.3 all-gather.10
  133.1 101.0 all-gather.14
  241.0 92.4 all-gather.12
  468.2 73.1 reduce-scatter.5
  544.9 79.4 reduce-scatter.7
  647.3 68.3 reduce-scatter.9
  724.4 73.2 reduce-scatter.11
  801.0 53.1 reduce-scatter.13

commit v16 on v15

--- a/solution.py
+++ b/solution.py
@@ -840,6 +840,8 @@
     stream = gather_ranks(tokens)
     out_rows = [w_o] + [cross_rep(w_o, step) for step in range(1, planes)]
     upstream_group = with_group(cotangent)
+    early_rows = cut_ends(out_parts[last_step].shape[0], (12,))[1]
+    early = cross_rep(out_parts[last_step][:early_rows], last_step)
     slab = cut_heads(
         w_qkv,
         jnp.concatenate(
@@ -854,7 +856,9 @@
     )
     slab = lax.all_to_all(slab, "ep", split_axis=0, concat_axis=0, tiled=True)
     slab = slab.reshape(ranks * dense_rows, 3 * width + PAD)
-    out_rows, upstream_group, slab = lax.optimization_barrier((out_rows, upstream_group, slab))
+    out_rows, upstream_group, slab, early = lax.optimization_barrier(
+        (out_rows, upstream_group, slab, early)
+    )
     gathered = gather_ranks(jnp.concatenate(out_rows, axis=0))
     segment = segments[0]
     cosine, sine = jax.vmap(lambda one: rope_tables(doc_positions(one), HD))(segment)
@@ -885,6 +889,7 @@
     payload, in_parts, out_parts = lax.optimization_barrier((payload, in_parts, out_parts))
     in_pieces.update(send(in_parts, [last_step]))
     in_pieces, out_parts = lax.optimization_barrier((in_pieces, out_parts))
+    out_parts[last_step] = out_parts[last_step][early_rows:]
     out_pieces = {0: out_parts[0], **send(out_parts, range(1, planes))}
     in_pieces = [in_pieces[step] for step in range(planes)]
     out_pieces = [out_pieces[step] for step in range(planes)]
@@ -915,6 +920,7 @@
         )
 
     tail, out_cut, out_pieces = lax.optimization_barrier((tail, out_cut, out_pieces))
+    out_pieces[last_step] = jnp.concatenate([early, out_pieces[last_step]], axis=0)
     first = cross_rep(out_cut[1][:16], 1)
     tail, out_cut, first = lax.optimization_barrier((tail, out_cut, first))
     out_sent = send([out_cut[0], out_cut[1][16:], *out_cut[2:]], range(1, planes))
@@ -942,72 +948,16 @@
     rows_in = after(rows_in, tail)
     rows_flat = rows_in.reshape(in_rows, D)
     grads_flat = [back[step][3].reshape(in_rows // micro, 2 * FF) for step in range(micro)]
-    (in_near,) = weight_gradient(
-        where, planes, rows_flat, grads_flat, first=1, steps=1, shift=True
+    in_near = weight_gradient(
+        where, planes, rows_flat, grads_flat, first=1, steps=1, shift=True, cuts={0: (24,)}
     )
     rows_flat, in_near = lax.optimization_barrier((rows_flat, in_near))
     cuts = {number: (20, 28) for number in range(planes - 3)}
     *in_rest, in_back, in_own = weight_gradient(
         where, planes, rows_flat, grads_flat, first=2, steps=last_step, shift=True, cuts=cuts
     )
-    in_sent = {0: in_own, 1: shift_rep(in_near, 1)}
-
-    def sum_rep(parts, shift=False):
-        sums = [
-            sum(parts[step].astype(f32) for step in range(first, planes, share))
-            for first in range(share)
-        ]
-        return jnp.stack(
-            [
-                sum(
-                    jnp.where(((own - step) % share if shift else own ^ step) == j, sums[step], 0.0)
-                    for step in range(share)
-                )
-                for j in range(share)
-            ]
-        )
-
-    tail, out_cut, out_pieces = lax.optimization_barrier((tail, out_cut, out_pieces))
-    first = cross_rep(out_cut[1][:16], 1)
-    tail, out_cut, first = lax.optimization_barrier((tail, out_cut, first))
-    out_sent = send([out_cut[0], out_cut[1][16:], *out_cut[2:]], range(1, planes))
-    back = []
-    returned = []
-
-    def scatter_ranks(value):
-        return lax.psum_scatter(value, "ep", scatter_dimension=0)
-
-    def exchange_back(value):
-        return [value] + [exchange(value[step], share - step) for step in range(1, share)]
-
-    for step in range(micro):
-        back.append(
-            expert_backward(
-                step, where, tail, both, active, grad_produced, up_rows, places, in_pieces,
-                out_pieces, share, rows, experts,
-            )
-        )
-        returned.append(scatter_ranks(back[step][2]))
-        if step == 0:
-            tail, out_sent[last_step] = after((tail, out_sent[last_step]), back[step][2])
-        else:
-            tail = after(tail, back[step][2])
-    rows_in = after(rows_in, tail)
-    rows_flat = rows_in.reshape(in_rows, D)
-    grads_flat = [back[step][3].reshape(in_rows // micro, 2 * FF) for step in range(micro)]
-    (in_near,) = weight_gradient(
-        where, planes, rows_flat, grads_flat, first=1, steps=1, shift=True
-    )
-    rows_flat, in_near = lax.optimization_barrier((rows_flat, in_near))
-    cuts = {number: (20, 28) for number in range(planes - 3)}
-    *in_rest, in_back, in_own = weight_gradient(
-        where, planes, rows_flat, grads_flat, first=2, steps=last_step, shift=True, cuts=cuts
-    )
-    in_sent = {0: in_own, 1: shift_rep(in_near, 1)}
-
-    def cuts(value, *places):
-        ends = [-(-value.shape[0] * place // 512) * 16 for place in (0, *places, 32)]
-        return [value[start:end] for start, end in zip(ends, ends[1:])]
+    in_sent = {0: in_own}
+    near_sent = [shift_rep(in_near[0], 1)]
 
     def swap(value, step):
         return lax.ppermute(value, "ep", [(i, i ^ step) for i in range(ranks)])
@@ -1040,23 +990,24 @@
 
     grad_inputs, branches, logit_grads, grad_projs, normed_sums = [], [], [], [], []
     gain_two_sum = gain_one_sum = qk_sum = 0.0
-    in_rest, in_back, out_sent, in_sent = lax.optimization_barrier(
-        (in_rest, in_back, out_sent, in_sent)
+    in_rest, in_back, in_near, out_sent, near_sent = lax.optimization_barrier(
+        (in_rest, in_back, in_near, out_sent, near_sent)
     )
     mixtures = [part[:2] for part in back]
     for step in range(micro):
         parts = after(returned[step], [one[1] for one in grad_inputs])
-        parts, in_sent = lax.optimization_barrier((parts, in_sent))
+        parts, near_sent = lax.optimization_barrier((parts, near_sent))
         if step == micro - 1:
             mixtures = after(mixtures, parts)
             crossed = [halve(number, value, 0) for number, value in enumerate(mixtures)]
         parts = exchange_back(parts)
-        parts, in_rest, in_back, mixtures = lax.optimization_barrier(
-            (parts, in_rest, in_back, mixtures)
+        parts, in_rest, in_back, in_near, mixtures = lax.optimization_barrier(
+            (parts, in_rest, in_back, in_near, mixtures)
         )
         if step == 0:
             mixtures = [pair_sum(number, *part) for number, part in enumerate(mixtures)]
             in_sent[last_step] = shift_rep(in_back, last_step)
+            near_sent.append(shift_rep(in_near[1], 1))
         if step == micro - 1:
             rest = [in_rest[3 * i : 3 * i + 3] for i in range(planes - 3)]
             rest_sent = [[shift_rep(part[0], i + 2) for i, part in enumerate(rest)]]
@@ -1083,7 +1034,9 @@
         )
         qk_sum = qk_sum + grad_qk.reshape(-1)
         if step < micro - 1:
-            grad_proj, in_sent = lax.optimization_barrier((grad_proj, in_sent))
+            grad_proj, in_sent, near_sent = lax.optimization_barrier(
+                (grad_proj, in_sent, near_sent)
+            )
         else:
             grad_proj, normed_sums, rest_sent, rest = lax.optimization_barrier(
                 (grad_proj, normed_sums, rest_sent, rest)
@@ -1181,6 +1134,7 @@
     grad_w_qkv, small = unpack(packed, count)
     out_sent[1] = jnp.concatenate([first, out_sent[1]], axis=0)
     grad_w_out = sum_rep({0: out_cut[0], **out_sent})
+    in_sent[1] = jnp.concatenate(near_sent, axis=0)
     for i in range(planes - 3):
         in_sent[i + 2] = jnp.concatenate([parts[i] for parts in rest_sent], axis=0)
     grad_w_in = sum_rep(in_sent, shift=True)

time: 931 us -> 917 us (0.985)
  waiting for transfers between devices: 310 us -> 290 us
    ppermute x19 -> x20, waiting for transfers between devices: 108 us -> 92.3 us  [cross_rep(): lax.ppermute(value, 'rep', [(i, i ^ bits) for i in range(lax.axis_size('r...]
    ppermute x8 -> x9, waiting for transfers between devices: 75.5 us -> 66.7 us  [shift_rep(): lax.ppermute(value, 'rep', [(i, (i + step) % count) for i in range(count)])]
    ppermute x19 -> x20, starting transfers between devices: 82.9 us -> 78.5 us  [cross_rep(): lax.ppermute(value, 'rep', [(i, i ^ bits) for i in range(lax.axis_size('r...]
    unnamed x129 -> x136, local copies, waits for them, and re-layouts: 23.8 us -> 25.5 us
  transfers between devices with their start and end apart: 53 -> 55, of which waited for: 27 -> 26; matrix products, arithmetic and copies ran while one was open for 12% -> 13% of each run, Pallas kernels for 34% -> 34%
where the time goes in v16:
time: 917 us; the launch traced here: 908 us
  Pallas kernels  312 us (34%)
  waiting for transfers between devices  290 us (32%)
  starting transfers between devices  140 us (15%)
  local copies, waits for them, and re-layouts  74.5 us (8%)
  other arithmetic  66 us (7%)
  between operations  15.2 us (2%)
  matrix products  10.1 us (1%)
    ppermute x20, waiting for transfers between devices, cross_rep(): lax.ppermute(value, 'rep', [(i, i ^ bits) for i in range(lax.axis_size('r...  92.3 us
    pallas_call x2, Pallas kernels, expert_backward(): pl.pallas_call(kernel, grid_spec=pltpu.PrefetchScalarGridSpec(num_scalar_...  85.1 us
    ppermute x20, starting transfers between devices, cross_rep(): lax.ppermute(value, 'rep', [(i, i ^ bits) for i in range(lax.axis_size('r...  78.5 us
    ppermute x6, waiting for transfers between devices, exchange(): return lax.ppermute(value, 'rep', pairs)  76.8 us
    ppermute x9, waiting for transfers between devices, shift_rep(): lax.ppermute(value, 'rep', [(i, (i + step) % count) for i in range(count)])  66.7 us
    pallas_call x4, Pallas kernels, weight_gradient(): pl.pallas_call(kernel, grid_spec=pltpu.PrefetchScalarGridSpec(num_scalar_...  65.9 us
    pallas_call x1, Pallas kernels, expert_forward(): pl.pallas_call(kernel, grid_spec=pltpu.PrefetchScalarGridSpec(num_scalar_...  40.4 us
    pallas_call x2, Pallas kernels, attention_backward(): pl.pallas_call(lambda *refs: backward_kernel(heads, *refs), grid=(1,), in...  34.1 us
  transfers between devices with their start and end apart: 55, of which 26 were waited for; matrix products, arithmetic and copies ran while one was open for 13% of the time, Pallas kernels for 34%

profile of v16, /device:TPU:0, one launch (start us, length us, event | category | flops | bytes accessed | tf_op | source)
XLA Modules:
  0.0 907.9 jit_solution(17660998650816050169)
XLA Ops:
  27.3 21.9 %collective-permute-done.3 = bf16[256,2048]{1,0:T(8,128)(2,1)S(1)} collective-permute-done((bf16[256,2048]{1,0:T(8,128)(2,1)}, bf16[256,2048]{1,0:T(8,128)(2,1)S(1)}, u32[]{:S(2)}, u32[]{:S(2)}) %collective-permute-start.3) | collective-permute-done | bytes 1048608 | tf_op jit(solution)/shard_map/ppermute | solution.py:819
  68.8 20.1 %collective-permute-done.5 = bf16[512,896]{1,0:T(8,128)(2,1)S(1)} collective-permute-done((bf16[512,896]{1,0:T(8,128)(2,1)S(1)}, bf16[512,896]{1,0:T(8,128)(2,1)S(1)}, u32[]{:S(2)}, u32[]{:S(2)}) %collective-permute-start.5) | collective-permute-done | bytes 917536 | tf_op jit(solution)/shard_map/ppermute | solution.py:767
  118.3 14.3 %collective-permute-done.7 = bf16[512,896]{1,0:T(8,128)(2,1)S(1)} collective-permute-done((bf16[512,896]{1,0:T(8,128)(2,1)}, bf16[512,896]{1,0:T(8,128)(2,1)S(1)}, u32[]{:S(2)}, u32[]{:S(2)}) %collective-permute-start.7) | collective-permute-done | bytes 917536 | tf_op jit(solution)/shard_map/ppermute | solution.py:767
  137.8 16.3 %shard_map.179 = (bf16[2,8,128,2048]{3,2,1,0:T(8,128)(2,1)}, f32[8,256,768]{2,1,0:T(8,128)}) custom-call(bf16[8,256,2048]{2,1,0:T(8,128)(2,1)} %bitcast.139, f32[1,2048]{1,0:T(1,128)S(1)} %broadcast_in_dim.56.gain, bf16[2048,896]{1,0:T(8,128)(2,1)} %constant_dynamic-update-slice_fusion.weight), custom_call_target="tpu_custom_call" | custom-call | tf_op jit(solution)/shard_map/pallas_call | solution.py:248
  154.1 21.8 %shard_map.180 = (bf16[8,2,128,256]{3,2,1,0:T(8,128)(2,1)}, bf16[2,1024,256]{2,1,0:T(8,128)(2,1)S(1)}, bf16[2,1024,256]{2,1,0:T(8,128)(2,1)S(1)}, bf16[2,1024,256]{2,1,0:T(8,128)(2,1)}, f32[2,2,1024,1]{3,2,1,0:T(8,128)}) custom-call(f32[8,2,128,768]{3,2,1,0:T(8,128)} %bitcast.142, f32[2,1024,128]{2,1,0:T(8,128)} %get-tuple-element.248.refs_1_, ...), custom_call_target="tpu_custom_call" | custom-call | tf_op jit(solution)/shard_map/pallas_call | solution.py:198
  183.4 25.0 %all-to-all-done.1 = bf16[8,2,128,256]{3,2,1,0:T(8,128)(2,1)S(1)} async-done(((bf16[8,2,128,256]{3,2,1,0:T(8,128)(2,1)}), bf16[8,2,128,256]{3,2,1,0:T(8,128)(2,1)S(1)}, u32[]{:S(2)}, u32[]{:S(2)}) %all-to-all-start.1) | async-done | bytes 1048608 | tf_op jit(solution)/shard_map/all_to_all | solution.py:881
  224.6 22.8 %collective-permute-done.10 = bf16[256,2176]{1,0:T(8,128)(2,1)S(1)} collective-permute-done((bf16[256,2176]{1,0:T(8,128)(2,1)S(1)}, bf16[256,2176]{1,0:T(8,128)(2,1)S(1)}, u32[]{:S(2)}, u32[]{:S(2)}) %collective-permute-start.10) | collective-permute-done | bytes 1114144 | tf_op jit(solution)/shard_map/ppermute | solution.py:819
  251.8 42.6 %collective-permute-done.11.refs_3_ = bf16[512,2048]{1,0:T(8,128)(2,1)} collective-permute-done((bf16[512,2048]{1,0:T(8,128)(2,1)}, bf16[512,2048]{1,0:T(8,128)(2,1)}, u32[]{:S(2)}, u32[]{:S(2)}) %collective-permute-start.11) | collective-permute-done | bytes 2097184 | tf_op jit(solution)/shard_map/ppermute | solution.py:771
  294.4 43.5 %collective-permute-start.12 = (bf16[256,2048]{1,0:T(8,128)(2,1)}, bf16[256,2048]{1,0:T(8,128)(2,1)}, u32[]{:S(2)}, u32[]{:S(2)}) collective-permute-start(bf16[256,2048]{1,0:T(8,128)(2,1)} %get-tuple-element.298), channel_id=1, source_target_pairs={{0,8},{8,0},{16,24},{24,16},{1,9},{9,1},{17,25},{25,17},{2,10},{10... | collective-permute-start | bytes 3145736 | tf_op jit(solution)/shard_map/ppermute | solution.py:771
  342.2 40.4 %shard_map.182 = (bf16[2,4,288,2048]{3,2,1,0:T(8,128)(2,1)}, f32[2,4,288,128]{3,2,1,0:T(8,128)S(1)}, f32[2,4,288,2048]{3,2,1,0:T(8,128)}, bf16[2,4,288,1024]{3,2...) custom-call(s32[3]{0:T(128)S(1)} %pad_add_fusion.where, ...), custom_call_target="tpu_custom_call" | custom-call | flops 241591910400 | tf_op jit(solution)/shard_map/pallas_call | solution.py:435
  384.0 16.8 %shard_map.183 = (bf16[256,2048]{1,0:T(8,128)(2,1)S(1)}, bf16[256,2048]{1,0:T(8,128)(2,1)S(1)}, bf16[256,2048]{1,0:T(8,128)(2,1)S(1)}, bf16[256,2048]{1,0:T(8,128)(2,1)}) custom-call(s32[3]{0:T(128)S(1)} %pad_add_fusion.where, bf16[2304,1024]{1,0:T(8,128)(2,1)} %bitcast.175, bf16[2304,2048]{1,0:T(8,128)(2,1)} %bitcast.174), custom_call_target="tpu_custom_call" | custom-call | flops 96636764160 | tf_op jit(solution)/shard_map/pallas_call | solution.py:611
  416.4 40.7 %shard_map.184 = (bf16[4,2,128,2048]{3,2,1,0:T(8,128)(2,1)}, bf16[4,2,128,2048]{3,2,1,0:T(8,128)(2,1)}, bf16[8,2,128,2176]{3,2,1,0:T(8,128)(2,1)}, bf16[4,288,2048]{2,1,0:T(8,128)(2,1)}) custom-call(s32[3]{0:T(128)S(1)} %pad_add_fusion.where, f32[2,4,288,128]{3,2,1,0:T(8,128)} %copy-done.36, f32[2,4,288,2048]{3,2,1,0:T(8,128)} %get-tuple-element.305.both, ...), custom_call_target="tpu_custom_call" | custom-call | flops 217432719360 | tf_op jit(solution)/shard_map/pallas_call | solution.py:533
  463.0 44.3 %shard_map.185 = (bf16[4,2,128,2048]{3,2,1,0:T(8,128)(2,1)}, bf16[4,2,128,2048]{3,2,1,0:T(8,128)(2,1)}, bf16[8,2,128,2176]{3,2,1,0:T(8,128)(2,1)}, bf16[4,288,2048]{2,1,0:T(8,128)(2,1)}) custom-call(s32[3]{0:T(128)S(1)} %pad_add_fusion.where, f32[2,4,288,128]{3,2,1,0:T(8,128)} %copy-done.36, f32[2,4,288,2048]{3,2,1,0:T(8,128)} %get-tuple-element.305.both, ...), custom_call_target="tpu_custom_call" | custom-call | flops 217432719360 | tf_op jit(solution)/shard_map/pallas_call | solution.py:533
  507.4 12.0 %shard_map.186 = (bf16[384,2048]{1,0:T(8,128)(2,1)}, bf16[128,2048]{1,0:T(8,128)(2,1)}) custom-call(s32[3]{0:T(128)S(1)} %pad_add_fusion.where, bf16[2304,2048]{1,0:T(8,128)(2,1)} %bitcast.172, bf16[1152,2048]{1,0:T(8,128)(2,1)} %bitcast.176, bf16[1152,2048]{1,0:T(8,128)(2,1)} %bitcast.178), custom_call_target="tpu_custom_call" | custom-call | flops 48318382080 | tf_op jit(solution)/shard_map/pallas_call | solution.py:611
  521.0 24.6 %shard_map.187 = (bf16[320,2048]{1,0:T(8,128)(2,1)S(1)}, bf16[128,2048]{1,0:T(8,128)(2,1)S(1)}, bf16[64,2048]{1,0:T(8,128)(2,1)S(1)}, bf16[512,2048]{1,0:T(8,128)(2,1)}, bf16[512,2048]{1,0:T(8,128)(2,1)}) custom-call(s32[3]{0:T(128)S(1)} %pad_add_fusion.where, bf16[2304,2048]{1,0:T(8,128)(2,1)} %bitcast.173, bf16[1152,2048]{1,0:T(8,128)(2,1)} %bitcast.177, ...), custom_call_target="tpu_custom_call" | custom-call | flops 144955146240 | tf_op jit(solution)/shard_map/pallas_call | solution.py:611
  600.7 16.7 %shard_map.189 = (bf16[8,128,768]{2,1,0:T(8,128)(2,1)}, f32[2,128]{1,0:T(2,128)S(1)}) custom-call(f32[8,2,128,768]{3,2,1,0:T(8,128)} %bitcast.143, f32[2,1024,128]{2,1,0:T(8,128)S(1)} %copy-done.2, f32[2,1024,128]{2,1,0:T(8,128)S(1)} %copy-done.1, s32[2,1024,1]{2,1,0:T(8,128)S(1)} %copy-done.3, s32[2,1,1024]{2,1,0:T(1,128)S(1)} %copy-done.25, ...), custom_call_target="tpu_custom_call" | custom-call | tf_op jit(solution)/shard_map/pallas_call | solution.py:220
  639.1 11.7 %collective-permute-done.25.refs_1_ = bf16[128,2176]{1,0:T(8,128)(2,1)S(1)} collective-permute-done((bf16[128,2176]{1,0:T(8,128)(2,1)S(1)}, bf16[128,2176]{1,0:T(8,128)(2,1)S(1)}, u32[]{:S(2)}, u32[]{:S(2)}) %collective-permute-start.25) | collective-permute-done | bytes 557088 | tf_op jit(solution)/shard_map/ppermute | solution.py:819
  686.9 18.3 %all-to-all-done.3 = bf16[128,8,256]{2,0,1:T(8,128)(2,1)} async-done(((bf16[128,8,256]{2,0,1:T(8,128)(2,1)}), bf16[128,8,256]{2,0,1:T(8,128)(2,1)}, u32[]{:S(2)}, u32[]{:S(2)}) %all-to-all-start.3) | async-done | bytes 524320 | tf_op jit(solution)/shard_map/all_to_all | solution.py:1024
  714.5 17.5 %shard_map.192 = (bf16[8,128,768]{2,1,0:T(8,128)(2,1)}, f32[2,128]{1,0:T(2,128)S(1)}) custom-call(f32[8,2,128,768]{3,2,1,0:T(8,128)} %bitcast.144, f32[2,1024,128]{2,1,0:T(8,128)S(1)} %copy-done.2, f32[2,1024,128]{2,1,0:T(8,128)S(1)} %copy-done.1, s32[2,1024,1]{2,1,0:T(8,128)S(1)} %copy-done.4, s32[2,1,1024]{2,1,0:T(1,128)S(1)} %copy-done.25, ...), custom_call_target="tpu_custom_call" | custom-call | tf_op jit(solution)/shard_map/pallas_call | solution.py:220
  750.7 12.5 %shard_map.194 = (bf16[512,896]{1,0:T(8,128)(2,1)S(1)}, bf16[512,896]{1,0:T(8,128)(2,1)}, bf16[512,896]{1,0:T(8,128)(2,1)}, bf16[512,896]{1,0:T(8,128)(2,1)}) custom-call(s32[3]{0:T(128)S(1)} %pad_add_fusion.where, bf16[2048,2048]{1,0:T(8,128)(2,1)} %bitcast.148, bf16[1024,768]{1,0:T(8,128)(2,1)} %bitcast.130, bf16[1024,768]{1,0:T(8,128)(2,1)} %bitcast.131, ...), custom_call_target="tpu_custom_call" | custom-call | tf_op jit(solution)/shard_map/pallas_call | solution.py:611
  792.6 10.1 %collective-permute-done.34 = bf16[1,2,128,2048]{3,2,1,0:T(8,128)(2,1)} collective-permute-done((bf16[1,2,128,2048]{3,2,1,0:T(8,128)(2,1)}, bf16[1,2,128,2048]{3,2,1,0:T(8,128)(2,1)}, u32[]{:S(2)}, u32[]{:S(2)}) %collective-permute-start.34) | collective-permute-done | bytes 1048608 | tf_op jit(solution)/shard_map/ppermute | solution.py:963
  809.8 19.6 %collective-permute-done.32 = bf16[512,896]{1,0:T(8,128)(2,1)} collective-permute-done((bf16[512,896]{1,0:T(8,128)(2,1)}, bf16[512,896]{1,0:T(8,128)(2,1)}, u32[]{:S(2)}, u32[]{:S(2)}) %collective-permute-start.32) | collective-permute-done | bytes 917536 | tf_op jit(solution)/shard_map/ppermute | solution.py:771
  839.1 18.8 %collective-permute-start.37 = (bf16[128,2048]{1,0:T(8,128)(2,1)S(1)}, bf16[128,2048]{1,0:T(8,128)(2,1)}, u32[]{:S(2)}, u32[]{:S(2)}) collective-permute-start(bf16[128,2048]{1,0:T(8,128)(2,1)S(1)} %fusion.23), channel_id=1, source_target_pairs={{0,8},{8,0},{16,24},{24,16},{1,9},{9,1},{17,25},{25,17},{2,10},{10... | collective-permute-start | bytes 1572872 | tf_op jit(solution)/shard_map/ppermute | solution.py:819
  865.3 11.0 %collective-permute-done.37 = bf16[128,2048]{1,0:T(8,128)(2,1)} collective-permute-done((bf16[128,2048]{1,0:T(8,128)(2,1)S(1)}, bf16[128,2048]{1,0:T(8,128)(2,1)}, u32[]{:S(2)}, u32[]{:S(2)}) %collective-permute-start.37) | collective-permute-done | bytes 524320 | tf_op jit(solution)/shard_map/ppermute | solution.py:819
  (342 shorter events, 349.3 us)
Async XLA Ops:
  7.2 126.4 %all-gather.9.cloned.1.call-start = ((), (), s32[]{:S(2)}) async-start(), calls=%async_computation.15 | async-start | bytes 9437184 | tf_op jit(solution)/shard_map/all_gather | solution.py:825
  18.6 190.7 %all-gather.11.cloned.1.call-start = ((), (), s32[]{:S(2)}) async-start(), calls=%async_computation.16 | async-start | bytes 9437184 | tf_op jit(solution)/shard_map/all_gather | solution.py:825
  64.5 277.6 %all-gather.15.cloned.1.call-start = ((), (), s32[]{:S(2)}) async-start(), calls=%async_computation.18 | async-start | bytes 18874368 | tf_op jit(solution)/shard_map/all_gather | solution.py:825
  133.6 87.9 %collective-permute-start.8 = (bf16[512,2048]{1,0:T(8,128)(2,1)}, bf16[512,2048]{1,0:T(8,128)(2,1)}, u32[]{:S(2)}, u32[]{:S(2)}) collective-permute-start(bf16[512,2048]{1,0:T(8,128)(2,1)} %get-tuple-element.279), channel_id=1, source_target_pairs={{0,8},{8,0},{16,24},{24,16},{1,9},{9,1},{17,25},{25,17},{2,10},{10... | collective-permute-start | bytes 6291464 | tf_op jit(solution)/shard_map/ppermute | solution.py:771
  133.7 90.9 %collective-permute-start.9 = (bf16[512,2048]{1,0:T(8,128)(2,1)}, bf16[512,2048]{1,0:T(8,128)(2,1)}, u32[]{:S(2)}, u32[]{:S(2)}) collective-permute-start(bf16[512,2048]{1,0:T(8,128)(2,1)} %get-tuple-element.284.refs_0_), channel_id=1, source_target_pairs={{0,16},{8,24},{16,0},{24,8},{1,17},{9,25},{17,1},{25,9},{2,18},{10... | collective-permute-start | bytes 6291464 | tf_op jit(solution)/shard_map/ppermute | solution.py:771
  181.6 160.6 %all-gather.13.cloned.1.call-start = ((), (), s32[]{:S(2)}) async-start(), calls=%async_computation.17 | async-start | bytes 20054016 | tf_op jit(solution)/shard_map/all_gather | solution.py:825
  249.1 305.4 %reduce-scatter.6.cloned.1.call-start = ((), (), s32[]{:S(2)}) async-start(), calls=%async_computation.10 | async-start | bytes 10027008 | tf_op jit(solution)/shard_map/reduce_scatter | solution.py:931
  294.4 108.4 %collective-permute-start.12 = (bf16[256,2048]{1,0:T(8,128)(2,1)}, bf16[256,2048]{1,0:T(8,128)(2,1)}, u32[]{:S(2)}, u32[]{:S(2)}) collective-permute-start(bf16[256,2048]{1,0:T(8,128)(2,1)} %get-tuple-element.298), channel_id=1, source_target_pairs={{0,8},{8,0},{16,24},{24,16},{1,9},{9,1},{17,25},{25,17},{2,10},{10... | collective-permute-start | bytes 3145736 | tf_op jit(solution)/shard_map/ppermute | solution.py:771
  337.8 65.0 %collective-permute-start.13 = (bf16[256,2048]{1,0:T(8,128)(2,1)}, bf16[256,2048]{1,0:T(8,128)(2,1)}, u32[]{:S(2)}, u32[]{:S(2)}) collective-permute-start(bf16[256,2048]{1,0:T(8,128)(2,1)} %get-tuple-element.308.refs_4_), channel_id=1, source_target_pairs={{0,16},{8,24},{16,0},{24,8},{1,17},{9,25},{17,1},{25,9},{2,18},{10... | collective-permute-start | bytes 3145736 | tf_op jit(solution)/shard_map/ppermute | solution.py:771
  340.3 62.5 %collective-permute-start.14 = (bf16[160,2048]{1,0:T(8,128)(2,1)}, bf16[160,2048]{1,0:T(8,128)(2,1)}, u32[]{:S(2)}, u32[]{:S(2)}) collective-permute-start(bf16[160,2048]{1,0:T(8,128)(2,1)} %slice.145), channel_id=1, source_target_pairs={{0,24},{8,16},{16,8},{24,0},{1,25},{9,17},{17,9},{25,1},{2,26},{10... | collective-permute-start | bytes 1966088 | tf_op jit(solution)/shard_map/ppermute | solution.py:771
  457.1 178.3 %reduce-scatter.8.cloned.1.call-start = ((), (), s32[]{:S(2)}) async-start(), calls=%async_computation.11 | async-start | bytes 10027008 | tf_op jit(solution)/shard_map/reduce_scatter | solution.py:931
  459.3 88.2 %collective-permute-start.17 = (bf16[240,2048]{1,0:T(8,128)(2,1)}, bf16[240,2048]{1,0:T(8,128)(2,1)}, u32[]{:S(2)}, u32[]{:S(2)}) collective-permute-start(bf16[240,2048]{1,0:T(8,128)(2,1)} %slice.147), channel_id=1, source_target_pairs={{0,8},{8,0},{16,24},{24,16},{1,9},{9,1},{17,25},{25,17},{2,10},{10... | collective-permute-start | bytes 2949128 | tf_op jit(solution)/shard_map/ppermute | solution.py:771
  461.1 86.4 %collective-permute-start.18 = (bf16[256,2048]{1,0:T(8,128)(2,1)}, bf16[256,2048]{1,0:T(8,128)(2,1)}, u32[]{:S(2)}, u32[]{:S(2)}) collective-permute-start(bf16[256,2048]{1,0:T(8,128)(2,1)} %copy-done.31), channel_id=1, source_target_pairs={{0,16},{8,24},{16,0},{24,8},{1,17},{9,25},{17,1},{25,9},{2,18},{10... | collective-permute-start | bytes 3145736 | tf_op jit(solution)/shard_map/ppermute | solution.py:771
  565.7 59.1 %collective-permute-start.23 = (bf16[512,2048]{1,0:T(8,128)(2,1)}, bf16[512,2048]{1,0:T(8,128)(2,1)}, u32[]{:S(2)}, u32[]{:S(2)}) collective-permute-start(bf16[512,2048]{1,0:T(8,128)(2,1)} %get-tuple-element.353), channel_id=1, source_target_pairs={{0,24},{8,0},{16,8},{24,16},{1,25},{9,1},{17,9},{25,17},{2,26},{10... | collective-permute-start | bytes 6291464 | tf_op jit(solution)/shard_map/ppermute | solution.py:767
  581.8 153.7 %reduce-scatter.10.cloned.1.call-start = ((), (), s32[]{:S(2)}) async-start(), calls=%async_computation.12 | async-start | bytes 4718592 | tf_op jit(solution)/shard_map/reduce_scatter | solution.py:1055
  635.4 74.6 %collective-permute-start.26 = (bf16[2,2,128,2048]{3,2,1,0:T(8,128)(2,1)}, bf16[2,2,128,2048]{3,2,1,0:T(8,128)(2,1)}, u32[]{:S(2)}, u32[]{:S(2)}) collective-permute-start(bf16[2,2,128,2048]{3,2,1,0:T(8,128)(2,1)} %get-tuple-element.371), channel_id=1, source_target_pairs={{0,2},{1,3},{2,0},{3,1},{4,6},{5,7},{6,4},{7,5},{8,10},{9,11},{10,... | collective-permute-start | bytes 6291464 | tf_op jit(solution)/shard_map/ppermute | solution.py:963
  635.7 74.3 %collective-permute-start.27 = (bf16[2,2,128,2048]{3,2,1,0:T(8,128)(2,1)}, bf16[2,2,128,2048]{3,2,1,0:T(8,128)(2,1)}, u32[]{:S(2)}, u32[]{:S(2)}) collective-permute-start(bf16[2,2,128,2048]{3,2,1,0:T(8,128)(2,1)} %get-tuple-element.373), channel_id=1, source_target_pairs={{0,4},{1,5},{2,6},{3,7},{4,0},{5,1},{6,2},{7,3},{8,12},{9,13},{10,... | collective-permute-start | bytes 6291464 | tf_op jit(solution)/shard_map/ppermute | solution.py:963
  650.8 59.2 %collective-permute-start.28 = (bf16[320,2048]{1,0:T(8,128)(2,1)}, bf16[320,2048]{1,0:T(8,128)(2,1)}, u32[]{:S(2)}, u32[]{:S(2)}) collective-permute-start(bf16[320,2048]{1,0:T(8,128)(2,1)} %copy-done.30), channel_id=1, source_target_pairs={{0,16},{8,24},{16,0},{24,8},{1,17},{9,25},{17,1},{25,9},{2,18},{10... | collective-permute-start | bytes 3932168 | tf_op jit(solution)/shard_map/ppermute | solution.py:767
  671.0 158.4 %reduce-scatter.12.cloned.1.call-start = ((), (), s32[]{:S(2)}) async-start(), calls=%async_computation.13 | async-start | bytes 9437184 | tf_op jit(solution)/shard_map/reduce_scatter | solution.py:1030
  710.0 166.3 %reduce-scatter.14.cloned.1.call-start = ((), (), s32[]{:S(2)}) async-start(), calls=%async_computation.14 | async-start | bytes 4718592 | tf_op jit(solution)/shard_map/reduce_scatter | solution.py:1094
  765.5 63.9 %collective-permute-start.32 = (bf16[512,896]{1,0:T(8,128)(2,1)}, bf16[512,896]{1,0:T(8,128)(2,1)}, u32[]{:S(2)}, u32[]{:S(2)}) collective-permute-start(bf16[512,896]{1,0:T(8,128)(2,1)} %get-tuple-element.421), channel_id=1, source_target_pairs={{0,16},{8,24},{16,0},{24,8},{1,17},{9,25},{17,1},{25,9},{2,18},{10... | collective-permute-start | bytes 2752520 | tf_op jit(solution)/shard_map/ppermute | solution.py:771
  767.6 61.8 %collective-permute-start.33 = (bf16[512,896]{1,0:T(8,128)(2,1)}, bf16[512,896]{1,0:T(8,128)(2,1)}, u32[]{:S(2)}, u32[]{:S(2)}) collective-permute-start(bf16[512,896]{1,0:T(8,128)(2,1)} %get-tuple-element.422), channel_id=1, source_target_pairs={{0,24},{8,16},{16,8},{24,0},{1,25},{9,17},{17,9},{25,1},{2,26},{10... | collective-permute-start | bytes 2752520 | tf_op jit(solution)/shard_map/ppermute | solution.py:771
  805.3 60.0 %collective-permute-start.35 = (bf16[128,2048]{1,0:T(8,128)(2,1)}, bf16[128,2048]{1,0:T(8,128)(2,1)}, u32[]{:S(2)}, u32[]{:S(2)}) collective-permute-start(bf16[128,2048]{1,0:T(8,128)(2,1)} %fusion.22), channel_id=1, source_target_pairs={{0,8},{8,0},{16,24},{24,16},{1,9},{9,1},{17,25},{25,17},{2,10},{10... | collective-permute-start | bytes 1572872 | tf_op jit(solution)/shard_map/ppermute | solution.py:819
  834.0 53.8 %all-to-all-start.4 = ((bf16[8,64,896]{2,1,0:T(8,128)(2,1)}), bf16[8,64,896]{2,1,0:T(8,128)(2,1)S(1)}, u32[]{:S(2)}, u32[]{:S(2)}) async-start(bf16[8,64,896]{2,1,0:T(8,128)(2,1)} %bitcast.154), calls=%async_computation.8 | async-start | bytes 1835008 | tf_op jit(solution)/shard_map/all_to_all | solution.py:1117
  (96 other events, 2272.0 us)
Sparse Core Ops, SparseCore 0:
  9.9 64.3 all-gather.8
  76.8 54.3 all-gather.10
  133.7 100.4 all-gather.14
  249.2 92.2 all-gather.12
  457.3 74.8 reduce-scatter.5
  535.6 79.3 reduce-scatter.7
  635.5 68.7 reduce-scatter.9
  710.2 77.5 reduce-scatter.11
  791.1 54.7 reduce-scatter.13

commit v17 on v16

--- a/solution.py
+++ b/solution.py
@@ -577,11 +577,15 @@
     width = width // planes
     step = min(TILE, columns & -columns)
     tails = [] if tail is None else [tail]
-    whole = columns + sum(value.shape[1] for value in tails)
+    split = columns // 3 * 2 if tails else columns
+    wholes = [split, columns - split + tail.shape[1]] if tails else [split]
 
     ends = [cut_ends(width, (cuts or {}).get(number, ())) for number in range(steps)]
     shapes = [
-        out((end - start, whole)) for one in ends for start, end in zip(one, one[1:])
+        out((end - start, whole))
+        for one in ends
+        for start, end in zip(one, one[1:])
+        for whole in wholes
     ]
 
     def of_plane(i, where):
@@ -592,20 +596,23 @@
 
         def fill(targets, ends):
             for value in tails:
-                targets[0][:, columns:] = value[...]
+                targets[1][:, columns - split :] = value[...]
             for number in range(columns // step):
                 at = slice(number * step, (number + 1) * step)
                 result = sum(
                     dot(left[part * part_rows : (part + 1) * part_rows], right[:, at], ((0,), (0,)))
                     for part, right in enumerate(rights)
                 ).astype(bf16)
-                for target, start, end in zip(targets, ends, ends[1:]):
+                if at.start >= split:
+                    targets[1][:, at.start - split : at.stop - split] = result
+                    continue
+                for target, start, end in zip(targets[:: len(wholes)], ends, ends[1:]):
                     target[:, at] = result[start:end]
 
         done = 0
         for number, one in enumerate(ends):
-            mine = targets[done : done + len(one) - 1]
-            done += len(one) - 1
+            mine = targets[done : done + (len(one) - 1) * len(wholes)]
+            done += len(mine)
             pl.when(pl.program_id(0) == number)(lambda mine=mine, one=one: fill(mine, one))
 
     return pl.pallas_call(
@@ -741,25 +748,26 @@
     )(weight, tail)
 
 
-def unpack(packed, count):
-    ranks, rows, columns = packed.shape
-    width = (columns - PAD) // 3
-
-    def kernel(packed, main, small):
+def unpack(heads, others, count):
+    ranks, rows, columns = heads.shape
+    width = columns // 2
+
+    def kernel(heads, others, main, small):
         for rank in range(ranks):
             for part in range(3):
                 at = part * D + rank * width
-                main[:, at : at + width] = packed[rank, :, part * width : (part + 1) * width].astype(
-                    f32
-                )
-        tails = sum(packed[rank, :, 3 * width :].astype(f32) for rank in range(ranks))
+                value = heads[rank, :, part * width : (part + 1) * width] if part < 2 else others[
+                    rank, :, :width
+                ]
+                main[:, at : at + width] = value.astype(f32)
+        tails = sum(others[rank, :, width:].astype(f32) for rank in range(ranks))
         small[...] = tails + pltpu.roll(tails, PAD - count, 1)
 
     return pl.pallas_call(
         kernel,
         out_shape=[out((rows, 3 * D), f32), out((rows, PAD), f32)],
         compiler_params=params(),
-    )(packed)
+    )(heads, others)
 
 
 def shift_rep(value, step):
@@ -952,7 +960,7 @@
         where, planes, rows_flat, grads_flat, first=1, steps=1, shift=True, cuts={0: (24,)}
     )
     rows_flat, in_near = lax.optimization_barrier((rows_flat, in_near))
-    cuts = {number: (20, 28) for number in range(planes - 3)}
+    cuts = {number: (19, 28) for number in range(planes - 3)}
     *in_rest, in_back, in_own = weight_gradient(
         where, planes, rows_flat, grads_flat, first=2, steps=last_step, shift=True, cuts=cuts
     )
@@ -1089,13 +1097,16 @@
     packed, rest_sent, out_cut, out_sent, crossed = lax.optimization_barrier(
         (packed, rest_sent, out_cut, out_sent, crossed)
     )
-    packed_sent = [packed[0]] + [cross_rep(packed[step], step) for step in range(1, planes)]
+    heads, others = packed[::2], packed[1::2]
+    heads_sent = [heads[0]] + [cross_rep(heads[step], step) for step in range(1, planes)]
+    heads_sent, others = lax.optimization_barrier((heads_sent, others))
+    others_sent = [others[0]] + [cross_rep(others[step], step) for step in range(1, planes)]
     normed_sums.append(
         lax.psum_scatter(
             after(grad_inputs[-1][1], packed), "ep", scatter_dimension=0, tiled=True
         )
     )
-    packed_sent, out_sum = lax.optimization_barrier((packed_sent, out_sum))
+    others_sent, out_sum = lax.optimization_barrier((others_sent, out_sum))
     for phase in range(1, len(bits)):
         mixtures = [total(parts).astype(bf16) for parts in crossed]
         crossed = [
@@ -1111,10 +1122,14 @@
         cross_rep(lax.dynamic_index_in_dim(out_sum, plane ^ step, 0, keepdims=False), step)
         for step in range(1, planes)
     ]
-    main = total([part[:, : 3 * width] for part in packed_sent]).astype(bf16)
-    small = sum(joined(part[:, 3 * width :]) for part in packed_sent)
-    packed = jnp.concatenate([main, halves(small)], axis=1).reshape(ranks, dense_rows, -1)
-    packed = lax.all_to_all(packed, "ep", split_axis=0, concat_axis=0, tiled=True)
+    def to_ranks(value):
+        value = value.reshape(ranks, dense_rows, -1)
+        return lax.all_to_all(value, "ep", split_axis=0, concat_axis=0, tiled=True)
+
+    heads = to_ranks(total(heads_sent).astype(bf16))
+    main = total([part[:, :width] for part in others_sent]).astype(bf16)
+    small = sum(joined(part[:, width:]) for part in others_sent)
+    packed = (heads, to_ranks(jnp.concatenate([main, halves(small)], axis=1)))
     packed, mixture, out_sent_back, normed_sums = lax.optimization_barrier(
         (packed, mixture, out_sent_back, normed_sums)
     )
@@ -1131,7 +1146,7 @@
     output = jnp.concatenate([mine_part + total(others) for mine_part, others in mixture], axis=0)
     output = (hidden + output).astype(bf16)
     grad_w_o = total([own_sum, *out_sent_back])
-    grad_w_qkv, small = unpack(packed, count)
+    grad_w_qkv, small = unpack(*packed, count)
     out_sent[1] = jnp.concatenate([first, out_sent[1]], axis=0)
     grad_w_out = sum_rep({0: out_cut[0], **out_sent})
     in_sent[1] = jnp.concatenate(near_sent, axis=0)

time: 917 us -> 916 us (level)
  waiting for transfers between devices: 290 us -> 280 us
    ppermute x20 -> x23, starting transfers between devices: 78.5 us -> 94.7 us  [cross_rep(): lax.ppermute(value, 'rep', [(i, i ^ bits) for i in range(lax.axis_size('r...]
    ppermute x6, starting transfers between devices: 25.3 us -> 9.06 us  [exchange(): return lax.ppermute(value, 'rep', pairs)]
    ppermute x6, waiting for transfers between devices: 10.1 us -> 0.02 us  [swap(): return lax.ppermute(value, 'ep', [(i, i ^ step) for i in range(ranks)])]
    ppermute x20 -> x23, waiting for transfers between devices: 92.3 us -> 101 us  [cross_rep(): lax.ppermute(value, 'rep', [(i, i ^ bits) for i in range(lax.axis_size('r...]
    unnamed x136 -> x150, local copies, waits for them, and re-layouts: 25.5 us -> 25.3 us
  transfers between devices with their start and end apart: 55 -> 59, of which waited for: 26 -> 27; matrix products, arithmetic and copies ran while one was open for 13% -> 13% of each run, Pallas kernels for 34% -> 34%
where the time goes in v17:
time: 916 us; the launch traced here: 906 us
  Pallas kernels  311 us (34%)
  waiting for transfers between devices  280 us (31%)
  starting transfers between devices  149 us (16%)
  local copies, waits for them, and re-layouts  74.6 us (8%)
  other arithmetic  67 us (7%)
  between operations  15.2 us (2%)
  matrix products  10 us (1%)
    ppermute x23, waiting for transfers between devices, cross_rep(): lax.ppermute(value, 'rep', [(i, i ^ bits) for i in range(lax.axis_size('r...  101 us
    ppermute x23, starting transfers between devices, cross_rep(): lax.ppermute(value, 'rep', [(i, i ^ bits) for i in range(lax.axis_size('r...  94.7 us
    pallas_call x2, Pallas kernels, expert_backward(): pl.pallas_call(kernel, grid_spec=pltpu.PrefetchScalarGridSpec(num_scalar_...  85.3 us
    ppermute x6, waiting for transfers between devices, exchange(): return lax.ppermute(value, 'rep', pairs)  68.4 us
    ppermute x9, waiting for transfers between devices, shift_rep(): lax.ppermute(value, 'rep', [(i, (i + step) % count) for i in range(count)])  66.5 us
    pallas_call x4, Pallas kernels, weight_gradient(): pl.pallas_call(kernel, grid_spec=pltpu.PrefetchScalarGridSpec(num_scalar_...  65.2 us
    pallas_call x1, Pallas kernels, expert_forward(): pl.pallas_call(kernel, grid_spec=pltpu.PrefetchScalarGridSpec(num_scalar_...  40.3 us
    pallas_call x2, Pallas kernels, attention_backward(): pl.pallas_call(lambda *refs: backward_kernel(heads, *refs), grid=(1,), in...  34.4 us
  transfers between devices with their start and end apart: 59, of which 27 were waited for; matrix products, arithmetic and copies ran while one was open for 13% of the time, Pallas kernels for 34%

profile of v17, /device:TPU:0, one launch (start us, length us, event | category | flops | bytes accessed | tf_op | source)
XLA Modules:
  0.0 906.2 jit_solution(5732980689563986196)
XLA Ops:
  26.6 22.7 %collective-permute-done.3 = bf16[256,2048]{1,0:T(8,128)(2,1)} collective-permute-done((bf16[256,2048]{1,0:T(8,128)(2,1)}, bf16[256,2048]{1,0:T(8,128)(2,1)}, u32[]{:S(2)}, u32[]{:S(2)}) %collective-permute-start.3) | collective-permute-done | bytes 1048608 | tf_op jit(solution)/shard_map/ppermute | solution.py:827
  67.6 20.9 %collective-permute-done.5 = bf16[512,896]{1,0:T(8,128)(2,1)S(1)} collective-permute-done((bf16[512,896]{1,0:T(8,128)(2,1)S(1)}, bf16[512,896]{1,0:T(8,128)(2,1)S(1)}, u32[]{:S(2)}, u32[]{:S(2)}) %collective-permute-start.5) | collective-permute-done | bytes 917536 | tf_op jit(solution)/shard_map/ppermute | solution.py:775
  100.2 10.4 %collective-permute-done.6 = bf16[512,896]{1,0:T(8,128)(2,1)} collective-permute-done((bf16[512,896]{1,0:T(8,128)(2,1)S(1)}, bf16[512,896]{1,0:T(8,128)(2,1)}, u32[]{:S(2)}, u32[]{:S(2)}) %collective-permute-start.6) | collective-permute-done | bytes 917536 | tf_op jit(solution)/shard_map/ppermute | solution.py:775
  117.0 15.0 %collective-permute-done.7 = bf16[512,896]{1,0:T(8,128)(2,1)S(1)} collective-permute-done((bf16[512,896]{1,0:T(8,128)(2,1)}, bf16[512,896]{1,0:T(8,128)(2,1)S(1)}, u32[]{:S(2)}, u32[]{:S(2)}) %collective-permute-start.7) | collective-permute-done | bytes 917536 | tf_op jit(solution)/shard_map/ppermute | solution.py:775
  136.7 15.8 %shard_map.179 = (bf16[2,8,128,2048]{3,2,1,0:T(8,128)(2,1)}, f32[8,256,768]{2,1,0:T(8,128)}) custom-call(bf16[8,256,2048]{2,1,0:T(8,128)(2,1)} %bitcast.140, f32[1,2048]{1,0:T(1,128)S(1)} %broadcast_in_dim.56.gain, bf16[2048,896]{1,0:T(8,128)(2,1)} %constant_dynamic-update-slice_fusion.weight), custom_call_target="tpu_custom_call" | custom-call | tf_op jit(solution)/shard_map/pallas_call | solution.py:248
  152.6 21.8 %shard_map.180 = (bf16[8,2,128,256]{3,2,1,0:T(8,128)(2,1)}, bf16[2,1024,256]{2,1,0:T(8,128)(2,1)S(1)}, bf16[2,1024,256]{2,1,0:T(8,128)(2,1)S(1)}, bf16[2,1024,256]{2,1,0:T(8,128)(2,1)}, f32[2,2,1024,1]{3,2,1,0:T(8,128)}) custom-call(f32[8,2,128,768]{3,2,1,0:T(8,128)} %bitcast.143, f32[2,1024,128]{2,1,0:T(8,128)} %get-tuple-element.265.refs_1_, ...), custom_call_target="tpu_custom_call" | custom-call | tf_op jit(solution)/shard_map/pallas_call | solution.py:198
  182.7 25.1 %all-to-all-done.1 = bf16[8,2,128,256]{3,2,1,0:T(8,128)(2,1)S(1)} async-done(((bf16[8,2,128,256]{3,2,1,0:T(8,128)(2,1)}), bf16[8,2,128,256]{3,2,1,0:T(8,128)(2,1)S(1)}, u32[]{:S(2)}, u32[]{:S(2)}) %all-to-all-start.1) | async-done | bytes 1048608 | tf_op jit(solution)/shard_map/all_to_all | solution.py:889
  223.1 23.7 %collective-permute-done.10 = bf16[256,2176]{1,0:T(8,128)(2,1)S(1)} collective-permute-done((bf16[256,2176]{1,0:T(8,128)(2,1)S(1)}, bf16[256,2176]{1,0:T(8,128)(2,1)S(1)}, u32[]{:S(2)}, u32[]{:S(2)}) %collective-permute-start.10) | collective-permute-done | bytes 1114144 | tf_op jit(solution)/shard_map/ppermute | solution.py:827
  250.9 43.8 %collective-permute-done.11.refs_3_ = bf16[512,2048]{1,0:T(8,128)(2,1)} collective-permute-done((bf16[512,2048]{1,0:T(8,128)(2,1)}, bf16[512,2048]{1,0:T(8,128)(2,1)}, u32[]{:S(2)}, u32[]{:S(2)}) %collective-permute-start.11) | collective-permute-done | bytes 2097184 | tf_op jit(solution)/shard_map/ppermute | solution.py:779
  294.7 42.9 %collective-permute-start.12 = (bf16[256,2048]{1,0:T(8,128)(2,1)}, bf16[256,2048]{1,0:T(8,128)(2,1)}, u32[]{:S(2)}, u32[]{:S(2)}) collective-permute-start(bf16[256,2048]{1,0:T(8,128)(2,1)} %get-tuple-element.315), channel_id=1, source_target_pairs={{0,8},{8,0},{16,24},{24,16},{1,9},{9,1},{17,25},{25,17},{2,10},{10... | collective-permute-start | bytes 3145736 | tf_op jit(solution)/shard_map/ppermute | solution.py:779
  342.0 40.3 %shard_map.182 = (bf16[2,4,288,2048]{3,2,1,0:T(8,128)(2,1)}, f32[2,4,288,128]{3,2,1,0:T(8,128)S(1)}, f32[2,4,288,2048]{3,2,1,0:T(8,128)}, bf16[2,4,288,1024]{3,2...) custom-call(s32[3]{0:T(128)S(1)} %pad_add_fusion.where, ...), custom_call_target="tpu_custom_call" | custom-call | flops 241591910400 | tf_op jit(solution)/shard_map/pallas_call | solution.py:435
  383.7 16.8 %shard_map.183 = (bf16[256,2048]{1,0:T(8,128)(2,1)S(1)}, bf16[256,2048]{1,0:T(8,128)(2,1)S(1)}, bf16[256,2048]{1,0:T(8,128)(2,1)S(1)}, bf16[256,2048]{1,0:T(8,128)(2,1)}) custom-call(s32[3]{0:T(128)S(1)} %pad_add_fusion.where, bf16[2304,1024]{1,0:T(8,128)(2,1)} %bitcast.175, bf16[2304,2048]{1,0:T(8,128)(2,1)} %bitcast.174), custom_call_target="tpu_custom_call" | custom-call | flops 96636764160 | tf_op jit(solution)/shard_map/pallas_call | solution.py:618
  416.0 40.7 %shard_map.184 = (bf16[4,2,128,2048]{3,2,1,0:T(8,128)(2,1)}, bf16[4,2,128,2048]{3,2,1,0:T(8,128)(2,1)}, bf16[8,2,128,2176]{3,2,1,0:T(8,128)(2,1)}, bf16[4,288,2048]{2,1,0:T(8,128)(2,1)}) custom-call(s32[3]{0:T(128)S(1)} %pad_add_fusion.where, f32[2,4,288,128]{3,2,1,0:T(8,128)} %copy-done.40, f32[2,4,288,2048]{3,2,1,0:T(8,128)} %get-tuple-element.322.both, ...), custom_call_target="tpu_custom_call" | custom-call | flops 217432719360 | tf_op jit(solution)/shard_map/pallas_call | solution.py:533
  462.3 44.6 %shard_map.185 = (bf16[4,2,128,2048]{3,2,1,0:T(8,128)(2,1)}, bf16[4,2,128,2048]{3,2,1,0:T(8,128)(2,1)}, bf16[8,2,128,2176]{3,2,1,0:T(8,128)(2,1)}, bf16[4,288,2048]{2,1,0:T(8,128)(2,1)}) custom-call(s32[3]{0:T(128)S(1)} %pad_add_fusion.where, f32[2,4,288,128]{3,2,1,0:T(8,128)} %copy-done.40, f32[2,4,288,2048]{3,2,1,0:T(8,128)} %get-tuple-element.322.both, ...), custom_call_target="tpu_custom_call" | custom-call | flops 217432719360 | tf_op jit(solution)/shard_map/pallas_call | solution.py:533
  506.8 12.0 %shard_map.186 = (bf16[384,2048]{1,0:T(8,128)(2,1)}, bf16[128,2048]{1,0:T(8,128)(2,1)}) custom-call(s32[3]{0:T(128)S(1)} %pad_add_fusion.where, bf16[2304,2048]{1,0:T(8,128)(2,1)} %bitcast.172, bf16[1152,2048]{1,0:T(8,128)(2,1)} %bitcast.176, bf16[1152,2048]{1,0:T(8,128)(2,1)} %bitcast.178), custom_call_target="tpu_custom_call" | custom-call | flops 48318382080 | tf_op jit(solution)/shard_map/pallas_call | solution.py:618
  520.3 24.3 %shard_map.187 = (bf16[304,2048]{1,0:T(8,128)(2,1)S(1)}, bf16[144,2048]{1,0:T(8,128)(2,1)S(1)}, bf16[64,2048]{1,0:T(8,128)(2,1)}, bf16[512,2048]{1,0:T(8,128)(2,1)}, bf16[512,2048]{1,0:T(8,128)(2,1)}) custom-call(s32[3]{0:T(128)S(1)} %pad_add_fusion.where, bf16[2304,2048]{1,0:T(8,128)(2,1)} %bitcast.173, bf16[1152,2048]{1,0:T(8,128)(2,1)} %bitcast.177, ...), custom_call_target="tpu_custom_call" | custom-call | flops 144955146240 | tf_op jit(solution)/shard_map/pallas_call | solution.py:618
  599.0 17.5 %shard_map.189 = (bf16[8,128,768]{2,1,0:T(8,128)(2,1)}, f32[2,128]{1,0:T(2,128)S(1)}) custom-call(f32[8,2,128,768]{3,2,1,0:T(8,128)} %bitcast.144, f32[2,1024,128]{2,1,0:T(8,128)S(1)} %copy-done.2, f32[2,1024,128]{2,1,0:T(8,128)S(1)} %copy-done.1, s32[2,1024,1]{2,1,0:T(8,128)S(1)} %copy-done.3, s32[2,1,1024]{2,1,0:T(1,128)S(1)} %copy-done.25, ...), custom_call_target="tpu_custom_call" | custom-call | tf_op jit(solution)/shard_map/pallas_call | solution.py:220
  640.7 11.7 %collective-permute-done.25.refs_1_ = bf16[128,2176]{1,0:T(8,128)(2,1)S(1)} collective-permute-done((bf16[128,2176]{1,0:T(8,128)(2,1)S(1)}, bf16[128,2176]{1,0:T(8,128)(2,1)S(1)}, u32[]{:S(2)}, u32[]{:S(2)}) %collective-permute-start.25) | collective-permute-done | bytes 557088 | tf_op jit(solution)/shard_map/ppermute | solution.py:827
  688.5 17.5 %all-to-all-done.3 = bf16[128,8,256]{2,0,1:T(8,128)(2,1)} async-done(((bf16[128,8,256]{2,0,1:T(8,128)(2,1)}), bf16[128,8,256]{2,0,1:T(8,128)(2,1)}, u32[]{:S(2)}, u32[]{:S(2)}) %all-to-all-start.3) | async-done | bytes 524320 | tf_op jit(solution)/shard_map/all_to_all | solution.py:1032
  713.5 17.0 %shard_map.192 = (bf16[8,128,768]{2,1,0:T(8,128)(2,1)}, f32[2,128]{1,0:T(2,128)S(1)}) custom-call(f32[8,2,128,768]{3,2,1,0:T(8,128)} %bitcast.145, f32[2,1024,128]{2,1,0:T(8,128)S(1)} %copy-done.2, f32[2,1024,128]{2,1,0:T(8,128)S(1)} %copy-done.1, s32[2,1024,1]{2,1,0:T(8,128)S(1)} %copy-done.4, s32[2,1,1024]{2,1,0:T(1,128)S(1)} %copy-done.25, ...), custom_call_target="tpu_custom_call" | custom-call | tf_op jit(solution)/shard_map/pallas_call | solution.py:220
  750.8 12.1 %shard_map.194 = (bf16[512,512]{1,0:T(8,128)(2,1)S(1)}, bf16[512,384]{1,0:T(8,128)(2,1)S(1)}, bf16[512,512]{1,0:T(8,128)(2,1)}, bf16[512,384]{1,0:T(8,128)(2,1)S...) custom-call(s32[3]{0:T(128)S(1)} %pad_add_fusion.where, ...), custom_call_target="tpu_custom_call" | custom-call | tf_op jit(solution)/shard_map/pallas_call | solution.py:618
  792.4 10.9 %collective-permute-done.32 = bf16[512,512]{1,0:T(8,128)(2,1)} collective-permute-done((bf16[512,512]{1,0:T(8,128)(2,1)}, bf16[512,512]{1,0:T(8,128)(2,1)}, u32[]{:S(2)}, u32[]{:S(2)}) %collective-permute-start.32) | collective-permute-done | bytes 524320 | tf_op jit(solution)/shard_map/ppermute | solution.py:779
  809.4 10.3 %collective-permute-start.34 = (bf16[512,384]{1,0:T(8,128)(2,1)S(1)}, bf16[512,384]{1,0:T(8,128)(2,1)S(1)}, u32[]{:S(2)}, u32[]{:S(2)}) collective-permute-start(bf16[512,384]{1,0:T(8,128)(2,1)S(1)} %copy-done.38), channel_id=1, source_target_pairs={{0,8},{8,0},{16,24},{24,16},{1,9},{9,1},{17,25},{25,17},{2,10},{10... | collective-permute-start | bytes 1179656 | tf_op jit(solution)/shard_map/ppermute | solution.py:779
  836.1 13.4 %collective-permute-done.35 = bf16[512,384]{1,0:T(8,128)(2,1)S(1)} collective-permute-done((bf16[512,384]{1,0:T(8,128)(2,1)S(1)}, bf16[512,384]{1,0:T(8,128)(2,1)S(1)}, u32[]{:S(2)}, u32[]{:S(2)}) %collective-permute-start.35) | collective-permute-done | bytes 393248 | tf_op jit(solution)/shard_map/ppermute | solution.py:779
  (365 shorter events, 359.9 us)
Async XLA Ops:
  7.2 125.8 %all-gather.9.cloned.1.call-start = ((), (), s32[]{:S(2)}) async-start(), calls=%async_computation.16 | async-start | bytes 9437184 | tf_op jit(solution)/shard_map/all_gather | solution.py:833
  18.6 190.1 %all-gather.11.cloned.1.call-start = ((), (), s32[]{:S(2)}) async-start(), calls=%async_computation.17 | async-start | bytes 9437184 | tf_op jit(solution)/shard_map/all_gather | solution.py:833
  64.3 277.7 %all-gather.15.cloned.1.call-start = ((), (), s32[]{:S(2)}) async-start(), calls=%async_computation.19 | async-start | bytes 18874368 | tf_op jit(solution)/shard_map/all_gather | solution.py:833
  133.0 88.1 %collective-permute-start.8 = (bf16[512,2048]{1,0:T(8,128)(2,1)}, bf16[512,2048]{1,0:T(8,128)(2,1)}, u32[]{:S(2)}, u32[]{:S(2)}) collective-permute-start(bf16[512,2048]{1,0:T(8,128)(2,1)} %get-tuple-element.296), channel_id=1, source_target_pairs={{0,8},{8,0},{16,24},{24,16},{1,9},{9,1},{17,25},{25,17},{2,10},{10... | collective-permute-start | bytes 6291464 | tf_op jit(solution)/shard_map/ppermute | solution.py:779
  133.1 90.0 %collective-permute-start.9 = (bf16[512,2048]{1,0:T(8,128)(2,1)}, bf16[512,2048]{1,0:T(8,128)(2,1)}, u32[]{:S(2)}, u32[]{:S(2)}) collective-permute-start(bf16[512,2048]{1,0:T(8,128)(2,1)} %get-tuple-element.301.refs_0_), channel_id=1, source_target_pairs={{0,16},{8,24},{16,0},{24,8},{1,17},{9,25},{17,1},{25,9},{2,18},{10... | collective-permute-start | bytes 6291464 | tf_op jit(solution)/shard_map/ppermute | solution.py:779
  180.9 161.1 %all-gather.13.cloned.1.call-start = ((), (), s32[]{:S(2)}) async-start(), calls=%async_computation.18 | async-start | bytes 20054016 | tf_op jit(solution)/shard_map/all_gather | solution.py:833
  248.5 303.1 %reduce-scatter.6.cloned.1.call-start = ((), (), s32[]{:S(2)}) async-start(), calls=%async_computation.11 | async-start | bytes 10027008 | tf_op jit(solution)/shard_map/reduce_scatter | solution.py:939
  294.7 107.8 %collective-permute-start.12 = (bf16[256,2048]{1,0:T(8,128)(2,1)}, bf16[256,2048]{1,0:T(8,128)(2,1)}, u32[]{:S(2)}, u32[]{:S(2)}) collective-permute-start(bf16[256,2048]{1,0:T(8,128)(2,1)} %get-tuple-element.315), channel_id=1, source_target_pairs={{0,8},{8,0},{16,24},{24,16},{1,9},{9,1},{17,25},{25,17},{2,10},{10... | collective-permute-start | bytes 3145736 | tf_op jit(solution)/shard_map/ppermute | solution.py:779
  337.6 64.9 %collective-permute-start.13 = (bf16[256,2048]{1,0:T(8,128)(2,1)}, bf16[256,2048]{1,0:T(8,128)(2,1)}, u32[]{:S(2)}, u32[]{:S(2)}) collective-permute-start(bf16[256,2048]{1,0:T(8,128)(2,1)} %get-tuple-element.325.refs_4_), channel_id=1, source_target_pairs={{0,16},{8,24},{16,0},{24,8},{1,17},{9,25},{17,1},{25,9},{2,18},{10... | collective-permute-start | bytes 3145736 | tf_op jit(solution)/shard_map/ppermute | solution.py:779
  339.6 62.9 %collective-permute-start.14 = (bf16[160,2048]{1,0:T(8,128)(2,1)}, bf16[160,2048]{1,0:T(8,128)(2,1)}, u32[]{:S(2)}, u32[]{:S(2)}) collective-permute-start(bf16[160,2048]{1,0:T(8,128)(2,1)} %slice.145), channel_id=1, source_target_pairs={{0,24},{8,16},{16,8},{24,0},{1,25},{9,17},{17,9},{25,1},{2,26},{10... | collective-permute-start | bytes 1966088 | tf_op jit(solution)/shard_map/ppermute | solution.py:779
  414.9 47.4 %collective-permute-start.16 = (bf16[256,2048]{1,0:T(8,128)(2,1)}, bf16[256,2048]{1,0:T(8,128)(2,1)}, u32[]{:S(2)}, u32[]{:S(2)}) collective-permute-start(bf16[256,2048]{1,0:T(8,128)(2,1)} %get-tuple-element.333), channel_id=1, source_target_pairs={{0,24},{8,16},{16,8},{24,0},{1,25},{9,17},{17,9},{25,1},{2,26},{10... | collective-permute-start | bytes 3145736 | tf_op jit(solution)/shard_map/ppermute | solution.py:779
  456.7 176.4 %reduce-scatter.8.cloned.1.call-start = ((), (), s32[]{:S(2)}) async-start(), calls=%async_computation.12 | async-start | bytes 10027008 | tf_op jit(solution)/shard_map/reduce_scatter | solution.py:939
  458.9 87.5 %collective-permute-start.17 = (bf16[240,2048]{1,0:T(8,128)(2,1)}, bf16[240,2048]{1,0:T(8,128)(2,1)}, u32[]{:S(2)}, u32[]{:S(2)}) collective-permute-start(bf16[240,2048]{1,0:T(8,128)(2,1)} %slice.147), channel_id=1, source_target_pairs={{0,8},{8,0},{16,24},{24,16},{1,9},{9,1},{17,25},{25,17},{2,10},{10... | collective-permute-start | bytes 2949128 | tf_op jit(solution)/shard_map/ppermute | solution.py:779
  460.5 86.0 %collective-permute-start.18 = (bf16[256,2048]{1,0:T(8,128)(2,1)}, bf16[256,2048]{1,0:T(8,128)(2,1)}, u32[]{:S(2)}, u32[]{:S(2)}) collective-permute-start(bf16[256,2048]{1,0:T(8,128)(2,1)} %copy-done.31), channel_id=1, source_target_pairs={{0,16},{8,24},{16,0},{24,8},{1,17},{9,25},{17,1},{25,9},{2,18},{10... | collective-permute-start | bytes 3145736 | tf_op jit(solution)/shard_map/ppermute | solution.py:779
  563.1 59.4 %collective-permute-start.23 = (bf16[512,2048]{1,0:T(8,128)(2,1)}, bf16[512,2048]{1,0:T(8,128)(2,1)}, u32[]{:S(2)}, u32[]{:S(2)}) collective-permute-start(bf16[512,2048]{1,0:T(8,128)(2,1)} %get-tuple-element.370), channel_id=1, source_target_pairs={{0,24},{8,0},{16,8},{24,16},{1,25},{9,1},{17,9},{25,17},{2,26},{10... | collective-permute-start | bytes 6291464 | tf_op jit(solution)/shard_map/ppermute | solution.py:775
  582.4 154.6 %reduce-scatter.10.cloned.1.call-start = ((), (), s32[]{:S(2)}) async-start(), calls=%async_computation.13 | async-start | bytes 4718592 | tf_op jit(solution)/shard_map/reduce_scatter | solution.py:1063
  633.1 75.6 %collective-permute-start.26 = (bf16[2,2,128,2048]{3,2,1,0:T(8,128)(2,1)}, bf16[2,2,128,2048]{3,2,1,0:T(8,128)(2,1)}, u32[]{:S(2)}, u32[]{:S(2)}) collective-permute-start(bf16[2,2,128,2048]{3,2,1,0:T(8,128)(2,1)} %get-tuple-element.388), channel_id=1, source_target_pairs={{0,2},{1,3},{2,0},{3,1},{4,6},{5,7},{6,4},{7,5},{8,10},{9,11},{10,... | collective-permute-start | bytes 6291464 | tf_op jit(solution)/shard_map/ppermute | solution.py:971
  636.5 72.2 %collective-permute-start.27 = (bf16[2,2,128,2048]{3,2,1,0:T(8,128)(2,1)}, bf16[2,2,128,2048]{3,2,1,0:T(8,128)(2,1)}, u32[]{:S(2)}, u32[]{:S(2)}) collective-permute-start(bf16[2,2,128,2048]{3,2,1,0:T(8,128)(2,1)} %get-tuple-element.390), channel_id=1, source_target_pairs={{0,4},{1,5},{2,6},{3,7},{4,0},{5,1},{6,2},{7,3},{8,12},{9,13},{10,... | collective-permute-start | bytes 6291464 | tf_op jit(solution)/shard_map/ppermute | solution.py:971
  652.4 56.3 %collective-permute-start.28 = (bf16[304,2048]{1,0:T(8,128)(2,1)}, bf16[304,2048]{1,0:T(8,128)(2,1)}, u32[]{:S(2)}, u32[]{:S(2)}) collective-permute-start(bf16[304,2048]{1,0:T(8,128)(2,1)} %copy-done.30), channel_id=1, source_target_pairs={{0,16},{8,24},{16,0},{24,8},{1,17},{9,25},{17,1},{25,9},{2,18},{10... | collective-permute-start | bytes 3735560 | tf_op jit(solution)/shard_map/ppermute | solution.py:775
  672.6 177.6 %reduce-scatter.12.cloned.1.call-start = ((), (), s32[]{:S(2)}) async-start(), calls=%async_computation.14 | async-start | bytes 9437184 | tf_op jit(solution)/shard_map/reduce_scatter | solution.py:1038
  708.8 165.9 %reduce-scatter.14.cloned.1.call-start = ((), (), s32[]{:S(2)}) async-start(), calls=%async_computation.15 | async-start | bytes 4718592 | tf_op jit(solution)/shard_map/reduce_scatter | solution.py:1105
  771.0 51.1 %collective-permute-start.37 = (bf16[1,2,128,2048]{3,2,1,0:T(8,128)(2,1)}, bf16[1,2,128,2048]{3,2,1,0:T(8,128)(2,1)}, u32[]{:S(2)}, u32[]{:S(2)}) collective-permute-start(bf16[1,2,128,2048]{3,2,1,0:T(8,128)(2,1)} %constant_dynamic-slice_fusion.1), channel_id=1, source_target_pairs={{0,4},{1,5},{2,6},{3,7},{4,0},{5,1},{6,2},{7,3},{8,12},{9,13},{10,... | collective-permute-start | bytes 3145736 | tf_op jit(solution)/shard_map/ppermute | solution.py:971
  777.5 48.4 %collective-permute-start.39 = (bf16[1,2,128,2048]{3,2,1,0:T(8,128)(2,1)}, bf16[1,2,128,2048]{3,2,1,0:T(8,128)(2,1)}, u32[]{:S(2)}, u32[]{:S(2)}) collective-permute-start(bf16[1,2,128,2048]{3,2,1,0:T(8,128)(2,1)} %constant_dynamic-slice_fusion), channel_id=1, source_target_pairs={{0,2},{1,3},{2,0},{3,1},{4,6},{5,7},{6,4},{7,5},{8,10},{9,11},{10,... | collective-permute-start | bytes 3145736 | tf_op jit(solution)/shard_map/ppermute | solution.py:971
  805.8 59.8 %all-to-all-start.4 = ((bf16[8,64,512]{2,1,0:T(8,128)(2,1)}), bf16[8,64,512]{2,1,0:T(8,128)(2,1)S(1)}, u32[]{:S(2)}, u32[]{:S(2)}) async-start(bf16[8,64,512]{2,1,0:T(8,128)(2,1)} %bitcast.161), calls=%async_computation.7 | async-start | bytes 1048576 | tf_op jit(solution)/shard_map/all_to_all | solution.py:1127
  (107 other events, 2483.5 us)
Sparse Core Ops, SparseCore 0:
  9.9 64.3 all-gather.8
  76.8 54.3 all-gather.10
  133.1 101.0 all-gather.14
  248.6 93.1 all-gather.12
  456.8 76.5 reduce-scatter.5
  536.9 79.4 reduce-scatter.7
  633.2 72.1 reduce-scatter.9
  709.3 79.6 reduce-scatter.11
  792.4 58.2 reduce-scatter.13

commit v18 on v17

--- a/solution.py
+++ b/solution.py
@@ -850,6 +850,7 @@
     upstream_group = with_group(cotangent)
     early_rows = cut_ends(out_parts[last_step].shape[0], (12,))[1]
     early = cross_rep(out_parts[last_step][:early_rows], last_step)
+    out_parts[last_step] = out_parts[last_step][early_rows:]
     slab = cut_heads(
         w_qkv,
         jnp.concatenate(
@@ -897,7 +898,6 @@
     payload, in_parts, out_parts = lax.optimization_barrier((payload, in_parts, out_parts))
     in_pieces.update(send(in_parts, [last_step]))
     in_pieces, out_parts = lax.optimization_barrier((in_pieces, out_parts))
-    out_parts[last_step] = out_parts[last_step][early_rows:]
     out_pieces = {0: out_parts[0], **send(out_parts, range(1, planes))}
     in_pieces = [in_pieces[step] for step in range(planes)]
     out_pieces = [out_pieces[step] for step in range(planes)]
@@ -909,7 +909,11 @@
     )
     in_rows = micro * ranks * slots
     out_cut = weight_gradient(
-        where, planes, active.reshape(in_rows, FF), [grad_produced.reshape(in_rows, D)]
+        where,
+        planes,
+        active.reshape(in_rows, FF),
+        [grad_produced.reshape(in_rows, D)],
+        cuts={1: (2,)},
     )
 
     def sum_rep(parts, shift=False):
@@ -929,9 +933,10 @@
 
     tail, out_cut, out_pieces = lax.optimization_barrier((tail, out_cut, out_pieces))
     out_pieces[last_step] = jnp.concatenate([early, out_pieces[last_step]], axis=0)
-    first = cross_rep(out_cut[1][:16], 1)
+    first, *out_cut = out_cut[1], out_cut[0], *out_cut[2:]
+    first = cross_rep(first, 1)
     tail, out_cut, first = lax.optimization_barrier((tail, out_cut, first))
-    out_sent = send([out_cut[0], out_cut[1][16:], *out_cut[2:]], range(1, planes))
+    out_sent = send(out_cut, range(1, planes))
     back = []
     returned = []
 

time: 916 us -> 915 us (level)
    unnamed x150 -> x146, local copies, waits for them, and re-layouts: 25.3 us -> 23.6 us
  transfers between devices with their start and end apart: 59 -> 59, of which waited for: 27 -> 28; matrix products, arithmetic and copies ran while one was open for 13% -> 13% of each run, Pallas kernels for 34% -> 34%
where the time goes in v18:
time: 915 us; the launch traced here: 906 us
  Pallas kernels  312 us (34%)
  waiting for transfers between devices  281 us (31%)
  starting transfers between devices  151 us (17%)
  local copies, waits for them, and re-layouts  71.4 us (8%)
  other arithmetic  65.8 us (7%)
  between operations  15.2 us (2%)
  matrix products  10.1 us (1%)
    ppermute x23, waiting for transfers between devices, cross_rep(): lax.ppermute(value, 'rep', [(i, i ^ bits) for i in range(lax.axis_size('r...  106 us
    ppermute x23, starting transfers between devices, cross_rep(): lax.ppermute(value, 'rep', [(i, i ^ bits) for i in range(lax.axis_size('r...  95.9 us
    pallas_call x2, Pallas kernels, expert_backward(): pl.pallas_call(kernel, grid_spec=pltpu.PrefetchScalarGridSpec(num_scalar_...  85.4 us
    ppermute x6, waiting for transfers between devices, exchange(): return lax.ppermute(value, 'rep', pairs)  67.8 us
    pallas_call x4, Pallas kernels, weight_gradient(): pl.pallas_call(kernel, grid_spec=pltpu.PrefetchScalarGridSpec(num_scalar_...  65.9 us
    ppermute x9, waiting for transfers between devices, shift_rep(): lax.ppermute(value, 'rep', [(i, (i + step) % count) for i in range(count)])  60.4 us
    pallas_call x1, Pallas kernels, expert_forward(): pl.pallas_call(kernel, grid_spec=pltpu.PrefetchScalarGridSpec(num_scalar_...  40.4 us
    pallas_call x2, Pallas kernels, attention_backward(): pl.pallas_call(lambda *refs: backward_kernel(heads, *refs), grid=(1,), in...  34.9 us
  transfers between devices with their start and end apart: 59, of which 28 were waited for; matrix products, arithmetic and copies ran while one was open for 13% of the time, Pallas kernels for 34%

profile of v18, /device:TPU:0, one launch (start us, length us, event | category | flops | bytes accessed | tf_op | source)
XLA Modules:
  0.0 905.9 jit_solution(17230362590988215478)
XLA Ops:
  27.2 22.1 %collective-permute-done.3 = bf16[256,2048]{1,0:T(8,128)(2,1)S(1)} collective-permute-done((bf16[256,2048]{1,0:T(8,128)(2,1)}, bf16[256,2048]{1,0:T(8,128)(2,1)S(1)}, u32[]{:S(2)}, u32[]{:S(2)}) %collective-permute-start.3) | collective-permute-done | bytes 1048608 | tf_op jit(solution)/shard_map/ppermute | solution.py:827
  69.0 19.9 %collective-permute-done.5 = bf16[512,896]{1,0:T(8,128)(2,1)} collective-permute-done((bf16[512,896]{1,0:T(8,128)(2,1)}, bf16[512,896]{1,0:T(8,128)(2,1)}, u32[]{:S(2)}, u32[]{:S(2)}) %collective-permute-start.5) | collective-permute-done | bytes 917536 | tf_op jit(solution)/shard_map/ppermute | solution.py:775
  99.3 11.9 %collective-permute-done.6 = bf16[512,896]{1,0:T(8,128)(2,1)} collective-permute-done((bf16[512,896]{1,0:T(8,128)(2,1)}, bf16[512,896]{1,0:T(8,128)(2,1)}, u32[]{:S(2)}, u32[]{:S(2)}) %collective-permute-start.6) | collective-permute-done | bytes 917536 | tf_op jit(solution)/shard_map/ppermute | solution.py:775
  120.3 12.3 %collective-permute-done.7 = bf16[512,896]{1,0:T(8,128)(2,1)S(1)} collective-permute-done((bf16[512,896]{1,0:T(8,128)(2,1)}, bf16[512,896]{1,0:T(8,128)(2,1)S(1)}, u32[]{:S(2)}, u32[]{:S(2)}) %collective-permute-start.7) | collective-permute-done | bytes 917536 | tf_op jit(solution)/shard_map/ppermute | solution.py:775
  137.3 15.8 %shard_map.179 = (bf16[2,8,128,2048]{3,2,1,0:T(8,128)(2,1)}, f32[8,256,768]{2,1,0:T(8,128)}) custom-call(bf16[8,256,2048]{2,1,0:T(8,128)(2,1)} %bitcast.142, f32[1,2048]{1,0:T(1,128)S(1)} %broadcast_in_dim.56.gain, bf16[2048,896]{1,0:T(8,128)(2,1)} %constant_dynamic-update-slice_fusion.weight), custom_call_target="tpu_custom_call" | custom-call | tf_op jit(solution)/shard_map/pallas_call | solution.py:248
  153.1 21.8 %shard_map.180 = (bf16[8,2,128,256]{3,2,1,0:T(8,128)(2,1)}, bf16[2,1024,256]{2,1,0:T(8,128)(2,1)S(1)}, bf16[2,1024,256]{2,1,0:T(8,128)(2,1)S(1)}, bf16[2,1024,256]{2,1,0:T(8,128)(2,1)}, f32[2,2,1024,1]{3,2,1,0:T(8,128)}) custom-call(f32[8,2,128,768]{3,2,1,0:T(8,128)} %bitcast.145, f32[2,1024,128]{2,1,0:T(8,128)} %get-tuple-element.267.refs_1_, ...), custom_call_target="tpu_custom_call" | custom-call | tf_op jit(solution)/shard_map/pallas_call | solution.py:198
  183.0 25.1 %all-to-all-done.1 = bf16[8,2,128,256]{3,2,1,0:T(8,128)(2,1)S(1)} async-done(((bf16[8,2,128,256]{3,2,1,0:T(8,128)(2,1)}), bf16[8,2,128,256]{3,2,1,0:T(8,128)(2,1)S(1)}, u32[]{:S(2)}, u32[]{:S(2)}) %all-to-all-start.1) | async-done | bytes 1048608 | tf_op jit(solution)/shard_map/all_to_all | solution.py:890
  224.0 23.5 %collective-permute-done.10 = bf16[256,2176]{1,0:T(8,128)(2,1)S(1)} collective-permute-done((bf16[256,2176]{1,0:T(8,128)(2,1)S(1)}, bf16[256,2176]{1,0:T(8,128)(2,1)S(1)}, u32[]{:S(2)}, u32[]{:S(2)}) %collective-permute-start.10) | collective-permute-done | bytes 1114144 | tf_op jit(solution)/shard_map/ppermute | solution.py:827
  251.3 43.9 %collective-permute-done.11.refs_3_ = bf16[512,2048]{1,0:T(8,128)(2,1)} collective-permute-done((bf16[512,2048]{1,0:T(8,128)(2,1)}, bf16[512,2048]{1,0:T(8,128)(2,1)}, u32[]{:S(2)}, u32[]{:S(2)}) %collective-permute-start.11) | collective-permute-done | bytes 2097184 | tf_op jit(solution)/shard_map/ppermute | solution.py:779
  295.2 42.6 %collective-permute-start.12 = (bf16[256,2048]{1,0:T(8,128)(2,1)}, bf16[256,2048]{1,0:T(8,128)(2,1)}, u32[]{:S(2)}, u32[]{:S(2)}) collective-permute-start(bf16[256,2048]{1,0:T(8,128)(2,1)} %get-tuple-element.316), channel_id=1, source_target_pairs={{0,8},{8,0},{16,24},{24,16},{1,9},{9,1},{17,25},{25,17},{2,10},{10... | collective-permute-start | bytes 3145736 | tf_op jit(solution)/shard_map/ppermute | solution.py:779
  342.1 40.4 %shard_map.182 = (bf16[2,4,288,2048]{3,2,1,0:T(8,128)(2,1)}, f32[2,4,288,128]{3,2,1,0:T(8,128)S(1)}, f32[2,4,288,2048]{3,2,1,0:T(8,128)}, bf16[2,4,288,1024]{3,2...) custom-call(s32[3]{0:T(128)S(1)} %pad_add_fusion.where, ...), custom_call_target="tpu_custom_call" | custom-call | flops 241591910400 | tf_op jit(solution)/shard_map/pallas_call | solution.py:435
  383.9 17.5 %shard_map.183 = (bf16[256,2048]{1,0:T(8,128)(2,1)S(1)}, bf16[16,2048]{1,0:T(8,128)(2,1)S(1)}, bf16[240,2048]{1,0:T(8,128)(2,1)}, bf16[256,2048]{1,0:T(8,128)(2,1)}, bf16[256,2048]{1,0:T(8,128)(2,1)}) custom-call(s32[3]{0:T(128)S(1)} %pad_add_fusion.where, bf16[2304,1024]{1,0:T(8,128)(2,1)} %bitcast.176, bf16[2304,2048]{1,0:T(8,128)(2,1)} %bitcast.175), custom_call_target="tpu_custom_call" | custom-call | flops 96636764160 | tf_op jit(solution)/shard_map/pallas_call | solution.py:618
  418.0 40.7 %shard_map.184 = (bf16[4,2,128,2048]{3,2,1,0:T(8,128)(2,1)}, bf16[4,2,128,2048]{3,2,1,0:T(8,128)(2,1)}, bf16[8,2,128,2176]{3,2,1,0:T(8,128)(2,1)}, bf16[4,288,2048]{2,1,0:T(8,128)(2,1)}) custom-call(s32[3]{0:T(128)S(1)} %pad_add_fusion.where, f32[2,4,288,128]{3,2,1,0:T(8,128)} %copy-done.37, f32[2,4,288,2048]{3,2,1,0:T(8,128)} %get-tuple-element.326.both, ...), custom_call_target="tpu_custom_call" | custom-call | flops 217432719360 | tf_op jit(solution)/shard_map/pallas_call | solution.py:533
  461.7 44.7 %shard_map.185 = (bf16[4,2,128,2048]{3,2,1,0:T(8,128)(2,1)}, bf16[4,2,128,2048]{3,2,1,0:T(8,128)(2,1)}, bf16[8,2,128,2176]{3,2,1,0:T(8,128)(2,1)}, bf16[4,288,2048]{2,1,0:T(8,128)(2,1)}) custom-call(s32[3]{0:T(128)S(1)} %pad_add_fusion.where, f32[2,4,288,128]{3,2,1,0:T(8,128)} %copy-done.37, f32[2,4,288,2048]{3,2,1,0:T(8,128)} %get-tuple-element.326.both, ...), custom_call_target="tpu_custom_call" | custom-call | flops 217432719360 | tf_op jit(solution)/shard_map/pallas_call | solution.py:533
  506.4 12.0 %shard_map.186 = (bf16[384,2048]{1,0:T(8,128)(2,1)}, bf16[128,2048]{1,0:T(8,128)(2,1)}) custom-call(s32[3]{0:T(128)S(1)} %pad_add_fusion.where, bf16[2304,2048]{1,0:T(8,128)(2,1)} %bitcast.173, bf16[1152,2048]{1,0:T(8,128)(2,1)} %bitcast.177, bf16[1152,2048]{1,0:T(8,128)(2,1)} %bitcast.179), custom_call_target="tpu_custom_call" | custom-call | flops 48318382080 | tf_op jit(solution)/shard_map/pallas_call | solution.py:618
  518.5 24.3 %shard_map.187 = (bf16[304,2048]{1,0:T(8,128)(2,1)S(1)}, bf16[144,2048]{1,0:T(8,128)(2,1)S(1)}, bf16[64,2048]{1,0:T(8,128)(2,1)}, bf16[512,2048]{1,0:T(8,128)(2,1)}, bf16[512,2048]{1,0:T(8,128)(2,1)}) custom-call(s32[3]{0:T(128)S(1)} %pad_add_fusion.where, bf16[2304,2048]{1,0:T(8,128)(2,1)} %bitcast.174, bf16[1152,2048]{1,0:T(8,128)(2,1)} %bitcast.178, ...), custom_call_target="tpu_custom_call" | custom-call | flops 144955146240 | tf_op jit(solution)/shard_map/pallas_call | solution.py:618
  597.9 17.4 %shard_map.189 = (bf16[8,128,768]{2,1,0:T(8,128)(2,1)}, f32[2,128]{1,0:T(2,128)S(1)}) custom-call(f32[8,2,128,768]{3,2,1,0:T(8,128)} %bitcast.146, f32[2,1024,128]{2,1,0:T(8,128)S(1)} %copy-done.2, f32[2,1024,128]{2,1,0:T(8,128)S(1)} %copy-done.1, s32[2,1024,1]{2,1,0:T(8,128)S(1)} %copy-done.3, s32[2,1,1024]{2,1,0:T(1,128)S(1)} %copy-done.23, ...), custom_call_target="tpu_custom_call" | custom-call | tf_op jit(solution)/shard_map/pallas_call | solution.py:220
  639.5 11.9 %collective-permute-done.25.refs_1_ = bf16[128,2176]{1,0:T(8,128)(2,1)S(1)} collective-permute-done((bf16[128,2176]{1,0:T(8,128)(2,1)S(1)}, bf16[128,2176]{1,0:T(8,128)(2,1)S(1)}, u32[]{:S(2)}, u32[]{:S(2)}) %collective-permute-start.25) | collective-permute-done | bytes 557088 | tf_op jit(solution)/shard_map/ppermute | solution.py:827
  687.3 18.7 %all-to-all-done.3 = bf16[128,8,256]{2,0,1:T(8,128)(2,1)} async-done(((bf16[128,8,256]{2,0,1:T(8,128)(2,1)}), bf16[128,8,256]{2,0,1:T(8,128)(2,1)}, u32[]{:S(2)}, u32[]{:S(2)}) %all-to-all-start.3) | async-done | bytes 524320 | tf_op jit(solution)/shard_map/all_to_all | solution.py:1037
  713.2 17.4 %shard_map.192 = (bf16[8,128,768]{2,1,0:T(8,128)(2,1)}, f32[2,128]{1,0:T(2,128)S(1)}) custom-call(f32[8,2,128,768]{3,2,1,0:T(8,128)} %bitcast.147, f32[2,1024,128]{2,1,0:T(8,128)S(1)} %copy-done.2, f32[2,1024,128]{2,1,0:T(8,128)S(1)} %copy-done.1, s32[2,1024,1]{2,1,0:T(8,128)S(1)} %copy-done.4, s32[2,1,1024]{2,1,0:T(1,128)S(1)} %copy-done.23, ...), custom_call_target="tpu_custom_call" | custom-call | tf_op jit(solution)/shard_map/pallas_call | solution.py:220
  749.5 12.1 %shard_map.194 = (bf16[512,512]{1,0:T(8,128)(2,1)S(1)}, bf16[512,384]{1,0:T(8,128)(2,1)S(1)}, bf16[512,512]{1,0:T(8,128)(2,1)}, bf16[512,384]{1,0:T(8,128)(2,1)S...) custom-call(s32[3]{0:T(128)S(1)} %pad_add_fusion.where, ...), custom_call_target="tpu_custom_call" | custom-call | tf_op jit(solution)/shard_map/pallas_call | solution.py:618
  791.6 11.6 %collective-permute-done.32 = bf16[512,512]{1,0:T(8,128)(2,1)} collective-permute-done((bf16[512,512]{1,0:T(8,128)(2,1)}, bf16[512,512]{1,0:T(8,128)(2,1)}, u32[]{:S(2)}, u32[]{:S(2)}) %collective-permute-start.32) | collective-permute-done | bytes 524320 | tf_op jit(solution)/shard_map/ppermute | solution.py:779
  809.3 10.3 %collective-permute-start.34 = (bf16[512,384]{1,0:T(8,128)(2,1)S(1)}, bf16[512,384]{1,0:T(8,128)(2,1)S(1)}, u32[]{:S(2)}, u32[]{:S(2)}) collective-permute-start(bf16[512,384]{1,0:T(8,128)(2,1)S(1)} %copy-done.35), channel_id=1, source_target_pairs={{0,8},{8,0},{16,24},{24,16},{1,9},{9,1},{17,25},{25,17},{2,10},{10... | collective-permute-start | bytes 1179656 | tf_op jit(solution)/shard_map/ppermute | solution.py:779
  835.9 13.6 %collective-permute-done.35 = bf16[512,384]{1,0:T(8,128)(2,1)S(1)} collective-permute-done((bf16[512,384]{1,0:T(8,128)(2,1)S(1)}, bf16[512,384]{1,0:T(8,128)(2,1)S(1)}, u32[]{:S(2)}, u32[]{:S(2)}) %collective-permute-start.35) | collective-permute-done | bytes 393248 | tf_op jit(solution)/shard_map/ppermute | solution.py:779
  (359 shorter events, 359.0 us)
Async XLA Ops:
  7.2 126.4 %all-gather.9.cloned.1.call-start = ((), (), s32[]{:S(2)}) async-start(), calls=%async_computation.16 | async-start | bytes 9437184 | tf_op jit(solution)/shard_map/all_gather | solution.py:833
  14.9 47.2 %all-to-all-start = ((bf16[8,64,896]{2,1,0:T(8,128)(2,1)}), bf16[8,64,896]{2,1,0:T(8,128)(2,1)}, u32[]{:S(2)}, u32[]{:S(2)}) async-start(bf16[8,64,896]{2,1,0:T(8,128)(2,1)} %shard_map.178), calls=%async_computation | async-start | bytes 1835008 | tf_op jit(solution)/shard_map/all_to_all | solution.py:866
  19.1 189.9 %all-gather.11.cloned.1.call-start = ((), (), s32[]{:S(2)}) async-start(), calls=%async_computation.17 | async-start | bytes 9437184 | tf_op jit(solution)/shard_map/all_gather | solution.py:833
  64.4 275.7 %all-gather.15.cloned.1.call-start = ((), (), s32[]{:S(2)}) async-start(), calls=%async_computation.19 | async-start | bytes 18874368 | tf_op jit(solution)/shard_map/all_gather | solution.py:833
  133.6 87.6 %collective-permute-start.8 = (bf16[512,2048]{1,0:T(8,128)(2,1)}, bf16[512,2048]{1,0:T(8,128)(2,1)}, u32[]{:S(2)}, u32[]{:S(2)}) collective-permute-start(bf16[512,2048]{1,0:T(8,128)(2,1)} %get-tuple-element.298), channel_id=1, source_target_pairs={{0,8},{8,0},{16,24},{24,16},{1,9},{9,1},{17,25},{25,17},{2,10},{10... | collective-permute-start | bytes 6291464 | tf_op jit(solution)/shard_map/ppermute | solution.py:779
  133.7 90.4 %collective-permute-start.9 = (bf16[512,2048]{1,0:T(8,128)(2,1)}, bf16[512,2048]{1,0:T(8,128)(2,1)}, u32[]{:S(2)}, u32[]{:S(2)}) collective-permute-start(bf16[512,2048]{1,0:T(8,128)(2,1)} %get-tuple-element.303.refs_0_), channel_id=1, source_target_pairs={{0,16},{8,24},{16,0},{24,8},{1,17},{9,25},{17,1},{25,9},{2,18},{10... | collective-permute-start | bytes 6291464 | tf_op jit(solution)/shard_map/ppermute | solution.py:779
  181.1 160.9 %all-gather.13.cloned.1.call-start = ((), (), s32[]{:S(2)}) async-start(), calls=%async_computation.18 | async-start | bytes 20054016 | tf_op jit(solution)/shard_map/all_gather | solution.py:833
  249.2 300.1 %reduce-scatter.6.cloned.1.call-start = ((), (), s32[]{:S(2)}) async-start(), calls=%async_computation.11 | async-start | bytes 10027008 | tf_op jit(solution)/shard_map/reduce_scatter | solution.py:944
  295.2 107.3 %collective-permute-start.12 = (bf16[256,2048]{1,0:T(8,128)(2,1)}, bf16[256,2048]{1,0:T(8,128)(2,1)}, u32[]{:S(2)}, u32[]{:S(2)}) collective-permute-start(bf16[256,2048]{1,0:T(8,128)(2,1)} %get-tuple-element.316), channel_id=1, source_target_pairs={{0,8},{8,0},{16,24},{24,16},{1,9},{9,1},{17,25},{25,17},{2,10},{10... | collective-permute-start | bytes 3145736 | tf_op jit(solution)/shard_map/ppermute | solution.py:779
  337.8 64.7 %collective-permute-start.13 = (bf16[256,2048]{1,0:T(8,128)(2,1)}, bf16[256,2048]{1,0:T(8,128)(2,1)}, u32[]{:S(2)}, u32[]{:S(2)}) collective-permute-start(bf16[256,2048]{1,0:T(8,128)(2,1)} %get-tuple-element.329.refs_4_), channel_id=1, source_target_pairs={{0,16},{8,24},{16,0},{24,8},{1,17},{9,25},{17,1},{25,9},{2,18},{10... | collective-permute-start | bytes 3145736 | tf_op jit(solution)/shard_map/ppermute | solution.py:779
  338.6 63.9 %collective-permute-start.14 = (bf16[160,2048]{1,0:T(8,128)(2,1)}, bf16[160,2048]{1,0:T(8,128)(2,1)}, u32[]{:S(2)}, u32[]{:S(2)}) collective-permute-start(bf16[160,2048]{1,0:T(8,128)(2,1)} %dynamic-slice_bitcast_fusion.4), channel_id=1, source_target_pairs={{0,24},{8,16},{16,8},{24,0},{1,25},{9,17},{17,9},{25,1},{2,26},{10... | collective-permute-start | bytes 1966088 | tf_op jit(solution)/shard_map/ppermute | solution.py:779
  458.7 172.4 %reduce-scatter.8.cloned.1.call-start = ((), (), s32[]{:S(2)}) async-start(), calls=%async_computation.12 | async-start | bytes 10027008 | tf_op jit(solution)/shard_map/reduce_scatter | solution.py:944
  458.8 85.9 %collective-permute-start.17 = (bf16[240,2048]{1,0:T(8,128)(2,1)}, bf16[240,2048]{1,0:T(8,128)(2,1)}, u32[]{:S(2)}, u32[]{:S(2)}) collective-permute-start(bf16[240,2048]{1,0:T(8,128)(2,1)} %get-tuple-element.349), channel_id=1, source_target_pairs={{0,8},{8,0},{16,24},{24,16},{1,9},{9,1},{17,25},{25,17},{2,10},{10... | collective-permute-start | bytes 2949128 | tf_op jit(solution)/shard_map/ppermute | solution.py:779
  459.4 85.3 %collective-permute-start.18 = (bf16[256,2048]{1,0:T(8,128)(2,1)}, bf16[256,2048]{1,0:T(8,128)(2,1)}, u32[]{:S(2)}, u32[]{:S(2)}) collective-permute-start(bf16[256,2048]{1,0:T(8,128)(2,1)} %get-tuple-element.350), channel_id=1, source_target_pairs={{0,16},{8,24},{16,0},{24,8},{1,17},{9,25},{17,1},{25,9},{2,18},{10... | collective-permute-start | bytes 3145736 | tf_op jit(solution)/shard_map/ppermute | solution.py:779
  561.1 59.4 %collective-permute-start.23 = (bf16[512,2048]{1,0:T(8,128)(2,1)}, bf16[512,2048]{1,0:T(8,128)(2,1)}, u32[]{:S(2)}, u32[]{:S(2)}) collective-permute-start(bf16[512,2048]{1,0:T(8,128)(2,1)} %get-tuple-element.374), channel_id=1, source_target_pairs={{0,24},{8,0},{16,8},{24,16},{1,25},{9,1},{17,9},{25,17},{2,26},{10... | collective-permute-start | bytes 6291464 | tf_op jit(solution)/shard_map/ppermute | solution.py:775
  581.3 154.5 %reduce-scatter.10.cloned.1.call-start = ((), (), s32[]{:S(2)}) async-start(), calls=%async_computation.13 | async-start | bytes 4718592 | tf_op jit(solution)/shard_map/reduce_scatter | solution.py:1068
  631.1 76.4 %collective-permute-start.26 = (bf16[2,2,128,2048]{3,2,1,0:T(8,128)(2,1)}, bf16[2,2,128,2048]{3,2,1,0:T(8,128)(2,1)}, u32[]{:S(2)}, u32[]{:S(2)}) collective-permute-start(bf16[2,2,128,2048]{3,2,1,0:T(8,128)(2,1)} %get-tuple-element.392), channel_id=1, source_target_pairs={{0,2},{1,3},{2,0},{3,1},{4,6},{5,7},{6,4},{7,5},{8,10},{9,11},{10,... | collective-permute-start | bytes 6291464 | tf_op jit(solution)/shard_map/ppermute | solution.py:976
  636.8 70.7 %collective-permute-start.27 = (bf16[2,2,128,2048]{3,2,1,0:T(8,128)(2,1)}, bf16[2,2,128,2048]{3,2,1,0:T(8,128)(2,1)}, u32[]{:S(2)}, u32[]{:S(2)}) collective-permute-start(bf16[2,2,128,2048]{3,2,1,0:T(8,128)(2,1)} %get-tuple-element.394), channel_id=1, source_target_pairs={{0,4},{1,5},{2,6},{3,7},{4,0},{5,1},{6,2},{7,3},{8,12},{9,13},{10,... | collective-permute-start | bytes 6291464 | tf_op jit(solution)/shard_map/ppermute | solution.py:976
  651.3 56.2 %collective-permute-start.28 = (bf16[304,2048]{1,0:T(8,128)(2,1)}, bf16[304,2048]{1,0:T(8,128)(2,1)}, u32[]{:S(2)}, u32[]{:S(2)}) collective-permute-start(bf16[304,2048]{1,0:T(8,128)(2,1)} %copy-done.28), channel_id=1, source_target_pairs={{0,16},{8,24},{16,0},{24,8},{1,17},{9,25},{17,1},{25,9},{2,18},{10... | collective-permute-start | bytes 3735560 | tf_op jit(solution)/shard_map/ppermute | solution.py:775
  671.3 178.9 %reduce-scatter.12.cloned.1.call-start = ((), (), s32[]{:S(2)}) async-start(), calls=%async_computation.14 | async-start | bytes 9437184 | tf_op jit(solution)/shard_map/reduce_scatter | solution.py:1043
  707.5 167.1 %reduce-scatter.14.cloned.1.call-start = ((), (), s32[]{:S(2)}) async-start(), calls=%async_computation.15 | async-start | bytes 4718592 | tf_op jit(solution)/shard_map/reduce_scatter | solution.py:1110
  770.8 51.3 %collective-permute-start.37 = (bf16[1,2,128,2048]{3,2,1,0:T(8,128)(2,1)}, bf16[1,2,128,2048]{3,2,1,0:T(8,128)(2,1)}, u32[]{:S(2)}, u32[]{:S(2)}) collective-permute-start(bf16[1,2,128,2048]{3,2,1,0:T(8,128)(2,1)} %constant_dynamic-slice_fusion.1), channel_id=1, source_target_pairs={{0,4},{1,5},{2,6},{3,7},{4,0},{5,1},{6,2},{7,3},{8,12},{9,13},{10,... | collective-permute-start | bytes 3145736 | tf_op jit(solution)/shard_map/ppermute | solution.py:976
  777.2 48.8 %collective-permute-start.39 = (bf16[1,2,128,2048]{3,2,1,0:T(8,128)(2,1)}, bf16[1,2,128,2048]{3,2,1,0:T(8,128)(2,1)}, u32[]{:S(2)}, u32[]{:S(2)}) collective-permute-start(bf16[1,2,128,2048]{3,2,1,0:T(8,128)(2,1)} %constant_dynamic-slice_fusion), channel_id=1, source_target_pairs={{0,2},{1,3},{2,0},{3,1},{4,6},{5,7},{6,4},{7,5},{8,10},{9,11},{10,... | collective-permute-start | bytes 3145736 | tf_op jit(solution)/shard_map/ppermute | solution.py:976
  805.8 59.7 %all-to-all-start.4 = ((bf16[8,64,512]{2,1,0:T(8,128)(2,1)}), bf16[8,64,512]{2,1,0:T(8,128)(2,1)S(1)}, u32[]{:S(2)}, u32[]{:S(2)}) async-start(bf16[8,64,512]{2,1,0:T(8,128)(2,1)} %bitcast.161), calls=%async_computation.7 | async-start | bytes 1048576 | tf_op jit(solution)/shard_map/all_to_all | solution.py:1132
  (105 other events, 2506.9 us)
Sparse Core Ops, SparseCore 0:
  9.9 64.8 all-gather.8
  77.2 54.3 all-gather.10
  133.7 100.9 all-gather.14
  249.3 92.7 all-gather.12
  458.8 73.8 reduce-scatter.5
  536.2 79.3 reduce-scatter.7
  631.2 73.5 reduce-scatter.9
  708.6 78.1 reduce-scatter.11
  790.3 59.1 reduce-scatter.13
